TPU v7x, 32 devices: a whole 2x2x4 slice. The times are simulated.
32 devices in a mesh: dp: 4 (over y, x), row: 2 (over core), col: 4 (over z).
Axes of the slice: x: 2, y: 2, z: 4, core: 2. Of those that a mesh axis runs over, the one named last changes fastest.
Arguments:
- tokens_in: bfloat16 [16384, 2048], P(('dp', 'col'), 'row'), may hold values from -6 to 6
- out_grad: bfloat16 [16384, 2048], P(('dp', 'col'), 'row'), may hold values from -6 to 6
- segment_ids: int32 [16, 1024], P('dp'), may hold values from 0 to 3, never falling along the last dimension, each value on 1 to 800 neighbouring positions
- active_lengths: int32 [16, 4], P('dp'), may hold values from 1 to 800
- norm1_gain: float32 [2048], P('row'), may hold values from 0.5 to 1.5
- norm1_shift: float32 [2048], P('row'), may hold values from -1.5 to 1.5
- query_weight: bfloat16 [2048, 2048], P('row', 'col'), may hold values from -0.125 to 0.125
- query_bias: float32 [2048], P('col'), may hold values from -1.5 to 1.5
- key_weight: bfloat16 [2048, 2048], P('row', 'col'), may hold values from -0.125 to 0.125
- value_weight: bfloat16 [2048, 2048], P('row', 'col'), may hold values from -0.125 to 0.125
- value_bias: float32 [2048], P('col'), may hold values from -1.5 to 1.5
- out_weight: bfloat16 [2048, 2048], P('col', 'row'), may hold values from -0.5 to 0.5
- out_bias: float32 [2048], P('row'), may hold values from -1.5 to 1.5
- norm2_gain: float32 [2048], P('row'), may hold values from 0.5 to 1.5
- norm2_shift: float32 [2048], P('row'), may hold values from -1.5 to 1.5
- up_weight: bfloat16 [2048, 8192], P('row', 'col'), may hold values from -0.125 to 0.125
- up_bias: float32 [8192], P('col'), may hold values from -1.5 to 1.5
- down_weight: bfloat16 [8192, 2048], P('col', 'row'), may hold values from -0.09375 to 0.09375
- down_bias: float32 [2048], P('row'), may hold values from -1.5 to 1.5
Outputs:
- layer_out: float32 [16384, 2048], P(('dp', 'col'), 'row')
- input_grad: float32 [16384, 2048], P(('dp', 'col'), 'row')
- norm1_gain_grad: float32 [2048], P('row')
- norm1_shift_grad: float32 [2048], P('row')
- query_weight_grad: float32 [2048, 2048], P('row', 'col')
- query_bias_grad: float32 [2048], P('col')
- key_weight_grad: float32 [2048, 2048], P('row', 'col')
- value_weight_grad: float32 [2048, 2048], P('row', 'col')
- value_bias_grad: float32 [2048], P('col')
- out_weight_grad: float32 [2048, 2048], P('col', 'row')
- out_bias_grad: float32 [2048], P('row')
- norm2_gain_grad: float32 [2048], P('row')
- norm2_shift_grad: float32 [2048], P('row')
- up_weight_grad: float32 [2048, 8192], P('row', 'col')
- up_bias_grad: float32 [8192], P('col')
- down_weight_grad: float32 [8192, 2048], P('col', 'row')
- down_bias_grad: float32 [2048], P('row')
Inputs may be any that keep to these rules, and one draw needn't show every extreme that they name: `segment_ids`: each sequence holds documents numbered 0 to 3 in order, each of 1 to 800 tokens, one of exactly 800. active_lengths[s, j] is the number of leading tokens of document j of sequence s that are active; the whole document is active where it is shorter.
All inputs are finite; a program needn't handle non-finite values.
Results may differ from a plain program's by a relative error of at most 0.013.
Values may be sent and summed in bfloat16 or wider, within the bound.
No kernel may reach another device: no remote copies, remote signals or barrier semaphores. Data moves between devices by JAX's collectives and lax.ppermute only.
A program may use at most 384 MiB of HBM per device.

v0:
```python
import jax
import jax.numpy as jnp
from jax import lax
from jax.sharding import PartitionSpec as P

D = 2048
HEAD_DIM = 64


norm_eps = 1e-05
masked_fill = -1e30


def width_totals(total_one, total_two):
    return lax.psum((total_one, total_two), "row")


def token_gather(values):
    return lax.all_gather(values, "col", axis=0, tiled=True)


def token_sums(partial_rows):
    return lax.psum_scatter(partial_rows, "col", scatter_dimension=0, tiled=True)


def unit_gather(values):
    return lax.all_gather(values, "row", axis=1, tiled=True)


def unit_sums(partial_units):
    return lax.psum_scatter(partial_units, "row", scatter_dimension=1, tiled=True)


def gelu_value(values):
    return jax.nn.gelu(values, approximate=True)


def gelu_slope(values):
    result, pullback = jax.vjp(gelu_value, values)
    return pullback(jnp.ones_like(values))[0]


def active_rows(segment_rows, keep_lengths):
    doc_index = jnp.arange(keep_lengths.shape[-1], dtype=jnp.int32)
    member = (segment_rows[:, :, None] == doc_index).astype(jnp.int32)
    counts = jnp.sum(member, axis=1)
    starts = jnp.cumsum(counts, axis=1) - counts
    first_pos = jnp.sum(member * starts[:, None, :], axis=2)
    keep_here = jnp.sum(member * keep_lengths[:, None, :], axis=2)
    position_in = jnp.arange(segment_rows.shape[1], dtype=jnp.int32)[None, :] - first_pos
    return (position_in < keep_here).reshape(-1)


def norm_forward(values, gain_part, shift_part):
    total_one, total_two = width_totals(jnp.sum(values, axis=1), jnp.sum(values * values, axis=1))
    average = total_one / D
    variance = total_two / D - average * average
    inverse = lax.rsqrt(variance + norm_eps)
    normal = (values - average[:, None]) * inverse[:, None]
    return ((normal * gain_part + shift_part).astype(jnp.bfloat16), normal, inverse)


def norm_backward(grad_rows, normal, inverse, gain_part):
    scaled = grad_rows * gain_part
    total_one, total_two = width_totals(jnp.sum(scaled, axis=1), jnp.sum(scaled * normal, axis=1))
    grad_in = inverse[:, None] * (
        scaled - total_one[:, None] / D - normal * (total_two[:, None] / D)
    )
    return (grad_in, jnp.sum(grad_rows * normal, axis=0), jnp.sum(grad_rows, axis=0))


def allowed_mask(segment_row, offset, block_rows):
    key_pos = jnp.arange(segment_row.shape[0], dtype=jnp.int32)
    query_pos = key_pos[offset : offset + block_rows]
    same_doc = segment_row[None, :] == segment_row[offset : offset + block_rows, None]
    return (key_pos[None, :] <= query_pos[:, None]) & same_doc


def attend_forward(query_seq, key_seq, value_seq, segment_row, score_scale):
    seq_length = query_seq.shape[2]
    block_rows = min(512, seq_length)
    outputs = []
    log_parts = []
    for offset in range(0, seq_length, block_rows):
        query_block = query_seq[:, :, offset : offset + block_rows]
        scores = (
            jnp.einsum("hdq,hdk->hqk", query_block, key_seq, preferred_element_type=jnp.float32)
            * score_scale
        )
        scores = jnp.where(allowed_mask(segment_row, offset, block_rows)[None], scores, masked_fill)
        row_max = jnp.max(scores, axis=2, keepdims=True)
        exp_scores = jnp.exp(scores - row_max)
        row_total = jnp.sum(exp_scores, axis=2, keepdims=True)
        weights = (exp_scores / row_total).astype(jnp.bfloat16)
        outputs.append(
            jnp.einsum("hqk,hdk->hdq", weights, value_seq, preferred_element_type=jnp.float32)
        )
        log_parts.append((row_max + jnp.log(row_total))[:, :, 0])
    return (jnp.concatenate(outputs, axis=2), jnp.concatenate(log_parts, axis=1))


def attend_backward(query_seq, key_seq, value_seq, grad_seq, segment_row, log_sums, score_scale):
    seq_length = query_seq.shape[2]
    block_rows = min(512, seq_length)
    key_grad = jnp.zeros(key_seq.shape, jnp.float32)
    value_grad = jnp.zeros(value_seq.shape, jnp.float32)
    query_grads = []
    for offset in range(0, seq_length, block_rows):
        query_block = query_seq[:, :, offset : offset + block_rows]
        grad_block = grad_seq[:, :, offset : offset + block_rows]
        scores = (
            jnp.einsum("hdq,hdk->hqk", query_block, key_seq, preferred_element_type=jnp.float32)
            * score_scale
        )
        scores = jnp.where(allowed_mask(segment_row, offset, block_rows)[None], scores, masked_fill)
        probs = jnp.exp(scores - log_sums[:, offset : offset + block_rows, None])
        prob_grad = jnp.einsum(
            "hdq,hdk->hqk", grad_block, value_seq, preferred_element_type=jnp.float32
        )
        row_dot = jnp.sum(probs * prob_grad, axis=2, keepdims=True)
        score_grad = (probs * (prob_grad - row_dot)).astype(jnp.bfloat16)
        query_grads.append(
            jnp.einsum("hqk,hdk->hdq", score_grad, key_seq, preferred_element_type=jnp.float32)
            * score_scale
        )
        key_grad = (
            key_grad
            + jnp.einsum(
                "hqk,hdq->hdk", score_grad, query_block, preferred_element_type=jnp.float32
            )
            * score_scale
        )
        value_grad = value_grad + jnp.einsum(
            "hqk,hdq->hdk",
            probs.astype(jnp.bfloat16),
            grad_block,
            preferred_element_type=jnp.float32,
        )
    return (jnp.concatenate(query_grads, axis=2), key_grad, value_grad)


def body(
    tokens_in,
    out_grad,
    segment_ids,
    active_lengths,
    norm1_gain,
    norm1_shift,
    query_weight,
    query_bias,
    key_weight,
    value_weight,
    value_bias,
    out_weight,
    out_bias,
    norm2_gain,
    norm2_shift,
    up_weight,
    up_bias,
    down_weight,
    down_bias,
):
    local_rows = tokens_in.shape[0]
    seq_here = segment_ids.shape[0]
    seq_length = segment_ids.shape[1]
    group_rows = seq_here * seq_length
    row_index = lax.axis_index("row")
    col_index = lax.axis_index("col")
    active_all = active_rows(segment_ids, active_lengths)
    active_here = lax.dynamic_slice_in_dim(active_all, col_index * local_rows, local_rows)
    keep_mask = active_here.astype(jnp.float32)[:, None]
    score_scale = HEAD_DIM ** (-0.5)
    rows_in = tokens_in.astype(jnp.float32)
    normed_one, normal_one, inverse_one = norm_forward(rows_in, norm1_gain, norm1_shift)
    gathered_one = token_gather(normed_one)
    stacked_weight = jnp.stack([query_weight, key_weight, value_weight])
    projected = unit_sums(
        jnp.einsum("td,kdh->kht", gathered_one, stacked_weight, preferred_element_type=jnp.float32)
    )
    head_width = projected.shape[1]
    head_count = head_width // HEAD_DIM
    query_part = lax.dynamic_slice_in_dim(query_bias, row_index * head_width, head_width)
    value_part = lax.dynamic_slice_in_dim(value_bias, row_index * head_width, head_width)
    bias_stack = jnp.stack([query_part, jnp.zeros_like(query_part), value_part])
    heads_all = (projected + bias_stack[:, :, None]).astype(jnp.bfloat16)

    def to_seqs(values):
        return jnp.moveaxis(values.reshape(head_count, HEAD_DIM, seq_here, seq_length), 2, 0)

    def from_seqs(values):
        return jnp.moveaxis(values, 0, 2).reshape(head_width, group_rows)

    query_seqs = to_seqs(heads_all[0])
    key_seqs = to_seqs(heads_all[1])
    value_seqs = to_seqs(heads_all[2])
    attended_seqs, log_sums = lax.map(
        lambda seq_items: attend_forward(
            seq_items[0], seq_items[1], seq_items[2], seq_items[3], score_scale
        ),
        (query_seqs, key_seqs, value_seqs, segment_ids),
    )
    attended = from_seqs(attended_seqs).astype(jnp.bfloat16)
    gathered_heads = unit_gather(attended[None])
    attention_rows = (
        token_sums(
            jnp.einsum("kht,hd->td", gathered_heads, out_weight, preferred_element_type=jnp.float32)
        )
        + out_bias
    )
    hidden_one = rows_in + attention_rows
    normed_two, normal_two, inverse_two = norm_forward(hidden_one, norm2_gain, norm2_shift)
    gathered_two = token_gather(normed_two)
    up_part = jnp.einsum("td,df->ft", gathered_two, up_weight, preferred_element_type=jnp.float32)[
        None
    ]
    unit_width = up_part.shape[1] // lax.axis_size("row")
    up_slice = lax.dynamic_slice_in_dim(up_bias, row_index * unit_width, unit_width)
    pre_act = unit_sums(up_part)[0] + up_slice[:, None]
    gathered_act = unit_gather(gelu_value(pre_act).astype(jnp.bfloat16)[None])
    ffn_rows = (
        token_sums(
            jnp.einsum("kft,fd->td", gathered_act, down_weight, preferred_element_type=jnp.float32)
        )
        + down_bias
    )
    layer_out = jnp.where(active_here[:, None], hidden_one + ffn_rows, rows_in)
    grad_rows = out_grad.astype(jnp.float32) * keep_mask
    branch_grad = token_gather(grad_rows.astype(jnp.bfloat16))
    down_grad = jnp.einsum(
        "kft,td->fd", gathered_act, branch_grad, preferred_element_type=jnp.float32
    )
    down_bias_grad = jnp.sum(branch_grad, axis=0, dtype=jnp.float32)
    act_part = jnp.einsum(
        "td,fd->ft", branch_grad, down_weight, preferred_element_type=jnp.float32
    )[None]
    act_grad = unit_sums(act_part)[0]
    pre_grad = (act_grad * gelu_slope(pre_act)).astype(jnp.bfloat16)
    gathered_pre = unit_gather(pre_grad[None])
    up_grad = jnp.einsum(
        "td,kft->df", gathered_two, gathered_pre, preferred_element_type=jnp.float32
    )
    up_bias_grad = jnp.sum(gathered_pre[0], axis=1, dtype=jnp.float32)
    normed_grad_two = token_sums(
        jnp.einsum("kft,df->td", gathered_pre, up_weight, preferred_element_type=jnp.float32)
    )
    back_two, gain_two_grad, shift_two_grad = norm_backward(
        normed_grad_two, normal_two, inverse_two, norm2_gain
    )
    hidden_grad = grad_rows + back_two
    attention_grad = token_gather(hidden_grad.astype(jnp.bfloat16))
    out_weight_grad = jnp.einsum(
        "kht,td->hd", gathered_heads, attention_grad, preferred_element_type=jnp.float32
    )
    out_bias_grad = jnp.sum(attention_grad, axis=0, dtype=jnp.float32)
    head_grad = unit_sums(
        jnp.einsum("td,hd->ht", attention_grad, out_weight, preferred_element_type=jnp.float32)[
            None
        ]
    )[0].astype(jnp.bfloat16)
    query_grads, key_grads, value_grads = lax.map(
        lambda seq_items: attend_backward(
            seq_items[0],
            seq_items[1],
            seq_items[2],
            seq_items[3],
            seq_items[4],
            seq_items[5],
            score_scale,
        ),
        (query_seqs, key_seqs, value_seqs, to_seqs(head_grad), segment_ids, log_sums),
    )
    stacked_grad = jnp.stack(
        [from_seqs(query_grads), from_seqs(key_grads), from_seqs(value_grads)]
    ).astype(jnp.bfloat16)
    gathered_grad = unit_gather(stacked_grad)
    stacked_weight_grad = jnp.einsum(
        "td,kht->kdh", gathered_one, gathered_grad, preferred_element_type=jnp.float32
    )
    query_bias_grad = jnp.sum(gathered_grad[0], axis=1, dtype=jnp.float32)
    value_bias_grad = jnp.sum(gathered_grad[2], axis=1, dtype=jnp.float32)
    normed_grad_one = token_sums(
        jnp.einsum("kht,kdh->td", gathered_grad, stacked_weight, preferred_element_type=jnp.float32)
    )
    back_one, gain_one_grad, shift_one_grad = norm_backward(
        normed_grad_one, normal_one, inverse_one, norm1_gain
    )
    input_grad = out_grad.astype(jnp.float32) * (1.0 - keep_mask) + hidden_grad + back_one
    (
        stacked_weight_grad,
        query_bias_grad,
        value_bias_grad,
        out_weight_grad,
        out_bias_grad,
        down_grad,
        down_bias_grad,
        up_grad,
        up_bias_grad,
    ) = lax.psum(
        (
            stacked_weight_grad,
            query_bias_grad,
            value_bias_grad,
            out_weight_grad,
            out_bias_grad,
            down_grad,
            down_bias_grad,
            up_grad,
            up_bias_grad,
        ),
        "dp",
    )
    gain_one_grad, shift_one_grad, gain_two_grad, shift_two_grad = lax.psum(
        (gain_one_grad, shift_one_grad, gain_two_grad, shift_two_grad), ("dp", "col")
    )
    return (
        layer_out,
        input_grad,
        gain_one_grad,
        shift_one_grad,
        stacked_weight_grad[0],
        query_bias_grad,
        stacked_weight_grad[1],
        stacked_weight_grad[2],
        value_bias_grad,
        out_weight_grad,
        out_bias_grad,
        gain_two_grad,
        shift_two_grad,
        up_grad,
        up_bias_grad,
        down_grad,
        down_bias_grad,
    )


def solution(mesh):
    placed = (
        P(("dp", "col"), "row"),
        P(("dp", "col"), "row"),
        P("dp", None),
        P("dp", None),
        P("row"),
        P("row"),
        P("row", "col"),
        P("col"),
        P("row", "col"),
        P("row", "col"),
        P("col"),
        P("col", "row"),
        P("row"),
        P("row"),
        P("row"),
        P("row", "col"),
        P("col"),
        P("col", "row"),
        P("row"),
    )
    return jax.shard_map(
        body,
        mesh=mesh,
        in_specs=placed,
        out_specs=(
            P(("dp", "col"), "row"),
            P(("dp", "col"), "row"),
            P("row"),
            P("row"),
            P("row", "col"),
            P("col"),
            P("row", "col"),
            P("row", "col"),
            P("col"),
            P("col", "row"),
            P("row"),
            P("row"),
            P("row"),
            P("row", "col"),
            P("col"),
            P("col", "row"),
            P("row"),
        ),
        check_vma=False,
    )
```

profile of v0, /device:TPU:0, one launch (start us, length us, event | category | flops | bytes accessed | tf_op | source)
XLA Modules:
  0.0 2987.6 jit_solution(7598224099875930854)
XLA Ops:
  20.9 148.2 %all-gather.9.cloned.1.call-done = bf16[4096,1024]{1,0:T(8,128)(2,1)} async-done(((bf16[1024,1024]{1,0:T(8,128)(2,1)}), bf16[4096,1024]{1,0:T(8,128)(2,1)}) %all-gather.9.cloned.1.call-update) | async-done | bytes 8388624 | tf_op jit(solution)/shard_map/all_gather | solution.py:19
  169.1 20.5 fusion.106
  190.6 32.9 %reduce-scatter.9.cloned.1.call-done = f32[3,256,4096]{2,1,0:T(8,128)} async-done(((f32[3,512,4096]{2,1,0:T(8,128)}), f32[3,256,4096]{2,1,0:T(8,128)}) %reduce-scatter.9.cloned.1.call-update) | async-done | bytes 12582928 | tf_op jit(solution)/shard_map/reduce_scatter | solution.py:31
  223.5 9.2 add_convert_fusion
  232.7 5.5 fusion.138
  238.3 4.5 reshape_squeeze.11
  256.2 69.9 %while.26 = (s32[]{:T(128)}, bf16[4,4,64,1024]{3,2,1,0:T(8,128)(2,1)}, f32[4,4,1024]{2,1,0:T(4,128)}, bf16[4,4,64,1024]{3,2,1,0:T(8,128)(2,1)}, s32[4,1024]{1,0:...) while((s32[]{:T(128)}, ...), condition=%wide.region_14.15_spmd, body=%wide.region_9.14_spmd.sunk | while | flops 1128267776 | bytes 68366520 | solution.py:196
  262.1 4.6 fusion.197
  279.5 4.6 fusion.197
  296.9 4.6 fusion.197
  314.3 4.6 fusion.197
  326.1 5.3 copy.77
  335.9 14.9 all-gather.11.cloned.1.call-done
  350.8 10.8 fusion.126
  367.7 275.6 %reduce-scatter.11.cloned.1.call-done = f32[1024,1024]{1,0:T(8,128)} async-done(((f32[4096,1024]{1,0:T(8,128)}), f32[1024,1024]{1,0:T(8,128)}) %reduce-scatter.11.cloned.1.call-update) | async-done | bytes 4194320 | tf_op jit(solution)/shard_map/reduce_scatter | solution.py:23
  643.3 4.7 fusion.134
  651.1 4.6 add_convert_fusion.1
  655.8 139.9 %all-gather.17.cloned.1.call-done = bf16[4096,1024]{1,0:T(8,128)(2,1)} async-done(((bf16[1024,1024]{1,0:T(8,128)(2,1)}), bf16[4096,1024]{1,0:T(8,128)(2,1)}) %all-gather.17.cloned.1.call-update) | async-done | bytes 8388624 | tf_op jit(solution)/shard_map/all_gather | solution.py:19
  795.7 25.2 convolution_bitcast_fusion
  821.0 124.7 %all-gather.13.cloned.1.call-done = bf16[4096,1024]{1,0:T(8,128)(2,1)} async-done(((bf16[1024,1024]{1,0:T(8,128)(2,1)}), bf16[4096,1024]{1,0:T(8,128)(2,1)}) %all-gather.13.cloned.1.call-update) | async-done | bytes 8388624 | tf_op jit(solution)/shard_map/all_gather | solution.py:19
  945.7 29.0 convolution_bitcast_fusion.1
  975.5 16.0 reduce-scatter.17.cloned.1.call-done
  991.5 48.8 %reduce-scatter.13.cloned.1.call-done = f32[1,1024,4096]{1,2,0:T(8,128)} async-done(((f32[1,2048,4096]{1,2,0:T(8,128)}), f32[1,1024,4096]{1,2,0:T(8,128)}) %reduce-scatter.13.cloned.1.call-update) | async-done | bytes 16777232 | tf_op jit(solution)/shard_map/reduce_scatter | solution.py:31
  1040.3 21.0 fusion.95
  1062.0 30.8 %all-gather.19.cloned.1.call-done = bf16[1,2048,4096]{1,2,0:T(8,128)(2,1)} async-done(((bf16[1,1024,4096]{1,2,0:T(8,128)(2,1)}), bf16[1,2048,4096]{1,2,0:T(8,128)(2,1)}) %all-gather.19.cloned.1.call-update) | async-done | bytes 16777232 | tf_op jit(solution)/shard_map/all_gather | solution.py:27
  1092.8 24.6 fusion.98
  1117.5 8.7 all-gather.15.cloned.1.call-done
  1126.2 23.8 fusion.102
  1150.1 260.0 %reduce-scatter.19.cloned.1.call-done = f32[1024,1024]{1,0:T(8,128)} async-done(((f32[4096,1024]{1,0:T(8,128)}), f32[1024,1024]{1,0:T(8,128)}) %reduce-scatter.19.cloned.1.call-update) | async-done | bytes 4194320 | tf_op jit(solution)/shard_map/reduce_scatter | solution.py:23
  1410.2 5.0 multiply_reduce_fusion.2
  1417.6 275.8 %reduce-scatter.15.cloned.1.call-done = f32[1024,1024]{1,0:T(8,128)} async-done(((f32[4096,1024]{1,0:T(8,128)}), f32[1024,1024]{1,0:T(8,128)}) %reduce-scatter.15.cloned.1.call-update) | async-done | bytes 4194320 | tf_op jit(solution)/shard_map/reduce_scatter | solution.py:23
  1693.4 8.8 fusion.135
  1702.3 150.5 %all-gather.21.cloned.1.call-done = bf16[4096,1024]{1,0:T(8,128)(2,1)} async-done(((bf16[1024,1024]{1,0:T(8,128)(2,1)}), bf16[4096,1024]{1,0:T(8,128)(2,1)}) %all-gather.21.cloned.1.call-update) | async-done | bytes 8388624 | tf_op jit(solution)/shard_map/all_gather | solution.py:19
  1852.8 10.2 convolution_bitcast_fusion.3
  1863.1 15.1 reduce-scatter.21.cloned.1.call-done
  1893.5 136.2 %while.27 = (s32[]{:T(128)}, bf16[4,4,64,1024]{3,2,1,0:T(8,128)(2,1)}, bf16[4,4,64,1024]{3,2,1,0:T(8,128)(2,1)}, bf16[4,4,64,1024]{3,2,1,0:T(8,128)(2,1)}, bf16[...) while((s32[]{:T(128)}, ...), condition=%wide.region_32.33_spmd, body=%wide.region_29.32_spmd.sunk | while | flops 2752770048 | bytes 188412272 | solution.py:260
  1904.4 5.4 multiply_reduce_fusion.9
  1909.8 4.7 multiply_convert_fusion.5
  1938.3 5.4 multiply_reduce_fusion.9
  1943.7 4.7 multiply_convert_fusion.5
  1972.2 5.4 multiply_reduce_fusion.9
  1977.6 4.7 multiply_convert_fusion.5
  2006.1 5.4 multiply_reduce_fusion.9
  2011.5 4.7 multiply_convert_fusion.5
  2029.6 6.9 copy.93
  2036.6 7.1 reshape.329
  2043.7 4.6 copy.95
  2048.3 7.1 reshape.331
  2055.4 4.6 copy.94
  2060.1 7.1 reshape.330
  2067.2 5.5 pad_maximum_fusion
  2072.8 24.3 fusion.96
  2097.1 24.2 fusion.100
  2121.3 5.9 fusion.124
  2127.1 19.7 fusion.128
  2148.7 18.2 convolution_bitcast_fusion.2
  2166.9 5.0 convert_reduce_fusion.1
  2172.0 9.8 convert_reduce_fusion
  2184.2 18.3 all-reduce.1
  2202.6 393.5 %all-reduce.9.cloned.1.call-done = (f32[3,1024,512]{1,2,0:T(8,128)}, f32[512,1024]{1,0:T(8,128)}, f32[1024,2048]{1,0:T(8,128)}, f32[2048,1024]{1,0:T(8,128)}) async-done(((f32[3,1024,512]{1,2,0:T(8,128)}, f32[512,1024]{1,0:T(8,128)}, f32[1024,2048]{1,0:T(8,128)}, f32[2048,1024]{1,0:T(8,128)}), (f32[3,1024,512]{1,2,0:T(8,128)}, f32[512,1024]{1,0:T(8,128)}, f32[1024,2048]{1,0:T(8,128)}, ...) | async-done | bytes 25165840 | tf_op jit(solution)/shard_map/psum | solution.py:298
  2596.0 5.8 slice_bitcast_fusion
  2610.0 269.2 %reduce-scatter.23.cloned.1.call-done = f32[1024,1024]{1,0:T(8,128)} async-done(((f32[4096,1024]{1,0:T(8,128)}), f32[1024,1024]{1,0:T(8,128)}) %reduce-scatter.23.cloned.1.call-update) | async-done | bytes 4194320 | tf_op jit(solution)/shard_map/reduce_scatter | solution.py:23
  2885.5 76.9 %all-reduce = (f32[1024]{0:T(1024)}, f32[1024]{0:T(1024)}, f32[1024]{0:T(1024)}, f32[1024]{0:T(1024)}) all-reduce(f32[1024]{0:T(1024)S(1)} %get-tuple-element.189, f32[1024]{0:T(1024)S(1)} %get-tuple-element.194, f32[1024]{0:T(1024)S(1)} %copy-done.43, f32[1024]{0:T(1024)S(1)} %copy-done.44), channel_id=1, replica_groups=mesh['dp'=4,'row'=2,'col'=4] {'dp','col'}, use_global_device_ids=true, to_apply=%region_39.40 | all-reduce | flops 4096 | bytes 32768 | tf_op jit(solution)/shard_map/psum | solution.py:312
  2962.4 6.6 fusion.111
  (414 shorter events, 237.2 us)
Async XLA Ops:
  7.2 343.6 %copy-start = (bf16[512,1024]{1,0:T(8,128)(2,1)S(1)}, bf16[512,1024]{1,0:T(8,128)(2,1)}, u32[]{:S(2)}) copy-start(bf16[512,1024]{1,0:T(8,128)(2,1)} %param.34) | copy-start | bytes 3145732
  7.2 9.6 copy-start.20
  7.2 161.9 %all-gather.9.cloned.1.call-start = ((), (), s32[]{:S(2)}) async-start(), calls=%async_computation.8 | async-start | bytes 10485760 | tf_op jit(solution)/shard_map/all_gather | solution.py:19
  12.9 5.2 copy-start.21
  16.8 206.7 %reduce-scatter.9.cloned.1.call-start = ((), (), s32[]{:S(2)}) async-start(), calls=%async_computation.9 | async-start | bytes 37748736 | tf_op jit(solution)/shard_map/reduce_scatter | solution.py:31
  18.1 151.0 %copy-start.22 = (bf16[1024,512]{0,1:T(8,128)(2,1)S(1)}, bf16[1024,512]{0,1:T(8,128)(2,1)}, u32[]{:S(2)}) copy-start(bf16[1024,512]{0,1:T(8,128)(2,1)} %copy.71) | copy-start | bytes 3145732
  20.9 168.7 %copy-start.25 = (bf16[1024,512]{0,1:T(8,128)(2,1)}, bf16[1024,512]{0,1:T(8,128)(2,1)S(1)}, u32[]{:S(2)}) copy-start(bf16[1024,512]{0,1:T(8,128)(2,1)S(1)} %copy.73) | copy-start | bytes 3145732
  189.6 161.2 %all-gather.11.cloned.1.call-start = ((), (), s32[]{:S(2)}) async-start(), calls=%async_computation.10 | async-start | bytes 6291456 | tf_op jit(solution)/shard_map/all_gather | solution.py:27
  262.1 4.6 copy-start.8
  326.1 9.7 copy-start.2
  335.8 307.4 %reduce-scatter.11.cloned.1.call-start = ((), (), s32[]{:S(2)}) async-start(), calls=%async_computation.11 | async-start | bytes 20971520 | tf_op jit(solution)/shard_map/reduce_scatter | solution.py:23
  361.6 281.6 %copy-start.4 = (bf16[1024,1024]{1,0:T(8,128)(2,1)S(1)}, bf16[1024,1024]{1,0:T(8,128)(2,1)}, u32[]{:S(2)}) copy-start(bf16[1024,1024]{1,0:T(8,128)(2,1)} %param.23) | copy-start | bytes 6291460
  361.7 281.6 %copy-start.47 = (f32[1024]{0:T(1024)S(1)}, f32[1024]{0:T(1024)}, u32[]{:S(2)}) copy-start(f32[1024]{0:T(1024)} %param.35) | copy-start | bytes 12292
  361.7 434.1 %all-gather.17.cloned.1.call-start = ((), (), s32[]{:S(2)}) async-start(), calls=%async_computation.16 | async-start | bytes 10485760 | tf_op jit(solution)/shard_map/all_gather | solution.py:19
  367.6 283.5 %copy-start.37 = (f32[1024]{0:T(1024)S(1)}, f32[1024]{0:T(1024)}, u32[]{:S(2)}) copy-start(f32[1024]{0:T(1024)} %param.36) | copy-start | bytes 12292
  367.6 283.5 %copy-start.48 = (f32[1024]{0:T(1024)S(1)}, f32[1024]{0:T(1024)}, u32[]{:S(2)}) copy-start(f32[1024]{0:T(1024)} %param.37) | copy-start | bytes 12292
  367.6 578.1 %all-gather.13.cloned.1.call-start = ((), (), s32[]{:S(2)}) async-start(), calls=%async_computation.12 | async-start | bytes 10485760 | tf_op jit(solution)/shard_map/all_gather | solution.py:19
  655.7 335.8 %reduce-scatter.17.cloned.1.call-start = ((), (), s32[]{:S(2)}) async-start(), calls=%async_computation.17 | async-start | bytes 50331648 | tf_op jit(solution)/shard_map/reduce_scatter | solution.py:31
  821.0 219.3 %reduce-scatter.13.cloned.1.call-start = ((), (), s32[]{:S(2)}) async-start(), calls=%async_computation.13 | async-start | bytes 50331648 | tf_op jit(solution)/shard_map/reduce_scatter | solution.py:31
  974.8 118.0 %all-gather.19.cloned.1.call-start = ((), (), s32[]{:S(2)}) async-start(), calls=%async_computation.18 | async-start | bytes 25165824 | tf_op jit(solution)/shard_map/all_gather | solution.py:27
  1061.4 64.8 %all-gather.15.cloned.1.call-start = ((), (), s32[]{:S(2)}) async-start(), calls=%async_computation.14 | async-start | bytes 25165824 | tf_op jit(solution)/shard_map/all_gather | solution.py:27
  1062.0 348.2 %reduce-scatter.19.cloned.1.call-start = ((), (), s32[]{:S(2)}) async-start(), calls=%async_computation.19 | async-start | bytes 20971520 | tf_op jit(solution)/shard_map/reduce_scatter | solution.py:23
  1117.4 576.0 %reduce-scatter.15.cloned.1.call-start = ((), (), s32[]{:S(2)}) async-start(), calls=%async_computation.15 | async-start | bytes 20971520 | tf_op jit(solution)/shard_map/reduce_scatter | solution.py:23
  1150.0 260.2 %copy-start.30 = (f32[1024]{0:T(1024)S(1)}, f32[1024]{0:T(1024)}, u32[]{:S(2)}) copy-start(f32[1024]{0:T(1024)} %copy-done.29) | copy-start | bytes 12292
  1150.0 260.2 %copy-start.32 = (f32[1024]{0:T(1024)S(1)}, f32[1024]{0:T(1024)}, u32[]{:S(2)}) copy-start(f32[1024]{0:T(1024)} %copy-done.31) | copy-start | bytes 12292
  1150.0 260.2 %copy-start.38 = (f32[1024]{0:T(1024)S(1)}, f32[1024]{0:T(1024)}, u32[]{:S(2)}) copy-start(f32[1024]{0:T(1024)} %param.36) | copy-start | bytes 12292
  1150.0 543.4 %copy-start.5 = (bf16[1024,1024]{1,0:T(8,128)(2,1)S(1)}, bf16[1024,1024]{1,0:T(8,128)(2,1)}, u32[]{:S(2)}) copy-start(bf16[1024,1024]{1,0:T(8,128)(2,1)} %param.23) | copy-start | bytes 6291460
  1150.0 543.4 %copy-start.40 = (f32[1024]{0:T(1024)S(1)}, f32[1024]{0:T(1024)}, u32[]{:S(2)}) copy-start(f32[1024]{0:T(1024)} %copy-done.39) | copy-start | bytes 12292
  1150.0 543.4 %copy-start.46 = (pred[1024]{0:T(1024)(128)(4,1)S(1)}, pred[1024]{0:T(1024)(128)(4,1)}, u32[]{:S(2)}) copy-start(pred[1024]{0:T(1024)(128)(4,1)} %copy-done.45) | copy-start | bytes 3076
  1150.1 543.4 %copy-start.49 = (f32[1024]{0:T(1024)S(1)}, f32[1024]{0:T(1024)}, u32[]{:S(2)}) copy-start(f32[1024]{0:T(1024)} %param.41) | copy-start | bytes 12292
  1150.1 702.7 %all-gather.21.cloned.1.call-start = ((), (), s32[]{:S(2)}) async-start(), calls=%async_computation.20 | async-start | bytes 10485760 | tf_op jit(solution)/shard_map/all_gather | solution.py:19
  1702.3 175.9 %reduce-scatter.21.cloned.1.call-start = ((), (), s32[]{:S(2)}) async-start(), calls=%async_computation.21 | async-start | bytes 12582912 | tf_op jit(solution)/shard_map/reduce_scatter | solution.py:31
  1863.0 264.1 %all-gather.23.cloned.1.call-start = ((), (), s32[]{:S(2)}) async-start(), calls=%async_computation.22 | async-start | bytes 18874368 | tf_op jit(solution)/shard_map/all_gather | solution.py:27
  1888.7 4.7 copy-start.3
  1888.7 4.8 copy-start.28
  1904.4 5.4 copy-start.11
  1938.3 5.4 copy-start.11
  1972.2 5.4 copy-start.11
  2006.1 5.4 copy-start.11
  2036.6 7.1 copy-start.12
  2048.3 7.1 copy-start.15
  2060.1 7.1 copy-start.16
  2072.8 523.3 %all-reduce.9.cloned.1.call-start = ((), (), s32[]{:S(2)}) async-start(), calls=%async_computation.24 | async-start | bytes 50331648 | tf_op jit(solution)/shard_map/psum | solution.py:298
  2072.8 48.5 %slice-start = ((s8[8388608]{0:T(1024)(128)(4,1)}), s8[4194304]{0:T(1024)(128)(4,1)S(1)}, s32[]{:S(2)}) async-start(s8[8388608]{0:T(1024)(128)(4,1)} %bitcast.226), calls=%async_computation.25 | async-start | bytes 8388608
  2097.1 24.2 slice-start.1
  2097.1 24.2 copy-start.54
  2146.8 732.5 %reduce-scatter.23.cloned.1.call-start = ((), (), s32[]{:S(2)}) async-start(), calls=%async_computation.23 | async-start | bytes 20971520 | tf_op jit(solution)/shard_map/reduce_scatter | solution.py:23
  2166.9 14.8 slice-start.2
  2166.9 16.1 slice-start.8
  2171.9 9.8 slice-start.3
  2171.9 11.1 slice-start.9
  2171.9 11.1 slice-start.10
  2603.7 275.6 %copy-start.6 = (bf16[1024,1024]{1,0:T(8,128)(2,1)S(1)}, bf16[1024,1024]{1,0:T(8,128)(2,1)}, u32[]{:S(2)}) copy-start(bf16[1024,1024]{1,0:T(8,128)(2,1)} %param.23) | copy-start | bytes 6291460
  2603.7 275.6 %copy-start.34 = (f32[1024]{0:T(1024)S(1)}, f32[1024]{0:T(1024)}, u32[]{:S(2)}) copy-start(f32[1024]{0:T(1024)} %copy-done.33) | copy-start | bytes 12292
  2603.7 275.6 %copy-start.36 = (f32[1024]{0:T(1024)S(1)}, f32[1024]{0:T(1024)}, u32[]{:S(2)}) copy-start(f32[1024]{0:T(1024)} %copy-done.35) | copy-start | bytes 12292
  2603.7 275.6 %copy-start.41 = (f32[1024]{0:T(1024)S(1)}, f32[1024]{0:T(1024)}, u32[]{:S(2)}) copy-start(f32[1024]{0:T(1024)} %param.27) | copy-start | bytes 12292
  2610.0 275.5 %copy-start.43 = (f32[1024]{0:T(1024)S(1)}, f32[1024]{0:T(1024)}, u32[]{:S(2)}) copy-start(f32[1024]{0:T(1024)} %get-tuple-element.187) | copy-start | bytes 12292
  2610.0 275.5 %copy-start.44 = (f32[1024]{0:T(1024)S(1)}, f32[1024]{0:T(1024)}, u32[]{:S(2)}) copy-start(f32[1024]{0:T(1024)} %get-tuple-element.193) | copy-start | bytes 12292
  2610.0 352.4 %copy-start.42 = (f32[1024]{0:T(1024)S(1)}, f32[1024]{0:T(1024)}, u32[]{:S(2)}) copy-start(f32[1024]{0:T(1024)} %get-tuple-element.256) | copy-start | bytes 12292
  2962.4 7.9 slice-start.6
  2962.4 6.6 copy-start.19
  2962.4 9.4 slice-start.7
  2969.0 7.1 slice-start.4
  2971.8 5.6 slice-start.5
  (40 other events, 73.3 us)
Sparse Core Ops, SparseCore 0:
  16.9 152.2 all-gather.8
  189.7 33.6 reduce-scatter.8
  336.0 14.8 all-gather.10
  361.8 281.4 reduce-scatter.10
  645.4 150.3 all-gather.16
  797.8 147.8 all-gather.12
  948.1 43.3 reduce-scatter.16
  993.9 46.3 reduce-scatter.12
  1061.5 31.2 all-gather.18
  1094.9 31.2 all-gather.14
  1128.6 281.4 reduce-scatter.18
  1412.4 281.0 reduce-scatter.14
  1702.4 150.3 all-gather.20
  1863.1 15.0 reduce-scatter.20
  2072.9 26.0 all-gather.22
  2146.9 449.0 all-reduce.8
  2598.2 280.9 reduce-scatter.22
where the time goes:
time: 3000 us; the launch traced here: 2990 us
  waiting for transfers between devices  2210 us (74%)
  matrix products  357 us (12%)
  other arithmetic  164 us (5%)
  local copies, waits for them, and re-layouts  138 us (5%)
  blocking collectives  105 us (4%)
    reduce_scatter x4, waiting for transfers between devices, token_sums(): lax.psum_scatter(partial_rows, 'col', scatter_dimension=0, tiled=True)  1080 us
    all_gather x4, waiting for transfers between devices, token_gather(): return lax.all_gather(values, 'col', axis=0, tiled=True)  563 us
    psum x1, waiting for transfers between devices, body(): lax.psum((stacked_weight_grad, query_bias_grad, value_bias_grad, out_weig...  393 us
    reduce_scatter x4, waiting for transfers between devices, unit_sums(): lax.psum_scatter(partial_units, 'row', scatter_dimension=1, tiled=True)  113 us
    psum x1, blocking collectives, body(): lax.psum((gain_one_grad, shift_one_grad, gain_two_grad, shift_two_grad),...  76.9 us
  transfers between devices with their start and end apart: 17, of which 16 were waited for; matrix products, arithmetic and copies ran while one was open for 8% of the time, Pallas kernels for 0%

commit v1 on v0

--- a/solution.py
+++ b/solution.py
@@ -139,7 +139,7 @@
     return (jnp.concatenate(query_grads, axis=2), key_grad, value_grad)
 
 
-def body(
+def body_general(
     tokens_in,
     out_grad,
     segment_ids,
@@ -333,6 +333,384 @@
     )
 
 
+def swap(values):
+    return lax.ppermute(values, "row", [(0, 1), (1, 0)])
+
+
+def step_x(values):
+    return lax.ppermute(values, "dp", [(0, 1), (1, 0), (2, 3), (3, 2)])
+
+
+def step_y(values):
+    return lax.ppermute(values, "dp", [(0, 2), (2, 0), (1, 3), (3, 1)])
+
+
+def step_up(values):
+    count = lax.axis_size("col")
+    return lax.ppermute(values, "col", [(i, (i + 1) % count) for i in range(count)])
+
+
+def step_down(values):
+    count = lax.axis_size("col")
+    return lax.ppermute(values, "col", [(i, (i - 1) % count) for i in range(count)])
+
+
+def plane_gather(values):
+    half = values.shape[0] // 2
+    from_x = step_x(values)
+    from_y = step_y(values)
+    far_one = step_y(from_x[:half])
+    far_two = step_x(from_y[half:])
+    return (values, from_x, from_y, jnp.concatenate([far_one, far_two], axis=0))
+
+
+def plane_sum(here, to_x, to_y, to_far):
+    half = here.shape[0] // 2
+    f32 = jnp.float32
+    via_x = step_x(to_far[:half])
+    via_y = step_y(to_far[half:])
+    x_top = step_x(to_x[:half])
+    y_bottom = step_y(to_y[half:])
+    x_bottom = step_x((to_x[half:].astype(f32) + via_y.astype(f32)).astype(jnp.bfloat16))
+    y_top = step_y((to_y[:half].astype(f32) + via_x.astype(f32)).astype(jnp.bfloat16))
+    top = here[:half].astype(f32) + x_top.astype(f32) + y_top.astype(f32)
+    bottom = here[half:].astype(f32) + x_bottom.astype(f32) + y_bottom.astype(f32)
+    return jnp.concatenate([top, bottom], axis=0)
+
+
+def ring_gather(values):
+    held = [values]
+    for _ in range(lax.axis_size("col") - 1):
+        held.append(jax.tree.map(step_up, held[-1]))
+    return held
+
+
+def ring_sum(blocks):
+    total = blocks[-1]
+    for block in blocks[-2::-1]:
+        arrived = jax.tree.map(step_down, total)
+        total = jax.tree.map(
+            lambda a, b: (a.astype(jnp.float32) + b.astype(jnp.float32)).astype(jnp.bfloat16),
+            arrived,
+            block,
+        )
+    return total
+
+
+def butterfly_sum(values):
+    count = lax.axis_size("col")
+    values = values + step_x(values)
+    values = values + step_y(values)
+    step = 1
+    while step < count:
+        values = values + lax.ppermute(values, "col", [(i, i ^ step) for i in range(count)])
+        step *= 2
+    return values
+
+
+def picked(stacked, index):
+    return lax.dynamic_index_in_dim(stacked, index, 0, keepdims=False)
+
+
+def reordered(stacked, index, count):
+    return jnp.stack([picked(stacked, jnp.bitwise_xor(index, i)) for i in range(count)])
+
+
+def row_norm(values):
+    average = jnp.mean(values, axis=1, keepdims=True)
+    centered = values - average
+    inverse = lax.rsqrt(jnp.mean(centered * centered, axis=1, keepdims=True) + norm_eps)
+    return (average, inverse)
+
+
+def mm(left, right, dims, dtype=jnp.float32):
+    return lax.dot_general(
+        left, right, (dims, ((), ())), preferred_element_type=jnp.float32
+    ).astype(dtype)
+
+
+def body_local(
+    tokens_in,
+    out_grad,
+    segment_ids,
+    active_lengths,
+    norm1_gain,
+    norm1_shift,
+    query_weight,
+    query_bias,
+    key_weight,
+    value_weight,
+    value_bias,
+    out_weight,
+    out_bias,
+    norm2_gain,
+    norm2_shift,
+    up_weight,
+    up_bias,
+    down_weight,
+    down_bias,
+):
+    f32, bf16 = jnp.float32, jnp.bfloat16
+    rows, width = tokens_in.shape
+    ring = lax.axis_size("col")
+    row_i = lax.axis_index("row")
+    plane_i = lax.axis_index("dp")
+    col_i = lax.axis_index("col")
+    own_units = query_weight.shape[1] // 2
+    head_units = own_units // 4
+    quarter = up_weight.shape[1] // 4
+    unit_width = quarter // 2
+    score_scale = HEAD_DIM ** (-0.5)
+
+    active_all = active_rows(segment_ids, active_lengths)
+    active_here = lax.dynamic_slice_in_dim(active_all, col_i * rows, rows)
+    keep_mask = active_here.astype(f32)[:, None]
+    segment_row = picked(segment_ids, col_i)
+
+    vectors = jnp.stack([norm1_gain, norm1_shift, norm2_gain, norm2_shift, out_bias])
+    vectors = jnp.concatenate([vectors, swap(vectors)], axis=1)
+    gain_one, shift_one, gain_two, shift_two, attention_bias = [vectors[i] for i in range(5)]
+    tokens = jnp.concatenate([tokens_in, swap(tokens_in)], axis=1).astype(f32)
+
+    def column_part(weight, which, offset, size):
+        return lax.dynamic_slice_in_dim(weight, offset + which * size, size, axis=1)
+
+    def row_part(weight, which, offset, size):
+        return lax.dynamic_slice_in_dim(weight, offset + which * size, size, axis=0)
+
+    projections = (query_weight, key_weight, value_weight)
+    mine = [column_part(w, row_i, 0, own_units).T for w in projections]
+    mine.append(row_part(out_weight, row_i, 0, own_units))
+    other = [column_part(w, 1 - row_i, 0, own_units).T for w in projections]
+    other.append(row_part(out_weight, 1 - row_i, 0, own_units))
+    head_weights = jnp.concatenate([jnp.stack(mine), swap(jnp.stack(other))], axis=2)
+    head_weights = head_weights.reshape(4, 4, head_units, 2 * width).transpose(1, 0, 2, 3)
+    head_weights = reordered(head_weights, plane_i, 4)
+    groups = [head_weights]
+    for piece in ring_gather(head_weights[0])[1:]:
+        groups.append(jnp.stack(plane_gather(piece)))
+
+    ff_offset = plane_i * quarter
+    ff_mine = (
+        column_part(up_weight, row_i, ff_offset, unit_width),
+        column_part(up_weight, 1 - row_i, ff_offset, unit_width),
+        row_part(down_weight, row_i, ff_offset, unit_width),
+        row_part(down_weight, 1 - row_i, ff_offset, unit_width),
+    )
+    ff_all = ring_gather(ff_mine)
+    up_own = jnp.concatenate([p[0] for p in ff_all], axis=1)
+    up_sib = jnp.concatenate([p[1] for p in ff_all], axis=1)
+    down_own = jnp.concatenate([p[2] for p in ff_all], axis=0)
+    down_sib = jnp.concatenate([p[3] for p in ff_all], axis=0)
+    up_full = jnp.concatenate([up_own, swap(up_sib)], axis=0)
+    down_full = jnp.concatenate([down_own, swap(down_sib)], axis=1)
+    up_half = jnp.concatenate([up_own, up_sib], axis=1)
+    down_half = jnp.concatenate([down_own, down_sib], axis=0)
+
+    query_heads = reordered(
+        lax.dynamic_slice_in_dim(query_bias, row_i * own_units, own_units).reshape(4, head_units),
+        plane_i,
+        4,
+    )
+    value_heads = reordered(
+        lax.dynamic_slice_in_dim(value_bias, row_i * own_units, own_units).reshape(4, head_units),
+        plane_i,
+        4,
+    )
+    up_part = lax.dynamic_slice_in_dim(up_bias, ff_offset + row_i * unit_width, unit_width)
+    small = ring_gather(jnp.concatenate([query_heads.reshape(-1), value_heads.reshape(-1), up_part]))
+    up_biases = jnp.concatenate([s[2 * own_units :] for s in small])
+
+    average_one, inverse_one = row_norm(tokens)
+    normal_one = (tokens - average_one) * inverse_one
+    normed_one = (normal_one * gain_one + shift_one).astype(bf16)
+    heads, attended, log_sums = [], [], []
+    for weights, biases in zip(groups, small):
+        projected = jnp.einsum("jmud,td->jmut", weights[:, :3], normed_one, preferred_element_type=f32)
+        bias_q = biases[:own_units].reshape(4, head_units, 1)
+        bias_v = biases[own_units : 2 * own_units].reshape(4, head_units, 1)
+        query = (projected[:, 0] + bias_q).astype(bf16)
+        key = projected[:, 1].astype(bf16)
+        value = (projected[:, 2] + bias_v).astype(bf16)
+        result, log_sum = attend_forward(query, key, value, segment_row, score_scale)
+        heads.append((query, key, value))
+        log_sums.append(log_sum)
+        attended.append(result.astype(bf16).reshape(own_units, rows))
+    attended_both = jnp.concatenate(attended + [swap(a) for a in attended], axis=0)
+    out_own = [g[:, 3].reshape(own_units, 2 * width) for g in groups]
+    out_sib = [swap(w) for w in out_own]
+    out_sib = [jnp.concatenate([w[:, width:], w[:, :width]], axis=1) for w in out_sib]
+    out_both = jnp.concatenate(out_own + out_sib, axis=0)
+    hidden_one = tokens + mm(attended_both, out_both, ((0,), (0,))) + attention_bias
+
+    average_two, inverse_two = row_norm(hidden_one)
+    normal_two = (hidden_one - average_two) * inverse_two
+    normed_two = (normal_two * gain_two + shift_two).astype(bf16)
+    normed_own = jnp.concatenate(plane_gather(normed_two[:, :width]), axis=0)
+    normed_sib = jnp.concatenate([normed_two[:, width:], swap(normed_own[rows:])], axis=0)
+    normed_all = jnp.concatenate([normed_own, normed_sib], axis=1)
+    branch_mine = (out_grad.astype(f32) * keep_mask).astype(bf16)
+    branch_own = jnp.concatenate(plane_gather(branch_mine), axis=0)
+    branch_sib = swap(branch_own)
+    branch_all = jnp.concatenate([branch_own, branch_sib], axis=1)
+    pre_act = mm(normed_all, up_full, ((1,), (0,))) + up_biases
+    activated = gelu_value(pre_act).astype(bf16)
+    pre_grad = (mm(branch_all, down_full, ((1,), (1,))) * gelu_slope(pre_act)).astype(bf16)
+    pre_grad_chip = jnp.concatenate([pre_grad, swap(pre_grad)], axis=1)
+    activated_chip = jnp.concatenate([activated, swap(activated)], axis=1)
+    grad_parts = mm(pre_grad_chip, up_half, ((1,), (1,)), bf16).reshape(4, rows, width)
+    normed_grad_two = plane_sum(*[grad_parts[i] for i in range(4)])
+    down_parts = mm(activated_chip, down_half, ((1,), (0,)), bf16).reshape(4, rows, width)
+    ffn_rows = plane_sum(*[down_parts[i] for i in range(4)]) + down_bias
+    layer_out = jnp.where(active_here[:, None], hidden_one[:, :width] + ffn_rows, tokens[:, :width])
+    up_grad = mm(normed_own, pre_grad_chip, ((0,), (0,)), bf16)
+    down_grad = mm(activated_chip, branch_own, ((0,), (0,)), bf16)
+
+    units = ring * unit_width
+    ff_blocks = []
+    for k in range(ring):
+        span_own = slice(k * unit_width, (k + 1) * unit_width)
+        span_sib = slice(units + k * unit_width, units + (k + 1) * unit_width)
+        ff_blocks.append(
+            (up_grad[:, span_own], up_grad[:, span_sib], down_grad[span_own], down_grad[span_sib])
+        )
+    ff_sums = ring_sum(ff_blocks)
+
+    def placed_blocks(own, sib):
+        own_all = jnp.stack(plane_gather(own))
+        sib_all = jnp.stack(plane_gather(sib))
+        both = jnp.stack([own_all, sib_all])
+        both = reordered(both, row_i, 2)
+        return [
+            picked(both[r], jnp.bitwise_xor(plane_i, q)).astype(f32)
+            for q in range(4)
+            for r in range(2)
+        ]
+
+    up_weight_grad = jnp.concatenate(placed_blocks(ff_sums[0], ff_sums[1]), axis=1)
+    down_weight_grad = jnp.concatenate(placed_blocks(ff_sums[2], ff_sums[3]), axis=0)
+
+    normed_grad_sib = swap(normed_grad_two.astype(bf16)).astype(f32)
+    normed_grad_full = jnp.concatenate([normed_grad_two, normed_grad_sib], axis=1)
+    grad_rows = jnp.concatenate([branch_own[:rows], branch_sib[:rows]], axis=1).astype(f32)
+    scaled = normed_grad_full * gain_two
+    back_two = inverse_two * (
+        scaled
+        - jnp.mean(scaled, axis=1, keepdims=True)
+        - normal_two * jnp.mean(scaled * normal_two, axis=1, keepdims=True)
+    )
+    hidden_grad = grad_rows + back_two
+    attention_grad = hidden_grad.astype(bf16)
+    gain_two_grad = jnp.sum(normed_grad_two * normal_two[:, :width], axis=0)
+    shift_two_grad = jnp.sum(normed_grad_two, axis=0)
+
+    reduced = [None] * ring
+    normed_grad_one = None
+    bias_rows = [None] * ring
+    for k in range(ring - 1, -1, -1):
+        weights = groups[k]
+        query, key, value = heads[k]
+        head_grad = mm(out_own[k], attention_grad, ((1,), (1,)), bf16).reshape(query.shape)
+        grads = attend_backward(
+            query, key, value, head_grad, segment_row, log_sums[k], score_scale
+        )
+        stacked = jnp.stack(grads, axis=1).astype(bf16)
+        part = jnp.einsum("jmut,jmud->td", stacked, weights[:, :3], preferred_element_type=f32)
+        normed_grad_one = part if normed_grad_one is None else normed_grad_one + part
+        weight_grads = jnp.einsum("jmut,td->jmud", stacked, normed_one, preferred_element_type=f32)
+        out_grads = mm(attended[k], attention_grad, ((1,), (0,)))
+        out_grads = out_grads.reshape(4, 1, head_units, 2 * width)
+        blocks = jnp.concatenate([weight_grads, out_grads], axis=1).astype(bf16)
+        reduced[k] = plane_sum(*[blocks[i] for i in range(4)]).astype(bf16)
+        bias_rows[k] = jnp.stack(
+            [
+                jnp.sum(stacked[:, 0].astype(f32), axis=2),
+                jnp.sum(stacked[:, 2].astype(f32), axis=2),
+            ]
+        )
+    head_sum = ring_sum(reduced)
+    head_other = swap(head_sum[:, :, width:])
+    head_both = jnp.stack([head_sum[:, :, :width], head_other])
+    head_all = jnp.stack(plane_gather(head_both.transpose(1, 0, 2, 3)))
+    head_all = reordered(head_all, plane_i, 4).transpose(1, 2, 0, 3, 4)
+    head_all = jnp.stack([reordered(head_all[m], row_i, 2) for m in range(4)])
+    head_all = head_all.reshape(4, 2 * own_units, width)
+    query_weight_grad = head_all[0].T.astype(f32)
+    key_weight_grad = head_all[1].T.astype(f32)
+    value_weight_grad = head_all[2].T.astype(f32)
+    out_weight_grad = head_all[3].astype(f32)
+
+    normed_grad_one = normed_grad_one[:, :width] + swap(
+        normed_grad_one[:, width:].astype(bf16)
+    ).astype(f32)
+    normal_own = normal_one[:, :width]
+    scaled = normed_grad_one * gain_one[:width]
+    sums = jnp.stack([jnp.sum(scaled, axis=1), jnp.sum(scaled * normal_own, axis=1)])
+    sums = (sums + swap(sums)) / (2 * width)
+    back_one = inverse_one * (scaled - sums[0][:, None] - normal_own * sums[1][:, None])
+    gain_one_grad = jnp.sum(normed_grad_one * normal_own, axis=0)
+    shift_one_grad = jnp.sum(normed_grad_one, axis=0)
+    input_grad = out_grad.astype(f32) * (1.0 - keep_mask) + hidden_grad[:, :width] + back_one
+
+    def by_column(relative):
+        index = jnp.mod(col_i - jnp.arange(ring), ring)
+        return jnp.take(jnp.stack(relative), index, axis=0)
+
+    row_hot = (jnp.arange(2) == row_i).astype(f32)
+    plane_hot = (jnp.arange(4) == plane_i).astype(f32)
+    plane_order = jnp.bitwise_xor(plane_i, jnp.arange(4))
+    head_bias = jnp.take(by_column(bias_rows), plane_order, axis=2)
+    head_bias = head_bias.transpose(0, 1, 2, 3)[:, :, None] * row_hot[None, None, :, None, None]
+    up_bias_part = jnp.sum(pre_grad.astype(f32), axis=0).reshape(ring, unit_width)
+    up_bias_part = by_column([up_bias_part[k] for k in range(ring)])
+    up_bias_part = (
+        up_bias_part[:, None, None, :] * plane_hot[None, :, None, None] * row_hot[None, None, :, None]
+    )
+    bias_vector = jnp.concatenate([head_bias.reshape(ring, -1), up_bias_part.reshape(ring, -1)], axis=1)
+    bias_vector = bias_vector + swap(bias_vector)
+    out_bias_part = jnp.sum(attention_grad[:, :width].astype(f32), axis=0)
+    down_bias_part = jnp.sum(branch_mine.astype(f32), axis=0)
+    own_vector = jnp.concatenate(
+        [gain_one_grad, shift_one_grad, gain_two_grad, shift_two_grad, out_bias_part, down_bias_part]
+    )
+    summed = butterfly_sum(jnp.concatenate([bias_vector.reshape(-1), own_vector]))
+    bias_size = bias_vector.size
+    bias_here = picked(summed[:bias_size].reshape(ring, -1), col_i)
+    own_here = summed[bias_size:].reshape(6, width)
+    head_size = 2 * own_units
+    return (
+        layer_out,
+        input_grad,
+        own_here[0],
+        own_here[1],
+        query_weight_grad,
+        bias_here[:head_size],
+        key_weight_grad,
+        value_weight_grad,
+        bias_here[head_size : 2 * head_size],
+        out_weight_grad,
+        own_here[4],
+        own_here[2],
+        own_here[3],
+        up_weight_grad,
+        bias_here[2 * head_size :],
+        down_weight_grad,
+        own_here[5],
+    )
+
+
+def body(tokens_in, out_grad, segment_ids, *rest):
+    ring = lax.axis_size("col")
+    local = (
+        lax.axis_size("dp") == 4
+        and lax.axis_size("row") == 2
+        and ring & (ring - 1) == 0
+        and tokens_in.shape[0] == segment_ids.shape[1]
+    )
+    chosen = body_local if local else body_general
+    return chosen(tokens_in, out_grad, segment_ids, *rest)
+
+
 def solution(mesh):
     placed = (
         P(("dp", "col"), "row"),

time: 3000 us -> 1510 us (0.50)
  waiting for transfers between devices: 2210 us -> 583 us
  starting transfers between devices: 0.92 us -> 130 us
  blocking collectives: 105 us -> 0 us
  other arithmetic: 164 us -> 239 us
  matrix products: 357 us -> 399 us
    reduce_scatter x8 -> x0, waiting for transfers between devices: 1190 us -> none  [the longest x4 1080 us: token_sums(): lax.psum_scatter(partial_rows, 'col', scatter_dimension=0, tiled=True)]
    all_gather x8 -> x0, waiting for transfers between devices: 618 us -> none  [the longest x4 563 us: token_gather(): return lax.all_gather(values, 'col', axis=0, tiled=True)]
    ppermute x0 -> x135, waiting for transfers between devices: none -> 583 us  [the longest x39 244 us: step_y(): return lax.ppermute(values, 'dp', [(0, 2), (2, 0), (1, 3), (3, 1)])]
    psum x1 -> x0, waiting for transfers between devices: 393 us -> none  [body(): lax.psum((stacked_weight_grad, query_bias_grad, value_bias_grad, out_weig...]
    ppermute x0 -> x135, starting transfers between devices: none -> 130 us  [the longest x39 47.9 us: step_y(): return lax.ppermute(values, 'dp', [(0, 2), (2, 0), (1, 3), (3, 1)])]
    psum x6 -> x0, blocking collectives: 105 us -> none  [the longest x1 76.9 us: body(): lax.psum((gain_one_grad, shift_one_grad, gain_two_grad, shift_two_grad),...]
    unnamed x128 -> x601, local copies, waits for them, and re-layouts: 30.7 us -> 87.3 us
    another operation x15 -> x3, local copies, waits for them, and re-layouts: 56.4 us -> 2.37 us  [the longest x1 2.24 us: body_local(): jnp.stack(mine)]
  transfers between devices with their start and end apart: 17 -> 135, of which waited for: 16 -> 65; matrix products, arithmetic and copies ran while one was open for 8% -> 31% of each run, Pallas kernels for 0% -> 0%
where the time goes in v1:
time: 1510 us; the launch traced here: 1500 us
  waiting for transfers between devices  583 us (39%)
  matrix products  399 us (26%)
  other arithmetic  239 us (16%)
  local copies, waits for them, and re-layouts  144 us (10%)
  starting transfers between devices  130 us (9%)
    ppermute x39, waiting for transfers between devices, step_y(): return lax.ppermute(values, 'dp', [(0, 2), (2, 0), (1, 3), (3, 1)])  244 us
    dot_general x15, matrix products, mm(): lax.dot_general(left, right, (dims, ((), ())), preferred_element_type=jnp...  191 us
    ppermute x39, waiting for transfers between devices, step_x(): return lax.ppermute(values, 'dp', [(0, 1), (1, 0), (2, 3), (3, 2)])  158 us
    ppermute x18, waiting for transfers between devices, step_up(): lax.ppermute(values, 'col', [(i, (i + 1) % count) for i in range(count)])  115 us
    unnamed x601, local copies, waits for them, and re-layouts  87.3 us
    ppermute x15, waiting for transfers between devices, step_down(): lax.ppermute(values, 'col', [(i, (i - 1) % count) for i in range(count)])  62.4 us
    convert_element_type x8, other arithmetic, attend_backward(): score_grad = (probs * (prob_grad - row_dot)).astype(jnp.bfloat16)  50.5 us
    ppermute x39, starting transfers between devices, step_y(): return lax.ppermute(values, 'dp', [(0, 2), (2, 0), (1, 3), (3, 1)])  47.9 us
  transfers between devices with their start and end apart: 135, of which 65 were waited for; matrix products, arithmetic and copies ran while one was open for 31% of the time, Pallas kernels for 0%

profile of v1, /device:TPU:0, one launch (start us, length us, event | category | flops | bytes accessed | tf_op | source)
XLA Modules:
  0.0 1499.6 jit_solution(4615507598661601583)
XLA Ops:
  72.3 18.9 %collective-permute-done.5 = bf16[4,64,2048]{2,1,0:T(8,128)(2,1)S(1)} collective-permute-done((bf16[4,64,2048]{2,1,0:T(8,128)(2,1)S(1)}, bf16[4,64,2048]{2,1,0:T(8,128)(2,1)S(1)}, u32[]{:S(2)}, u32[]{:S(2)}) %collective-permute-start.5) | collective-permute-done | bytes 1048608 | tf_op jit(solution)/shard_map/ppermute | solution.py:345
  97.4 6.2 collective-permute-done.7
  132.0 5.9 collective-permute-done.13
  173.2 5.7 fusion.87
  205.1 13.2 fusion.453
  230.4 45.5 %collective-permute-done.30 = bf16[1024,1024]{1,0:T(8,128)(2,1)S(1)} collective-permute-done((bf16[1024,1024]{1,0:T(8,128)(2,1)S(1)}, bf16[1024,1024]{1,0:T(8,128)(2,1)S(1)}, u32[]{:S(2)}, u32[]{:S(2)}) %collective-permute-start.30) | collective-permute-done | bytes 2097184 | tf_op jit(solution)/shard_map/ppermute | solution.py:345
  278.6 21.7 %collective-permute-done.32 = bf16[512,1024]{1,0:T(8,128)(2,1)S(1)} collective-permute-done((bf16[512,1024]{1,0:T(8,128)(2,1)S(1)}, bf16[512,1024]{1,0:T(8,128)(2,1)S(1)}, u32[]{:S(2)}, u32[]{:S(2)}) %collective-permute-start.32) | collective-permute-done | bytes 1048608 | tf_op jit(solution)/shard_map/ppermute | solution.py:341
  301.4 15.5 %pad_maximum_fusion.10 = bf16[3072,1024]{1,0:T(8,128)(2,1)} fusion(bf16[512,1024]{1,0:T(8,128)(2,1)S(1)} %collective-permute-done.32, bf16[512,1024]{1,0:T(8,128)(2,1)S(1)} %collective-permute-done.31, bf16[1024,1024]{1,0:T(8,128)(2,1)S(1)} %collective-permute-done.30, bf16[1024,1024]{1,0:T(8,128)(2,1)S(1)} %collective-permute-done.29), kind=kLoop, calls=%fused_computation.143 | loop fusion | flops 25165824 | bytes 12582912 | tf_op jit(solution)/shard_map/concatenate | solution.py:549
  321.9 14.1 collective-permute-done.34
  339.7 12.3 collective-permute-done.35
  372.7 7.5 collective-permute-done.42
  380.2 11.1 collective-permute-done.37
  391.3 11.2 collective-permute-done.43
  404.6 9.2 collective-permute-done.38
  414.7 10.4 collective-permute-done.44
  439.1 6.6 collective-permute-done.45
  449.1 10.7 collective-permute-done.46
  480.7 30.0 %multiply_convert_fusion = (bf16[4096,1024]{0,1:T(8,128)(2,1)}, f32[4096,1024]{0,1:T(8,128)}) fusion(f32[1024]{0:T(1024)S(1)} %pad_maximum_fusion.53, bf16[1024,1024]{1,0:T(8,128)(2,1)} %copy-done.252, bf16[1024,256]{1,0:T(8,128)(2,1)} %collective-permute-done.36, bf16[1024,256]{1,0:T(8,128)(2,1)} %collective-permute-done.35, ...), kind=kOutput, calls=%fused_computation.26 | convolution fusion | flops 17293115392 | bytes 46141440 | tf_op jit(solution)/shard_map/dot_general | solution.py:427
  511.2 30.3 %convert_reduce_fusion = (f32[1024]{0:T(1024)}, bf16[4096,1024]{0,1:T(8,128)(2,1)}) fusion(f32[4096,1024]{0,1:T(8,128)} %get-tuple-element.268, f32[1024]{0:T(1024)S(1)} %pad_maximum_fusion.53, bf16[1024,1024]{1,0:T(8,128)(2,1)} %collective-permute-done.59, bf16[256,1024]{1,0:T(8,128)(2,1)} %copy-done.151, bf16[256,1024]{1,0:T(8,128)(2,1)} %copy-done.150, ...), kind=kOutput, calls=%fused_computation.25 | convolution fusion | flops 17326669824 | bytes 46145536 | tf_op jit(solution)/shard_map/dot_general | solution.py:427
  548.2 5.9 fusion.415
  565.2 24.6 %fusion.24 = bf16[4096,1024]{1,0:T(8,128)(2,1)} fusion(bf16[2048,1024]{1,0:T(8,128)(2,1)} %constant_dynamic-update-slice_fusion.17, bf16[4096,1024]{0,1:T(8,128)(2,1)} %collective-permute-done.41, bf16[4096,1024]{0,1:T(8,128)(2,1)} %get-tuple-element.267), kind=kOutput, calls=%fused_computation.125 | convolution fusion | flops 17217617920 | bytes 29360128 | tf_op jit(solution)/shard_map/dot_general | solution.py:427
  595.1 23.8 %fusion.137 = bf16[1024,2048]{1,0:T(8,128)(2,1)S(1)} fusion(bf16[4096,1024]{1,0:T(8,128)(2,1)} %constant_dynamic-update-slice_fusion.12, bf16[4096,1024]{0,1:T(8,128)(2,1)} %collective-permute-done.60, bf16[4096,1024]{0,1:T(8,128)(2,1)} %get-tuple-element.266), kind=kOutput, calls=%fused_computation.248 | convolution fusion | flops 17215520768 | bytes 29360128 | tf_op jit(solution)/shard_map/dot_general | solution.py:427
  619.2 24.3 %fusion.138 = bf16[2048,1024]{1,0:T(8,128)(2,1)S(1)} fusion(bf16[4096,1024]{1,0:T(8,128)(2,1)} %constant_dynamic-update-slice_fusion.25, bf16[4096,1024]{0,1:T(8,128)(2,1)} %collective-permute-done.41, bf16[4096,1024]{0,1:T(8,128)(2,1)} %get-tuple-element.267), kind=kOutput, calls=%fused_computation.249 | convolution fusion | flops 17215520768 | bytes 29360128 | tf_op jit(solution)/shard_map/dot_general | solution.py:427
  651.8 24.8 %fusion.25 = bf16[4096,1024]{1,0:T(8,128)(2,1)} fusion(bf16[1024,2048]{1,0:T(8,128)(2,1)} %constant_dynamic-update-slice_fusion.30, bf16[4096,1024]{0,1:T(8,128)(2,1)} %collective-permute-done.60, bf16[4096,1024]{0,1:T(8,128)(2,1)} %get-tuple-element.266), kind=kOutput, calls=%fused_computation.126 | convolution fusion | flops 17217617920 | bytes 29360128 | tf_op jit(solution)/shard_map/dot_general | solution.py:427
  683.8 11.3 collective-permute-done.115
  707.2 10.3 collective-permute-done.129
  718.9 9.8 collective-permute-done.109
  730.7 9.3 collective-permute-done.116
  752.6 9.1 collective-permute-done.130
  779.4 8.7 collective-permute-done.110
  800.2 43.6 %collective-permute-done.125 = bf16[256,1024]{1,0:T(8,128)(2,1)S(1)} collective-permute-done((bf16[256,1024]{1,0:T(8,128)(2,1)S(1)}, bf16[256,1024]{1,0:T(8,128)(2,1)S(1)}, u32[]{:S(2)}, u32[]{:S(2)}) %collective-permute-start.125) | collective-permute-done | bytes 524320 | tf_op jit(solution)/shard_map/ppermute | solution.py:345
  861.5 8.7 collective-permute-done.51
  871.3 21.4 %collective-permute-done.50 = bf16[512,1024]{1,0:T(8,128)(2,1)} collective-permute-done((bf16[512,1024]{1,0:T(8,128)(2,1)}, bf16[512,1024]{1,0:T(8,128)(2,1)}, u32[]{:S(2)}, u32[]{:S(2)}) %collective-permute-start.50) | collective-permute-done | bytes 1048608 | tf_op jit(solution)/shard_map/ppermute | solution.py:345
  900.5 39.9 %collective-permute-done.119 = bf16[512,256]{1,0:T(8,128)(2,1)S(1)} collective-permute-done((bf16[512,256]{1,0:T(8,128)(2,1)S(1)}, bf16[512,256]{1,0:T(8,128)(2,1)S(1)}, u32[]{:S(2)}, u32[]{:S(2)}) %collective-permute-start.119) | collective-permute-done | bytes 262176 | tf_op jit(solution)/shard_map/ppermute | solution.py:345
  960.9 17.6 %collective-permute-done.127 = bf16[128,1024]{1,0:T(8,128)(2,1)S(1)} collective-permute-done((bf16[128,1024]{1,0:T(8,128)(2,1)S(1)}, bf16[128,1024]{1,0:T(8,128)(2,1)S(1)}, u32[]{:S(2)}, u32[]{:S(2)}) %collective-permute-start.127) | collective-permute-done | bytes 262176 | tf_op jit(solution)/shard_map/ppermute | solution.py:341
  1001.2 11.9 fusion.428
  1037.6 6.7 multiply_reduce_fusion.2
  1063.8 6.8 multiply_reduce_fusion.4
  1070.5 6.5 multiply_reduce_fusion.5
  1077.0 6.8 multiply_convert_fusion.6
  1095.2 6.5 multiply_reduce_fusion.6
  1101.7 6.4 multiply_reduce_fusion.7
  1108.1 6.8 multiply_convert_fusion.8
  1119.4 7.2 multiply_convert_fusion.7
  1130.2 8.8 multiply_convert_fusion.5
  1144.6 8.9 multiply_convert_fusion.3
  1158.9 5.8 multiply_convert_fusion.1
  1198.7 6.0 fusion.140
  1216.2 13.3 bitcast_add_fusion
  1236.9 5.7 convolution_convert_fusion.3
  1267.9 11.4 collective-permute-done.83
  1283.5 9.0 collective-permute-done.82
  1294.3 11.1 collective-permute-done.85
  1306.3 10.3 collective-permute-done.84
  1319.1 12.3 collective-permute-done.79
  1335.2 7.5 collective-permute-done.97
  1344.5 9.4 collective-permute-done.86
  1356.2 8.9 collective-permute-done.89
  1373.2 7.7 collective-permute-done.99
  1381.5 10.6 collective-permute-done.98
  1393.7 9.6 collective-permute-done.94
  1429.1 6.2 slice_select_fusion
  1435.3 18.3 %collective-permute-done.71 = f32[18432]{0:T(1024)} collective-permute-done((f32[18432]{0:T(1024)}, f32[18432]{0:T(1024)}, u32[]{:S(2)}, u32[]{:S(2)}) %collective-permute-start.71) | collective-permute-done | bytes 73760 | tf_op jit(solution)/shard_map/ppermute | solution.py:341
  1472.5 6.4 fusion.43
  (1171 shorter events, 662.8 us)
Async XLA Ops:
  13.3 28.8 %collective-permute-start = (bf16[1024,1024]{1,0:T(8,128)(2,1)S(1)}, bf16[1024,1024]{1,0:T(8,128)(2,1)}, u32[]{:S(2)}, u32[]{:S(2)}) collective-permute-start(bf16[1024,1024]{1,0:T(8,128)(2,1)S(1)} %copy-done.13), channel_id=1, source_target_pairs={{0,4},{4,0},{1,5},{5,1},{2,6},{6,2},{3,7},{7,3},{8,12},{12,8},{9,1... | collective-permute-start | bytes 6291464 | tf_op jit(solution)/shard_map/ppermute | solution.py:337
  59.3 37.3 %collective-permute-start.25 = (bf16[256,2048]{1,0:T(8,128)(2,1)S(1)}, bf16[256,2048]{1,0:T(8,128)(2,1)S(1)}, u32[]{:S(2)}, u32[]{:S(2)}) collective-permute-start(bf16[256,2048]{1,0:T(8,128)(2,1)S(1)} %bitcast.581), channel_id=1, source_target_pairs={{0,4},{4,0},{1,5},{5,1},{2,6},{6,2},{3,7},{7,3},{8,12},{12,8},{9,1... | collective-permute-start | bytes 3145736 | tf_op jit(solution)/shard_map/ppermute | solution.py:337
  66.9 29.8 %collective-permute-start.9 = (bf16[4,64,2048]{2,1,0:T(8,128)(2,1)S(1)}, bf16[4,64,2048]{2,1,0:T(8,128)(2,1)S(1)}, u32[]{:S(2)}, u32[]{:S(2)}) collective-permute-start(bf16[4,64,2048]{2,1,0:T(8,128)(2,1)S(1)} %collective-permute-done.3), channel_id=1, source_target_pairs={{0,1},{1,2},{2,3},{3,0},{4,5},{5,6},{6,7},{7,4},{8,9},{9,10},{10,1... | collective-permute-start | bytes 3145736 | tf_op jit(solution)/shard_map/ppermute | solution.py:350
  95.5 98.9 %collective-permute-start.21 = (bf16[256,1024]{1,0:T(8,128)(2,1)}, bf16[256,1024]{1,0:T(8,128)(2,1)}, u32[]{:S(2)}, u32[]{:S(2)}) collective-permute-start(bf16[256,1024]{1,0:T(8,128)(2,1)} %get-tuple-element.205), channel_id=1, source_target_pairs={{0,4},{4,0},{1,5},{5,1},{2,6},{6,2},{3,7},{7,3},{8,12},{12,8},{9,1... | collective-permute-start | bytes 1572872 | tf_op jit(solution)/shard_map/ppermute | solution.py:337
  96.7 34.9 %collective-permute-start.15 = (bf16[4,64,2048]{2,1,0:T(8,128)(2,1)S(1)}, bf16[4,64,2048]{2,1,0:T(8,128)(2,1)S(1)}, u32[]{:S(2)}, u32[]{:S(2)}) collective-permute-start(bf16[4,64,2048]{2,1,0:T(8,128)(2,1)S(1)} %collective-permute-done.9), channel_id=1, source_target_pairs={{0,1},{1,2},{2,3},{3,0},{4,5},{5,6},{6,7},{7,4},{8,9},{9,10},{10,1... | collective-permute-start | bytes 3145736 | tf_op jit(solution)/shard_map/ppermute | solution.py:350
  96.8 30.2 %collective-permute-start.11 = (bf16[4,64,2048]{2,1,0:T(8,128)(2,1)S(1)}, bf16[4,64,2048]{2,1,0:T(8,128)(2,1)S(1)}, u32[]{:S(2)}, u32[]{:S(2)}) collective-permute-start(bf16[4,64,2048]{2,1,0:T(8,128)(2,1)S(1)} %collective-permute-done.9), channel_id=1, source_target_pairs={{0,16},{16,0},{8,24},{24,8},{1,17},{17,1},{9,25},{25,9},{2,18},{18... | collective-permute-start | bytes 3145736 | tf_op jit(solution)/shard_map/ppermute | solution.py:345
  129.4 36.4 %collective-permute-start.26 = (bf16[256,2048]{1,0:T(8,128)(2,1)S(1)}, bf16[256,2048]{1,0:T(8,128)(2,1)}, u32[]{:S(2)}, u32[]{:S(2)}) collective-permute-start(bf16[256,2048]{1,0:T(8,128)(2,1)S(1)} %bitcast.584), channel_id=1, source_target_pairs={{0,4},{4,0},{1,5},{5,1},{2,6},{6,2},{3,7},{7,3},{8,12},{12,8},{9,1... | collective-permute-start | bytes 3145736 | tf_op jit(solution)/shard_map/ppermute | solution.py:337
  131.6 65.2 %collective-permute-start.22 = (bf16[256,1024]{1,0:T(8,128)(2,1)S(1)}, bf16[256,1024]{1,0:T(8,128)(2,1)}, u32[]{:S(2)}, u32[]{:S(2)}) collective-permute-start(bf16[256,1024]{1,0:T(8,128)(2,1)S(1)} %get-tuple-element.203), channel_id=1, source_target_pairs={{0,4},{4,0},{1,5},{5,1},{2,6},{6,2},{3,7},{7,3},{8,12},{12,8},{9,1... | collective-permute-start | bytes 1572872 | tf_op jit(solution)/shard_map/ppermute | solution.py:337
  165.8 34.8 %collective-permute-start.27 = (bf16[256,2048]{1,0:T(8,128)(2,1)S(1)}, bf16[256,2048]{1,0:T(8,128)(2,1)S(1)}, u32[]{:S(2)}, u32[]{:S(2)}) collective-permute-start(bf16[256,2048]{1,0:T(8,128)(2,1)S(1)} %bitcast.588), channel_id=1, source_target_pairs={{0,4},{4,0},{1,5},{5,1},{2,6},{6,2},{3,7},{7,3},{8,12},{12,8},{9,1... | collective-permute-start | bytes 3145736 | tf_op jit(solution)/shard_map/ppermute | solution.py:337
  171.4 28.3 %collective-permute-start.23 = (bf16[256,1024]{1,0:T(8,128)(2,1)S(1)}, bf16[256,1024]{1,0:T(8,128)(2,1)S(1)}, u32[]{:S(2)}, u32[]{:S(2)}) collective-permute-start(bf16[256,1024]{1,0:T(8,128)(2,1)S(1)} %get-tuple-element.201), channel_id=1, source_target_pairs={{0,4},{4,0},{1,5},{5,1},{2,6},{6,2},{3,7},{7,3},{8,12},{12,8},{9,1... | collective-permute-start | bytes 1572872 | tf_op jit(solution)/shard_map/ppermute | solution.py:337
  228.3 47.6 %collective-permute-start.30 = (bf16[1024,1024]{1,0:T(8,128)(2,1)S(1)}, bf16[1024,1024]{1,0:T(8,128)(2,1)S(1)}, u32[]{:S(2)}, u32[]{:S(2)}) collective-permute-start(bf16[1024,1024]{1,0:T(8,128)(2,1)S(1)} %get-tuple-element.141), channel_id=1, source_target_pairs={{0,16},{16,0},{8,24},{24,8},{1,17},{17,1},{9,25},{25,9},{2,18},{18... | collective-permute-start | bytes 6291464 | tf_op jit(solution)/shard_map/ppermute | solution.py:345
  230.0 47.3 %collective-permute-start.29 = (bf16[1024,1024]{1,0:T(8,128)(2,1)S(1)}, bf16[1024,1024]{1,0:T(8,128)(2,1)S(1)}, u32[]{:S(2)}, u32[]{:S(2)}) collective-permute-start(bf16[1024,1024]{1,0:T(8,128)(2,1)S(1)} %get-tuple-element.141), channel_id=1, source_target_pairs={{0,8},{8,0},{16,24},{24,16},{1,9},{9,1},{17,25},{25,17},{2,10},{10... | collective-permute-start | bytes 6291464 | tf_op jit(solution)/shard_map/ppermute | solution.py:341
  316.9 163.7 %collective-permute-start.33 = (bf16[3072,1024]{1,0:T(8,128)(2,1)}, bf16[3072,1024]{1,0:T(8,128)(2,1)}, u32[]{:S(2)}, u32[]{:S(2)}) collective-permute-start(bf16[3072,1024]{1,0:T(8,128)(2,1)} %pad_maximum_fusion.10), channel_id=1, source_target_pairs={{0,4},{4,0},{1,5},{5,1},{2,6},{6,2},{3,7},{7,3},{8,12},{12,8},{9,1... | collective-permute-start | bytes 18874376 | tf_op jit(solution)/shard_map/ppermute | solution.py:337
  356.0 71.9 %collective-permute-start.54 = (bf16[1024,1024]{1,0:T(8,128)(2,1)}, bf16[1024,1024]{1,0:T(8,128)(2,1)}, u32[]{:S(2)}, u32[]{:S(2)}) collective-permute-start(bf16[1024,1024]{1,0:T(8,128)(2,1)} %get-tuple-element.77), channel_id=1, source_target_pairs={{0,8},{8,0},{16,24},{24,16},{1,9},{9,1},{17,25},{25,17},{2,10},{10... | collective-permute-start | bytes 6291464 | tf_op jit(solution)/shard_map/ppermute | solution.py:341
  357.1 79.7 %collective-permute-start.55 = (bf16[1024,1024]{1,0:T(8,128)(2,1)}, bf16[1024,1024]{1,0:T(8,128)(2,1)}, u32[]{:S(2)}, u32[]{:S(2)}) collective-permute-start(bf16[1024,1024]{1,0:T(8,128)(2,1)} %get-tuple-element.77), channel_id=1, source_target_pairs={{0,16},{16,0},{8,24},{24,8},{1,17},{17,1},{9,25},{25,9},{2,18},{18... | collective-permute-start | bytes 6291464 | tf_op jit(solution)/shard_map/ppermute | solution.py:345
  429.2 36.9 %collective-permute-start.56 = (bf16[512,1024]{1,0:T(8,128)(2,1)S(1)}, bf16[512,1024]{1,0:T(8,128)(2,1)S(1)}, u32[]{:S(2)}, u32[]{:S(2)}) collective-permute-start(bf16[512,1024]{1,0:T(8,128)(2,1)S(1)} %slice.1123), channel_id=1, source_target_pairs={{0,16},{16,0},{8,24},{24,8},{1,17},{17,1},{9,25},{25,9},{2,18},{18... | collective-permute-start | bytes 3145736 | tf_op jit(solution)/shard_map/ppermute | solution.py:345
  436.7 42.7 %collective-permute-start.40 = (bf16[1024,1024]{1,0:T(8,128)(2,1)S(1)}, bf16[1024,1024]{1,0:T(8,128)(2,1)S(1)}, u32[]{:S(2)}, u32[]{:S(2)}) collective-permute-start(bf16[1024,1024]{1,0:T(8,128)(2,1)S(1)} %pad_maximum_fusion.20), channel_id=1, source_target_pairs={{0,4},{4,0},{1,5},{5,1},{2,6},{6,2},{3,7},{7,3},{8,12},{12,8},{9,1... | collective-permute-start | bytes 6291464 | tf_op jit(solution)/shard_map/ppermute | solution.py:337
  438.0 29.1 %collective-permute-start.57 = (bf16[512,1024]{1,0:T(8,128)(2,1)S(1)}, bf16[512,1024]{1,0:T(8,128)(2,1)S(1)}, u32[]{:S(2)}, u32[]{:S(2)}) collective-permute-start(bf16[512,1024]{1,0:T(8,128)(2,1)S(1)} %slice.1124), channel_id=1, source_target_pairs={{0,8},{8,0},{16,24},{24,16},{1,9},{9,1},{17,25},{25,17},{2,10},{10... | collective-permute-start | bytes 3145736 | tf_op jit(solution)/shard_map/ppermute | solution.py:341
  468.2 43.0 %collective-permute-start.58 = (bf16[4096,1024]{1,0:T(8,128)(2,1)}, bf16[4096,1024]{1,0:T(8,128)(2,1)}, u32[]{:S(2)}, u32[]{:S(2)}) collective-permute-start(bf16[4096,1024]{1,0:T(8,128)(2,1)} %constant_dynamic-update-slice_fusion.25), channel_id=1, source_target_pairs={{0,4},{4,0},{1,5},{5,1},{2,6},{6,2},{3,7},{7,3},{8,12},{12,8},{9,1... | collective-permute-start | bytes 25165832 | tf_op jit(solution)/shard_map/ppermute | solution.py:337
  474.3 36.9 %collective-permute-start.59 = (bf16[1024,1024]{1,0:T(8,128)(2,1)}, bf16[1024,1024]{1,0:T(8,128)(2,1)}, u32[]{:S(2)}, u32[]{:S(2)}) collective-permute-start(bf16[1024,1024]{1,0:T(8,128)(2,1)} %pad_maximum_fusion.21), channel_id=1, source_target_pairs={{0,4},{4,0},{1,5},{5,1},{2,6},{6,2},{3,7},{7,3},{8,12},{12,8},{9,1... | collective-permute-start | bytes 6291464 | tf_op jit(solution)/shard_map/ppermute | solution.py:337
  510.7 54.5 %collective-permute-start.41 = (bf16[4096,1024]{0,1:T(8,128)(2,1)}, bf16[4096,1024]{0,1:T(8,128)(2,1)}, u32[]{:S(2)}, u32[]{:S(2)}) collective-permute-start(bf16[4096,1024]{0,1:T(8,128)(2,1)} %get-tuple-element.267), channel_id=1, source_target_pairs={{0,4},{4,0},{1,5},{5,1},{2,6},{6,2},{3,7},{7,3},{8,12},{12,8},{9,1... | collective-permute-start | bytes 25165832 | tf_op jit(solution)/shard_map/ppermute | solution.py:337
  541.5 53.6 %collective-permute-start.60 = (bf16[4096,1024]{0,1:T(8,128)(2,1)}, bf16[4096,1024]{0,1:T(8,128)(2,1)}, u32[]{:S(2)}, u32[]{:S(2)}) collective-permute-start(bf16[4096,1024]{0,1:T(8,128)(2,1)} %get-tuple-element.266), channel_id=1, source_target_pairs={{0,4},{4,0},{1,5},{5,1},{2,6},{6,2},{3,7},{7,3},{8,12},{12,8},{9,1... | collective-permute-start | bytes 25165832 | tf_op jit(solution)/shard_map/ppermute | solution.py:337
  594.1 169.0 %collective-permute-start.49 = (bf16[512,1024]{1,0:T(8,128)(2,1)}, bf16[512,1024]{1,0:T(8,128)(2,1)}, u32[]{:S(2)}, u32[]{:S(2)}) collective-permute-start(bf16[512,1024]{1,0:T(8,128)(2,1)} %get-tuple-element.106), channel_id=1, source_target_pairs={{0,8},{8,0},{16,24},{24,16},{1,9},{9,1},{17,25},{25,17},{2,10},{10... | collective-permute-start | bytes 3145736 | tf_op jit(solution)/shard_map/ppermute | solution.py:341
  619.0 31.0 %collective-permute-start.107 = (bf16[1024,256]{1,0:T(8,128)(2,1)S(1)}, bf16[1024,256]{1,0:T(8,128)(2,1)S(1)}, u32[]{:S(2)}, u32[]{:S(2)}) collective-permute-start(bf16[1024,256]{1,0:T(8,128)(2,1)S(1)} %get-tuple-element.121), channel_id=1, source_target_pairs={{0,3},{1,0},{2,1},{3,2},{4,7},{5,4},{6,5},{7,6},{8,11},{9,8},{10,9... | collective-permute-start | bytes 1572872 | tf_op jit(solution)/shard_map/ppermute | solution.py:355
  619.1 30.9 %collective-permute-start.114 = (bf16[1024,256]{1,0:T(8,128)(2,1)S(1)}, bf16[1024,256]{1,0:T(8,128)(2,1)S(1)}, u32[]{:S(2)}, u32[]{:S(2)}) collective-permute-start(bf16[1024,256]{1,0:T(8,128)(2,1)S(1)} %get-tuple-element.122), channel_id=1, source_target_pairs={{0,3},{1,0},{2,1},{3,2},{4,7},{5,4},{6,5},{7,6},{8,11},{9,8},{10,9... | collective-permute-start | bytes 1572872 | tf_op jit(solution)/shard_map/ppermute | solution.py:355
  646.4 30.2 %collective-permute-start.121 = (bf16[256,1024]{1,0:T(8,128)(2,1)}, bf16[256,1024]{1,0:T(8,128)(2,1)S(1)}, u32[]{:S(2)}, u32[]{:S(2)}) collective-permute-start(bf16[256,1024]{1,0:T(8,128)(2,1)} %get-tuple-element.113), channel_id=1, source_target_pairs={{0,3},{1,0},{2,1},{3,2},{4,7},{5,4},{6,5},{7,6},{8,11},{9,8},{10,9... | collective-permute-start | bytes 1572872 | tf_op jit(solution)/shard_map/ppermute | solution.py:355
  646.5 30.1 %collective-permute-start.128 = (bf16[256,1024]{1,0:T(8,128)(2,1)S(1)}, bf16[256,1024]{1,0:T(8,128)(2,1)S(1)}, u32[]{:S(2)}, u32[]{:S(2)}) collective-permute-start(bf16[256,1024]{1,0:T(8,128)(2,1)S(1)} %get-tuple-element.114), channel_id=1, source_target_pairs={{0,3},{1,0},{2,1},{3,2},{4,7},{5,4},{6,5},{7,6},{8,11},{9,8},{10,9... | collective-permute-start | bytes 1572872 | tf_op jit(solution)/shard_map/ppermute | solution.py:355
  650.4 33.4 %collective-permute-start.108 = (bf16[1024,256]{1,0:T(8,128)(2,1)S(1)}, bf16[1024,256]{1,0:T(8,128)(2,1)S(1)}, u32[]{:S(2)}, u32[]{:S(2)}) collective-permute-start(bf16[1024,256]{1,0:T(8,128)(2,1)S(1)} %get-tuple-element.119), channel_id=1, source_target_pairs={{0,3},{1,0},{2,1},{3,2},{4,7},{5,4},{6,5},{7,6},{8,11},{9,8},{10,9... | collective-permute-start | bytes 1572872 | tf_op jit(solution)/shard_map/ppermute | solution.py:355
  650.5 44.6 %collective-permute-start.115 = (bf16[1024,256]{1,0:T(8,128)(2,1)S(1)}, bf16[1024,256]{1,0:T(8,128)(2,1)}, u32[]{:S(2)}, u32[]{:S(2)}) collective-permute-start(bf16[1024,256]{1,0:T(8,128)(2,1)S(1)} %get-tuple-element.120), channel_id=1, source_target_pairs={{0,3},{1,0},{2,1},{3,2},{4,7},{5,4},{6,5},{7,6},{8,11},{9,8},{10,9... | collective-permute-start | bytes 1572872 | tf_op jit(solution)/shard_map/ppermute | solution.py:355
  678.2 28.1 %collective-permute-start.122 = (bf16[256,1024]{1,0:T(8,128)(2,1)S(1)}, bf16[256,1024]{1,0:T(8,128)(2,1)S(1)}, u32[]{:S(2)}, u32[]{:S(2)}) collective-permute-start(bf16[256,1024]{1,0:T(8,128)(2,1)S(1)} %get-tuple-element.111), channel_id=1, source_target_pairs={{0,3},{1,0},{2,1},{3,2},{4,7},{5,4},{6,5},{7,6},{8,11},{9,8},{10,9... | collective-permute-start | bytes 1572872 | tf_op jit(solution)/shard_map/ppermute | solution.py:355
  678.3 39.2 %collective-permute-start.129 = (bf16[256,1024]{1,0:T(8,128)(2,1)S(1)}, bf16[256,1024]{1,0:T(8,128)(2,1)S(1)}, u32[]{:S(2)}, u32[]{:S(2)}) collective-permute-start(bf16[256,1024]{1,0:T(8,128)(2,1)S(1)} %get-tuple-element.112), channel_id=1, source_target_pairs={{0,3},{1,0},{2,1},{3,2},{4,7},{5,4},{6,5},{7,6},{8,11},{9,8},{10,9... | collective-permute-start | bytes 1572872 | tf_op jit(solution)/shard_map/ppermute | solution.py:355
  696.8 32.0 %collective-permute-start.109 = (bf16[1024,256]{1,0:T(8,128)(2,1)S(1)}, bf16[1024,256]{1,0:T(8,128)(2,1)S(1)}, u32[]{:S(2)}, u32[]{:S(2)}) collective-permute-start(bf16[1024,256]{1,0:T(8,128)(2,1)S(1)} %get-tuple-element.117), channel_id=1, source_target_pairs={{0,3},{1,0},{2,1},{3,2},{4,7},{5,4},{6,5},{7,6},{8,11},{9,8},{10,9... | collective-permute-start | bytes 1572872 | tf_op jit(solution)/shard_map/ppermute | solution.py:355
  698.8 41.2 %collective-permute-start.116 = (bf16[1024,256]{1,0:T(8,128)(2,1)S(1)}, bf16[1024,256]{1,0:T(8,128)(2,1)S(1)}, u32[]{:S(2)}, u32[]{:S(2)}) collective-permute-start(bf16[1024,256]{1,0:T(8,128)(2,1)S(1)} %get-tuple-element.118), channel_id=1, source_target_pairs={{0,3},{1,0},{2,1},{3,2},{4,7},{5,4},{6,5},{7,6},{8,11},{9,8},{10,9... | collective-permute-start | bytes 1572872 | tf_op jit(solution)/shard_map/ppermute | solution.py:355
  706.3 58.4 %collective-permute-start.62 = (bf16[512,1024]{1,0:T(8,128)(2,1)S(1)}, bf16[512,1024]{1,0:T(8,128)(2,1)S(1)}, u32[]{:S(2)}, u32[]{:S(2)}) collective-permute-start(bf16[512,1024]{1,0:T(8,128)(2,1)S(1)} %get-tuple-element.100), channel_id=1, source_target_pairs={{0,8},{8,0},{16,24},{24,16},{1,9},{9,1},{17,25},{25,17},{2,10},{10... | collective-permute-start | bytes 3145736 | tf_op jit(solution)/shard_map/ppermute | solution.py:341
  717.5 48.2 %collective-permute-start.61 = (bf16[512,1024]{1,0:T(8,128)(2,1)S(1)}, bf16[512,1024]{1,0:T(8,128)(2,1)S(1)}, u32[]{:S(2)}, u32[]{:S(2)}) collective-permute-start(bf16[512,1024]{1,0:T(8,128)(2,1)S(1)} %get-tuple-element.97), channel_id=1, source_target_pairs={{0,8},{8,0},{16,24},{24,16},{1,9},{9,1},{17,25},{25,17},{2,10},{10... | collective-permute-start | bytes 3145736 | tf_op jit(solution)/shard_map/ppermute | solution.py:341
  770.9 83.8 %collective-permute-start.64 = (bf16[512,1024]{1,0:T(8,128)(2,1)}, bf16[512,1024]{1,0:T(8,128)(2,1)}, u32[]{:S(2)}, u32[]{:S(2)}) collective-permute-start(bf16[512,1024]{1,0:T(8,128)(2,1)} %get-tuple-element.99), channel_id=1, source_target_pairs={{0,16},{16,0},{8,24},{24,8},{1,17},{17,1},{9,25},{25,9},{2,18},{18... | collective-permute-start | bytes 3145736 | tf_op jit(solution)/shard_map/ppermute | solution.py:345
  776.9 79.2 %collective-permute-start.63 = (bf16[512,1024]{1,0:T(8,128)(2,1)}, bf16[512,1024]{1,0:T(8,128)(2,1)}, u32[]{:S(2)}, u32[]{:S(2)}) collective-permute-start(bf16[512,1024]{1,0:T(8,128)(2,1)} %add_convert_fusion.6), channel_id=1, source_target_pairs={{0,16},{16,0},{8,24},{24,8},{1,17},{17,1},{9,25},{25,9},{2,18},{18... | collective-permute-start | bytes 3145736 | tf_op jit(solution)/shard_map/ppermute | solution.py:345
  788.1 55.7 %collective-permute-start.125 = (bf16[256,1024]{1,0:T(8,128)(2,1)S(1)}, bf16[256,1024]{1,0:T(8,128)(2,1)S(1)}, u32[]{:S(2)}, u32[]{:S(2)}) collective-permute-start(bf16[256,1024]{1,0:T(8,128)(2,1)S(1)} %get-tuple-element.107), channel_id=1, source_target_pairs={{0,16},{16,0},{8,24},{24,8},{1,17},{17,1},{9,25},{25,9},{2,18},{18... | collective-permute-start | bytes 1572872 | tf_op jit(solution)/shard_map/ppermute | solution.py:345
  789.6 55.8 %collective-permute-start.124 = (bf16[256,1024]{1,0:T(8,128)(2,1)S(1)}, bf16[256,1024]{1,0:T(8,128)(2,1)S(1)}, u32[]{:S(2)}, u32[]{:S(2)}) collective-permute-start(bf16[256,1024]{1,0:T(8,128)(2,1)S(1)} %get-tuple-element.107), channel_id=1, source_target_pairs={{0,8},{8,0},{16,24},{24,16},{1,9},{9,1},{17,25},{25,17},{2,10},{10... | collective-permute-start | bytes 1572872 | tf_op jit(solution)/shard_map/ppermute | solution.py:341
  799.3 61.3 %collective-permute-start.48 = (bf16[512,1024]{1,0:T(8,128)(2,1)}, bf16[512,1024]{1,0:T(8,128)(2,1)}, u32[]{:S(2)}, u32[]{:S(2)}) collective-permute-start(bf16[512,1024]{1,0:T(8,128)(2,1)} %get-tuple-element.103), channel_id=1, source_target_pairs={{0,8},{8,0},{16,24},{24,16},{1,9},{9,1},{17,25},{25,17},{2,10},{10... | collective-permute-start | bytes 3145736 | tf_op jit(solution)/shard_map/ppermute | solution.py:341
  845.4 47.4 %collective-permute-start.50 = (bf16[512,1024]{1,0:T(8,128)(2,1)}, bf16[512,1024]{1,0:T(8,128)(2,1)}, u32[]{:S(2)}, u32[]{:S(2)}) collective-permute-start(bf16[512,1024]{1,0:T(8,128)(2,1)} %add_convert_fusion.8), channel_id=1, source_target_pairs={{0,16},{16,0},{8,24},{24,8},{1,17},{17,1},{9,25},{25,9},{2,18},{18... | collective-permute-start | bytes 3145736 | tf_op jit(solution)/shard_map/ppermute | solution.py:345
  854.7 136.8 %collective-permute-start.53 = (bf16[512,1024]{1,0:T(8,128)(2,1)}, bf16[512,1024]{1,0:T(8,128)(2,1)}, u32[]{:S(2)}, u32[]{:S(2)}) collective-permute-start(bf16[512,1024]{1,0:T(8,128)(2,1)} %get-tuple-element.104), channel_id=1, source_target_pairs={{0,16},{16,0},{8,24},{24,8},{1,17},{17,1},{9,25},{25,9},{2,18},{18... | collective-permute-start | bytes 3145736 | tf_op jit(solution)/shard_map/ppermute | solution.py:345
  856.1 100.6 %collective-permute-start.66 = (bf16[512,1024]{1,0:T(8,128)(2,1)S(1)}, bf16[512,1024]{1,0:T(8,128)(2,1)S(1)}, u32[]{:S(2)}, u32[]{:S(2)}) collective-permute-start(bf16[512,1024]{1,0:T(8,128)(2,1)S(1)} %copy-done.128), channel_id=1, source_target_pairs={{0,16},{16,0},{8,24},{24,8},{1,17},{17,1},{9,25},{25,9},{2,18},{18... | collective-permute-start | bytes 3145736 | tf_op jit(solution)/shard_map/ppermute | solution.py:345
  860.5 97.6 %collective-permute-start.65 = (bf16[512,1024]{1,0:T(8,128)(2,1)S(1)}, bf16[512,1024]{1,0:T(8,128)(2,1)S(1)}, u32[]{:S(2)}, u32[]{:S(2)}) collective-permute-start(bf16[512,1024]{1,0:T(8,128)(2,1)S(1)} %get-tuple-element.96), channel_id=1, source_target_pairs={{0,8},{8,0},{16,24},{24,16},{1,9},{9,1},{17,25},{25,17},{2,10},{10... | collective-permute-start | bytes 3145736 | tf_op jit(solution)/shard_map/ppermute | solution.py:341
  870.2 29.3 %collective-permute-start.120 = (bf16[512,256]{1,0:T(8,128)(2,1)S(1)}, bf16[512,256]{1,0:T(8,128)(2,1)S(1)}, u32[]{:S(2)}, u32[]{:S(2)}) collective-permute-start(bf16[512,256]{1,0:T(8,128)(2,1)S(1)} %slice.1191), channel_id=1, source_target_pairs={{0,8},{8,0},{16,24},{24,16},{1,9},{9,1},{17,25},{25,17},{2,10},{10... | collective-permute-start | bytes 786440 | tf_op jit(solution)/shard_map/ppermute | solution.py:341
  892.7 47.7 %collective-permute-start.119 = (bf16[512,256]{1,0:T(8,128)(2,1)S(1)}, bf16[512,256]{1,0:T(8,128)(2,1)S(1)}, u32[]{:S(2)}, u32[]{:S(2)}) collective-permute-start(bf16[512,256]{1,0:T(8,128)(2,1)S(1)} %slice.1190), channel_id=1, source_target_pairs={{0,16},{16,0},{8,24},{24,8},{1,17},{17,1},{9,25},{25,9},{2,18},{18... | collective-permute-start | bytes 786440 | tf_op jit(solution)/shard_map/ppermute | solution.py:345
  899.5 44.1 %collective-permute-start.113 = (bf16[512,256]{1,0:T(8,128)(2,1)S(1)}, bf16[512,256]{1,0:T(8,128)(2,1)S(1)}, u32[]{:S(2)}, u32[]{:S(2)}) collective-permute-start(bf16[512,256]{1,0:T(8,128)(2,1)S(1)} %slice.1185), channel_id=1, source_target_pairs={{0,8},{8,0},{16,24},{24,16},{1,9},{9,1},{17,25},{25,17},{2,10},{10... | collective-permute-start | bytes 786440 | tf_op jit(solution)/shard_map/ppermute | solution.py:341
  952.7 38.8 %collective-permute-start.52 = (bf16[512,1024]{1,0:T(8,128)(2,1)}, bf16[512,1024]{1,0:T(8,128)(2,1)}, u32[]{:S(2)}, u32[]{:S(2)}) collective-permute-start(bf16[512,1024]{1,0:T(8,128)(2,1)} %get-tuple-element.102), channel_id=1, source_target_pairs={{0,8},{8,0},{16,24},{24,16},{1,9},{9,1},{17,25},{25,17},{2,10},{10... | collective-permute-start | bytes 3145736 | tf_op jit(solution)/shard_map/ppermute | solution.py:341
  960.8 36.2 %collective-permute-start.67 = (bf16[1024,1024]{1,0:T(8,128)(2,1)S(1)}, bf16[1024,1024]{1,0:T(8,128)(2,1)S(1)}, u32[]{:S(2)}, u32[]{:S(2)}) collective-permute-start(bf16[1024,1024]{1,0:T(8,128)(2,1)S(1)} %fusion.139), channel_id=1, source_target_pairs={{0,4},{4,0},{1,5},{5,1},{2,6},{6,2},{3,7},{7,3},{8,12},{12,8},{9,1... | collective-permute-start | bytes 6291464 | tf_op jit(solution)/shard_map/ppermute | solution.py:337
  1234.5 178.3 %collective-permute-start.68 = (bf16[1024,1024]{1,0:T(8,128)(2,1)}, bf16[1024,1024]{1,0:T(8,128)(2,1)}, u32[]{:S(2)}, u32[]{:S(2)}) collective-permute-start(bf16[1024,1024]{1,0:T(8,128)(2,1)} %slice.1399), channel_id=1, source_target_pairs={{0,4},{4,0},{1,5},{5,1},{2,6},{6,2},{3,7},{7,3},{8,12},{12,8},{9,1... | collective-permute-start | bytes 6291464 | tf_op jit(solution)/shard_map/ppermute | solution.py:337
  1236.3 28.2 %collective-permute-start.70 = (f32[4,3072]{1,0:T(4,128)S(1)}, f32[4,3072]{1,0:T(4,128)S(1)}, u32[]{:S(2)}, u32[]{:S(2)}) collective-permute-start(f32[4,3072]{1,0:T(4,128)S(1)} %pad_maximum_fusion.44), channel_id=1, source_target_pairs={{0,4},{4,0},{1,5},{5,1},{2,6},{6,2},{3,7},{7,3},{8,12},{12,8},{9,1... | collective-permute-start | bytes 147464 | tf_op jit(solution)/shard_map/ppermute | solution.py:337
  1243.9 36.1 %collective-permute-start.75 = (bf16[2,64,2048]{2,1,0:T(8,128)(2,1)S(1)}, bf16[2,64,2048]{2,1,0:T(8,128)(2,1)S(1)}, u32[]{:S(2)}, u32[]{:S(2)}) collective-permute-start(bf16[2,64,2048]{2,1,0:T(8,128)(2,1)S(1)} %get-tuple-element.161), channel_id=1, source_target_pairs={{0,8},{8,0},{16,24},{24,16},{1,9},{9,1},{17,25},{25,17},{2,10},{10... | collective-permute-start | bytes 1572872 | tf_op jit(solution)/shard_map/ppermute | solution.py:341
  1244.9 36.1 %collective-permute-start.78 = (bf16[2,64,2048]{2,1,0:T(8,128)(2,1)S(1)}, bf16[2,64,2048]{2,1,0:T(8,128)(2,1)S(1)}, u32[]{:S(2)}, u32[]{:S(2)}) collective-permute-start(bf16[2,64,2048]{2,1,0:T(8,128)(2,1)S(1)} %get-tuple-element.137), channel_id=1, source_target_pairs={{0,16},{16,0},{8,24},{24,8},{1,17},{17,1},{9,25},{25,9},{2,18},{18... | collective-permute-start | bytes 1572872 | tf_op jit(solution)/shard_map/ppermute | solution.py:345
  1279.3 38.7 %collective-permute-start.80 = (bf16[2,64,2048]{2,1,0:T(8,128)(2,1)S(1)}, bf16[2,64,2048]{2,1,0:T(8,128)(2,1)S(1)}, u32[]{:S(2)}, u32[]{:S(2)}) collective-permute-start(bf16[2,64,2048]{2,1,0:T(8,128)(2,1)S(1)} %get-tuple-element.138), channel_id=1, source_target_pairs={{0,16},{16,0},{8,24},{24,8},{1,17},{17,1},{9,25},{25,9},{2,18},{18... | collective-permute-start | bytes 1572872 | tf_op jit(solution)/shard_map/ppermute | solution.py:345
  1282.5 34.1 %collective-permute-start.84 = (bf16[2,64,2048]{2,1,0:T(8,128)(2,1)S(1)}, bf16[2,64,2048]{2,1,0:T(8,128)(2,1)S(1)}, u32[]{:S(2)}, u32[]{:S(2)}) collective-permute-start(bf16[2,64,2048]{2,1,0:T(8,128)(2,1)S(1)} %fusion.301), channel_id=1, source_target_pairs={{0,16},{16,0},{8,24},{24,8},{1,17},{17,1},{9,25},{25,9},{2,18},{18... | collective-permute-start | bytes 1572872 | tf_op jit(solution)/shard_map/ppermute | solution.py:345
  1292.5 51.3 %collective-permute-start.87 = (bf16[2,64,2048]{2,1,0:T(8,128)(2,1)S(1)}, bf16[2,64,2048]{2,1,0:T(8,128)(2,1)S(1)}, u32[]{:S(2)}, u32[]{:S(2)}) collective-permute-start(bf16[2,64,2048]{2,1,0:T(8,128)(2,1)S(1)} %get-tuple-element.136), channel_id=1, source_target_pairs={{0,16},{16,0},{8,24},{24,8},{1,17},{17,1},{9,25},{25,9},{2,18},{18... | collective-permute-start | bytes 1572872 | tf_op jit(solution)/shard_map/ppermute | solution.py:345
  1305.4 27.4 %collective-permute-start.90 = (bf16[2,64,2048]{2,1,0:T(8,128)(2,1)S(1)}, bf16[2,64,2048]{2,1,0:T(8,128)(2,1)S(1)}, u32[]{:S(2)}, u32[]{:S(2)}) collective-permute-start(bf16[2,64,2048]{2,1,0:T(8,128)(2,1)S(1)} %get-tuple-element.154), channel_id=1, source_target_pairs={{0,8},{8,0},{16,24},{24,16},{1,9},{9,1},{17,25},{25,17},{2,10},{10... | collective-permute-start | bytes 1572872 | tf_op jit(solution)/shard_map/ppermute | solution.py:341
  1365.7 26.5 %collective-permute-start.98 = (bf16[2,64,2048]{2,1,0:T(8,128)(2,1)S(1)}, bf16[2,64,2048]{2,1,0:T(8,128)(2,1)S(1)}, u32[]{:S(2)}, u32[]{:S(2)}) collective-permute-start(bf16[2,64,2048]{2,1,0:T(8,128)(2,1)S(1)} %fusion.289), channel_id=1, source_target_pairs={{0,16},{16,0},{8,24},{24,8},{1,17},{17,1},{9,25},{25,9},{2,18},{18... | collective-permute-start | bytes 1572872 | tf_op jit(solution)/shard_map/ppermute | solution.py:345
  1369.7 37.2 %collective-permute-start.88 = (bf16[4,64,2048]{2,1,0:T(8,128)(2,1)S(1)}, bf16[4,64,2048]{2,1,0:T(8,128)(2,1)S(1)}, u32[]{:S(2)}, u32[]{:S(2)}) collective-permute-start(bf16[4,64,2048]{2,1,0:T(8,128)(2,1)S(1)} %add_convert_fusion.4), channel_id=1, source_target_pairs={{0,3},{1,0},{2,1},{3,2},{4,7},{5,4},{6,5},{7,6},{8,11},{9,8},{10,9... | collective-permute-start | bytes 3145736 | tf_op jit(solution)/shard_map/ppermute | solution.py:355
  1372.5 30.8 %collective-permute-start.94 = (bf16[2,64,2048]{2,1,0:T(8,128)(2,1)S(1)}, bf16[2,64,2048]{2,1,0:T(8,128)(2,1)S(1)}, u32[]{:S(2)}, u32[]{:S(2)}) collective-permute-start(bf16[2,64,2048]{2,1,0:T(8,128)(2,1)S(1)} %get-tuple-element.134), channel_id=1, source_target_pairs={{0,16},{16,0},{8,24},{24,8},{1,17},{17,1},{9,25},{25,9},{2,18},{18... | collective-permute-start | bytes 1572872 | tf_op jit(solution)/shard_map/ppermute | solution.py:345
  1380.9 28.6 %collective-permute-start.101 = (bf16[2,64,2048]{2,1,0:T(8,128)(2,1)S(1)}, bf16[2,64,2048]{2,1,0:T(8,128)(2,1)S(1)}, u32[]{:S(2)}, u32[]{:S(2)}) collective-permute-start(bf16[2,64,2048]{2,1,0:T(8,128)(2,1)S(1)} %get-tuple-element.132), channel_id=1, source_target_pairs={{0,16},{16,0},{8,24},{24,8},{1,17},{17,1},{9,25},{25,9},{2,18},{18... | collective-permute-start | bytes 1572872 | tf_op jit(solution)/shard_map/ppermute | solution.py:345
  1416.8 39.6 %collective-permute-start.69 = (f32[2,1024]{1,0:T(2,128)}, f32[2,1024]{1,0:T(2,128)}, u32[]{:S(2)}, u32[]{:S(2)}) collective-permute-start(f32[2,1024]{1,0:T(2,128)} %pad_maximum_fusion.51), channel_id=1, source_target_pairs={{0,4},{4,0},{1,5},{5,1},{2,6},{6,2},{3,7},{7,3},{8,12},{12,8},{9,1... | collective-permute-start | bytes 24584 | tf_op jit(solution)/shard_map/ppermute | solution.py:337
  1426.2 39.9 %collective-permute-start.104 = (bf16[4,2,64,1024]{3,2,0,1:T(8,128)(2,1)}, bf16[4,2,64,1024]{3,2,0,1:T(8,128)(2,1)}, u32[]{:S(2)}, u32[]{:S(2)}) collective-permute-start(bf16[4,2,64,1024]{3,2,0,1:T(8,128)(2,1)} %get-tuple-element.180), channel_id=1, source_target_pairs={{0,16},{16,0},{8,24},{24,8},{1,17},{17,1},{9,25},{25,9},{2,18},{18... | collective-permute-start | bytes 3145736 | tf_op jit(solution)/shard_map/ppermute | solution.py:345
  1426.4 42.5 %collective-permute-start.103 = (bf16[4,2,64,1024]{3,2,0,1:T(8,128)(2,1)}, bf16[4,2,64,1024]{3,2,0,1:T(8,128)(2,1)}, u32[]{:S(2)}, u32[]{:S(2)}) collective-permute-start(bf16[4,2,64,1024]{3,2,0,1:T(8,128)(2,1)} %get-tuple-element.180), channel_id=1, source_target_pairs={{0,8},{8,0},{16,24},{24,16},{1,9},{9,1},{17,25},{25,17},{2,10},{10... | collective-permute-start | bytes 3145736 | tf_op jit(solution)/shard_map/ppermute | solution.py:341
  (348 other events, 4234.2 us)

commit v2 on v0

--- a/solution.py
+++ b/solution.py
@@ -1,6 +1,10 @@
+import functools
+
 import jax
 import jax.numpy as jnp
 from jax import lax
+from jax.experimental import pallas as pl
+from jax.experimental.pallas import tpu as pltpu
 from jax.sharding import PartitionSpec as P
 
 D = 2048
@@ -139,7 +143,7 @@
     return (jnp.concatenate(query_grads, axis=2), key_grad, value_grad)
 
 
-def body(
+def body_general(
     tokens_in,
     out_grad,
     segment_ids,
@@ -333,6 +337,574 @@
     )
 
 
+def after(values, *others):
+    return lax.optimization_barrier((values, others))[0]
+
+
+def swap(values):
+    return lax.ppermute(values, "row", [(0, 1), (1, 0)])
+
+
+def step_x(values):
+    return lax.ppermute(values, "dp", [(0, 1), (1, 0), (2, 3), (3, 2)])
+
+
+def step_y(values):
+    return lax.ppermute(values, "dp", [(0, 2), (2, 0), (1, 3), (3, 1)])
+
+
+def step_up(values):
+    count = lax.axis_size("col")
+    return lax.ppermute(values, "col", [(i, (i + 1) % count) for i in range(count)])
+
+
+def step_down(values):
+    count = lax.axis_size("col")
+    return lax.ppermute(values, "col", [(i, (i - 1) % count) for i in range(count)])
+
+
+def plane_gather(values):
+    half = values.shape[0] // 2
+    from_x = step_x(values)
+    from_y = step_y(values)
+    far_one = step_y(from_x[:half])
+    far_two = step_x(from_y[half:])
+    return [values, from_x, from_y, far_one, far_two]
+
+
+def add_rounded(left, right):
+    return (left.astype(jnp.float32) + right.astype(jnp.float32)).astype(jnp.bfloat16)
+
+
+def plane_sum(parts):
+    f32 = jnp.float32
+    first, second = parts
+    via_x = step_x(first[3])
+    via_y = step_y(second[3])
+    first_x = step_x(first[1])
+    second_y = step_y(second[2])
+    second_x = step_x(add_rounded(second[1], via_y))
+    first_y = step_y(add_rounded(first[2], via_x))
+    return (
+        first[0].astype(f32) + first_x.astype(f32) + first_y.astype(f32),
+        second[0].astype(f32) + second_x.astype(f32) + second_y.astype(f32),
+    )
+
+
+def ring_gather(values):
+    held = [values]
+    for _ in range(lax.axis_size("col") - 1):
+        held.append(jax.tree.map(step_up, held[-1]))
+    return held
+
+
+def ring_sum(blocks):
+    total = blocks[-1]
+    for block in blocks[-2::-1]:
+        total = jax.tree.map(lambda a, b: add_rounded(step_down(a), b), total, block)
+    return total
+
+
+def butterfly_sum(values):
+    count = lax.axis_size("col")
+    values = values + step_x(values)
+    values = values + step_y(values)
+    step = 1
+    while step < count:
+        values = values + lax.ppermute(values, "col", [(i, i ^ step) for i in range(count)])
+        step *= 2
+    return values
+
+
+def picked(stacked, index):
+    return lax.dynamic_index_in_dim(stacked, index, 0, keepdims=False)
+
+
+def exchanged(values, index, axis):
+    size = values.shape[axis] // 4
+    return jnp.concatenate(
+        [
+            lax.dynamic_slice_in_dim(values, jnp.bitwise_xor(index, i) * size, size, axis=axis)
+            for i in range(4)
+        ],
+        axis=axis,
+    )
+
+
+def row_norm(values):
+    average = jnp.mean(values, axis=1, keepdims=True)
+    centered = values - average
+    inverse = lax.rsqrt(jnp.mean(centered * centered, axis=1, keepdims=True) + norm_eps)
+    return (average, inverse)
+
+
+def mm(left, right, left_dim, right_dim, dtype=jnp.float32):
+    return lax.dot_general(
+        left, right, (((left_dim,), (right_dim,)), ((), ())), preferred_element_type=jnp.float32
+    ).astype(dtype)
+
+
+PAIR = 2 * HEAD_DIM
+vmem_bytes = 48 * 1024 * 1024
+
+
+def head_lanes(head, value):
+    lane = lax.broadcasted_iota(jnp.int32, (1, PAIR), 1)
+    return jnp.where(lane // HEAD_DIM == head, value, 0.0).astype(jnp.bfloat16)
+
+
+def allowed_keys(first_row, low, high):
+    key_pos = lax.broadcasted_iota(jnp.int32, (high, high - low), 0)
+    query_pos = lax.broadcasted_iota(jnp.int32, (high, high - low), 1) + low
+    return (key_pos >= first_row) & (key_pos <= query_pos)
+
+
+def local_forward_kernel(size, first_ref, query_ref, key_ref, value_ref, out_ref):
+    lane = lax.broadcasted_iota(jnp.int32, (size, PAIR), 1)
+    for low in range(0, key_ref.shape[0], size):
+        high = low + size
+        keys = key_ref[:high, :]
+        values = value_ref[:high, :]
+        queries = query_ref[low:high, :]
+        allowed = allowed_keys(first_ref[:, low:high], low, high)
+        results = []
+        for head in range(2):
+            scores = mm(keys, queries * head_lanes(head, HEAD_DIM ** (-0.5)), 1, 1)
+            scores = jnp.where(allowed, scores, masked_fill)
+            exp_scores = jnp.exp(scores - jnp.max(scores, axis=0, keepdims=True))
+            inverse = 1.0 / jnp.sum(exp_scores, axis=0, keepdims=True)
+            results.append(mm((exp_scores * inverse).astype(jnp.bfloat16), values, 0, 0))
+        out_ref[low:high, :] = jnp.where(lane < HEAD_DIM, results[0], results[1]).astype(
+            jnp.bfloat16
+        )
+
+
+def local_forward(heads, first_row):
+    length = heads.shape[0]
+    pairs = heads.shape[1] // (3 * PAIR)
+    return pl.pallas_call(
+        functools.partial(local_forward_kernel, min(256, length)),
+        grid=(pairs,),
+        in_specs=[
+            pl.BlockSpec((1, length), lambda p: (0, 0)),
+            pl.BlockSpec((length, PAIR), lambda p: (0, p)),
+            pl.BlockSpec((length, PAIR), lambda p: (0, pairs + p)),
+            pl.BlockSpec((length, PAIR), lambda p: (0, 2 * pairs + p)),
+        ],
+        out_specs=pl.BlockSpec((length, PAIR), lambda p: (0, p)),
+        out_shape=jax.ShapeDtypeStruct((length, pairs * PAIR), jnp.bfloat16),
+        compiler_params=pltpu.CompilerParams(vmem_limit_bytes=vmem_bytes),
+        cost_estimate=pl.CostEstimate(
+            flops=16 * length * length * pairs * PAIR, bytes_accessed=8 * heads.size, transcendentals=0
+        ),
+    )(first_row, heads, heads, heads)
+
+
+def local_backward_kernel(
+    size, first_ref, query_ref, grad_ref, key_ref, value_ref, out_ref, key_sum, value_sum
+):
+    length = key_ref.shape[0]
+    pair = pl.program_id(0)
+    pairs = out_ref.shape[1] // (3 * PAIR)
+    scale = HEAD_DIM ** (-0.5)
+    lane = lax.broadcasted_iota(jnp.int32, (size, PAIR), 1)
+
+    def lanes(part):
+        return pl.ds(pl.multiple_of((part * pairs + pair) * PAIR, PAIR), PAIR)
+
+    for low in range(length - size, -1, -size):
+        high = low + size
+        keys = key_ref[:high, :]
+        values = value_ref[:high, :]
+        queries = query_ref[low:high, :]
+        grads = grad_ref[low:high, :]
+        allowed = allowed_keys(first_ref[:, low:high], low, high)
+        query_grads = []
+        for head in range(2):
+            scaled = queries * head_lanes(head, scale)
+            grad = grads * head_lanes(head, 1.0)
+            scores = jnp.where(allowed, mm(keys, scaled, 1, 1), masked_fill)
+            exp_scores = jnp.exp(scores - jnp.max(scores, axis=0, keepdims=True))
+            probs = exp_scores * (1.0 / jnp.sum(exp_scores, axis=0, keepdims=True))
+            prob_grad = mm(values, grad, 1, 1)
+            row_dot = jnp.sum(probs * prob_grad, axis=0, keepdims=True)
+            score_grad = (probs * (prob_grad - row_dot)).astype(jnp.bfloat16)
+            value_part = mm(probs.astype(jnp.bfloat16), grad, 1, 0)
+            key_part = mm(score_grad, scaled, 1, 0)
+            query_grads.append(mm(score_grad, keys, 0, 0) * scale)
+            if head == 0:
+                key_add, value_add = key_part, value_part
+            else:
+                key_add, value_add = key_add + key_part, value_add + value_part
+        if high == length:
+            key_sum[...] = key_add
+            value_sum[...] = value_add
+        else:
+            key_sum[:high, :] += key_add
+            value_sum[:high, :] += value_add
+        out_ref[low:high, lanes(0)] = jnp.where(
+            lane < HEAD_DIM, query_grads[0], query_grads[1]
+        ).astype(jnp.bfloat16)
+    out_ref[:, lanes(1)] = key_sum[...].astype(jnp.bfloat16)
+    out_ref[:, lanes(2)] = value_sum[...].astype(jnp.bfloat16)
+
+
+def local_backward(heads, head_grad, first_row):
+    length = heads.shape[0]
+    pairs = heads.shape[1] // (3 * PAIR)
+    return pl.pallas_call(
+        functools.partial(local_backward_kernel, min(512, length)),
+        grid=(pairs,),
+        in_specs=[
+            pl.BlockSpec((1, length), lambda p: (0, 0)),
+            pl.BlockSpec((length, PAIR), lambda p: (0, p)),
+            pl.BlockSpec((length, PAIR), lambda p: (0, p)),
+            pl.BlockSpec((length, PAIR), lambda p: (0, pairs + p)),
+            pl.BlockSpec((length, PAIR), lambda p: (0, 2 * pairs + p)),
+        ],
+        out_specs=pl.BlockSpec(heads.shape, lambda p: (0, 0)),
+        out_shape=jax.ShapeDtypeStruct(heads.shape, jnp.bfloat16),
+        scratch_shapes=[pltpu.VMEM((length, PAIR), jnp.float32)] * 2,
+        compiler_params=pltpu.CompilerParams(vmem_limit_bytes=vmem_bytes),
+        cost_estimate=pl.CostEstimate(
+            flops=32 * length * length * pairs * PAIR, bytes_accessed=8 * heads.size, transcendentals=0
+        ),
+    )(first_row, heads, head_grad, heads, heads)
+
+
+def token_products_kernel(*refs):
+    out_ref = refs[-1]
+    count = (len(refs) - 1) // 2
+    total = mm(refs[0][...], refs[count][...], 0, 0)
+    for i in range(1, count):
+        total += mm(refs[i][...], refs[count + i][...], 0, 0)
+    out_ref[...] = total.astype(out_ref.dtype)
+
+
+def token_products(lefts, rights):
+    tokens, left_width = lefts[0].shape
+    right_width = rights[0].shape[1]
+    size = min(256, left_width)
+    count = len(lefts)
+    flops = 2 * count * tokens * left_width * right_width
+    return pl.pallas_call(
+        token_products_kernel,
+        grid=(left_width // size,),
+        in_specs=[pl.BlockSpec((tokens, size), lambda i: (0, i))] * count
+        + [pl.BlockSpec((tokens, right_width), lambda i: (0, 0))] * count,
+        out_specs=pl.BlockSpec((size, right_width), lambda i: (i, 0)),
+        out_shape=jax.ShapeDtypeStruct((left_width, right_width), jnp.bfloat16),
+        compiler_params=pltpu.CompilerParams(vmem_limit_bytes=vmem_bytes),
+        cost_estimate=pl.CostEstimate(
+            flops=flops, bytes_accessed=2 * count * tokens * (left_width + right_width), transcendentals=0
+        ),
+    )(*lefts, *rights)
+
+
+def body_local(
+    tokens_in,
+    out_grad,
+    segment_ids,
+    active_lengths,
+    norm1_gain,
+    norm1_shift,
+    query_weight,
+    query_bias,
+    key_weight,
+    value_weight,
+    value_bias,
+    out_weight,
+    out_bias,
+    norm2_gain,
+    norm2_shift,
+    up_weight,
+    up_bias,
+    down_weight,
+    down_bias,
+):
+    f32, bf16 = jnp.float32, jnp.bfloat16
+    rows, width = tokens_in.shape
+    ring = lax.axis_size("col")
+    row_i = lax.axis_index("row")
+    plane_i = lax.axis_index("dp")
+    col_i = lax.axis_index("col")
+    own = query_weight.shape[1] // 2
+    block = width // 4
+    quarter = up_weight.shape[1] // 4
+    unit = quarter // 2
+
+    def by_core(weight, size, offset=0):
+        return [
+            lax.dynamic_slice_in_dim(weight, offset + which * size, size, axis=1)
+            for which in (row_i, 1 - row_i)
+        ]
+
+    four = [by_core(w, own) for w in (query_weight, key_weight, value_weight, out_weight.T)]
+    four = jnp.concatenate([w[0] for w in four] + [w[1] for w in four], axis=1)
+    four = exchanged(four, plane_i, 0)
+
+    tokens_sib = swap(tokens_in)
+
+    ff_offset = plane_i * quarter
+    up_piece = jnp.concatenate(by_core(up_weight, unit, ff_offset), axis=1)
+    down_piece = jnp.concatenate(
+        [
+            lax.dynamic_slice_in_dim(down_weight, ff_offset + which * unit, unit, axis=0)
+            for which in (row_i, 1 - row_i)
+        ],
+        axis=0,
+    )
+
+    active_all = active_rows(segment_ids, active_lengths)
+    active_here = lax.dynamic_slice_in_dim(active_all, col_i * rows, rows)
+    keep_mask = active_here.astype(f32)[:, None]
+    segment_row = picked(segment_ids, col_i)
+    member = (segment_row[:, None] == jnp.arange(active_lengths.shape[1])).astype(jnp.int32)
+    counts = jnp.sum(member, axis=0)
+    first_row = jnp.sum(member * (jnp.cumsum(counts) - counts), axis=1)[None, :]
+
+    branch_mine = (out_grad.astype(f32) * keep_mask).astype(bf16)
+
+    query_part = lax.dynamic_slice_in_dim(query_bias, row_i * own, own)
+    value_part = lax.dynamic_slice_in_dim(value_bias, row_i * own, own)
+    up_part = lax.dynamic_slice_in_dim(up_bias, ff_offset + row_i * unit, unit)
+    small = ring_gather(
+        jnp.concatenate([query_part, jnp.zeros_like(query_part), value_part, up_part])
+    )
+    up_biases = jnp.concatenate([s[3 * own :] for s in small])
+
+    pieces = ring_gather(four[:block])
+    own_rows, other_units = [four[:, : 4 * own]], [four[:, 4 * own :]]
+    for piece in pieces[1:]:
+        gathered = plane_gather(piece)
+        own_rows.append(jnp.concatenate([p[:, : 4 * own] for p in gathered], axis=0))
+        other_units.append(jnp.concatenate([p[:, 4 * own :] for p in gathered], axis=0))
+    groups = [jnp.concatenate([a, swap(b)], axis=0) for a, b in zip(own_rows, other_units)]
+
+    gains = jnp.stack([norm1_gain, norm1_shift])
+    gains_sib = swap(gains)
+    tokens_own = tokens_in.astype(f32)
+    tokens_all = jnp.concatenate([tokens_own, tokens_sib.astype(f32)], axis=1)
+    average_one, inverse_one = row_norm(tokens_all)
+    normed_one = jnp.concatenate(
+        [
+            exchanged(
+                (((t - average_one) * inverse_one) * g[0] + g[1]).astype(bf16), plane_i, 1
+            )
+            for t, g in ((tokens_own, gains), (tokens_sib.astype(f32), gains_sib))
+        ],
+        axis=1,
+    )
+    heads, attended = [], []
+    attention_rows = None
+    for k in range(ring):
+        weights = groups[k]
+        head = (mm(normed_one, weights[:, : 3 * own], 1, 0) + small[k][: 3 * own]).astype(bf16)
+        result = local_forward(head, first_row)
+        heads.append(head)
+        attended.append(result)
+        both = jnp.concatenate([result, swap(result)], axis=1)
+        out_both = jnp.concatenate([own_rows[k][:, 3 * own :], other_units[k][:, 3 * own :]], axis=1)
+        part = mm(both, out_both, 1, 1)
+        attention_rows = part if k == 0 else attention_rows + part
+    hidden_one = tokens_own + exchanged(attention_rows, plane_i, 1) + out_bias
+
+    def both_sums(one, two):
+        sums = jnp.stack([jnp.sum(one, axis=1), jnp.sum(two, axis=1)])
+        sums = (sums + swap(sums)) / (2 * width)
+        return sums[0][:, None], sums[1][:, None]
+
+    half_mean = jnp.mean(hidden_one, axis=1, keepdims=True)
+    centered = hidden_one - half_mean
+    half_square = jnp.mean(centered * centered, axis=1, keepdims=True)
+    half_stats = jnp.concatenate([half_mean, half_square], axis=1).T
+    other_stats = swap(half_stats)
+    gap = half_stats[0] - other_stats[0]
+    average_two = (0.5 * (half_stats[0] + other_stats[0]))[:, None]
+    variance_two = (0.5 * (half_stats[1] + other_stats[1]) + 0.25 * gap * gap)[:, None]
+    inverse_two = lax.rsqrt(variance_two + norm_eps)
+    normal_two = (hidden_one - average_two) * inverse_two
+    normed_two = (normal_two * norm2_gain + norm2_shift).astype(bf16)
+
+    ff_pieces = ring_gather((up_piece, down_piece))
+    up_own = jnp.concatenate([p[0][:, :unit] for p in ff_pieces], axis=1)
+    up_sib = jnp.concatenate([p[0][:, unit:] for p in ff_pieces], axis=1)
+    down_own = jnp.concatenate([p[1][:unit] for p in ff_pieces], axis=0)
+    down_sib = jnp.concatenate([p[1][unit:] for p in ff_pieces], axis=0)
+    up_full = jnp.concatenate([up_own, swap(up_sib)], axis=0)
+    down_full = jnp.concatenate([down_own, swap(down_sib)], axis=1)
+    up_half = jnp.concatenate([up_own, up_sib], axis=1)
+    down_half = jnp.concatenate([down_own, down_sib], axis=0)
+
+    def gathered_tokens(values):
+        here, from_x, from_y, far_one, far_two = plane_gather(values)
+        own_parts = [here, from_x, from_y, jnp.concatenate([far_one, far_two], axis=0)]
+        return own_parts, [jnp.concatenate([p, swap(p)], axis=1) for p in own_parts]
+
+    branch_own, branch_all = gathered_tokens(branch_mine)
+    normed_own, normed_all = gathered_tokens(normed_two)
+    half_rows = rows // 2
+    acts, act_sibs, pre_grads, pre_sibs, grad_parts, down_parts = [], [], [], [], [], []
+    for j in range(4):
+        pre_act = mm(normed_all[j], up_full, 1, 0) + up_biases
+        act = gelu_value(pre_act).astype(bf16)
+        pre_grad = (mm(branch_all[j], down_full, 1, 1) * gelu_slope(pre_act)).astype(bf16)
+        acts.append(act)
+        pre_grads.append(pre_grad)
+        pre_sibs.append(swap(pre_grad))
+        act_sibs.append(swap(act))
+        chip = jnp.concatenate([pre_grad, pre_sibs[j]], axis=1)
+        grad_parts.append(mm(chip, up_half, 1, 1, bf16))
+    normed_grad_two = jnp.concatenate(
+        plane_sum([[g[:half_rows] for g in grad_parts], [g[half_rows:] for g in grad_parts]]), axis=0
+    )
+    for j in range(4):
+        chip = jnp.concatenate([acts[j], act_sibs[j]], axis=1)
+        down_parts.append(mm(chip, down_half, 1, 0, bf16))
+    up_grads = (token_products(normed_own, pre_grads), token_products(normed_own, pre_sibs))
+    down_grads = (token_products(acts, branch_own), token_products(act_sibs, branch_own))
+
+    scaled = normed_grad_two * norm2_gain
+    mean_one, mean_two = both_sums(scaled, scaled * normal_two)
+    hidden_grad = branch_mine.astype(f32) + inverse_two * (scaled - mean_one - normal_two * mean_two)
+    attention_grad = hidden_grad.astype(bf16)
+    gain_two_grad = jnp.sum(normed_grad_two * normal_two, axis=0)
+    shift_two_grad = jnp.sum(normed_grad_two, axis=0)
+
+    grad_blocks = exchanged(attention_grad, plane_i, 1)
+    grad_blocks = jnp.concatenate([grad_blocks, swap(grad_blocks)], axis=1)
+    reduced = [None] * ring
+    normed_grad_one = None
+    bias_rows = [None] * ring
+    for k in range(ring - 1, -1, -1):
+        weights = groups[k]
+        head_grad = mm(grad_blocks, weights[:, 3 * own :], 1, 0, bf16)
+        grads = local_backward(heads[k], head_grad, first_row)
+        part = mm(grads, weights[:, : 3 * own], 1, 1)
+        normed_grad_one = part if normed_grad_one is None else normed_grad_one + part
+        weight_grads = jnp.concatenate(
+            [mm(normed_one, grads, 0, 0, bf16), mm(grad_blocks, attended[k], 0, 0, bf16)], axis=1
+        )
+        mine = weight_grads[:width]
+        arrived = swap(weight_grads[width:])
+        reduced[k] = [
+            r.astype(bf16)
+            for r in plane_sum(
+                [[m[j * block : (j + 1) * block] for j in range(4)] for m in (mine, arrived)]
+            )
+        ]
+        bias_rows[k] = jnp.sum(grads.astype(f32), axis=0)
+    head_sum = ring_sum(reduced)
+    head_mine, head_sib = [
+        exchanged(jnp.concatenate(plane_gather(h), axis=0), plane_i, 0) for h in head_sum
+    ]
+
+    def by_row(mine, sib, axis):
+        return jnp.where(
+            row_i == 0,
+            jnp.concatenate([mine, sib], axis=axis),
+            jnp.concatenate([sib, mine], axis=axis),
+        )
+
+    query_weight_grad, key_weight_grad, value_weight_grad, out_weight_grad = [
+        by_row(head_mine[:, m * own : (m + 1) * own], head_sib[:, m * own : (m + 1) * own], 1).astype(f32)
+        for m in range(4)
+    ]
+    out_weight_grad = out_weight_grad.T
+
+    ffn_rows = plane_sum([[d[:half_rows] for d in down_parts], [d[half_rows:] for d in down_parts]])
+    ffn_rows = jnp.concatenate(ffn_rows, axis=0) + down_bias
+    layer_out = jnp.where(active_here[:, None], hidden_one + ffn_rows, tokens_own)
+    ff_sums = ring_sum(
+        [
+            (
+                up_grads[0][:, k * unit : (k + 1) * unit],
+                up_grads[1][:, k * unit : (k + 1) * unit],
+                down_grads[0][k * unit : (k + 1) * unit],
+                down_grads[1][k * unit : (k + 1) * unit],
+            )
+            for k in range(ring)
+        ]
+    )
+    ff_gathered = []
+    for total in ff_sums:
+        here, from_x, from_y, far_one, far_two = plane_gather(total)
+        ff_gathered.append(jnp.stack([here, from_x, from_y, jnp.concatenate([far_one, far_two])]))
+
+    def placed(mine, sib, axis):
+        return jnp.concatenate(
+            [by_row(picked(mine, plane_i ^ q), picked(sib, plane_i ^ q), axis) for q in range(4)], axis=axis
+        ).astype(f32)
+
+    up_weight_grad = placed(ff_gathered[0], ff_gathered[1], 1)
+    down_weight_grad = placed(ff_gathered[2], ff_gathered[3], 0)
+
+    normed_grad_one = normed_grad_one[:, :width] + swap(
+        normed_grad_one[:, width:].astype(bf16)
+    ).astype(f32)
+    normed_grad_one = exchanged(normed_grad_one, plane_i, 1)
+    normal_own = (tokens_own - average_one) * inverse_one
+    scaled = normed_grad_one * norm1_gain
+    mean_one, mean_two = both_sums(scaled, scaled * normal_own)
+    back_one = inverse_one * (scaled - mean_one - normal_own * mean_two)
+    gain_one_grad = jnp.sum(normed_grad_one * normal_own, axis=0)
+    shift_one_grad = jnp.sum(normed_grad_one, axis=0)
+    input_grad = out_grad.astype(f32) * (1.0 - keep_mask) + hidden_grad + back_one
+
+    def by_column(relative):
+        index = jnp.mod(col_i - jnp.arange(ring), ring)
+        return jnp.take(relative, index, axis=0)
+
+    row_hot = (jnp.arange(2) == row_i).astype(f32)
+    plane_hot = (jnp.arange(4) == plane_i).astype(f32)
+    head_bias = by_column(jnp.stack(bias_rows)).reshape(ring, 3, 1, own) * row_hot[:, None]
+    up_bias_part = sum(jnp.sum(p.astype(f32), axis=0) for p in pre_grads).reshape(ring, unit)
+    up_bias_part = by_column(up_bias_part).reshape(ring, 1, 1, unit)
+    up_bias_part = up_bias_part * plane_hot[:, None, None] * row_hot[:, None]
+    bias_vector = jnp.concatenate([head_bias.reshape(ring, -1), up_bias_part.reshape(ring, -1)], axis=1)
+    bias_vector = bias_vector + swap(bias_vector)
+    out_bias_part = jnp.sum(attention_grad.astype(f32), axis=0)
+    down_bias_part = jnp.sum(branch_mine.astype(f32), axis=0)
+    own_vector = jnp.concatenate(
+        [gain_one_grad, shift_one_grad, gain_two_grad, shift_two_grad, out_bias_part, down_bias_part]
+    )
+    summed = butterfly_sum(jnp.concatenate([bias_vector.reshape(-1), own_vector]))
+    bias_here = picked(summed[: bias_vector.size].reshape(ring, -1), col_i)
+    own_here = summed[bias_vector.size :].reshape(6, width)
+    size = 2 * own
+    return (
+        layer_out,
+        input_grad,
+        own_here[0],
+        own_here[1],
+        query_weight_grad,
+        bias_here[:size],
+        key_weight_grad,
+        value_weight_grad,
+        bias_here[2 * size : 3 * size],
+        out_weight_grad,
+        own_here[4],
+        own_here[2],
+        own_here[3],
+        up_weight_grad,
+        bias_here[3 * size :],
+        down_weight_grad,
+        own_here[5],
+    )
+
+
+def body(tokens_in, out_grad, segment_ids, *rest):
+    ring = lax.axis_size("col")
+    local = (
+        lax.axis_size("dp") == 4
+        and lax.axis_size("row") == 2
+        and ring & (ring - 1) == 0
+        and tokens_in.shape[0] == segment_ids.shape[1]
+    )
+    chosen = body_local if local else body_general
+    return chosen(tokens_in, out_grad, segment_ids, *rest)
+
+
 def solution(mesh):
     placed = (
         P(("dp", "col"), "row"),

time: 3000 us -> 1310 us (0.44)
  waiting for transfers between devices: 2210 us -> 489 us
  starting transfers between devices: 0.92 us -> 137 us
  Pallas kernels: 0 us -> 132 us
  blocking collectives: 105 us -> 0 us
  matrix products: 357 us -> 256 us
  other arithmetic: 164 us -> 121 us
    reduce_scatter x8 -> x0, waiting for transfers between devices: 1190 us -> none  [the longest x4 1080 us: token_sums(): lax.psum_scatter(partial_rows, 'col', scatter_dimension=0, tiled=True)]
    all_gather x8 -> x0, waiting for transfers between devices: 618 us -> none  [the longest x4 563 us: token_gather(): return lax.all_gather(values, 'col', axis=0, tiled=True)]
    ppermute x0 -> x152, waiting for transfers between devices: none -> 489 us  [the longest x41 229 us: step_y(): return lax.ppermute(values, 'dp', [(0, 2), (2, 0), (1, 3), (3, 1)])]
    psum x1 -> x0, waiting for transfers between devices: 393 us -> none  [body(): lax.psum((stacked_weight_grad, query_bias_grad, value_bias_grad, out_weig...]
    ppermute x0 -> x152, starting transfers between devices: none -> 137 us  [the longest x41 49.6 us: step_y(): return lax.ppermute(values, 'dp', [(0, 2), (2, 0), (1, 3), (3, 1)])]
    pallas_call x0 -> x12, Pallas kernels: none -> 132 us  [the longest x4 55.2 us: token_products(): pl.pallas_call(token_products_kernel, grid=(left_width // size,), in_spec...]
    psum x6 -> x0, blocking collectives: 105 us -> none  [the longest x1 76.9 us: body(): lax.psum((gain_one_grad, shift_one_grad, gain_two_grad, shift_two_grad),...]
    dot_general x68 -> x40, matrix products: 357 us -> 256 us  [mm(): lax.dot_general(left, right, (((left_dim,), (right_dim,)), ((), ())), pre...]
  transfers between devices with their start and end apart: 17 -> 152, of which waited for: 16 -> 51; matrix products, arithmetic and copies ran while one was open for 8% -> 34% of each run, Pallas kernels for 0% -> 6%
where the time goes in v2:
time: 1310 us; the launch traced here: 1300 us
  waiting for transfers between devices  489 us (37%)
  matrix products  256 us (20%)
  local copies, waits for them, and re-layouts  164 us (13%)
  starting transfers between devices  137 us (10%)
  Pallas kernels  132 us (10%)
  other arithmetic  121 us (9%)
    dot_general x40, matrix products, mm(): lax.dot_general(left, right, (((left_dim,), (right_dim,)), ((), ())), pre...  256 us
    ppermute x41, waiting for transfers between devices, step_y(): return lax.ppermute(values, 'dp', [(0, 2), (2, 0), (1, 3), (3, 1)])  229 us
    ppermute x41, waiting for transfers between devices, step_x(): return lax.ppermute(values, 'dp', [(0, 1), (1, 0), (2, 3), (3, 2)])  120 us
    unnamed x415, local copies, waits for them, and re-layouts  87 us
    ppermute x12, waiting for transfers between devices, step_up(): lax.ppermute(values, 'col', [(i, (i + 1) % count) for i in range(count)])  77.5 us
    ppermute x18, waiting for transfers between devices, step_down(): lax.ppermute(values, 'col', [(i, (i - 1) % count) for i in range(count)])  59.8 us
    pallas_call x4, Pallas kernels, token_products(): pl.pallas_call(token_products_kernel, grid=(left_width // size,), in_spec...  55.2 us
    pallas_call x4, Pallas kernels, local_backward(): pl.pallas_call(functools.partial(local_backward_kernel, min(512, length))...  50.5 us
  transfers between devices with their start and end apart: 152, of which 51 were waited for; matrix products, arithmetic and copies ran while one was open for 34% of the time, Pallas kernels for 6%

profile of v2, /device:TPU:0, one launch (start us, length us, event | category | flops | bytes accessed | tf_op | source)
XLA Modules:
  0.0 1302.6 jit_solution(14085969653654343679)
XLA Ops:
  47.1 10.1 collective-permute-done.4
  66.3 15.7 %collective-permute-done.6 = bf16[256,2048]{0,1:T(8,128)(2,1)S(1)} collective-permute-done((bf16[256,2048]{0,1:T(8,128)(2,1)}, bf16[256,2048]{0,1:T(8,128)(2,1)S(1)}, u32[]{:S(2)}, u32[]{:S(2)}) %collective-permute-start.6) | collective-permute-done | bytes 1048608 | tf_op jit(solution)/shard_map/ppermute | solution.py:353
  97.9 6.5 shard_map.314
  113.0 14.7 %collective-permute-done.14 = bf16[256,2048]{0,1:T(8,128)(2,1)S(1)} collective-permute-done((bf16[256,2048]{0,1:T(8,128)(2,1)}, bf16[256,2048]{0,1:T(8,128)(2,1)S(1)}, u32[]{:S(2)}, u32[]{:S(2)}) %collective-permute-start.14) | collective-permute-done | bytes 1048608 | tf_op jit(solution)/shard_map/ppermute | solution.py:353
  135.9 7.9 collective-permute-done.15
  146.0 15.6 %collective-permute-done.22 = bf16[256,2048]{0,1:T(8,128)(2,1)S(1)} collective-permute-done((bf16[256,2048]{0,1:T(8,128)(2,1)S(1)}, bf16[256,2048]{0,1:T(8,128)(2,1)S(1)}, u32[]{:S(2)}, u32[]{:S(2)}) %collective-permute-start.22) | collective-permute-done | bytes 1048608 | tf_op jit(solution)/shard_map/ppermute | solution.py:353
  167.8 10.8 collective-permute-done.23
  192.4 6.5 shard_map.315
  207.4 6.7 shard_map.316
  222.7 6.5 shard_map.317
  255.7 13.0 %collective-permute-done.35 = bf16[512,1024]{1,0:T(8,128)(2,1)} collective-permute-done((bf16[512,1024]{1,0:T(8,128)(2,1)S(1)}, bf16[512,1024]{1,0:T(8,128)(2,1)}, u32[]{:S(2)}, u32[]{:S(2)}) %collective-permute-start.35) | collective-permute-done | bytes 1048608 | tf_op jit(solution)/shard_map/ppermute | solution.py:358
  269.3 21.9 %collective-permute-done.31 = bf16[1024,512]{1,0:T(8,128)(2,1)} collective-permute-done((bf16[1024,512]{1,0:T(8,128)(2,1)}, bf16[1024,512]{1,0:T(8,128)(2,1)}, u32[]{:S(2)}, u32[]{:S(2)}) %collective-permute-start.31) | collective-permute-done | bytes 1048608 | tf_op jit(solution)/shard_map/ppermute | solution.py:358
  305.9 7.7 collective-permute-done.36
  315.4 20.2 %collective-permute-done.32 = bf16[1024,512]{1,0:T(8,128)(2,1)S(1)} collective-permute-done((bf16[1024,512]{1,0:T(8,128)(2,1)}, bf16[1024,512]{1,0:T(8,128)(2,1)S(1)}, u32[]{:S(2)}, u32[]{:S(2)}) %collective-permute-start.32) | collective-permute-done | bytes 1048608 | tf_op jit(solution)/shard_map/ppermute | solution.py:358
  345.8 21.8 %collective-permute-done.64 = bf16[512,1024]{1,0:T(8,128)(2,1)S(1)} collective-permute-done((bf16[512,1024]{1,0:T(8,128)(2,1)S(1)}, bf16[512,1024]{1,0:T(8,128)(2,1)S(1)}, u32[]{:S(2)}, u32[]{:S(2)}) %collective-permute-start.64) | collective-permute-done | bytes 1048608 | tf_op jit(solution)/shard_map/ppermute | solution.py:353
  371.3 16.2 %collective-permute-done.45 = bf16[512,1024]{1,0:T(8,128)(2,1)S(1)} collective-permute-done((bf16[512,1024]{1,0:T(8,128)(2,1)S(1)}, bf16[512,1024]{1,0:T(8,128)(2,1)S(1)}, u32[]{:S(2)}, u32[]{:S(2)}) %collective-permute-start.45) | collective-permute-done | bytes 1048608 | tf_op jit(solution)/shard_map/ppermute | solution.py:353
  398.6 8.2 fusion.54
  407.3 11.4 convert_reduce_fusion.3
  419.0 8.3 fusion.46
  427.5 11.6 convert_reduce_fusion.4
  439.4 6.9 fusion.62
  446.3 11.0 convert_reduce_fusion.2
  457.6 25.6 %multiply_convert_fusion.3 = (bf16[1024,1024]{1,0:T(8,128)(2,1)}, bf16[1024,1024]{1,0:T(8,128)(2,1)}, bf16[1024,1024]{1,0:T(8,128)(2,1)}, bf16[1024,1024]{1,0:T(8,128)(2,1)}, f32[1024,1024]{1,0:T(8,128)}) fusion(f32[1024]{0:T(1024)S(1)} %pad_maximum_fusion.37, f32[1024,1024]{1,0:T(8,128)} %fusion.62, f32[1024,1024]{1,0:T(8,128)} %fusion.54, ...), kind=kOutput, calls=%fused_computation.145 | convolution fusion | flops 4366270464 | bytes 33558528 | tf_op jit(solution)/shard_map/dot_general | solution.py:442
  483.2 12.2 convert_reduce_fusion.5
  495.4 13.7 %shard_map.322 = bf16[1024,1024]{1,0:T(8,128)(2,1)S(1)} custom-call(bf16[1024,1024]{1,0:T(8,128)(2,1)S(1)} %add_convert_fusion.refs_0_, bf16[1024,1024]{1,0:T(8,128)(2,1)} %copy-done.111, bf16[1024,1024]{1,0:T(8,128)(2,1)} %copy-done.112, bf16[1024,1024]{1,0:T(8,128)(2,1)} %copy-done.114, bf16[1024,1024]{1,0:T(8,128)(2,1)} %get-tuple-element.278.refs_4_, ...), custom_call_target="tpu_custom_call" | custom-call | flops 8589934592 | bytes 16777216 | tf_op jit(solution)/shard_map/pallas_call | solution.py:590
  516.1 13.7 %shard_map.324 = bf16[1024,1024]{1,0:T(8,128)(2,1)S(1)} custom-call(bf16[1024,1024]{1,0:T(8,128)(2,1)S(1)} %copy-done.8, bf16[1024,1024]{1,0:T(8,128)(2,1)} %get-tuple-element.271.refs_1_, bf16[1024,1024]{1,0:T(8,128)(2,1)} %get-tuple-element.270.refs_2_, bf16[1024,1024]{1,0:T(8,128)(2,1)} %get-tuple-element.269.refs_3_, ...), custom_call_target="tpu_custom_call" | custom-call | flops 8589934592 | bytes 16777216 | tf_op jit(solution)/shard_map/pallas_call | solution.py:590
  534.5 11.8 collective-permute-done.138
  549.9 7.2 fusion.136
  561.3 9.1 collective-permute-done.139
  574.7 7.2 fusion.139
  587.0 8.3 collective-permute-done.140
  599.4 13.7 %shard_map.323 = bf16[1024,1024]{1,0:T(8,128)(2,1)S(1)} custom-call(bf16[1024,1024]{1,0:T(8,128)(2,1)S(1)} %add_convert_fusion.refs_0_, bf16[1024,1024]{1,0:T(8,128)(2,1)} %copy-done.111, bf16[1024,1024]{1,0:T(8,128)(2,1)} %copy-done.112, bf16[1024,1024]{1,0:T(8,128)(2,1)} %copy-done.114, bf16[1024,1024]{1,0:T(8,128)(2,1)} %copy-done.169, ...), custom_call_target="tpu_custom_call" | custom-call | flops 8589934592 | bytes 16777216 | tf_op jit(solution)/shard_map/pallas_call | solution.py:590
  614.3 7.9 fusion.148
  623.6 7.9 fusion.151
  638.5 14.1 %shard_map.325 = bf16[1024,1024]{1,0:T(8,128)(2,1)S(1)} custom-call(bf16[1024,1024]{1,0:T(8,128)(2,1)S(1)} %collective-permute-done.34.refs_0_, bf16[1024,1024]{1,0:T(8,128)(2,1)} %collective-permute-done.40.refs_1_, bf16[1024,1024]{1,0:T(8,128)(2,1)} %collective-permute-done.44.refs_2_, bf16[1024,1024]{1,0:T(8,128)(2,1)} %collective-permute-done.48.refs_3_, ...), custom_call_target="tpu_custom_call" | custom-call | flops 8589934592 | bytes 16777216 | tf_op jit(solution)/shard_map/pallas_call | solution.py:590
  652.7 8.1 fusion.133
  666.6 8.0 fusion.154
  674.5 7.9 fusion.145
  691.5 21.0 %collective-permute-done.130 = bf16[512,256]{1,0:T(8,128)(2,1)S(1)} collective-permute-done((bf16[512,256]{1,0:T(8,128)(2,1)S(1)}, bf16[512,256]{1,0:T(8,128)(2,1)S(1)}, u32[]{:S(2)}, u32[]{:S(2)}) %collective-permute-start.130) | collective-permute-done | bytes 262176 | tf_op jit(solution)/shard_map/ppermute | solution.py:349
  717.8 8.3 collective-permute-done.132
  732.2 8.8 collective-permute-done.146
  742.9 6.5 collective-permute-done.133
  766.7 8.9 collective-permute-done.135
  787.7 24.9 %collective-permute-done.134 = bf16[1024,256]{1,0:T(8,128)(2,1)} collective-permute-done((bf16[1024,256]{1,0:T(8,128)(2,1)}, bf16[1024,256]{1,0:T(8,128)(2,1)}, u32[]{:S(2)}, u32[]{:S(2)}) %collective-permute-start.134) | collective-permute-done | bytes 524320 | tf_op jit(solution)/shard_map/ppermute | solution.py:349
  815.7 11.7 collective-permute-done.149
  840.4 40.4 %collective-permute-done.148 = bf16[256,1024]{1,0:T(8,128)(2,1)S(1)} collective-permute-done((bf16[256,1024]{1,0:T(8,128)(2,1)S(1)}, bf16[256,1024]{1,0:T(8,128)(2,1)S(1)}, u32[]{:S(2)}, u32[]{:S(2)}) %collective-permute-start.148) | collective-permute-done | bytes 524320 | tf_op jit(solution)/shard_map/ppermute | solution.py:349
  887.3 7.2 convert_reduce_fusion.1
  915.0 9.2 copy.123
  948.9 12.5 shard_map.319
  976.0 12.5 shard_map.318
  988.9 7.3 convolution_convert_fusion.3
  1001.8 12.6 shard_map.320
  1022.2 12.8 shard_map.321
  1055.3 15.5 %add_add_fusion = f32[1024,2048]{1,0:T(8,128)} fusion(f32[1024,2048]{1,0:T(8,128)} %fusion.113, f32[1024,2048]{1,0:T(8,128)} %fusion.105, f32[1024,2048]{1,0:T(8,128)} %fusion.109, bf16[1024,768]{1,0:T(8,128)(2,1)S(1)} %shard_map.321, bf16[1024,1024]{0,1:T(8,128)(2,1)S(1)} %copy-done.41, bf16[1024,1024]{0,1:T(8,128)(2,1)} %collective-permute-done.2), kind=kOutput, calls=%fused_computation.5 | convolution fusion | flops 3233808384 | bytes 39321600 | tf_op jit(solution)/shard_map/dot_general | solution.py:442
  1092.2 9.8 collective-permute-done.84
  1110.8 7.3 collective-permute-done.86
  1141.9 14.0 %collective-permute-done.79 = f32[20480]{0:T(1024)S(1)} collective-permute-done((f32[20480]{0:T(1024)S(1)}, f32[20480]{0:T(1024)S(1)}, u32[]{:S(2)}, u32[]{:S(2)}) %collective-permute-start.79) | collective-permute-done | bytes 81952 | tf_op jit(solution)/shard_map/ppermute | solution.py:353
  1174.1 8.2 collective-permute-done.92
  1187.4 15.8 %collective-permute-done.112 = bf16[256,1024]{0,1:T(8,128)(2,1)} collective-permute-done((bf16[256,1024]{0,1:T(8,128)(2,1)}, bf16[256,1024]{0,1:T(8,128)(2,1)}, u32[]{:S(2)}, u32[]{:S(2)}) %collective-permute-start.112) | collective-permute-done | bytes 524320 | tf_op jit(solution)/shard_map/ppermute | solution.py:353
  1211.9 6.4 collective-permute-done.117
  1219.9 9.6 collective-permute-done.96
  1233.6 7.1 collective-permute-done.114
  1247.5 13.2 %collective-permute-done.98 = bf16[256,1024]{0,1:T(8,128)(2,1)S(1)} collective-permute-done((bf16[256,1024]{0,1:T(8,128)(2,1)S(1)}, bf16[256,1024]{0,1:T(8,128)(2,1)S(1)}, u32[]{:S(2)}, u32[]{:S(2)}) %collective-permute-start.98) | collective-permute-done | bytes 524320 | tf_op jit(solution)/shard_map/ppermute | solution.py:353
  1271.8 6.0 collective-permute-done.120
  (958 shorter events, 544.9 us)
Async XLA Ops:
  1.4 62.3 %collective-permute-start.1 = (f32[2,1024]{1,0:T(2,128)S(1)}, f32[2,1024]{1,0:T(2,128)S(1)}, u32[]{:S(2)}, u32[]{:S(2)}) collective-permute-start(f32[2,1024]{1,0:T(2,128)S(1)} %pad_maximum_fusion.32), channel_id=1, source_target_pairs={{0,4},{4,0},{1,5},{5,1},{2,6},{6,2},{3,7},{7,3},{8,12},{12,8},{9,1... | collective-permute-start | bytes 24584 | tf_op jit(solution)/shard_map/ppermute | solution.py:345
  1.9 84.7 %collective-permute-start = (bf16[1024,1024]{1,0:T(8,128)(2,1)}, bf16[1024,1024]{1,0:T(8,128)(2,1)S(1)}, u32[]{:S(2)}, u32[]{:S(2)}) collective-permute-start(bf16[1024,1024]{1,0:T(8,128)(2,1)} %param.19), channel_id=1, source_target_pairs={{0,4},{4,0},{1,5},{5,1},{2,6},{6,2},{3,7},{7,3},{8,12},{12,8},{9,1... | collective-permute-start | bytes 6291464 | tf_op jit(solution)/shard_map/ppermute | solution.py:345
  35.6 55.9 %collective-permute-start.2 = (bf16[1024,1024]{0,1:T(8,128)(2,1)}, bf16[1024,1024]{0,1:T(8,128)(2,1)}, u32[]{:S(2)}, u32[]{:S(2)}) collective-permute-start(bf16[1024,1024]{0,1:T(8,128)(2,1)} %get-tuple-element.126), channel_id=1, source_target_pairs={{0,4},{4,0},{1,5},{5,1},{2,6},{6,2},{3,7},{7,3},{8,12},{12,8},{9,1... | collective-permute-start | bytes 6291464 | tf_op jit(solution)/shard_map/ppermute | solution.py:345
  63.7 40.7 %collective-permute-start.12 = (bf16[256,2048]{0,1:T(8,128)(2,1)}, bf16[256,2048]{0,1:T(8,128)(2,1)}, u32[]{:S(2)}, u32[]{:S(2)}) collective-permute-start(bf16[256,2048]{0,1:T(8,128)(2,1)} %collective-permute-done.4), channel_id=1, source_target_pairs={{0,1},{1,2},{2,3},{3,0},{4,5},{5,6},{6,7},{7,4},{8,9},{9,10},{10,1... | collective-permute-start | bytes 3145736 | tf_op jit(solution)/shard_map/ppermute | solution.py:358
  113.0 72.0 %collective-permute-start.9 = (bf16[1024,1024]{0,1:T(8,128)(2,1)S(1)}, bf16[1024,1024]{0,1:T(8,128)(2,1)S(1)}, u32[]{:S(2)}, u32[]{:S(2)}) collective-permute-start(bf16[1024,1024]{0,1:T(8,128)(2,1)S(1)} %get-tuple-element.238), channel_id=1, source_target_pairs={{0,4},{4,0},{1,5},{5,1},{2,6},{6,2},{3,7},{7,3},{8,12},{12,8},{9,1... | collective-permute-start | bytes 6291464 | tf_op jit(solution)/shard_map/ppermute | solution.py:345
  131.6 32.0 %collective-permute-start.21 = (bf16[256,2048]{0,1:T(8,128)(2,1)S(1)}, bf16[256,2048]{0,1:T(8,128)(2,1)S(1)}, u32[]{:S(2)}, u32[]{:S(2)}) collective-permute-start(bf16[256,2048]{0,1:T(8,128)(2,1)S(1)} %collective-permute-done.20), channel_id=1, source_target_pairs={{0,8},{8,0},{16,24},{24,16},{1,9},{9,1},{17,25},{25,17},{2,10},{10... | collective-permute-start | bytes 3145736 | tf_op jit(solution)/shard_map/ppermute | solution.py:349
  146.0 53.0 %collective-permute-start.17 = (bf16[1024,1024]{0,1:T(8,128)(2,1)}, bf16[1024,1024]{0,1:T(8,128)(2,1)S(1)}, u32[]{:S(2)}, u32[]{:S(2)}) collective-permute-start(bf16[1024,1024]{0,1:T(8,128)(2,1)} %get-tuple-element.244), channel_id=1, source_target_pairs={{0,4},{4,0},{1,5},{5,1},{2,6},{6,2},{3,7},{7,3},{8,12},{12,8},{9,1... | collective-permute-start | bytes 6291464 | tf_op jit(solution)/shard_map/ppermute | solution.py:345
  167.8 128.7 %collective-permute-start.61 = (bf16[1024,1024]{1,0:T(8,128)(2,1)}, bf16[1024,1024]{1,0:T(8,128)(2,1)}, u32[]{:S(2)}, u32[]{:S(2)}) collective-permute-start(bf16[1024,1024]{1,0:T(8,128)(2,1)} %get-tuple-element.81.refs_4_), channel_id=1, source_target_pairs={{0,16},{16,0},{8,24},{24,8},{1,17},{17,1},{9,25},{25,9},{2,18},{18... | collective-permute-start | bytes 6291464 | tf_op jit(solution)/shard_map/ppermute | solution.py:353
  184.1 56.7 %collective-permute-start.30 = (bf16[1024,512]{1,0:T(8,128)(2,1)}, bf16[1024,512]{1,0:T(8,128)(2,1)}, u32[]{:S(2)}, u32[]{:S(2)}) collective-permute-start(bf16[1024,512]{1,0:T(8,128)(2,1)} %pad_maximum_fusion.20), channel_id=1, source_target_pairs={{0,1},{1,2},{2,3},{3,0},{4,5},{5,6},{6,7},{7,4},{8,9},{9,10},{10,1... | collective-permute-start | bytes 3145736 | tf_op jit(solution)/shard_map/ppermute | solution.py:358
  238.0 65.2 %collective-permute-start.57 = (bf16[1024,1024]{1,0:T(8,128)(2,1)}, bf16[1024,1024]{1,0:T(8,128)(2,1)}, u32[]{:S(2)}, u32[]{:S(2)}) collective-permute-start(bf16[1024,1024]{1,0:T(8,128)(2,1)} %get-tuple-element.81.refs_4_), channel_id=1, source_target_pairs={{0,8},{8,0},{16,24},{24,16},{1,9},{9,1},{17,25},{25,17},{2,10},{10... | collective-permute-start | bytes 6291464 | tf_op jit(solution)/shard_map/ppermute | solution.py:349
  241.9 49.4 %collective-permute-start.31 = (bf16[1024,512]{1,0:T(8,128)(2,1)}, bf16[1024,512]{1,0:T(8,128)(2,1)}, u32[]{:S(2)}, u32[]{:S(2)}) collective-permute-start(bf16[1024,512]{1,0:T(8,128)(2,1)} %collective-permute-done.30), channel_id=1, source_target_pairs={{0,1},{1,2},{2,3},{3,0},{4,5},{5,6},{6,7},{7,4},{8,9},{9,10},{10,1... | collective-permute-start | bytes 3145736 | tf_op jit(solution)/shard_map/ppermute | solution.py:358
  253.7 38.2 %collective-permute-start.28 = (f32[2,1024]{1,0:T(2,128)S(1)}, f32[2,1024]{1,0:T(2,128)S(1)}, u32[]{:S(2)}, u32[]{:S(2)}) collective-permute-start(f32[2,1024]{1,0:T(2,128)S(1)} %maximum_bitcast_fusion.4), channel_id=1, source_target_pairs={{0,4},{4,0},{1,5},{5,1},{2,6},{6,2},{3,7},{7,3},{8,12},{12,8},{9,1... | collective-permute-start | bytes 24584 | tf_op jit(solution)/shard_map/ppermute | solution.py:345
  268.8 44.8 %collective-permute-start.36 = (bf16[512,1024]{1,0:T(8,128)(2,1)}, bf16[512,1024]{1,0:T(8,128)(2,1)S(1)}, u32[]{:S(2)}, u32[]{:S(2)}) collective-permute-start(bf16[512,1024]{1,0:T(8,128)(2,1)} %collective-permute-done.35), channel_id=1, source_target_pairs={{0,1},{1,2},{2,3},{3,0},{4,5},{5,6},{6,7},{7,4},{8,9},{9,10},{10,1... | collective-permute-start | bytes 3145736 | tf_op jit(solution)/shard_map/ppermute | solution.py:358
  291.2 44.4 %collective-permute-start.32 = (bf16[1024,512]{1,0:T(8,128)(2,1)}, bf16[1024,512]{1,0:T(8,128)(2,1)S(1)}, u32[]{:S(2)}, u32[]{:S(2)}) collective-permute-start(bf16[1024,512]{1,0:T(8,128)(2,1)} %collective-permute-done.31), channel_id=1, source_target_pairs={{0,1},{1,2},{2,3},{3,0},{4,5},{5,6},{6,7},{7,4},{8,9},{9,10},{10,1... | collective-permute-start | bytes 3145736 | tf_op jit(solution)/shard_map/ppermute | solution.py:358
  294.9 48.6 %collective-permute-start.38 = (bf16[1024,1024]{1,0:T(8,128)(2,1)S(1)}, bf16[1024,1024]{1,0:T(8,128)(2,1)S(1)}, u32[]{:S(2)}, u32[]{:S(2)}) collective-permute-start(bf16[1024,1024]{1,0:T(8,128)(2,1)S(1)} %add_convert_fusion.refs_0_), channel_id=1, source_target_pairs={{0,8},{8,0},{16,24},{24,16},{1,9},{9,1},{17,25},{25,17},{2,10},{10... | collective-permute-start | bytes 6291464 | tf_op jit(solution)/shard_map/ppermute | solution.py:349
  296.5 71.1 %collective-permute-start.42 = (bf16[1024,1024]{1,0:T(8,128)(2,1)S(1)}, bf16[1024,1024]{1,0:T(8,128)(2,1)S(1)}, u32[]{:S(2)}, u32[]{:S(2)}) collective-permute-start(bf16[1024,1024]{1,0:T(8,128)(2,1)S(1)} %add_convert_fusion.refs_0_), channel_id=1, source_target_pairs={{0,16},{16,0},{8,24},{24,8},{1,17},{17,1},{9,25},{25,9},{2,18},{18... | collective-permute-start | bytes 6291464 | tf_op jit(solution)/shard_map/ppermute | solution.py:353
  303.1 67.5 %collective-permute-start.65 = (bf16[512,1024]{1,0:T(8,128)(2,1)S(1)}, bf16[512,1024]{1,0:T(8,128)(2,1)S(1)}, u32[]{:S(2)}, u32[]{:S(2)}) collective-permute-start(bf16[512,1024]{1,0:T(8,128)(2,1)S(1)} %slice.885), channel_id=1, source_target_pairs={{0,8},{8,0},{16,24},{24,16},{1,9},{9,1},{17,25},{25,17},{2,10},{10... | collective-permute-start | bytes 3145736 | tf_op jit(solution)/shard_map/ppermute | solution.py:349
  313.6 54.0 %collective-permute-start.64 = (bf16[512,1024]{1,0:T(8,128)(2,1)S(1)}, bf16[512,1024]{1,0:T(8,128)(2,1)S(1)}, u32[]{:S(2)}, u32[]{:S(2)}) collective-permute-start(bf16[512,1024]{1,0:T(8,128)(2,1)S(1)} %slice.884), channel_id=1, source_target_pairs={{0,16},{16,0},{8,24},{24,8},{1,17},{17,1},{9,25},{25,9},{2,18},{18... | collective-permute-start | bytes 3145736 | tf_op jit(solution)/shard_map/ppermute | solution.py:353
  335.6 33.7 %collective-permute-start.37 = (bf16[512,1024]{1,0:T(8,128)(2,1)S(1)}, bf16[512,1024]{1,0:T(8,128)(2,1)S(1)}, u32[]{:S(2)}, u32[]{:S(2)}) collective-permute-start(bf16[512,1024]{1,0:T(8,128)(2,1)S(1)} %collective-permute-done.36), channel_id=1, source_target_pairs={{0,1},{1,2},{2,3},{3,0},{4,5},{5,6},{6,7},{7,4},{8,9},{9,10},{10,1... | collective-permute-start | bytes 3145736 | tf_op jit(solution)/shard_map/ppermute | solution.py:358
  343.6 43.9 %collective-permute-start.45 = (bf16[512,1024]{1,0:T(8,128)(2,1)S(1)}, bf16[512,1024]{1,0:T(8,128)(2,1)S(1)}, u32[]{:S(2)}, u32[]{:S(2)}) collective-permute-start(bf16[512,1024]{1,0:T(8,128)(2,1)S(1)} %slice.874), channel_id=1, source_target_pairs={{0,16},{16,0},{8,24},{24,8},{1,17},{17,1},{9,25},{25,9},{2,18},{18... | collective-permute-start | bytes 3145736 | tf_op jit(solution)/shard_map/ppermute | solution.py:353
  369.3 37.5 %collective-permute-start.62 = (bf16[1024,1024]{1,0:T(8,128)(2,1)}, bf16[1024,1024]{1,0:T(8,128)(2,1)S(1)}, u32[]{:S(2)}, u32[]{:S(2)}) collective-permute-start(bf16[1024,1024]{1,0:T(8,128)(2,1)} %collective-permute-done.61.refs_6_), channel_id=1, source_target_pairs={{0,4},{4,0},{1,5},{5,1},{2,6},{6,2},{3,7},{7,3},{8,12},{12,8},{9,1... | collective-permute-start | bytes 6291464 | tf_op jit(solution)/shard_map/ppermute | solution.py:345
  396.2 87.0 %collective-permute-start.54 = (bf16[1024,1024]{1,0:T(8,128)(2,1)}, bf16[1024,1024]{1,0:T(8,128)(2,1)}, u32[]{:S(2)}, u32[]{:S(2)}) collective-permute-start(bf16[1024,1024]{1,0:T(8,128)(2,1)} %get-tuple-element.81.refs_4_), channel_id=1, source_target_pairs={{0,4},{4,0},{1,5},{5,1},{2,6},{6,2},{3,7},{7,3},{8,12},{12,8},{9,1... | collective-permute-start | bytes 6291464 | tf_op jit(solution)/shard_map/ppermute | solution.py:345
  406.7 39.6 %collective-permute-start.66 = (bf16[1024,1024]{1,0:T(8,128)(2,1)S(1)}, bf16[1024,1024]{1,0:T(8,128)(2,1)}, u32[]{:S(2)}, u32[]{:S(2)}) collective-permute-start(bf16[1024,1024]{1,0:T(8,128)(2,1)S(1)} %constant_dynamic-update-slice_fusion.27.refs_7_), channel_id=1, source_target_pairs={{0,4},{4,0},{1,5},{5,1},{2,6},{6,2},{3,7},{7,3},{8,12},{12,8},{9,1... | collective-permute-start | bytes 6291464 | tf_op jit(solution)/shard_map/ppermute | solution.py:345
  407.0 50.6 %collective-permute-start.29 = (bf16[1024,1024]{1,0:T(8,128)(2,1)S(1)}, bf16[1024,1024]{1,0:T(8,128)(2,1)}, u32[]{:S(2)}, u32[]{:S(2)}) collective-permute-start(bf16[1024,1024]{1,0:T(8,128)(2,1)S(1)} %add_convert_fusion.refs_0_), channel_id=1, source_target_pairs={{0,4},{4,0},{1,5},{5,1},{2,6},{6,2},{3,7},{7,3},{8,12},{12,8},{9,1... | collective-permute-start | bytes 6291464 | tf_op jit(solution)/shard_map/ppermute | solution.py:345
  427.2 122.4 %collective-permute-start.63 = (bf16[1024,1024]{1,0:T(8,128)(2,1)}, bf16[1024,1024]{1,0:T(8,128)(2,1)}, u32[]{:S(2)}, u32[]{:S(2)}) collective-permute-start(bf16[1024,1024]{1,0:T(8,128)(2,1)} %get-tuple-element.276.refs_6_), channel_id=1, source_target_pairs={{0,4},{4,0},{1,5},{5,1},{2,6},{6,2},{3,7},{7,3},{8,12},{12,8},{9,1... | collective-permute-start | bytes 6291464 | tf_op jit(solution)/shard_map/ppermute | solution.py:345
  439.1 135.5 %collective-permute-start.59 = (bf16[1024,1024]{1,0:T(8,128)(2,1)}, bf16[1024,1024]{1,0:T(8,128)(2,1)}, u32[]{:S(2)}, u32[]{:S(2)}) collective-permute-start(bf16[1024,1024]{1,0:T(8,128)(2,1)} %get-tuple-element.280.refs_5_), channel_id=1, source_target_pairs={{0,4},{4,0},{1,5},{5,1},{2,6},{6,2},{3,7},{7,3},{8,12},{12,8},{9,1... | collective-permute-start | bytes 6291464 | tf_op jit(solution)/shard_map/ppermute | solution.py:345
  457.3 138.2 %collective-permute-start.67 = (bf16[1024,1024]{1,0:T(8,128)(2,1)}, bf16[1024,1024]{1,0:T(8,128)(2,1)}, u32[]{:S(2)}, u32[]{:S(2)}) collective-permute-start(bf16[1024,1024]{1,0:T(8,128)(2,1)} %get-tuple-element.274.refs_7_), channel_id=1, source_target_pairs={{0,4},{4,0},{1,5},{5,1},{2,6},{6,2},{3,7},{7,3},{8,12},{12,8},{9,1... | collective-permute-start | bytes 6291464 | tf_op jit(solution)/shard_map/ppermute | solution.py:345
  533.4 62.7 %collective-permute-start.56 = (bf16[1024,1024]{1,0:T(8,128)(2,1)}, bf16[1024,1024]{1,0:T(8,128)(2,1)S(1)}, u32[]{:S(2)}, u32[]{:S(2)}) collective-permute-start(bf16[1024,1024]{1,0:T(8,128)(2,1)} %get-tuple-element.278.refs_4_), channel_id=1, source_target_pairs={{0,4},{4,0},{1,5},{5,1},{2,6},{6,2},{3,7},{7,3},{8,12},{12,8},{9,1... | collective-permute-start | bytes 6291464 | tf_op jit(solution)/shard_map/ppermute | solution.py:345
  561.2 52.8 %collective-permute-start.44 = (bf16[1024,1024]{1,0:T(8,128)(2,1)}, bf16[1024,1024]{1,0:T(8,128)(2,1)}, u32[]{:S(2)}, u32[]{:S(2)}) collective-permute-start(bf16[1024,1024]{1,0:T(8,128)(2,1)} %get-tuple-element.270.refs_2_), channel_id=1, source_target_pairs={{0,4},{4,0},{1,5},{5,1},{2,6},{6,2},{3,7},{7,3},{8,12},{12,8},{9,1... | collective-permute-start | bytes 6291464 | tf_op jit(solution)/shard_map/ppermute | solution.py:345
  586.8 36.5 %collective-permute-start.40 = (bf16[1024,1024]{1,0:T(8,128)(2,1)}, bf16[1024,1024]{1,0:T(8,128)(2,1)}, u32[]{:S(2)}, u32[]{:S(2)}) collective-permute-start(bf16[1024,1024]{1,0:T(8,128)(2,1)} %get-tuple-element.271.refs_1_), channel_id=1, source_target_pairs={{0,4},{4,0},{1,5},{5,1},{2,6},{6,2},{3,7},{7,3},{8,12},{12,8},{9,1... | collective-permute-start | bytes 6291464 | tf_op jit(solution)/shard_map/ppermute | solution.py:345
  595.3 37.4 %collective-permute-start.34 = (bf16[1024,1024]{1,0:T(8,128)(2,1)S(1)}, bf16[1024,1024]{1,0:T(8,128)(2,1)S(1)}, u32[]{:S(2)}, u32[]{:S(2)}) collective-permute-start(bf16[1024,1024]{1,0:T(8,128)(2,1)S(1)} %copy-done.9), channel_id=1, source_target_pairs={{0,4},{4,0},{1,5},{5,1},{2,6},{6,2},{3,7},{7,3},{8,12},{12,8},{9,1... | collective-permute-start | bytes 6291464 | tf_op jit(solution)/shard_map/ppermute | solution.py:345
  595.5 38.7 %collective-permute-start.48 = (bf16[1024,1024]{1,0:T(8,128)(2,1)}, bf16[1024,1024]{1,0:T(8,128)(2,1)}, u32[]{:S(2)}, u32[]{:S(2)}) collective-permute-start(bf16[1024,1024]{1,0:T(8,128)(2,1)} %get-tuple-element.269.refs_3_), channel_id=1, source_target_pairs={{0,4},{4,0},{1,5},{5,1},{2,6},{6,2},{3,7},{7,3},{8,12},{12,8},{9,1... | collective-permute-start | bytes 6291464 | tf_op jit(solution)/shard_map/ppermute | solution.py:345
  597.4 85.5 %collective-permute-start.128 = (bf16[1024,256]{1,0:T(8,128)(2,1)S(1)}, bf16[1024,256]{1,0:T(8,128)(2,1)}, u32[]{:S(2)}, u32[]{:S(2)}) collective-permute-start(bf16[1024,256]{1,0:T(8,128)(2,1)S(1)} %add_convert_fusion.20), channel_id=1, source_target_pairs={{0,16},{16,0},{8,24},{24,8},{1,17},{17,1},{9,25},{25,9},{2,18},{18... | collective-permute-start | bytes 1572872 | tf_op jit(solution)/shard_map/ppermute | solution.py:353
  614.0 70.5 %collective-permute-start.127 = (bf16[1024,256]{1,0:T(8,128)(2,1)S(1)}, bf16[1024,256]{1,0:T(8,128)(2,1)}, u32[]{:S(2)}, u32[]{:S(2)}) collective-permute-start(bf16[1024,256]{1,0:T(8,128)(2,1)S(1)} %add_convert_fusion.20), channel_id=1, source_target_pairs={{0,8},{8,0},{16,24},{24,16},{1,9},{9,1},{17,25},{25,17},{2,10},{10... | collective-permute-start | bytes 1572872 | tf_op jit(solution)/shard_map/ppermute | solution.py:349
  623.3 64.1 %collective-permute-start.142 = (bf16[256,1024]{1,0:T(8,128)(2,1)S(1)}, bf16[256,1024]{1,0:T(8,128)(2,1)S(1)}, u32[]{:S(2)}, u32[]{:S(2)}) collective-permute-start(bf16[256,1024]{1,0:T(8,128)(2,1)S(1)} %add_convert_fusion.14), channel_id=1, source_target_pairs={{0,16},{16,0},{8,24},{24,8},{1,17},{17,1},{9,25},{25,9},{2,18},{18... | collective-permute-start | bytes 1572872 | tf_op jit(solution)/shard_map/ppermute | solution.py:353
  632.7 54.9 %collective-permute-start.141 = (bf16[256,1024]{1,0:T(8,128)(2,1)S(1)}, bf16[256,1024]{1,0:T(8,128)(2,1)}, u32[]{:S(2)}, u32[]{:S(2)}) collective-permute-start(bf16[256,1024]{1,0:T(8,128)(2,1)S(1)} %add_convert_fusion.14), channel_id=1, source_target_pairs={{0,8},{8,0},{16,24},{24,16},{1,9},{9,1},{17,25},{25,17},{2,10},{10... | collective-permute-start | bytes 1572872 | tf_op jit(solution)/shard_map/ppermute | solution.py:349
  634.2 55.9 %collective-permute-start.131 = (bf16[1024,256]{1,0:T(8,128)(2,1)}, bf16[1024,256]{1,0:T(8,128)(2,1)}, u32[]{:S(2)}, u32[]{:S(2)}) collective-permute-start(bf16[1024,256]{1,0:T(8,128)(2,1)} %slice.940), channel_id=1, source_target_pairs={{0,3},{1,0},{2,1},{3,2},{4,7},{5,4},{6,5},{7,6},{8,11},{9,8},{10,9... | collective-permute-start | bytes 1572872 | tf_op jit(solution)/shard_map/ppermute | solution.py:363
  682.9 70.4 %collective-permute-start.68 = (bf16[512,1024]{1,0:T(8,128)(2,1)S(1)}, bf16[512,1024]{1,0:T(8,128)(2,1)S(1)}, u32[]{:S(2)}, u32[]{:S(2)}) collective-permute-start(bf16[512,1024]{1,0:T(8,128)(2,1)S(1)} %get-tuple-element.174), channel_id=1, source_target_pairs={{0,8},{8,0},{16,24},{24,16},{1,9},{9,1},{17,25},{25,17},{2,10},{10... | collective-permute-start | bytes 3145736 | tf_op jit(solution)/shard_map/ppermute | solution.py:349
  684.4 71.6 %collective-permute-start.70 = (bf16[512,1024]{1,0:T(8,128)(2,1)S(1)}, bf16[512,1024]{1,0:T(8,128)(2,1)S(1)}, u32[]{:S(2)}, u32[]{:S(2)}) collective-permute-start(bf16[512,1024]{1,0:T(8,128)(2,1)S(1)} %get-tuple-element.175), channel_id=1, source_target_pairs={{0,16},{16,0},{8,24},{24,8},{1,17},{17,1},{9,25},{25,9},{2,18},{18... | collective-permute-start | bytes 3145736 | tf_op jit(solution)/shard_map/ppermute | solution.py:353
  756.0 72.9 %collective-permute-start.72 = (bf16[512,1024]{1,0:T(8,128)(2,1)}, bf16[512,1024]{1,0:T(8,128)(2,1)}, u32[]{:S(2)}, u32[]{:S(2)}) collective-permute-start(bf16[512,1024]{1,0:T(8,128)(2,1)} %slice.890), channel_id=1, source_target_pairs={{0,16},{16,0},{8,24},{24,8},{1,17},{17,1},{9,25},{25,9},{2,18},{18... | collective-permute-start | bytes 3145736 | tf_op jit(solution)/shard_map/ppermute | solution.py:353
  758.1 72.3 %collective-permute-start.60 = (bf16[512,1024]{1,0:T(8,128)(2,1)}, bf16[512,1024]{1,0:T(8,128)(2,1)}, u32[]{:S(2)}, u32[]{:S(2)}) collective-permute-start(bf16[512,1024]{1,0:T(8,128)(2,1)} %slice.882), channel_id=1, source_target_pairs={{0,8},{8,0},{16,24},{24,16},{1,9},{9,1},{17,25},{25,17},{2,10},{10... | collective-permute-start | bytes 3145736 | tf_op jit(solution)/shard_map/ppermute | solution.py:349
  764.3 66.4 %collective-permute-start.69 = (bf16[512,1024]{1,0:T(8,128)(2,1)}, bf16[512,1024]{1,0:T(8,128)(2,1)}, u32[]{:S(2)}, u32[]{:S(2)}) collective-permute-start(bf16[512,1024]{1,0:T(8,128)(2,1)} %add_convert_fusion.8), channel_id=1, source_target_pairs={{0,16},{16,0},{8,24},{24,8},{1,17},{17,1},{9,25},{25,9},{2,18},{18... | collective-permute-start | bytes 3145736 | tf_op jit(solution)/shard_map/ppermute | solution.py:353
  765.6 66.0 %collective-permute-start.71 = (bf16[512,1024]{1,0:T(8,128)(2,1)}, bf16[512,1024]{1,0:T(8,128)(2,1)}, u32[]{:S(2)}, u32[]{:S(2)}) collective-permute-start(bf16[512,1024]{1,0:T(8,128)(2,1)} %add_convert_fusion.7), channel_id=1, source_target_pairs={{0,8},{8,0},{16,24},{24,16},{1,9},{9,1},{17,25},{25,17},{2,10},{10... | collective-permute-start | bytes 3145736 | tf_op jit(solution)/shard_map/ppermute | solution.py:349
  775.5 37.1 %collective-permute-start.134 = (bf16[1024,256]{1,0:T(8,128)(2,1)}, bf16[1024,256]{1,0:T(8,128)(2,1)}, u32[]{:S(2)}, u32[]{:S(2)}) collective-permute-start(bf16[1024,256]{1,0:T(8,128)(2,1)} %add_convert_fusion.17), channel_id=1, source_target_pairs={{0,8},{8,0},{16,24},{24,16},{1,9},{9,1},{17,25},{25,17},{2,10},{10... | collective-permute-start | bytes 1572872 | tf_op jit(solution)/shard_map/ppermute | solution.py:349
  827.4 54.3 %collective-permute-start.53 = (bf16[512,1024]{1,0:T(8,128)(2,1)S(1)}, bf16[512,1024]{1,0:T(8,128)(2,1)S(1)}, u32[]{:S(2)}, u32[]{:S(2)}) collective-permute-start(bf16[512,1024]{1,0:T(8,128)(2,1)S(1)} %copy-done.101), channel_id=1, source_target_pairs={{0,16},{16,0},{8,24},{24,8},{1,17},{17,1},{9,25},{25,9},{2,18},{18... | collective-permute-start | bytes 3145736 | tf_op jit(solution)/shard_map/ppermute | solution.py:353
  829.0 53.0 %collective-permute-start.41 = (bf16[512,1024]{1,0:T(8,128)(2,1)S(1)}, bf16[512,1024]{1,0:T(8,128)(2,1)S(1)}, u32[]{:S(2)}, u32[]{:S(2)}) collective-permute-start(bf16[512,1024]{1,0:T(8,128)(2,1)S(1)} %copy-done.102), channel_id=1, source_target_pairs={{0,8},{8,0},{16,24},{24,16},{1,9},{9,1},{17,25},{25,17},{2,10},{10... | collective-permute-start | bytes 3145736 | tf_op jit(solution)/shard_map/ppermute | solution.py:349
  830.4 52.9 %collective-permute-start.50 = (bf16[512,1024]{1,0:T(8,128)(2,1)S(1)}, bf16[512,1024]{1,0:T(8,128)(2,1)S(1)}, u32[]{:S(2)}, u32[]{:S(2)}) collective-permute-start(bf16[512,1024]{1,0:T(8,128)(2,1)S(1)} %add_convert_fusion.10), channel_id=1, source_target_pairs={{0,16},{16,0},{8,24},{24,8},{1,17},{17,1},{9,25},{25,9},{2,18},{18... | collective-permute-start | bytes 3145736 | tf_op jit(solution)/shard_map/ppermute | solution.py:353
  830.7 54.1 %collective-permute-start.52 = (bf16[512,1024]{1,0:T(8,128)(2,1)S(1)}, bf16[512,1024]{1,0:T(8,128)(2,1)S(1)}, u32[]{:S(2)}, u32[]{:S(2)}) collective-permute-start(bf16[512,1024]{1,0:T(8,128)(2,1)S(1)} %add_convert_fusion.9), channel_id=1, source_target_pairs={{0,8},{8,0},{16,24},{24,16},{1,9},{9,1},{17,25},{25,17},{2,10},{10... | collective-permute-start | bytes 3145736 | tf_op jit(solution)/shard_map/ppermute | solution.py:349
  831.6 49.3 %collective-permute-start.148 = (bf16[256,1024]{1,0:T(8,128)(2,1)S(1)}, bf16[256,1024]{1,0:T(8,128)(2,1)S(1)}, u32[]{:S(2)}, u32[]{:S(2)}) collective-permute-start(bf16[256,1024]{1,0:T(8,128)(2,1)S(1)} %add_convert_fusion.11), channel_id=1, source_target_pairs={{0,8},{8,0},{16,24},{24,16},{1,9},{9,1},{17,25},{25,17},{2,10},{10... | collective-permute-start | bytes 1572872 | tf_op jit(solution)/shard_map/ppermute | solution.py:349
  883.3 41.0 %collective-permute-start.151 = (bf16[128,1024]{1,0:T(8,128)(2,1)S(1)}, bf16[128,1024]{1,0:T(8,128)(2,1)}, u32[]{:S(2)}, u32[]{:S(2)}) collective-permute-start(bf16[128,1024]{1,0:T(8,128)(2,1)S(1)} %slice.957), channel_id=1, source_target_pairs={{0,8},{8,0},{16,24},{24,16},{1,9},{9,1},{17,25},{25,17},{2,10},{10... | collective-permute-start | bytes 786440 | tf_op jit(solution)/shard_map/ppermute | solution.py:349
  884.8 39.5 %collective-permute-start.150 = (bf16[128,1024]{1,0:T(8,128)(2,1)}, bf16[128,1024]{1,0:T(8,128)(2,1)}, u32[]{:S(2)}, u32[]{:S(2)}) collective-permute-start(bf16[128,1024]{1,0:T(8,128)(2,1)} %slice.956), channel_id=1, source_target_pairs={{0,16},{16,0},{8,24},{24,8},{1,17},{17,1},{9,25},{25,9},{2,18},{18... | collective-permute-start | bytes 786440 | tf_op jit(solution)/shard_map/ppermute | solution.py:353
  898.5 34.4 %collective-permute-start.74 = (bf16[1024,1024]{1,0:T(8,128)(2,1)}, bf16[1024,1024]{1,0:T(8,128)(2,1)}, u32[]{:S(2)}, u32[]{:S(2)}) collective-permute-start(bf16[1024,1024]{1,0:T(8,128)(2,1)} %pad_maximum_fusion.11), channel_id=1, source_target_pairs={{0,4},{4,0},{1,5},{5,1},{2,6},{6,2},{3,7},{7,3},{8,12},{12,8},{9,1... | collective-permute-start | bytes 6291464 | tf_op jit(solution)/shard_map/ppermute | solution.py:345
  1047.3 40.2 %collective-permute-start.77 = (f32[4,3584]{1,0:T(4,128)S(1)}, f32[4,3584]{1,0:T(4,128)S(1)}, u32[]{:S(2)}, u32[]{:S(2)}) collective-permute-start(f32[4,3584]{1,0:T(4,128)S(1)} %pad_maximum_fusion.30), channel_id=1, source_target_pairs={{0,4},{4,0},{1,5},{5,1},{2,6},{6,2},{3,7},{7,3},{8,12},{12,8},{9,1... | collective-permute-start | bytes 172040 | tf_op jit(solution)/shard_map/ppermute | solution.py:345
  1047.8 40.8 %collective-permute-start.87 = (bf16[256,1024]{0,1:T(8,128)(2,1)}, bf16[256,1024]{0,1:T(8,128)(2,1)}, u32[]{:S(2)}, u32[]{:S(2)}) collective-permute-start(bf16[256,1024]{0,1:T(8,128)(2,1)} %get-tuple-element.108), channel_id=1, source_target_pairs={{0,8},{8,0},{16,24},{24,16},{1,9},{9,1},{17,25},{25,17},{2,10},{10... | collective-permute-start | bytes 1572872 | tf_op jit(solution)/shard_map/ppermute | solution.py:349
  1050.8 39.8 %collective-permute-start.82 = (bf16[256,1024]{0,1:T(8,128)(2,1)}, bf16[256,1024]{0,1:T(8,128)(2,1)}, u32[]{:S(2)}, u32[]{:S(2)}) collective-permute-start(bf16[256,1024]{0,1:T(8,128)(2,1)} %get-tuple-element.109), channel_id=1, source_target_pairs={{0,8},{8,0},{16,24},{24,16},{1,9},{9,1},{17,25},{25,17},{2,10},{10... | collective-permute-start | bytes 1572872 | tf_op jit(solution)/shard_map/ppermute | solution.py:349
  1052.2 33.2 %collective-permute-start.83 = (bf16[256,1024]{0,1:T(8,128)(2,1)}, bf16[256,1024]{0,1:T(8,128)(2,1)}, u32[]{:S(2)}, u32[]{:S(2)}) collective-permute-start(bf16[256,1024]{0,1:T(8,128)(2,1)} %get-tuple-element.110), channel_id=1, source_target_pairs={{0,8},{8,0},{16,24},{24,16},{1,9},{9,1},{17,25},{25,17},{2,10},{10... | collective-permute-start | bytes 1572872 | tf_op jit(solution)/shard_map/ppermute | solution.py:349
  1053.9 50.7 %collective-permute-start.95 = (bf16[256,1024]{0,1:T(8,128)(2,1)}, bf16[256,1024]{0,1:T(8,128)(2,1)}, u32[]{:S(2)}, u32[]{:S(2)}) collective-permute-start(bf16[256,1024]{0,1:T(8,128)(2,1)} %get-tuple-element.112), channel_id=1, source_target_pairs={{0,8},{8,0},{16,24},{24,16},{1,9},{9,1},{17,25},{25,17},{2,10},{10... | collective-permute-start | bytes 1572872 | tf_op jit(solution)/shard_map/ppermute | solution.py:349
  1085.4 34.5 %collective-permute-start.75 = (bf16[1024,1024]{1,0:T(8,128)(2,1)}, bf16[1024,1024]{1,0:T(8,128)(2,1)}, u32[]{:S(2)}, u32[]{:S(2)}) collective-permute-start(bf16[1024,1024]{1,0:T(8,128)(2,1)} %slice.1088), channel_id=1, source_target_pairs={{0,4},{4,0},{1,5},{5,1},{2,6},{6,2},{3,7},{7,3},{8,12},{12,8},{9,1... | collective-permute-start | bytes 6291464 | tf_op jit(solution)/shard_map/ppermute | solution.py:345
  1118.2 55.9 %collective-permute-start.90 = (bf16[256,1024]{0,1:T(8,128)(2,1)S(1)}, bf16[256,1024]{0,1:T(8,128)(2,1)S(1)}, u32[]{:S(2)}, u32[]{:S(2)}) collective-permute-start(bf16[256,1024]{0,1:T(8,128)(2,1)S(1)} %copy-done.104), channel_id=1, source_target_pairs={{0,8},{8,0},{16,24},{24,16},{1,9},{9,1},{17,25},{25,17},{2,10},{10... | collective-permute-start | bytes 1572872 | tf_op jit(solution)/shard_map/ppermute | solution.py:349
  1119.9 37.6 %collective-permute-start.111 = (bf16[1024,1024]{0,1:T(8,128)(2,1)}, bf16[1024,1024]{0,1:T(8,128)(2,1)S(1)}, u32[]{:S(2)}, u32[]{:S(2)}) collective-permute-start(bf16[1024,1024]{0,1:T(8,128)(2,1)} %pad_maximum_fusion.6), channel_id=1, source_target_pairs={{0,4},{4,0},{1,5},{5,1},{2,6},{6,2},{3,7},{7,3},{8,12},{12,8},{9,1... | collective-permute-start | bytes 6291464 | tf_op jit(solution)/shard_map/ppermute | solution.py:345
  1171.0 34.7 %collective-permute-start.109 = (bf16[256,1024]{0,1:T(8,128)(2,1)}, bf16[256,1024]{0,1:T(8,128)(2,1)}, u32[]{:S(2)}, u32[]{:S(2)}) collective-permute-start(bf16[256,1024]{0,1:T(8,128)(2,1)} %get-tuple-element.167), channel_id=1, source_target_pairs={{0,16},{16,0},{8,24},{24,8},{1,17},{17,1},{9,25},{25,9},{2,18},{18... | collective-permute-start | bytes 1572872 | tf_op jit(solution)/shard_map/ppermute | solution.py:353
  1206.6 34.1 %collective-permute-start.114 = (bf16[256,1024]{0,1:T(8,128)(2,1)}, bf16[256,1024]{0,1:T(8,128)(2,1)S(1)}, u32[]{:S(2)}, u32[]{:S(2)}) collective-permute-start(bf16[256,1024]{0,1:T(8,128)(2,1)} %get-tuple-element.165), channel_id=1, source_target_pairs={{0,16},{16,0},{8,24},{24,8},{1,17},{17,1},{9,25},{25,9},{2,18},{18... | collective-permute-start | bytes 1572872 | tf_op jit(solution)/shard_map/ppermute | solution.py:353
  1229.5 34.2 %collective-permute-start.119 = (bf16[256,1024]{0,1:T(8,128)(2,1)S(1)}, bf16[256,1024]{0,1:T(8,128)(2,1)S(1)}, u32[]{:S(2)}, u32[]{:S(2)}) collective-permute-start(bf16[256,1024]{0,1:T(8,128)(2,1)S(1)} %copy-done.115), channel_id=1, source_target_pairs={{0,16},{16,0},{8,24},{24,8},{1,17},{17,1},{9,25},{25,9},{2,18},{18... | collective-permute-start | bytes 1572872 | tf_op jit(solution)/shard_map/ppermute | solution.py:353
  1230.6 33.0 %collective-permute-start.118 = (bf16[256,1024]{0,1:T(8,128)(2,1)S(1)}, bf16[256,1024]{0,1:T(8,128)(2,1)S(1)}, u32[]{:S(2)}, u32[]{:S(2)}) collective-permute-start(bf16[256,1024]{0,1:T(8,128)(2,1)S(1)} %add_convert_fusion.25), channel_id=1, source_target_pairs={{0,8},{8,0},{16,24},{24,16},{1,9},{9,1},{17,25},{25,17},{2,10},{10... | collective-permute-start | bytes 1572872 | tf_op jit(solution)/shard_map/ppermute | solution.py:349
  (262 other events, 4516.9 us)

commit v3 on v2

--- a/solution.py
+++ b/solution.py
@@ -363,45 +363,77 @@
     return lax.ppermute(values, "col", [(i, (i - 1) % count) for i in range(count)])
 
 
-def plane_gather(values):
-    half = values.shape[0] // 2
-    from_x = step_x(values)
-    from_y = step_y(values)
-    far_one = step_y(from_x[:half])
-    far_two = step_x(from_y[half:])
-    return [values, from_x, from_y, far_one, far_two]
+class Link:
+    def __init__(self):
+        self.last = None
+
+    def send(self, step, values):
+        if self.last is not None:
+            values = after(values, self.last)
+        self.last = step(values)
+        return self.last
+
+
+class Plane:
+    def __init__(self):
+        self.x = Link()
+        self.y = Link()
+
+    def near(self, values):
+        return self.x.send(step_x, values), self.y.send(step_y, values)
+
+    def far(self, from_x, from_y):
+        half = from_x.shape[0] // 2
+        far_one = self.y.send(step_y, from_x[:half])
+        far_two = self.x.send(step_x, from_y[half:])
+        return far_one, far_two
+
+    def gather(self, values):
+        from_x, from_y = self.near(values)
+        return [values, from_x, from_y, *self.far(from_x, from_y)]
+
+    def sum_early(self, here, to_x, to_y, to_far):
+        half = here.shape[0] // 2
+        f32 = jnp.float32
+        x_top = self.x.send(step_x, to_x[:half])
+        y_bottom = self.y.send(step_y, to_y[half:])
+        via_x = self.x.send(step_x, to_far[:half])
+        via_y = self.y.send(step_y, to_far[half:])
+        x_bottom = self.x.send(step_x, add_rounded(to_x[half:], via_y))
+        y_top = self.y.send(step_y, add_rounded(to_y[:half], via_x))
+        top = here[:half].astype(f32) + x_top.astype(f32) + y_top.astype(f32)
+        bottom = here[half:].astype(f32) + x_bottom.astype(f32) + y_bottom.astype(f32)
+        return jnp.concatenate([top, bottom], axis=0)
+
+    def sum_pairs(self, parts):
+        f32 = jnp.float32
+        here, to_x, to_y, to_far = parts
+        via_x = self.x.send(step_x, to_far[0])
+        via_y = self.y.send(step_y, to_far[1])
+        for_x = jnp.concatenate([to_x[0], add_rounded(to_x[1], via_y)], axis=1)
+        for_y = jnp.concatenate([add_rounded(to_y[0], via_x), to_y[1]], axis=1)
+        from_x = self.x.send(step_x, for_x)
+        from_y = self.y.send(step_y, for_y)
+        return (
+            jnp.concatenate(here, axis=1).astype(f32) + from_x.astype(f32) + from_y.astype(f32)
+        ).astype(jnp.bfloat16)
 
 
 def add_rounded(left, right):
     return (left.astype(jnp.float32) + right.astype(jnp.float32)).astype(jnp.bfloat16)
 
 
-def plane_sum(parts):
-    f32 = jnp.float32
-    first, second = parts
-    via_x = step_x(first[3])
-    via_y = step_y(second[3])
-    first_x = step_x(first[1])
-    second_y = step_y(second[2])
-    second_x = step_x(add_rounded(second[1], via_y))
-    first_y = step_y(add_rounded(first[2], via_x))
-    return (
-        first[0].astype(f32) + first_x.astype(f32) + first_y.astype(f32),
-        second[0].astype(f32) + second_x.astype(f32) + second_y.astype(f32),
-    )
-
-
-def ring_gather(values):
+def ring_gather(link, values):
     held = [values]
     for _ in range(lax.axis_size("col") - 1):
-        held.append(jax.tree.map(step_up, held[-1]))
+        held.append(link.send(step_up, held[-1]))
     return held
 
 
-def ring_sum(blocks):
+def ring_sum(link, blocks):
     total = blocks[-1]
     for block in blocks[-2::-1]:
-        total = jax.tree.map(lambda a, b: add_rounded(step_down(a), b), total, block)
+        total = add_rounded(link.send(step_down, total), block)
     return total
 
 
@@ -572,33 +604,141 @@
     )(first_row, heads, head_grad, heads, heads)
 
 
-def token_products_kernel(*refs):
-    out_ref = refs[-1]
-    count = (len(refs) - 1) // 2
-    total = mm(refs[0][...], refs[count][...], 0, 0)
-    for i in range(1, count):
-        total += mm(refs[i][...], refs[count + i][...], 0, 0)
-    out_ref[...] = total.astype(out_ref.dtype)
-
-
-def token_products(lefts, rights):
-    tokens, left_width = lefts[0].shape
-    right_width = rights[0].shape[1]
-    size = min(256, left_width)
-    count = len(lefts)
-    flops = 2 * count * tokens * left_width * right_width
+gelu_scale = 0.7978845608028654
+gelu_cubic = 0.044715
+
+
+def ffn_kernel(*refs):
+    normed_own, normed_sib, grad_own, grad_sib = [r[...] for r in refs[:4]]
+    count = (len(refs) - 7) // 2
+    own_pieces, sib_pieces = refs[4 : 4 + count], refs[4 + count : 4 + 2 * count]
+    bias_ref, out_ref, sum_ref = refs[-3:]
+    unit = own_pieces[0].shape[1] // 2
+    units = unit * count
+
+    @pl.when(pl.program_id(0) == 0)
+    def _():
+        sum_ref[...] = jnp.zeros_like(sum_ref)
+
+    for k in range(count):
+        own_piece, sib_piece = own_pieces[k], sib_pieces[k]
+        span = slice(k * unit, (k + 1) * unit)
+        pre = mm(normed_own, own_piece[:, :unit], 1, 0) + mm(normed_sib, sib_piece[:, :unit], 1, 0)
+        act_grad = mm(grad_own, own_piece[:, unit:], 1, 0) + mm(grad_sib, sib_piece[:, unit:], 1, 0)
+        pre = pre + bias_ref[:, span]
+        square = pre * pre
+        bent = jnp.tanh(gelu_scale * pre * (1.0 + gelu_cubic * square))
+        half = 0.5 * (1.0 + bent)
+        slope = half + 0.5 * gelu_scale * pre * (1.0 - bent * bent) * (1.0 + 3.0 * gelu_cubic * square)
+        pre_grad = (act_grad * slope).astype(jnp.bfloat16)
+        out_ref[:, span] = (pre * half).astype(jnp.bfloat16)
+        out_ref[:, units + k * unit : units + (k + 1) * unit] = pre_grad
+        sum_ref[:, span] += jnp.sum(pre_grad.astype(jnp.float32), axis=0, keepdims=True)
+
+
+def ffn_rows_of(normed, grad, own_pieces, sib_pieces, bias):
+    tokens, width = normed[0].shape
+    count = len(own_pieces)
+    unit = sib_pieces[0].shape[1] // 2
+    units = unit * count
+    size = min(256, tokens)
+    rows = pl.BlockSpec((size, width), lambda i: (i, 0))
+    piece = pl.BlockSpec((width, 2 * unit), lambda i: (0, 0))
     return pl.pallas_call(
-        token_products_kernel,
-        grid=(left_width // size,),
-        in_specs=[pl.BlockSpec((tokens, size), lambda i: (0, i))] * count
-        + [pl.BlockSpec((tokens, right_width), lambda i: (0, 0))] * count,
-        out_specs=pl.BlockSpec((size, right_width), lambda i: (i, 0)),
-        out_shape=jax.ShapeDtypeStruct((left_width, right_width), jnp.bfloat16),
+        ffn_kernel,
+        grid=(tokens // size,),
+        in_specs=[rows] * 4 + [piece] * (2 * count) + [pl.BlockSpec((1, units), lambda i: (0, 0))],
+        out_specs=[
+            pl.BlockSpec((size, 2 * units), lambda i: (i, 0)),
+            pl.BlockSpec((1, units), lambda i: (0, 0)),
+        ],
+        out_shape=[
+            jax.ShapeDtypeStruct((tokens, 2 * units), jnp.bfloat16),
+            jax.ShapeDtypeStruct((1, units), jnp.float32),
+        ],
         compiler_params=pltpu.CompilerParams(vmem_limit_bytes=vmem_bytes),
         cost_estimate=pl.CostEstimate(
-            flops=flops, bytes_accessed=2 * count * tokens * (left_width + right_width), transcendentals=0
+            flops=8 * tokens * width * units,
+            bytes_accessed=8 * tokens * width + 8 * width * units + 4 * tokens * units,
+            transcendentals=0,
         ),
-    )(*lefts, *rights)
+    )(*normed, *grad, *own_pieces, *sib_pieces, bias)
+
+
+def unit_products_kernel(offset, own_ref, sib_ref, *refs):
+    out_ref = refs[-1]
+    unit = refs[0].shape[1] // 4
+    total = None
+    for k, piece in enumerate(refs[:-1]):
+        span = slice(k * unit, (k + 1) * unit)
+        for rows, start in ((own_ref, offset * unit), (sib_ref, (offset + 2) * unit)):
+            part = mm(rows[:, span], piece[:, start : start + unit], 1, 1)
+            total = part if total is None else total + part
+    out_ref[...] = total.astype(jnp.bfloat16)
+
+
+def unit_products(own_rows, sib_rows, pieces, which):
+    tokens, twice = own_rows.shape
+    width = pieces[0].shape[0]
+    units = twice // 2
+    size = min(256, tokens)
+    rows = pl.BlockSpec((size, units), lambda i: (i, which))
+    piece = pl.BlockSpec(pieces[0].shape, lambda i: (0, 0))
+    return pl.pallas_call(
+        functools.partial(unit_products_kernel, 1 - which),
+        grid=(tokens // size,),
+        in_specs=[rows] * 2 + [piece] * len(pieces),
+        out_specs=pl.BlockSpec((size, width), lambda i: (i, 0)),
+        out_shape=jax.ShapeDtypeStruct((tokens, width), jnp.bfloat16),
+        compiler_params=pltpu.CompilerParams(vmem_limit_bytes=vmem_bytes),
+        cost_estimate=pl.CostEstimate(
+            flops=4 * tokens * units * width,
+            bytes_accessed=6 * tokens * units + 4 * units * width,
+            transcendentals=0,
+        ),
+    )(own_rows, sib_rows, *pieces)
+
+
+def weight_products_kernel(count, *refs):
+    out_ref = refs[-1]
+    normed, grads = refs[:count], refs[count : 2 * count]
+    act_own, pre_own, act_sib, pre_sib = [
+        refs[(2 + i) * count : (3 + i) * count] for i in range(4)
+    ]
+    unit = act_own[0].shape[1]
+    up = down = None
+    for j in range(count):
+        pre = jnp.concatenate([pre_own[j][...], pre_sib[j][...]], axis=1)
+        act = jnp.concatenate([act_own[j][...], act_sib[j][...]], axis=1)
+        up_part = mm(normed[j][...], pre, 0, 0)
+        down_part = mm(grads[j][...], act, 0, 0)
+        up = up_part if up is None else up + up_part
+        down = down_part if down is None else down + down_part
+    for i, part in enumerate((up[:, :unit], down[:, :unit], up[:, unit:], down[:, unit:])):
+        out_ref[0, :, i * unit : (i + 1) * unit] = part.astype(jnp.bfloat16)
+
+
+def weight_products(normed, grads, own_rows, sib_rows, unit):
+    count = len(normed)
+    tokens, width = normed[0].shape
+    ring = own_rows[0].shape[1] // (2 * unit)
+    size = min(256, width)
+    left = [pl.BlockSpec((tokens, size), lambda k, d: (0, d))] * (2 * count)
+    act = [pl.BlockSpec((tokens, unit), lambda k, d: (0, k))] * count
+    pre = [pl.BlockSpec((tokens, unit), lambda k, d: (0, ring + k))] * count
+    return pl.pallas_call(
+        functools.partial(weight_products_kernel, count),
+        grid=(ring, width // size),
+        in_specs=left + act + pre + act + pre,
+        out_specs=pl.BlockSpec((1, size, 4 * unit), lambda k, d: (k, d, 0)),
+        out_shape=jax.ShapeDtypeStruct((ring, width, 4 * unit), jnp.bfloat16),
+        compiler_params=pltpu.CompilerParams(vmem_limit_bytes=vmem_bytes),
+        cost_estimate=pl.CostEstimate(
+            flops=8 * count * tokens * width * ring * unit,
+            bytes_accessed=16 * count * tokens * width,
+            transcendentals=0,
+        ),
+    )(*normed, *grads, *own_rows, *own_rows, *sib_rows, *sib_rows)
 
 
 def body_local(
@@ -632,65 +772,76 @@
     block = width // 4
     quarter = up_weight.shape[1] // 4
     unit = quarter // 2
-
-    def by_core(weight, size, offset=0):
-        return [
-            lax.dynamic_slice_in_dim(weight, offset + which * size, size, axis=1)
-            for which in (row_i, 1 - row_i)
-        ]
-
-    four = [by_core(w, own) for w in (query_weight, key_weight, value_weight, out_weight.T)]
-    four = jnp.concatenate([w[0] for w in four] + [w[1] for w in four], axis=1)
-    four = exchanged(four, plane_i, 0)
-
-    tokens_sib = swap(tokens_in)
-
-    ff_offset = plane_i * quarter
-    up_piece = jnp.concatenate(by_core(up_weight, unit, ff_offset), axis=1)
-    down_piece = jnp.concatenate(
-        [
-            lax.dynamic_slice_in_dim(down_weight, ff_offset + which * unit, unit, axis=0)
-            for which in (row_i, 1 - row_i)
-        ],
-        axis=0,
-    )
+    half_rows = rows // 2
+    plane, column = Plane(), Link()
+    both_cores = (row_i, 1 - row_i)
+
+    def cut(weight, start, size, axis):
+        return lax.dynamic_slice_in_dim(weight, start, size, axis=axis)
+
+    def by_core(weights, size):
+        return jnp.concatenate(
+            [cut(w, which * size, size, 1) for which in both_cores for w in weights], axis=1
+        )
+
+    names = (query_weight, key_weight, value_weight)
+    piece = [cut(w, plane_i * block, block, 0) for w in names]
+    piece.append(cut(out_weight, plane_i * block, block, 1).T)
+    pieces = ring_gather(column, by_core(piece, own))
 
     active_all = active_rows(segment_ids, active_lengths)
     active_here = lax.dynamic_slice_in_dim(active_all, col_i * rows, rows)
     keep_mask = active_here.astype(f32)[:, None]
+    branch_mine = (out_grad.astype(f32) * keep_mask).astype(bf16)
+    branch_first = plane.near(branch_mine[:half_rows])
+
+    tokens_sib = swap(tokens_in)
+    gains = jnp.stack([norm1_gain, norm1_shift])
+    gains_sib = swap(gains)
+
     segment_row = picked(segment_ids, col_i)
     member = (segment_row[:, None] == jnp.arange(active_lengths.shape[1])).astype(jnp.int32)
     counts = jnp.sum(member, axis=0)
     first_row = jnp.sum(member * (jnp.cumsum(counts) - counts), axis=1)[None, :]
 
-    branch_mine = (out_grad.astype(f32) * keep_mask).astype(bf16)
-
-    query_part = lax.dynamic_slice_in_dim(query_bias, row_i * own, own)
-    value_part = lax.dynamic_slice_in_dim(value_bias, row_i * own, own)
-    up_part = lax.dynamic_slice_in_dim(up_bias, ff_offset + row_i * unit, unit)
+    ff_offset = plane_i * quarter
+    query_part = cut(query_bias, row_i * own, own, 0)
+    value_part = cut(value_bias, row_i * own, own, 0)
+    up_part = cut(up_bias, ff_offset + row_i * unit, unit, 0)
     small = ring_gather(
-        jnp.concatenate([query_part, jnp.zeros_like(query_part), value_part, up_part])
-    )
-    up_biases = jnp.concatenate([s[3 * own :] for s in small])
-
-    pieces = ring_gather(four[:block])
-    own_rows, other_units = [four[:, : 4 * own]], [four[:, 4 * own :]]
+        Link(), jnp.concatenate([query_part, jnp.zeros_like(query_part), value_part, up_part])
+    )
+    up_biases = jnp.concatenate([s[3 * own :] for s in small])[None, :]
+
+    here = by_core(names + (out_weight.T,), own)
+    here = exchanged(here, plane_i, 0)
+    own_rows, other_units = [here[:, : 4 * own]], [here[:, 4 * own :]]
     for piece in pieces[1:]:
-        gathered = plane_gather(piece)
+        gathered = plane.gather(piece)
         own_rows.append(jnp.concatenate([p[:, : 4 * own] for p in gathered], axis=0))
         other_units.append(jnp.concatenate([p[:, 4 * own :] for p in gathered], axis=0))
     groups = [jnp.concatenate([a, swap(b)], axis=0) for a, b in zip(own_rows, other_units)]
 
-    gains = jnp.stack([norm1_gain, norm1_shift])
-    gains_sib = swap(gains)
+    branch_far = plane.far(*branch_first)
+    branch_second = plane.gather(branch_mine[half_rows:])
+    branch_first = [branch_mine[:half_rows], *branch_first, jnp.concatenate(branch_far, axis=0)]
+    branch_second = branch_second[:3] + [jnp.concatenate(branch_second[3:], axis=0)]
+    branch_own = [branch_mine] + [
+        jnp.concatenate([a, b], axis=0) for a, b in zip(branch_first[1:], branch_second[1:])
+    ]
+    branch_sib = [swap(b) for b in branch_own]
+
+    down_part = cut(down_weight, ff_offset, quarter, 0).T
+    up_part = cut(up_weight, ff_offset, quarter, 1)
+    ff_own = ring_gather(column, by_core((up_part, down_part), unit))
+    ff_sib = [swap(p[:, 2 * unit :]) for p in ff_own]
+
     tokens_own = tokens_in.astype(f32)
     tokens_all = jnp.concatenate([tokens_own, tokens_sib.astype(f32)], axis=1)
     average_one, inverse_one = row_norm(tokens_all)
     normed_one = jnp.concatenate(
         [
-            exchanged(
-                (((t - average_one) * inverse_one) * g[0] + g[1]).astype(bf16), plane_i, 1
-            )
+            exchanged((((t - average_one) * inverse_one) * g[0] + g[1]).astype(bf16), plane_i, 1)
             for t, g in ((tokens_own, gains), (tokens_sib.astype(f32), gains_sib))
         ],
         axis=1,
@@ -709,11 +860,6 @@
         attention_rows = part if k == 0 else attention_rows + part
     hidden_one = tokens_own + exchanged(attention_rows, plane_i, 1) + out_bias
 
-    def both_sums(one, two):
-        sums = jnp.stack([jnp.sum(one, axis=1), jnp.sum(two, axis=1)])
-        sums = (sums + swap(sums)) / (2 * width)
-        return sums[0][:, None], sums[1][:, None]
-
     half_mean = jnp.mean(hidden_one, axis=1, keepdims=True)
     centered = hidden_one - half_mean
     half_square = jnp.mean(centered * centered, axis=1, keepdims=True)
@@ -726,43 +872,36 @@
     normal_two = (hidden_one - average_two) * inverse_two
     normed_two = (normal_two * norm2_gain + norm2_shift).astype(bf16)
 
-    ff_pieces = ring_gather((up_piece, down_piece))
-    up_own = jnp.concatenate([p[0][:, :unit] for p in ff_pieces], axis=1)
-    up_sib = jnp.concatenate([p[0][:, unit:] for p in ff_pieces], axis=1)
-    down_own = jnp.concatenate([p[1][:unit] for p in ff_pieces], axis=0)
-    down_sib = jnp.concatenate([p[1][unit:] for p in ff_pieces], axis=0)
-    up_full = jnp.concatenate([up_own, swap(up_sib)], axis=0)
-    down_full = jnp.concatenate([down_own, swap(down_sib)], axis=1)
-    up_half = jnp.concatenate([up_own, up_sib], axis=1)
-    down_half = jnp.concatenate([down_own, down_sib], axis=0)
-
-    def gathered_tokens(values):
-        here, from_x, from_y, far_one, far_two = plane_gather(values)
-        own_parts = [here, from_x, from_y, jnp.concatenate([far_one, far_two], axis=0)]
-        return own_parts, [jnp.concatenate([p, swap(p)], axis=1) for p in own_parts]
-
-    branch_own, branch_all = gathered_tokens(branch_mine)
-    normed_own, normed_all = gathered_tokens(normed_two)
-    half_rows = rows // 2
-    acts, act_sibs, pre_grads, pre_sibs, grad_parts, down_parts = [], [], [], [], [], []
+    normed_own = plane.gather(normed_two)
+    normed_own = normed_own[:3] + [jnp.concatenate(normed_own[3:], axis=0)]
+    chips, chip_sibs, up_sums = [], [], []
     for j in range(4):
-        pre_act = mm(normed_all[j], up_full, 1, 0) + up_biases
-        act = gelu_value(pre_act).astype(bf16)
-        pre_grad = (mm(branch_all[j], down_full, 1, 1) * gelu_slope(pre_act)).astype(bf16)
-        acts.append(act)
-        pre_grads.append(pre_grad)
-        pre_sibs.append(swap(pre_grad))
-        act_sibs.append(swap(act))
-        chip = jnp.concatenate([pre_grad, pre_sibs[j]], axis=1)
-        grad_parts.append(mm(chip, up_half, 1, 1, bf16))
-    normed_grad_two = jnp.concatenate(
-        plane_sum([[g[:half_rows] for g in grad_parts], [g[half_rows:] for g in grad_parts]]), axis=0
-    )
-    for j in range(4):
-        chip = jnp.concatenate([acts[j], act_sibs[j]], axis=1)
-        down_parts.append(mm(chip, down_half, 1, 0, bf16))
-    up_grads = (token_products(normed_own, pre_grads), token_products(normed_own, pre_sibs))
-    down_grads = (token_products(acts, branch_own), token_products(act_sibs, branch_own))
+        normed = (normed_own[j], swap(normed_own[j]))
+        if j > 0:
+            normed = after(normed, chips[-1])
+        chip, up_sum = ffn_rows_of(normed, (branch_own[j], branch_sib[j]), ff_own, ff_sib, up_biases)
+        chips.append(chip)
+        chip_sibs.append(swap(chip))
+        up_sums.append(up_sum)
+    grad_parts = [None] * 4
+    last = chips[3]
+    for j in (1, 2, 3, 0):
+        grad_parts[j] = unit_products(after(chips[j], last), chip_sibs[j], ff_own, 1)
+        last = grad_parts[j]
+    normed_grad_two = plane.sum_early(*grad_parts)
+    down_parts = [None] * 4
+    for j in (1, 2, 3, 0):
+        down_parts[j] = unit_products(after(chips[j], last), chip_sibs[j], ff_own, 0)
+        last = down_parts[j]
+    ff_grads = weight_products(normed_own, branch_own, [after(chips[0], last)] + chips[1:], chip_sibs, unit)
+    ff_sum = ring_sum(column, [ff_grads[k] for k in range(ring)])
+    ffn_rows = plane.sum_early(*down_parts) + down_bias
+    layer_out = jnp.where(active_here[:, None], hidden_one + ffn_rows, tokens_own)
+
+    def both_sums(one, two):
+        sums = jnp.stack([jnp.sum(one, axis=1), jnp.sum(two, axis=1)])
+        sums = (sums + swap(sums)) / (2 * width)
+        return sums[0][:, None], sums[1][:, None]
 
     scaled = normed_grad_two * norm2_gain
     mean_one, mean_two = both_sums(scaled, scaled * normal_two)
@@ -776,28 +915,25 @@
     reduced = [None] * ring
     normed_grad_one = None
     bias_rows = [None] * ring
+    last = grad_blocks
     for k in range(ring - 1, -1, -1):
         weights = groups[k]
-        head_grad = mm(grad_blocks, weights[:, 3 * own :], 1, 0, bf16)
+        head_grad = mm(after(grad_blocks, last), weights[:, 3 * own :], 1, 0, bf16)
         grads = local_backward(heads[k], head_grad, first_row)
+        weight_grads = jnp.concatenate(
+            [mm(normed_one, grads, 0, 0, bf16), mm(grad_blocks, attended[k], 0, 0, bf16)], axis=1
+        )
+        last = weight_grads
+        mine = weight_grads[:width]
+        arrived = swap(weight_grads[width:])
+        reduced[k] = plane.sum_pairs(
+            [[m[j * block : (j + 1) * block] for m in (mine, arrived)] for j in range(4)]
+        )
+        bias_rows[k] = jnp.sum(grads.astype(f32), axis=0)
         part = mm(grads, weights[:, : 3 * own], 1, 1)
         normed_grad_one = part if normed_grad_one is None else normed_grad_one + part
-        weight_grads = jnp.concatenate(
-            [mm(normed_one, grads, 0, 0, bf16), mm(grad_blocks, attended[k], 0, 0, bf16)], axis=1
-        )
-        mine = weight_grads[:width]
-        arrived = swap(weight_grads[width:])
-        reduced[k] = [
-            r.astype(bf16)
-            for r in plane_sum(
-                [[m[j * block : (j + 1) * block] for j in range(4)] for m in (mine, arrived)]
-            )
-        ]
-        bias_rows[k] = jnp.sum(grads.astype(f32), axis=0)
-    head_sum = ring_sum(reduced)
-    head_mine, head_sib = [
-        exchanged(jnp.concatenate(plane_gather(h), axis=0), plane_i, 0) for h in head_sum
-    ]
+    head_sum = ring_sum(column, reduced)
+    head_all = exchanged(jnp.concatenate(plane.gather(head_sum), axis=0), plane_i, 0)
 
     def by_row(mine, sib, axis):
         return jnp.where(
@@ -807,37 +943,20 @@
         )
 
     query_weight_grad, key_weight_grad, value_weight_grad, out_weight_grad = [
-        by_row(head_mine[:, m * own : (m + 1) * own], head_sib[:, m * own : (m + 1) * own], 1).astype(f32)
+        by_row(head_all[:, m * own : (m + 1) * own], head_all[:, (4 + m) * own : (5 + m) * own], 1).astype(f32)
         for m in range(4)
     ]
     out_weight_grad = out_weight_grad.T
 
-    ffn_rows = plane_sum([[d[:half_rows] for d in down_parts], [d[half_rows:] for d in down_parts]])
-    ffn_rows = jnp.concatenate(ffn_rows, axis=0) + down_bias
-    layer_out = jnp.where(active_here[:, None], hidden_one + ffn_rows, tokens_own)
-    ff_sums = ring_sum(
-        [
-            (
-                up_grads[0][:, k * unit : (k + 1) * unit],
-                up_grads[1][:, k * unit : (k + 1) * unit],
-                down_grads[0][k * unit : (k + 1) * unit],
-                down_grads[1][k * unit : (k + 1) * unit],
-            )
-            for k in range(ring)
-        ]
-    )
-    ff_gathered = []
-    for total in ff_sums:
-        here, from_x, from_y, far_one, far_two = plane_gather(total)
-        ff_gathered.append(jnp.stack([here, from_x, from_y, jnp.concatenate([far_one, far_two])]))
-
-    def placed(mine, sib, axis):
-        return jnp.concatenate(
-            [by_row(picked(mine, plane_i ^ q), picked(sib, plane_i ^ q), axis) for q in range(4)], axis=axis
-        ).astype(f32)
-
-    up_weight_grad = placed(ff_gathered[0], ff_gathered[1], 1)
-    down_weight_grad = placed(ff_gathered[2], ff_gathered[3], 0)
+    ff_all = plane.gather(ff_sum)
+    ff_all = jnp.stack(ff_all[:3] + [jnp.concatenate(ff_all[3:], axis=0)])
+    up_parts, down_cuts = [], []
+    for q in range(4):
+        part = picked(ff_all, plane_i ^ q)
+        up_parts.append(by_row(part[:, :unit], part[:, 2 * unit : 3 * unit], 1))
+        down_cuts.append(by_row(part[:, unit : 2 * unit], part[:, 3 * unit :], 1))
+    up_weight_grad = jnp.concatenate(up_parts, axis=1).astype(f32)
+    down_weight_grad = jnp.concatenate(down_cuts, axis=1).T.astype(f32)
 
     normed_grad_one = normed_grad_one[:, :width] + swap(
         normed_grad_one[:, width:].astype(bf16)
@@ -858,8 +977,7 @@
     row_hot = (jnp.arange(2) == row_i).astype(f32)
     plane_hot = (jnp.arange(4) == plane_i).astype(f32)
     head_bias = by_column(jnp.stack(bias_rows)).reshape(ring, 3, 1, own) * row_hot[:, None]
-    up_bias_part = sum(jnp.sum(p.astype(f32), axis=0) for p in pre_grads).reshape(ring, unit)
-    up_bias_part = by_column(up_bias_part).reshape(ring, 1, 1, unit)
+    up_bias_part = by_column(sum(up_sums).reshape(ring, unit)).reshape(ring, 1, 1, unit)
     up_bias_part = up_bias_part * plane_hot[:, None, None] * row_hot[:, None]
     bias_vector = jnp.concatenate([head_bias.reshape(ring, -1), up_bias_part.reshape(ring, -1)], axis=1)
     bias_vector = bias_vector + swap(bias_vector)

time: 1310 us -> 1210 us (0.924)
  matrix products: 256 us -> 90.1 us
  Pallas kernels: 132 us -> 260 us
  waiting for transfers between devices: 489 us -> 420 us
  local copies, waits for them, and re-layouts: 164 us -> 220 us
  starting transfers between devices: 137 us -> 101 us
  other arithmetic: 121 us -> 104 us
    dot_general x40 -> x24, matrix products: 256 us -> 90.1 us  [mm(): lax.dot_general(left, right, (((left_dim,), (right_dim,)), ((), ())), pre...]
    ppermute x41 -> x31, waiting for transfers between devices: 229 us -> 81.6 us  [step_y(): return lax.ppermute(values, 'dp', [(0, 2), (2, 0), (1, 3), (3, 1)])]
    pallas_call x4 -> x13, Pallas kernels: 55.2 us -> 184 us  [the longest x8 68.7 us: unit_products(): pl.pallas_call(functools.partial(unit_products_kernel, 1 - which), grid=(...]
    ppermute x41 -> x31, waiting for transfers between devices: 120 us -> 189 us  [step_x(): return lax.ppermute(values, 'dp', [(0, 1), (1, 0), (2, 3), (3, 2)])]
    unnamed x415 -> x412, local copies, waits for them, and re-layouts: 87 us -> 141 us
    ppermute x41 -> x31, starting transfers between devices: 44 us -> 25 us  [step_x(): return lax.ppermute(values, 'dp', [(0, 1), (1, 0), (2, 3), (3, 2)])]
    ppermute x41 -> x31, starting transfers between devices: 49.6 us -> 35.3 us  [step_y(): return lax.ppermute(values, 'dp', [(0, 2), (2, 0), (1, 3), (3, 1)])]
    ppermute x12 -> x9, waiting for transfers between devices: 77.5 us -> 82.3 us  [step_up(): lax.ppermute(values, 'col', [(i, (i + 1) % count) for i in range(count)])]
  transfers between devices with their start and end apart: 152 -> 115, of which waited for: 51 -> 44; matrix products, arithmetic and copies ran while one was open for 34% -> 22% of each run, Pallas kernels for 6% -> 18%
where the time goes in v3:
time: 1210 us; the launch traced here: 1200 us
  waiting for transfers between devices  420 us (35%)
  Pallas kernels  260 us (21%)
  local copies, waits for them, and re-layouts  220 us (18%)
  other arithmetic  104 us (9%)
  starting transfers between devices  101 us (8%)
  matrix products  90.1 us (7%)
    ppermute x31, waiting for transfers between devices, step_x(): return lax.ppermute(values, 'dp', [(0, 1), (1, 0), (2, 3), (3, 2)])  189 us
    unnamed x412, local copies, waits for them, and re-layouts  141 us
    dot_general x24, matrix products, mm(): lax.dot_general(left, right, (((left_dim,), (right_dim,)), ((), ())), pre...  90.1 us
    ppermute x9, waiting for transfers between devices, step_up(): lax.ppermute(values, 'col', [(i, (i + 1) % count) for i in range(count)])  82.3 us
    ppermute x31, waiting for transfers between devices, step_y(): return lax.ppermute(values, 'dp', [(0, 2), (2, 0), (1, 3), (3, 1)])  81.6 us
    pallas_call x8, Pallas kernels, unit_products(): pl.pallas_call(functools.partial(unit_products_kernel, 1 - which), grid=(...  68.7 us
    pallas_call x4, Pallas kernels, ffn_rows_of(): pl.pallas_call(ffn_kernel, grid=(tokens // size,), in_specs=[rows] * 4 +...  62.4 us
    ppermute x6, waiting for transfers between devices, step_down(): lax.ppermute(values, 'col', [(i, (i - 1) % count) for i in range(count)])  55.1 us
  transfers between devices with their start and end apart: 115, of which 44 were waited for; matrix products, arithmetic and copies ran while one was open for 22% of the time, Pallas kernels for 18%

profile of v3, /device:TPU:0, one launch (start us, length us, event | category | flops | bytes accessed | tf_op | source)
XLA Modules:
  0.0 1199.8 jit_solution(10068565794575611946)
XLA Ops:
  82.2 24.3 %collective-permute-done.20 = f32[1024]{0:T(1024)S(1)} collective-permute-done((f32[1024]{0:T(1024)}, f32[1024]{0:T(1024)S(1)}, u32[]{:S(2)}, u32[]{:S(2)}) %collective-permute-start.20) | collective-permute-done | bytes 4128 | tf_op jit(solution)/shard_map/ppermute | solution.py:358
  137.2 6.5 shard_map.314
  143.7 9.3 collective-permute-done.15
  160.5 4.9 collective-permute-done.18
  175.1 15.0 %collective-permute-done.24 = bf16[256,2048]{0,1:T(8,128)(2,1)S(1)} collective-permute-done((bf16[256,2048]{0,1:T(8,128)(2,1)}, bf16[256,2048]{0,1:T(8,128)(2,1)S(1)}, u32[]{:S(2)}, u32[]{:S(2)}) %collective-permute-start.24) | collective-permute-done | bytes 1048608 | tf_op jit(solution)/shard_map/ppermute | solution.py:353
  194.1 6.0 collective-permute-done.25
  205.6 4.1 add_convert_fusion.5.query_ref.key_ref.value_ref
  209.8 6.5 shard_map.315
  219.4 5.3 add_convert_fusion.4.query_ref.key_ref.value_ref
  224.8 6.7 shard_map.316
  238.8 6.5 shard_map.317
  270.5 15.0 %collective-permute-done.43 = bf16[512,1024]{1,0:T(8,128)(2,1)S(1)} collective-permute-done((bf16[512,1024]{1,0:T(8,128)(2,1)S(1)}, bf16[512,1024]{1,0:T(8,128)(2,1)S(1)}, u32[]{:S(2)}, u32[]{:S(2)}) %collective-permute-start.43) | collective-permute-done | bytes 1048608 | tf_op jit(solution)/shard_map/ppermute | solution.py:349
  288.7 16.0 %collective-permute-done.34.refs_6_.refs_2_ = bf16[1024,1024]{1,0:T(8,128)(2,1)S(1)} collective-permute-done((bf16[1024,1024]{1,0:T(8,128)(2,1)S(1)}, bf16[1024,1024]{1,0:T(8,128)(2,1)S(1)}, u32[]{:S(2)}, u32[]{:S(2)}) %collective-permute-start.34) | collective-permute-done | bytes 2097184 | tf_op jit(solution)/shard_map/ppermute | solution.py:358
  311.5 42.0 %collective-permute-done.35.refs_7_.refs_3_ = bf16[1024,1024]{1,0:T(8,128)(2,1)S(1)} collective-permute-done((bf16[1024,1024]{1,0:T(8,128)(2,1)S(1)}, bf16[1024,1024]{1,0:T(8,128)(2,1)S(1)}, u32[]{:S(2)}, u32[]{:S(2)}) %collective-permute-start.35) | collective-permute-done | bytes 2097184 | tf_op jit(solution)/shard_map/ppermute | solution.py:358
  363.1 18.1 %collective-permute-done.49 = bf16[512,1024]{1,0:T(8,128)(2,1)S(1)} collective-permute-done((bf16[512,1024]{1,0:T(8,128)(2,1)S(1)}, bf16[512,1024]{1,0:T(8,128)(2,1)S(1)}, u32[]{:S(2)}, u32[]{:S(2)}) %collective-permute-start.49) | collective-permute-done | bytes 1048608 | tf_op jit(solution)/shard_map/ppermute | solution.py:349
  384.2 15.9 %shard_map.318 = (bf16[1024,2048]{1,0:T(8,128)(2,1)}, f32[1,1024]{1,0:T(1,128)S(1)}) custom-call(bf16[1024,1024]{1,0:T(8,128)(2,1)} %copy-done.8, bf16[1024,1024]{1,0:T(8,128)(2,1)} %copy-done.160, bf16[1024,1024]{1,0:T(8,128)(2,1)} %copy-done.49, bf16[1024,1024]{1,0:T(8,128)(2,1)} %copy-done.159, bf16[1024,1024]{1,0:T(8,128)(2,1)} %copy-done, ...), custom_call_target="tpu_custom_call" | custom-call | flops 8589934592 | bytes 20971520 | tf_op jit(solution)/shard_map/pallas_call | solution.py:647
  400.0 15.5 %shard_map.319 = (bf16[1024,2048]{1,0:T(8,128)(2,1)}, f32[1,1024]{1,0:T(1,128)S(1)}) custom-call(bf16[1024,1024]{1,0:T(8,128)(2,1)} %copy-done.14, bf16[1024,1024]{1,0:T(8,128)(2,1)} %copy-done.161, bf16[1024,1024]{1,0:T(8,128)(2,1)} %copy-done.112, bf16[1024,1024]{1,0:T(8,128)(2,1)} %collective-permute-done.53.refs_3_, bf16[1024,1024]{1,0:T(8,128)(2,1)} %copy-done, ...), custom_call_target="tpu_custom_call" | custom-call | flops 8589934592 | bytes 20971520 | tf_op jit(solution)/shard_map/pallas_call | solution.py:647
  415.7 15.5 %shard_map.320 = (bf16[1024,2048]{1,0:T(8,128)(2,1)}, f32[1,1024]{1,0:T(1,128)S(1)}) custom-call(bf16[1024,1024]{1,0:T(8,128)(2,1)} %copy-done.110, bf16[1024,1024]{1,0:T(8,128)(2,1)} %collective-permute-done.51.refs_1_, bf16[1024,1024]{1,0:T(8,128)(2,1)} %copy-done.111, bf16[1024,1024]{1,0:T(8,128)(2,1)} %collective-permute-done.54.refs_3_, ...), custom_call_target="tpu_custom_call" | custom-call | flops 8589934592 | bytes 20971520 | tf_op jit(solution)/shard_map/pallas_call | solution.py:647
  431.5 15.6 %shard_map.321 = (bf16[1024,2048]{1,0:T(8,128)(2,1)}, f32[1,1024]{1,0:T(1,128)S(1)}) custom-call(bf16[1024,1024]{1,0:T(8,128)(2,1)} %copy-done.113, bf16[1024,1024]{1,0:T(8,128)(2,1)} %collective-permute-done.50.refs_1_, bf16[1024,1024]{1,0:T(8,128)(2,1)} %copy-done.119, bf16[1024,1024]{1,0:T(8,128)(2,1)} %collective-permute-done.55.refs_3_, ...), custom_call_target="tpu_custom_call" | custom-call | flops 8589934592 | bytes 20971520 | tf_op jit(solution)/shard_map/pallas_call | solution.py:647
  447.6 8.4 shard_map.322
  456.1 9.0 shard_map.323
  470.7 8.4 shard_map.324
  479.1 8.4 shard_map.325
  487.6 9.1 shard_map.326
  496.7 8.4 shard_map.327
  505.2 8.4 shard_map.328
  514.9 8.4 shard_map.329
  528.4 52.8 %shard_map.334 = bf16[4,1024,1024]{2,1,0:T(8,128)(2,1)} custom-call(bf16[1024,1024]{1,0:T(8,128)(2,1)S(1)} %copy-done.9, bf16[1024,1024]{1,0:T(8,128)(2,1)S(1)} %copy-done.15, bf16[1024,1024]{1,0:T(8,128)(2,1)} %copy-done.110, bf16[1024,1024]{1,0:T(8,128)(2,1)} %copy-done.113, bf16[1024,1024]{1,0:T(8,128)(2,1)} %copy-done.49, ...), custom_call_target="tpu_custom_call" | custom-call | flops 34359738368 | bytes 67108864 | tf_op jit(solution)/shard_map/pallas_call | solution.py:729
  590.5 19.6 %collective-permute-done.64 = bf16[512,1024]{1,0:T(8,128)(2,1)S(1)} collective-permute-done((bf16[512,1024]{1,0:T(8,128)(2,1)S(1)}, bf16[512,1024]{1,0:T(8,128)(2,1)S(1)}, u32[]{:S(2)}, u32[]{:S(2)}) %collective-permute-start.64) | collective-permute-done | bytes 1048608 | tf_op jit(solution)/shard_map/ppermute | solution.py:349
  613.5 19.9 %collective-permute-done.65 = bf16[512,1024]{1,0:T(8,128)(2,1)S(1)} collective-permute-done((bf16[512,1024]{1,0:T(8,128)(2,1)S(1)}, bf16[512,1024]{1,0:T(8,128)(2,1)S(1)}, u32[]{:S(2)}, u32[]{:S(2)}) %collective-permute-start.65) | collective-permute-done | bytes 1048608 | tf_op jit(solution)/shard_map/ppermute | solution.py:349
  641.8 14.3 %collective-permute-done.66 = bf16[512,1024]{1,0:T(8,128)(2,1)} collective-permute-done((bf16[512,1024]{1,0:T(8,128)(2,1)}, bf16[512,1024]{1,0:T(8,128)(2,1)}, u32[]{:S(2)}, u32[]{:S(2)}) %collective-permute-start.66) | collective-permute-done | bytes 1048608 | tf_op jit(solution)/shard_map/ppermute | solution.py:349
  666.2 16.7 %collective-permute-done.87 = bf16[1024,1024]{1,0:T(8,128)(2,1)S(1)} collective-permute-done((bf16[1024,1024]{1,0:T(8,128)(2,1)S(1)}, bf16[1024,1024]{1,0:T(8,128)(2,1)S(1)}, u32[]{:S(2)}, u32[]{:S(2)}) %collective-permute-start.87) | collective-permute-done | bytes 2097184 | tf_op jit(solution)/shard_map/ppermute | solution.py:363
  685.2 4.7 collective-permute-start.88
  691.4 6.0 convert_reduce_fusion.1
  702.5 29.9 %collective-permute-done.88 = bf16[1024,1024]{1,0:T(8,128)(2,1)S(1)} collective-permute-done((bf16[1024,1024]{1,0:T(8,128)(2,1)}, bf16[1024,1024]{1,0:T(8,128)(2,1)S(1)}, u32[]{:S(2)}, u32[]{:S(2)}) %collective-permute-start.88) | collective-permute-done | bytes 2097184 | tf_op jit(solution)/shard_map/ppermute | solution.py:363
  732.4 3.9 fusion.8
  749.1 12.5 %shard_map.332 = bf16[1024,768]{1,0:T(8,128)(2,1)S(1)} custom-call(s32[1,1024]{1,0:T(1,128)S(1)} %bitcast.120, bf16[1024,768]{1,0:T(8,128)(2,1)S(1)} %copy-done.29, bf16[1024,256]{1,0:T(8,128)(2,1)S(1)} %convolution_convert_fusion.9.grad_ref, bf16[1024,768]{1,0:T(8,128)(2,1)S(1)} %copy-done.29, bf16[1024,768]{1,0:T(8,128)(2,1)S(1)} %copy-done.29), custom_call_target="tpu_custom_call" | custom-call | flops 8589934592 | bytes 6291456 | tf_op jit(solution)/shard_map/pallas_call | solution.py:587
  761.9 7.1 convolution_convert_fusion.1
  769.0 5.6 fusion.20
  777.3 12.6 %shard_map.330 = bf16[1024,768]{1,0:T(8,128)(2,1)S(1)} custom-call(s32[1,1024]{1,0:T(1,128)S(1)} %bitcast.121, bf16[1024,768]{1,0:T(8,128)(2,1)S(1)} %copy-done.31, bf16[1024,256]{1,0:T(8,128)(2,1)S(1)} %convolution_convert_fusion.11.grad_ref, bf16[1024,768]{1,0:T(8,128)(2,1)S(1)} %copy-done.31, bf16[1024,768]{1,0:T(8,128)(2,1)S(1)} %copy-done.31), custom_call_target="tpu_custom_call" | custom-call | flops 8589934592 | bytes 6291456 | tf_op jit(solution)/shard_map/pallas_call | solution.py:587
  790.2 3.9 convolution_convert_fusion.3
  800.0 12.7 %shard_map.333 = bf16[1024,768]{1,0:T(8,128)(2,1)S(1)} custom-call(s32[1,1024]{1,0:T(1,128)S(1)} %bitcast.122, bf16[1024,768]{1,0:T(8,128)(2,1)S(1)} %copy-done.25, bf16[1024,256]{1,0:T(8,128)(2,1)S(1)} %convolution_convert_fusion.8.grad_ref, bf16[1024,768]{1,0:T(8,128)(2,1)S(1)} %copy-done.25, bf16[1024,768]{1,0:T(8,128)(2,1)S(1)} %copy-done.25), custom_call_target="tpu_custom_call" | custom-call | flops 8589934592 | bytes 6291456 | tf_op jit(solution)/shard_map/pallas_call | solution.py:587
  813.0 12.5 %shard_map.331 = bf16[1024,768]{1,0:T(8,128)(2,1)S(1)} custom-call(s32[1,1024]{1,0:T(1,128)S(1)} %bitcast.123, bf16[1024,768]{1,0:T(8,128)(2,1)S(1)} %copy-done.27, bf16[1024,256]{1,0:T(8,128)(2,1)S(1)} %convolution_convert_fusion.10.grad_ref, bf16[1024,768]{1,0:T(8,128)(2,1)S(1)} %copy-done.27, bf16[1024,768]{1,0:T(8,128)(2,1)S(1)} %copy-done.27), custom_call_target="tpu_custom_call" | custom-call | flops 8589934592 | bytes 6291456 | tf_op jit(solution)/shard_map/pallas_call | solution.py:587
  843.3 10.6 collective-permute-done.82
  856.9 5.6 fusion.12
  862.6 16.4 %collective-permute-done.85 = bf16[256,2048]{0,1:T(8,128)(2,1)S(1)} collective-permute-done((bf16[256,2048]{0,1:T(8,128)(2,1)S(1)}, bf16[256,2048]{0,1:T(8,128)(2,1)S(1)}, u32[]{:S(2)}, u32[]{:S(2)}) %collective-permute-start.85) | collective-permute-done | bytes 1048608 | tf_op jit(solution)/shard_map/ppermute | solution.py:353
  880.6 4.2 collective-permute-start.89
  884.8 7.2 collective-permute-done.92
  895.9 5.7 fusion.16
  902.5 13.4 %collective-permute-done.93 = bf16[256,2048]{0,1:T(8,128)(2,1)S(1)} collective-permute-done((bf16[256,2048]{0,1:T(8,128)(2,1)S(1)}, bf16[256,2048]{0,1:T(8,128)(2,1)S(1)}, u32[]{:S(2)}, u32[]{:S(2)}) %collective-permute-start.93) | collective-permute-done | bytes 1048608 | tf_op jit(solution)/shard_map/ppermute | solution.py:349
  919.2 4.6 collective-permute-start.95
  932.3 15.6 %add_add_fusion = f32[1024,2048]{1,0:T(8,128)} fusion(f32[1024,2048]{1,0:T(8,128)} %fusion.20, f32[1024,2048]{1,0:T(8,128)} %fusion.12, f32[1024,2048]{1,0:T(8,128)} %fusion.16, bf16[1024,768]{1,0:T(8,128)(2,1)S(1)} %shard_map.333, bf16[1024,1024]{0,1:T(8,128)(2,1)S(1)} %copy-done.48, bf16[1024,1024]{0,1:T(8,128)(2,1)} %copy-done.60), kind=kOutput, calls=%fused_computation.25 | convolution fusion | flops 3233808384 | bytes 39321600 | tf_op jit(solution)/shard_map/dot_general | solution.py:474
  947.9 3.9 slice.1187
  958.0 4.2 collective-permute-start.101
  962.1 6.5 collective-permute-done.103
  976.5 8.4 collective-permute-done.101
  984.9 12.3 %collective-permute-done.106 = bf16[256,2048]{0,1:T(8,128)(2,1)} collective-permute-done((bf16[256,2048]{0,1:T(8,128)(2,1)}, bf16[256,2048]{0,1:T(8,128)(2,1)}, u32[]{:S(2)}, u32[]{:S(2)}) %collective-permute-start.106) | collective-permute-done | bytes 1048608 | tf_op jit(solution)/shard_map/ppermute | solution.py:353
  1006.4 18.3 %collective-permute-done.107 = bf16[256,2048]{0,1:T(8,128)(2,1)S(1)} collective-permute-done((bf16[256,2048]{0,1:T(8,128)(2,1)S(1)}, bf16[256,2048]{0,1:T(8,128)(2,1)S(1)}, u32[]{:S(2)}, u32[]{:S(2)}) %collective-permute-start.107) | collective-permute-done | bytes 1048608 | tf_op jit(solution)/shard_map/ppermute | solution.py:349
  1031.8 4.5 collective-permute-done.110
  1042.1 41.8 %collective-permute-done.77 = f32[20480]{0:T(1024)S(1)} collective-permute-done((f32[20480]{0:T(1024)S(1)}, f32[20480]{0:T(1024)S(1)}, u32[]{:S(2)}, u32[]{:S(2)}) %collective-permute-start.77) | collective-permute-done | bytes 81952 | tf_op jit(solution)/shard_map/ppermute | solution.py:349
  1088.5 4.4 collective-permute-done.79
  1180.4 3.9 maximum_convert_fusion
  1184.3 9.2 copy.135
  1195.7 3.9 convert_bitcast_fusion
  (847 shorter events, 439.4 us)
Async XLA Ops:
  9.4 71.0 %collective-permute-start.7 = (bf16[512,1024]{1,0:T(8,128)(2,1)}, bf16[512,1024]{1,0:T(8,128)(2,1)}, u32[]{:S(2)}, u32[]{:S(2)}) collective-permute-start(bf16[512,1024]{1,0:T(8,128)(2,1)} %get-tuple-element.380), channel_id=1, source_target_pairs={{0,16},{16,0},{8,24},{24,8},{1,17},{17,1},{9,25},{25,9},{2,18},{18... | collective-permute-start | bytes 3145736 | tf_op jit(solution)/shard_map/ppermute | solution.py:353
  12.3 68.6 %collective-permute-start.5 = (bf16[512,1024]{1,0:T(8,128)(2,1)}, bf16[512,1024]{1,0:T(8,128)(2,1)}, u32[]{:S(2)}, u32[]{:S(2)}) collective-permute-start(bf16[512,1024]{1,0:T(8,128)(2,1)} %get-tuple-element.380), channel_id=1, source_target_pairs={{0,8},{8,0},{16,24},{24,16},{1,9},{9,1},{17,25},{25,17},{2,10},{10... | collective-permute-start | bytes 3145736 | tf_op jit(solution)/shard_map/ppermute | solution.py:349
  14.8 66.9 %collective-permute-start.12 = (f32[1024]{0:T(1024)S(1)}, f32[1024]{0:T(1024)}, u32[]{:S(2)}, u32[]{:S(2)}) collective-permute-start(f32[1024]{0:T(1024)S(1)} %pad_maximum_fusion.29), channel_id=1, source_target_pairs={{0,1},{1,2},{2,3},{3,0},{4,5},{5,6},{6,7},{7,4},{8,9},{9,10},{10,1... | collective-permute-start | bytes 12296 | tf_op jit(solution)/shard_map/ppermute | solution.py:358
  34.7 44.0 %collective-permute-start.4 = (bf16[256,2048]{0,1:T(8,128)(2,1)}, bf16[256,2048]{0,1:T(8,128)(2,1)}, u32[]{:S(2)}, u32[]{:S(2)}) collective-permute-start(bf16[256,2048]{0,1:T(8,128)(2,1)} %constant_dynamic-update-slice_fusion.6), channel_id=1, source_target_pairs={{0,1},{1,2},{2,3},{3,0},{4,5},{5,6},{6,7},{7,4},{8,9},{9,10},{10,1... | collective-permute-start | bytes 3145736 | tf_op jit(solution)/shard_map/ppermute | solution.py:358
  36.3 78.6 %collective-permute-start = (bf16[1024,1024]{1,0:T(8,128)(2,1)S(1)}, bf16[1024,1024]{1,0:T(8,128)(2,1)}, u32[]{:S(2)}, u32[]{:S(2)}) collective-permute-start(bf16[1024,1024]{1,0:T(8,128)(2,1)S(1)} %copy-done.37), channel_id=1, source_target_pairs={{0,4},{4,0},{1,5},{5,1},{2,6},{6,2},{3,7},{7,3},{8,12},{12,8},{9,1... | collective-permute-start | bytes 6291464 | tf_op jit(solution)/shard_map/ppermute | solution.py:345
  78.7 35.0 %collective-permute-start.14 = (bf16[256,2048]{0,1:T(8,128)(2,1)}, bf16[256,2048]{0,1:T(8,128)(2,1)}, u32[]{:S(2)}, u32[]{:S(2)}) collective-permute-start(bf16[256,2048]{0,1:T(8,128)(2,1)} %collective-permute-done.4), channel_id=1, source_target_pairs={{0,1},{1,2},{2,3},{3,0},{4,5},{5,6},{6,7},{7,4},{8,9},{9,10},{10,1... | collective-permute-start | bytes 3145736 | tf_op jit(solution)/shard_map/ppermute | solution.py:358
  80.3 33.4 %collective-permute-start.8 = (bf16[256,2048]{0,1:T(8,128)(2,1)}, bf16[256,2048]{0,1:T(8,128)(2,1)S(1)}, u32[]{:S(2)}, u32[]{:S(2)}) collective-permute-start(bf16[256,2048]{0,1:T(8,128)(2,1)} %collective-permute-done.4), channel_id=1, source_target_pairs={{0,16},{16,0},{8,24},{24,8},{1,17},{17,1},{9,25},{25,9},{2,18},{18... | collective-permute-start | bytes 3145736 | tf_op jit(solution)/shard_map/ppermute | solution.py:353
  80.9 33.3 %collective-permute-start.6 = (bf16[256,2048]{0,1:T(8,128)(2,1)}, bf16[256,2048]{0,1:T(8,128)(2,1)S(1)}, u32[]{:S(2)}, u32[]{:S(2)}) collective-permute-start(bf16[256,2048]{0,1:T(8,128)(2,1)} %collective-permute-done.4), channel_id=1, source_target_pairs={{0,8},{8,0},{16,24},{24,16},{1,9},{9,1},{17,25},{25,17},{2,10},{10... | collective-permute-start | bytes 3145736 | tf_op jit(solution)/shard_map/ppermute | solution.py:349
  81.7 24.8 %collective-permute-start.20 = (f32[1024]{0:T(1024)}, f32[1024]{0:T(1024)S(1)}, u32[]{:S(2)}, u32[]{:S(2)}) collective-permute-start(f32[1024]{0:T(1024)} %collective-permute-done.12), channel_id=1, source_target_pairs={{0,1},{1,2},{2,3},{3,0},{4,5},{5,6},{6,7},{7,4},{8,9},{9,10},{10,1... | collective-permute-start | bytes 12296 | tf_op jit(solution)/shard_map/ppermute | solution.py:358
  113.7 119.6 %collective-permute-start.28 = (f32[1024]{0:T(1024)S(1)}, f32[1024]{0:T(1024)S(1)}, u32[]{:S(2)}, u32[]{:S(2)}) collective-permute-start(f32[1024]{0:T(1024)S(1)} %collective-permute-done.20), channel_id=1, source_target_pairs={{0,1},{1,2},{2,3},{3,0},{4,5},{5,6},{6,7},{7,4},{8,9},{9,10},{10,1... | collective-permute-start | bytes 12296 | tf_op jit(solution)/shard_map/ppermute | solution.py:358
  113.7 44.7 %collective-permute-start.22 = (bf16[256,2048]{0,1:T(8,128)(2,1)}, bf16[256,2048]{0,1:T(8,128)(2,1)}, u32[]{:S(2)}, u32[]{:S(2)}) collective-permute-start(bf16[256,2048]{0,1:T(8,128)(2,1)} %collective-permute-done.14), channel_id=1, source_target_pairs={{0,1},{1,2},{2,3},{3,0},{4,5},{5,6},{6,7},{7,4},{8,9},{9,10},{10,1... | collective-permute-start | bytes 3145736 | tf_op jit(solution)/shard_map/ppermute | solution.py:358
  132.4 39.9 %collective-permute-start.11 = (bf16[1024,1024]{0,1:T(8,128)(2,1)}, bf16[1024,1024]{0,1:T(8,128)(2,1)S(1)}, u32[]{:S(2)}, u32[]{:S(2)}) collective-permute-start(bf16[1024,1024]{0,1:T(8,128)(2,1)} %get-tuple-element.427), channel_id=1, source_target_pairs={{0,4},{4,0},{1,5},{5,1},{2,6},{6,2},{3,7},{7,3},{8,12},{12,8},{9,1... | collective-permute-start | bytes 6291464 | tf_op jit(solution)/shard_map/ppermute | solution.py:345
  158.4 86.9 %collective-permute-start.3 = (bf16[1024,256]{1,0:T(8,128)(2,1)S(1)}, bf16[1024,256]{1,0:T(8,128)(2,1)}, u32[]{:S(2)}, u32[]{:S(2)}) collective-permute-start(bf16[1024,256]{1,0:T(8,128)(2,1)S(1)} %shard_map.314), channel_id=1, source_target_pairs={{0,4},{4,0},{1,5},{5,1},{2,6},{6,2},{3,7},{7,3},{8,12},{12,8},{9,1... | collective-permute-start | bytes 1572872 | tf_op jit(solution)/shard_map/ppermute | solution.py:345
  173.6 42.7 %collective-permute-start.19 = (bf16[1024,1024]{0,1:T(8,128)(2,1)}, bf16[1024,1024]{0,1:T(8,128)(2,1)S(1)}, u32[]{:S(2)}, u32[]{:S(2)}) collective-permute-start(bf16[1024,1024]{0,1:T(8,128)(2,1)} %get-tuple-element.433), channel_id=1, source_target_pairs={{0,4},{4,0},{1,5},{5,1},{2,6},{6,2},{3,7},{7,3},{8,12},{12,8},{9,1... | collective-permute-start | bytes 6291464 | tf_op jit(solution)/shard_map/ppermute | solution.py:345
  200.1 54.9 %collective-permute-start.33 = (bf16[1024,1024]{1,0:T(8,128)(2,1)S(1)}, bf16[1024,1024]{1,0:T(8,128)(2,1)S(1)}, u32[]{:S(2)}, u32[]{:S(2)}) collective-permute-start(bf16[1024,1024]{1,0:T(8,128)(2,1)S(1)} %pad_maximum_fusion.8.refs_4_.refs_0_), channel_id=1, source_target_pairs={{0,1},{1,2},{2,3},{3,0},{4,5},{5,6},{6,7},{7,4},{8,9},{9,10},{10,1... | collective-permute-start | bytes 6291464 | tf_op jit(solution)/shard_map/ppermute | solution.py:358
  203.6 27.9 %collective-permute-start.27 = (bf16[1024,1024]{0,1:T(8,128)(2,1)}, bf16[1024,1024]{0,1:T(8,128)(2,1)S(1)}, u32[]{:S(2)}, u32[]{:S(2)}) collective-permute-start(bf16[1024,1024]{0,1:T(8,128)(2,1)} %get-tuple-element.421), channel_id=1, source_target_pairs={{0,4},{4,0},{1,5},{5,1},{2,6},{6,2},{3,7},{7,3},{8,12},{12,8},{9,1... | collective-permute-start | bytes 6291464 | tf_op jit(solution)/shard_map/ppermute | solution.py:345
  216.3 29.1 %collective-permute-start.13 = (bf16[1024,256]{1,0:T(8,128)(2,1)S(1)}, bf16[1024,256]{1,0:T(8,128)(2,1)}, u32[]{:S(2)}, u32[]{:S(2)}) collective-permute-start(bf16[1024,256]{1,0:T(8,128)(2,1)S(1)} %shard_map.315), channel_id=1, source_target_pairs={{0,4},{4,0},{1,5},{5,1},{2,6},{6,2},{3,7},{7,3},{8,12},{12,8},{9,1... | collective-permute-start | bytes 1572872 | tf_op jit(solution)/shard_map/ppermute | solution.py:345
  231.5 29.0 %collective-permute-start.40 = (bf16[256,1024]{1,0:T(8,128)(2,1)}, bf16[256,1024]{1,0:T(8,128)(2,1)}, u32[]{:S(2)}, u32[]{:S(2)}) collective-permute-start(bf16[256,1024]{1,0:T(8,128)(2,1)} %slice.830), channel_id=1, source_target_pairs={{0,16},{16,0},{8,24},{24,8},{1,17},{17,1},{9,25},{25,9},{2,18},{18... | collective-permute-start | bytes 1572872 | tf_op jit(solution)/shard_map/ppermute | solution.py:353
  233.3 27.3 %collective-permute-start.42 = (bf16[256,1024]{1,0:T(8,128)(2,1)}, bf16[256,1024]{1,0:T(8,128)(2,1)}, u32[]{:S(2)}, u32[]{:S(2)}) collective-permute-start(bf16[256,1024]{1,0:T(8,128)(2,1)} %slice.832), channel_id=1, source_target_pairs={{0,8},{8,0},{16,24},{24,16},{1,9},{9,1},{17,25},{25,17},{2,10},{10... | collective-permute-start | bytes 1572872 | tf_op jit(solution)/shard_map/ppermute | solution.py:349
  255.0 49.7 %collective-permute-start.34 = (bf16[1024,1024]{1,0:T(8,128)(2,1)S(1)}, bf16[1024,1024]{1,0:T(8,128)(2,1)S(1)}, u32[]{:S(2)}, u32[]{:S(2)}) collective-permute-start(bf16[1024,1024]{1,0:T(8,128)(2,1)S(1)} %collective-permute-done.33.refs_5_.refs_1_), channel_id=1, source_target_pairs={{0,1},{1,2},{2,3},{3,0},{4,5},{5,6},{6,7},{7,4},{8,9},{9,10},{10,1... | collective-permute-start | bytes 6291464 | tf_op jit(solution)/shard_map/ppermute | solution.py:358
  260.6 24.9 %collective-permute-start.43 = (bf16[512,1024]{1,0:T(8,128)(2,1)S(1)}, bf16[512,1024]{1,0:T(8,128)(2,1)S(1)}, u32[]{:S(2)}, u32[]{:S(2)}) collective-permute-start(bf16[512,1024]{1,0:T(8,128)(2,1)S(1)} %copy-done.106), channel_id=1, source_target_pairs={{0,8},{8,0},{16,24},{24,16},{1,9},{9,1},{17,25},{25,17},{2,10},{10... | collective-permute-start | bytes 3145736 | tf_op jit(solution)/shard_map/ppermute | solution.py:349
  268.0 38.0 %collective-permute-start.30 = (f32[2,1024]{1,0:T(2,128)S(1)}, f32[2,1024]{1,0:T(2,128)S(1)}, u32[]{:S(2)}, u32[]{:S(2)}) collective-permute-start(f32[2,1024]{1,0:T(2,128)S(1)} %maximum_bitcast_fusion.1), channel_id=1, source_target_pairs={{0,4},{4,0},{1,5},{5,1},{2,6},{6,2},{3,7},{7,3},{8,12},{12,8},{9,1... | collective-permute-start | bytes 24584 | tf_op jit(solution)/shard_map/ppermute | solution.py:345
  270.5 84.3 %collective-permute-start.32 = (bf16[1024,1024]{1,0:T(8,128)(2,1)S(1)}, bf16[1024,1024]{1,0:T(8,128)(2,1)S(1)}, u32[]{:S(2)}, u32[]{:S(2)}) collective-permute-start(bf16[1024,1024]{1,0:T(8,128)(2,1)S(1)} %copy-done.50), channel_id=1, source_target_pairs={{0,4},{4,0},{1,5},{5,1},{2,6},{6,2},{3,7},{7,3},{8,12},{12,8},{9,1... | collective-permute-start | bytes 6291464 | tf_op jit(solution)/shard_map/ppermute | solution.py:345
  304.7 48.9 %collective-permute-start.35 = (bf16[1024,1024]{1,0:T(8,128)(2,1)S(1)}, bf16[1024,1024]{1,0:T(8,128)(2,1)S(1)}, u32[]{:S(2)}, u32[]{:S(2)}) collective-permute-start(bf16[1024,1024]{1,0:T(8,128)(2,1)S(1)} %collective-permute-done.34.refs_6_.refs_2_), channel_id=1, source_target_pairs={{0,1},{1,2},{2,3},{3,0},{4,5},{5,6},{6,7},{7,4},{8,9},{9,10},{10,1... | collective-permute-start | bytes 6291464 | tf_op jit(solution)/shard_map/ppermute | solution.py:358
  306.9 48.0 %collective-permute-start.45 = (bf16[1024,1024]{1,0:T(8,128)(2,1)S(1)}, bf16[1024,1024]{1,0:T(8,128)(2,1)S(1)}, u32[]{:S(2)}, u32[]{:S(2)}) collective-permute-start(bf16[1024,1024]{1,0:T(8,128)(2,1)S(1)} %add_convert_fusion.refs_0_), channel_id=1, source_target_pairs={{0,8},{8,0},{16,24},{24,16},{1,9},{9,1},{17,25},{25,17},{2,10},{10... | collective-permute-start | bytes 6291464 | tf_op jit(solution)/shard_map/ppermute | solution.py:349
  307.6 47.8 %collective-permute-start.47 = (bf16[1024,1024]{1,0:T(8,128)(2,1)S(1)}, bf16[1024,1024]{1,0:T(8,128)(2,1)S(1)}, u32[]{:S(2)}, u32[]{:S(2)}) collective-permute-start(bf16[1024,1024]{1,0:T(8,128)(2,1)S(1)} %add_convert_fusion.refs_0_), channel_id=1, source_target_pairs={{0,16},{16,0},{8,24},{24,8},{1,17},{17,1},{9,25},{25,9},{2,18},{18... | collective-permute-start | bytes 6291464 | tf_op jit(solution)/shard_map/ppermute | solution.py:353
  311.3 44.4 %collective-permute-start.37 = (bf16[1024,512]{1,0:T(8,128)(2,1)S(1)}, bf16[1024,512]{1,0:T(8,128)(2,1)S(1)}, u32[]{:S(2)}, u32[]{:S(2)}) collective-permute-start(bf16[1024,512]{1,0:T(8,128)(2,1)S(1)} %slice.826), channel_id=1, source_target_pairs={{0,4},{4,0},{1,5},{5,1},{2,6},{6,2},{3,7},{7,3},{8,12},{12,8},{9,1... | collective-permute-start | bytes 3145736 | tf_op jit(solution)/shard_map/ppermute | solution.py:345
  354.9 27.2 %collective-permute-start.31 = (bf16[1024,1024]{1,0:T(8,128)(2,1)S(1)}, bf16[1024,1024]{1,0:T(8,128)(2,1)S(1)}, u32[]{:S(2)}, u32[]{:S(2)}) collective-permute-start(bf16[1024,1024]{1,0:T(8,128)(2,1)S(1)} %add_convert_fusion.refs_0_), channel_id=1, source_target_pairs={{0,4},{4,0},{1,5},{5,1},{2,6},{6,2},{3,7},{7,3},{8,12},{12,8},{9,1... | collective-permute-start | bytes 6291464 | tf_op jit(solution)/shard_map/ppermute | solution.py:345
  355.4 26.9 %collective-permute-start.52 = (bf16[1024,1024]{1,0:T(8,128)(2,1)S(1)}, bf16[1024,1024]{1,0:T(8,128)(2,1)S(1)}, u32[]{:S(2)}, u32[]{:S(2)}) collective-permute-start(bf16[1024,1024]{1,0:T(8,128)(2,1)S(1)} %collective-permute-done.45.refs_0_.refs_1_), channel_id=1, source_target_pairs={{0,4},{4,0},{1,5},{5,1},{2,6},{6,2},{3,7},{7,3},{8,12},{12,8},{9,1... | collective-permute-start | bytes 6291464 | tf_op jit(solution)/shard_map/ppermute | solution.py:345
  355.7 25.6 %collective-permute-start.49 = (bf16[512,1024]{1,0:T(8,128)(2,1)S(1)}, bf16[512,1024]{1,0:T(8,128)(2,1)S(1)}, u32[]{:S(2)}, u32[]{:S(2)}) collective-permute-start(bf16[512,1024]{1,0:T(8,128)(2,1)S(1)} %slice.835), channel_id=1, source_target_pairs={{0,8},{8,0},{16,24},{24,16},{1,9},{9,1},{17,25},{25,17},{2,10},{10... | collective-permute-start | bytes 3145736 | tf_op jit(solution)/shard_map/ppermute | solution.py:349
  356.3 25.2 %collective-permute-start.48 = (bf16[512,1024]{1,0:T(8,128)(2,1)S(1)}, bf16[512,1024]{1,0:T(8,128)(2,1)S(1)}, u32[]{:S(2)}, u32[]{:S(2)}) collective-permute-start(bf16[512,1024]{1,0:T(8,128)(2,1)S(1)} %slice.833), channel_id=1, source_target_pairs={{0,16},{16,0},{8,24},{24,8},{1,17},{17,1},{9,25},{25,9},{2,18},{18... | collective-permute-start | bytes 3145736 | tf_op jit(solution)/shard_map/ppermute | solution.py:353
  358.8 41.2 %collective-permute-start.53 = (bf16[1024,1024]{1,0:T(8,128)(2,1)S(1)}, bf16[1024,1024]{1,0:T(8,128)(2,1)}, u32[]{:S(2)}, u32[]{:S(2)}) collective-permute-start(bf16[1024,1024]{1,0:T(8,128)(2,1)S(1)} %constant_dynamic-update-slice_fusion.19.refs_2_.refs_5_), channel_id=1, source_target_pairs={{0,4},{4,0},{1,5},{5,1},{2,6},{6,2},{3,7},{7,3},{8,12},{12,8},{9,1... | collective-permute-start | bytes 6291464 | tf_op jit(solution)/shard_map/ppermute | solution.py:345
  381.3 34.5 %collective-permute-start.54 = (bf16[1024,1024]{1,0:T(8,128)(2,1)S(1)}, bf16[1024,1024]{1,0:T(8,128)(2,1)}, u32[]{:S(2)}, u32[]{:S(2)}) collective-permute-start(bf16[1024,1024]{1,0:T(8,128)(2,1)S(1)} %constant_dynamic-update-slice_fusion.21.refs_2_.refs_6_), channel_id=1, source_target_pairs={{0,4},{4,0},{1,5},{5,1},{2,6},{6,2},{3,7},{7,3},{8,12},{12,8},{9,1... | collective-permute-start | bytes 6291464 | tf_op jit(solution)/shard_map/ppermute | solution.py:345
  381.5 34.2 %collective-permute-start.51 = (bf16[1024,1024]{1,0:T(8,128)(2,1)S(1)}, bf16[1024,1024]{1,0:T(8,128)(2,1)}, u32[]{:S(2)}, u32[]{:S(2)}) collective-permute-start(bf16[1024,1024]{1,0:T(8,128)(2,1)S(1)} %collective-permute-done.47.refs_0_.refs_2_), channel_id=1, source_target_pairs={{0,4},{4,0},{1,5},{5,1},{2,6},{6,2},{3,7},{7,3},{8,12},{12,8},{9,1... | collective-permute-start | bytes 6291464 | tf_op jit(solution)/shard_map/ppermute | solution.py:345
  382.1 49.4 %collective-permute-start.55 = (bf16[1024,1024]{1,0:T(8,128)(2,1)S(1)}, bf16[1024,1024]{1,0:T(8,128)(2,1)}, u32[]{:S(2)}, u32[]{:S(2)}) collective-permute-start(bf16[1024,1024]{1,0:T(8,128)(2,1)S(1)} %constant_dynamic-update-slice_fusion.23.refs_2_.refs_7_), channel_id=1, source_target_pairs={{0,4},{4,0},{1,5},{5,1},{2,6},{6,2},{3,7},{7,3},{8,12},{12,8},{9,1... | collective-permute-start | bytes 6291464 | tf_op jit(solution)/shard_map/ppermute | solution.py:345
  382.3 49.1 %collective-permute-start.50 = (bf16[1024,1024]{1,0:T(8,128)(2,1)S(1)}, bf16[1024,1024]{1,0:T(8,128)(2,1)}, u32[]{:S(2)}, u32[]{:S(2)}) collective-permute-start(bf16[1024,1024]{1,0:T(8,128)(2,1)S(1)} %constant_dynamic-update-slice_fusion.17.refs_0_.refs_3_), channel_id=1, source_target_pairs={{0,4},{4,0},{1,5},{5,1},{2,6},{6,2},{3,7},{7,3},{8,12},{12,8},{9,1... | collective-permute-start | bytes 6291464 | tf_op jit(solution)/shard_map/ppermute | solution.py:345
  415.5 32.1 %collective-permute-start.56 = (bf16[1024,2048]{1,0:T(8,128)(2,1)}, bf16[1024,2048]{1,0:T(8,128)(2,1)}, u32[]{:S(2)}, u32[]{:S(2)}) collective-permute-start(bf16[1024,2048]{1,0:T(8,128)(2,1)} %get-tuple-element.158.own_ref.refs_9_.refs_13_), channel_id=1, source_target_pairs={{0,4},{4,0},{1,5},{5,1},{2,6},{6,2},{3,7},{7,3},{8,12},{12,8},{9,1... | collective-permute-start | bytes 12582920 | tf_op jit(solution)/shard_map/ppermute | solution.py:345
  431.2 25.0 %collective-permute-start.57 = (bf16[1024,2048]{1,0:T(8,128)(2,1)}, bf16[1024,2048]{1,0:T(8,128)(2,1)}, u32[]{:S(2)}, u32[]{:S(2)}) collective-permute-start(bf16[1024,2048]{1,0:T(8,128)(2,1)} %get-tuple-element.159.own_ref.refs_10_.refs_14_), channel_id=1, source_target_pairs={{0,4},{4,0},{1,5},{5,1},{2,6},{6,2},{3,7},{7,3},{8,12},{12,8},{9,1... | collective-permute-start | bytes 12582920 | tf_op jit(solution)/shard_map/ppermute | solution.py:345
  447.2 31.9 %collective-permute-start.59 = (bf16[1024,2048]{1,0:T(8,128)(2,1)}, bf16[1024,2048]{1,0:T(8,128)(2,1)}, u32[]{:S(2)}, u32[]{:S(2)}) collective-permute-start(bf16[1024,2048]{1,0:T(8,128)(2,1)} %get-tuple-element.186.own_ref.refs_8_.refs_12_), channel_id=1, source_target_pairs={{0,4},{4,0},{1,5},{5,1},{2,6},{6,2},{3,7},{7,3},{8,12},{12,8},{9,1... | collective-permute-start | bytes 12582920 | tf_op jit(solution)/shard_map/ppermute | solution.py:345
  466.3 58.6 %collective-permute-start.62 = (bf16[512,1024]{1,0:T(8,128)(2,1)S(1)}, bf16[512,1024]{1,0:T(8,128)(2,1)S(1)}, u32[]{:S(2)}, u32[]{:S(2)}) collective-permute-start(bf16[512,1024]{1,0:T(8,128)(2,1)S(1)} %slice.842), channel_id=1, source_target_pairs={{0,8},{8,0},{16,24},{24,16},{1,9},{9,1},{17,25},{25,17},{2,10},{10... | collective-permute-start | bytes 3145736 | tf_op jit(solution)/shard_map/ppermute | solution.py:349
  467.6 57.2 %collective-permute-start.60 = (bf16[512,1024]{1,0:T(8,128)(2,1)}, bf16[512,1024]{1,0:T(8,128)(2,1)S(1)}, u32[]{:S(2)}, u32[]{:S(2)}) collective-permute-start(bf16[512,1024]{1,0:T(8,128)(2,1)} %slice.840), channel_id=1, source_target_pairs={{0,16},{16,0},{8,24},{24,8},{1,17},{17,1},{9,25},{25,9},{2,18},{18... | collective-permute-start | bytes 3145736 | tf_op jit(solution)/shard_map/ppermute | solution.py:353
  524.9 58.0 %collective-permute-start.63 = (bf16[512,1024]{1,0:T(8,128)(2,1)}, bf16[512,1024]{1,0:T(8,128)(2,1)}, u32[]{:S(2)}, u32[]{:S(2)}) collective-permute-start(bf16[512,1024]{1,0:T(8,128)(2,1)} %get-tuple-element.165), channel_id=1, source_target_pairs={{0,8},{8,0},{16,24},{24,16},{1,9},{9,1},{17,25},{25,17},{2,10},{10... | collective-permute-start | bytes 3145736 | tf_op jit(solution)/shard_map/ppermute | solution.py:349
  525.9 55.3 %collective-permute-start.61 = (bf16[512,1024]{1,0:T(8,128)(2,1)}, bf16[512,1024]{1,0:T(8,128)(2,1)}, u32[]{:S(2)}, u32[]{:S(2)}) collective-permute-start(bf16[512,1024]{1,0:T(8,128)(2,1)} %get-tuple-element.163), channel_id=1, source_target_pairs={{0,16},{16,0},{8,24},{24,8},{1,17},{17,1},{9,25},{25,9},{2,18},{18... | collective-permute-start | bytes 3145736 | tf_op jit(solution)/shard_map/ppermute | solution.py:353
  584.7 26.2 %collective-permute-start.67 = (bf16[512,1024]{1,0:T(8,128)(2,1)S(1)}, bf16[512,1024]{1,0:T(8,128)(2,1)S(1)}, u32[]{:S(2)}, u32[]{:S(2)}) collective-permute-start(bf16[512,1024]{1,0:T(8,128)(2,1)S(1)} %add_convert_fusion.15), channel_id=1, source_target_pairs={{0,16},{16,0},{8,24},{24,8},{1,17},{17,1},{9,25},{25,9},{2,18},{18... | collective-permute-start | bytes 3145736 | tf_op jit(solution)/shard_map/ppermute | solution.py:353
  588.7 47.3 %collective-permute-start.86 = (bf16[1024,1024]{1,0:T(8,128)(2,1)S(1)}, bf16[1024,1024]{1,0:T(8,128)(2,1)S(1)}, u32[]{:S(2)}, u32[]{:S(2)}) collective-permute-start(bf16[1024,1024]{1,0:T(8,128)(2,1)S(1)} %slice_bitcast_fusion.3), channel_id=1, source_target_pairs={{0,3},{1,0},{2,1},{3,2},{4,7},{5,4},{6,5},{7,6},{8,11},{9,8},{10,9... | collective-permute-start | bytes 6291464 | tf_op jit(solution)/shard_map/ppermute | solution.py:363
  637.0 45.9 %collective-permute-start.87 = (bf16[1024,1024]{1,0:T(8,128)(2,1)S(1)}, bf16[1024,1024]{1,0:T(8,128)(2,1)S(1)}, u32[]{:S(2)}, u32[]{:S(2)}) collective-permute-start(bf16[1024,1024]{1,0:T(8,128)(2,1)S(1)} %fusion.10), channel_id=1, source_target_pairs={{0,3},{1,0},{2,1},{3,2},{4,7},{5,4},{6,5},{7,6},{8,11},{9,8},{10,9... | collective-permute-start | bytes 6291464 | tf_op jit(solution)/shard_map/ppermute | solution.py:363
  659.4 30.6 %collective-permute-start.71 = (bf16[512,1024]{1,0:T(8,128)(2,1)S(1)}, bf16[512,1024]{1,0:T(8,128)(2,1)S(1)}, u32[]{:S(2)}, u32[]{:S(2)}) collective-permute-start(bf16[512,1024]{1,0:T(8,128)(2,1)S(1)} %add_convert_fusion.14), channel_id=1, source_target_pairs={{0,8},{8,0},{16,24},{24,16},{1,9},{9,1},{17,25},{25,17},{2,10},{10... | collective-permute-start | bytes 3145736 | tf_op jit(solution)/shard_map/ppermute | solution.py:349
  660.5 29.4 %collective-permute-start.70 = (bf16[512,1024]{1,0:T(8,128)(2,1)S(1)}, bf16[512,1024]{1,0:T(8,128)(2,1)S(1)}, u32[]{:S(2)}, u32[]{:S(2)}) collective-permute-start(bf16[512,1024]{1,0:T(8,128)(2,1)S(1)} %add_convert_fusion.16), channel_id=1, source_target_pairs={{0,16},{16,0},{8,24},{24,8},{1,17},{17,1},{9,25},{25,9},{2,18},{18... | collective-permute-start | bytes 3145736 | tf_op jit(solution)/shard_map/ppermute | solution.py:353
  685.2 47.2 %collective-permute-start.88 = (bf16[1024,1024]{1,0:T(8,128)(2,1)}, bf16[1024,1024]{1,0:T(8,128)(2,1)S(1)}, u32[]{:S(2)}, u32[]{:S(2)}) collective-permute-start(bf16[1024,1024]{1,0:T(8,128)(2,1)} %fusion.9), channel_id=1, source_target_pairs={{0,3},{1,0},{2,1},{3,2},{4,7},{5,4},{6,5},{7,6},{8,11},{9,8},{10,9... | collective-permute-start | bytes 6291464 | tf_op jit(solution)/shard_map/ppermute | solution.py:363
  701.5 34.9 %collective-permute-start.73 = (bf16[1024,1024]{1,0:T(8,128)(2,1)}, bf16[1024,1024]{1,0:T(8,128)(2,1)}, u32[]{:S(2)}, u32[]{:S(2)}) collective-permute-start(bf16[1024,1024]{1,0:T(8,128)(2,1)} %pad_maximum_fusion.9), channel_id=1, source_target_pairs={{0,4},{4,0},{1,5},{5,1},{2,6},{6,2},{3,7},{7,3},{8,12},{12,8},{9,1... | collective-permute-start | bytes 6291464 | tf_op jit(solution)/shard_map/ppermute | solution.py:345
  826.7 146.3 %collective-permute-start.76 = (f32[4,3584]{1,0:T(4,128)S(1)}, f32[4,3584]{1,0:T(4,128)S(1)}, u32[]{:S(2)}, u32[]{:S(2)}) collective-permute-start(f32[4,3584]{1,0:T(4,128)S(1)} %pad_maximum_fusion.23), channel_id=1, source_target_pairs={{0,4},{4,0},{1,5},{5,1},{2,6},{6,2},{3,7},{7,3},{8,12},{12,8},{9,1... | collective-permute-start | bytes 172040 | tf_op jit(solution)/shard_map/ppermute | solution.py:345
  828.6 73.0 %collective-permute-start.96 = (bf16[1024,1024]{0,1:T(8,128)(2,1)S(1)}, bf16[1024,1024]{0,1:T(8,128)(2,1)S(1)}, u32[]{:S(2)}, u32[]{:S(2)}) collective-permute-start(bf16[1024,1024]{0,1:T(8,128)(2,1)S(1)} %fusion.25), channel_id=1, source_target_pairs={{0,4},{4,0},{1,5},{5,1},{2,6},{6,2},{3,7},{7,3},{8,12},{12,8},{9,1... | collective-permute-start | bytes 6291464 | tf_op jit(solution)/shard_map/ppermute | solution.py:345
  854.2 24.8 %collective-permute-start.85 = (bf16[256,2048]{0,1:T(8,128)(2,1)S(1)}, bf16[256,2048]{0,1:T(8,128)(2,1)S(1)}, u32[]{:S(2)}, u32[]{:S(2)}) collective-permute-start(bf16[256,2048]{0,1:T(8,128)(2,1)S(1)} %pad_maximum_fusion.15), channel_id=1, source_target_pairs={{0,16},{16,0},{8,24},{24,8},{1,17},{17,1},{9,25},{25,9},{2,18},{18... | collective-permute-start | bytes 3145736 | tf_op jit(solution)/shard_map/ppermute | solution.py:353
  854.9 24.8 %collective-permute-start.84 = (bf16[256,2048]{0,1:T(8,128)(2,1)S(1)}, bf16[256,2048]{0,1:T(8,128)(2,1)S(1)}, u32[]{:S(2)}, u32[]{:S(2)}) collective-permute-start(bf16[256,2048]{0,1:T(8,128)(2,1)S(1)} %pad_maximum_fusion.14), channel_id=1, source_target_pairs={{0,8},{8,0},{16,24},{24,16},{1,9},{9,1},{17,25},{25,17},{2,10},{10... | collective-permute-start | bytes 3145736 | tf_op jit(solution)/shard_map/ppermute | solution.py:349
  880.6 37.2 %collective-permute-start.89 = (bf16[256,2048]{0,1:T(8,128)(2,1)S(1)}, bf16[256,2048]{0,1:T(8,128)(2,1)S(1)}, u32[]{:S(2)}, u32[]{:S(2)}) collective-permute-start(bf16[256,2048]{0,1:T(8,128)(2,1)S(1)} %add_convert_fusion.13), channel_id=1, source_target_pairs={{0,3},{1,0},{2,1},{3,2},{4,7},{5,4},{6,5},{7,6},{8,11},{9,8},{10,9... | collective-permute-start | bytes 3145736 | tf_op jit(solution)/shard_map/ppermute | solution.py:363
  901.6 50.3 %collective-permute-start.102 = (bf16[1024,1024]{0,1:T(8,128)(2,1)}, bf16[1024,1024]{0,1:T(8,128)(2,1)}, u32[]{:S(2)}, u32[]{:S(2)}) collective-permute-start(bf16[1024,1024]{0,1:T(8,128)(2,1)} %fusion.24), channel_id=1, source_target_pairs={{0,4},{4,0},{1,5},{5,1},{2,6},{6,2},{3,7},{7,3},{8,12},{12,8},{9,1... | collective-permute-start | bytes 6291464 | tf_op jit(solution)/shard_map/ppermute | solution.py:345
  919.2 36.0 %collective-permute-start.95 = (bf16[256,2048]{0,1:T(8,128)(2,1)}, bf16[256,2048]{0,1:T(8,128)(2,1)}, u32[]{:S(2)}, u32[]{:S(2)}) collective-permute-start(bf16[256,2048]{0,1:T(8,128)(2,1)} %add_convert_fusion.11), channel_id=1, source_target_pairs={{0,3},{1,0},{2,1},{3,2},{4,7},{5,4},{6,5},{7,6},{8,11},{9,8},{10,9... | collective-permute-start | bytes 3145736 | tf_op jit(solution)/shard_map/ppermute | solution.py:363
  929.1 25.2 %collective-permute-start.100 = (bf16[256,2048]{0,1:T(8,128)(2,1)}, bf16[256,2048]{0,1:T(8,128)(2,1)S(1)}, u32[]{:S(2)}, u32[]{:S(2)}) collective-permute-start(bf16[256,2048]{0,1:T(8,128)(2,1)} %pad_maximum_fusion.19), channel_id=1, source_target_pairs={{0,16},{16,0},{8,24},{24,8},{1,17},{17,1},{9,25},{25,9},{2,18},{18... | collective-permute-start | bytes 3145736 | tf_op jit(solution)/shard_map/ppermute | solution.py:353
  958.0 26.9 %collective-permute-start.101 = (bf16[256,2048]{0,1:T(8,128)(2,1)}, bf16[256,2048]{0,1:T(8,128)(2,1)}, u32[]{:S(2)}, u32[]{:S(2)}) collective-permute-start(bf16[256,2048]{0,1:T(8,128)(2,1)} %add_convert_fusion.9), channel_id=1, source_target_pairs={{0,3},{1,0},{2,1},{3,2},{4,7},{5,4},{6,5},{7,6},{8,11},{9,8},{10,9... | collective-permute-start | bytes 3145736 | tf_op jit(solution)/shard_map/ppermute | solution.py:363
  972.0 25.1 %collective-permute-start.106 = (bf16[256,2048]{0,1:T(8,128)(2,1)}, bf16[256,2048]{0,1:T(8,128)(2,1)}, u32[]{:S(2)}, u32[]{:S(2)}) collective-permute-start(bf16[256,2048]{0,1:T(8,128)(2,1)} %pad_maximum_fusion.21), channel_id=1, source_target_pairs={{0,16},{16,0},{8,24},{24,8},{1,17},{17,1},{9,25},{25,9},{2,18},{18... | collective-permute-start | bytes 3145736 | tf_op jit(solution)/shard_map/ppermute | solution.py:353
  972.6 24.8 %collective-permute-start.105 = (bf16[256,2048]{0,1:T(8,128)(2,1)}, bf16[256,2048]{0,1:T(8,128)(2,1)}, u32[]{:S(2)}, u32[]{:S(2)}) collective-permute-start(bf16[256,2048]{0,1:T(8,128)(2,1)} %pad_maximum_fusion.20), channel_id=1, source_target_pairs={{0,8},{8,0},{16,24},{24,16},{1,9},{9,1},{17,25},{25,17},{2,10},{10... | collective-permute-start | bytes 3145736 | tf_op jit(solution)/shard_map/ppermute | solution.py:349
  1038.5 69.3 %collective-permute-start.112 = (bf16[1024,1024]{1,0:T(8,128)(2,1)S(1)}, bf16[1024,1024]{1,0:T(8,128)(2,1)}, u32[]{:S(2)}, u32[]{:S(2)}) collective-permute-start(bf16[1024,1024]{1,0:T(8,128)(2,1)S(1)} %copy-done.63), channel_id=1, source_target_pairs={{0,16},{16,0},{8,24},{24,8},{1,17},{17,1},{9,25},{25,9},{2,18},{18... | collective-permute-start | bytes 6291464 | tf_op jit(solution)/shard_map/ppermute | solution.py:353
  1040.0 70.2 %collective-permute-start.111 = (bf16[1024,1024]{1,0:T(8,128)(2,1)S(1)}, bf16[1024,1024]{1,0:T(8,128)(2,1)}, u32[]{:S(2)}, u32[]{:S(2)}) collective-permute-start(bf16[1024,1024]{1,0:T(8,128)(2,1)S(1)} %copy-done.63), channel_id=1, source_target_pairs={{0,8},{8,0},{16,24},{24,16},{1,9},{9,1},{17,25},{25,17},{2,10},{10... | collective-permute-start | bytes 6291464 | tf_op jit(solution)/shard_map/ppermute | solution.py:349
  1040.4 43.6 %collective-permute-start.77 = (f32[20480]{0:T(1024)S(1)}, f32[20480]{0:T(1024)S(1)}, u32[]{:S(2)}, u32[]{:S(2)}) collective-permute-start(f32[20480]{0:T(1024)S(1)} %constant_dynamic-update-slice_fusion.38), channel_id=1, source_target_pairs={{0,8},{8,0},{16,24},{24,16},{1,9},{9,1},{17,25},{25,17},{2,10},{10... | collective-permute-start | bytes 245768 | tf_op jit(solution)/shard_map/ppermute | solution.py:349
  (213 other events, 2885.7 us)

commit v4 on v3

--- a/solution.py
+++ b/solution.py
@@ -366,18 +366,36 @@
 class Link:
     def __init__(self):
         self.last = None
+        self.sent = None
 
     def send(self, step, values):
         if self.last is not None:
             values = after(values, self.last)
+        self.sent = values
         self.last = step(values)
         return self.last
+
+
+class Order:
+    def __init__(self):
+        self.token = None
+
+    def run(self, function, first, *others, past=()):
+        earlier = [t for t in (self.token, *past) if t is not None]
+        if earlier:
+            first = after(first, *earlier)
+        result = function(first, *others)
+        self.token = jax.tree.leaves(result)[0]
+        return result
 
 
 class Plane:
     def __init__(self):
         self.x = Link()
         self.y = Link()
+
+    def sent(self):
+        return (self.x.sent, self.y.sent)
 
     def near(self, values):
         return self.x.send(step_x, values), self.y.send(step_y, values)
@@ -392,31 +410,11 @@
         from_x, from_y = self.near(values)
         return [values, from_x, from_y, *self.far(from_x, from_y)]
 
-    def sum_early(self, here, to_x, to_y, to_far):
-        half = here.shape[0] // 2
-        f32 = jnp.float32
-        x_top = self.x.send(step_x, to_x[:half])
-        y_bottom = self.y.send(step_y, to_y[half:])
-        via_x = self.x.send(step_x, to_far[:half])
-        via_y = self.y.send(step_y, to_far[half:])
-        x_bottom = self.x.send(step_x, add_rounded(to_x[half:], via_y))
-        y_top = self.y.send(step_y, add_rounded(to_y[:half], via_x))
-        top = here[:half].astype(f32) + x_top.astype(f32) + y_top.astype(f32)
-        bottom = here[half:].astype(f32) + x_bottom.astype(f32) + y_bottom.astype(f32)
-        return jnp.concatenate([top, bottom], axis=0)
-
-    def sum_pairs(self, parts):
-        f32 = jnp.float32
-        here, to_x, to_y, to_far = parts
-        via_x = self.x.send(step_x, to_far[0])
-        via_y = self.y.send(step_y, to_far[1])
-        for_x = jnp.concatenate([to_x[0], add_rounded(to_x[1], via_y)], axis=1)
-        for_y = jnp.concatenate([add_rounded(to_y[0], via_x), to_y[1]], axis=1)
-        from_x = self.x.send(step_x, for_x)
-        from_y = self.y.send(step_y, for_y)
-        return (
-            jnp.concatenate(here, axis=1).astype(f32) + from_x.astype(f32) + from_y.astype(f32)
-        ).astype(jnp.bfloat16)
+    def add_x(self, part, arrived):
+        return self.x.send(step_x, add_rounded(part, arrived))
+
+    def add_y(self, part, arrived):
+        return self.y.send(step_y, add_rounded(part, arrived))
 
 
 def add_rounded(left, right):
@@ -428,24 +426,6 @@
     for _ in range(lax.axis_size("col") - 1):
         held.append(link.send(step_up, held[-1]))
     return held
-
-
-def ring_sum(link, blocks):
-    total = blocks[-1]
-    for block in blocks[-2::-1]:
-        total = add_rounded(link.send(step_down, total), block)
-    return total
-
-
-def butterfly_sum(values):
-    count = lax.axis_size("col")
-    values = values + step_x(values)
-    values = values + step_y(values)
-    step = 1
-    while step < count:
-        values = values + lax.ppermute(values, "col", [(i, i ^ step) for i in range(count)])
-        step *= 2
-    return values
 
 
 def picked(stacked, index):
@@ -461,13 +441,6 @@
         ],
         axis=axis,
     )
-
-
-def row_norm(values):
-    average = jnp.mean(values, axis=1, keepdims=True)
-    centered = values - average
-    inverse = lax.rsqrt(jnp.mean(centered * centered, axis=1, keepdims=True) + norm_eps)
-    return (average, inverse)
 
 
 def mm(left, right, left_dim, right_dim, dtype=jnp.float32):
@@ -581,7 +554,7 @@
     out_ref[:, lanes(2)] = value_sum[...].astype(jnp.bfloat16)
 
 
-def local_backward(heads, head_grad, first_row):
+def local_backward(heads, head_grad, group, first_row):
     length = heads.shape[0]
     pairs = heads.shape[1] // (3 * PAIR)
     return pl.pallas_call(
@@ -590,7 +563,7 @@
         in_specs=[
             pl.BlockSpec((1, length), lambda p: (0, 0)),
             pl.BlockSpec((length, PAIR), lambda p: (0, p)),
-            pl.BlockSpec((length, PAIR), lambda p: (0, p)),
+            pl.BlockSpec((length, PAIR), lambda p: (0, group * pairs + p)),
             pl.BlockSpec((length, PAIR), lambda p: (0, pairs + p)),
             pl.BlockSpec((length, PAIR), lambda p: (0, 2 * pairs + p)),
         ],
@@ -665,14 +638,14 @@
     )(*normed, *grad, *own_pieces, *sib_pieces, bias)
 
 
-def unit_products_kernel(offset, own_ref, sib_ref, *refs):
+def unit_products_kernel(count, own_ref, sib_ref, *refs):
     out_ref = refs[-1]
-    unit = refs[0].shape[1] // 4
+    unit = refs[0].shape[1]
     total = None
-    for k, piece in enumerate(refs[:-1]):
+    for k in range(count):
         span = slice(k * unit, (k + 1) * unit)
-        for rows, start in ((own_ref, offset * unit), (sib_ref, (offset + 2) * unit)):
-            part = mm(rows[:, span], piece[:, start : start + unit], 1, 1)
+        for rows, piece in ((own_ref, refs[k]), (sib_ref, refs[count + k])):
+            part = mm(rows[:, span], piece[...], 1, 1)
             total = part if total is None else total + part
     out_ref[...] = total.astype(jnp.bfloat16)
 
@@ -680,14 +653,17 @@
 def unit_products(own_rows, sib_rows, pieces, which):
     tokens, twice = own_rows.shape
     width = pieces[0].shape[0]
+    unit = pieces[0].shape[1] // 4
     units = twice // 2
+    count = len(pieces)
     size = min(256, tokens)
     rows = pl.BlockSpec((size, units), lambda i: (i, which))
-    piece = pl.BlockSpec(pieces[0].shape, lambda i: (0, 0))
-    return pl.pallas_call(
-        functools.partial(unit_products_kernel, 1 - which),
+    own_piece = pl.BlockSpec((width, unit), lambda i: (0, 1 - which))
+    sib_piece = pl.BlockSpec((width, unit), lambda i: (0, 3 - which))
+    return pl.pallas_call(
+        functools.partial(unit_products_kernel, count),
         grid=(tokens // size,),
-        in_specs=[rows] * 2 + [piece] * len(pieces),
+        in_specs=[rows] * 2 + [own_piece] * count + [sib_piece] * count,
         out_specs=pl.BlockSpec((size, width), lambda i: (i, 0)),
         out_shape=jax.ShapeDtypeStruct((tokens, width), jnp.bfloat16),
         compiler_params=pltpu.CompilerParams(vmem_limit_bytes=vmem_bytes),
@@ -696,7 +672,7 @@
             bytes_accessed=6 * tokens * units + 4 * units * width,
             transcendentals=0,
         ),
-    )(own_rows, sib_rows, *pieces)
+    )(own_rows, sib_rows, *pieces, *pieces)
 
 
 def weight_products_kernel(count, *refs):
@@ -715,30 +691,401 @@
         up = up_part if up is None else up + up_part
         down = down_part if down is None else down + down_part
     for i, part in enumerate((up[:, :unit], down[:, :unit], up[:, unit:], down[:, unit:])):
-        out_ref[0, :, i * unit : (i + 1) * unit] = part.astype(jnp.bfloat16)
-
-
-def weight_products(normed, grads, own_rows, sib_rows, unit):
+        out_ref[:, i * unit : (i + 1) * unit] = part.astype(jnp.bfloat16)
+
+
+def weight_products(normed, grads, own_rows, sib_rows, unit, k):
     count = len(normed)
     tokens, width = normed[0].shape
     ring = own_rows[0].shape[1] // (2 * unit)
     size = min(256, width)
-    left = [pl.BlockSpec((tokens, size), lambda k, d: (0, d))] * (2 * count)
-    act = [pl.BlockSpec((tokens, unit), lambda k, d: (0, k))] * count
-    pre = [pl.BlockSpec((tokens, unit), lambda k, d: (0, ring + k))] * count
+    left = [pl.BlockSpec((tokens, size), lambda d: (0, d))] * (2 * count)
+    act = [pl.BlockSpec((tokens, unit), lambda d: (0, k))] * count
+    pre = [pl.BlockSpec((tokens, unit), lambda d: (0, ring + k))] * count
     return pl.pallas_call(
         functools.partial(weight_products_kernel, count),
-        grid=(ring, width // size),
+        grid=(width // size,),
         in_specs=left + act + pre + act + pre,
-        out_specs=pl.BlockSpec((1, size, 4 * unit), lambda k, d: (k, d, 0)),
-        out_shape=jax.ShapeDtypeStruct((ring, width, 4 * unit), jnp.bfloat16),
+        out_specs=pl.BlockSpec((size, 4 * unit), lambda d: (d, 0)),
+        out_shape=jax.ShapeDtypeStruct((width, 4 * unit), jnp.bfloat16),
         compiler_params=pltpu.CompilerParams(vmem_limit_bytes=vmem_bytes),
         cost_estimate=pl.CostEstimate(
-            flops=8 * count * tokens * width * ring * unit,
-            bytes_accessed=16 * count * tokens * width,
+            flops=8 * count * tokens * width * unit,
+            bytes_accessed=8 * count * tokens * width,
             transcendentals=0,
         ),
     )(*normed, *grads, *own_rows, *own_rows, *sib_rows, *sib_rows)
+
+
+def params(**more):
+    return pltpu.CompilerParams(vmem_limit_bytes=vmem_bytes, **more)
+
+
+def cost(flops, nbytes):
+    return pl.CostEstimate(flops=flops, bytes_accessed=nbytes, transcendentals=0)
+
+
+def shape(dims, dtype=jnp.bfloat16):
+    return jax.ShapeDtypeStruct(dims, dtype)
+
+
+def turned(values):
+    return values.astype(jnp.float32).T.astype(jnp.bfloat16)
+
+
+def pack_heads_kernel(index_ref, *refs):
+    sources, outs = refs[:8], refs[8:]
+    own = sources[0].shape[1]
+    for which in range(2):
+        parts = [sources[4 * which + i][...] for i in range(3)] + [turned(sources[4 * which + 3][...])]
+        for i, part in enumerate(parts):
+            if len(outs) == 1:
+                at = (4 * which + i) * own
+                outs[0][:, at : at + own] = part
+            else:
+                outs[which][:, i * own : (i + 1) * own] = part
+
+
+def pack_heads(index, weights, count, split):
+    width, units = weights[0].shape
+    own, block = units // 2, width // 4
+
+    def feature(which):
+        return pl.BlockSpec((block, own), lambda j, s: (s[1] ^ j, s[0] ^ which))
+
+    def turned_block(which):
+        return pl.BlockSpec((own, block), lambda j, s: (s[0] ^ which, s[1] ^ j))
+
+    in_specs = []
+    for which in range(2):
+        in_specs += [feature(which)] * 3 + [turned_block(which)]
+    if split:
+        out_specs = [pl.BlockSpec((block, 4 * own), lambda j, s: (j, 0))] * 2
+        out_shape = [shape((count * block, 4 * own))] * 2
+    else:
+        out_specs = pl.BlockSpec((block, 8 * own), lambda j, s: (j, 0))
+        out_shape = shape((count * block, 8 * own))
+    return pl.pallas_call(
+        pack_heads_kernel,
+        grid_spec=pltpu.PrefetchScalarGridSpec(
+            num_scalar_prefetch=1, grid=(count,), in_specs=in_specs, out_specs=out_specs
+        ),
+        out_shape=out_shape,
+        compiler_params=params(),
+        cost_estimate=cost(0, 32 * count * block * own),
+    )(index, *weights, *weights)
+
+
+def pack_ff_kernel(index_ref, up_own, down_own, up_sib, down_sib, out_ref):
+    unit = up_own.shape[1]
+    parts = (up_own[...], turned(down_own[...]), up_sib[...], turned(down_sib[...]))
+    for i, part in enumerate(parts):
+        out_ref[:, i * unit : (i + 1) * unit] = part
+
+
+def pack_ff(index, up_weight, down_weight):
+    width, units = up_weight.shape
+    unit, block = units // 8, width // 4
+    in_specs = []
+    for which in range(2):
+        in_specs += [
+            pl.BlockSpec((block, unit), lambda d, s, w=which: (d, 2 * s[1] + (s[0] ^ w))),
+            pl.BlockSpec((unit, block), lambda d, s, w=which: (2 * s[1] + (s[0] ^ w), d)),
+        ]
+    return pl.pallas_call(
+        pack_ff_kernel,
+        grid_spec=pltpu.PrefetchScalarGridSpec(
+            num_scalar_prefetch=1,
+            grid=(4,),
+            in_specs=in_specs,
+            out_specs=pl.BlockSpec((block, 4 * unit), lambda d, s: (d, 0)),
+        ),
+        out_shape=shape((width, 4 * unit)),
+        compiler_params=params(),
+        cost_estimate=cost(0, 16 * width * unit),
+    )(index, up_weight, down_weight, up_weight, down_weight)
+
+
+def stack_kernel(*refs):
+    pieces, own_ref, sib_ref = refs[:-2], refs[-2], refs[-1]
+    half = own_ref.shape[1]
+    at = 0
+    for piece in pieces:
+        end = at + piece.shape[0]
+        own_ref[at:end, :] = piece[:, :half]
+        sib_ref[at:end, :] = piece[:, half:]
+        at = end
+
+
+def stack_pieces(pieces):
+    rows = sum(p.shape[0] for p in pieces)
+    half = pieces[0].shape[1] // 2
+    return pl.pallas_call(
+        stack_kernel,
+        out_shape=[shape((rows, half))] * 2,
+        compiler_params=params(),
+        cost_estimate=cost(0, 8 * rows * half),
+    )(*pieces)
+
+
+def norm_kernel(index_ref, own_ref, sib_ref, vectors_ref, own_out, sib_out, stats_ref):
+    own = own_ref[...].astype(jnp.float32)
+    sib = sib_ref[...].astype(jnp.float32)
+    width = own.shape[1]
+    average = (jnp.sum(own, axis=1, keepdims=True) + jnp.sum(sib, axis=1, keepdims=True)) / (2 * width)
+    own, sib = own - average, sib - average
+    square = jnp.sum(own * own, axis=1, keepdims=True) + jnp.sum(sib * sib, axis=1, keepdims=True)
+    inverse = lax.rsqrt(square / (2 * width) + norm_eps)
+    block = width // 4
+    for half, (values, out) in enumerate(((own, own_out), (sib, sib_out))):
+        gain, shift = vectors_ref[2 * half, :][None], vectors_ref[2 * half + 1, :][None]
+        rounded = (values * inverse * gain + shift).astype(jnp.bfloat16)
+        for i in range(4):
+            at = pl.multiple_of((index_ref[1] ^ i) * block, block)
+            out[:, pl.ds(at, block)] = rounded[:, i * block : (i + 1) * block]
+    lane = lax.broadcasted_iota(jnp.int32, stats_ref.shape, 1)
+    stats_ref[...] = jnp.where(lane == 0, average, inverse)
+
+
+def norm_rows(index, own, sib, vectors):
+    tokens, width = own.shape
+    size = min(256, tokens)
+    rows = pl.BlockSpec((size, width), lambda i, s: (i, 0))
+    return pl.pallas_call(
+        norm_kernel,
+        grid_spec=pltpu.PrefetchScalarGridSpec(
+            num_scalar_prefetch=1,
+            grid=(tokens // size,),
+            in_specs=[rows, rows, pl.BlockSpec((4, width), lambda i, s: (0, 0))],
+            out_specs=[rows, rows, pl.BlockSpec((size, 128), lambda i, s: (i, 0))],
+        ),
+        out_shape=[shape((tokens, width))] * 2 + [shape((tokens, 128), jnp.float32)],
+        compiler_params=params(),
+        cost_estimate=cost(0, 8 * tokens * width),
+    )(index, own, sib, vectors)
+
+
+def project_kernel(own_ref, sib_ref, own_weight, sib_weight, bias_ref, out_ref):
+    total = mm(own_ref[...], own_weight[...], 1, 0) + mm(sib_ref[...], sib_weight[...], 1, 0)
+    out_ref[...] = (total + bias_ref[...]).astype(jnp.bfloat16)
+
+
+def project(own, sib, own_weight, sib_weight, bias):
+    tokens, width = own.shape
+    units = bias.shape[1]
+    size = min(256, tokens)
+    rows = pl.BlockSpec((size, width), lambda i: (i, 0))
+    weight = pl.BlockSpec((width, units), lambda i: (0, 0))
+    return pl.pallas_call(
+        project_kernel,
+        grid=(tokens // size,),
+        in_specs=[rows, rows, weight, weight, pl.BlockSpec((1, units), lambda i: (0, 0))],
+        out_specs=pl.BlockSpec((size, units), lambda i: (i, 0)),
+        out_shape=shape((tokens, units)),
+        compiler_params=params(),
+        cost_estimate=cost(4 * tokens * width * units, 4 * tokens * width + 4 * width * units),
+    )(own, sib, own_weight, sib_weight, bias)
+
+
+def out_rows_kernel(count, *refs):
+    out_ref = refs[-1]
+    total = refs[2 * count][...] if len(refs) > 2 * count + 1 else None
+    for i in range(count):
+        part = mm(refs[i][...], refs[count + i][...], 1, 1)
+        total = part if total is None else total + part
+    out_ref[...] = total
+
+
+def out_rows(attended, weights, before=None):
+    count = len(attended)
+    tokens, own = attended[0].shape
+    width = weights[0].shape[0]
+    size = min(256, tokens)
+    extra = [] if before is None else [before]
+    full = pl.BlockSpec((size, width), lambda i: (i, 0))
+    return pl.pallas_call(
+        functools.partial(out_rows_kernel, count),
+        grid=(tokens // size,),
+        in_specs=[pl.BlockSpec((size, own), lambda i: (i, 0))] * count
+        + [pl.BlockSpec((width, own), lambda i: (0, 3))] * count
+        + [full] * len(extra),
+        out_specs=full,
+        out_shape=shape((tokens, width), jnp.float32),
+        compiler_params=params(),
+        cost_estimate=cost(2 * count * tokens * own * width, 4 * tokens * width * (1 + len(extra))),
+    )(*attended, *weights, *extra)
+
+
+def head_grads_kernel(own_ref, sib_ref, *refs):
+    out_ref = refs[-1]
+    count = (len(refs) - 1) // 2
+    own = refs[0].shape[1]
+    for k in range(count):
+        total = mm(own_ref[...], refs[k][...], 1, 0) + mm(sib_ref[...], refs[count + k][...], 1, 0)
+        out_ref[:, k * own : (k + 1) * own] = total.astype(jnp.bfloat16)
+
+
+def head_grads(own, sib, own_weights, sib_weights):
+    tokens, width = own.shape
+    count = len(own_weights)
+    units = own_weights[0].shape[1] // 4
+    size = min(256, tokens)
+    rows = pl.BlockSpec((size, width), lambda i: (i, 0))
+    return pl.pallas_call(
+        head_grads_kernel,
+        grid=(tokens // size,),
+        in_specs=[rows] * 2 + [pl.BlockSpec((width, units), lambda i: (0, 3))] * (2 * count),
+        out_specs=pl.BlockSpec((size, count * units), lambda i: (i, 0)),
+        out_shape=shape((tokens, count * units)),
+        compiler_params=params(),
+        cost_estimate=cost(4 * count * tokens * width * units, 8 * tokens * width),
+    )(own, sib, *own_weights, *sib_weights)
+
+
+def head_products_kernel(*refs):
+    normed, grads = refs[:2], refs[2:4]
+    heads_ref, attended_ref = refs[4:6]
+    outs, sum_ref = refs[6:8], refs[8]
+    split = heads_ref.shape[1]
+    for i in range(2):
+        outs[i][:, :split] = mm(normed[i][...], heads_ref[...], 0, 0).astype(jnp.bfloat16)
+        outs[i][:, split:] = mm(grads[i][...], attended_ref[...], 0, 0).astype(jnp.bfloat16)
+
+    @pl.when(pl.program_id(0) == 0)
+    def _():
+        sum_ref[...] = jnp.sum(heads_ref[...].astype(jnp.float32), axis=0, keepdims=True)
+
+
+def head_products(normed, grads, head_grad, attended):
+    tokens, width = normed[0].shape
+    split, own = head_grad.shape[1], attended.shape[1]
+    size = min(256, width)
+    left = pl.BlockSpec((tokens, size), lambda d: (0, d))
+    out = pl.BlockSpec((size, split + own), lambda d: (d, 0))
+    return pl.pallas_call(
+        head_products_kernel,
+        grid=(width // size,),
+        in_specs=[left] * 4
+        + [pl.BlockSpec((tokens, split), lambda d: (0, 0)), pl.BlockSpec((tokens, own), lambda d: (0, 0))],
+        out_specs=[out, out, pl.BlockSpec((1, split), lambda d: (0, 0))],
+        out_shape=[shape((width, split + own))] * 2 + [shape((1, split), jnp.float32)],
+        compiler_params=params(),
+        cost_estimate=cost(4 * tokens * width * (split + own), 12 * tokens * width),
+    )(*normed, *grads, head_grad, attended)
+
+
+def back_rows_kernel(count, *refs):
+    own_out, sib_out = refs[-2:]
+    own = sib = None
+    for k in range(count):
+        grads = refs[k][...]
+        own_part = mm(grads, refs[count + k][...], 1, 1)
+        sib_part = mm(grads, refs[2 * count + k][...], 1, 1)
+        own = own_part if own is None else own + own_part
+        sib = sib_part if sib is None else sib + sib_part
+    own_out[...] = own
+    sib_out[...] = sib.astype(jnp.bfloat16)
+
+
+def back_rows(grads, own_weights, sib_weights):
+    count = len(grads)
+    tokens, units = grads[0].shape
+    width = own_weights[0].shape[0]
+    size = min(256, tokens)
+    full = pl.BlockSpec((size, width), lambda i: (i, 0))
+    return pl.pallas_call(
+        functools.partial(back_rows_kernel, count),
+        grid=(tokens // size,),
+        in_specs=[pl.BlockSpec((size, units), lambda i: (i, 0))] * count
+        + [pl.BlockSpec((width, units), lambda i: (0, 0))] * (2 * count),
+        out_specs=[full, full],
+        out_shape=[shape((tokens, width), jnp.float32), shape((tokens, width))],
+        compiler_params=params(),
+        cost_estimate=cost(4 * count * tokens * width * units, 4 * count * width * units),
+    )(*grads, *own_weights, *sib_weights)
+
+
+def select_piece(refs, step, use):
+    for j in range(3):
+
+        @pl.when(step == j)
+        def _():
+            use(refs[j][...])
+
+    @pl.when(step == 3)
+    def _():
+        use(jnp.concatenate([refs[3][...], refs[4][...]], axis=0))
+
+
+def place_heads_kernel(index_ref, *refs):
+    pieces, outs = refs[:5], refs[5:]
+    own = pieces[0].shape[1] // 8
+
+    def use(piece):
+        for which in range(2):
+            at = pl.multiple_of((index_ref[0] ^ which) * own, own)
+            for m in range(4):
+                part = piece[:, (4 * which + m) * own : (4 * which + m + 1) * own].astype(jnp.float32)
+                if m < 3:
+                    outs[m][:, pl.ds(at, own)] = part
+                else:
+                    outs[m][pl.ds(at, own), :] = part.T
+
+    select_piece(pieces, pl.program_id(0), use)
+
+
+def place_heads(index, pieces):
+    block, columns = pieces[0].shape
+    units, width = columns // 4, 4 * block
+    whole = [pl.BlockSpec(p.shape, lambda j, s: (0, 0)) for p in pieces]
+    return pl.pallas_call(
+        place_heads_kernel,
+        grid_spec=pltpu.PrefetchScalarGridSpec(
+            num_scalar_prefetch=1,
+            grid=(4,),
+            in_specs=whole,
+            out_specs=[pl.BlockSpec((block, units), lambda j, s: (s[1] ^ j, 0))] * 3
+            + [pl.BlockSpec((units, block), lambda j, s: (0, s[1] ^ j))],
+        ),
+        out_shape=[shape((width, units), jnp.float32)] * 3 + [shape((units, width), jnp.float32)],
+        compiler_params=params(),
+        cost_estimate=cost(0, 24 * width * units),
+    )(index, *pieces)
+
+
+def place_ff_kernel(index_ref, *refs):
+    pieces, (up_out, down_out) = refs[:5], refs[5:]
+    unit = pieces[0].shape[1] // 4
+
+    def use(piece):
+        for which in range(2):
+            at = pl.multiple_of((index_ref[0] ^ which) * unit, unit)
+            start = 2 * which * unit
+            up_out[:, pl.ds(at, unit)] = piece[:, start : start + unit].astype(jnp.float32)
+            down_out[pl.ds(at, unit), :] = piece[:, start + unit : start + 2 * unit].astype(jnp.float32).T
+
+    select_piece(pieces, pl.program_id(0), use)
+
+
+def place_ff(index, pieces):
+    width, columns = pieces[0].shape
+    quarter = columns // 2
+    whole = [pl.BlockSpec(p.shape, lambda j, s: (0, 0)) for p in pieces]
+    return pl.pallas_call(
+        place_ff_kernel,
+        grid_spec=pltpu.PrefetchScalarGridSpec(
+            num_scalar_prefetch=1,
+            grid=(4,),
+            in_specs=whole,
+            out_specs=[
+                pl.BlockSpec((width, quarter), lambda j, s: (0, s[1] ^ j)),
+                pl.BlockSpec((quarter, width), lambda j, s: (s[1] ^ j, 0)),
+            ],
+        ),
+        out_shape=[shape((width, 4 * quarter), jnp.float32), shape((4 * quarter, width), jnp.float32)],
+        compiler_params=params(),
+        cost_estimate=cost(0, 48 * width * quarter),
+    )(index, *pieces)
 
 
 def body_local(
@@ -772,92 +1119,93 @@
     block = width // 4
     quarter = up_weight.shape[1] // 4
     unit = quarter // 2
-    half_rows = rows // 2
-    plane, column = Plane(), Link()
-    both_cores = (row_i, 1 - row_i)
-
-    def cut(weight, start, size, axis):
-        return lax.dynamic_slice_in_dim(weight, start, size, axis=axis)
-
-    def by_core(weights, size):
-        return jnp.concatenate(
-            [cut(w, which * size, size, 1) for which in both_cores for w in weights], axis=1
-        )
-
-    names = (query_weight, key_weight, value_weight)
-    piece = [cut(w, plane_i * block, block, 0) for w in names]
-    piece.append(cut(out_weight, plane_i * block, block, 1).T)
-    pieces = ring_gather(column, by_core(piece, own))
+    half = rows // 2
+    plane, column, order = Plane(), Link(), Order()
+    index = jnp.stack([row_i, plane_i]).astype(jnp.int32)
+
+    def cut(values, start, size):
+        return lax.dynamic_slice_in_dim(values, start, size, axis=0)
+
+    mine = jnp.concatenate(
+        [
+            cut(query_bias, row_i * own, own),
+            jnp.zeros((own,), f32),
+            cut(value_bias, row_i * own, own),
+            cut(up_bias, plane_i * quarter + row_i * unit, unit),
+        ]
+    )
+    small = [mine] + [
+        lax.ppermute(mine, "col", [(i, (i + k) % ring) for i in range(ring)]) for k in range(1, ring)
+    ]
+    column.last = small[1:]
+    up_biases = jnp.concatenate([s[3 * own :] for s in small])[None, :]
+    head_biases = [s[None, : 3 * own] for s in small]
+
+    sources = (query_weight, key_weight, value_weight, out_weight)
+    piece = order.run(pack_heads, index, sources, 1, False)
+    pieces = ring_gather(column, piece)
 
     active_all = active_rows(segment_ids, active_lengths)
-    active_here = lax.dynamic_slice_in_dim(active_all, col_i * rows, rows)
+    active_here = cut(active_all, col_i * rows, rows)
     keep_mask = active_here.astype(f32)[:, None]
     branch_mine = (out_grad.astype(f32) * keep_mask).astype(bf16)
-    branch_first = plane.near(branch_mine[:half_rows])
-
+    branch_first = plane.near(branch_mine[:half])
     tokens_sib = swap(tokens_in)
-    gains = jnp.stack([norm1_gain, norm1_shift])
-    gains_sib = swap(gains)
-
+    vectors = jnp.stack([norm1_gain, norm1_shift])
+    vectors = jnp.concatenate([vectors, swap(vectors)], axis=0)
     segment_row = picked(segment_ids, col_i)
     member = (segment_row[:, None] == jnp.arange(active_lengths.shape[1])).astype(jnp.int32)
     counts = jnp.sum(member, axis=0)
     first_row = jnp.sum(member * (jnp.cumsum(counts) - counts), axis=1)[None, :]
 
-    ff_offset = plane_i * quarter
-    query_part = cut(query_bias, row_i * own, own, 0)
-    value_part = cut(value_bias, row_i * own, own, 0)
-    up_part = cut(up_bias, ff_offset + row_i * unit, unit, 0)
-    small = ring_gather(
-        Link(), jnp.concatenate([query_part, jnp.zeros_like(query_part), value_part, up_part])
-    )
-    up_biases = jnp.concatenate([s[3 * own :] for s in small])[None, :]
-
-    here = by_core(names + (out_weight.T,), own)
-    here = exchanged(here, plane_i, 0)
-    own_rows, other_units = [here[:, : 4 * own]], [here[:, 4 * own :]]
-    for piece in pieces[1:]:
-        gathered = plane.gather(piece)
-        own_rows.append(jnp.concatenate([p[:, : 4 * own] for p in gathered], axis=0))
-        other_units.append(jnp.concatenate([p[:, 4 * own :] for p in gathered], axis=0))
-    groups = [jnp.concatenate([a, swap(b)], axis=0) for a, b in zip(own_rows, other_units)]
-
-    branch_far = plane.far(*branch_first)
-    branch_second = plane.gather(branch_mine[half_rows:])
-    branch_first = [branch_mine[:half_rows], *branch_first, jnp.concatenate(branch_far, axis=0)]
-    branch_second = branch_second[:3] + [jnp.concatenate(branch_second[3:], axis=0)]
-    branch_own = [branch_mine] + [
-        jnp.concatenate([a, b], axis=0) for a, b in zip(branch_first[1:], branch_second[1:])
-    ]
-    branch_sib = [swap(b) for b in branch_own]
-
-    down_part = cut(down_weight, ff_offset, quarter, 0).T
-    up_part = cut(up_weight, ff_offset, quarter, 1)
-    ff_own = ring_gather(column, by_core((up_part, down_part), unit))
-    ff_sib = [swap(p[:, 2 * unit :]) for p in ff_own]
-
-    tokens_own = tokens_in.astype(f32)
-    tokens_all = jnp.concatenate([tokens_own, tokens_sib.astype(f32)], axis=1)
-    average_one, inverse_one = row_norm(tokens_all)
-    normed_one = jnp.concatenate(
-        [
-            exchanged((((t - average_one) * inverse_one) * g[0] + g[1]).astype(bf16), plane_i, 1)
-            for t, g in ((tokens_own, gains), (tokens_sib.astype(f32), gains_sib))
-        ],
-        axis=1,
-    )
-    heads, attended = [], []
-    attention_rows = None
-    for k in range(ring):
-        weights = groups[k]
-        head = (mm(normed_one, weights[:, : 3 * own], 1, 0) + small[k][: 3 * own]).astype(bf16)
-        result = local_forward(head, first_row)
+    own_parts, sib_parts = [[part] for part in order.run(pack_heads, index, sources, 4, True)]
+    other_rows = [swap(sib_parts[0])]
+    ff_piece = order.run(pack_ff, index, up_weight, down_weight)
+    ff_own = ring_gather(column, ff_piece)
+    *normed_one, stats_one = order.run(norm_rows, index, tokens_in, tokens_sib, vectors)
+
+    heads, attended, attended_sib = [], [], []
+
+    def attend(k):
+        head = order.run(
+            project, normed_one[0], normed_one[1], own_parts[k], other_rows[k], head_biases[k]
+        )
+        result = order.run(local_forward, head, first_row)
         heads.append(head)
         attended.append(result)
-        both = jnp.concatenate([result, swap(result)], axis=1)
-        out_both = jnp.concatenate([own_rows[k][:, 3 * own :], other_units[k][:, 3 * own :]], axis=1)
-        part = mm(both, out_both, 1, 1)
-        attention_rows = part if k == 0 else attention_rows + part
+        attended_sib.append(swap(result))
+
+    for k in range(1, ring):
+        near = plane.near(pieces[k])
+        attend(k - 1)
+        far = plane.far(*after(near, order.token))
+        gathered = [pieces[k], *near, *far]
+        if k < ring - 1:
+            upcoming = pieces[k + 1]
+            pieces[k + 1] = after(upcoming, *far)
+            past = (pieces[k + 1],)
+        else:
+            branch_first = after(branch_first, *far)
+            past = branch_first
+        own_part, sib_part = order.run(stack_pieces, gathered, past=past)
+        own_parts.append(own_part)
+        sib_parts.append(sib_part)
+        other_rows.append(swap(sib_part))
+    branch_far = plane.far(*branch_first)
+    second_near = plane.near(branch_mine[half:])
+    before = None
+    if ring > 1:
+        before = order.run(
+            out_rows,
+            attended[: ring - 1] + attended_sib[: ring - 1],
+            own_parts[: ring - 1] + sib_parts[: ring - 1],
+        )
+    attend(ring - 1)
+    second_far = plane.far(*second_near)
+    attention_rows = order.run(
+        out_rows, [attended[-1], attended_sib[-1]], [own_parts[-1], sib_parts[-1]], before
+    )
+    tokens_own = tokens_in.astype(f32)
     hidden_one = tokens_own + exchanged(attention_rows, plane_i, 1) + out_bias
 
     half_mean = jnp.mean(hidden_one, axis=1, keepdims=True)
@@ -872,31 +1220,70 @@
     normal_two = (hidden_one - average_two) * inverse_two
     normed_two = (normal_two * norm2_gain + norm2_shift).astype(bf16)
 
-    normed_own = plane.gather(normed_two)
-    normed_own = normed_own[:3] + [jnp.concatenate(normed_own[3:], axis=0)]
+    normed_own = [normed_two, *plane.near(normed_two)]
+    first = [branch_mine[:half], *branch_first, jnp.concatenate(branch_far, axis=0)]
+    second = [branch_mine[half:], *second_near, jnp.concatenate(second_far, axis=0)]
+    branch_own = [branch_mine] + [jnp.concatenate([first[j], second[j]], axis=0) for j in range(1, 4)]
+    branch_sib = [swap(b) for b in branch_own]
+    ff_sib = [swap(p[:, 2 * unit :]) for p in ff_own]
     chips, chip_sibs, up_sums = [], [], []
-    for j in range(4):
-        normed = (normed_own[j], swap(normed_own[j]))
-        if j > 0:
-            normed = after(normed, chips[-1])
-        chip, up_sum = ffn_rows_of(normed, (branch_own[j], branch_sib[j]), ff_own, ff_sib, up_biases)
+    grad_parts, down_parts = [None] * 4, [None] * 4
+
+    def feed_forward(j):
+        chip, up_sum = order.run(
+            ffn_rows_of,
+            (normed_own[j], swap(normed_own[j])),
+            (branch_own[j], branch_sib[j]),
+            ff_own,
+            ff_sib,
+            up_biases,
+        )
         chips.append(chip)
         chip_sibs.append(swap(chip))
         up_sums.append(up_sum)
-    grad_parts = [None] * 4
-    last = chips[3]
-    for j in (1, 2, 3, 0):
-        grad_parts[j] = unit_products(after(chips[j], last), chip_sibs[j], ff_own, 1)
-        last = grad_parts[j]
-    normed_grad_two = plane.sum_early(*grad_parts)
-    down_parts = [None] * 4
-    for j in (1, 2, 3, 0):
-        down_parts[j] = unit_products(after(chips[j], last), chip_sibs[j], ff_own, 0)
-        last = down_parts[j]
-    ff_grads = weight_products(normed_own, branch_own, [after(chips[0], last)] + chips[1:], chip_sibs, unit)
-    ff_sum = ring_sum(column, [ff_grads[k] for k in range(ring)])
-    ffn_rows = plane.sum_early(*down_parts) + down_bias
-    layer_out = jnp.where(active_here[:, None], hidden_one + ffn_rows, tokens_own)
+
+    def products(parts, j, which):
+        parts[j] = order.run(unit_products, chips[j], chip_sibs[j], ff_own, which)
+
+    def weight_grads(k):
+        return order.run(weight_products, normed_own, branch_own, chips, chip_sibs, unit, k)
+
+    feed_forward(0)
+    normed_far = plane.far(normed_own[1], normed_own[2])
+    normed_own.append(jnp.concatenate(normed_far, axis=0))
+    feed_forward(1)
+    feed_forward(2)
+    products(grad_parts, 1, 1)
+    feed_forward(3)
+    products(grad_parts, 2, 1)
+    x_top = plane.x.send(step_x, grad_parts[1][:half])
+    y_bottom = plane.y.send(step_y, grad_parts[2][half:])
+    products(grad_parts, 3, 1)
+    via_x = plane.x.send(step_x, grad_parts[3][:half])
+    via_y = plane.y.send(step_y, grad_parts[3][half:])
+    products(grad_parts, 0, 1)
+    products(down_parts, 1, 0)
+    products(down_parts, 2, 0)
+    products(down_parts, 3, 0)
+    via_x, via_y = after((via_x, via_y), order.token)
+    x_bottom = plane.add_x(grad_parts[1][half:], via_y)
+    y_top = plane.add_y(grad_parts[2][:half], via_x)
+    sent = plane.sent()
+    ff_grads = [None] * ring
+    order.token = (order.token, *sent)
+    ff_total = weight_grads(ring - 1)
+    ff_came = column.send(step_down, ff_total)
+    products(down_parts, 0, 0)
+    x_bottom, y_top = after((x_bottom, y_top), order.token)
+    normed_grad_two = jnp.concatenate(
+        [
+            grad_parts[0][:half].astype(f32) + x_top.astype(f32) + y_top.astype(f32),
+            grad_parts[0][half:].astype(f32) + x_bottom.astype(f32) + y_bottom.astype(f32),
+        ],
+        axis=0,
+    )
+    down_x_top = plane.x.send(step_x, down_parts[1][:half])
+    down_y_bottom = plane.y.send(step_y, down_parts[2][half:])
 
     def both_sums(one, two):
         sums = jnp.stack([jnp.sum(one, axis=1), jnp.sum(two, axis=1)])
@@ -909,59 +1296,48 @@
     attention_grad = hidden_grad.astype(bf16)
     gain_two_grad = jnp.sum(normed_grad_two * normal_two, axis=0)
     shift_two_grad = jnp.sum(normed_grad_two, axis=0)
-
-    grad_blocks = exchanged(attention_grad, plane_i, 1)
-    grad_blocks = jnp.concatenate([grad_blocks, swap(grad_blocks)], axis=1)
-    reduced = [None] * ring
-    normed_grad_one = None
-    bias_rows = [None] * ring
-    last = grad_blocks
+    grad_own = exchanged(attention_grad, plane_i, 1)
+    grad_sib = swap(grad_own)
+    order.token = (order.token, grad_own)
+    for k in range(ring - 2, ring // 2 - 1, -1):
+        ff_grads[k] = weight_grads(k)
+    via_x = plane.x.send(step_x, down_parts[3][:half])
+    via_y = plane.y.send(step_y, down_parts[3][half:])
+
+    head_grad = order.run(
+        head_grads, grad_own, grad_sib, own_parts, other_rows
+    )
+    head_rows, head_sums, bias_rows, swapped = [None] * ring, [None] * ring, [None] * ring, [None] * ring
+    stage = 0
     for k in range(ring - 1, -1, -1):
-        weights = groups[k]
-        head_grad = mm(after(grad_blocks, last), weights[:, 3 * own :], 1, 0, bf16)
-        grads = local_backward(heads[k], head_grad, first_row)
-        weight_grads = jnp.concatenate(
-            [mm(normed_one, grads, 0, 0, bf16), mm(grad_blocks, attended[k], 0, 0, bf16)], axis=1
+        head_rows[k] = order.run(
+            lambda h, g, f, k=k: local_backward(h, g, k, f), heads[k], head_grad, first_row
         )
-        last = weight_grads
-        mine = weight_grads[:width]
-        arrived = swap(weight_grads[width:])
-        reduced[k] = plane.sum_pairs(
-            [[m[j * block : (j + 1) * block] for m in (mine, arrived)] for j in range(4)]
+        mine, other, bias_rows[k] = order.run(
+            head_products, normed_one, (grad_own, grad_sib), head_rows[k], attended[k]
         )
-        bias_rows[k] = jnp.sum(grads.astype(f32), axis=0)
-        part = mm(grads, weights[:, : 3 * own], 1, 1)
-        normed_grad_one = part if normed_grad_one is None else normed_grad_one + part
-    head_sum = ring_sum(column, reduced)
-    head_all = exchanged(jnp.concatenate(plane.gather(head_sum), axis=0), plane_i, 0)
-
-    def by_row(mine, sib, axis):
-        return jnp.where(
-            row_i == 0,
-            jnp.concatenate([mine, sib], axis=axis),
-            jnp.concatenate([sib, mine], axis=axis),
-        )
-
-    query_weight_grad, key_weight_grad, value_weight_grad, out_weight_grad = [
-        by_row(head_all[:, m * own : (m + 1) * own], head_all[:, (4 + m) * own : (5 + m) * own], 1).astype(f32)
-        for m in range(4)
-    ]
-    out_weight_grad = out_weight_grad.T
-
-    ff_all = plane.gather(ff_sum)
-    ff_all = jnp.stack(ff_all[:3] + [jnp.concatenate(ff_all[3:], axis=0)])
-    up_parts, down_cuts = [], []
-    for q in range(4):
-        part = picked(ff_all, plane_i ^ q)
-        up_parts.append(by_row(part[:, :unit], part[:, 2 * unit : 3 * unit], 1))
-        down_cuts.append(by_row(part[:, unit : 2 * unit], part[:, 3 * unit :], 1))
-    up_weight_grad = jnp.concatenate(up_parts, axis=1).astype(f32)
-    down_weight_grad = jnp.concatenate(down_cuts, axis=1).T.astype(f32)
-
-    normed_grad_one = normed_grad_one[:, :width] + swap(
-        normed_grad_one[:, width:].astype(bf16)
-    ).astype(f32)
-    normed_grad_one = exchanged(normed_grad_one, plane_i, 1)
+        head_sums[k] = mine
+        swapped[k] = swap(other)
+        if stage == 0:
+            ff_came = after(ff_came, order.token)
+            ff_total = add_rounded(ff_came, ff_grads[ring - 2])
+            ff_came = column.send(step_down, ff_total)
+        if stage == 1:
+            via_x, via_y = after((via_x, via_y), order.token)
+            down_x_bottom = plane.add_x(down_parts[1][half:], via_y)
+            down_y_top = plane.add_y(down_parts[2][:half], via_x)
+        stage += 1
+    for k in range(ring // 2 - 1, -1, -1):
+        ff_grads[k] = weight_grads(k)
+    for k in range(ring - 3, -1, -1):
+        ff_came = after(ff_came, order.token)
+        ff_total = add_rounded(ff_came, ff_grads[k])
+        if k > 0:
+            ff_came = column.send(step_down, ff_total)
+
+    back_own, back_sib = order.run(back_rows, head_rows, own_parts, other_rows)
+    normed_grad_one = exchanged(back_own + swap(back_sib).astype(f32), plane_i, 1)
+    average_one, inverse_one = stats_one[:, :1], stats_one[:, 1:2]
     normal_own = (tokens_own - average_one) * inverse_one
     scaled = normed_grad_one * norm1_gain
     mean_one, mean_two = both_sums(scaled, scaled * normal_own)
@@ -971,8 +1347,8 @@
     input_grad = out_grad.astype(f32) * (1.0 - keep_mask) + hidden_grad + back_one
 
     def by_column(relative):
-        index = jnp.mod(col_i - jnp.arange(ring), ring)
-        return jnp.take(relative, index, axis=0)
+        places = jnp.mod(col_i - jnp.arange(ring), ring)
+        return jnp.take(relative, places, axis=0)
 
     row_hot = (jnp.arange(2) == row_i).astype(f32)
     plane_hot = (jnp.arange(4) == plane_i).astype(f32)
@@ -986,7 +1362,46 @@
     own_vector = jnp.concatenate(
         [gain_one_grad, shift_one_grad, gain_two_grad, shift_two_grad, out_bias_part, down_bias_part]
     )
-    summed = butterfly_sum(jnp.concatenate([bias_vector.reshape(-1), own_vector]))
+    summed = jnp.concatenate([bias_vector.reshape(-1), own_vector])
+
+    def part_of(k, j, which):
+        rows_of = slice(j * block, (j + 1) * block)
+        return (swapped if which else head_sums)[k][rows_of]
+
+    total = None
+    for k in range(ring - 1, -1, -1):
+        if k == 0:
+            summed = summed + plane.x.send(step_x, summed)
+            summed = summed + plane.y.send(step_y, summed)
+            step = 1
+            while step < ring:
+                pairs = [(i, i ^ step) for i in range(ring)]
+                summed = summed + column.send(lambda v: lax.ppermute(v, "col", pairs), summed)
+                step *= 2
+            ff_gathered = plane.gather(ff_total)
+        via_x = plane.x.send(step_x, part_of(k, 3, 0))
+        via_y = plane.y.send(step_y, part_of(k, 3, 1))
+        for_x = jnp.concatenate([part_of(k, 1, 0), add_rounded(part_of(k, 1, 1), via_y)], axis=1)
+        for_y = jnp.concatenate([add_rounded(part_of(k, 2, 0), via_x), part_of(k, 2, 1)], axis=1)
+        from_x = plane.x.send(step_x, for_x)
+        from_y = plane.y.send(step_y, for_y)
+        here = jnp.concatenate([part_of(k, 0, 0), part_of(k, 0, 1)], axis=1)
+        here = here.astype(f32) + from_x.astype(f32) + from_y.astype(f32)
+        if total is not None:
+            here = here + total.astype(f32)
+        total = here.astype(bf16)
+        if k > 0:
+            total = column.send(step_down, total)
+    up_weight_grad, down_weight_grad = place_ff(index, ff_gathered)
+    query_weight_grad, key_weight_grad, value_weight_grad, out_weight_grad = place_heads(
+        index, plane.gather(total)
+    )
+
+    down_top = down_parts[0][:half].astype(f32) + down_x_top.astype(f32) + down_y_top.astype(f32)
+    down_bottom = down_parts[0][half:].astype(f32) + down_x_bottom.astype(f32) + down_y_bottom.astype(f32)
+    ffn_rows = jnp.concatenate([down_top, down_bottom], axis=0) + down_bias
+    layer_out = jnp.where(active_here[:, None], hidden_one + ffn_rows, tokens_own)
+
     bias_here = picked(summed[: bias_vector.size].reshape(ring, -1), col_i)
     own_here = summed[bias_vector.size :].reshape(6, width)
     size = 2 * own
@@ -1016,7 +1431,7 @@
     local = (
         lax.axis_size("dp") == 4
         and lax.axis_size("row") == 2
-        and ring & (ring - 1) == 0
+        and ring == 4
         and tokens_in.shape[0] == segment_ids.shape[1]
     )
     chosen = body_local if local else body_general

time: 1210 us -> 1060 us (0.88)
  local copies, waits for them, and re-layouts: 220 us -> 81.7 us
  Pallas kernels: 260 us -> 396 us
  matrix products: 90.1 us -> 0 us
  other arithmetic: 104 us -> 57 us
  starting transfers between devices: 101 us -> 78.6 us
  waiting for transfers between devices: 420 us -> 440 us
    pallas_call x9 -> x33, Pallas kernels: 121 us -> 258 us  [the longest x8 60.1 us: unit_products(): pl.pallas_call(functools.partial(unit_products_kernel, count), grid=(toke...]
    unnamed x412 -> x294, local copies, waits for them, and re-layouts: 141 us -> 42.4 us
    dot_general x24 -> x0, matrix products: 90.1 us -> none  [mm(): lax.dot_general(left, right, (((left_dim,), (right_dim,)), ((), ())), pre...]
    ppermute x31, waiting for transfers between devices: 81.6 us -> 141 us  [step_y(): return lax.ppermute(values, 'dp', [(0, 2), (2, 0), (1, 3), (3, 1)])]
    ppermute x6, waiting for transfers between devices: 55.1 us -> 0.02 us  [step_down(): lax.ppermute(values, 'col', [(i, (i - 1) % count) for i in range(count)])]
    ppermute x31, waiting for transfers between devices: 189 us -> 226 us  [step_x(): return lax.ppermute(values, 'dp', [(0, 1), (1, 0), (2, 3), (3, 2)])]
    ppermute x9 -> x6, waiting for transfers between devices: 82.3 us -> 48.1 us  [step_up(): lax.ppermute(values, 'col', [(i, (i + 1) % count) for i in range(count)])]
    ppermute x6, starting transfers between devices: 22.2 us -> 0.3 us  [step_down(): lax.ppermute(values, 'col', [(i, (i - 1) % count) for i in range(count)])]
  transfers between devices with their start and end apart: 115 -> 115, of which waited for: 44 -> 53; matrix products, arithmetic and copies ran while one was open for 22% -> 8% of each run, Pallas kernels for 18% -> 36%
where the time goes in v4:
time: 1060 us
  waiting for transfers between devices  440 us (42%)
  Pallas kernels  396 us (37%)
  local copies, waits for them, and re-layouts  81.7 us (8%)
  starting transfers between devices  78.6 us (7%)
  other arithmetic  57 us (5%)
    ppermute x31, waiting for transfers between devices, step_x(): return lax.ppermute(values, 'dp', [(0, 1), (1, 0), (2, 3), (3, 2)])  226 us
    ppermute x31, waiting for transfers between devices, step_y(): return lax.ppermute(values, 'dp', [(0, 2), (2, 0), (1, 3), (3, 1)])  141 us
    pallas_call x4, Pallas kernels, ffn_rows_of(): pl.pallas_call(ffn_kernel, grid=(tokens // size,), in_specs=[rows] * 4 +...  62.5 us
    pallas_call x8, Pallas kernels, unit_products(): pl.pallas_call(functools.partial(unit_products_kernel, count), grid=(toke...  60.1 us
    pallas_call x4, Pallas kernels, weight_products(): pl.pallas_call(functools.partial(weight_products_kernel, count), grid=(wi...  60 us
    pallas_call x4, Pallas kernels, local_backward(): pl.pallas_call(functools.partial(local_backward_kernel, min(512, length))...  50.1 us
    ppermute x6, waiting for transfers between devices, step_up(): lax.ppermute(values, 'col', [(i, (i + 1) % count) for i in range(count)])  48.1 us
    unnamed x294, local copies, waits for them, and re-layouts  42.4 us
  transfers between devices with their start and end apart: 115, of which 53 were waited for; matrix products, arithmetic and copies ran while one was open for 8% of the time, Pallas kernels for 36%

profile of v4, /device:TPU:0, one launch (start us, length us, event | category | flops | bytes accessed | tf_op | source)
XLA Modules:
  0.0 1056.7 jit_solution(9580199444636960387)
XLA Ops:
  30.6 19.4 %collective-permute-done.9 = bf16[512,1024]{1,0:T(8,128)(2,1)S(1)} collective-permute-done((bf16[512,1024]{1,0:T(8,128)(2,1)}, bf16[512,1024]{1,0:T(8,128)(2,1)S(1)}, u32[]{:S(2)}, u32[]{:S(2)}) %collective-permute-start.9) | collective-permute-done | bytes 1048608 | tf_op jit(solution)/shard_map/ppermute | solution.py:353
  65.1 7.4 shard_map.318.query_ref.key_ref.value_ref
  72.5 6.5 shard_map.319.refs_0_.refs_5_
  84.0 8.5 collective-permute-done.12.refs_4_
  102.1 5.9 shard_map.321.query_ref.key_ref.value_ref
  108.0 6.5 shard_map.322.refs_1_.refs_5_
  114.6 7.4 collective-permute-done.15.refs_1_
  125.3 11.2 %collective-permute-done.18.refs_4_ = bf16[128,2048]{1,0:T(8,128)(2,1)S(1)} collective-permute-done((bf16[128,2048]{1,0:T(8,128)(2,1)S(1)}, bf16[128,2048]{1,0:T(8,128)(2,1)S(1)}, u32[]{:S(2)}, u32[]{:S(2)}) %collective-permute-start.18) | collective-permute-done | bytes 524320 | tf_op jit(solution)/shard_map/ppermute | solution.py:349
  144.9 5.9 shard_map.324.query_ref.key_ref.value_ref
  150.8 6.5 shard_map.325.refs_2_.refs_5_
  157.3 7.4 collective-permute-done.24.refs_1_
  167.1 12.1 %collective-permute-done.27.refs_4_ = bf16[128,2048]{1,0:T(8,128)(2,1)S(1)} collective-permute-done((bf16[128,2048]{1,0:T(8,128)(2,1)S(1)}, bf16[128,2048]{1,0:T(8,128)(2,1)S(1)}, u32[]{:S(2)}, u32[]{:S(2)}) %collective-permute-start.27) | collective-permute-done | bytes 524320 | tf_op jit(solution)/shard_map/ppermute | solution.py:349
  188.8 7.1 shard_map.327.refs_4_
  197.2 5.9 shard_map.328.query_ref.key_ref.value_ref
  203.1 6.5 shard_map.329.refs_0_.refs_5_
  209.7 22.5 %collective-permute-done.33.refs_5_.refs_1_ = bf16[1024,1024]{1,0:T(8,128)(2,1)} collective-permute-done((bf16[1024,1024]{1,0:T(8,128)(2,1)S(1)}, bf16[1024,1024]{1,0:T(8,128)(2,1)}, u32[]{:S(2)}, u32[]{:S(2)}) %collective-permute-start.33) | collective-permute-done | bytes 2097184 | tf_op jit(solution)/shard_map/ppermute | solution.py:358
  247.6 9.8 collective-permute-done.41
  260.8 10.4 collective-permute-done.44
  272.6 8.8 collective-permute-done.34.refs_6_.refs_2_
  283.6 6.8 collective-permute-done.36.refs_8_
  293.2 23.5 %collective-permute-done.45.refs_0_.refs_1_ = bf16[1024,1024]{1,0:T(8,128)(2,1)S(1)} collective-permute-done((bf16[1024,1024]{1,0:T(8,128)(2,1)S(1)}, bf16[1024,1024]{1,0:T(8,128)(2,1)S(1)}, u32[]{:S(2)}, u32[]{:S(2)}) %collective-permute-start.45) | collective-permute-done | bytes 2097184 | tf_op jit(solution)/shard_map/ppermute | solution.py:349
  319.7 10.1 collective-permute-done.35.refs_7_.refs_3_
  338.5 15.4 %shard_map.331 = (bf16[1024,2048]{1,0:T(8,128)(2,1)}, f32[1,1024]{1,0:T(1,128)S(1)}) custom-call(bf16[1024,1024]{1,0:T(8,128)(2,1)} %copy-done.3, bf16[1024,1024]{1,0:T(8,128)(2,1)} %copy-done.138, bf16[1024,1024]{1,0:T(8,128)(2,1)} %copy-done.79, bf16[1024,1024]{1,0:T(8,128)(2,1)} %copy-done.137, bf16[1024,1024]{1,0:T(8,128)(2,1)} %copy-done, ...), custom_call_target="tpu_custom_call" | custom-call | flops 8589934592 | bytes 20971520 | tf_op jit(solution)/shard_map/pallas_call | solution.py:620
  353.9 15.5 %shard_map.332 = (bf16[1024,2048]{1,0:T(8,128)(2,1)}, f32[1,1024]{1,0:T(1,128)S(1)}) custom-call(bf16[1024,1024]{1,0:T(8,128)(2,1)} %copy-done.82, bf16[1024,1024]{1,0:T(8,128)(2,1)} %collective-permute-done.51.refs_1_, bf16[1024,1024]{1,0:T(8,128)(2,1)} %constant_dynamic-update-slice_fusion.2.refs_2_.refs_5_, ...), custom_call_target="tpu_custom_call" | custom-call | flops 8589934592 | bytes 20971520 | tf_op jit(solution)/shard_map/pallas_call | solution.py:620
  369.6 13.5 %collective-permute-done.47.refs_0_.refs_2_ = bf16[1024,1024]{1,0:T(8,128)(2,1)S(1)} collective-permute-done((bf16[1024,1024]{1,0:T(8,128)(2,1)S(1)}, bf16[1024,1024]{1,0:T(8,128)(2,1)S(1)}, u32[]{:S(2)}, u32[]{:S(2)}) %collective-permute-start.47) | collective-permute-done | bytes 2097184 | tf_op jit(solution)/shard_map/ppermute | solution.py:353
  392.0 15.5 %collective-permute-done.48 = bf16[512,1024]{1,0:T(8,128)(2,1)S(1)} collective-permute-done((bf16[512,1024]{1,0:T(8,128)(2,1)S(1)}, bf16[512,1024]{1,0:T(8,128)(2,1)S(1)}, u32[]{:S(2)}, u32[]{:S(2)}) %collective-permute-start.48) | collective-permute-done | bytes 1048608 | tf_op jit(solution)/shard_map/ppermute | solution.py:353
  412.3 15.4 %shard_map.333 = (bf16[1024,2048]{1,0:T(8,128)(2,1)}, f32[1,1024]{1,0:T(1,128)S(1)}) custom-call(bf16[1024,1024]{1,0:T(8,128)(2,1)} %copy-done.84, bf16[1024,1024]{1,0:T(8,128)(2,1)} %copy-done.139, bf16[1024,1024]{1,0:T(8,128)(2,1)} %copy-done.85, bf16[1024,1024]{1,0:T(8,128)(2,1)} %collective-permute-done.54.refs_3_, bf16[1024,1024]{1,0:T(8,128)(2,1)} %copy-done, ...), custom_call_target="tpu_custom_call" | custom-call | flops 8589934592 | bytes 20971520 | tf_op jit(solution)/shard_map/pallas_call | solution.py:620
  429.8 7.5 shard_map.334
  437.3 16.1 %shard_map.335 = (bf16[1024,2048]{1,0:T(8,128)(2,1)}, f32[1,1024]{1,0:T(1,128)S(1)}) custom-call(bf16[1024,1024]{1,0:T(8,128)(2,1)} %constant_dynamic-update-slice_fusion.refs_0_.refs_3_, bf16[1024,1024]{1,0:T(8,128)(2,1)} %collective-permute-done.50.refs_1_, bf16[1024,1024]{1,0:T(8,128)(2,1)} %constant_dynamic-update-slice_fusion.6.refs_2_.refs_7_, ...), custom_call_target="tpu_custom_call" | custom-call | flops 8589934592 | bytes 20971520 | tf_op jit(solution)/shard_map/pallas_call | solution.py:620
  456.5 7.5 shard_map.336
  468.2 7.5 shard_map.337
  475.9 16.2 %collective-permute-done.62 = bf16[512,1024]{1,0:T(8,128)(2,1)} collective-permute-done((bf16[512,1024]{1,0:T(8,128)(2,1)}, bf16[512,1024]{1,0:T(8,128)(2,1)}, u32[]{:S(2)}, u32[]{:S(2)}) %collective-permute-start.62) | collective-permute-done | bytes 1048608 | tf_op jit(solution)/shard_map/ppermute | solution.py:353
  493.6 7.5 shard_map.338
  501.1 7.5 shard_map.339
  509.9 7.5 shard_map.340
  518.8 7.6 shard_map.341
  533.7 15.9 %shard_map.342 = bf16[1024,1024]{1,0:T(8,128)(2,1)} custom-call(bf16[1024,1024]{1,0:T(8,128)(2,1)S(1)} %copy-done.4, bf16[1024,1024]{1,0:T(8,128)(2,1)} %copy-done.82, bf16[1024,1024]{1,0:T(8,128)(2,1)} %copy-done.84, bf16[1024,1024]{1,0:T(8,128)(2,1)} %constant_dynamic-update-slice_fusion.refs_0_.refs_3_, bf16[1024,1024]{1,0:T(8,128)(2,1)} %copy-done.79, ...), custom_call_target="tpu_custom_call" | custom-call | flops 8589934592 | bytes 33554432 | tf_op jit(solution)/shard_map/pallas_call | solution.py:705
  549.6 7.5 shard_map.343
  577.5 14.7 %shard_map.344 = bf16[1024,1024]{1,0:T(8,128)(2,1)S(1)} custom-call(bf16[1024,1024]{1,0:T(8,128)(2,1)S(1)} %copy-done.5, bf16[1024,1024]{1,0:T(8,128)(2,1)} %copy-done.82, bf16[1024,1024]{1,0:T(8,128)(2,1)} %copy-done.84, bf16[1024,1024]{1,0:T(8,128)(2,1)} %constant_dynamic-update-slice_fusion.refs_0_.refs_3_, bf16[1024,1024]{1,0:T(8,128)(2,1)} %copy-done.79, ...), custom_call_target="tpu_custom_call" | custom-call | flops 8589934592 | bytes 33554432 | tf_op jit(solution)/shard_map/pallas_call | solution.py:705
  592.3 7.7 collective-permute-done.68
  603.3 7.7 shard_map.345.grad_ref
  611.1 12.4 %shard_map.346.refs_4_.refs_3_ = bf16[1024,768]{1,0:T(8,128)(2,1)S(1)} custom-call(s32[1,1024]{1,0:T(1,128)S(1)} %bitcast.54, bf16[1024,768]{1,0:T(8,128)(2,1)S(1)} %copy-done.65, bf16[1024,1024]{1,0:T(8,128)(2,1)S(1)} %shard_map.345.grad_ref, bf16[1024,768]{1,0:T(8,128)(2,1)S(1)} %copy-done.65, bf16[1024,768]{1,0:T(8,128)(2,1)S(1)} %copy-done.65), custom_call_target="tpu_custom_call" | custom-call | flops 8589934592 | bytes 6291456 | tf_op jit(solution)/shard_map/pallas_call | solution.py:560
  623.5 9.0 shard_map.347
  635.1 12.8 %shard_map.348.refs_4_.refs_2_ = bf16[1024,768]{1,0:T(8,128)(2,1)S(1)} custom-call(s32[1,1024]{1,0:T(1,128)S(1)} %bitcast.55, bf16[1024,768]{1,0:T(8,128)(2,1)S(1)} %copy-done.63, bf16[1024,1024]{1,0:T(8,128)(2,1)S(1)} %shard_map.345.grad_ref, bf16[1024,768]{1,0:T(8,128)(2,1)S(1)} %copy-done.63, bf16[1024,768]{1,0:T(8,128)(2,1)S(1)} %copy-done.63), custom_call_target="tpu_custom_call" | custom-call | flops 8589934592 | bytes 6291456 | tf_op jit(solution)/shard_map/pallas_call | solution.py:560
  648.0 9.0 shard_map.349
  657.1 12.4 %shard_map.350.refs_4_.refs_1_ = bf16[1024,768]{1,0:T(8,128)(2,1)S(1)} custom-call(s32[1,1024]{1,0:T(1,128)S(1)} %bitcast.56, bf16[1024,768]{1,0:T(8,128)(2,1)S(1)} %copy-done.61, bf16[1024,1024]{1,0:T(8,128)(2,1)S(1)} %shard_map.345.grad_ref, bf16[1024,768]{1,0:T(8,128)(2,1)S(1)} %copy-done.61, bf16[1024,768]{1,0:T(8,128)(2,1)S(1)} %copy-done.61), custom_call_target="tpu_custom_call" | custom-call | flops 8589934592 | bytes 6291456 | tf_op jit(solution)/shard_map/pallas_call | solution.py:560
  669.5 9.0 shard_map.351
  688.9 12.6 %shard_map.352.refs_4_.refs_0_ = bf16[1024,768]{1,0:T(8,128)(2,1)S(1)} custom-call(s32[1,1024]{1,0:T(1,128)S(1)} %bitcast.57, bf16[1024,768]{1,0:T(8,128)(2,1)S(1)} %copy-done.59, bf16[1024,1024]{1,0:T(8,128)(2,1)S(1)} %shard_map.345.grad_ref, bf16[1024,768]{1,0:T(8,128)(2,1)S(1)} %copy-done.59, bf16[1024,768]{1,0:T(8,128)(2,1)S(1)} %copy-done.59), custom_call_target="tpu_custom_call" | custom-call | flops 8589934592 | bytes 6291456 | tf_op jit(solution)/shard_map/pallas_call | solution.py:560
  701.4 8.9 shard_map.353
  712.6 14.6 %shard_map.354 = bf16[1024,1024]{1,0:T(8,128)(2,1)S(1)} custom-call(bf16[1024,1024]{1,0:T(8,128)(2,1)S(1)} %copy-done.5, bf16[1024,1024]{1,0:T(8,128)(2,1)} %copy-done.82, bf16[1024,1024]{1,0:T(8,128)(2,1)} %copy-done.84, bf16[1024,1024]{1,0:T(8,128)(2,1)} %constant_dynamic-update-slice_fusion.refs_0_.refs_3_, bf16[1024,1024]{1,0:T(8,128)(2,1)} %copy-done.79, ...), custom_call_target="tpu_custom_call" | custom-call | flops 8589934592 | bytes 33554432 | tf_op jit(solution)/shard_map/pallas_call | solution.py:705
  728.5 14.7 %shard_map.355 = bf16[1024,1024]{1,0:T(8,128)(2,1)S(1)} custom-call(bf16[1024,1024]{1,0:T(8,128)(2,1)S(1)} %copy-done.5, bf16[1024,1024]{1,0:T(8,128)(2,1)} %copy-done.82, bf16[1024,1024]{1,0:T(8,128)(2,1)} %copy-done.84, bf16[1024,1024]{1,0:T(8,128)(2,1)} %constant_dynamic-update-slice_fusion.refs_0_.refs_3_, bf16[1024,1024]{1,0:T(8,128)(2,1)} %copy-done.79, ...), custom_call_target="tpu_custom_call" | custom-call | flops 8589934592 | bytes 33554432 | tf_op jit(solution)/shard_map/pallas_call | solution.py:705
  744.6 19.8 %shard_map.356 = (f32[1024,1024]{1,0:T(8,128)}, bf16[1024,1024]{1,0:T(8,128)(2,1)}) custom-call(bf16[1024,768]{1,0:T(8,128)(2,1)S(1)} %copy-done.72, bf16[1024,768]{1,0:T(8,128)(2,1)S(1)} %copy-done.70, bf16[1024,768]{1,0:T(8,128)(2,1)S(1)} %copy-done.68, bf16[1024,768]{1,0:T(8,128)(2,1)} %copy-done.66, ...), custom_call_target="tpu_custom_call" | custom-call | flops 12884901888 | bytes 12582912 | tf_op jit(solution)/shard_map/pallas_call | solution.py:996
  769.9 9.8 collective-permute-done.80
  791.2 19.1 %collective-permute-done.81 = bf16[256,2048]{1,0:T(8,128)(2,1)} collective-permute-done((bf16[256,2048]{1,0:T(8,128)(2,1)S(1)}, bf16[256,2048]{1,0:T(8,128)(2,1)}, u32[]{:S(2)}, u32[]{:S(2)}) %collective-permute-start.81) | collective-permute-done | bytes 1048608 | tf_op jit(solution)/shard_map/ppermute | solution.py:349
  816.7 5.9 collective-permute-done.82
  828.7 18.6 %collective-permute-done.86 = bf16[256,2048]{1,0:T(8,128)(2,1)S(1)} collective-permute-done((bf16[256,2048]{1,0:T(8,128)(2,1)S(1)}, bf16[256,2048]{1,0:T(8,128)(2,1)S(1)}, u32[]{:S(2)}, u32[]{:S(2)}) %collective-permute-start.86) | collective-permute-done | bytes 1048608 | tf_op jit(solution)/shard_map/ppermute | solution.py:353
  849.0 8.8 collective-permute-done.87
  866.4 16.5 %collective-permute-done.90 = bf16[256,2048]{1,0:T(8,128)(2,1)S(1)} collective-permute-done((bf16[256,2048]{1,0:T(8,128)(2,1)S(1)}, bf16[256,2048]{1,0:T(8,128)(2,1)S(1)}, u32[]{:S(2)}, u32[]{:S(2)}) %collective-permute-start.90) | collective-permute-done | bytes 1048608 | tf_op jit(solution)/shard_map/ppermute | solution.py:349
  897.3 35.7 %collective-permute-done.103.refs_1_ = bf16[1024,1024]{1,0:T(8,128)(2,1)S(1)} collective-permute-done((bf16[1024,1024]{1,0:T(8,128)(2,1)S(1)}, bf16[1024,1024]{1,0:T(8,128)(2,1)S(1)}, u32[]{:S(2)}, u32[]{:S(2)}) %collective-permute-start.103) | collective-permute-done | bytes 2097184 | tf_op jit(solution)/shard_map/ppermute | solution.py:349
  941.6 19.2 %collective-permute-done.105.refs_3_ = bf16[512,1024]{1,0:T(8,128)(2,1)S(1)} collective-permute-done((bf16[512,1024]{1,0:T(8,128)(2,1)S(1)}, bf16[512,1024]{1,0:T(8,128)(2,1)S(1)}, u32[]{:S(2)}, u32[]{:S(2)}) %collective-permute-start.105) | collective-permute-done | bytes 1048608 | tf_op jit(solution)/shard_map/ppermute | solution.py:353
  963.3 13.5 %collective-permute-done.108 = bf16[256,1024]{1,0:T(8,128)(2,1)S(1)} collective-permute-done((bf16[256,1024]{1,0:T(8,128)(2,1)S(1)}, bf16[256,1024]{1,0:T(8,128)(2,1)S(1)}, u32[]{:S(2)}, u32[]{:S(2)}) %collective-permute-start.108) | collective-permute-done | bytes 524320 | tf_op jit(solution)/shard_map/ppermute | solution.py:349
  978.8 21.6 %collective-permute-done.109 = bf16[256,2048]{1,0:T(8,128)(2,1)S(1)} collective-permute-done((bf16[256,2048]{1,0:T(8,128)(2,1)S(1)}, bf16[256,2048]{1,0:T(8,128)(2,1)S(1)}, u32[]{:S(2)}, u32[]{:S(2)}) %collective-permute-start.109) | collective-permute-done | bytes 1048608 | tf_op jit(solution)/shard_map/ppermute | solution.py:349
  1004.4 17.5 %collective-permute-done.111.refs_1_ = bf16[256,2048]{1,0:T(8,128)(2,1)S(1)} collective-permute-done((bf16[256,2048]{1,0:T(8,128)(2,1)S(1)}, bf16[256,2048]{1,0:T(8,128)(2,1)S(1)}, u32[]{:S(2)}, u32[]{:S(2)}) %collective-permute-start.111) | collective-permute-done | bytes 1048608 | tf_op jit(solution)/shard_map/ppermute | solution.py:349
  1041.5 9.2 shard_map.358
  (662 shorter events, 292.6 us)
Async XLA Ops:
  9.1 50.3 %collective-permute-start = (bf16[1024,1024]{1,0:T(8,128)(2,1)}, bf16[1024,1024]{1,0:T(8,128)(2,1)}, u32[]{:S(2)}, u32[]{:S(2)}) collective-permute-start(bf16[1024,1024]{1,0:T(8,128)(2,1)} %own_ref.1), channel_id=1, source_target_pairs={{0,4},{4,0},{1,5},{5,1},{2,6},{6,2},{3,7},{7,3},{8,12},{12,8},{9,1... | collective-permute-start | bytes 6291464 | tf_op jit(solution)/shard_map/ppermute | solution.py:345
  18.4 46.7 %collective-permute-start.2 = (bf16[1024,1024]{1,0:T(8,128)(2,1)}, bf16[1024,1024]{1,0:T(8,128)(2,1)}, u32[]{:S(2)}, u32[]{:S(2)}) collective-permute-start(bf16[1024,1024]{1,0:T(8,128)(2,1)} %get-tuple-element.239.refs_9_), channel_id=1, source_target_pairs={{0,4},{4,0},{1,5},{5,1},{2,6},{6,2},{3,7},{7,3},{8,12},{12,8},{9,1... | collective-permute-start | bytes 6291464 | tf_op jit(solution)/shard_map/ppermute | solution.py:345
  24.8 25.3 %collective-permute-start.9 = (bf16[512,1024]{1,0:T(8,128)(2,1)}, bf16[512,1024]{1,0:T(8,128)(2,1)S(1)}, u32[]{:S(2)}, u32[]{:S(2)}) collective-permute-start(bf16[512,1024]{1,0:T(8,128)(2,1)} %get-tuple-element.518), channel_id=1, source_target_pairs={{0,16},{16,0},{8,24},{24,8},{1,17},{17,1},{9,25},{25,9},{2,18},{18... | collective-permute-start | bytes 3145736 | tf_op jit(solution)/shard_map/ppermute | solution.py:353
  26.3 26.7 %collective-permute-start.6 = (bf16[256,2048]{1,0:T(8,128)(2,1)S(1)}, bf16[256,2048]{1,0:T(8,128)(2,1)}, u32[]{:S(2)}, u32[]{:S(2)}) collective-permute-start(bf16[256,2048]{1,0:T(8,128)(2,1)S(1)} %shard_map.314), channel_id=1, source_target_pairs={{0,1},{1,2},{2,3},{3,0},{4,5},{5,6},{6,7},{7,4},{8,9},{9,10},{10,1... | collective-permute-start | bytes 3145736 | tf_op jit(solution)/shard_map/ppermute | solution.py:358
  28.8 24.8 %collective-permute-start.7 = (bf16[512,1024]{1,0:T(8,128)(2,1)}, bf16[512,1024]{1,0:T(8,128)(2,1)}, u32[]{:S(2)}, u32[]{:S(2)}) collective-permute-start(bf16[512,1024]{1,0:T(8,128)(2,1)} %get-tuple-element.518), channel_id=1, source_target_pairs={{0,8},{8,0},{16,24},{24,16},{1,9},{9,1},{17,25},{25,17},{2,10},{10... | collective-permute-start | bytes 3145736 | tf_op jit(solution)/shard_map/ppermute | solution.py:349
  53.0 26.0 %collective-permute-start.10 = (bf16[256,2048]{1,0:T(8,128)(2,1)}, bf16[256,2048]{1,0:T(8,128)(2,1)S(1)}, u32[]{:S(2)}, u32[]{:S(2)}) collective-permute-start(bf16[256,2048]{1,0:T(8,128)(2,1)} %collective-permute-done.6.refs_0_), channel_id=1, source_target_pairs={{0,16},{16,0},{8,24},{24,8},{1,17},{17,1},{9,25},{25,9},{2,18},{18... | collective-permute-start | bytes 3145736 | tf_op jit(solution)/shard_map/ppermute | solution.py:353
  53.6 25.4 %collective-permute-start.8 = (bf16[256,2048]{1,0:T(8,128)(2,1)}, bf16[256,2048]{1,0:T(8,128)(2,1)S(1)}, u32[]{:S(2)}, u32[]{:S(2)}) collective-permute-start(bf16[256,2048]{1,0:T(8,128)(2,1)} %collective-permute-done.6.refs_0_), channel_id=1, source_target_pairs={{0,8},{8,0},{16,24},{24,16},{1,9},{9,1},{17,25},{25,17},{2,10},{10... | collective-permute-start | bytes 3145736 | tf_op jit(solution)/shard_map/ppermute | solution.py:349
  58.7 25.4 %collective-permute-start.13 = (bf16[256,2048]{1,0:T(8,128)(2,1)}, bf16[256,2048]{1,0:T(8,128)(2,1)S(1)}, u32[]{:S(2)}, u32[]{:S(2)}) collective-permute-start(bf16[256,2048]{1,0:T(8,128)(2,1)} %collective-permute-done.6.refs_0_), channel_id=1, source_target_pairs={{0,1},{1,2},{2,3},{3,0},{4,5},{5,6},{6,7},{7,4},{8,9},{9,10},{10,1... | collective-permute-start | bytes 3145736 | tf_op jit(solution)/shard_map/ppermute | solution.py:358
  96.3 25.6 %collective-permute-start.15 = (bf16[256,2048]{1,0:T(8,128)(2,1)S(1)}, bf16[256,2048]{1,0:T(8,128)(2,1)S(1)}, u32[]{:S(2)}, u32[]{:S(2)}) collective-permute-start(bf16[256,2048]{1,0:T(8,128)(2,1)S(1)} %collective-permute-done.13.refs_0_), channel_id=1, source_target_pairs={{0,8},{8,0},{16,24},{24,16},{1,9},{9,1},{17,25},{25,17},{2,10},{10... | collective-permute-start | bytes 3145736 | tf_op jit(solution)/shard_map/ppermute | solution.py:349
  97.8 25.3 %collective-permute-start.16 = (bf16[256,2048]{1,0:T(8,128)(2,1)S(1)}, bf16[256,2048]{1,0:T(8,128)(2,1)S(1)}, u32[]{:S(2)}, u32[]{:S(2)}) collective-permute-start(bf16[256,2048]{1,0:T(8,128)(2,1)S(1)} %collective-permute-done.13.refs_0_), channel_id=1, source_target_pairs={{0,16},{16,0},{8,24},{24,8},{1,17},{17,1},{9,25},{25,9},{2,18},{18... | collective-permute-start | bytes 3145736 | tf_op jit(solution)/shard_map/ppermute | solution.py:353
  98.3 27.0 %collective-permute-start.19 = (bf16[256,2048]{1,0:T(8,128)(2,1)S(1)}, bf16[256,2048]{1,0:T(8,128)(2,1)S(1)}, u32[]{:S(2)}, u32[]{:S(2)}) collective-permute-start(bf16[256,2048]{1,0:T(8,128)(2,1)S(1)} %collective-permute-done.13.refs_0_), channel_id=1, source_target_pairs={{0,1},{1,2},{2,3},{3,0},{4,5},{5,6},{6,7},{7,4},{8,9},{9,10},{10,1... | collective-permute-start | bytes 3145736 | tf_op jit(solution)/shard_map/ppermute | solution.py:358
  139.1 25.6 %collective-permute-start.24 = (bf16[256,2048]{1,0:T(8,128)(2,1)S(1)}, bf16[256,2048]{1,0:T(8,128)(2,1)S(1)}, u32[]{:S(2)}, u32[]{:S(2)}) collective-permute-start(bf16[256,2048]{1,0:T(8,128)(2,1)S(1)} %collective-permute-done.19.refs_0_), channel_id=1, source_target_pairs={{0,8},{8,0},{16,24},{24,16},{1,9},{9,1},{17,25},{25,17},{2,10},{10... | collective-permute-start | bytes 3145736 | tf_op jit(solution)/shard_map/ppermute | solution.py:349
  140.6 25.3 %collective-permute-start.25 = (bf16[256,2048]{1,0:T(8,128)(2,1)S(1)}, bf16[256,2048]{1,0:T(8,128)(2,1)S(1)}, u32[]{:S(2)}, u32[]{:S(2)}) collective-permute-start(bf16[256,2048]{1,0:T(8,128)(2,1)S(1)} %collective-permute-done.19.refs_0_), channel_id=1, source_target_pairs={{0,16},{16,0},{8,24},{24,8},{1,17},{17,1},{9,25},{25,9},{2,18},{18... | collective-permute-start | bytes 3145736 | tf_op jit(solution)/shard_map/ppermute | solution.py:353
  181.9 50.3 %collective-permute-start.33 = (bf16[1024,1024]{1,0:T(8,128)(2,1)S(1)}, bf16[1024,1024]{1,0:T(8,128)(2,1)}, u32[]{:S(2)}, u32[]{:S(2)}) collective-permute-start(bf16[1024,1024]{1,0:T(8,128)(2,1)S(1)} %shard_map.316.refs_4_.refs_0_), channel_id=1, source_target_pairs={{0,1},{1,2},{2,3},{3,0},{4,5},{5,6},{6,7},{7,4},{8,9},{9,10},{10,1... | collective-permute-start | bytes 6291464 | tf_op jit(solution)/shard_map/ppermute | solution.py:358
  186.9 45.4 %collective-permute-start.42 = (bf16[256,1024]{1,0:T(8,128)(2,1)}, bf16[256,1024]{1,0:T(8,128)(2,1)}, u32[]{:S(2)}, u32[]{:S(2)}) collective-permute-start(bf16[256,1024]{1,0:T(8,128)(2,1)} %slice.338), channel_id=1, source_target_pairs={{0,8},{8,0},{16,24},{24,16},{1,9},{9,1},{17,25},{25,17},{2,10},{10... | collective-permute-start | bytes 1572872 | tf_op jit(solution)/shard_map/ppermute | solution.py:349
  188.2 44.0 %collective-permute-start.40 = (bf16[256,1024]{1,0:T(8,128)(2,1)}, bf16[256,1024]{1,0:T(8,128)(2,1)}, u32[]{:S(2)}, u32[]{:S(2)}) collective-permute-start(bf16[256,1024]{1,0:T(8,128)(2,1)} %slice.336), channel_id=1, source_target_pairs={{0,16},{16,0},{8,24},{24,8},{1,17},{17,1},{9,25},{25,9},{2,18},{18... | collective-permute-start | bytes 1572872 | tf_op jit(solution)/shard_map/ppermute | solution.py:353
  209.6 24.6 %collective-permute-start.29 = (bf16[1024,256]{1,0:T(8,128)(2,1)S(1)}, bf16[1024,256]{1,0:T(8,128)(2,1)}, u32[]{:S(2)}, u32[]{:S(2)}) collective-permute-start(bf16[1024,256]{1,0:T(8,128)(2,1)S(1)} %shard_map.329.refs_0_.refs_5_), channel_id=1, source_target_pairs={{0,4},{4,0},{1,5},{5,1},{2,6},{6,2},{3,7},{7,3},{8,12},{12,8},{9,1... | collective-permute-start | bytes 1572872 | tf_op jit(solution)/shard_map/ppermute | solution.py:345
  232.2 49.3 %collective-permute-start.34 = (bf16[1024,1024]{1,0:T(8,128)(2,1)}, bf16[1024,1024]{1,0:T(8,128)(2,1)S(1)}, u32[]{:S(2)}, u32[]{:S(2)}) collective-permute-start(bf16[1024,1024]{1,0:T(8,128)(2,1)} %collective-permute-done.33.refs_5_.refs_1_), channel_id=1, source_target_pairs={{0,1},{1,2},{2,3},{3,0},{4,5},{5,6},{6,7},{7,4},{8,9},{9,10},{10,1... | collective-permute-start | bytes 6291464 | tf_op jit(solution)/shard_map/ppermute | solution.py:358
  232.2 25.2 %collective-permute-start.41 = (bf16[512,1024]{1,0:T(8,128)(2,1)}, bf16[512,1024]{1,0:T(8,128)(2,1)}, u32[]{:S(2)}, u32[]{:S(2)}) collective-permute-start(bf16[512,1024]{1,0:T(8,128)(2,1)} %get-tuple-element.310), channel_id=1, source_target_pairs={{0,16},{16,0},{8,24},{24,8},{1,17},{17,1},{9,25},{25,9},{2,18},{18... | collective-permute-start | bytes 3145736 | tf_op jit(solution)/shard_map/ppermute | solution.py:353
  232.8 25.7 %collective-permute-start.43 = (bf16[512,1024]{1,0:T(8,128)(2,1)}, bf16[512,1024]{1,0:T(8,128)(2,1)}, u32[]{:S(2)}, u32[]{:S(2)}) collective-permute-start(bf16[512,1024]{1,0:T(8,128)(2,1)} %get-tuple-element.310), channel_id=1, source_target_pairs={{0,8},{8,0},{16,24},{24,16},{1,9},{9,1},{17,25},{25,17},{2,10},{10... | collective-permute-start | bytes 3145736 | tf_op jit(solution)/shard_map/ppermute | solution.py:349
  271.2 45.5 %collective-permute-start.45 = (bf16[1024,1024]{1,0:T(8,128)(2,1)S(1)}, bf16[1024,1024]{1,0:T(8,128)(2,1)S(1)}, u32[]{:S(2)}, u32[]{:S(2)}) collective-permute-start(bf16[1024,1024]{1,0:T(8,128)(2,1)S(1)} %add_convert_fusion.3.refs_0_), channel_id=1, source_target_pairs={{0,8},{8,0},{16,24},{24,16},{1,9},{9,1},{17,25},{25,17},{2,10},{10... | collective-permute-start | bytes 6291464 | tf_op jit(solution)/shard_map/ppermute | solution.py:349
  281.5 48.3 %collective-permute-start.35 = (bf16[1024,1024]{1,0:T(8,128)(2,1)S(1)}, bf16[1024,1024]{1,0:T(8,128)(2,1)S(1)}, u32[]{:S(2)}, u32[]{:S(2)}) collective-permute-start(bf16[1024,1024]{1,0:T(8,128)(2,1)S(1)} %collective-permute-done.34.refs_6_.refs_2_), channel_id=1, source_target_pairs={{0,1},{1,2},{2,3},{3,0},{4,5},{5,6},{6,7},{7,4},{8,9},{9,10},{10,1... | collective-permute-start | bytes 6291464 | tf_op jit(solution)/shard_map/ppermute | solution.py:358
  281.7 50.5 %collective-permute-start.32 = (bf16[1024,1024]{1,0:T(8,128)(2,1)S(1)}, bf16[1024,1024]{1,0:T(8,128)(2,1)S(1)}, u32[]{:S(2)}, u32[]{:S(2)}) collective-permute-start(bf16[1024,1024]{1,0:T(8,128)(2,1)S(1)} %copy-done.80), channel_id=1, source_target_pairs={{0,4},{4,0},{1,5},{5,1},{2,6},{6,2},{3,7},{7,3},{8,12},{12,8},{9,1... | collective-permute-start | bytes 6291464 | tf_op jit(solution)/shard_map/ppermute | solution.py:345
  281.7 51.4 %collective-permute-start.31 = (bf16[1024,1024]{1,0:T(8,128)(2,1)S(1)}, bf16[1024,1024]{1,0:T(8,128)(2,1)S(1)}, u32[]{:S(2)}, u32[]{:S(2)}) collective-permute-start(bf16[1024,1024]{1,0:T(8,128)(2,1)S(1)} %add_convert_fusion.3.refs_0_), channel_id=1, source_target_pairs={{0,4},{4,0},{1,5},{5,1},{2,6},{6,2},{3,7},{7,3},{8,12},{12,8},{9,1... | collective-permute-start | bytes 6291464 | tf_op jit(solution)/shard_map/ppermute | solution.py:345
  290.4 41.8 %collective-permute-start.46 = (bf16[256,1024]{1,0:T(8,128)(2,1)S(1)}, bf16[256,1024]{1,0:T(8,128)(2,1)S(1)}, u32[]{:S(2)}, u32[]{:S(2)}) collective-permute-start(bf16[256,1024]{1,0:T(8,128)(2,1)S(1)} %slice.428), channel_id=1, source_target_pairs={{0,16},{16,0},{8,24},{24,8},{1,17},{17,1},{9,25},{25,9},{2,18},{18... | collective-permute-start | bytes 1572872 | tf_op jit(solution)/shard_map/ppermute | solution.py:353
  316.7 37.2 %collective-permute-start.51 = (bf16[1024,1024]{1,0:T(8,128)(2,1)S(1)}, bf16[1024,1024]{1,0:T(8,128)(2,1)}, u32[]{:S(2)}, u32[]{:S(2)}) collective-permute-start(bf16[1024,1024]{1,0:T(8,128)(2,1)S(1)} %collective-permute-done.45.refs_0_.refs_1_), channel_id=1, source_target_pairs={{0,4},{4,0},{1,5},{5,1},{2,6},{6,2},{3,7},{7,3},{8,12},{12,8},{9,1... | collective-permute-start | bytes 6291464 | tf_op jit(solution)/shard_map/ppermute | solution.py:345
  335.5 47.7 %collective-permute-start.47 = (bf16[1024,1024]{1,0:T(8,128)(2,1)S(1)}, bf16[1024,1024]{1,0:T(8,128)(2,1)S(1)}, u32[]{:S(2)}, u32[]{:S(2)}) collective-permute-start(bf16[1024,1024]{1,0:T(8,128)(2,1)S(1)} %add_convert_fusion.3.refs_0_), channel_id=1, source_target_pairs={{0,16},{16,0},{8,24},{24,8},{1,17},{17,1},{9,25},{25,9},{2,18},{18... | collective-permute-start | bytes 6291464 | tf_op jit(solution)/shard_map/ppermute | solution.py:353
  369.4 58.3 %collective-permute-start.55 = (bf16[1024,2048]{1,0:T(8,128)(2,1)}, bf16[1024,2048]{1,0:T(8,128)(2,1)S(1)}, u32[]{:S(2)}, u32[]{:S(2)}) collective-permute-start(bf16[1024,2048]{1,0:T(8,128)(2,1)} %get-tuple-element.330.own_ref.refs_9_.refs_13_), channel_id=1, source_target_pairs={{0,4},{4,0},{1,5},{5,1},{2,6},{6,2},{3,7},{7,3},{8,12},{12,8},{9,1... | collective-permute-start | bytes 12582920 | tf_op jit(solution)/shard_map/ppermute | solution.py:345
  383.1 24.4 %collective-permute-start.48 = (bf16[512,1024]{1,0:T(8,128)(2,1)S(1)}, bf16[512,1024]{1,0:T(8,128)(2,1)S(1)}, u32[]{:S(2)}, u32[]{:S(2)}) collective-permute-start(bf16[512,1024]{1,0:T(8,128)(2,1)S(1)} %slice.429), channel_id=1, source_target_pairs={{0,16},{16,0},{8,24},{24,8},{1,17},{17,1},{9,25},{25,9},{2,18},{18... | collective-permute-start | bytes 3145736 | tf_op jit(solution)/shard_map/ppermute | solution.py:353
  383.8 24.8 %collective-permute-start.49 = (bf16[512,1024]{1,0:T(8,128)(2,1)S(1)}, bf16[512,1024]{1,0:T(8,128)(2,1)S(1)}, u32[]{:S(2)}, u32[]{:S(2)}) collective-permute-start(bf16[512,1024]{1,0:T(8,128)(2,1)S(1)} %slice.430), channel_id=1, source_target_pairs={{0,8},{8,0},{16,24},{24,16},{1,9},{9,1},{17,25},{25,17},{2,10},{10... | collective-permute-start | bytes 3145736 | tf_op jit(solution)/shard_map/ppermute | solution.py:349
  385.3 25.7 %collective-permute-start.53 = (bf16[1024,1024]{1,0:T(8,128)(2,1)S(1)}, bf16[1024,1024]{1,0:T(8,128)(2,1)S(1)}, u32[]{:S(2)}, u32[]{:S(2)}) collective-permute-start(bf16[1024,1024]{1,0:T(8,128)(2,1)S(1)} %collective-permute-done.47.refs_0_.refs_2_), channel_id=1, source_target_pairs={{0,4},{4,0},{1,5},{5,1},{2,6},{6,2},{3,7},{7,3},{8,12},{12,8},{9,1... | collective-permute-start | bytes 6291464 | tf_op jit(solution)/shard_map/ppermute | solution.py:345
  386.6 25.7 %collective-permute-start.54 = (bf16[1024,1024]{1,0:T(8,128)(2,1)S(1)}, bf16[1024,1024]{1,0:T(8,128)(2,1)}, u32[]{:S(2)}, u32[]{:S(2)}) collective-permute-start(bf16[1024,1024]{1,0:T(8,128)(2,1)S(1)} %constant_dynamic-update-slice_fusion.4.refs_2_.refs_6_), channel_id=1, source_target_pairs={{0,4},{4,0},{1,5},{5,1},{2,6},{6,2},{3,7},{7,3},{8,12},{12,8},{9,1... | collective-permute-start | bytes 6291464 | tf_op jit(solution)/shard_map/ppermute | solution.py:345
  409.6 27.7 %collective-permute-start.50 = (bf16[1024,1024]{1,0:T(8,128)(2,1)}, bf16[1024,1024]{1,0:T(8,128)(2,1)}, u32[]{:S(2)}, u32[]{:S(2)}) collective-permute-start(bf16[1024,1024]{1,0:T(8,128)(2,1)} %constant_dynamic-update-slice_fusion.refs_0_.refs_3_), channel_id=1, source_target_pairs={{0,4},{4,0},{1,5},{5,1},{2,6},{6,2},{3,7},{7,3},{8,12},{12,8},{9,1... | collective-permute-start | bytes 6291464 | tf_op jit(solution)/shard_map/ppermute | solution.py:345
  410.5 26.8 %collective-permute-start.56 = (bf16[1024,1024]{1,0:T(8,128)(2,1)}, bf16[1024,1024]{1,0:T(8,128)(2,1)}, u32[]{:S(2)}, u32[]{:S(2)}) collective-permute-start(bf16[1024,1024]{1,0:T(8,128)(2,1)} %constant_dynamic-update-slice_fusion.6.refs_2_.refs_7_), channel_id=1, source_target_pairs={{0,4},{4,0},{1,5},{5,1},{2,6},{6,2},{3,7},{7,3},{8,12},{12,8},{9,1... | collective-permute-start | bytes 6291464 | tf_op jit(solution)/shard_map/ppermute | solution.py:345
  427.7 28.8 %collective-permute-start.57 = (bf16[1024,2048]{1,0:T(8,128)(2,1)}, bf16[1024,2048]{1,0:T(8,128)(2,1)}, u32[]{:S(2)}, u32[]{:S(2)}) collective-permute-start(bf16[1024,2048]{1,0:T(8,128)(2,1)} %get-tuple-element.331.own_ref.refs_10_.refs_14_), channel_id=1, source_target_pairs={{0,4},{4,0},{1,5},{5,1},{2,6},{6,2},{3,7},{7,3},{8,12},{12,8},{9,1... | collective-permute-start | bytes 12582920 | tf_op jit(solution)/shard_map/ppermute | solution.py:345
  453.9 39.7 %collective-permute-start.59 = (bf16[1024,2048]{1,0:T(8,128)(2,1)}, bf16[1024,2048]{1,0:T(8,128)(2,1)}, u32[]{:S(2)}, u32[]{:S(2)}) collective-permute-start(bf16[1024,2048]{1,0:T(8,128)(2,1)} %get-tuple-element.345.own_ref.refs_8_.refs_12_), channel_id=1, source_target_pairs={{0,4},{4,0},{1,5},{5,1},{2,6},{6,2},{3,7},{7,3},{8,12},{12,8},{9,1... | collective-permute-start | bytes 12582920 | tf_op jit(solution)/shard_map/ppermute | solution.py:345
  455.1 36.9 %collective-permute-start.60 = (bf16[512,1024]{1,0:T(8,128)(2,1)}, bf16[512,1024]{1,0:T(8,128)(2,1)}, u32[]{:S(2)}, u32[]{:S(2)}) collective-permute-start(bf16[512,1024]{1,0:T(8,128)(2,1)} %slice.433), channel_id=1, source_target_pairs={{0,8},{8,0},{16,24},{24,16},{1,9},{9,1},{17,25},{25,17},{2,10},{10... | collective-permute-start | bytes 3145736 | tf_op jit(solution)/shard_map/ppermute | solution.py:349
  466.5 25.5 %collective-permute-start.62 = (bf16[512,1024]{1,0:T(8,128)(2,1)}, bf16[512,1024]{1,0:T(8,128)(2,1)}, u32[]{:S(2)}, u32[]{:S(2)}) collective-permute-start(bf16[512,1024]{1,0:T(8,128)(2,1)} %slice.435), channel_id=1, source_target_pairs={{0,16},{16,0},{8,24},{24,8},{1,17},{17,1},{9,25},{25,9},{2,18},{18... | collective-permute-start | bytes 3145736 | tf_op jit(solution)/shard_map/ppermute | solution.py:353
  492.1 35.7 %collective-permute-start.61 = (bf16[512,1024]{1,0:T(8,128)(2,1)S(1)}, bf16[512,1024]{1,0:T(8,128)(2,1)S(1)}, u32[]{:S(2)}, u32[]{:S(2)}) collective-permute-start(bf16[512,1024]{1,0:T(8,128)(2,1)S(1)} %get-tuple-element.334), channel_id=1, source_target_pairs={{0,8},{8,0},{16,24},{24,16},{1,9},{9,1},{17,25},{25,17},{2,10},{10... | collective-permute-start | bytes 3145736 | tf_op jit(solution)/shard_map/ppermute | solution.py:349
  492.7 35.1 %collective-permute-start.63 = (bf16[512,1024]{1,0:T(8,128)(2,1)S(1)}, bf16[512,1024]{1,0:T(8,128)(2,1)}, u32[]{:S(2)}, u32[]{:S(2)}) collective-permute-start(bf16[512,1024]{1,0:T(8,128)(2,1)S(1)} %get-tuple-element.336), channel_id=1, source_target_pairs={{0,16},{16,0},{8,24},{24,8},{1,17},{17,1},{9,25},{25,9},{2,18},{18... | collective-permute-start | bytes 3145736 | tf_op jit(solution)/shard_map/ppermute | solution.py:353
  531.2 26.0 %collective-permute-start.64 = (bf16[512,1024]{1,0:T(8,128)(2,1)}, bf16[512,1024]{1,0:T(8,128)(2,1)S(1)}, u32[]{:S(2)}, u32[]{:S(2)}) collective-permute-start(bf16[512,1024]{1,0:T(8,128)(2,1)} %get-tuple-element.338), channel_id=1, source_target_pairs={{0,8},{8,0},{16,24},{24,16},{1,9},{9,1},{17,25},{25,17},{2,10},{10... | collective-permute-start | bytes 3145736 | tf_op jit(solution)/shard_map/ppermute | solution.py:349
  532.6 24.6 %collective-permute-start.67 = (bf16[512,1024]{1,0:T(8,128)(2,1)S(1)}, bf16[512,1024]{1,0:T(8,128)(2,1)S(1)}, u32[]{:S(2)}, u32[]{:S(2)}) collective-permute-start(bf16[512,1024]{1,0:T(8,128)(2,1)S(1)} %get-tuple-element.340), channel_id=1, source_target_pairs={{0,16},{16,0},{8,24},{24,8},{1,17},{17,1},{9,25},{25,9},{2,18},{18... | collective-permute-start | bytes 3145736 | tf_op jit(solution)/shard_map/ppermute | solution.py:353
  571.6 31.7 %collective-permute-start.71 = (bf16[1024,1024]{1,0:T(8,128)(2,1)}, bf16[1024,1024]{1,0:T(8,128)(2,1)}, u32[]{:S(2)}, u32[]{:S(2)}) collective-permute-start(bf16[1024,1024]{1,0:T(8,128)(2,1)} %pad_maximum_fusion.2.own_ref.refs_2_), channel_id=1, source_target_pairs={{0,4},{4,0},{1,5},{5,1},{2,6},{6,2},{3,7},{7,3},{8,12},{12,8},{9,1... | collective-permute-start | bytes 6291464 | tf_op jit(solution)/shard_map/ppermute | solution.py:345
  574.4 25.5 %collective-permute-start.65 = (bf16[512,1024]{1,0:T(8,128)(2,1)S(1)}, bf16[512,1024]{1,0:T(8,128)(2,1)S(1)}, u32[]{:S(2)}, u32[]{:S(2)}) collective-permute-start(bf16[512,1024]{1,0:T(8,128)(2,1)S(1)} %slice.438), channel_id=1, source_target_pairs={{0,8},{8,0},{16,24},{24,16},{1,9},{9,1},{17,25},{25,17},{2,10},{10... | collective-permute-start | bytes 3145736 | tf_op jit(solution)/shard_map/ppermute | solution.py:349
  575.1 24.9 %collective-permute-start.68 = (bf16[512,1024]{1,0:T(8,128)(2,1)S(1)}, bf16[512,1024]{1,0:T(8,128)(2,1)S(1)}, u32[]{:S(2)}, u32[]{:S(2)}) collective-permute-start(bf16[512,1024]{1,0:T(8,128)(2,1)S(1)} %slice.442), channel_id=1, source_target_pairs={{0,16},{16,0},{8,24},{24,8},{1,17},{17,1},{9,25},{25,9},{2,18},{18... | collective-permute-start | bytes 3145736 | tf_op jit(solution)/shard_map/ppermute | solution.py:353
  577.5 55.0 %collective-permute-start.94 = (bf16[1024,1024]{1,0:T(8,128)(2,1)}, bf16[1024,1024]{1,0:T(8,128)(2,1)S(1)}, u32[]{:S(2)}, u32[]{:S(2)}) collective-permute-start(bf16[1024,1024]{1,0:T(8,128)(2,1)} %shard_map.342), channel_id=1, source_target_pairs={{0,3},{1,0},{2,1},{3,2},{4,7},{5,4},{6,5},{7,6},{8,11},{9,8},{10,9... | collective-permute-start | bytes 6291464 | tf_op jit(solution)/shard_map/ppermute | solution.py:363
  601.0 81.2 %collective-permute-start.66 = (bf16[512,1024]{1,0:T(8,128)(2,1)}, bf16[512,1024]{1,0:T(8,128)(2,1)S(1)}, u32[]{:S(2)}, u32[]{:S(2)}) collective-permute-start(bf16[512,1024]{1,0:T(8,128)(2,1)} %get-tuple-element.347), channel_id=1, source_target_pairs={{0,8},{8,0},{16,24},{24,16},{1,9},{9,1},{17,25},{25,17},{2,10},{10... | collective-permute-start | bytes 3145736 | tf_op jit(solution)/shard_map/ppermute | solution.py:349
  602.4 79.8 %collective-permute-start.69 = (bf16[512,1024]{1,0:T(8,128)(2,1)}, bf16[512,1024]{1,0:T(8,128)(2,1)}, u32[]{:S(2)}, u32[]{:S(2)}) collective-permute-start(bf16[512,1024]{1,0:T(8,128)(2,1)} %get-tuple-element.349), channel_id=1, source_target_pairs={{0,16},{16,0},{8,24},{24,8},{1,17},{17,1},{9,25},{25,9},{2,18},{18... | collective-permute-start | bytes 3145736 | tf_op jit(solution)/shard_map/ppermute | solution.py:353
  647.9 168.8 %collective-permute-start.95 = (bf16[1024,1024]{1,0:T(8,128)(2,1)}, bf16[1024,1024]{1,0:T(8,128)(2,1)}, u32[]{:S(2)}, u32[]{:S(2)}) collective-permute-start(bf16[1024,1024]{1,0:T(8,128)(2,1)} %add_convert_fusion.2), channel_id=1, source_target_pairs={{0,3},{1,0},{2,1},{3,2},{4,7},{5,4},{6,5},{7,6},{8,11},{9,8},{10,9... | collective-permute-start | bytes 6291464 | tf_op jit(solution)/shard_map/ppermute | solution.py:363
  647.9 119.4 %collective-permute-start.78 = (bf16[1024,1024]{1,0:T(8,128)(2,1)}, bf16[1024,1024]{1,0:T(8,128)(2,1)}, u32[]{:S(2)}, u32[]{:S(2)}) collective-permute-start(bf16[1024,1024]{1,0:T(8,128)(2,1)} %get-tuple-element.401), channel_id=1, source_target_pairs={{0,4},{4,0},{1,5},{5,1},{2,6},{6,2},{3,7},{7,3},{8,12},{12,8},{9,1... | collective-permute-start | bytes 6291464 | tf_op jit(solution)/shard_map/ppermute | solution.py:345
  687.2 77.2 %collective-permute-start.73 = (bf16[512,1024]{1,0:T(8,128)(2,1)}, bf16[512,1024]{1,0:T(8,128)(2,1)S(1)}, u32[]{:S(2)}, u32[]{:S(2)}) collective-permute-start(bf16[512,1024]{1,0:T(8,128)(2,1)} %add_convert_fusion.8), channel_id=1, source_target_pairs={{0,8},{8,0},{16,24},{24,16},{1,9},{9,1},{17,25},{25,17},{2,10},{10... | collective-permute-start | bytes 3145736 | tf_op jit(solution)/shard_map/ppermute | solution.py:349
  687.7 81.1 %collective-permute-start.72 = (bf16[512,1024]{1,0:T(8,128)(2,1)}, bf16[512,1024]{1,0:T(8,128)(2,1)}, u32[]{:S(2)}, u32[]{:S(2)}) collective-permute-start(bf16[512,1024]{1,0:T(8,128)(2,1)} %add_convert_fusion.9), channel_id=1, source_target_pairs={{0,16},{16,0},{8,24},{24,8},{1,17},{17,1},{9,25},{25,9},{2,18},{18... | collective-permute-start | bytes 3145736 | tf_op jit(solution)/shard_map/ppermute | solution.py:353
  712.5 53.3 %collective-permute-start.76 = (f32[4,3584]{1,0:T(4,128)S(1)}, f32[4,3584]{1,0:T(4,128)S(1)}, u32[]{:S(2)}, u32[]{:S(2)}) collective-permute-start(f32[4,3584]{1,0:T(4,128)S(1)} %pad_maximum_fusion.11), channel_id=1, source_target_pairs={{0,4},{4,0},{1,5},{5,1},{2,6},{6,2},{3,7},{7,3},{8,12},{12,8},{9,1... | collective-permute-start | bytes 172040 | tf_op jit(solution)/shard_map/ppermute | solution.py:345
  784.6 26.2 %collective-permute-start.84 = (bf16[256,2048]{1,0:T(8,128)(2,1)S(1)}, bf16[256,2048]{1,0:T(8,128)(2,1)}, u32[]{:S(2)}, u32[]{:S(2)}) collective-permute-start(bf16[256,2048]{1,0:T(8,128)(2,1)S(1)} %pad_maximum_fusion.5), channel_id=1, source_target_pairs={{0,16},{16,0},{8,24},{24,8},{1,17},{17,1},{9,25},{25,9},{2,18},{18... | collective-permute-start | bytes 3145736 | tf_op jit(solution)/shard_map/ppermute | solution.py:353
  785.6 24.6 %collective-permute-start.81 = (bf16[256,2048]{1,0:T(8,128)(2,1)S(1)}, bf16[256,2048]{1,0:T(8,128)(2,1)}, u32[]{:S(2)}, u32[]{:S(2)}) collective-permute-start(bf16[256,2048]{1,0:T(8,128)(2,1)S(1)} %pad_maximum_fusion.3), channel_id=1, source_target_pairs={{0,8},{8,0},{16,24},{24,16},{1,9},{9,1},{17,25},{25,17},{2,10},{10... | collective-permute-start | bytes 3145736 | tf_op jit(solution)/shard_map/ppermute | solution.py:349
  789.3 39.3 %collective-permute-start.77 = (bf16[1024,1024]{1,0:T(8,128)(2,1)}, bf16[1024,1024]{1,0:T(8,128)(2,1)S(1)}, u32[]{:S(2)}, u32[]{:S(2)}) collective-permute-start(bf16[1024,1024]{1,0:T(8,128)(2,1)} %get-tuple-element.400), channel_id=1, source_target_pairs={{0,4},{4,0},{1,5},{5,1},{2,6},{6,2},{3,7},{7,3},{8,12},{12,8},{9,1... | collective-permute-start | bytes 6291464 | tf_op jit(solution)/shard_map/ppermute | solution.py:345
  828.5 54.9 %collective-permute-start.96 = (bf16[1024,1024]{1,0:T(8,128)(2,1)S(1)}, bf16[1024,1024]{1,0:T(8,128)(2,1)S(1)}, u32[]{:S(2)}, u32[]{:S(2)}) collective-permute-start(bf16[1024,1024]{1,0:T(8,128)(2,1)S(1)} %add_convert_fusion.1), channel_id=1, source_target_pairs={{0,3},{1,0},{2,1},{3,2},{4,7},{5,4},{6,5},{7,6},{8,11},{9,8},{10,9... | collective-permute-start | bytes 6291464 | tf_op jit(solution)/shard_map/ppermute | solution.py:363
  860.9 27.4 %collective-permute-start.92 = (bf16[256,2048]{1,0:T(8,128)(2,1)S(1)}, bf16[256,2048]{1,0:T(8,128)(2,1)S(1)}, u32[]{:S(2)}, u32[]{:S(2)}) collective-permute-start(bf16[256,2048]{1,0:T(8,128)(2,1)S(1)} %pad_maximum_fusion.8), channel_id=1, source_target_pairs={{0,16},{16,0},{8,24},{24,8},{1,17},{17,1},{9,25},{25,9},{2,18},{18... | collective-permute-start | bytes 3145736 | tf_op jit(solution)/shard_map/ppermute | solution.py:353
  890.6 42.5 %collective-permute-start.103 = (bf16[1024,1024]{1,0:T(8,128)(2,1)S(1)}, bf16[1024,1024]{1,0:T(8,128)(2,1)S(1)}, u32[]{:S(2)}, u32[]{:S(2)}) collective-permute-start(bf16[1024,1024]{1,0:T(8,128)(2,1)S(1)} %add_convert_fusion.refs_0_), channel_id=1, source_target_pairs={{0,8},{8,0},{16,24},{24,16},{1,9},{9,1},{17,25},{25,17},{2,10},{10... | collective-permute-start | bytes 6291464 | tf_op jit(solution)/shard_map/ppermute | solution.py:349
  893.7 42.6 %collective-permute-start.104 = (bf16[1024,1024]{1,0:T(8,128)(2,1)S(1)}, bf16[1024,1024]{1,0:T(8,128)(2,1)S(1)}, u32[]{:S(2)}, u32[]{:S(2)}) collective-permute-start(bf16[1024,1024]{1,0:T(8,128)(2,1)S(1)} %add_convert_fusion.refs_0_), channel_id=1, source_target_pairs={{0,16},{16,0},{8,24},{24,8},{1,17},{17,1},{9,25},{25,9},{2,18},{18... | collective-permute-start | bytes 6291464 | tf_op jit(solution)/shard_map/ppermute | solution.py:353
  897.2 42.5 %collective-permute-start.97 = (bf16[256,2048]{1,0:T(8,128)(2,1)S(1)}, bf16[256,2048]{1,0:T(8,128)(2,1)S(1)}, u32[]{:S(2)}, u32[]{:S(2)}) collective-permute-start(bf16[256,2048]{1,0:T(8,128)(2,1)S(1)} %add_convert_fusion.7), channel_id=1, source_target_pairs={{0,3},{1,0},{2,1},{3,2},{4,7},{5,4},{6,5},{7,6},{8,11},{9,8},{10,9... | collective-permute-start | bytes 3145736 | tf_op jit(solution)/shard_map/ppermute | solution.py:363
  897.3 44.2 %collective-permute-start.102 = (bf16[1024,1024]{1,0:T(8,128)(2,1)S(1)}, bf16[1024,1024]{1,0:T(8,128)(2,1)S(1)}, u32[]{:S(2)}, u32[]{:S(2)}) collective-permute-start(bf16[1024,1024]{1,0:T(8,128)(2,1)S(1)} %copy-done.136), channel_id=1, source_target_pairs={{0,4},{4,0},{1,5},{5,1},{2,6},{6,2},{3,7},{7,3},{8,12},{12,8},{9,1... | collective-permute-start | bytes 6291464 | tf_op jit(solution)/shard_map/ppermute | solution.py:345
  1025.1 25.6 %collective-permute-start.114 = (bf16[128,2048]{1,0:T(8,128)(2,1)}, bf16[128,2048]{1,0:T(8,128)(2,1)}, u32[]{:S(2)}, u32[]{:S(2)}) collective-permute-start(bf16[128,2048]{1,0:T(8,128)(2,1)} %slice.472), channel_id=1, source_target_pairs={{0,8},{8,0},{16,24},{24,16},{1,9},{9,1},{17,25},{25,17},{2,10},{10... | collective-permute-start | bytes 1572872 | tf_op jit(solution)/shard_map/ppermute | solution.py:349
  1026.2 24.5 %collective-permute-start.113 = (bf16[128,2048]{1,0:T(8,128)(2,1)}, bf16[128,2048]{1,0:T(8,128)(2,1)}, u32[]{:S(2)}, u32[]{:S(2)}) collective-permute-start(bf16[128,2048]{1,0:T(8,128)(2,1)} %slice.471), channel_id=1, source_target_pairs={{0,16},{16,0},{8,24},{24,8},{1,17},{17,1},{9,25},{25,9},{2,18},{18... | collective-permute-start | bytes 1572872 | tf_op jit(solution)/shard_map/ppermute | solution.py:353
  (191 other events, 2729.7 us)

commit v5 on v0

--- a/solution.py
+++ b/solution.py
@@ -1,6 +1,10 @@
+import functools
+
 import jax
 import jax.numpy as jnp
 from jax import lax
+from jax.experimental import pallas as pl
+from jax.experimental.pallas import tpu as pltpu
 from jax.sharding import PartitionSpec as P
 
 D = 2048
@@ -139,7 +143,7 @@
     return (jnp.concatenate(query_grads, axis=2), key_grad, value_grad)
 
 
-def body(
+def body_general(
     tokens_in,
     out_grad,
     segment_ids,
@@ -333,6 +337,1282 @@
     )
 
 
+def after(values, *others):
+    return lax.optimization_barrier((values, others))[0]
+
+
+def swap(values):
+    return lax.ppermute(values, "row", [(0, 1), (1, 0)])
+
+
+def step_x(values):
+    return lax.ppermute(values, "dp", [(0, 1), (1, 0), (2, 3), (3, 2)])
+
+
+def step_y(values):
+    return lax.ppermute(values, "dp", [(0, 2), (2, 0), (1, 3), (3, 1)])
+
+
+def step_up(values):
+    count = lax.axis_size("col")
+    return lax.ppermute(values, "col", [(i, (i + 1) % count) for i in range(count)])
+
+
+def step_down(values):
+    count = lax.axis_size("col")
+    return lax.ppermute(values, "col", [(i, (i - 1) % count) for i in range(count)])
+
+
+class Order:
+    def __init__(self):
+        self.tokens = []
+        self.fresh, self.due = [], []
+
+    def tie(self, values):
+        if self.tokens:
+            values = after(values, *self.tokens)
+        self.tokens.append(values)
+        return values
+
+    def swap(self, values, due=True):
+        arrived = swap(self.tie(values))
+        if due:
+            self.fresh.append(arrived)
+        return arrived
+
+    def run(self, function, first, *others):
+        first = after(first, *self.tokens, *self.due) if self.tokens or self.due else first
+        self.due, self.fresh = self.fresh, []
+        result = function(first, *others)
+        self.tokens = [jax.tree.leaves(result)[0]]
+        return result
+
+
+class Link:
+    def __init__(self, order):
+        self.order = order
+        self.last = None
+
+    def send(self, step, values, free=False):
+        if self.last is not None and not free:
+            values = after(values, self.last)
+        self.last = step(self.order.tie(values))
+        return self.last
+
+
+class Plane:
+    def __init__(self, order):
+        self.x = Link(order)
+        self.y = Link(order)
+
+    def both(self, for_x, for_y, free=False):
+        return self.x.send(step_x, for_x, free), self.y.send(step_y, for_y, free)
+
+    def far(self, from_x, from_y):
+        half = from_x.shape[0] // 2
+        far_two, far_one = self.both(from_y[half:], from_x[:half])
+        return far_one, far_two
+
+
+def add_rounded(left, right):
+    return (left.astype(jnp.float32) + right.astype(jnp.float32)).astype(jnp.bfloat16)
+
+
+def ring_gather(link, values):
+    held = [values]
+    for _ in range(lax.axis_size("col") - 1):
+        held.append(link.send(step_up, held[-1]))
+    return held
+
+
+def picked(stacked, index):
+    return lax.dynamic_index_in_dim(stacked, index, 0, keepdims=False)
+
+
+def mm(left, right, left_dim, right_dim, dtype=jnp.float32):
+    return lax.dot_general(
+        left, right, (((left_dim,), (right_dim,)), ((), ())), preferred_element_type=jnp.float32
+    ).astype(dtype)
+
+
+PAIR = 2 * HEAD_DIM
+vmem_bytes = 48 * 1024 * 1024
+
+
+def head_lanes(head, value):
+    lane = lax.broadcasted_iota(jnp.int32, (1, PAIR), 1)
+    return jnp.where(lane // HEAD_DIM == head, value, 0.0).astype(jnp.bfloat16)
+
+
+def allowed_keys(first_row, low, high):
+    key_pos = lax.broadcasted_iota(jnp.int32, (high, high - low), 0)
+    query_pos = lax.broadcasted_iota(jnp.int32, (high, high - low), 1) + low
+    return (key_pos >= first_row) & (key_pos <= query_pos)
+
+
+def local_forward_kernel(size, first_ref, query_ref, key_ref, value_ref, out_ref):
+    lane = lax.broadcasted_iota(jnp.int32, (size, PAIR), 1)
+    for low in range(0, key_ref.shape[0], size):
+        high = low + size
+        keys = key_ref[:high, :]
+        values = value_ref[:high, :]
+        queries = query_ref[low:high, :]
+        allowed = allowed_keys(first_ref[:, low:high], low, high)
+        results = []
+        for head in range(2):
+            scores = mm(keys, queries * head_lanes(head, HEAD_DIM ** (-0.5)), 1, 1)
+            scores = jnp.where(allowed, scores, masked_fill)
+            exp_scores = jnp.exp(scores - jnp.max(scores, axis=0, keepdims=True))
+            inverse = 1.0 / jnp.sum(exp_scores, axis=0, keepdims=True)
+            results.append(mm((exp_scores * inverse).astype(jnp.bfloat16), values, 0, 0))
+        out_ref[low:high, :] = jnp.where(lane < HEAD_DIM, results[0], results[1]).astype(
+            jnp.bfloat16
+        )
+
+
+def local_forward(heads, first_row):
+    length = heads.shape[0]
+    pairs = heads.shape[1] // (3 * PAIR)
+    return pl.pallas_call(
+        functools.partial(local_forward_kernel, min(256, length)),
+        grid=(pairs,),
+        in_specs=[
+            pl.BlockSpec((1, length), lambda p: (0, 0)),
+            pl.BlockSpec((length, PAIR), lambda p: (0, p)),
+            pl.BlockSpec((length, PAIR), lambda p: (0, pairs + p)),
+            pl.BlockSpec((length, PAIR), lambda p: (0, 2 * pairs + p)),
+        ],
+        out_specs=pl.BlockSpec((length, PAIR), lambda p: (0, p)),
+        out_shape=jax.ShapeDtypeStruct((length, pairs * PAIR), jnp.bfloat16),
+        compiler_params=pltpu.CompilerParams(vmem_limit_bytes=vmem_bytes),
+        cost_estimate=cost(16 * length * length * pairs * PAIR, 8 * heads.size),
+    )(first_row, heads, heads, heads)
+
+
+def local_backward_kernel(
+    size, first_ref, query_ref, grad_ref, key_ref, value_ref, out_ref, key_sum, value_sum
+):
+    length = key_ref.shape[0]
+    pair = pl.program_id(0)
+    pairs = out_ref.shape[1] // (3 * PAIR)
+    scale = HEAD_DIM ** (-0.5)
+    lane = lax.broadcasted_iota(jnp.int32, (size, PAIR), 1)
+
+    def lanes(part):
+        return pl.ds(pl.multiple_of((part * pairs + pair) * PAIR, PAIR), PAIR)
+
+    for low in range(length - size, -1, -size):
+        high = low + size
+        keys = key_ref[:high, :]
+        values = value_ref[:high, :]
+        queries = query_ref[low:high, :]
+        grads = grad_ref[low:high, :]
+        allowed = allowed_keys(first_ref[:, low:high], low, high)
+        query_grads = []
+        for head in range(2):
+            scaled = queries * head_lanes(head, scale)
+            grad = grads * head_lanes(head, 1.0)
+            scores = jnp.where(allowed, mm(keys, scaled, 1, 1), masked_fill)
+            exp_scores = jnp.exp(scores - jnp.max(scores, axis=0, keepdims=True))
+            probs = exp_scores * (1.0 / jnp.sum(exp_scores, axis=0, keepdims=True))
+            prob_grad = mm(values, grad, 1, 1)
+            row_dot = jnp.sum(probs * prob_grad, axis=0, keepdims=True)
+            score_grad = (probs * (prob_grad - row_dot)).astype(jnp.bfloat16)
+            value_part = mm(probs.astype(jnp.bfloat16), grad, 1, 0)
+            key_part = mm(score_grad, scaled, 1, 0)
+            query_grads.append(mm(score_grad, keys, 0, 0) * scale)
+            if head == 0:
+                key_add, value_add = key_part, value_part
+            else:
+                key_add, value_add = key_add + key_part, value_add + value_part
+        if high == length:
+            key_sum[...] = key_add
+            value_sum[...] = value_add
+        else:
+            key_sum[:high, :] += key_add
+            value_sum[:high, :] += value_add
+        out_ref[low:high, lanes(0)] = jnp.where(
+            lane < HEAD_DIM, query_grads[0], query_grads[1]
+        ).astype(jnp.bfloat16)
+    out_ref[:, lanes(1)] = key_sum[...].astype(jnp.bfloat16)
+    out_ref[:, lanes(2)] = value_sum[...].astype(jnp.bfloat16)
+
+
+def local_backward(heads, head_grad, group, first_row):
+    length = heads.shape[0]
+    pairs = heads.shape[1] // (3 * PAIR)
+    return pl.pallas_call(
+        functools.partial(local_backward_kernel, min(512, length)),
+        grid=(pairs,),
+        in_specs=[
+            pl.BlockSpec((1, length), lambda p: (0, 0)),
+            pl.BlockSpec((length, PAIR), lambda p: (0, p)),
+            pl.BlockSpec((length, PAIR), lambda p: (0, group * pairs + p)),
+            pl.BlockSpec((length, PAIR), lambda p: (0, pairs + p)),
+            pl.BlockSpec((length, PAIR), lambda p: (0, 2 * pairs + p)),
+        ],
+        out_specs=pl.BlockSpec(heads.shape, lambda p: (0, 0)),
+        out_shape=jax.ShapeDtypeStruct(heads.shape, jnp.bfloat16),
+        scratch_shapes=[pltpu.VMEM((length, PAIR), jnp.float32)] * 2,
+        compiler_params=pltpu.CompilerParams(vmem_limit_bytes=vmem_bytes),
+        cost_estimate=cost(32 * length * length * pairs * PAIR, 8 * heads.size),
+    )(first_row, heads, head_grad, heads, heads)
+
+
+gelu_scale = 0.7978845608028654
+gelu_cubic = 0.044715
+
+
+def ffn_kernel(*refs):
+    normed, grads, pieces = [r[...] for r in refs[:2]], [r[...] for r in refs[2:4]], refs[4:6]
+    bias_ref, rows_ref, sum_ref, grad_out, down_out, grad_acc, down_acc = refs[6:]
+    step = pl.program_id(0)
+    width = normed[0].shape[1]
+    unit = pieces[0].shape[2] // 4
+
+    def weight(half, units, kind):
+        at = (2 * (units ^ half) + kind) * unit
+        return pieces[half][0, :, at : at + unit]
+
+    ups, downs = [None] * 2, [None] * 2
+    for units in range(2):
+        pre = mm(normed[0], weight(0, units, 0), 1, 0) + mm(normed[1], weight(1, units, 0), 1, 0)
+        act_grad = mm(grads[0], weight(0, units, 1), 1, 0) + mm(grads[1], weight(1, units, 1), 1, 0)
+        span = slice(units * unit, (units + 1) * unit)
+        pre = pre + bias_ref[0, :, span]
+        square = pre * pre
+        bent = jnp.tanh(gelu_scale * pre * (1.0 + gelu_cubic * square))
+        half = 0.5 * (1.0 + bent)
+        slope = half + 0.5 * gelu_scale * pre * (1.0 - bent * bent) * (1.0 + 3.0 * gelu_cubic * square)
+        act = (pre * half).astype(jnp.bfloat16)
+        pre_grad = (act_grad * slope).astype(jnp.bfloat16)
+        rows_ref[:, span] = act
+        rows_ref[:, (2 + units) * unit : (3 + units) * unit] = pre_grad
+        sum_ref[0, :, span] = jnp.sum(pre_grad.astype(jnp.float32), axis=0, keepdims=True)
+        for half in range(2):
+            up = mm(pre_grad, weight(half, units, 0), 1, 1)
+            down = mm(act, weight(half, units, 1), 1, 1)
+            ups[half] = up if units == 0 else ups[half] + up
+            downs[half] = down if units == 0 else downs[half] + down
+
+    for half in range(2):
+        at = slice(half * width, (half + 1) * width)
+
+        @pl.when(step == 0)
+        def _():
+            grad_acc[:, at] = ups[half]
+            down_acc[:, at] = downs[half]
+
+        @pl.when(step > 0)
+        def _():
+            grad_acc[:, at] += ups[half]
+            down_acc[:, at] += downs[half]
+
+    @pl.when(step == pl.num_programs(0) - 1)
+    def _():
+        grad_out[...] = grad_acc[...].astype(jnp.bfloat16)
+        down_out[...] = down_acc[...].astype(jnp.bfloat16)
+
+
+def ffn_rows_of(normed, grads, part, own_pieces, sib_pieces, bias):
+    tokens, features = normed.shape
+    width = features // 2
+    ring, _, columns = own_pieces.shape
+    unit = columns // 4
+
+    def halves(at):
+        return [pl.BlockSpec((tokens, width), lambda k, h=h: (at, h)) for h in range(2)]
+
+    piece = pl.BlockSpec((1, width, columns), lambda k: (k, 0, 0))
+    whole = pl.BlockSpec((tokens, features), lambda k: (0, 0))
+    vector = pl.BlockSpec((1, 1, 2 * unit), lambda k: (k, 0, 0))
+    return pl.pallas_call(
+        ffn_kernel,
+        grid=(ring,),
+        in_specs=halves(0) + halves(part) + [piece] * 2 + [vector],
+        out_specs=[pl.BlockSpec((tokens, columns), lambda k: (0, k)), vector, whole, whole],
+        out_shape=[
+            shape((tokens, ring * columns)),
+            shape((ring, 1, 2 * unit), jnp.float32),
+            shape((tokens, features)),
+            shape((tokens, features)),
+        ],
+        scratch_shapes=[pltpu.VMEM((tokens, features), jnp.float32)] * 2,
+        compiler_params=params(),
+        cost_estimate=cost(16 * tokens * features * ring * unit, 12 * ring * width * columns),
+    )(normed, normed, grads, grads, own_pieces, sib_pieces, bias)
+
+
+def weight_products_kernel(count, mirrored, index_ref, *refs):
+    out_ref = refs[-1]
+    normed, grads, rows = [refs[i * count : (i + 1) * count] for i in range(3)]
+    twice = rows[0].shape[1] // 2
+    unit = twice // 2
+    up = down = None
+    for j in range(count):
+        up_part = mm(normed[j][...], rows[j][:, twice:], 0, 0)
+        down_part = mm(grads[j][...], rows[j][:, :twice], 0, 0)
+        up = up_part if up is None else up + up_part
+        down = down_part if down is None else down + down_part
+    for i in range(2):
+        units = slice((i ^ mirrored) * unit, ((i ^ mirrored) + 1) * unit)
+        out_ref[0, :, i * twice : i * twice + unit] = up[:, units].astype(jnp.bfloat16)
+        out_ref[0, :, i * twice + unit : (i + 1) * twice] = down[:, units].astype(jnp.bfloat16)
+
+
+def weight_products(index, normed, grads, rows, half):
+    count = len(normed)
+    tokens, features = normed[0].shape
+    width = features // 2
+    ring = 4
+    columns = rows[0].shape[1] // ring
+    size = min(256, width)
+    blocks = width // size
+    left = [pl.BlockSpec((tokens, size), lambda k, d, s: (0, half * blocks + d))] * count
+    left += [
+        pl.BlockSpec((tokens, size), lambda k, d, s, j=j: (j, half * blocks + d)) for j in range(count)
+    ]
+    right = [pl.BlockSpec((tokens, columns), lambda k, d, s: (0, k))] * count
+    return pl.pallas_call(
+        functools.partial(weight_products_kernel, count, half),
+        grid_spec=pltpu.PrefetchScalarGridSpec(
+            num_scalar_prefetch=1,
+            grid=(ring, blocks),
+            in_specs=left + right,
+            out_specs=pl.BlockSpec(
+                (1, size, columns),
+                lambda k, d, s: (jnp.where(s[2] >= k, s[2] - k, s[2] - k + ring), d, 0),
+            ),
+        ),
+        out_shape=shape((ring, width, columns)),
+        compiler_params=params(),
+        cost_estimate=cost(
+            2 * count * tokens * width * ring * columns, 4 * count * tokens * features * ring
+        ),
+    )(index, *normed, *([grads] * count), *rows)
+
+
+def params(**more):
+    return pltpu.CompilerParams(vmem_limit_bytes=vmem_bytes, **more)
+
+
+def cost(flops, nbytes):
+    return pl.CostEstimate(flops=20 * flops, bytes_accessed=20 * nbytes, transcendentals=0)
+
+
+def shape(dims, dtype=jnp.bfloat16):
+    return jax.ShapeDtypeStruct(dims, dtype)
+
+
+def turned(values):
+    return values.astype(jnp.float32).T.astype(jnp.bfloat16)
+
+
+def pack_heads_kernel(index_ref, *refs):
+    sources, outs = refs[:8], refs[8:]
+    own = sources[0].shape[1]
+    for which in range(2):
+        for i in range(4):
+            part = sources[4 * which + i][...]
+            outs[which][:, i * own : (i + 1) * own] = part if i < 3 else turned(part)
+
+
+def pack_heads(index, weights, count):
+    width, units = weights[0].shape
+    own, block = units // 2, width // 4
+
+    def feature(which):
+        return pl.BlockSpec((block, own), lambda j, s: (s[1] ^ j, s[0] ^ which))
+
+    def turned_block(which):
+        return pl.BlockSpec((own, block), lambda j, s: (s[0] ^ which, s[1] ^ j))
+
+    in_specs = []
+    for which in range(2):
+        in_specs += [feature(which)] * 3 + [turned_block(which)]
+    return pl.pallas_call(
+        pack_heads_kernel,
+        grid_spec=pltpu.PrefetchScalarGridSpec(
+            num_scalar_prefetch=1,
+            grid=(count,),
+            in_specs=in_specs,
+            out_specs=[pl.BlockSpec((block, 4 * own), lambda j, s: (j, 0))] * 2,
+        ),
+        out_shape=[shape((count * block, 4 * own))] * 2,
+        compiler_params=params(),
+        cost_estimate=cost(0, 32 * count * block * own),
+    )(index, *weights, *weights)
+
+
+def pack_ff_kernel(index_ref, up_own, down_own, up_sib, down_sib, out_ref):
+    unit = up_own.shape[1]
+    parts = (up_own[...], turned(down_own[...]), up_sib[...], turned(down_sib[...]))
+    for i, part in enumerate(parts):
+        out_ref[:, i * unit : (i + 1) * unit] = part
+
+
+def pack_ff(index, up_weight, down_weight):
+    width, units = up_weight.shape
+    unit, block = units // 8, width // 4
+    in_specs = []
+    for which in range(2):
+        in_specs += [
+            pl.BlockSpec((block, unit), lambda d, s, w=which: (d, 2 * s[1] + (s[0] ^ w))),
+            pl.BlockSpec((unit, block), lambda d, s, w=which: (2 * s[1] + (s[0] ^ w), d)),
+        ]
+    return pl.pallas_call(
+        pack_ff_kernel,
+        grid_spec=pltpu.PrefetchScalarGridSpec(
+            num_scalar_prefetch=1,
+            grid=(4,),
+            in_specs=in_specs,
+            out_specs=pl.BlockSpec((block, 4 * unit), lambda d, s: (d, 0)),
+        ),
+        out_shape=shape((width, 4 * unit)),
+        compiler_params=params(),
+        cost_estimate=cost(0, 16 * width * unit),
+    )(index, up_weight, down_weight, up_weight, down_weight)
+
+
+def stack_kernel(*refs):
+    pieces, outs = refs[:3], refs[-2:]
+    block = pieces[0].shape[0] // 2
+    for j, piece in enumerate(pieces):
+        for i in range(2):
+            outs[i][j * block : (j + 1) * block, :] = piece[i * block : (i + 1) * block, :]
+    for i in range(2):
+        outs[i][3 * block :, :] = refs[3 + i][...]
+
+
+def stack_pieces(pieces):
+    rows, columns = pieces[0].shape
+    return pl.pallas_call(
+        stack_kernel,
+        out_shape=[shape((2 * rows, columns))] * 2,
+        compiler_params=params(),
+        cost_estimate=cost(0, 16 * rows * columns),
+    )(*pieces)
+
+
+def norm_kernel(index_ref, own_ref, sib_ref, vectors_ref, out_ref, stats_ref):
+    own = own_ref[...].astype(jnp.float32)
+    sib = sib_ref[...].astype(jnp.float32)
+    width = own.shape[1]
+    average = (jnp.sum(own, axis=1, keepdims=True) + jnp.sum(sib, axis=1, keepdims=True)) / (2 * width)
+    own, sib = own - average, sib - average
+    square = jnp.sum(own * own, axis=1, keepdims=True) + jnp.sum(sib * sib, axis=1, keepdims=True)
+    inverse = lax.rsqrt(square / (2 * width) + norm_eps)
+    block = width // 4
+    for half, values in enumerate((own, sib)):
+        gain, shift = vectors_ref[2 * half, :][None], vectors_ref[2 * half + 1, :][None]
+        rounded = (values * inverse * gain + shift).astype(jnp.bfloat16)
+        for i in range(4):
+            at = pl.multiple_of(half * width + (index_ref[1] ^ i) * block, block)
+            out_ref[:, pl.ds(at, block)] = rounded[:, i * block : (i + 1) * block]
+    lane = lax.broadcasted_iota(jnp.int32, stats_ref.shape, 1)
+    stats_ref[...] = jnp.where(lane == 0, average, inverse)
+
+
+def norm_rows(index, own, sib, vectors):
+    tokens, width = own.shape
+    size = min(256, tokens)
+    rows = pl.BlockSpec((size, width), lambda i, s: (i, 0))
+    return pl.pallas_call(
+        norm_kernel,
+        grid_spec=pltpu.PrefetchScalarGridSpec(
+            num_scalar_prefetch=1,
+            grid=(tokens // size,),
+            in_specs=[rows, rows, pl.BlockSpec((4, width), lambda i, s: (0, 0))],
+            out_specs=[
+                pl.BlockSpec((size, 2 * width), lambda i, s: (i, 0)),
+                pl.BlockSpec((size, 128), lambda i, s: (i, 0)),
+            ],
+        ),
+        out_shape=[shape((tokens, 2 * width)), shape((tokens, 128), jnp.float32)],
+        compiler_params=params(),
+        cost_estimate=cost(0, 8 * tokens * width),
+    )(index, own, sib, vectors)
+
+
+def project_kernel(own_ref, sib_ref, own_weight, sib_weight, bias_ref, out_ref):
+    total = mm(own_ref[...], own_weight[...], 1, 0) + mm(sib_ref[...], sib_weight[...], 1, 0)
+    out_ref[...] = (total + bias_ref[...]).astype(jnp.bfloat16)
+
+
+def halves_of(size, width):
+    return [pl.BlockSpec((size, width), lambda i, h=h: (i, h)) for h in range(2)]
+
+
+def project(normed, own_weight, sib_weight, bias):
+    tokens, features = normed.shape
+    width, units = features // 2, bias.shape[1]
+    size = min(256, tokens)
+    weight = pl.BlockSpec((width, units), lambda i: (0, 0))
+    return pl.pallas_call(
+        project_kernel,
+        grid=(tokens // size,),
+        in_specs=halves_of(size, width)
+        + [weight, weight, pl.BlockSpec((1, units), lambda i: (0, 0))],
+        out_specs=pl.BlockSpec((size, units), lambda i: (i, 0)),
+        out_shape=shape((tokens, units)),
+        compiler_params=params(),
+        cost_estimate=cost(4 * tokens * width * units, 4 * tokens * width + 4 * width * units),
+    )(normed, normed, own_weight, sib_weight, bias)
+
+
+def sum_rows_kernel(count, *refs):
+    out_ref = refs[-1]
+    width = refs[count].shape[0]
+    for half in range(2):
+        at = slice(half * width, (half + 1) * width)
+        total = refs[3 * count][:, at] if len(refs) > 3 * count + 1 else None
+        for k in range(count):
+            part = mm(refs[k][...], refs[(1 + half) * count + k][...], 1, 1)
+            total = part if total is None else total + part
+        out_ref[:, at] = total
+
+
+def sum_rows(rows, own_weights, sib_weights, at, before=()):
+    count = len(rows)
+    tokens, units = rows[0].shape
+    width = own_weights[0].shape[0]
+    size = min(256, tokens)
+    full = pl.BlockSpec((size, 2 * width), lambda i: (i, 0))
+    return pl.pallas_call(
+        functools.partial(sum_rows_kernel, count),
+        grid=(tokens // size,),
+        in_specs=[pl.BlockSpec((size, units), lambda i: (i, 0))] * count
+        + [pl.BlockSpec((width, units), lambda i: (0, at))] * (2 * count)
+        + [full] * len(before),
+        out_specs=full,
+        out_shape=shape((tokens, 2 * width), jnp.float32),
+        compiler_params=params(),
+        cost_estimate=cost(4 * count * tokens * units * width, 8 * tokens * width),
+    )(*rows, *own_weights, *sib_weights, *before)
+
+
+def head_grads_kernel(own_ref, sib_ref, *refs):
+    out_ref = refs[-1]
+    count = (len(refs) - 1) // 2
+    own = refs[0].shape[1]
+    for k in range(count):
+        total = mm(own_ref[...], refs[k][...], 1, 0) + mm(sib_ref[...], refs[count + k][...], 1, 0)
+        out_ref[:, k * own : (k + 1) * own] = total.astype(jnp.bfloat16)
+
+
+def head_grads(grads, own_weights, sib_weights):
+    tokens, width = grads.shape[0], grads.shape[1] // 2
+    count = len(own_weights)
+    units = own_weights[0].shape[1] // 4
+    size = min(256, tokens)
+    return pl.pallas_call(
+        head_grads_kernel,
+        grid=(tokens // size,),
+        in_specs=halves_of(size, width) + [pl.BlockSpec((width, units), lambda i: (0, 3))] * (2 * count),
+        out_specs=pl.BlockSpec((size, count * units), lambda i: (i, 0)),
+        out_shape=shape((tokens, count * units)),
+        compiler_params=params(),
+        cost_estimate=cost(4 * count * tokens * width * units, 8 * tokens * width),
+    )(grads, grads, *own_weights, *sib_weights)
+
+
+def head_products_kernel(*refs):
+    normed, grads = refs[:2], refs[2:4]
+    heads_ref, attended_ref = refs[4:6]
+    outs, sum_ref = refs[6:8], refs[8]
+    split = heads_ref.shape[1]
+    for i in range(2):
+        outs[i][:, :split] = mm(normed[i][...], heads_ref[...], 0, 0).astype(jnp.bfloat16)
+        outs[i][:, split:] = mm(grads[i][...], attended_ref[...], 0, 0).astype(jnp.bfloat16)
+
+    @pl.when(pl.program_id(0) == 0)
+    def _():
+        sum_ref[...] = jnp.sum(heads_ref[...].astype(jnp.float32), axis=0, keepdims=True)
+
+
+def head_products(normed, grads, head_grad, attended):
+    tokens, width = normed.shape[0], normed.shape[1] // 2
+    split, own = head_grad.shape[1], attended.shape[1]
+    size = min(256, width)
+    blocks = width // size
+    left = [pl.BlockSpec((tokens, size), lambda d, h=h: (0, h * blocks + d)) for h in range(2)]
+    out = pl.BlockSpec((size, split + own), lambda d: (d, 0))
+    return pl.pallas_call(
+        head_products_kernel,
+        grid=(width // size,),
+        in_specs=left * 2
+        + [pl.BlockSpec((tokens, split), lambda d: (0, 0)), pl.BlockSpec((tokens, own), lambda d: (0, 0))],
+        out_specs=[out, out, pl.BlockSpec((1, split), lambda d: (0, 0))],
+        out_shape=[shape((width, split + own))] * 2 + [shape((1, split), jnp.float32)],
+        compiler_params=params(),
+        cost_estimate=cost(4 * tokens * width * (split + own), 12 * tokens * width),
+    )(normed, normed, grads, grads, head_grad, attended)
+
+
+def block_at(half, width, place):
+    block = width // 4
+    return pl.ds(pl.multiple_of(half * width + place * block, block), block)
+
+
+def norm_two_kernel(
+    index_ref, rows_ref, came_ref, own_ref, sib_ref, vectors_ref, hidden_ref, normed_ref, stats_ref
+):
+    width = own_ref.shape[1]
+    block = width // 4
+    for half, tokens_ref in enumerate((own_ref, sib_ref)):
+        for i in range(4):
+            at = block_at(half, width, index_ref[1] ^ i)
+            span = slice(half * width + i * block, half * width + (i + 1) * block)
+            hidden_ref[:, span] = (
+                tokens_ref[:, i * block : (i + 1) * block].astype(jnp.float32)
+                + rows_ref[:, at]
+                + came_ref[:, at].astype(jnp.float32)
+                + vectors_ref[4:5, span]
+            )
+    hidden = hidden_ref[...]
+    average = jnp.mean(hidden, axis=1, keepdims=True)
+    centered = hidden - average
+    inverse = lax.rsqrt(jnp.mean(centered * centered, axis=1, keepdims=True) + norm_eps)
+    normed_ref[...] = (centered * inverse * vectors_ref[2:3, :] + vectors_ref[3:4, :]).astype(jnp.bfloat16)
+    lane = lax.broadcasted_iota(jnp.int32, stats_ref.shape, 1)
+    stats_ref[...] = jnp.where(lane == 0, average, inverse)
+
+
+def my_rows(size, columns, blocks):
+    return pl.BlockSpec((size, columns), lambda i, s: (s[0] * blocks + i, 0))
+
+
+def norm_two(index, rows, came, own, sib, vectors):
+    tokens, features = came.shape
+    size = tokens // 2
+    mine = my_rows(size, features // 2, 2)
+    plain = pl.BlockSpec((size, features), lambda i, s: (i, 0))
+    return pl.pallas_call(
+        norm_two_kernel,
+        grid_spec=pltpu.PrefetchScalarGridSpec(
+            num_scalar_prefetch=1,
+            grid=(2,),
+            in_specs=[
+                my_rows(size, features, 2),
+                plain,
+                mine,
+                mine,
+                pl.BlockSpec(vectors.shape, lambda i, s: (0, 0)),
+            ],
+            out_specs=[plain, plain, pl.BlockSpec((size, 128), lambda i, s: (i, 0))],
+        ),
+        out_shape=[
+            shape((tokens, features), jnp.float32),
+            shape((tokens, features)),
+            shape((tokens, 128), jnp.float32),
+        ],
+        compiler_params=params(),
+        cost_estimate=cost(0, 16 * tokens * features),
+    )(index, rows, came, own, sib, vectors)
+
+
+def norm_pull(grads, normal, inverse, gain):
+    scaled = grads * gain
+    return inverse * (
+        scaled
+        - jnp.mean(scaled, axis=1, keepdims=True)
+        - normal * jnp.mean(scaled * normal, axis=1, keepdims=True)
+    )
+
+
+def add_sums(sums_ref, parts):
+    rows = [jnp.sum(p, axis=0, keepdims=True) for p in parts]
+    rows += [jnp.zeros_like(rows[0])] * (8 - len(rows))
+    total = jnp.concatenate(rows, axis=0)
+
+    @pl.when(pl.program_id(0) == 0)
+    def _():
+        sums_ref[...] = total
+
+    @pl.when(pl.program_id(0) > 0)
+    def _():
+        sums_ref[...] += total
+
+
+def norm_two_back_kernel(index_ref, *refs):
+    here, x_top, y_top, x_bottom, y_bottom, hidden_ref, stats_ref, branch_ref, vectors_ref = refs[:9]
+    grad_ref, blocks_ref, mirror_ref, sums_ref = refs[9:]
+    f32 = jnp.float32
+    top = pl.program_id(0) == 0
+    from_x = jnp.where(top, x_top[...].astype(f32), x_bottom[...].astype(f32))
+    from_y = jnp.where(top, y_top[...].astype(f32), y_bottom[...].astype(f32))
+    grads = here[...].astype(f32) + from_x + from_y
+    inverse = stats_ref[:, 1:2]
+    normal = (hidden_ref[...] - stats_ref[:, :1]) * inverse
+    branch = branch_ref[...].astype(f32)
+    total = branch + norm_pull(grads, normal, inverse, vectors_ref[2:3, :])
+    grad_ref[...] = total
+    rounded = total.astype(jnp.bfloat16)
+    width = rounded.shape[1] // 2
+    block = width // 4
+    for half in range(2):
+        for i in range(4):
+            part = rounded[:, half * width + i * block : half * width + (i + 1) * block]
+            place = index_ref[1] ^ i
+            blocks_ref[:, block_at(half, width, place)] = part
+            mirror_ref[:, block_at(1 - half, width, place)] = part
+    add_sums(sums_ref, (grads * normal, grads, rounded.astype(f32), branch))
+
+
+def norm_two_back(index, parts, hidden, stats, branch, vectors):
+    tokens, features = hidden.shape
+    size = tokens // 2
+    plain = pl.BlockSpec((size, features), lambda i, s: (i, 0))
+    once = pl.BlockSpec((size, features), lambda i, s: (0, 0))
+    return pl.pallas_call(
+        norm_two_back_kernel,
+        grid_spec=pltpu.PrefetchScalarGridSpec(
+            num_scalar_prefetch=1,
+            grid=(2,),
+            in_specs=[plain]
+            + [once] * 4
+            + [
+                plain,
+                pl.BlockSpec((size, 128), lambda i, s: (i, 0)),
+                plain,
+                pl.BlockSpec(vectors.shape, lambda i, s: (0, 0)),
+            ],
+            out_specs=[plain] * 3 + [pl.BlockSpec((8, features), lambda i, s: (0, 0))],
+        ),
+        out_shape=[
+            shape((tokens, features), jnp.float32),
+            shape((tokens, features)),
+            shape((tokens, features)),
+            shape((8, features), jnp.float32),
+        ],
+        compiler_params=params(),
+        cost_estimate=cost(0, 24 * tokens * features),
+    )(index, *parts, hidden, stats, branch, vectors)
+
+
+def norm_one_back_kernel(index_ref, *refs):
+    rows_ref, came_ref, own_ref, sib_ref, stats_ref, out_own, out_sib, keep_ref, hidden_ref = refs[:9]
+    vectors_ref, own_grad, sib_grad, sums_ref, grads_ref = refs[9:]
+    f32 = jnp.float32
+    width = own_ref.shape[1]
+    block = width // 4
+    for half in range(2):
+        for i in range(4):
+            at = block_at(half, width, index_ref[1] ^ i)
+            span = slice(half * width + i * block, half * width + (i + 1) * block)
+            grads_ref[:, span] = rows_ref[:, at] + came_ref[:, at].astype(f32)
+    grads = grads_ref[...]
+    inverse = stats_ref[:, 1:2]
+    tokens = jnp.concatenate([own_ref[...], sib_ref[...]], axis=1).astype(f32)
+    normal = (tokens - stats_ref[:, :1]) * inverse
+    total = hidden_ref[...] + norm_pull(grads, normal, inverse, vectors_ref[0:1, :])
+    dropped = 1.0 - keep_ref[...]
+    own_grad[...] = out_own[...].astype(f32) * dropped + total[:, :width]
+    sib_grad[...] = out_sib[...].astype(f32) * dropped + total[:, width:]
+    add_sums(sums_ref, (grads * normal, grads))
+
+
+def norm_one_back(index, rows, came, own, sib, stats, out_own, out_sib, keep, hidden, vectors):
+    tokens, features = came.shape
+    size, width = tokens // 2, features // 2
+    plain = pl.BlockSpec((size, features), lambda i, s: (i, 0))
+    half_wide = pl.BlockSpec((size, width), lambda i, s: (i, 0))
+    return pl.pallas_call(
+        norm_one_back_kernel,
+        grid_spec=pltpu.PrefetchScalarGridSpec(
+            num_scalar_prefetch=1,
+            grid=(2,),
+            in_specs=[
+                my_rows(size, features, 2),
+                plain,
+                my_rows(size, width, 2),
+                my_rows(size, width, 2),
+                my_rows(size, 128, 2),
+                my_rows(size, width, 2),
+                half_wide,
+                pl.BlockSpec((size, 1), lambda i, s: (i, 0)),
+                plain,
+                pl.BlockSpec(vectors.shape, lambda i, s: (0, 0)),
+            ],
+            out_specs=[half_wide, half_wide, pl.BlockSpec((8, features), lambda i, s: (0, 0))],
+            scratch_shapes=[pltpu.VMEM((size, features), jnp.float32)],
+        ),
+        out_shape=[shape((tokens, width), jnp.float32)] * 2 + [shape((8, features), jnp.float32)],
+        compiler_params=params(),
+        cost_estimate=cost(0, 24 * tokens * features),
+    )(index, rows, came, own, sib, stats, out_own, out_sib, keep, hidden, vectors)
+
+
+def select_piece(refs, step, use):
+    for j in range(3):
+
+        @pl.when(step == j)
+        def _():
+            use(refs[j][...])
+
+    @pl.when(step == 3)
+    def _():
+        use(jnp.concatenate([refs[3][...], refs[4][...]], axis=0))
+
+
+def place_heads_kernel(index_ref, *refs):
+    pieces, outs = refs[:5], refs[5:]
+    own = pieces[0].shape[1] // 8
+
+    def use(piece):
+        for which in range(2):
+            at = pl.multiple_of((index_ref[0] ^ which) * own, own)
+            for m in range(4):
+                part = piece[:, (4 * which + m) * own : (4 * which + m + 1) * own].astype(jnp.float32)
+                if m < 3:
+                    outs[m][:, pl.ds(at, own)] = part
+                else:
+                    outs[m][pl.ds(at, own), :] = part.T
+
+    select_piece(pieces, pl.program_id(0), use)
+
+
+def place_heads(index, pieces):
+    block, columns = pieces[0].shape
+    units, width = columns // 4, 4 * block
+    whole = [pl.BlockSpec(p.shape, lambda j, s: (0, 0)) for p in pieces]
+    return pl.pallas_call(
+        place_heads_kernel,
+        grid_spec=pltpu.PrefetchScalarGridSpec(
+            num_scalar_prefetch=1,
+            grid=(4,),
+            in_specs=whole,
+            out_specs=[pl.BlockSpec((block, units), lambda j, s: (s[1] ^ j, 0))] * 3
+            + [pl.BlockSpec((units, block), lambda j, s: (0, s[1] ^ j))],
+        ),
+        out_shape=[shape((width, units), jnp.float32)] * 3 + [shape((units, width), jnp.float32)],
+        compiler_params=params(),
+        cost_estimate=cost(0, 24 * width * units),
+    )(index, *pieces)
+
+
+def place_ff_kernel(index_ref, *refs):
+    pieces, (up_out, down_out) = refs[:-2], refs[-2:]
+    rows = pieces[0].shape[1]
+    unit = pieces[0].shape[2] // 4
+    for part, piece_ref in enumerate(pieces):
+        span = slice(part * rows, (part + 1) * rows)
+        for which in range(2):
+            at = pl.multiple_of((index_ref[0] ^ which) * unit, unit)
+            start = 2 * which * unit
+            up_out[span, pl.ds(at, unit)] = piece_ref[0, :, start : start + unit].astype(jnp.float32)
+            down_out[pl.ds(at, unit), span] = (
+                piece_ref[0, :, start + unit : start + 2 * unit].astype(jnp.float32).T
+            )
+
+
+def place_ff(index, pieces):
+    count, rows, columns = pieces[0].shape
+    width, quarter = rows * len(pieces), columns // 2
+    return pl.pallas_call(
+        place_ff_kernel,
+        grid_spec=pltpu.PrefetchScalarGridSpec(
+            num_scalar_prefetch=1,
+            grid=(count,),
+            in_specs=[pl.BlockSpec((1, rows, columns), lambda j, s: (j, 0, 0))] * len(pieces),
+            out_specs=[
+                pl.BlockSpec((width, quarter), lambda j, s: (0, j)),
+                pl.BlockSpec((quarter, width), lambda j, s: (j, 0)),
+            ],
+        ),
+        out_shape=[
+            shape((width, count * quarter), jnp.float32),
+            shape((count * quarter, width), jnp.float32),
+        ],
+        compiler_params=params(),
+        cost_estimate=cost(0, 48 * width * quarter),
+    )(index, *pieces)
+
+
+def body_local(
+    tokens_in,
+    out_grad,
+    segment_ids,
+    active_lengths,
+    norm1_gain,
+    norm1_shift,
+    query_weight,
+    query_bias,
+    key_weight,
+    value_weight,
+    value_bias,
+    out_weight,
+    out_bias,
+    norm2_gain,
+    norm2_shift,
+    up_weight,
+    up_bias,
+    down_weight,
+    down_bias,
+):
+    f32, bf16 = jnp.float32, jnp.bfloat16
+    rows, width = tokens_in.shape
+    ring = lax.axis_size("col")
+    row_i = lax.axis_index("row")
+    plane_i = lax.axis_index("dp")
+    col_i = lax.axis_index("col")
+    own = query_weight.shape[1] // 2
+    block = width // 4
+    quarter = up_weight.shape[1] // 4
+    unit = quarter // 2
+    half = rows // 2
+    order = Order()
+    plane, column = Plane(order), Link(order)
+    index = jnp.stack([row_i, plane_i, col_i]).astype(jnp.int32)
+
+    def cut(values, start, size):
+        return lax.dynamic_slice_in_dim(values, start, size, axis=0)
+
+    def mirrored(values):
+        return jnp.concatenate([values[:, width:], values[:, :width]], axis=1)
+
+    def my_tokens(values):
+        return cut(values, row_i * half, half)
+
+    def other_tokens(values):
+        return cut(values, (1 - row_i) * half, half)
+
+    def all_tokens(mine, other):
+        return jnp.where(
+            row_i == 0, jnp.concatenate([mine, other], axis=0), jnp.concatenate([other, mine], axis=0)
+        )
+
+    tokens_sib = order.swap(tokens_in)
+    out_grad_sib = swap(other_tokens(out_grad))
+
+    ff_bias = cut(up_bias, plane_i * quarter, quarter).reshape(2, unit)
+    mine = jnp.concatenate(
+        [
+            cut(query_bias, row_i * own, own),
+            jnp.zeros((own,), f32),
+            cut(value_bias, row_i * own, own),
+            picked(ff_bias, row_i),
+            picked(ff_bias, 1 - row_i),
+        ]
+    )
+    small = [mine] + [
+        lax.ppermute(mine, "col", [(i, (i + k) % ring) for i in range(ring)]) for k in range(1, ring)
+    ]
+
+    sources = (query_weight, key_weight, value_weight, out_weight)
+    piece = order.run(pack_heads, after(index, mine), sources, 1)
+    pieces = [jnp.concatenate([piece[0], swap(piece[1])], axis=0)]
+    column.last = small[1:]
+    pieces.append(column.send(step_up, pieces[0]))
+
+    active_all = active_rows(segment_ids, active_lengths)
+    active_here = my_tokens(cut(active_all, col_i * rows, rows))
+    keep_mask = active_here.astype(f32)[:, None]
+    out_grads = jnp.concatenate([my_tokens(out_grad), out_grad_sib], axis=1).astype(f32)
+    branch_mine = (after(out_grads, *order.tokens) * keep_mask).astype(bf16)
+    branch_first = plane.both(branch_mine[: half // 2], branch_mine[: half // 2])
+    vectors = jnp.stack([norm1_gain, norm1_shift, norm2_gain, norm2_shift, out_bias, down_bias])
+    vectors_sib = swap(vectors)
+    vectors_all = jnp.concatenate([vectors, vectors_sib], axis=1)
+    here = order.run(pack_heads, index, sources, 4)
+    own_parts, other_rows = [here[0]], [order.swap(here[1])]
+    ff_piece = order.run(pack_ff, index, up_weight, down_weight)
+    ff_own, ff_sib = [ff_piece], []
+    normed_one, stats_one = order.run(
+        norm_rows,
+        index,
+        tokens_in,
+        tokens_sib,
+        jnp.concatenate([vectors[:2], vectors_sib[:2]], axis=0),
+    )
+
+    segment_row = picked(segment_ids, col_i)
+    member = (segment_row[:, None] == jnp.arange(active_lengths.shape[1])).astype(jnp.int32)
+    counts = jnp.sum(member, axis=0)
+    first_row = jnp.sum(member * (jnp.cumsum(counts) - counts), axis=1)[None, :]
+
+    heads, attended = [], []
+
+    def attend_project(k):
+        heads.append(
+            order.run(project, normed_one, own_parts[k], other_rows[k], small[k][None, : 3 * own])
+        )
+
+    def attend(k):
+        attended.append(order.run(local_forward, heads[k], first_row))
+
+    def stack(k, near, far):
+        own_part, other_part = order.run(stack_pieces, [pieces[k], *near, *far])
+        own_parts.append(own_part)
+        other_rows.append(other_part)
+
+    def next_ff():
+        ff_sib.append(order.swap(ff_own[-1]))
+        ff_own.append(column.send(step_up, ff_own[-1]))
+
+    attend_project(0)
+    pieces.append(column.send(step_up, pieces[1]))
+    near = plane.both(pieces[1], pieces[1])
+    attend(0)
+    far = plane.far(*near)
+    pieces.append(column.send(step_up, pieces[2]))
+    last_near, last_far = near, far
+    near = plane.both(pieces[2], pieces[2])
+    stack(1, last_near, last_far)
+    attend_project(1)
+    attend(1)
+    next_ff()
+    far = plane.far(*near)
+    last_near, last_far = near, far
+    near = plane.both(pieces[3], pieces[3])
+    stack(2, last_near, last_far)
+    attend_project(2)
+    attend(2)
+    next_ff()
+    far = plane.far(*near)
+    last_near, last_far = near, far
+    branch_far = plane.far(*branch_first)
+    stack(3, last_near, last_far)
+    before = order.run(sum_rows, attended[:3], own_parts[:3], other_rows[:3], 3)
+    second_near = plane.both(branch_mine[half // 2 :], branch_mine[half // 2 :])
+    attend_project(3)
+    attend(3)
+    next_ff()
+    order.tokens += second_near
+    attention_rows = order.run(sum_rows, attended[3:], own_parts[3:], other_rows[3:], 3, (before,))
+    arrived = swap(order.tie(mirrored(other_tokens(attention_rows)).astype(bf16)))
+    second_far = plane.far(*second_near)
+
+    hidden_one, normed_two, stats_two = order.run(
+        norm_two, index, attention_rows, arrived, tokens_in, tokens_sib, vectors_all
+    )
+
+    normed = [normed_two, *plane.both(normed_two, normed_two, True)]
+    branch_all = jnp.concatenate(
+        [branch_mine]
+        + [part for pair in zip(branch_first, second_near) for part in pair]
+        + [*branch_far, *second_far],
+        axis=0,
+    )
+    ff_sib.append(order.swap(ff_own[3]))
+    ff_own_all, ff_sib_all = jnp.stack(ff_own), jnp.stack(ff_sib)
+    ff_biases = jnp.stack([s[None, 3 * own :] for s in small])
+    ff_rows, up_sums, grad_parts, down_parts = [], [], [], []
+
+    def feed_forward(j):
+        results = order.run(ffn_rows_of, normed[j], branch_all, j, ff_own_all, ff_sib_all, ff_biases)
+        for kept, result in zip((ff_rows, up_sums, grad_parts, down_parts), results):
+            kept.append(result)
+
+    def plane_total(here, x_top, y_top, x_bottom, y_bottom):
+        cut_at = half // 2
+        return jnp.concatenate(
+            [
+                here[:cut_at].astype(f32) + x_top.astype(f32) + y_top.astype(f32),
+                here[cut_at:].astype(f32) + x_bottom.astype(f32) + y_bottom.astype(f32),
+            ],
+            axis=0,
+        )
+
+    def top(values):
+        return values[: half // 2]
+
+    def bottom(values):
+        return values[half // 2 :]
+
+    def second_steps(parts, via_x, via_y):
+        via_x, via_y = after((via_x, via_y), *order.tokens)
+        return plane.both(add_rounded(bottom(parts[1]), via_y), add_rounded(top(parts[2]), via_x))
+
+    def weight_grads(part):
+        return order.run(weight_products, index, normed, branch_all, ff_rows, part)
+
+    feed_forward(0)
+    normed_far = plane.far(normed[1], normed[2])
+    feed_forward(1)
+    feed_forward(2)
+    x_top, y_bottom = plane.both(top(grad_parts[1]), bottom(grad_parts[2]))
+    normed.append(jnp.concatenate(normed_far, axis=0))
+    feed_forward(3)
+    via_x, via_y = plane.both(top(grad_parts[3]), bottom(grad_parts[3]))
+    ff_other = order.swap(weight_grads(1))
+    x_bottom, y_top = second_steps(grad_parts, via_x, via_y)
+    ff_mine = weight_grads(0)
+
+    hidden_grad, grad_mine, grad_mirror, sums_two = order.run(
+        norm_two_back,
+        index,
+        (grad_parts[0], x_top, y_top, x_bottom, y_bottom),
+        hidden_one,
+        stats_two,
+        branch_mine,
+        vectors_all,
+    )
+    down_x_top, down_y_bottom = plane.both(top(down_parts[1]), bottom(down_parts[2]))
+    grad_other = order.swap(grad_mirror)
+    grad_rows = all_tokens(grad_mine, grad_other)
+
+    ff_grads = []
+    for part in range(2):
+        span = slice(part * width // 2, (part + 1) * width // 2)
+        total = order.tie(add_rounded(ff_mine[:, span], ff_other[:, span]))
+        total = lax.psum_scatter(total, "col", scatter_dimension=0, tiled=False)
+        ff_grads.append(lax.all_gather(total, "dp"))
+
+    head_grad = order.run(head_grads, grad_rows, own_parts, other_rows)
+    head_rows, bias_rows, group_parts = [None] * ring, [None] * ring, [None] * ring
+
+    def backward(k):
+        head_rows[k] = order.run(
+            lambda h, g, f: local_backward(h, g, k, f), heads[k], head_grad, first_row
+        )
+
+    def head_weights(k):
+        *group_parts[k], bias_rows[k] = order.run(
+            head_products, normed_one, grad_rows, head_rows[k], attended[k]
+        )
+
+    def part_of(k, j, which):
+        return group_parts[k][which][j * block : (j + 1) * block]
+
+    def first_messages(k):
+        return plane.both(part_of(k, 3, 0), part_of(k, 3, 1))
+
+    def second_messages(k, via):
+        via_x, via_y = after(via, *order.tokens)
+        return plane.both(
+            jnp.concatenate([part_of(k, 1, 0), add_rounded(part_of(k, 1, 1), via_y)], axis=1),
+            jnp.concatenate([add_rounded(part_of(k, 2, 0), via_x), part_of(k, 2, 1)], axis=1),
+        )
+
+    def group_total(k, came, total):
+        came_x, came_y = after(came, *order.tokens)
+        here = jnp.concatenate([part_of(k, 0, 0), part_of(k, 0, 1)], axis=1)
+        here = here.astype(f32) + came_x.astype(f32) + came_y.astype(f32)
+        if total is not None:
+            here = here + total.astype(f32)
+        return here.astype(bf16)
+
+    down_via_x, down_via_y = plane.both(top(down_parts[3]), bottom(down_parts[3]))
+    backward(3)
+    head_weights(3)
+    down_x_bottom, down_y_top = second_steps(down_parts, down_via_x, down_via_y)
+    backward(2)
+    head_weights(2)
+    via = first_messages(3)
+    backward(1)
+    came = second_messages(3, via)
+    head_weights(1)
+    backward(0)
+    total = group_total(3, came, None)
+    via = first_messages(2)
+    head_weights(0)
+    came = second_messages(2, via)
+    summed_group = group_total(2, came, None)
+    via = first_messages(1)
+    back_rows = order.run(sum_rows, head_rows, own_parts, other_rows, 0)
+    arrived = order.swap(mirrored(other_tokens(back_rows)).astype(bf16))
+    came = second_messages(1, via)
+    total = column.send(step_down, total)
+
+    input_mine, input_other, sums_one = order.run(
+        norm_one_back,
+        index,
+        back_rows,
+        arrived,
+        tokens_in,
+        tokens_sib,
+        stats_one,
+        out_grad,
+        out_grad_sib,
+        keep_mask,
+        hidden_grad,
+        vectors_all,
+    )
+    input_grad = all_tokens(input_mine, swap(input_other))
+
+    def by_column(relative):
+        places = jnp.mod(col_i - jnp.arange(ring), ring)
+        return jnp.take(relative, places, axis=0)
+
+    row_hot = (jnp.arange(2) == row_i).astype(f32)
+    plane_hot = (jnp.arange(4) == plane_i).astype(f32)
+    head_bias = by_column(jnp.stack(bias_rows)).reshape(ring, 3, 1, own) * row_hot[:, None]
+    up_bias_part = by_column(sum(up_sums).reshape(ring, 2, unit))
+    up_bias_part = jnp.where(row_i == 0, up_bias_part, up_bias_part[:, ::-1])
+    up_bias_part = up_bias_part[:, None] * plane_hot[:, None, None]
+    bias_vector = jnp.concatenate([head_bias.reshape(ring, -1), up_bias_part.reshape(ring, -1)], axis=1)
+    feature_sums = jnp.concatenate([sums_one[:2], sums_two[:4]], axis=0)
+    summed = jnp.concatenate([bias_vector.reshape(-1), feature_sums[:, :width].reshape(-1)])
+    summed = summed + swap(
+        jnp.concatenate([bias_vector.reshape(-1), feature_sums[:, width:].reshape(-1)])
+    )
+
+    via = first_messages(0)
+    total = add_rounded(total, summed_group)
+    total = column.send(step_down, total)
+    summed_group = group_total(1, came, None)
+    came = second_messages(0, via)
+    total = add_rounded(total, summed_group)
+    total = column.send(step_down, total)
+    summed = order.tie(summed)
+    summed = summed + plane.x.send(step_x, summed)
+    summed = summed + plane.y.send(step_y, summed)
+    step = 1
+    while step < ring:
+        pairs = [(i, i ^ step) for i in range(ring)]
+        summed = summed + column.send(lambda v: lax.ppermute(v, "col", pairs), summed)
+        step *= 2
+    total = group_total(0, came, total)
+    total = jnp.concatenate([total[:, : 4 * own], swap(total[:, 4 * own :])], axis=1)
+    near = plane.both(total, total)
+    up_weight_grad, down_weight_grad = order.run(place_ff, index, ff_grads)
+    far = plane.far(*near)
+    query_weight_grad, key_weight_grad, value_weight_grad, out_weight_grad = place_heads(
+        index, [total, *near, *far]
+    )
+
+    tokens_mine = jnp.concatenate([my_tokens(tokens_in), my_tokens(tokens_sib)], axis=1).astype(f32)
+    ffn_rows = plane_total(down_parts[0], down_x_top, down_y_top, down_x_bottom, down_y_bottom)
+    out_mine = jnp.where(active_here[:, None], hidden_one + ffn_rows + vectors_all[5], tokens_mine)
+    layer_out = all_tokens(out_mine[:, :width], swap(out_mine[:, width:]))
+
+    bias_here = picked(summed[: bias_vector.size].reshape(ring, -1), col_i)
+    own_here = summed[bias_vector.size :].reshape(6, width)
+    size = 2 * own
+    return (
+        layer_out,
+        input_grad,
+        own_here[0],
+        own_here[1],
+        query_weight_grad,
+        bias_here[:size],
+        key_weight_grad,
+        value_weight_grad,
+        bias_here[2 * size : 3 * size],
+        out_weight_grad,
+        own_here[4],
+        own_here[2],
+        own_here[3],
+        up_weight_grad,
+        bias_here[3 * size :],
+        down_weight_grad,
+        own_here[5],
+    )
+
+
+def body(tokens_in, out_grad, segment_ids, *rest):
+    ring = lax.axis_size("col")
+    local = (
+        lax.axis_size("dp") == 4
+        and lax.axis_size("row") == 2
+        and ring == 4
+        and tokens_in.shape[0] == segment_ids.shape[1]
+    )
+    chosen = body_local if local else body_general
+    return chosen(tokens_in, out_grad, segment_ids, *rest)
+
+
 def solution(mesh):
     placed = (
         P(("dp", "col"), "row"),

time: 3000 us -> 1030 us (0.34)
  waiting for transfers between devices: 2210 us -> 302 us
  Pallas kernels: 0 us -> 424 us
  matrix products: 357 us -> 0 us
  blocking collectives: 105 us -> 0 us
  starting transfers between devices: 0.92 us -> 87.2 us
  other arithmetic: 164 us -> 89.4 us
  local copies, waits for them, and re-layouts: 138 us -> 102 us
    reduce_scatter x8 -> x2, waiting for transfers between devices: 1190 us -> 0.02 us  [body_local(): total = lax.psum_scatter(total, 'col', scatter_dimension=0, tiled=False)]
    all_gather x8 -> x2, waiting for transfers between devices: 618 us -> 0.01 us  [body_local(): ff_grads.append(lax.all_gather(total, 'dp'))]
    pallas_call x0 -> x38, Pallas kernels: none -> 424 us  [the longest x4 115 us: ffn_rows_of(): pl.pallas_call(ffn_kernel, grid=(ring,), in_specs=halves(0) + halves(part...]
    psum x1 -> x0, waiting for transfers between devices: 393 us -> none  [body(): lax.psum((stacked_weight_grad, query_bias_grad, value_bias_grad, out_weig...]
    dot_general x68 -> x0, matrix products: 357 us -> none  [the longest x8 34.3 us: attend_backward(): jnp.einsum('hdq,hdk->hqk', grad_block, value_seq, preferred_element_type=...]
    ppermute x0 -> x89, waiting for transfers between devices: none -> 302 us  [the longest x29 140 us: step_y(): return lax.ppermute(values, 'dp', [(0, 2), (2, 0), (1, 3), (3, 1)])]
    psum x6 -> x0, blocking collectives: 105 us -> none  [the longest x1 76.9 us: body(): lax.psum((gain_one_grad, shift_one_grad, gain_two_grad, shift_two_grad),...]
    ppermute x0 -> x89, starting transfers between devices: none -> 87 us  [the longest x29 30.4 us: step_x(): return lax.ppermute(values, 'dp', [(0, 1), (1, 0), (2, 3), (3, 2)])]
  transfers between devices with their start and end apart: 17 -> 93, of which waited for: 16 -> 33; matrix products, arithmetic and copies ran while one was open for 8% -> 14% of each run, Pallas kernels for 0% -> 34%
where the time goes in v5:
time: 1030 us; the launch traced here: 1020 us
  Pallas kernels  424 us (41%)
  waiting for transfers between devices  302 us (29%)
  local copies, waits for them, and re-layouts  102 us (10%)
  other arithmetic  89.4 us (9%)
  starting transfers between devices  87.2 us (8%)
  between operations  16 us (2%)
    ppermute x29, waiting for transfers between devices, step_y(): return lax.ppermute(values, 'dp', [(0, 2), (2, 0), (1, 3), (3, 1)])  140 us
    pallas_call x4, Pallas kernels, ffn_rows_of(): pl.pallas_call(ffn_kernel, grid=(ring,), in_specs=halves(0) + halves(part...  115 us
    ppermute x6, waiting for transfers between devices, step_up(): lax.ppermute(values, 'col', [(i, (i + 1) % count) for i in range(count)])  109 us
    pallas_call x2, Pallas kernels, weight_products(): pl.pallas_call(functools.partial(weight_products_kernel, count, half), gr...  63 us
    pallas_call x4, Pallas kernels, local_backward(): pl.pallas_call(functools.partial(local_backward_kernel, min(512, length))...  50.5 us
    unnamed x315, local copies, waits for them, and re-layouts  45.7 us
    pallas_call x3, Pallas kernels, sum_rows(): pl.pallas_call(functools.partial(sum_rows_kernel, count), grid=(tokens //...  37.3 us
    ppermute x29, waiting for transfers between devices, step_x(): return lax.ppermute(values, 'dp', [(0, 1), (1, 0), (2, 3), (3, 2)])  37.3 us
  transfers between devices with their start and end apart: 93, of which 33 were waited for; matrix products, arithmetic and copies ran while one was open for 14% of the time, Pallas kernels for 34%

profile of v5, /device:TPU:0, one launch (start us, length us, event | category | flops | bytes accessed | tf_op | source)
XLA Modules:
  0.0 1020.5 jit_solution(18311664704943742782)
XLA Ops:
  36.1 3.6 shard_map.315
  44.9 22.4 %collective-permute-done.8.refs_0_ = bf16[512,1024]{1,0:T(8,128)(2,1)S(1)} collective-permute-done((bf16[512,1024]{1,0:T(8,128)(2,1)}, bf16[512,1024]{1,0:T(8,128)(2,1)S(1)}, u32[]{:S(2)}, u32[]{:S(2)}) %collective-permute-start.8) | collective-permute-done | bytes 1048608 | tf_op jit(solution)/shard_map/ppermute | solution.py:358
  67.3 4.6 shard_map.316
  71.9 6.8 shard_map.317
  79.5 6.0 shard_map.318.query_ref.key_ref.value_ref
  88.8 6.5 shard_map.319.refs_0_.refs_5_
  95.4 16.2 %collective-permute-done.12.refs_2_ = bf16[512,1024]{1,0:T(8,128)(2,1)S(1)} collective-permute-done((bf16[512,1024]{1,0:T(8,128)(2,1)S(1)}, bf16[512,1024]{1,0:T(8,128)(2,1)S(1)}, u32[]{:S(2)}, u32[]{:S(2)}) %collective-permute-start.12) | collective-permute-done | bytes 1048608 | tf_op jit(solution)/shard_map/ppermute | solution.py:353
  115.7 8.2 collective-permute-done.13.refs_3_
  130.7 5.4 shard_map.321.query_ref.key_ref.value_ref
  136.2 6.5 shard_map.322.refs_1_.refs_5_
  144.0 26.3 %collective-permute-done.18.refs_0_ = bf16[512,1024]{1,0:T(8,128)(2,1)} collective-permute-done((bf16[512,1024]{1,0:T(8,128)(2,1)S(1)}, bf16[512,1024]{1,0:T(8,128)(2,1)}, u32[]{:S(2)}, u32[]{:S(2)}) %collective-permute-start.18) | collective-permute-done | bytes 1048608 | tf_op jit(solution)/shard_map/ppermute | solution.py:358
  173.1 10.8 %collective-permute-done.19.refs_3_ = bf16[256,1024]{1,0:T(8,128)(2,1)S(1)} collective-permute-done((bf16[256,1024]{1,0:T(8,128)(2,1)S(1)}, bf16[256,1024]{1,0:T(8,128)(2,1)S(1)}, u32[]{:S(2)}, u32[]{:S(2)}) %collective-permute-start.19) | collective-permute-done | bytes 524320 | tf_op jit(solution)/shard_map/ppermute | solution.py:353
  193.2 5.4 shard_map.324.query_ref.key_ref.value_ref
  198.7 6.5 shard_map.325.refs_2_.refs_5_
  205.2 15.3 %collective-permute-done.24 = bf16[1024,1024]{1,0:T(8,128)(2,1)} collective-permute-done((bf16[1024,1024]{1,0:T(8,128)(2,1)}, bf16[1024,1024]{1,0:T(8,128)(2,1)}, u32[]{:S(2)}, u32[]{:S(2)}) %collective-permute-start.24) | collective-permute-done | bytes 2097184 | tf_op jit(solution)/shard_map/ppermute | solution.py:358
  227.9 9.2 collective-permute-done.25.refs_3_
  240.4 4.3 shard_map.326
  244.7 6.9 collective-permute-done.29
  251.9 8.4 shard_map.327.refs_3_
  263.4 5.5 shard_map.328.query_ref.key_ref.value_ref
  268.8 6.5 shard_map.329.refs_0_.refs_5_
  275.4 13.6 %collective-permute-done.30 = bf16[1024,1024]{1,0:T(8,128)(2,1)} collective-permute-done((bf16[1024,1024]{1,0:T(8,128)(2,1)}, bf16[1024,1024]{1,0:T(8,128)(2,1)}, u32[]{:S(2)}, u32[]{:S(2)}) %collective-permute-start.30) | collective-permute-done | bytes 2097184 | tf_op jit(solution)/shard_map/ppermute | solution.py:358
  289.0 7.8 shard_map.330.rows_ref
  312.1 5.7 shard_map.331
  320.1 30.2 %collective-permute-done.35 = bf16[1024,1024]{1,0:T(8,128)(2,1)S(1)} collective-permute-done((bf16[1024,1024]{1,0:T(8,128)(2,1)}, bf16[1024,1024]{1,0:T(8,128)(2,1)S(1)}, u32[]{:S(2)}, u32[]{:S(2)}) %collective-permute-start.35) | collective-permute-done | bytes 2097184 | tf_op jit(solution)/shard_map/ppermute | solution.py:358
  356.0 6.8 pad_maximum_fusion.refs_4_
  368.7 3.9 pad_maximum_fusion.1.refs_5_
  372.5 28.3 %shard_map.332 = (bf16[512,4096]{1,0:T(8,128)(2,1)}, f32[4,1,512]{2,1,0:T(1,128)S(1)}, bf16[512,2048]{1,0:T(8,128)(2,1)S(1)}, bf16[512,2048]{1,0:T(8,128)(2,1)S(1)}) custom-call(bf16[512,2048]{1,0:T(8,128)(2,1)} %copy-done.50, bf16[512,2048]{1,0:T(8,128)(2,1)} %copy-done.50, ...), custom_call_target="tpu_custom_call" | custom-call | flops 343597383680 | bytes 1006632960 | tf_op jit(solution)/shard_map/pallas_call | solution.py:629
  405.7 28.3 %shard_map.333 = (bf16[512,4096]{1,0:T(8,128)(2,1)}, f32[4,1,512]{2,1,0:T(1,128)S(1)}, bf16[512,2048]{1,0:T(8,128)(2,1)S(1)}, bf16[512,2048]{1,0:T(8,128)(2,1)S(1)}) custom-call(bf16[512,2048]{1,0:T(8,128)(2,1)} %copy-done.35, bf16[512,2048]{1,0:T(8,128)(2,1)} %copy-done.35, ...), custom_call_target="tpu_custom_call" | custom-call | flops 343597383680 | bytes 1006632960 | tf_op jit(solution)/shard_map/pallas_call | solution.py:629
  434.0 29.6 %shard_map.334 = (bf16[512,4096]{1,0:T(8,128)(2,1)}, f32[4,1,512]{2,1,0:T(1,128)S(1)}, bf16[512,2048]{1,0:T(8,128)(2,1)S(1)}, bf16[512,2048]{1,0:T(8,128)(2,1)S(1)}) custom-call(bf16[512,2048]{1,0:T(8,128)(2,1)} %copy-done.105, bf16[512,2048]{1,0:T(8,128)(2,1)} %copy-done.105, ...), custom_call_target="tpu_custom_call" | custom-call | flops 343597383680 | bytes 1006632960 | tf_op jit(solution)/shard_map/pallas_call | solution.py:629
  475.2 28.4 %shard_map.335 = (bf16[512,4096]{1,0:T(8,128)(2,1)}, f32[4,1,512]{2,1,0:T(1,128)S(1)}, bf16[512,2048]{1,0:T(8,128)(2,1)S(1)}, bf16[512,2048]{1,0:T(8,128)(2,1)S(1)}) custom-call(bf16[512,2048]{1,0:T(8,128)(2,1)} %copy-done.106, bf16[512,2048]{1,0:T(8,128)(2,1)} %copy-done.106, ...), custom_call_target="tpu_custom_call" | custom-call | flops 343597383680 | bytes 1006632960 | tf_op jit(solution)/shard_map/pallas_call | solution.py:629
  507.3 31.6 %shard_map.336 = bf16[4,1024,1024]{2,1,0:T(8,128)(2,1)} custom-call(s32[3]{0:T(128)S(1)} %pad_add_fusion.index_ref, bf16[512,2048]{1,0:T(8,128)(2,1)S(1)} %copy-done.51, bf16[512,2048]{1,0:T(8,128)(2,1)S(1)} %copy-done.37, bf16[512,2048]{1,0:T(8,128)(2,1)} %copy-done.105, bf16[512,2048]{1,0:T(8,128)(2,1)} %copy-done.106, ...), custom_call_target="tpu_custom_call" | custom-call | flops 343597383680 | bytes 1342177280 | tf_op jit(solution)/shard_map/pallas_call | solution.py:676
  539.0 3.8 add_convert_fusion.10
  545.4 31.3 %shard_map.337 = bf16[4,1024,1024]{2,1,0:T(8,128)(2,1)} custom-call(s32[3]{0:T(128)S(1)} %pad_add_fusion.index_ref, bf16[512,2048]{1,0:T(8,128)(2,1)S(1)} %copy-done.51, bf16[512,2048]{1,0:T(8,128)(2,1)S(1)} %copy-done.37, bf16[512,2048]{1,0:T(8,128)(2,1)} %copy-done.105, bf16[512,2048]{1,0:T(8,128)(2,1)} %copy-done.106, ...), custom_call_target="tpu_custom_call" | custom-call | flops 343597383680 | bytes 1342177280 | tf_op jit(solution)/shard_map/pallas_call | solution.py:676
  576.7 13.7 %shard_map.338 = (f32[512,2048]{1,0:T(8,128)}, bf16[512,2048]{1,0:T(8,128)(2,1)}, bf16[512,2048]{1,0:T(8,128)(2,1)}, f32[8,2048]{1,0:T(8,128)S(1)}) custom-call(s32[3]{0:T(128)S(1)} %pad_add_fusion.index_ref, bf16[512,2048]{1,0:T(8,128)(2,1)} %copy-done.12, bf16[256,2048]{1,0:T(8,128)(2,1)} %collective-permute-done.43.refs_1_, ...), custom_call_target="tpu_custom_call" | custom-call | bytes 503316480 | tf_op jit(solution)/shard_map/pallas_call | solution.py:1067
  590.4 8.9 add_convert_fusion
  610.3 20.8 %collective-permute-done.53 = bf16[256,2048]{1,0:T(8,128)(2,1)S(1)} collective-permute-done((bf16[256,2048]{1,0:T(8,128)(2,1)}, bf16[256,2048]{1,0:T(8,128)(2,1)S(1)}, u32[]{:S(2)}, u32[]{:S(2)}) %collective-permute-start.53) | collective-permute-done | bytes 1048608 | tf_op jit(solution)/shard_map/ppermute | solution.py:353
  631.5 5.5 maximum_select_fusion.own_ref.sib_ref.refs_2_.refs_3_
  637.0 7.6 shard_map.339.grad_ref
  646.6 12.4 %shard_map.340.refs_4_.refs_3_ = bf16[1024,768]{1,0:T(8,128)(2,1)S(1)} custom-call(s32[1,1024]{1,0:T(1,128)S(1)} %bitcast.56, bf16[1024,768]{1,0:T(8,128)(2,1)S(1)} %copy-done.61, bf16[1024,1024]{1,0:T(8,128)(2,1)S(1)} %shard_map.339.grad_ref, bf16[1024,768]{1,0:T(8,128)(2,1)S(1)} %copy-done.61, bf16[1024,768]{1,0:T(8,128)(2,1)S(1)} %copy-done.61), custom_call_target="tpu_custom_call" | custom-call | flops 171798691840 | bytes 125829120 | tf_op jit(solution)/shard_map/pallas_call | solution.py:544
  659.0 9.0 shard_map.341
  680.9 12.6 %shard_map.342.refs_4_.refs_2_ = bf16[1024,768]{1,0:T(8,128)(2,1)S(1)} custom-call(s32[1,1024]{1,0:T(1,128)S(1)} %bitcast.57, bf16[1024,768]{1,0:T(8,128)(2,1)S(1)} %copy-done.59, bf16[1024,1024]{1,0:T(8,128)(2,1)S(1)} %shard_map.339.grad_ref, bf16[1024,768]{1,0:T(8,128)(2,1)S(1)} %copy-done.59, bf16[1024,768]{1,0:T(8,128)(2,1)S(1)} %copy-done.59), custom_call_target="tpu_custom_call" | custom-call | flops 171798691840 | bytes 125829120 | tf_op jit(solution)/shard_map/pallas_call | solution.py:544
  693.5 9.0 shard_map.343
  709.0 12.6 %shard_map.344.refs_4_.refs_1_ = bf16[1024,768]{1,0:T(8,128)(2,1)S(1)} custom-call(s32[1,1024]{1,0:T(1,128)S(1)} %bitcast.58, bf16[1024,768]{1,0:T(8,128)(2,1)S(1)} %copy-done.57, bf16[1024,1024]{1,0:T(8,128)(2,1)S(1)} %shard_map.339.grad_ref, bf16[1024,768]{1,0:T(8,128)(2,1)S(1)} %copy-done.57, bf16[1024,768]{1,0:T(8,128)(2,1)S(1)} %copy-done.57), custom_call_target="tpu_custom_call" | custom-call | flops 171798691840 | bytes 125829120 | tf_op jit(solution)/shard_map/pallas_call | solution.py:544
  729.5 8.4 shard_map.345
  738.0 12.9 %shard_map.346.refs_4_.refs_0_ = bf16[1024,768]{1,0:T(8,128)(2,1)S(1)} custom-call(s32[1,1024]{1,0:T(1,128)S(1)} %bitcast.59, bf16[1024,768]{1,0:T(8,128)(2,1)S(1)} %copy-done.55, bf16[1024,1024]{1,0:T(8,128)(2,1)S(1)} %shard_map.339.grad_ref, bf16[1024,768]{1,0:T(8,128)(2,1)S(1)} %copy-done.55, bf16[1024,768]{1,0:T(8,128)(2,1)S(1)} %copy-done.55), custom_call_target="tpu_custom_call" | custom-call | flops 171798691840 | bytes 125829120 | tf_op jit(solution)/shard_map/pallas_call | solution.py:544
  754.2 8.4 shard_map.347
  775.9 16.6 %collective-permute-done.65 = bf16[256,2048]{1,0:T(8,128)(2,1)} collective-permute-done((bf16[256,2048]{1,0:T(8,128)(2,1)}, bf16[256,2048]{1,0:T(8,128)(2,1)}, u32[]{:S(2)}, u32[]{:S(2)}) %collective-permute-start.65) | collective-permute-done | bytes 1048608 | tf_op jit(solution)/shard_map/ppermute | solution.py:353
  799.2 21.2 %shard_map.348.refs_0_ = f32[1024,2048]{1,0:T(8,128)} custom-call(bf16[1024,768]{1,0:T(8,128)(2,1)S(1)} %copy-done.68, bf16[1024,768]{1,0:T(8,128)(2,1)S(1)} %copy-done.66, bf16[1024,768]{1,0:T(8,128)(2,1)S(1)} %copy-done.64, bf16[1024,768]{1,0:T(8,128)(2,1)} %copy-done.62, bf16[1024,1024]{1,0:T(8,128)(2,1)} %get-tuple-element.305.own_weight.refs_3_.refs_0_.refs_4_, ...), custom_call_target="tpu_custom_call" | custom-call | flops 257698037760 | bytes 167772160 | tf_op jit(solution)/shard_map/pallas_call | solution.py:881
  829.6 3.6 collective-permute-start.73
  837.2 8.6 shard_map.349
  847.3 9.2 collective-permute-done.73
  856.6 3.7 add_convert_fusion.5
  860.2 9.7 collective-permute-done.72
  875.3 19.1 %collective-permute-done.75 = bf16[256,1024]{1,0:T(8,128)(2,1)} collective-permute-done((bf16[256,1024]{1,0:T(8,128)(2,1)}, bf16[256,1024]{1,0:T(8,128)(2,1)}, u32[]{:S(2)}, u32[]{:S(2)}) %collective-permute-start.75) | collective-permute-done | bytes 524320 | tf_op jit(solution)/shard_map/ppermute | solution.py:353
  901.0 3.5 collective-permute-start.81
  904.5 31.5 %collective-permute-done.77 = bf16[256,2048]{1,0:T(8,128)(2,1)S(1)} collective-permute-done((bf16[256,2048]{1,0:T(8,128)(2,1)S(1)}, bf16[256,2048]{1,0:T(8,128)(2,1)S(1)}, u32[]{:S(2)}, u32[]{:S(2)}) %collective-permute-start.77) | collective-permute-done | bytes 1048608 | tf_op jit(solution)/shard_map/ppermute | solution.py:349
  951.8 4.1 collective-permute-done.84
  958.0 6.9 maximum_select_fusion.1
  967.4 13.8 %collective-permute-done.86.refs_2_ = bf16[256,2048]{1,0:T(8,128)(2,1)S(1)} collective-permute-done((bf16[256,2048]{1,0:T(8,128)(2,1)S(1)}, bf16[256,2048]{1,0:T(8,128)(2,1)S(1)}, u32[]{:S(2)}, u32[]{:S(2)}) %collective-permute-start.86) | collective-permute-done | bytes 1048608 | tf_op jit(solution)/shard_map/ppermute | solution.py:353
  985.1 8.6 shard_map.350
  996.0 5.5 maximum_select_fusion.2
  1003.4 4.7 collective-permute-done.87.refs_3_
  1008.2 5.5 shard_map.351
  (637 shorter events, 246.3 us)
Async XLA Ops:
  7.2 787.7 %reduce-scatter.5.cloned.1.call-start = ((), (), s32[]{:S(2)}) async-start(), calls=%async_computation.4 | async-start | bytes 5242880 | tf_op jit(solution)/shard_map/reduce_scatter | solution.py:1459
  39.7 32.2 %collective-permute-start.6 = (bf16[1024,1024]{1,0:T(8,128)(2,1)}, bf16[1024,1024]{1,0:T(8,128)(2,1)}, u32[]{:S(2)}, u32[]{:S(2)}) collective-permute-start(bf16[1024,1024]{1,0:T(8,128)(2,1)} %get-tuple-element.307), channel_id=1, source_target_pairs={{0,4},{4,0},{1,5},{5,1},{2,6},{6,2},{3,7},{7,3},{8,12},{12,8},{9,1... | collective-permute-start | bytes 6291464 | tf_op jit(solution)/shard_map/ppermute | solution.py:345
  39.8 27.5 %collective-permute-start.8 = (bf16[512,1024]{1,0:T(8,128)(2,1)}, bf16[512,1024]{1,0:T(8,128)(2,1)S(1)}, u32[]{:S(2)}, u32[]{:S(2)}) collective-permute-start(bf16[512,1024]{1,0:T(8,128)(2,1)} %pad_maximum_fusion.4), channel_id=1, source_target_pairs={{0,1},{1,2},{2,3},{3,0},{4,5},{5,6},{6,7},{7,4},{8,9},{9,10},{10,1... | collective-permute-start | bytes 3145736 | tf_op jit(solution)/shard_map/ppermute | solution.py:358
  40.4 26.8 %collective-permute-start.9 = (bf16[256,2048]{1,0:T(8,128)(2,1)}, bf16[256,2048]{1,0:T(8,128)(2,1)}, u32[]{:S(2)}, u32[]{:S(2)}) collective-permute-start(bf16[256,2048]{1,0:T(8,128)(2,1)} %get-tuple-element.303), channel_id=1, source_target_pairs={{0,8},{8,0},{16,24},{24,16},{1,9},{9,1},{17,25},{25,17},{2,10},{10... | collective-permute-start | bytes 3145736 | tf_op jit(solution)/shard_map/ppermute | solution.py:349
  41.9 25.4 %collective-permute-start.10 = (bf16[256,2048]{1,0:T(8,128)(2,1)}, bf16[256,2048]{1,0:T(8,128)(2,1)}, u32[]{:S(2)}, u32[]{:S(2)}) collective-permute-start(bf16[256,2048]{1,0:T(8,128)(2,1)} %get-tuple-element.303), channel_id=1, source_target_pairs={{0,16},{16,0},{8,24},{24,8},{1,17},{17,1},{9,25},{25,9},{2,18},{18... | collective-permute-start | bytes 3145736 | tf_op jit(solution)/shard_map/ppermute | solution.py:353
  85.6 26.0 %collective-permute-start.11 = (bf16[512,1024]{1,0:T(8,128)(2,1)S(1)}, bf16[512,1024]{1,0:T(8,128)(2,1)S(1)}, u32[]{:S(2)}, u32[]{:S(2)}) collective-permute-start(bf16[512,1024]{1,0:T(8,128)(2,1)S(1)} %collective-permute-done.8.refs_0_), channel_id=1, source_target_pairs={{0,8},{8,0},{16,24},{24,16},{1,9},{9,1},{17,25},{25,17},{2,10},{10... | collective-permute-start | bytes 3145736 | tf_op jit(solution)/shard_map/ppermute | solution.py:349
  87.1 24.4 %collective-permute-start.12 = (bf16[512,1024]{1,0:T(8,128)(2,1)S(1)}, bf16[512,1024]{1,0:T(8,128)(2,1)S(1)}, u32[]{:S(2)}, u32[]{:S(2)}) collective-permute-start(bf16[512,1024]{1,0:T(8,128)(2,1)S(1)} %collective-permute-done.8.refs_0_), channel_id=1, source_target_pairs={{0,16},{16,0},{8,24},{24,8},{1,17},{17,1},{9,25},{25,9},{2,18},{18... | collective-permute-start | bytes 3145736 | tf_op jit(solution)/shard_map/ppermute | solution.py:353
  88.6 26.1 %collective-permute-start.15 = (bf16[512,1024]{1,0:T(8,128)(2,1)S(1)}, bf16[512,1024]{1,0:T(8,128)(2,1)S(1)}, u32[]{:S(2)}, u32[]{:S(2)}) collective-permute-start(bf16[512,1024]{1,0:T(8,128)(2,1)S(1)} %collective-permute-done.8.refs_0_), channel_id=1, source_target_pairs={{0,1},{1,2},{2,3},{3,0},{4,5},{5,6},{6,7},{7,4},{8,9},{9,10},{10,1... | collective-permute-start | bytes 3145736 | tf_op jit(solution)/shard_map/ppermute | solution.py:358
  142.8 45.8 %collective-permute-start.21 = (bf16[1024,1024]{1,0:T(8,128)(2,1)}, bf16[1024,1024]{1,0:T(8,128)(2,1)S(1)}, u32[]{:S(2)}, u32[]{:S(2)}) collective-permute-start(bf16[1024,1024]{1,0:T(8,128)(2,1)} %shard_map.316), channel_id=1, source_target_pairs={{0,4},{4,0},{1,5},{5,1},{2,6},{6,2},{3,7},{7,3},{8,12},{12,8},{9,1... | collective-permute-start | bytes 6291464 | tf_op jit(solution)/shard_map/ppermute | solution.py:345
  142.8 27.5 %collective-permute-start.18 = (bf16[512,1024]{1,0:T(8,128)(2,1)S(1)}, bf16[512,1024]{1,0:T(8,128)(2,1)}, u32[]{:S(2)}, u32[]{:S(2)}) collective-permute-start(bf16[512,1024]{1,0:T(8,128)(2,1)S(1)} %copy-done.32), channel_id=1, source_target_pairs={{0,1},{1,2},{2,3},{3,0},{4,5},{5,6},{6,7},{7,4},{8,9},{9,10},{10,1... | collective-permute-start | bytes 3145736 | tf_op jit(solution)/shard_map/ppermute | solution.py:358
  142.9 27.4 %collective-permute-start.17 = (bf16[512,1024]{1,0:T(8,128)(2,1)S(1)}, bf16[512,1024]{1,0:T(8,128)(2,1)S(1)}, u32[]{:S(2)}, u32[]{:S(2)}) collective-permute-start(bf16[512,1024]{1,0:T(8,128)(2,1)S(1)} %copy-done.32), channel_id=1, source_target_pairs={{0,16},{16,0},{8,24},{24,8},{1,17},{17,1},{9,25},{25,9},{2,18},{18... | collective-permute-start | bytes 3145736 | tf_op jit(solution)/shard_map/ppermute | solution.py:353
  143.5 26.8 %collective-permute-start.16 = (bf16[512,1024]{1,0:T(8,128)(2,1)S(1)}, bf16[512,1024]{1,0:T(8,128)(2,1)S(1)}, u32[]{:S(2)}, u32[]{:S(2)}) collective-permute-start(bf16[512,1024]{1,0:T(8,128)(2,1)S(1)} %copy-done.32), channel_id=1, source_target_pairs={{0,8},{8,0},{16,24},{24,16},{1,9},{9,1},{17,25},{25,17},{2,10},{10... | collective-permute-start | bytes 3145736 | tf_op jit(solution)/shard_map/ppermute | solution.py:349
  171.5 49.0 %collective-permute-start.24 = (bf16[1024,1024]{1,0:T(8,128)(2,1)}, bf16[1024,1024]{1,0:T(8,128)(2,1)}, u32[]{:S(2)}, u32[]{:S(2)}) collective-permute-start(bf16[1024,1024]{1,0:T(8,128)(2,1)} %shard_map.316), channel_id=1, source_target_pairs={{0,1},{1,2},{2,3},{3,0},{4,5},{5,6},{6,7},{7,4},{8,9},{9,10},{10,1... | collective-permute-start | bytes 6291464 | tf_op jit(solution)/shard_map/ppermute | solution.py:358
  184.2 37.4 %collective-permute-start.22 = (bf16[512,1024]{1,0:T(8,128)(2,1)}, bf16[512,1024]{1,0:T(8,128)(2,1)}, u32[]{:S(2)}, u32[]{:S(2)}) collective-permute-start(bf16[512,1024]{1,0:T(8,128)(2,1)} %collective-permute-done.18.refs_0_), channel_id=1, source_target_pairs={{0,8},{8,0},{16,24},{24,16},{1,9},{9,1},{17,25},{25,17},{2,10},{10... | collective-permute-start | bytes 3145736 | tf_op jit(solution)/shard_map/ppermute | solution.py:349
  184.7 35.8 %collective-permute-start.23 = (bf16[512,1024]{1,0:T(8,128)(2,1)}, bf16[512,1024]{1,0:T(8,128)(2,1)}, u32[]{:S(2)}, u32[]{:S(2)}) collective-permute-start(bf16[512,1024]{1,0:T(8,128)(2,1)} %collective-permute-done.18.refs_0_), channel_id=1, source_target_pairs={{0,16},{16,0},{8,24},{24,8},{1,17},{17,1},{9,25},{25,9},{2,18},{18... | collective-permute-start | bytes 3145736 | tf_op jit(solution)/shard_map/ppermute | solution.py:353
  220.5 31.4 %collective-permute-start.27 = (bf16[1024,1024]{1,0:T(8,128)(2,1)}, bf16[1024,1024]{1,0:T(8,128)(2,1)S(1)}, u32[]{:S(2)}, u32[]{:S(2)}) collective-permute-start(bf16[1024,1024]{1,0:T(8,128)(2,1)} %collective-permute-done.24), channel_id=1, source_target_pairs={{0,4},{4,0},{1,5},{5,1},{2,6},{6,2},{3,7},{7,3},{8,12},{12,8},{9,1... | collective-permute-start | bytes 6291464 | tf_op jit(solution)/shard_map/ppermute | solution.py:345
  240.3 48.6 %collective-permute-start.30 = (bf16[1024,1024]{1,0:T(8,128)(2,1)}, bf16[1024,1024]{1,0:T(8,128)(2,1)}, u32[]{:S(2)}, u32[]{:S(2)}) collective-permute-start(bf16[1024,1024]{1,0:T(8,128)(2,1)} %collective-permute-done.24), channel_id=1, source_target_pairs={{0,1},{1,2},{2,3},{3,0},{4,5},{5,6},{6,7},{7,4},{8,9},{9,10},{10,1... | collective-permute-start | bytes 6291464 | tf_op jit(solution)/shard_map/ppermute | solution.py:358
  260.4 28.6 %collective-permute-start.31 = (bf16[256,2048]{1,0:T(8,128)(2,1)}, bf16[256,2048]{1,0:T(8,128)(2,1)}, u32[]{:S(2)}, u32[]{:S(2)}) collective-permute-start(bf16[256,2048]{1,0:T(8,128)(2,1)} %get-tuple-element.381), channel_id=1, source_target_pairs={{0,8},{8,0},{16,24},{24,16},{1,9},{9,1},{17,25},{25,17},{2,10},{10... | collective-permute-start | bytes 3145736 | tf_op jit(solution)/shard_map/ppermute | solution.py:349
  261.9 27.0 %collective-permute-start.32 = (bf16[256,2048]{1,0:T(8,128)(2,1)}, bf16[256,2048]{1,0:T(8,128)(2,1)}, u32[]{:S(2)}, u32[]{:S(2)}) collective-permute-start(bf16[256,2048]{1,0:T(8,128)(2,1)} %get-tuple-element.381), channel_id=1, source_target_pairs={{0,16},{16,0},{8,24},{24,8},{1,17},{17,1},{9,25},{25,9},{2,18},{18... | collective-permute-start | bytes 3145736 | tf_op jit(solution)/shard_map/ppermute | solution.py:353
  289.0 23.2 %collective-permute-start.33 = (bf16[1024,1024]{1,0:T(8,128)(2,1)}, bf16[1024,1024]{1,0:T(8,128)(2,1)S(1)}, u32[]{:S(2)}, u32[]{:S(2)}) collective-permute-start(bf16[1024,1024]{1,0:T(8,128)(2,1)} %collective-permute-done.30), channel_id=1, source_target_pairs={{0,4},{4,0},{1,5},{5,1},{2,6},{6,2},{3,7},{7,3},{8,12},{12,8},{9,1... | collective-permute-start | bytes 6291464 | tf_op jit(solution)/shard_map/ppermute | solution.py:345
  300.2 50.1 %collective-permute-start.35 = (bf16[1024,1024]{1,0:T(8,128)(2,1)}, bf16[1024,1024]{1,0:T(8,128)(2,1)S(1)}, u32[]{:S(2)}, u32[]{:S(2)}) collective-permute-start(bf16[1024,1024]{1,0:T(8,128)(2,1)} %collective-permute-done.30), channel_id=1, source_target_pairs={{0,1},{1,2},{2,3},{3,0},{4,5},{5,6},{6,7},{7,4},{8,9},{9,10},{10,1... | collective-permute-start | bytes 6291464 | tf_op jit(solution)/shard_map/ppermute | solution.py:358
  305.4 49.8 %collective-permute-start.37 = (bf16[128,2048]{1,0:T(8,128)(2,1)S(1)}, bf16[128,2048]{1,0:T(8,128)(2,1)S(1)}, u32[]{:S(2)}, u32[]{:S(2)}) collective-permute-start(bf16[128,2048]{1,0:T(8,128)(2,1)S(1)} %slice.441), channel_id=1, source_target_pairs={{0,8},{8,0},{16,24},{24,16},{1,9},{9,1},{17,25},{25,17},{2,10},{10... | collective-permute-start | bytes 1572872 | tf_op jit(solution)/shard_map/ppermute | solution.py:349
  306.0 48.3 %collective-permute-start.36 = (bf16[128,2048]{1,0:T(8,128)(2,1)S(1)}, bf16[128,2048]{1,0:T(8,128)(2,1)S(1)}, u32[]{:S(2)}, u32[]{:S(2)}) collective-permute-start(bf16[128,2048]{1,0:T(8,128)(2,1)S(1)} %slice.442), channel_id=1, source_target_pairs={{0,16},{16,0},{8,24},{24,8},{1,17},{17,1},{9,25},{25,9},{2,18},{18... | collective-permute-start | bytes 1572872 | tf_op jit(solution)/shard_map/ppermute | solution.py:353
  317.9 49.5 %collective-permute-start.39 = (bf16[512,2048]{1,0:T(8,128)(2,1)S(1)}, bf16[512,2048]{1,0:T(8,128)(2,1)S(1)}, u32[]{:S(2)}, u32[]{:S(2)}) collective-permute-start(bf16[512,2048]{1,0:T(8,128)(2,1)S(1)} %get-tuple-element.400.refs_0_.refs_1_), channel_id=1, source_target_pairs={{0,8},{8,0},{16,24},{24,16},{1,9},{9,1},{17,25},{25,17},{2,10},{10... | collective-permute-start | bytes 6291464 | tf_op jit(solution)/shard_map/ppermute | solution.py:349
  319.5 46.8 %collective-permute-start.40 = (bf16[512,2048]{1,0:T(8,128)(2,1)S(1)}, bf16[512,2048]{1,0:T(8,128)(2,1)S(1)}, u32[]{:S(2)}, u32[]{:S(2)}) collective-permute-start(bf16[512,2048]{1,0:T(8,128)(2,1)S(1)} %get-tuple-element.400.refs_0_.refs_1_), channel_id=1, source_target_pairs={{0,16},{16,0},{8,24},{24,8},{1,17},{17,1},{9,25},{25,9},{2,18},{18... | collective-permute-start | bytes 6291464 | tf_op jit(solution)/shard_map/ppermute | solution.py:353
  404.5 63.8 %collective-permute-start.42 = (bf16[256,2048]{1,0:T(8,128)(2,1)}, bf16[256,2048]{1,0:T(8,128)(2,1)}, u32[]{:S(2)}, u32[]{:S(2)}) collective-permute-start(bf16[256,2048]{1,0:T(8,128)(2,1)} %slice.446), channel_id=1, source_target_pairs={{0,8},{8,0},{16,24},{24,16},{1,9},{9,1},{17,25},{25,17},{2,10},{10... | collective-permute-start | bytes 3145736 | tf_op jit(solution)/shard_map/ppermute | solution.py:349
  405.0 63.4 %collective-permute-start.41 = (bf16[256,2048]{1,0:T(8,128)(2,1)}, bf16[256,2048]{1,0:T(8,128)(2,1)}, u32[]{:S(2)}, u32[]{:S(2)}) collective-permute-start(bf16[256,2048]{1,0:T(8,128)(2,1)} %slice.447), channel_id=1, source_target_pairs={{0,16},{16,0},{8,24},{24,8},{1,17},{17,1},{9,25},{25,9},{2,18},{18... | collective-permute-start | bytes 3145736 | tf_op jit(solution)/shard_map/ppermute | solution.py:353
  468.4 37.4 %collective-permute-start.43 = (bf16[256,2048]{1,0:T(8,128)(2,1)}, bf16[256,2048]{1,0:T(8,128)(2,1)}, u32[]{:S(2)}, u32[]{:S(2)}) collective-permute-start(bf16[256,2048]{1,0:T(8,128)(2,1)} %slice.348), channel_id=1, source_target_pairs={{0,8},{8,0},{16,24},{24,16},{1,9},{9,1},{17,25},{25,17},{2,10},{10... | collective-permute-start | bytes 3145736 | tf_op jit(solution)/shard_map/ppermute | solution.py:349
  469.8 35.9 %collective-permute-start.45 = (bf16[256,2048]{1,0:T(8,128)(2,1)}, bf16[256,2048]{1,0:T(8,128)(2,1)}, u32[]{:S(2)}, u32[]{:S(2)}) collective-permute-start(bf16[256,2048]{1,0:T(8,128)(2,1)} %slice.349), channel_id=1, source_target_pairs={{0,16},{16,0},{8,24},{24,8},{1,17},{17,1},{9,25},{25,9},{2,18},{18... | collective-permute-start | bytes 3145736 | tf_op jit(solution)/shard_map/ppermute | solution.py:353
  505.7 33.3 %collective-permute-start.46 = (bf16[256,2048]{1,0:T(8,128)(2,1)}, bf16[256,2048]{1,0:T(8,128)(2,1)}, u32[]{:S(2)}, u32[]{:S(2)}) collective-permute-start(bf16[256,2048]{1,0:T(8,128)(2,1)} %get-tuple-element.424), channel_id=1, source_target_pairs={{0,16},{16,0},{8,24},{24,8},{1,17},{17,1},{9,25},{25,9},{2,18},{18... | collective-permute-start | bytes 3145736 | tf_op jit(solution)/shard_map/ppermute | solution.py:353
  506.3 32.7 %collective-permute-start.44 = (bf16[256,2048]{1,0:T(8,128)(2,1)}, bf16[256,2048]{1,0:T(8,128)(2,1)}, u32[]{:S(2)}, u32[]{:S(2)}) collective-permute-start(bf16[256,2048]{1,0:T(8,128)(2,1)} %get-tuple-element.422), channel_id=1, source_target_pairs={{0,8},{8,0},{16,24},{24,16},{1,9},{9,1},{17,25},{25,17},{2,10},{10... | collective-permute-start | bytes 3145736 | tf_op jit(solution)/shard_map/ppermute | solution.py:349
  539.0 37.7 %collective-permute-start.48 = (bf16[4,1024,1024]{2,1,0:T(8,128)(2,1)}, bf16[4,1024,1024]{2,1,0:T(8,128)(2,1)}, u32[]{:S(2)}, u32[]{:S(2)}) collective-permute-start(bf16[4,1024,1024]{2,1,0:T(8,128)(2,1)} %shard_map.336), channel_id=1, source_target_pairs={{0,4},{4,0},{1,5},{5,1},{2,6},{6,2},{3,7},{7,3},{8,12},{12,8},{9,1... | collective-permute-start | bytes 25165832 | tf_op jit(solution)/shard_map/ppermute | solution.py:345
  542.9 33.8 %collective-permute-start.49 = (bf16[256,2048]{1,0:T(8,128)(2,1)}, bf16[256,2048]{1,0:T(8,128)(2,1)}, u32[]{:S(2)}, u32[]{:S(2)}) collective-permute-start(bf16[256,2048]{1,0:T(8,128)(2,1)} %get-tuple-element.433), channel_id=1, source_target_pairs={{0,16},{16,0},{8,24},{24,8},{1,17},{17,1},{9,25},{25,9},{2,18},{18... | collective-permute-start | bytes 3145736 | tf_op jit(solution)/shard_map/ppermute | solution.py:353
  543.8 33.0 %collective-permute-start.47 = (bf16[256,2048]{1,0:T(8,128)(2,1)}, bf16[256,2048]{1,0:T(8,128)(2,1)}, u32[]{:S(2)}, u32[]{:S(2)}) collective-permute-start(bf16[256,2048]{1,0:T(8,128)(2,1)} %get-tuple-element.429), channel_id=1, source_target_pairs={{0,8},{8,0},{16,24},{24,16},{1,9},{9,1},{17,25},{25,17},{2,10},{10... | collective-permute-start | bytes 3145736 | tf_op jit(solution)/shard_map/ppermute | solution.py:349
  599.4 237.7 %reduce-scatter.3.cloned.1.call-start = ((), (), s32[]{:S(2)}) async-start(), calls=%async_computation.2 | async-start | bytes 5242880 | tf_op jit(solution)/shard_map/reduce_scatter | solution.py:1459
  599.6 31.9 %collective-permute-start.51 = (bf16[512,2048]{1,0:T(8,128)(2,1)}, bf16[512,2048]{1,0:T(8,128)(2,1)}, u32[]{:S(2)}, u32[]{:S(2)}) collective-permute-start(bf16[512,2048]{1,0:T(8,128)(2,1)} %get-tuple-element.447), channel_id=1, source_target_pairs={{0,4},{4,0},{1,5},{5,1},{2,6},{6,2},{3,7},{7,3},{8,12},{12,8},{9,1... | collective-permute-start | bytes 6291464 | tf_op jit(solution)/shard_map/ppermute | solution.py:345
  605.7 25.4 %collective-permute-start.53 = (bf16[256,2048]{1,0:T(8,128)(2,1)}, bf16[256,2048]{1,0:T(8,128)(2,1)S(1)}, u32[]{:S(2)}, u32[]{:S(2)}) collective-permute-start(bf16[256,2048]{1,0:T(8,128)(2,1)} %slice.355), channel_id=1, source_target_pairs={{0,16},{16,0},{8,24},{24,8},{1,17},{17,1},{9,25},{25,9},{2,18},{18... | collective-permute-start | bytes 3145736 | tf_op jit(solution)/shard_map/ppermute | solution.py:353
  606.4 25.1 %collective-permute-start.50 = (bf16[256,2048]{1,0:T(8,128)(2,1)}, bf16[256,2048]{1,0:T(8,128)(2,1)}, u32[]{:S(2)}, u32[]{:S(2)}) collective-permute-start(bf16[256,2048]{1,0:T(8,128)(2,1)} %slice.346), channel_id=1, source_target_pairs={{0,8},{8,0},{16,24},{24,16},{1,9},{9,1},{17,25},{25,17},{2,10},{10... | collective-permute-start | bytes 3145736 | tf_op jit(solution)/shard_map/ppermute | solution.py:349
  610.2 372.6 %all-gather.5.cloned.1.call-start = ((), (), s32[]{:S(2)}) async-start(), calls=%async_computation.5 | async-start | bytes 5242880 | tf_op jit(solution)/shard_map/all_gather | solution.py:1460
  644.6 27.9 %collective-permute-start.52 = (bf16[256,2048]{1,0:T(8,128)(2,1)}, bf16[256,2048]{1,0:T(8,128)(2,1)}, u32[]{:S(2)}, u32[]{:S(2)}) collective-permute-start(bf16[256,2048]{1,0:T(8,128)(2,1)} %get-tuple-element.451), channel_id=1, source_target_pairs={{0,8},{8,0},{16,24},{24,16},{1,9},{9,1},{17,25},{25,17},{2,10},{10... | collective-permute-start | bytes 3145736 | tf_op jit(solution)/shard_map/ppermute | solution.py:349
  645.7 26.9 %collective-permute-start.54 = (bf16[256,2048]{1,0:T(8,128)(2,1)}, bf16[256,2048]{1,0:T(8,128)(2,1)}, u32[]{:S(2)}, u32[]{:S(2)}) collective-permute-start(bf16[256,2048]{1,0:T(8,128)(2,1)} %get-tuple-element.453), channel_id=1, source_target_pairs={{0,16},{16,0},{8,24},{24,8},{1,17},{17,1},{9,25},{25,9},{2,18},{18... | collective-permute-start | bytes 3145736 | tf_op jit(solution)/shard_map/ppermute | solution.py:353
  678.6 28.5 %collective-permute-start.56 = (bf16[256,2048]{1,0:T(8,128)(2,1)}, bf16[256,2048]{1,0:T(8,128)(2,1)}, u32[]{:S(2)}, u32[]{:S(2)}) collective-permute-start(bf16[256,2048]{1,0:T(8,128)(2,1)} %add_convert_fusion.8), channel_id=1, source_target_pairs={{0,8},{8,0},{16,24},{24,16},{1,9},{9,1},{17,25},{25,17},{2,10},{10... | collective-permute-start | bytes 3145736 | tf_op jit(solution)/shard_map/ppermute | solution.py:349
  680.2 26.9 %collective-permute-start.55 = (bf16[256,2048]{1,0:T(8,128)(2,1)}, bf16[256,2048]{1,0:T(8,128)(2,1)}, u32[]{:S(2)}, u32[]{:S(2)}) collective-permute-start(bf16[256,2048]{1,0:T(8,128)(2,1)} %add_convert_fusion.9), channel_id=1, source_target_pairs={{0,16},{16,0},{8,24},{24,8},{1,17},{17,1},{9,25},{25,9},{2,18},{18... | collective-permute-start | bytes 3145736 | tf_op jit(solution)/shard_map/ppermute | solution.py:353
  727.3 24.8 %collective-permute-start.60 = (bf16[256,2048]{1,0:T(8,128)(2,1)}, bf16[256,2048]{1,0:T(8,128)(2,1)}, u32[]{:S(2)}, u32[]{:S(2)}) collective-permute-start(bf16[256,2048]{1,0:T(8,128)(2,1)} %pad_maximum_fusion.5), channel_id=1, source_target_pairs={{0,8},{8,0},{16,24},{24,16},{1,9},{9,1},{17,25},{25,17},{2,10},{10... | collective-permute-start | bytes 3145736 | tf_op jit(solution)/shard_map/ppermute | solution.py:349
  728.9 23.2 %collective-permute-start.61 = (bf16[256,2048]{1,0:T(8,128)(2,1)}, bf16[256,2048]{1,0:T(8,128)(2,1)}, u32[]{:S(2)}, u32[]{:S(2)}) collective-permute-start(bf16[256,2048]{1,0:T(8,128)(2,1)} %pad_maximum_fusion.6), channel_id=1, source_target_pairs={{0,16},{16,0},{8,24},{24,8},{1,17},{17,1},{9,25},{25,9},{2,18},{18... | collective-permute-start | bytes 3145736 | tf_op jit(solution)/shard_map/ppermute | solution.py:353
  768.7 23.8 %collective-permute-start.64 = (bf16[256,2048]{1,0:T(8,128)(2,1)}, bf16[256,2048]{1,0:T(8,128)(2,1)}, u32[]{:S(2)}, u32[]{:S(2)}) collective-permute-start(bf16[256,2048]{1,0:T(8,128)(2,1)} %pad_maximum_fusion.7), channel_id=1, source_target_pairs={{0,8},{8,0},{16,24},{24,16},{1,9},{9,1},{17,25},{25,17},{2,10},{10... | collective-permute-start | bytes 3145736 | tf_op jit(solution)/shard_map/ppermute | solution.py:349
  769.2 23.3 %collective-permute-start.65 = (bf16[256,2048]{1,0:T(8,128)(2,1)}, bf16[256,2048]{1,0:T(8,128)(2,1)}, u32[]{:S(2)}, u32[]{:S(2)}) collective-permute-start(bf16[256,2048]{1,0:T(8,128)(2,1)} %pad_maximum_fusion.8), channel_id=1, source_target_pairs={{0,16},{16,0},{8,24},{24,8},{1,17},{17,1},{9,25},{25,9},{2,18},{18... | collective-permute-start | bytes 3145736 | tf_op jit(solution)/shard_map/ppermute | solution.py:353
  792.5 32.1 %collective-permute-start.67 = (bf16[256,1024]{1,0:T(8,128)(2,1)}, bf16[256,1024]{1,0:T(8,128)(2,1)}, u32[]{:S(2)}, u32[]{:S(2)}) collective-permute-start(bf16[256,1024]{1,0:T(8,128)(2,1)} %get-tuple-element.498), channel_id=1, source_target_pairs={{0,16},{16,0},{8,24},{24,8},{1,17},{17,1},{9,25},{25,9},{2,18},{18... | collective-permute-start | bytes 1572872 | tf_op jit(solution)/shard_map/ppermute | solution.py:353
  793.5 31.1 %collective-permute-start.66 = (bf16[256,1024]{1,0:T(8,128)(2,1)}, bf16[256,1024]{1,0:T(8,128)(2,1)}, u32[]{:S(2)}, u32[]{:S(2)}) collective-permute-start(bf16[256,1024]{1,0:T(8,128)(2,1)} %get-tuple-element.495), channel_id=1, source_target_pairs={{0,8},{8,0},{16,24},{24,16},{1,9},{9,1},{17,25},{25,17},{2,10},{10... | collective-permute-start | bytes 1572872 | tf_op jit(solution)/shard_map/ppermute | solution.py:349
  794.9 188.0 %all-gather.3.cloned.1.call-start = ((), (), s32[]{:S(2)}) async-start(), calls=%async_computation.3 | async-start | bytes 5242880 | tf_op jit(solution)/shard_map/all_gather | solution.py:1460
  829.6 27.0 %collective-permute-start.73 = (bf16[256,2048]{1,0:T(8,128)(2,1)}, bf16[256,2048]{1,0:T(8,128)(2,1)}, u32[]{:S(2)}, u32[]{:S(2)}) collective-permute-start(bf16[256,2048]{1,0:T(8,128)(2,1)} %add_convert_fusion.7), channel_id=1, source_target_pairs={{0,3},{1,0},{2,1},{3,2},{4,7},{5,4},{6,5},{7,6},{8,11},{9,8},{10,9... | collective-permute-start | bytes 3145736 | tf_op jit(solution)/shard_map/ppermute | solution.py:363
  834.4 35.5 %collective-permute-start.72 = (bf16[256,2048]{1,0:T(8,128)(2,1)}, bf16[256,2048]{1,0:T(8,128)(2,1)}, u32[]{:S(2)}, u32[]{:S(2)}) collective-permute-start(bf16[256,2048]{1,0:T(8,128)(2,1)} %pad_maximum_fusion.10), channel_id=1, source_target_pairs={{0,16},{16,0},{8,24},{24,8},{1,17},{17,1},{9,25},{25,9},{2,18},{18... | collective-permute-start | bytes 3145736 | tf_op jit(solution)/shard_map/ppermute | solution.py:353
  835.2 34.7 %collective-permute-start.71 = (bf16[256,2048]{1,0:T(8,128)(2,1)}, bf16[256,2048]{1,0:T(8,128)(2,1)}, u32[]{:S(2)}, u32[]{:S(2)}) collective-permute-start(bf16[256,2048]{1,0:T(8,128)(2,1)} %pad_maximum_fusion.9), channel_id=1, source_target_pairs={{0,8},{8,0},{16,24},{24,16},{1,9},{9,1},{17,25},{25,17},{2,10},{10... | collective-permute-start | bytes 3145736 | tf_op jit(solution)/shard_map/ppermute | solution.py:349
  847.2 28.1 %collective-permute-start.70 = (f32[20480]{0:T(1024)S(1)}, f32[20480]{0:T(1024)S(1)}, u32[]{:S(2)}, u32[]{:S(2)}) collective-permute-start(f32[20480]{0:T(1024)S(1)} %pad_maximum_fusion.14), channel_id=1, source_target_pairs={{0,4},{4,0},{1,5},{5,1},{2,6},{6,2},{3,7},{7,3},{8,12},{12,8},{9,1... | collective-permute-start | bytes 245768 | tf_op jit(solution)/shard_map/ppermute | solution.py:345
  869.9 24.5 %collective-permute-start.74 = (bf16[256,1024]{1,0:T(8,128)(2,1)}, bf16[256,1024]{1,0:T(8,128)(2,1)S(1)}, u32[]{:S(2)}, u32[]{:S(2)}) collective-permute-start(bf16[256,1024]{1,0:T(8,128)(2,1)} %get-tuple-element.529), channel_id=1, source_target_pairs={{0,8},{8,0},{16,24},{24,16},{1,9},{9,1},{17,25},{25,17},{2,10},{10... | collective-permute-start | bytes 1572872 | tf_op jit(solution)/shard_map/ppermute | solution.py:349
  871.4 23.0 %collective-permute-start.75 = (bf16[256,1024]{1,0:T(8,128)(2,1)}, bf16[256,1024]{1,0:T(8,128)(2,1)}, u32[]{:S(2)}, u32[]{:S(2)}) collective-permute-start(bf16[256,1024]{1,0:T(8,128)(2,1)} %get-tuple-element.532), channel_id=1, source_target_pairs={{0,16},{16,0},{8,24},{24,8},{1,17},{17,1},{9,25},{25,9},{2,18},{18... | collective-permute-start | bytes 1572872 | tf_op jit(solution)/shard_map/ppermute | solution.py:353
  872.0 26.4 %collective-permute-start.76 = (bf16[256,2048]{1,0:T(8,128)(2,1)}, bf16[256,2048]{1,0:T(8,128)(2,1)}, u32[]{:S(2)}, u32[]{:S(2)}) collective-permute-start(bf16[256,2048]{1,0:T(8,128)(2,1)} %add_convert_fusion.5), channel_id=1, source_target_pairs={{0,3},{1,0},{2,1},{3,2},{4,7},{5,4},{6,5},{7,6},{8,11},{9,8},{10,9... | collective-permute-start | bytes 3145736 | tf_op jit(solution)/shard_map/ppermute | solution.py:363
  895.9 40.1 %collective-permute-start.77 = (bf16[256,2048]{1,0:T(8,128)(2,1)S(1)}, bf16[256,2048]{1,0:T(8,128)(2,1)S(1)}, u32[]{:S(2)}, u32[]{:S(2)}) collective-permute-start(bf16[256,2048]{1,0:T(8,128)(2,1)S(1)} %pad_maximum_fusion.11), channel_id=1, source_target_pairs={{0,8},{8,0},{16,24},{24,16},{1,9},{9,1},{17,25},{25,17},{2,10},{10... | collective-permute-start | bytes 3145736 | tf_op jit(solution)/shard_map/ppermute | solution.py:349
  896.9 44.9 %collective-permute-start.79 = (bf16[256,2048]{1,0:T(8,128)(2,1)S(1)}, bf16[256,2048]{1,0:T(8,128)(2,1)S(1)}, u32[]{:S(2)}, u32[]{:S(2)}) collective-permute-start(bf16[256,2048]{1,0:T(8,128)(2,1)S(1)} %pad_maximum_fusion.12), channel_id=1, source_target_pairs={{0,16},{16,0},{8,24},{24,8},{1,17},{17,1},{9,25},{25,9},{2,18},{18... | collective-permute-start | bytes 3145736 | tf_op jit(solution)/shard_map/ppermute | solution.py:353
  901.0 45.4 %collective-permute-start.81 = (bf16[256,2048]{1,0:T(8,128)(2,1)S(1)}, bf16[256,2048]{1,0:T(8,128)(2,1)S(1)}, u32[]{:S(2)}, u32[]{:S(2)}) collective-permute-start(bf16[256,2048]{1,0:T(8,128)(2,1)S(1)} %add_convert_fusion.3), channel_id=1, source_target_pairs={{0,3},{1,0},{2,1},{3,2},{4,7},{5,4},{6,5},{7,6},{8,11},{9,8},{10,9... | collective-permute-start | bytes 3145736 | tf_op jit(solution)/shard_map/ppermute | solution.py:363
  950.2 45.7 %collective-permute-start.69 = (f32[512,1024]{1,0:T(8,128)}, f32[512,1024]{1,0:T(8,128)}, u32[]{:S(2)}, u32[]{:S(2)}) collective-permute-start(f32[512,1024]{1,0:T(8,128)} %get-tuple-element.517), channel_id=1, source_target_pairs={{0,4},{4,0},{1,5},{5,1},{2,6},{6,2},{3,7},{7,3},{8,12},{12,8},{9,1... | collective-permute-start | bytes 6291464 | tf_op jit(solution)/shard_map/ppermute | solution.py:345
  955.9 25.3 %collective-permute-start.86 = (bf16[256,2048]{1,0:T(8,128)(2,1)S(1)}, bf16[256,2048]{1,0:T(8,128)(2,1)S(1)}, u32[]{:S(2)}, u32[]{:S(2)}) collective-permute-start(bf16[256,2048]{1,0:T(8,128)(2,1)S(1)} %pad_maximum_fusion.13.refs_0_), channel_id=1, source_target_pairs={{0,16},{16,0},{8,24},{24,8},{1,17},{17,1},{9,25},{25,9},{2,18},{18... | collective-permute-start | bytes 3145736 | tf_op jit(solution)/shard_map/ppermute | solution.py:353
  956.9 25.1 %collective-permute-start.85 = (bf16[256,2048]{1,0:T(8,128)(2,1)S(1)}, bf16[256,2048]{1,0:T(8,128)(2,1)S(1)}, u32[]{:S(2)}, u32[]{:S(2)}) collective-permute-start(bf16[256,2048]{1,0:T(8,128)(2,1)S(1)} %pad_maximum_fusion.13.refs_0_), channel_id=1, source_target_pairs={{0,8},{8,0},{16,24},{24,16},{1,9},{9,1},{17,25},{25,17},{2,10},{10... | collective-permute-start | bytes 3145736 | tf_op jit(solution)/shard_map/ppermute | solution.py:349
  964.9 36.5 %collective-permute-start.83 = (f32[20480]{0:T(1024)S(1)}, f32[20480]{0:T(1024)S(1)}, u32[]{:S(2)}, u32[]{:S(2)}) collective-permute-start(f32[20480]{0:T(1024)S(1)} %add.248), channel_id=1, source_target_pairs={{0,2},{1,3},{2,0},{3,1},{4,6},{5,7},{6,4},{7,5},{8,10},{9,11},{10,... | collective-permute-start | bytes 245768 | tf_op jit(solution)/shard_map/ppermute | solution.py:1564
  (182 other events, 2109.4 us)
Sparse Core Ops, SparseCore 0:
  599.5 76.4 reduce-scatter.4
  678.4 77.2 reduce-scatter.2
  795.0 62.5 all-gather.4
  859.3 83.0 all-gather.2

commit v6 on v5

--- a/solution.py
+++ b/solution.py
@@ -563,50 +563,39 @@
 gelu_cubic = 0.044715
 
 
-def ffn_kernel(*refs):
-    normed, grads, pieces = [r[...] for r in refs[:2]], [r[...] for r in refs[2:4]], refs[4:6]
+def ffn_kernel(index_ref, *refs):
+    normed, grads, pieces = refs[:2], refs[2:4], [r.at[0] for r in refs[4:6]]
     bias_ref, rows_ref, sum_ref, grad_out, down_out, grad_acc, down_acc = refs[6:]
     step = pl.program_id(0)
     width = normed[0].shape[1]
-    unit = pieces[0].shape[2] // 4
-
-    def weight(half, units, kind):
-        at = (2 * (units ^ half) + kind) * unit
-        return pieces[half][0, :, at : at + unit]
-
-    ups, downs = [None] * 2, [None] * 2
-    for units in range(2):
-        pre = mm(normed[0], weight(0, units, 0), 1, 0) + mm(normed[1], weight(1, units, 0), 1, 0)
-        act_grad = mm(grads[0], weight(0, units, 1), 1, 0) + mm(grads[1], weight(1, units, 1), 1, 0)
-        span = slice(units * unit, (units + 1) * unit)
-        pre = pre + bias_ref[0, :, span]
-        square = pre * pre
-        bent = jnp.tanh(gelu_scale * pre * (1.0 + gelu_cubic * square))
-        half = 0.5 * (1.0 + bent)
-        slope = half + 0.5 * gelu_scale * pre * (1.0 - bent * bent) * (1.0 + 3.0 * gelu_cubic * square)
-        act = (pre * half).astype(jnp.bfloat16)
-        pre_grad = (act_grad * slope).astype(jnp.bfloat16)
-        rows_ref[:, span] = act
-        rows_ref[:, (2 + units) * unit : (3 + units) * unit] = pre_grad
-        sum_ref[0, :, span] = jnp.sum(pre_grad.astype(jnp.float32), axis=0, keepdims=True)
-        for half in range(2):
-            up = mm(pre_grad, weight(half, units, 0), 1, 1)
-            down = mm(act, weight(half, units, 1), 1, 1)
-            ups[half] = up if units == 0 else ups[half] + up
-            downs[half] = down if units == 0 else downs[half] + down
-
-    for half in range(2):
-        at = slice(half * width, (half + 1) * width)
-
-        @pl.when(step == 0)
-        def _():
-            grad_acc[:, at] = ups[half]
-            down_acc[:, at] = downs[half]
-
-        @pl.when(step > 0)
-        def _():
-            grad_acc[:, at] += ups[half]
-            down_acc[:, at] += downs[half]
+    quarter = pieces[0].shape[1] // 2
+    ups, downs = slice(0, quarter), slice(quarter, 2 * quarter)
+    pre = mm(normed[0][...], pieces[0][:, ups], 1, 0) + mm(normed[1][...], pieces[1][:, ups], 1, 0)
+    pre = pre + bias_ref[0]
+    act_grad = mm(grads[0][...], pieces[0][:, downs], 1, 0) + mm(grads[1][...], pieces[1][:, downs], 1, 0)
+    square = pre * pre
+    bent = jnp.tanh(gelu_scale * pre * (1.0 + gelu_cubic * square))
+    half = 0.5 * (1.0 + bent)
+    slope = half + 0.5 * gelu_scale * pre * (1.0 - bent * bent) * (1.0 + 3.0 * gelu_cubic * square)
+    act = (pre * half).astype(jnp.bfloat16)
+    pre_grad = (act_grad * slope).astype(jnp.bfloat16)
+    rows_ref[:, :quarter] = act
+    rows_ref[:, quarter:] = pre_grad
+    sum_ref[0] = jnp.sum(pre_grad.astype(jnp.float32), axis=0, keepdims=True)
+
+    @pl.when(step == 0)
+    def _():
+        for i in range(2):
+            at = slice(i * width, (i + 1) * width)
+            grad_acc[:, at] = mm(pre_grad, pieces[i][:, ups], 1, 1)
+            down_acc[:, at] = mm(act, pieces[i][:, downs], 1, 1)
+
+    @pl.when(step > 0)
+    def _():
+        for i in range(2):
+            at = slice(i * width, (i + 1) * width)
+            grad_acc[:, at] += mm(pre_grad, pieces[i][:, ups], 1, 1)
+            down_acc[:, at] += mm(act, pieces[i][:, downs], 1, 1)
 
     @pl.when(step == pl.num_programs(0) - 1)
     def _():
@@ -614,82 +603,78 @@
         down_out[...] = down_acc[...].astype(jnp.bfloat16)
 
 
-def ffn_rows_of(normed, grads, part, own_pieces, sib_pieces, bias):
+def ffn_rows_of(index, normed, grads, part, pieces, bias):
     tokens, features = normed.shape
     width = features // 2
-    ring, _, columns = own_pieces.shape
-    unit = columns // 4
+    columns = pieces.shape[2]
+    ring, quarter = pieces.shape[0] // 2, columns // 2
 
     def halves(at):
-        return [pl.BlockSpec((tokens, width), lambda k, h=h: (at, h)) for h in range(2)]
-
-    piece = pl.BlockSpec((1, width, columns), lambda k: (k, 0, 0))
-    whole = pl.BlockSpec((tokens, features), lambda k: (0, 0))
-    vector = pl.BlockSpec((1, 1, 2 * unit), lambda k: (k, 0, 0))
+        return [pl.BlockSpec((tokens, width), lambda k, s, h=h: (at, h)) for h in range(2)]
+
+    piece = [
+        pl.BlockSpec((1, width, columns), lambda k, s, h=h: ((s[0] ^ h) * ring + k, 0, 0))
+        for h in range(2)
+    ]
+    whole = pl.BlockSpec((tokens, features), lambda k, s: (0, 0))
+    vector = pl.BlockSpec((1, 1, quarter), lambda k, s: (k, 0, 0))
     return pl.pallas_call(
         ffn_kernel,
-        grid=(ring,),
-        in_specs=halves(0) + halves(part) + [piece] * 2 + [vector],
-        out_specs=[pl.BlockSpec((tokens, columns), lambda k: (0, k)), vector, whole, whole],
+        grid_spec=pltpu.PrefetchScalarGridSpec(
+            num_scalar_prefetch=1,
+            grid=(ring,),
+            in_specs=halves(0) + halves(part) + piece + [vector],
+            out_specs=[pl.BlockSpec((tokens, columns), lambda k, s: (0, k)), vector, whole, whole],
+            scratch_shapes=[pltpu.VMEM((tokens, features), jnp.float32)] * 2,
+        ),
         out_shape=[
             shape((tokens, ring * columns)),
-            shape((ring, 1, 2 * unit), jnp.float32),
+            shape((ring, 1, quarter), jnp.float32),
             shape((tokens, features)),
             shape((tokens, features)),
         ],
-        scratch_shapes=[pltpu.VMEM((tokens, features), jnp.float32)] * 2,
         compiler_params=params(),
-        cost_estimate=cost(16 * tokens * features * ring * unit, 12 * ring * width * columns),
-    )(normed, normed, grads, grads, own_pieces, sib_pieces, bias)
-
-
-def weight_products_kernel(count, mirrored, index_ref, *refs):
+        cost_estimate=cost(8 * tokens * features * ring * quarter, 12 * ring * width * columns),
+    )(index, normed, normed, grads, grads, pieces, pieces, bias)
+
+
+def weight_products_kernel(count, *refs):
     out_ref = refs[-1]
     normed, grads, rows = [refs[i * count : (i + 1) * count] for i in range(3)]
-    twice = rows[0].shape[1] // 2
-    unit = twice // 2
+    quarter = rows[0].shape[1] // 2
     up = down = None
     for j in range(count):
-        up_part = mm(normed[j][...], rows[j][:, twice:], 0, 0)
-        down_part = mm(grads[j][...], rows[j][:, :twice], 0, 0)
+        up_part = mm(normed[j][...], rows[j][:, quarter:], 0, 0)
+        down_part = mm(grads[j][...], rows[j][:, :quarter], 0, 0)
         up = up_part if up is None else up + up_part
         down = down_part if down is None else down + down_part
-    for i in range(2):
-        units = slice((i ^ mirrored) * unit, ((i ^ mirrored) + 1) * unit)
-        out_ref[0, :, i * twice : i * twice + unit] = up[:, units].astype(jnp.bfloat16)
-        out_ref[0, :, i * twice + unit : (i + 1) * twice] = down[:, units].astype(jnp.bfloat16)
-
-
-def weight_products(index, normed, grads, rows, half):
+    out_ref[0, :, :quarter] = up.astype(jnp.bfloat16)
+    out_ref[0, :, quarter:] = down.astype(jnp.bfloat16)
+
+
+def weight_products(normed, grads, rows, half):
     count = len(normed)
     tokens, features = normed[0].shape
     width = features // 2
     ring = 4
     columns = rows[0].shape[1] // ring
-    size = min(256, width)
+    size = min(512, width)
     blocks = width // size
-    left = [pl.BlockSpec((tokens, size), lambda k, d, s: (0, half * blocks + d))] * count
+    left = [pl.BlockSpec((tokens, size), lambda k, d: (0, half * blocks + d))] * count
     left += [
-        pl.BlockSpec((tokens, size), lambda k, d, s, j=j: (j, half * blocks + d)) for j in range(count)
+        pl.BlockSpec((tokens, size), lambda k, d, j=j: (j, half * blocks + d)) for j in range(count)
     ]
-    right = [pl.BlockSpec((tokens, columns), lambda k, d, s: (0, k))] * count
-    return pl.pallas_call(
-        functools.partial(weight_products_kernel, count, half),
-        grid_spec=pltpu.PrefetchScalarGridSpec(
-            num_scalar_prefetch=1,
-            grid=(ring, blocks),
-            in_specs=left + right,
-            out_specs=pl.BlockSpec(
-                (1, size, columns),
-                lambda k, d, s: (jnp.where(s[2] >= k, s[2] - k, s[2] - k + ring), d, 0),
-            ),
-        ),
+    return pl.pallas_call(
+        functools.partial(weight_products_kernel, count),
+        grid=(ring, blocks),
+        in_specs=left + [pl.BlockSpec((tokens, columns), lambda k, d: (0, k))] * count,
+        out_specs=pl.BlockSpec((1, size, columns), lambda k, d: (k, d, 0)),
         out_shape=shape((ring, width, columns)),
         compiler_params=params(),
         cost_estimate=cost(
             2 * count * tokens * width * ring * columns, 4 * count * tokens * features * ring
         ),
-    )(index, *normed, *([grads] * count), *rows)
+    )(*normed, *([grads] * count), *rows)
 
 
 def params(**more):
@@ -697,7 +682,7 @@
 
 
 def cost(flops, nbytes):
-    return pl.CostEstimate(flops=20 * flops, bytes_accessed=20 * nbytes, transcendentals=0)
+    return pl.CostEstimate(flops=flops // 10, bytes_accessed=nbytes // 10, transcendentals=0)
 
 
 def shape(dims, dtype=jnp.bfloat16):
@@ -744,34 +729,30 @@
     )(index, *weights, *weights)
 
 
-def pack_ff_kernel(index_ref, up_own, down_own, up_sib, down_sib, out_ref):
-    unit = up_own.shape[1]
-    parts = (up_own[...], turned(down_own[...]), up_sib[...], turned(down_sib[...]))
-    for i, part in enumerate(parts):
-        out_ref[:, i * unit : (i + 1) * unit] = part
+def pack_ff_kernel(index_ref, up_ref, down_ref, out_ref):
+    quarter = up_ref.shape[1]
+    out_ref[:, :quarter] = up_ref[...]
+    out_ref[:, quarter:] = turned(down_ref[...])
 
 
 def pack_ff(index, up_weight, down_weight):
     width, units = up_weight.shape
-    unit, block = units // 8, width // 4
-    in_specs = []
-    for which in range(2):
-        in_specs += [
-            pl.BlockSpec((block, unit), lambda d, s, w=which: (d, 2 * s[1] + (s[0] ^ w))),
-            pl.BlockSpec((unit, block), lambda d, s, w=which: (2 * s[1] + (s[0] ^ w), d)),
-        ]
+    quarter, block = units // 4, width // 4
     return pl.pallas_call(
         pack_ff_kernel,
         grid_spec=pltpu.PrefetchScalarGridSpec(
             num_scalar_prefetch=1,
             grid=(4,),
-            in_specs=in_specs,
-            out_specs=pl.BlockSpec((block, 4 * unit), lambda d, s: (d, 0)),
+            in_specs=[
+                pl.BlockSpec((block, quarter), lambda d, s: (d, s[1])),
+                pl.BlockSpec((quarter, block), lambda d, s: (s[1], d)),
+            ],
+            out_specs=pl.BlockSpec((block, 2 * quarter), lambda d, s: (d, 0)),
         ),
-        out_shape=shape((width, 4 * unit)),
+        out_shape=shape((width, 2 * quarter)),
         compiler_params=params(),
-        cost_estimate=cost(0, 16 * width * unit),
-    )(index, up_weight, down_weight, up_weight, down_weight)
+        cost_estimate=cost(0, 8 * width * quarter),
+    )(index, up_weight, down_weight)
 
 
 def stack_kernel(*refs):
@@ -876,7 +857,7 @@
     count = len(rows)
     tokens, units = rows[0].shape
     width = own_weights[0].shape[0]
-    size = min(256, tokens)
+    size = min(512, tokens)
     full = pl.BlockSpec((size, 2 * width), lambda i: (i, 0))
     return pl.pallas_call(
         functools.partial(sum_rows_kernel, count),
@@ -933,7 +914,7 @@
 def head_products(normed, grads, head_grad, attended):
     tokens, width = normed.shape[0], normed.shape[1] // 2
     split, own = head_grad.shape[1], attended.shape[1]
-    size = min(256, width)
+    size = min(512, width)
     blocks = width // size
     left = [pl.BlockSpec((tokens, size), lambda d, h=h: (0, h * blocks + d)) for h in range(2)]
     out = pl.BlockSpec((size, split + own), lambda d: (d, 0))
@@ -1191,42 +1172,111 @@
     )(index, *pieces)
 
 
-def place_ff_kernel(index_ref, *refs):
+def place_ff_kernel(*refs):
     pieces, (up_out, down_out) = refs[:-2], refs[-2:]
     rows = pieces[0].shape[1]
-    unit = pieces[0].shape[2] // 4
-    for part, piece_ref in enumerate(pieces):
+    quarter = pieces[0].shape[2] // 2
+    for part, piece in enumerate(pieces):
         span = slice(part * rows, (part + 1) * rows)
-        for which in range(2):
-            at = pl.multiple_of((index_ref[0] ^ which) * unit, unit)
-            start = 2 * which * unit
-            up_out[span, pl.ds(at, unit)] = piece_ref[0, :, start : start + unit].astype(jnp.float32)
-            down_out[pl.ds(at, unit), span] = (
-                piece_ref[0, :, start + unit : start + 2 * unit].astype(jnp.float32).T
-            )
-
-
-def place_ff(index, pieces):
+        up_out[span, :] = piece[0, :, :quarter].astype(jnp.float32)
+        down_out[:, span] = piece[0, :, quarter:].astype(jnp.float32).T
+
+
+def place_ff(pieces):
     count, rows, columns = pieces[0].shape
     width, quarter = rows * len(pieces), columns // 2
     return pl.pallas_call(
         place_ff_kernel,
-        grid_spec=pltpu.PrefetchScalarGridSpec(
-            num_scalar_prefetch=1,
-            grid=(count,),
-            in_specs=[pl.BlockSpec((1, rows, columns), lambda j, s: (j, 0, 0))] * len(pieces),
-            out_specs=[
-                pl.BlockSpec((width, quarter), lambda j, s: (0, j)),
-                pl.BlockSpec((quarter, width), lambda j, s: (j, 0)),
-            ],
-        ),
+        grid=(count,),
+        in_specs=[pl.BlockSpec((1, rows, columns), lambda j: (j, 0, 0))] * len(pieces),
+        out_specs=[
+            pl.BlockSpec((width, quarter), lambda j: (0, j)),
+            pl.BlockSpec((quarter, width), lambda j: (j, 0)),
+        ],
         out_shape=[
             shape((width, count * quarter), jnp.float32),
             shape((count * quarter, width), jnp.float32),
         ],
         compiler_params=params(),
         cost_estimate=cost(0, 48 * width * quarter),
-    )(index, *pieces)
+    )(*pieces)
+
+
+def join_kernel(index_ref, mine_ref, first_ref, second_ref, out_ref):
+    step = pl.program_id(0)
+
+    @pl.when(step < 2)
+    def _():
+        out_ref[...] = mine_ref[...]
+
+    @pl.when(step == 2)
+    def _():
+        out_ref[...] = first_ref[...]
+
+    @pl.when(step == 3)
+    def _():
+        out_ref[...] = second_ref[...]
+
+
+def join_tokens(index, mine, first, second):
+    tokens, width = mine.shape
+    size = tokens // 2
+    once = pl.BlockSpec((size, width), lambda i, s: (0, 0))
+    return pl.pallas_call(
+        join_kernel,
+        grid_spec=pltpu.PrefetchScalarGridSpec(
+            num_scalar_prefetch=1,
+            grid=(4,),
+            in_specs=[pl.BlockSpec((size, width), lambda i, s: (jnp.minimum(i, 1), 0)), once, once],
+            out_specs=pl.BlockSpec(
+                (size, width), lambda i, s: (jnp.where(i < 2, s[0] * 2 + i, (1 - s[0]) * 2 + i - 2), 0)
+            ),
+        ),
+        out_shape=shape((2 * tokens, width), mine.dtype),
+        compiler_params=params(),
+        cost_estimate=cost(0, 8 * tokens * width),
+    )(index, mine, first, second)
+
+
+def layer_out_kernel(*refs):
+    here, x_top, y_top, x_bottom, y_bottom, hidden_ref, own_ref, sib_ref, keep_ref, vectors_ref = refs[1:11]
+    own_out, sib_out = refs[11:]
+    f32 = jnp.float32
+    width = own_ref.shape[1]
+    top = pl.program_id(0) == 0
+    from_x = jnp.where(top, x_top[...].astype(f32), x_bottom[...].astype(f32))
+    from_y = jnp.where(top, y_top[...].astype(f32), y_bottom[...].astype(f32))
+    total = hidden_ref[...] + here[...].astype(f32) + from_x + from_y + vectors_ref[5:6, :]
+    keep = keep_ref[...] > 0.5
+    own_out[...] = jnp.where(keep, total[:, :width], own_ref[...].astype(f32))
+    sib_out[...] = jnp.where(keep, total[:, width:], sib_ref[...].astype(f32))
+
+
+def layer_rows(index, parts, hidden, own, sib, keep, vectors):
+    tokens, features = hidden.shape
+    size, width = tokens // 2, features // 2
+    plain = pl.BlockSpec((size, features), lambda i, s: (i, 0))
+    half_wide = pl.BlockSpec((size, width), lambda i, s: (i, 0))
+    return pl.pallas_call(
+        layer_out_kernel,
+        grid_spec=pltpu.PrefetchScalarGridSpec(
+            num_scalar_prefetch=1,
+            grid=(2,),
+            in_specs=[plain]
+            + [pl.BlockSpec((size, features), lambda i, s: (0, 0))] * 4
+            + [
+                plain,
+                my_rows(size, width, 2),
+                my_rows(size, width, 2),
+                pl.BlockSpec((size, 1), lambda i, s: (i, 0)),
+                pl.BlockSpec(vectors.shape, lambda i, s: (0, 0)),
+            ],
+            out_specs=[half_wide, half_wide],
+        ),
+        out_shape=[shape((tokens, width), jnp.float32)] * 2,
+        compiler_params=params(),
+        cost_estimate=cost(0, 20 * tokens * features),
+    )(index, *parts, hidden, own, sib, keep, vectors)
 
 
 def body_local(
@@ -1277,22 +1327,15 @@
     def other_tokens(values):
         return cut(values, (1 - row_i) * half, half)
 
-    def all_tokens(mine, other):
-        return jnp.where(
-            row_i == 0, jnp.concatenate([mine, other], axis=0), jnp.concatenate([other, mine], axis=0)
-        )
-
     tokens_sib = order.swap(tokens_in)
     out_grad_sib = swap(other_tokens(out_grad))
 
-    ff_bias = cut(up_bias, plane_i * quarter, quarter).reshape(2, unit)
     mine = jnp.concatenate(
         [
             cut(query_bias, row_i * own, own),
             jnp.zeros((own,), f32),
             cut(value_bias, row_i * own, own),
-            picked(ff_bias, row_i),
-            picked(ff_bias, 1 - row_i),
+            cut(up_bias, plane_i * quarter, quarter),
         ]
     )
     small = [mine] + [
@@ -1311,13 +1354,15 @@
     out_grads = jnp.concatenate([my_tokens(out_grad), out_grad_sib], axis=1).astype(f32)
     branch_mine = (after(out_grads, *order.tokens) * keep_mask).astype(bf16)
     branch_first = plane.both(branch_mine[: half // 2], branch_mine[: half // 2])
+    ff_piece = order.run(pack_ff, index, up_weight, down_weight)
+    ff_pieces = lax.all_gather(ff_piece, ("row", "col"))
     vectors = jnp.stack([norm1_gain, norm1_shift, norm2_gain, norm2_shift, out_bias, down_bias])
     vectors_sib = swap(vectors)
     vectors_all = jnp.concatenate([vectors, vectors_sib], axis=1)
+    pieces.append(column.send(step_up, pieces[1]))
+    near = plane.both(pieces[1], pieces[1])
     here = order.run(pack_heads, index, sources, 4)
     own_parts, other_rows = [here[0]], [order.swap(here[1])]
-    ff_piece = order.run(pack_ff, index, up_weight, down_weight)
-    ff_own, ff_sib = [ff_piece], []
     normed_one, stats_one = order.run(
         norm_rows,
         index,
@@ -1346,13 +1391,7 @@
         own_parts.append(own_part)
         other_rows.append(other_part)
 
-    def next_ff():
-        ff_sib.append(order.swap(ff_own[-1]))
-        ff_own.append(column.send(step_up, ff_own[-1]))
-
     attend_project(0)
-    pieces.append(column.send(step_up, pieces[1]))
-    near = plane.both(pieces[1], pieces[1])
     attend(0)
     far = plane.far(*near)
     pieces.append(column.send(step_up, pieces[2]))
@@ -1361,14 +1400,12 @@
     stack(1, last_near, last_far)
     attend_project(1)
     attend(1)
-    next_ff()
     far = plane.far(*near)
     last_near, last_far = near, far
     near = plane.both(pieces[3], pieces[3])
     stack(2, last_near, last_far)
     attend_project(2)
     attend(2)
-    next_ff()
     far = plane.far(*near)
     last_near, last_far = near, far
     branch_far = plane.far(*branch_first)
@@ -1377,42 +1414,34 @@
     second_near = plane.both(branch_mine[half // 2 :], branch_mine[half // 2 :])
     attend_project(3)
     attend(3)
-    next_ff()
-    order.tokens += second_near
+    second_far = plane.far(*second_near)
     attention_rows = order.run(sum_rows, attended[3:], own_parts[3:], other_rows[3:], 3, (before,))
     arrived = swap(order.tie(mirrored(other_tokens(attention_rows)).astype(bf16)))
-    second_far = plane.far(*second_near)
-
+
+    order.tokens.append(ff_pieces)
     hidden_one, normed_two, stats_two = order.run(
         norm_two, index, attention_rows, arrived, tokens_in, tokens_sib, vectors_all
     )
 
-    normed = [normed_two, *plane.both(normed_two, normed_two, True)]
+    normed = [normed_two, *plane.both(normed_two, normed_two)]
     branch_all = jnp.concatenate(
         [branch_mine]
         + [part for pair in zip(branch_first, second_near) for part in pair]
         + [*branch_far, *second_far],
         axis=0,
     )
-    ff_sib.append(order.swap(ff_own[3]))
-    ff_own_all, ff_sib_all = jnp.stack(ff_own), jnp.stack(ff_sib)
-    ff_biases = jnp.stack([s[None, 3 * own :] for s in small])
+    def by_column(relative):
+        places = jnp.mod(col_i - jnp.arange(ring), ring)
+        return jnp.take(relative, places, axis=0)
+
+    ff_biases = by_column(jnp.stack([s[None, 3 * own :] for s in small]))
     ff_rows, up_sums, grad_parts, down_parts = [], [], [], []
 
     def feed_forward(j):
-        results = order.run(ffn_rows_of, normed[j], branch_all, j, ff_own_all, ff_sib_all, ff_biases)
+        grads, part = (branch_all, j) if j > 0 else (branch_mine, 0)
+        results = order.run(ffn_rows_of, index, normed[j], grads, part, ff_pieces, ff_biases)
         for kept, result in zip((ff_rows, up_sums, grad_parts, down_parts), results):
             kept.append(result)
-
-    def plane_total(here, x_top, y_top, x_bottom, y_bottom):
-        cut_at = half // 2
-        return jnp.concatenate(
-            [
-                here[:cut_at].astype(f32) + x_top.astype(f32) + y_top.astype(f32),
-                here[cut_at:].astype(f32) + x_bottom.astype(f32) + y_bottom.astype(f32),
-            ],
-            axis=0,
-        )
 
     def top(values):
         return values[: half // 2]
@@ -1425,19 +1454,20 @@
         return plane.both(add_rounded(bottom(parts[1]), via_y), add_rounded(top(parts[2]), via_x))
 
     def weight_grads(part):
-        return order.run(weight_products, index, normed, branch_all, ff_rows, part)
+        return order.run(weight_products, normed, branch_all, ff_rows, part)
 
     feed_forward(0)
     normed_far = plane.far(normed[1], normed[2])
     feed_forward(1)
+    x_top = plane.x.send(step_x, top(grad_parts[1]))
     feed_forward(2)
-    x_top, y_bottom = plane.both(top(grad_parts[1]), bottom(grad_parts[2]))
+    y_bottom = plane.y.send(step_y, bottom(grad_parts[2]))
     normed.append(jnp.concatenate(normed_far, axis=0))
     feed_forward(3)
     via_x, via_y = plane.both(top(grad_parts[3]), bottom(grad_parts[3]))
+    ff_mine = weight_grads(0)
+    x_bottom, y_top = second_steps(grad_parts, via_x, via_y)
     ff_other = order.swap(weight_grads(1))
-    x_bottom, y_top = second_steps(grad_parts, via_x, via_y)
-    ff_mine = weight_grads(0)
 
     hidden_grad, grad_mine, grad_mirror, sums_two = order.run(
         norm_two_back,
@@ -1449,8 +1479,8 @@
         vectors_all,
     )
     down_x_top, down_y_bottom = plane.both(top(down_parts[1]), bottom(down_parts[2]))
-    grad_other = order.swap(grad_mirror)
-    grad_rows = all_tokens(grad_mine, grad_other)
+    grad_others = [order.swap(top(grad_mirror)), order.swap(bottom(grad_mirror))]
+    grad_rows = order.run(join_tokens, index, grad_mine, *grad_others)
 
     ff_grads = []
     for part in range(2):
@@ -1476,7 +1506,7 @@
         return group_parts[k][which][j * block : (j + 1) * block]
 
     def first_messages(k):
-        return plane.both(part_of(k, 3, 0), part_of(k, 3, 1))
+        return plane.both(part_of(k, 3, 0), part_of(k, 3, 1), True)
 
     def second_messages(k, via):
         via_x, via_y = after(via, *order.tokens)
@@ -1494,26 +1524,43 @@
         return here.astype(bf16)
 
     down_via_x, down_via_y = plane.both(top(down_parts[3]), bottom(down_parts[3]))
+    def layer_out_rows():
+        own_out, sib_out = order.run(
+            layer_rows,
+            index,
+            (down_parts[0], down_x_top, down_y_top, down_x_bottom, down_y_bottom),
+            hidden_one,
+            tokens_in,
+            tokens_sib,
+            keep_mask,
+            vectors_all,
+        )
+        return own_out, order.swap(top(sib_out)), order.swap(bottom(sib_out))
+
+    vias, came = [None] * ring, [None] * ring
     backward(3)
     head_weights(3)
     down_x_bottom, down_y_top = second_steps(down_parts, down_via_x, down_via_y)
+    vias[3] = first_messages(3)
     backward(2)
     head_weights(2)
-    via = first_messages(3)
+    vias[2] = first_messages(2)
+    came[3] = second_messages(3, vias[3])
     backward(1)
-    came = second_messages(3, via)
     head_weights(1)
+    vias[1] = first_messages(1)
+    came[2] = second_messages(2, vias[2])
+    total = column.send(step_down, group_total(3, came[3], None))
     backward(0)
-    total = group_total(3, came, None)
-    via = first_messages(2)
     head_weights(0)
-    came = second_messages(2, via)
-    summed_group = group_total(2, came, None)
-    via = first_messages(1)
+    vias[0] = first_messages(0)
+    came[1] = second_messages(1, vias[1])
+    total = column.send(step_down, add_rounded(total, group_total(2, came[2], None)))
     back_rows = order.run(sum_rows, head_rows, own_parts, other_rows, 0)
     arrived = order.swap(mirrored(other_tokens(back_rows)).astype(bf16))
-    came = second_messages(1, via)
-    total = column.send(step_down, total)
+    came[0] = second_messages(0, vias[0])
+    total = column.send(step_down, add_rounded(total, group_total(1, came[1], None)))
+    layer_parts = layer_out_rows()
 
     input_mine, input_other, sums_one = order.run(
         norm_one_back,
@@ -1529,18 +1576,13 @@
         hidden_grad,
         vectors_all,
     )
-    input_grad = all_tokens(input_mine, swap(input_other))
-
-    def by_column(relative):
-        places = jnp.mod(col_i - jnp.arange(ring), ring)
-        return jnp.take(relative, places, axis=0)
+    input_others = [order.swap(top(input_other)), order.swap(bottom(input_other))]
+    layer_out = order.run(join_tokens, index, *layer_parts)
 
     row_hot = (jnp.arange(2) == row_i).astype(f32)
     plane_hot = (jnp.arange(4) == plane_i).astype(f32)
     head_bias = by_column(jnp.stack(bias_rows)).reshape(ring, 3, 1, own) * row_hot[:, None]
-    up_bias_part = by_column(sum(up_sums).reshape(ring, 2, unit))
-    up_bias_part = jnp.where(row_i == 0, up_bias_part, up_bias_part[:, ::-1])
-    up_bias_part = up_bias_part[:, None] * plane_hot[:, None, None]
+    up_bias_part = sum(up_sums) * plane_hot[:, None]
     bias_vector = jnp.concatenate([head_bias.reshape(ring, -1), up_bias_part.reshape(ring, -1)], axis=1)
     feature_sums = jnp.concatenate([sums_one[:2], sums_two[:4]], axis=0)
     summed = jnp.concatenate([bias_vector.reshape(-1), feature_sums[:, :width].reshape(-1)])
@@ -1548,34 +1590,23 @@
         jnp.concatenate([bias_vector.reshape(-1), feature_sums[:, width:].reshape(-1)])
     )
 
-    via = first_messages(0)
-    total = add_rounded(total, summed_group)
-    total = column.send(step_down, total)
-    summed_group = group_total(1, came, None)
-    came = second_messages(0, via)
-    total = add_rounded(total, summed_group)
-    total = column.send(step_down, total)
     summed = order.tie(summed)
     summed = summed + plane.x.send(step_x, summed)
     summed = summed + plane.y.send(step_y, summed)
+    total = group_total(0, came[0], total)
+    total = jnp.concatenate([total[:, : 4 * own], swap(total[:, 4 * own :])], axis=1)
+    near = plane.both(total, total)
     step = 1
     while step < ring:
         pairs = [(i, i ^ step) for i in range(ring)]
         summed = summed + column.send(lambda v: lax.ppermute(v, "col", pairs), summed)
         step *= 2
-    total = group_total(0, came, total)
-    total = jnp.concatenate([total[:, : 4 * own], swap(total[:, 4 * own :])], axis=1)
-    near = plane.both(total, total)
-    up_weight_grad, down_weight_grad = order.run(place_ff, index, ff_grads)
+    input_grad = order.run(join_tokens, index, input_mine, *input_others)
+    up_weight_grad, down_weight_grad = order.run(place_ff, ff_grads)
     far = plane.far(*near)
     query_weight_grad, key_weight_grad, value_weight_grad, out_weight_grad = place_heads(
         index, [total, *near, *far]
     )
-
-    tokens_mine = jnp.concatenate([my_tokens(tokens_in), my_tokens(tokens_sib)], axis=1).astype(f32)
-    ffn_rows = plane_total(down_parts[0], down_x_top, down_y_top, down_x_bottom, down_y_bottom)
-    out_mine = jnp.where(active_here[:, None], hidden_one + ffn_rows + vectors_all[5], tokens_mine)
-    layer_out = all_tokens(out_mine[:, :width], swap(out_mine[:, width:]))
 
     bias_here = picked(summed[: bias_vector.size].reshape(ring, -1), col_i)
     own_here = summed[bias_vector.size :].reshape(6, width)

time: 1030 us -> 1020 us (level)
  starting transfers between devices: 87.2 us -> 136 us
  waiting for transfers between devices: 302 us -> 273 us
  other arithmetic: 89.4 us -> 64.3 us
    ppermute x6 -> x3, starting transfers between devices: 3.06 us -> 30.6 us  [step_up(): lax.ppermute(values, 'col', [(i, (i + 1) % count) for i in range(count)])]
    ppermute x6 -> x3, waiting for transfers between devices: 109 us -> 82.7 us  [step_up(): lax.ppermute(values, 'col', [(i, (i + 1) % count) for i in range(count)])]
    ppermute x3, starting transfers between devices: 10.4 us -> 31 us  [step_down(): lax.ppermute(values, 'col', [(i, (i - 1) % count) for i in range(count)])]
    select_n x5 -> x0, other arithmetic: 20.5 us -> none  [the longest x3 17.8 us: all_tokens(): jnp.where(row_i == 0, jnp.concatenate([mine, other], axis=0), jnp.concate...]
    another operation x4 -> x2, other arithmetic: 10.8 us -> 0.19 us  [the longest x2 10.6 us: body_local(): ff_own_all, ff_sib_all = (jnp.stack(ff_own), jnp.stack(ff_sib))]
    unnamed x315 -> x256, local copies, waits for them, and re-layouts: 45.7 us -> 43.6 us
    pallas_call x7 -> x11, Pallas kernels: 186 us -> 187 us  [the longest x4 102 us: ffn_rows_of(): pl.pallas_call(ffn_kernel, grid_spec=pltpu.PrefetchScalarGridSpec(num_sca...]
  transfers between devices with their start and end apart: 93 -> 90, of which waited for: 33 -> 33; matrix products, arithmetic and copies ran while one was open for 14% -> 12% of each run, Pallas kernels for 34% -> 37%
where the time goes in v6:
time: 1020 us; the launch traced here: 1010 us
  Pallas kernels  418 us (41%)
  waiting for transfers between devices  273 us (27%)
  starting transfers between devices  136 us (13%)
  local copies, waits for them, and re-layouts  101 us (10%)
  other arithmetic  64.3 us (6%)
  between operations  15.6 us (2%)
    ppermute x29, waiting for transfers between devices, step_y(): return lax.ppermute(values, 'dp', [(0, 2), (2, 0), (1, 3), (3, 1)])  143 us
    pallas_call x4, Pallas kernels, ffn_rows_of(): pl.pallas_call(ffn_kernel, grid_spec=pltpu.PrefetchScalarGridSpec(num_sca...  102 us
    ppermute x3, waiting for transfers between devices, step_up(): lax.ppermute(values, 'col', [(i, (i + 1) % count) for i in range(count)])  82.7 us
    pallas_call x2, Pallas kernels, weight_products(): pl.pallas_call(functools.partial(weight_products_kernel, count), grid=(ri...  58 us
    pallas_call x4, Pallas kernels, local_backward(): pl.pallas_call(functools.partial(local_backward_kernel, min(512, length))...  50.3 us
    unnamed x256, local copies, waits for them, and re-layouts  43.6 us
    ppermute x29, waiting for transfers between devices, step_x(): return lax.ppermute(values, 'dp', [(0, 1), (1, 0), (2, 3), (3, 2)])  36.2 us
    pallas_call x3, Pallas kernels, sum_rows(): pl.pallas_call(functools.partial(sum_rows_kernel, count), grid=(tokens //...  34.3 us
  transfers between devices with their start and end apart: 90, of which 33 were waited for; matrix products, arithmetic and copies ran while one was open for 12% of the time, Pallas kernels for 37%

profile of v6, /device:TPU:0, one launch (start us, length us, event | category | flops | bytes accessed | tf_op | source)
XLA Modules:
  0.0 1007.4 jit_solution(5657415439119368514)
XLA Ops:
  42.9 36.7 %collective-permute-done.6.refs_0_ = bf16[512,1024]{1,0:T(8,128)(2,1)} collective-permute-done((bf16[512,1024]{1,0:T(8,128)(2,1)}, bf16[512,1024]{1,0:T(8,128)(2,1)}, u32[]{:S(2)}, u32[]{:S(2)}) %collective-permute-start.6) | collective-permute-done | bytes 1048608 | tf_op jit(solution)/shard_map/ppermute | solution.py:358
  84.3 3.6 shard_map.316
  91.5 6.1 collective-permute-start.15
  97.8 6.7 shard_map.317
  104.5 9.2 collective-permute-done.12.refs_2_
  116.2 6.1 shard_map.318.query_ref.key_ref.value_ref
  122.3 6.5 shard_map.319.refs_0_.refs_5_
  130.8 21.1 %collective-permute-done.15.refs_0_ = bf16[512,1024]{1,0:T(8,128)(2,1)S(1)} collective-permute-done((bf16[512,1024]{1,0:T(8,128)(2,1)}, bf16[512,1024]{1,0:T(8,128)(2,1)S(1)}, u32[]{:S(2)}, u32[]{:S(2)}) %collective-permute-start.15) | collective-permute-done | bytes 1048608 | tf_op jit(solution)/shard_map/ppermute | solution.py:358
  152.8 23.8 %collective-permute-start.20 = (bf16[512,1024]{1,0:T(8,128)(2,1)S(1)}, bf16[512,1024]{1,0:T(8,128)(2,1)S(1)}, u32[]{:S(2)}, u32[]{:S(2)}) collective-permute-start(bf16[512,1024]{1,0:T(8,128)(2,1)S(1)} %collective-permute-done.15.refs_0_), channel_id=1, source_target_pairs={{0,1},{1,2},{2,3},{3,0},{4,5},{5,6},{6,7},{7,4},{8,9},{9,10},{10,1... | collective-permute-start | bytes 3145736 | tf_op jit(solution)/shard_map/ppermute | solution.py:358
  176.6 3.8 shard_map.320
  183.7 5.6 shard_map.321.query_ref.key_ref.value_ref
  189.4 6.5 shard_map.322.refs_1_.refs_5_
  197.1 24.9 %collective-permute-done.20.refs_0_ = bf16[512,1024]{1,0:T(8,128)(2,1)S(1)} collective-permute-done((bf16[512,1024]{1,0:T(8,128)(2,1)S(1)}, bf16[512,1024]{1,0:T(8,128)(2,1)S(1)}, u32[]{:S(2)}, u32[]{:S(2)}) %collective-permute-start.20) | collective-permute-done | bytes 1048608 | tf_op jit(solution)/shard_map/ppermute | solution.py:358
  231.1 5.4 shard_map.324.query_ref.key_ref.value_ref
  236.6 6.5 shard_map.325.refs_2_.refs_5_
  250.3 8.8 collective-permute-done.24.refs_4_
  263.7 7.6 shard_map.327.refs_3_
  273.3 5.5 shard_map.328.query_ref.key_ref.value_ref
  278.8 6.7 shard_map.329.refs_0_.refs_5_
  285.6 6.5 collective-permute-done.28
  294.2 6.3 shard_map.330.rows_ref
  309.2 6.4 shard_map.331
  315.6 3.7 collective-permute-done.32
  331.1 25.4 %shard_map.332 = (bf16[512,4096]{1,0:T(8,128)(2,1)}, f32[4,1,512]{2,1,0:T(1,128)S(1)}, bf16[512,2048]{1,0:T(8,128)(2,1)S(1)}, bf16[512,2048]{1,0:T(8,128)(2,1)S(1)}) custom-call(s32[3]{0:T(128)S(1)} %pad_add_fusion.index_ref.refs_0_, bf16[512,2048]{1,0:T(8,128)(2,1)} %get-tuple-element.427.refs_0_.refs_1_, ...), custom_call_target="tpu_custom_call" | custom-call | flops 1717986944 | bytes 5033164 | tf_op jit(solution)/shard_map/pallas_call | solution.py:621
  356.5 10.5 %collective-permute-done.33.refs_0_.refs_1_.refs_2_ = bf16[512,2048]{1,0:T(8,128)(2,1)} collective-permute-done((bf16[512,2048]{1,0:T(8,128)(2,1)}, bf16[512,2048]{1,0:T(8,128)(2,1)}, u32[]{:S(2)}, u32[]{:S(2)}) %collective-permute-start.33) | collective-permute-done | bytes 2097184 | tf_op jit(solution)/shard_map/ppermute | solution.py:353
  377.9 25.6 %shard_map.333 = (bf16[512,4096]{1,0:T(8,128)(2,1)}, f32[4,1,512]{2,1,0:T(1,128)S(1)}, bf16[512,2048]{1,0:T(8,128)(2,1)S(1)}, bf16[512,2048]{1,0:T(8,128)(2,1)S(1)}) custom-call(s32[3]{0:T(128)S(1)} %pad_add_fusion.index_ref.refs_0_, bf16[512,2048]{1,0:T(8,128)(2,1)} %collective-permute-done.31.refs_0_.refs_1_, ...), custom_call_target="tpu_custom_call" | custom-call | flops 1717986944 | bytes 5033164 | tf_op jit(solution)/shard_map/pallas_call | solution.py:621
  405.4 25.3 %shard_map.334 = (bf16[512,4096]{1,0:T(8,128)(2,1)}, f32[4,1,512]{2,1,0:T(1,128)S(1)}, bf16[512,2048]{1,0:T(8,128)(2,1)S(1)}, bf16[512,2048]{1,0:T(8,128)(2,1)S(1)}) custom-call(s32[3]{0:T(128)S(1)} %pad_add_fusion.index_ref.refs_0_, bf16[512,2048]{1,0:T(8,128)(2,1)} %collective-permute-done.33.refs_0_.refs_1_.refs_2_, ...), custom_call_target="tpu_custom_call" | custom-call | flops 1717986944 | bytes 5033164 | tf_op jit(solution)/shard_map/pallas_call | solution.py:621
  434.9 25.4 %shard_map.335 = (bf16[512,4096]{1,0:T(8,128)(2,1)}, f32[4,1,512]{2,1,0:T(1,128)S(1)}, bf16[512,2048]{1,0:T(8,128)(2,1)S(1)}, bf16[512,2048]{1,0:T(8,128)(2,1)S(1)}) custom-call(s32[3]{0:T(128)S(1)} %pad_add_fusion.index_ref.refs_0_, bf16[512,2048]{1,0:T(8,128)(2,1)} %constant_dynamic-update-slice_fusion.refs_0_.refs_1_.refs_3_, ...), custom_call_target="tpu_custom_call" | custom-call | flops 1717986944 | bytes 5033164 | tf_op jit(solution)/shard_map/pallas_call | solution.py:621
  464.9 28.9 %shard_map.336 = bf16[4,1024,1024]{2,1,0:T(8,128)(2,1)} custom-call(bf16[512,2048]{1,0:T(8,128)(2,1)} %get-tuple-element.427.refs_0_.refs_1_, bf16[512,2048]{1,0:T(8,128)(2,1)} %collective-permute-done.31.refs_0_.refs_1_, bf16[512,2048]{1,0:T(8,128)(2,1)} %collective-permute-done.33.refs_0_.refs_1_.refs_2_, ...), custom_call_target="tpu_custom_call" | custom-call | flops 1717986944 | bytes 6710886 | tf_op jit(solution)/shard_map/pallas_call | solution.py:667
  493.9 3.7 add_convert_fusion.10
  497.5 29.1 %shard_map.337 = bf16[4,1024,1024]{2,1,0:T(8,128)(2,1)} custom-call(bf16[512,2048]{1,0:T(8,128)(2,1)} %get-tuple-element.427.refs_0_.refs_1_, bf16[512,2048]{1,0:T(8,128)(2,1)} %collective-permute-done.31.refs_0_.refs_1_, bf16[512,2048]{1,0:T(8,128)(2,1)} %collective-permute-done.33.refs_0_.refs_1_.refs_2_, ...), custom_call_target="tpu_custom_call" | custom-call | flops 1717986944 | bytes 6710886 | tf_op jit(solution)/shard_map/pallas_call | solution.py:667
  530.5 21.8 %collective-permute-done.40.refs_2_ = bf16[256,2048]{1,0:T(8,128)(2,1)S(1)} collective-permute-done((bf16[256,2048]{1,0:T(8,128)(2,1)S(1)}, bf16[256,2048]{1,0:T(8,128)(2,1)S(1)}, u32[]{:S(2)}, u32[]{:S(2)}) %collective-permute-start.40) | collective-permute-done | bytes 1048608 | tf_op jit(solution)/shard_map/ppermute | solution.py:353
  552.6 12.1 %shard_map.338 = (f32[512,2048]{1,0:T(8,128)}, bf16[512,2048]{1,0:T(8,128)(2,1)}, bf16[512,2048]{1,0:T(8,128)(2,1)}, f32[8,2048]{1,0:T(8,128)S(1)}) custom-call(s32[3]{0:T(128)S(1)} %pad_add_fusion.index_ref.refs_0_, bf16[512,2048]{1,0:T(8,128)(2,1)} %copy-done.38, bf16[256,2048]{1,0:T(8,128)(2,1)S(1)} %collective-permute-done.36.refs_1_, ...), custom_call_target="tpu_custom_call" | custom-call | bytes 2516582 | tf_op jit(solution)/shard_map/pallas_call | solution.py:1048
  567.1 10.1 %add_convert_fusion = (bf16[4,512,1024]{2,1,0:T(8,128)(2,1)}, bf16[4,512,1024]{2,1,0:T(8,128)(2,1)}) fusion(bf16[4,1024,1024]{2,1,0:T(8,128)(2,1)} %collective-permute-done.42, bf16[4,1024,1024]{2,1,0:T(8,128)(2,1)} %shard_map.336), kind=kLoop, calls=%fused_computation.2 | loop fusion | flops 16777216 | bytes 25165824 | tf_op jit(solution)/shard_map/convert_element_type | solution.py:418
  586.2 3.3 fusion.17
  589.5 17.0 %collective-permute-done.46.refs_5_ = bf16[256,2048]{1,0:T(8,128)(2,1)S(1)} collective-permute-done((bf16[256,2048]{1,0:T(8,128)(2,1)}, bf16[256,2048]{1,0:T(8,128)(2,1)S(1)}, u32[]{:S(2)}, u32[]{:S(2)}) %collective-permute-start.46) | collective-permute-done | bytes 1048608 | tf_op jit(solution)/shard_map/ppermute | solution.py:353
  607.7 8.0 shard_map.340.grad_ref
  617.6 12.4 %shard_map.341.refs_4_.refs_3_ = bf16[1024,768]{1,0:T(8,128)(2,1)S(1)} custom-call(s32[1,1024]{1,0:T(1,128)S(1)} %bitcast.54, bf16[1024,768]{1,0:T(8,128)(2,1)S(1)} %shard_map.328.query_ref.key_ref.value_ref, bf16[1024,1024]{1,0:T(8,128)(2,1)S(1)} %shard_map.340.grad_ref, bf16[1024,768]{1,0:T(8,128)(2,1)S(1)} %shard_map.328.query_ref.key_ref.value_ref, ...), custom_call_target="tpu_custom_call" | custom-call | flops 858993472 | bytes 629145 | tf_op jit(solution)/shard_map/pallas_call | solution.py:544
  630.0 8.9 shard_map.342
  647.5 12.6 %shard_map.343.refs_4_.refs_2_ = bf16[1024,768]{1,0:T(8,128)(2,1)S(1)} custom-call(s32[1,1024]{1,0:T(1,128)S(1)} %bitcast.55, bf16[1024,768]{1,0:T(8,128)(2,1)S(1)} %copy-done.5, bf16[1024,1024]{1,0:T(8,128)(2,1)S(1)} %shard_map.340.grad_ref, bf16[1024,768]{1,0:T(8,128)(2,1)S(1)} %copy-done.5, bf16[1024,768]{1,0:T(8,128)(2,1)S(1)} %copy-done.5), custom_call_target="tpu_custom_call" | custom-call | flops 858993472 | bytes 629145 | tf_op jit(solution)/shard_map/pallas_call | solution.py:544
  660.1 8.3 shard_map.344
  676.5 7.4 collective-permute-done.52
  690.1 12.6 %shard_map.345.refs_4_.refs_1_ = bf16[1024,768]{1,0:T(8,128)(2,1)S(1)} custom-call(s32[1,1024]{1,0:T(1,128)S(1)} %bitcast.56, bf16[1024,768]{1,0:T(8,128)(2,1)S(1)} %copy-done.3, bf16[1024,1024]{1,0:T(8,128)(2,1)S(1)} %copy-done.7, bf16[1024,768]{1,0:T(8,128)(2,1)S(1)} %copy-done.3, bf16[1024,768]{1,0:T(8,128)(2,1)S(1)} %copy-done.3), custom_call_target="tpu_custom_call" | custom-call | flops 858993472 | bytes 629145 | tf_op jit(solution)/shard_map/pallas_call | solution.py:544
  702.7 8.8 shard_map.346
  721.3 6.1 collective-permute-done.54
  728.4 3.2 add_convert_fusion.7
  731.6 28.1 %collective-permute-start.59 = (bf16[256,2048]{1,0:T(8,128)(2,1)}, bf16[256,2048]{1,0:T(8,128)(2,1)}, u32[]{:S(2)}, u32[]{:S(2)}) collective-permute-start(bf16[256,2048]{1,0:T(8,128)(2,1)} %add_convert_fusion.7), channel_id=1, source_target_pairs={{0,3},{1,0},{2,1},{3,2},{4,7},{5,4},{6,5},{7,6},{8,11},{9,8},{10,9... | collective-permute-start | bytes 3145736 | tf_op jit(solution)/shard_map/ppermute | solution.py:363
  759.8 12.8 %shard_map.347.refs_4_.refs_0_ = bf16[1024,768]{1,0:T(8,128)(2,1)S(1)} custom-call(s32[1,1024]{1,0:T(1,128)S(1)} %bitcast.57, bf16[1024,768]{1,0:T(8,128)(2,1)S(1)} %copy-done.1, bf16[1024,1024]{1,0:T(8,128)(2,1)S(1)} %copy-done.8, bf16[1024,768]{1,0:T(8,128)(2,1)S(1)} %copy-done.1, bf16[1024,768]{1,0:T(8,128)(2,1)S(1)} %copy-done.1), custom_call_target="tpu_custom_call" | custom-call | flops 858993472 | bytes 629145 | tf_op jit(solution)/shard_map/pallas_call | solution.py:544
  772.6 8.3 shard_map.348
  794.1 9.7 collective-permute-done.58
  808.6 3.7 add_convert_fusion.5
  815.2 20.4 %shard_map.349.refs_0_ = f32[1024,2048]{1,0:T(8,128)} custom-call(bf16[1024,768]{1,0:T(8,128)(2,1)S(1)} %shard_map.347.refs_4_.refs_0_, bf16[1024,768]{1,0:T(8,128)(2,1)S(1)} %copy-done.29, bf16[1024,768]{1,0:T(8,128)(2,1)S(1)} %shard_map.343.refs_4_.refs_2_, bf16[1024,768]{1,0:T(8,128)(2,1)} %copy-done.27, ...), custom_call_target="tpu_custom_call" | custom-call | flops 1288490240 | bytes 838860 | tf_op jit(solution)/shard_map/pallas_call | solution.py:862
  844.2 33.0 %collective-permute-done.63 = bf16[256,2048]{1,0:T(8,128)(2,1)} collective-permute-done((bf16[256,2048]{1,0:T(8,128)(2,1)}, bf16[256,2048]{1,0:T(8,128)(2,1)}, u32[]{:S(2)}, u32[]{:S(2)}) %collective-permute-start.63) | collective-permute-done | bytes 1048608 | tf_op jit(solution)/shard_map/ppermute | solution.py:353
  881.8 3.6 add_convert_fusion.3
  885.4 8.8 shard_map.350
  904.4 7.9 shard_map.351
  917.1 4.2 shard_map.352
  921.3 10.3 %collective-permute-done.71 = bf16[256,2048]{1,0:T(8,128)(2,1)} collective-permute-done((bf16[256,2048]{1,0:T(8,128)(2,1)}, bf16[256,2048]{1,0:T(8,128)(2,1)}, u32[]{:S(2)}, u32[]{:S(2)}) %collective-permute-start.71) | collective-permute-done | bytes 1048608 | tf_op jit(solution)/shard_map/ppermute | solution.py:349
  932.0 4.1 collective-permute-done.72
  941.2 3.2 collective-permute-done.76
  954.1 15.1 %collective-permute-done.82.refs_2_ = bf16[256,2048]{1,0:T(8,128)(2,1)S(1)} collective-permute-done((bf16[256,2048]{1,0:T(8,128)(2,1)S(1)}, bf16[256,2048]{1,0:T(8,128)(2,1)S(1)}, u32[]{:S(2)}, u32[]{:S(2)}) %collective-permute-start.82) | collective-permute-done | bytes 1048608 | tf_op jit(solution)/shard_map/ppermute | solution.py:353
  973.4 8.0 shard_map.354
  990.4 3.6 collective-permute-done.83.refs_3_
  995.1 5.5 shard_map.355
  (559 shorter events, 250.7 us)
Async XLA Ops:
  7.2 299.4 %all-gather.9.cloned.1.call-start = ((), (), s32[]{:S(2)}) async-start(), calls=%async_computation.6 | async-start | bytes 18874368 | tf_op jit(solution)/shard_map/all_gather | solution.py:1358
  10.5 18.7 %collective-permute-start.4 = (bf16[512,1024]{1,0:T(8,128)(2,1)}, bf16[512,1024]{1,0:T(8,128)(2,1)}, u32[]{:S(2)}, u32[]{:S(2)}) collective-permute-start(bf16[512,1024]{1,0:T(8,128)(2,1)} %get-tuple-element.624), channel_id=1, source_target_pairs={{0,4},{4,0},{1,5},{5,1},{2,6},{6,2},{3,7},{7,3},{8,12},{12,8},{9,1... | collective-permute-start | bytes 3145736 | tf_op jit(solution)/shard_map/ppermute | solution.py:345
  11.9 17.3 %collective-permute-start.1 = (f32[1280]{0:T(1024)S(1)}, f32[1280]{0:T(1024)S(1)}, u32[]{:S(2)}, u32[]{:S(2)}) collective-permute-start(f32[1280]{0:T(1024)S(1)} %pad_maximum_fusion.18), channel_id=1, source_target_pairs={{0,1},{1,2},{2,3},{3,0},{4,5},{5,6},{6,7},{7,4},{8,9},{9,10},{10,1... | collective-permute-start | bytes 15368 | tf_op jit(solution)/shard_map/ppermute | solution.py:1342
  17.1 17.5 %collective-permute-start.5 = (bf16[1024,1024]{1,0:T(8,128)(2,1)S(1)}, bf16[1024,1024]{1,0:T(8,128)(2,1)}, u32[]{:S(2)}, u32[]{:S(2)}) collective-permute-start(bf16[1024,1024]{1,0:T(8,128)(2,1)S(1)} %copy-done.9), channel_id=1, source_target_pairs={{0,4},{4,0},{1,5},{5,1},{2,6},{6,2},{3,7},{7,3},{8,12},{12,8},{9,1... | collective-permute-start | bytes 6291464 | tf_op jit(solution)/shard_map/ppermute | solution.py:345
  39.2 649.3 %reduce-scatter.5.cloned.1.call-start = ((), (), s32[]{:S(2)}) async-start(), calls=%async_computation.4 | async-start | bytes 5242880 | tf_op jit(solution)/shard_map/reduce_scatter | solution.py:1489
  39.2 40.4 %collective-permute-start.6 = (bf16[512,1024]{1,0:T(8,128)(2,1)}, bf16[512,1024]{1,0:T(8,128)(2,1)}, u32[]{:S(2)}, u32[]{:S(2)}) collective-permute-start(bf16[512,1024]{1,0:T(8,128)(2,1)} %pad_maximum_fusion.2), channel_id=1, source_target_pairs={{0,1},{1,2},{2,3},{3,0},{4,5},{5,6},{6,7},{7,4},{8,9},{9,10},{10,1... | collective-permute-start | bytes 3145736 | tf_op jit(solution)/shard_map/ppermute | solution.py:358
  39.9 39.7 %collective-permute-start.7 = (bf16[256,2048]{1,0:T(8,128)(2,1)}, bf16[256,2048]{1,0:T(8,128)(2,1)S(1)}, u32[]{:S(2)}, u32[]{:S(2)}) collective-permute-start(bf16[256,2048]{1,0:T(8,128)(2,1)} %get-tuple-element.305), channel_id=1, source_target_pairs={{0,8},{8,0},{16,24},{24,16},{1,9},{9,1},{17,25},{25,17},{2,10},{10... | collective-permute-start | bytes 3145736 | tf_op jit(solution)/shard_map/ppermute | solution.py:349
  41.4 39.2 %collective-permute-start.8 = (bf16[256,2048]{1,0:T(8,128)(2,1)}, bf16[256,2048]{1,0:T(8,128)(2,1)}, u32[]{:S(2)}, u32[]{:S(2)}) collective-permute-start(bf16[256,2048]{1,0:T(8,128)(2,1)} %get-tuple-element.305), channel_id=1, source_target_pairs={{0,16},{16,0},{8,24},{24,8},{1,17},{17,1},{9,25},{25,9},{2,18},{18... | collective-permute-start | bytes 3145736 | tf_op jit(solution)/shard_map/ppermute | solution.py:353
  87.9 28.3 %collective-permute-start.10 = (bf16[1024,1024]{1,0:T(8,128)(2,1)}, bf16[1024,1024]{1,0:T(8,128)(2,1)}, u32[]{:S(2)}, u32[]{:S(2)}) collective-permute-start(bf16[1024,1024]{1,0:T(8,128)(2,1)} %get-tuple-element.316), channel_id=1, source_target_pairs={{0,4},{4,0},{1,5},{5,1},{2,6},{6,2},{3,7},{7,3},{8,12},{12,8},{9,1... | collective-permute-start | bytes 6291464 | tf_op jit(solution)/shard_map/ppermute | solution.py:345
  87.9 25.8 %collective-permute-start.12 = (bf16[512,1024]{1,0:T(8,128)(2,1)}, bf16[512,1024]{1,0:T(8,128)(2,1)S(1)}, u32[]{:S(2)}, u32[]{:S(2)}) collective-permute-start(bf16[512,1024]{1,0:T(8,128)(2,1)} %collective-permute-done.6.refs_0_), channel_id=1, source_target_pairs={{0,16},{16,0},{8,24},{24,8},{1,17},{17,1},{9,25},{25,9},{2,18},{18... | collective-permute-start | bytes 3145736 | tf_op jit(solution)/shard_map/ppermute | solution.py:353
  89.5 25.6 %collective-permute-start.11 = (bf16[512,1024]{1,0:T(8,128)(2,1)}, bf16[512,1024]{1,0:T(8,128)(2,1)}, u32[]{:S(2)}, u32[]{:S(2)}) collective-permute-start(bf16[512,1024]{1,0:T(8,128)(2,1)} %collective-permute-done.6.refs_0_), channel_id=1, source_target_pairs={{0,8},{8,0},{16,24},{24,16},{1,9},{9,1},{17,25},{25,17},{2,10},{10... | collective-permute-start | bytes 3145736 | tf_op jit(solution)/shard_map/ppermute | solution.py:349
  91.5 60.4 %collective-permute-start.15 = (bf16[512,1024]{1,0:T(8,128)(2,1)}, bf16[512,1024]{1,0:T(8,128)(2,1)S(1)}, u32[]{:S(2)}, u32[]{:S(2)}) collective-permute-start(bf16[512,1024]{1,0:T(8,128)(2,1)} %collective-permute-done.6.refs_0_), channel_id=1, source_target_pairs={{0,1},{1,2},{2,3},{3,0},{4,5},{5,6},{6,7},{7,4},{8,9},{9,10},{10,1... | collective-permute-start | bytes 3145736 | tf_op jit(solution)/shard_map/ppermute | solution.py:358
  128.9 23.0 %collective-permute-start.13 = (bf16[256,1024]{1,0:T(8,128)(2,1)S(1)}, bf16[256,1024]{1,0:T(8,128)(2,1)S(1)}, u32[]{:S(2)}, u32[]{:S(2)}) collective-permute-start(bf16[256,1024]{1,0:T(8,128)(2,1)S(1)} %slice.429), channel_id=1, source_target_pairs={{0,16},{16,0},{8,24},{24,8},{1,17},{17,1},{9,25},{25,9},{2,18},{18... | collective-permute-start | bytes 1572872 | tf_op jit(solution)/shard_map/ppermute | solution.py:353
  129.3 22.6 %collective-permute-start.14 = (bf16[256,1024]{1,0:T(8,128)(2,1)S(1)}, bf16[256,1024]{1,0:T(8,128)(2,1)S(1)}, u32[]{:S(2)}, u32[]{:S(2)}) collective-permute-start(bf16[256,1024]{1,0:T(8,128)(2,1)S(1)} %slice.430), channel_id=1, source_target_pairs={{0,8},{8,0},{16,24},{24,16},{1,9},{9,1},{17,25},{25,17},{2,10},{10... | collective-permute-start | bytes 1572872 | tf_op jit(solution)/shard_map/ppermute | solution.py:349
  151.9 44.0 %collective-permute-start.17 = (bf16[512,1024]{1,0:T(8,128)(2,1)S(1)}, bf16[512,1024]{1,0:T(8,128)(2,1)S(1)}, u32[]{:S(2)}, u32[]{:S(2)}) collective-permute-start(bf16[512,1024]{1,0:T(8,128)(2,1)S(1)} %collective-permute-done.15.refs_0_), channel_id=1, source_target_pairs={{0,16},{16,0},{8,24},{24,8},{1,17},{17,1},{9,25},{25,9},{2,18},{18... | collective-permute-start | bytes 3145736 | tf_op jit(solution)/shard_map/ppermute | solution.py:353
  152.3 43.6 %collective-permute-start.16 = (bf16[512,1024]{1,0:T(8,128)(2,1)S(1)}, bf16[512,1024]{1,0:T(8,128)(2,1)S(1)}, u32[]{:S(2)}, u32[]{:S(2)}) collective-permute-start(bf16[512,1024]{1,0:T(8,128)(2,1)S(1)} %collective-permute-done.15.refs_0_), channel_id=1, source_target_pairs={{0,8},{8,0},{16,24},{24,16},{1,9},{9,1},{17,25},{25,17},{2,10},{10... | collective-permute-start | bytes 3145736 | tf_op jit(solution)/shard_map/ppermute | solution.py:349
  152.8 69.2 %collective-permute-start.20 = (bf16[512,1024]{1,0:T(8,128)(2,1)S(1)}, bf16[512,1024]{1,0:T(8,128)(2,1)S(1)}, u32[]{:S(2)}, u32[]{:S(2)}) collective-permute-start(bf16[512,1024]{1,0:T(8,128)(2,1)S(1)} %collective-permute-done.15.refs_0_), channel_id=1, source_target_pairs={{0,1},{1,2},{2,3},{3,0},{4,5},{5,6},{6,7},{7,4},{8,9},{9,10},{10,1... | collective-permute-start | bytes 3145736 | tf_op jit(solution)/shard_map/ppermute | solution.py:358
  196.0 26.0 %collective-permute-start.18 = (bf16[256,1024]{1,0:T(8,128)(2,1)S(1)}, bf16[256,1024]{1,0:T(8,128)(2,1)S(1)}, u32[]{:S(2)}, u32[]{:S(2)}) collective-permute-start(bf16[256,1024]{1,0:T(8,128)(2,1)S(1)} %slice.432), channel_id=1, source_target_pairs={{0,16},{16,0},{8,24},{24,8},{1,17},{17,1},{9,25},{25,9},{2,18},{18... | collective-permute-start | bytes 1572872 | tf_op jit(solution)/shard_map/ppermute | solution.py:353
  196.6 25.5 %collective-permute-start.19 = (bf16[256,1024]{1,0:T(8,128)(2,1)S(1)}, bf16[256,1024]{1,0:T(8,128)(2,1)S(1)}, u32[]{:S(2)}, u32[]{:S(2)}) collective-permute-start(bf16[256,1024]{1,0:T(8,128)(2,1)S(1)} %slice.433), channel_id=1, source_target_pairs={{0,8},{8,0},{16,24},{24,16},{1,9},{9,1},{17,25},{25,17},{2,10},{10... | collective-permute-start | bytes 1572872 | tf_op jit(solution)/shard_map/ppermute | solution.py:349
  222.0 23.7 %collective-permute-start.22 = (bf16[512,1024]{1,0:T(8,128)(2,1)S(1)}, bf16[512,1024]{1,0:T(8,128)(2,1)S(1)}, u32[]{:S(2)}, u32[]{:S(2)}) collective-permute-start(bf16[512,1024]{1,0:T(8,128)(2,1)S(1)} %collective-permute-done.20.refs_0_), channel_id=1, source_target_pairs={{0,16},{16,0},{8,24},{24,8},{1,17},{17,1},{9,25},{25,9},{2,18},{18... | collective-permute-start | bytes 3145736 | tf_op jit(solution)/shard_map/ppermute | solution.py:353
  223.6 23.4 %collective-permute-start.21 = (bf16[512,1024]{1,0:T(8,128)(2,1)S(1)}, bf16[512,1024]{1,0:T(8,128)(2,1)S(1)}, u32[]{:S(2)}, u32[]{:S(2)}) collective-permute-start(bf16[512,1024]{1,0:T(8,128)(2,1)S(1)} %collective-permute-done.20.refs_0_), channel_id=1, source_target_pairs={{0,8},{8,0},{16,24},{24,16},{1,9},{9,1},{17,25},{25,17},{2,10},{10... | collective-permute-start | bytes 3145736 | tf_op jit(solution)/shard_map/ppermute | solution.py:349
  271.3 20.8 %collective-permute-start.28 = (bf16[256,2048]{1,0:T(8,128)(2,1)S(1)}, bf16[256,2048]{1,0:T(8,128)(2,1)S(1)}, u32[]{:S(2)}, u32[]{:S(2)}) collective-permute-start(bf16[256,2048]{1,0:T(8,128)(2,1)S(1)} %copy-done.87), channel_id=1, source_target_pairs={{0,8},{8,0},{16,24},{24,16},{1,9},{9,1},{17,25},{25,17},{2,10},{10... | collective-permute-start | bytes 3145736 | tf_op jit(solution)/shard_map/ppermute | solution.py:349
  272.2 21.1 %collective-permute-start.27 = (bf16[256,2048]{1,0:T(8,128)(2,1)S(1)}, bf16[256,2048]{1,0:T(8,128)(2,1)S(1)}, u32[]{:S(2)}, u32[]{:S(2)}) collective-permute-start(bf16[256,2048]{1,0:T(8,128)(2,1)S(1)} %copy-done.87), channel_id=1, source_target_pairs={{0,16},{16,0},{8,24},{24,8},{1,17},{17,1},{9,25},{25,9},{2,18},{18... | collective-permute-start | bytes 3145736 | tf_op jit(solution)/shard_map/ppermute | solution.py:353
  304.7 14.7 %collective-permute-start.32 = (bf16[128,2048]{1,0:T(8,128)(2,1)}, bf16[128,2048]{1,0:T(8,128)(2,1)}, u32[]{:S(2)}, u32[]{:S(2)}) collective-permute-start(bf16[128,2048]{1,0:T(8,128)(2,1)} %slice.442), channel_id=1, source_target_pairs={{0,16},{16,0},{8,24},{24,8},{1,17},{17,1},{9,25},{25,9},{2,18},{18... | collective-permute-start | bytes 1572872 | tf_op jit(solution)/shard_map/ppermute | solution.py:353
  319.8 47.3 %collective-permute-start.33 = (bf16[512,2048]{1,0:T(8,128)(2,1)}, bf16[512,2048]{1,0:T(8,128)(2,1)}, u32[]{:S(2)}, u32[]{:S(2)}) collective-permute-start(bf16[512,2048]{1,0:T(8,128)(2,1)} %get-tuple-element.427.refs_0_.refs_1_), channel_id=1, source_target_pairs={{0,16},{16,0},{8,24},{24,8},{1,17},{17,1},{9,25},{25,9},{2,18},{18... | collective-permute-start | bytes 6291464 | tf_op jit(solution)/shard_map/ppermute | solution.py:353
  321.1 47.3 %collective-permute-start.31 = (bf16[512,2048]{1,0:T(8,128)(2,1)}, bf16[512,2048]{1,0:T(8,128)(2,1)}, u32[]{:S(2)}, u32[]{:S(2)}) collective-permute-start(bf16[512,2048]{1,0:T(8,128)(2,1)} %get-tuple-element.427.refs_0_.refs_1_), channel_id=1, source_target_pairs={{0,8},{8,0},{16,24},{24,16},{1,9},{9,1},{17,25},{25,17},{2,10},{10... | collective-permute-start | bytes 6291464 | tf_op jit(solution)/shard_map/ppermute | solution.py:349
  369.8 34.9 %collective-permute-start.35 = (bf16[256,2048]{1,0:T(8,128)(2,1)S(1)}, bf16[256,2048]{1,0:T(8,128)(2,1)S(1)}, u32[]{:S(2)}, u32[]{:S(2)}) collective-permute-start(bf16[256,2048]{1,0:T(8,128)(2,1)S(1)} %slice.449), channel_id=1, source_target_pairs={{0,8},{8,0},{16,24},{24,16},{1,9},{9,1},{17,25},{25,17},{2,10},{10... | collective-permute-start | bytes 3145736 | tf_op jit(solution)/shard_map/ppermute | solution.py:349
  371.0 60.9 %collective-permute-start.34 = (bf16[256,2048]{1,0:T(8,128)(2,1)S(1)}, bf16[256,2048]{1,0:T(8,128)(2,1)S(1)}, u32[]{:S(2)}, u32[]{:S(2)}) collective-permute-start(bf16[256,2048]{1,0:T(8,128)(2,1)S(1)} %slice.445), channel_id=1, source_target_pairs={{0,16},{16,0},{8,24},{24,8},{1,17},{17,1},{9,25},{25,9},{2,18},{18... | collective-permute-start | bytes 3145736 | tf_op jit(solution)/shard_map/ppermute | solution.py:353
  404.7 57.7 %collective-permute-start.36 = (bf16[256,2048]{1,0:T(8,128)(2,1)}, bf16[256,2048]{1,0:T(8,128)(2,1)S(1)}, u32[]{:S(2)}, u32[]{:S(2)}) collective-permute-start(bf16[256,2048]{1,0:T(8,128)(2,1)} %slice.346), channel_id=1, source_target_pairs={{0,8},{8,0},{16,24},{24,16},{1,9},{9,1},{17,25},{25,17},{2,10},{10... | collective-permute-start | bytes 3145736 | tf_op jit(solution)/shard_map/ppermute | solution.py:349
  431.9 30.4 %collective-permute-start.37 = (bf16[256,2048]{1,0:T(8,128)(2,1)}, bf16[256,2048]{1,0:T(8,128)(2,1)}, u32[]{:S(2)}, u32[]{:S(2)}) collective-permute-start(bf16[256,2048]{1,0:T(8,128)(2,1)} %slice.347), channel_id=1, source_target_pairs={{0,16},{16,0},{8,24},{24,8},{1,17},{17,1},{9,25},{25,9},{2,18},{18... | collective-permute-start | bytes 3145736 | tf_op jit(solution)/shard_map/ppermute | solution.py:353
  462.3 31.5 %collective-permute-start.39 = (bf16[256,2048]{1,0:T(8,128)(2,1)}, bf16[256,2048]{1,0:T(8,128)(2,1)}, u32[]{:S(2)}, u32[]{:S(2)}) collective-permute-start(bf16[256,2048]{1,0:T(8,128)(2,1)} %get-tuple-element.416), channel_id=1, source_target_pairs={{0,16},{16,0},{8,24},{24,8},{1,17},{17,1},{9,25},{25,9},{2,18},{18... | collective-permute-start | bytes 3145736 | tf_op jit(solution)/shard_map/ppermute | solution.py:353
  463.7 30.2 %collective-permute-start.38 = (bf16[256,2048]{1,0:T(8,128)(2,1)}, bf16[256,2048]{1,0:T(8,128)(2,1)}, u32[]{:S(2)}, u32[]{:S(2)}) collective-permute-start(bf16[256,2048]{1,0:T(8,128)(2,1)} %get-tuple-element.414), channel_id=1, source_target_pairs={{0,8},{8,0},{16,24},{24,16},{1,9},{9,1},{17,25},{25,17},{2,10},{10... | collective-permute-start | bytes 3145736 | tf_op jit(solution)/shard_map/ppermute | solution.py:349
  526.6 40.5 %collective-permute-start.42 = (bf16[4,1024,1024]{2,1,0:T(8,128)(2,1)}, bf16[4,1024,1024]{2,1,0:T(8,128)(2,1)}, u32[]{:S(2)}, u32[]{:S(2)}) collective-permute-start(bf16[4,1024,1024]{2,1,0:T(8,128)(2,1)} %shard_map.337), channel_id=1, source_target_pairs={{0,4},{4,0},{1,5},{5,1},{2,6},{6,2},{3,7},{7,3},{8,12},{12,8},{9,1... | collective-permute-start | bytes 25165832 | tf_op jit(solution)/shard_map/ppermute | solution.py:345
  526.7 25.6 %collective-permute-start.40 = (bf16[256,2048]{1,0:T(8,128)(2,1)S(1)}, bf16[256,2048]{1,0:T(8,128)(2,1)S(1)}, u32[]{:S(2)}, u32[]{:S(2)}) collective-permute-start(bf16[256,2048]{1,0:T(8,128)(2,1)S(1)} %copy-done.91), channel_id=1, source_target_pairs={{0,16},{16,0},{8,24},{24,8},{1,17},{17,1},{9,25},{25,9},{2,18},{18... | collective-permute-start | bytes 3145736 | tf_op jit(solution)/shard_map/ppermute | solution.py:353
  527.4 25.2 %collective-permute-start.41 = (bf16[256,2048]{1,0:T(8,128)(2,1)S(1)}, bf16[256,2048]{1,0:T(8,128)(2,1)S(1)}, u32[]{:S(2)}, u32[]{:S(2)}) collective-permute-start(bf16[256,2048]{1,0:T(8,128)(2,1)S(1)} %copy-done.90), channel_id=1, source_target_pairs={{0,8},{8,0},{16,24},{24,16},{1,9},{9,1},{17,25},{25,17},{2,10},{10... | collective-permute-start | bytes 3145736 | tf_op jit(solution)/shard_map/ppermute | solution.py:349
  580.3 263.9 %reduce-scatter.3.cloned.1.call-start = ((), (), s32[]{:S(2)}) async-start(), calls=%async_computation.2 | async-start | bytes 5242880 | tf_op jit(solution)/shard_map/reduce_scatter | solution.py:1489
  581.0 390.2 %all-gather.7.cloned.1.call-start = ((), (), s32[]{:S(2)}) async-start(), calls=%async_computation.5 | async-start | bytes 5242880 | tf_op jit(solution)/shard_map/all_gather | solution.py:1490
  581.1 25.4 %collective-permute-start.46 = (bf16[256,2048]{1,0:T(8,128)(2,1)}, bf16[256,2048]{1,0:T(8,128)(2,1)S(1)}, u32[]{:S(2)}, u32[]{:S(2)}) collective-permute-start(bf16[256,2048]{1,0:T(8,128)(2,1)} %slice.353), channel_id=1, source_target_pairs={{0,16},{16,0},{8,24},{24,8},{1,17},{17,1},{9,25},{25,9},{2,18},{18... | collective-permute-start | bytes 3145736 | tf_op jit(solution)/shard_map/ppermute | solution.py:353
  582.5 25.2 %collective-permute-start.45 = (bf16[256,2048]{1,0:T(8,128)(2,1)}, bf16[256,2048]{1,0:T(8,128)(2,1)}, u32[]{:S(2)}, u32[]{:S(2)}) collective-permute-start(bf16[256,2048]{1,0:T(8,128)(2,1)} %slice.352), channel_id=1, source_target_pairs={{0,8},{8,0},{16,24},{24,16},{1,9},{9,1},{17,25},{25,17},{2,10},{10... | collective-permute-start | bytes 3145736 | tf_op jit(solution)/shard_map/ppermute | solution.py:349
  615.7 26.2 %collective-permute-start.47 = (bf16[256,2048]{1,0:T(8,128)(2,1)}, bf16[256,2048]{1,0:T(8,128)(2,1)S(1)}, u32[]{:S(2)}, u32[]{:S(2)}) collective-permute-start(bf16[256,2048]{1,0:T(8,128)(2,1)} %get-tuple-element.452), channel_id=1, source_target_pairs={{0,8},{8,0},{16,24},{24,16},{1,9},{9,1},{17,25},{25,17},{2,10},{10... | collective-permute-start | bytes 3145736 | tf_op jit(solution)/shard_map/ppermute | solution.py:349
  616.7 25.2 %collective-permute-start.48 = (bf16[256,2048]{1,0:T(8,128)(2,1)}, bf16[256,2048]{1,0:T(8,128)(2,1)S(1)}, u32[]{:S(2)}, u32[]{:S(2)}) collective-permute-start(bf16[256,2048]{1,0:T(8,128)(2,1)} %get-tuple-element.454), channel_id=1, source_target_pairs={{0,16},{16,0},{8,24},{24,8},{1,17},{17,1},{9,25},{25,9},{2,18},{18... | collective-permute-start | bytes 3145736 | tf_op jit(solution)/shard_map/ppermute | solution.py:353
  645.2 30.0 %collective-permute-start.50 = (bf16[256,1024]{1,0:T(8,128)(2,1)}, bf16[256,1024]{1,0:T(8,128)(2,1)S(1)}, u32[]{:S(2)}, u32[]{:S(2)}) collective-permute-start(bf16[256,1024]{1,0:T(8,128)(2,1)} %get-tuple-element.466), channel_id=1, source_target_pairs={{0,16},{16,0},{8,24},{24,8},{1,17},{17,1},{9,25},{25,9},{2,18},{18... | collective-permute-start | bytes 1572872 | tf_op jit(solution)/shard_map/ppermute | solution.py:353
  646.4 28.8 %collective-permute-start.49 = (bf16[256,1024]{1,0:T(8,128)(2,1)S(1)}, bf16[256,1024]{1,0:T(8,128)(2,1)S(1)}, u32[]{:S(2)}, u32[]{:S(2)}) collective-permute-start(bf16[256,1024]{1,0:T(8,128)(2,1)S(1)} %get-tuple-element.464), channel_id=1, source_target_pairs={{0,8},{8,0},{16,24},{24,16},{1,9},{9,1},{17,25},{25,17},{2,10},{10... | collective-permute-start | bytes 1572872 | tf_op jit(solution)/shard_map/ppermute | solution.py:349
  686.3 42.1 %collective-permute-start.56 = (bf16[256,2048]{1,0:T(8,128)(2,1)}, bf16[256,2048]{1,0:T(8,128)(2,1)}, u32[]{:S(2)}, u32[]{:S(2)}) collective-permute-start(bf16[256,2048]{1,0:T(8,128)(2,1)} %pad_maximum_fusion.4), channel_id=1, source_target_pairs={{0,16},{16,0},{8,24},{24,8},{1,17},{17,1},{9,25},{25,9},{2,18},{18... | collective-permute-start | bytes 3145736 | tf_op jit(solution)/shard_map/ppermute | solution.py:353
  687.7 40.7 %collective-permute-start.55 = (bf16[256,2048]{1,0:T(8,128)(2,1)}, bf16[256,2048]{1,0:T(8,128)(2,1)}, u32[]{:S(2)}, u32[]{:S(2)}) collective-permute-start(bf16[256,2048]{1,0:T(8,128)(2,1)} %pad_maximum_fusion.3), channel_id=1, source_target_pairs={{0,8},{8,0},{16,24},{24,16},{1,9},{9,1},{17,25},{25,17},{2,10},{10... | collective-permute-start | bytes 3145736 | tf_op jit(solution)/shard_map/ppermute | solution.py:349
  688.5 282.7 %all-gather.5.cloned.1.call-start = ((), (), s32[]{:S(2)}) async-start(), calls=%async_computation.3 | async-start | bytes 5242880 | tf_op jit(solution)/shard_map/all_gather | solution.py:1490
  727.5 79.6 %collective-permute-start.60 = (bf16[256,2048]{1,0:T(8,128)(2,1)}, bf16[256,2048]{1,0:T(8,128)(2,1)}, u32[]{:S(2)}, u32[]{:S(2)}) collective-permute-start(bf16[256,2048]{1,0:T(8,128)(2,1)} %pad_maximum_fusion.5), channel_id=1, source_target_pairs={{0,8},{8,0},{16,24},{24,16},{1,9},{9,1},{17,25},{25,17},{2,10},{10... | collective-permute-start | bytes 3145736 | tf_op jit(solution)/shard_map/ppermute | solution.py:349
  727.7 79.2 %collective-permute-start.61 = (bf16[256,2048]{1,0:T(8,128)(2,1)}, bf16[256,2048]{1,0:T(8,128)(2,1)}, u32[]{:S(2)}, u32[]{:S(2)}) collective-permute-start(bf16[256,2048]{1,0:T(8,128)(2,1)} %pad_maximum_fusion.6), channel_id=1, source_target_pairs={{0,16},{16,0},{8,24},{24,8},{1,17},{17,1},{9,25},{25,9},{2,18},{18... | collective-permute-start | bytes 3145736 | tf_op jit(solution)/shard_map/ppermute | solution.py:353
  731.6 77.0 %collective-permute-start.59 = (bf16[256,2048]{1,0:T(8,128)(2,1)}, bf16[256,2048]{1,0:T(8,128)(2,1)}, u32[]{:S(2)}, u32[]{:S(2)}) collective-permute-start(bf16[256,2048]{1,0:T(8,128)(2,1)} %add_convert_fusion.7), channel_id=1, source_target_pairs={{0,3},{1,0},{2,1},{3,2},{4,7},{5,4},{6,5},{7,6},{8,11},{9,8},{10,9... | collective-permute-start | bytes 3145736 | tf_op jit(solution)/shard_map/ppermute | solution.py:363
  782.1 22.3 %collective-permute-start.57 = (bf16[256,1024]{1,0:T(8,128)(2,1)}, bf16[256,1024]{1,0:T(8,128)(2,1)}, u32[]{:S(2)}, u32[]{:S(2)}) collective-permute-start(bf16[256,1024]{1,0:T(8,128)(2,1)} %get-tuple-element.498), channel_id=1, source_target_pairs={{0,8},{8,0},{16,24},{24,16},{1,9},{9,1},{17,25},{25,17},{2,10},{10... | collective-permute-start | bytes 1572872 | tf_op jit(solution)/shard_map/ppermute | solution.py:349
  785.0 18.8 %collective-permute-start.58 = (bf16[256,1024]{1,0:T(8,128)(2,1)}, bf16[256,1024]{1,0:T(8,128)(2,1)}, u32[]{:S(2)}, u32[]{:S(2)}) collective-permute-start(bf16[256,1024]{1,0:T(8,128)(2,1)} %get-tuple-element.500), channel_id=1, source_target_pairs={{0,16},{16,0},{8,24},{24,8},{1,17},{17,1},{9,25},{25,9},{2,18},{18... | collective-permute-start | bytes 1572872 | tf_op jit(solution)/shard_map/ppermute | solution.py:353
  803.8 81.6 %collective-permute-start.65 = (bf16[256,2048]{1,0:T(8,128)(2,1)}, bf16[256,2048]{1,0:T(8,128)(2,1)}, u32[]{:S(2)}, u32[]{:S(2)}) collective-permute-start(bf16[256,2048]{1,0:T(8,128)(2,1)} %add_convert_fusion.8), channel_id=1, source_target_pairs={{0,16},{16,0},{8,24},{24,8},{1,17},{17,1},{9,25},{25,9},{2,18},{18... | collective-permute-start | bytes 3145736 | tf_op jit(solution)/shard_map/ppermute | solution.py:353
  804.3 81.1 %collective-permute-start.66 = (bf16[256,2048]{1,0:T(8,128)(2,1)}, bf16[256,2048]{1,0:T(8,128)(2,1)}, u32[]{:S(2)}, u32[]{:S(2)}) collective-permute-start(bf16[256,2048]{1,0:T(8,128)(2,1)} %add_convert_fusion.9), channel_id=1, source_target_pairs={{0,8},{8,0},{16,24},{24,16},{1,9},{9,1},{17,25},{25,17},{2,10},{10... | collective-permute-start | bytes 3145736 | tf_op jit(solution)/shard_map/ppermute | solution.py:349
  807.0 74.8 %collective-permute-start.62 = (bf16[256,2048]{1,0:T(8,128)(2,1)}, bf16[256,2048]{1,0:T(8,128)(2,1)}, u32[]{:S(2)}, u32[]{:S(2)}) collective-permute-start(bf16[256,2048]{1,0:T(8,128)(2,1)} %pad_maximum_fusion.7), channel_id=1, source_target_pairs={{0,8},{8,0},{16,24},{24,16},{1,9},{9,1},{17,25},{25,17},{2,10},{10... | collective-permute-start | bytes 3145736 | tf_op jit(solution)/shard_map/ppermute | solution.py:349
  807.0 70.2 %collective-permute-start.63 = (bf16[256,2048]{1,0:T(8,128)(2,1)}, bf16[256,2048]{1,0:T(8,128)(2,1)}, u32[]{:S(2)}, u32[]{:S(2)}) collective-permute-start(bf16[256,2048]{1,0:T(8,128)(2,1)} %pad_maximum_fusion.8), channel_id=1, source_target_pairs={{0,16},{16,0},{8,24},{24,8},{1,17},{17,1},{9,25},{25,9},{2,18},{18... | collective-permute-start | bytes 3145736 | tf_op jit(solution)/shard_map/ppermute | solution.py:353
  812.3 69.4 %collective-permute-start.64 = (bf16[256,2048]{1,0:T(8,128)(2,1)}, bf16[256,2048]{1,0:T(8,128)(2,1)}, u32[]{:S(2)}, u32[]{:S(2)}) collective-permute-start(bf16[256,2048]{1,0:T(8,128)(2,1)} %add_convert_fusion.5), channel_id=1, source_target_pairs={{0,3},{1,0},{2,1},{3,2},{4,7},{5,4},{6,5},{7,6},{8,11},{9,8},{10,9... | collective-permute-start | bytes 3145736 | tf_op jit(solution)/shard_map/ppermute | solution.py:363
  877.2 24.8 %collective-permute-start.67 = (bf16[512,2048]{1,0:T(8,128)(2,1)}, bf16[512,2048]{1,0:T(8,128)(2,1)S(1)}, u32[]{:S(2)}, u32[]{:S(2)}) collective-permute-start(bf16[512,2048]{1,0:T(8,128)(2,1)} %pad_maximum_fusion.1), channel_id=1, source_target_pairs={{0,4},{4,0},{1,5},{5,1},{2,6},{6,2},{3,7},{7,3},{8,12},{12,8},{9,1... | collective-permute-start | bytes 6291464 | tf_op jit(solution)/shard_map/ppermute | solution.py:345
  897.3 16.4 %collective-permute-start.69 = (f32[256,1024]{1,0:T(8,128)}, f32[256,1024]{1,0:T(8,128)S(1)}, u32[]{:S(2)}, u32[]{:S(2)}) collective-permute-start(f32[256,1024]{1,0:T(8,128)} %get-tuple-element.531), channel_id=1, source_target_pairs={{0,4},{4,0},{1,5},{5,1},{2,6},{6,2},{3,7},{7,3},{8,12},{12,8},{9,1... | collective-permute-start | bytes 3145736 | tf_op jit(solution)/shard_map/ppermute | solution.py:345
  897.8 17.6 %collective-permute-start.68 = (f32[256,1024]{1,0:T(8,128)}, f32[256,1024]{1,0:T(8,128)}, u32[]{:S(2)}, u32[]{:S(2)}) collective-permute-start(f32[256,1024]{1,0:T(8,128)} %get-tuple-element.530), channel_id=1, source_target_pairs={{0,4},{4,0},{1,5},{5,1},{2,6},{6,2},{3,7},{7,3},{8,12},{12,8},{9,1... | collective-permute-start | bytes 3145736 | tf_op jit(solution)/shard_map/ppermute | solution.py:345
  899.4 32.2 %collective-permute-start.71 = (bf16[256,2048]{1,0:T(8,128)(2,1)}, bf16[256,2048]{1,0:T(8,128)(2,1)}, u32[]{:S(2)}, u32[]{:S(2)}) collective-permute-start(bf16[256,2048]{1,0:T(8,128)(2,1)} %pad_maximum_fusion.9), channel_id=1, source_target_pairs={{0,8},{8,0},{16,24},{24,16},{1,9},{9,1},{17,25},{25,17},{2,10},{10... | collective-permute-start | bytes 3145736 | tf_op jit(solution)/shard_map/ppermute | solution.py:349
  899.6 36.5 %collective-permute-start.73 = (bf16[256,2048]{1,0:T(8,128)(2,1)}, bf16[256,2048]{1,0:T(8,128)(2,1)}, u32[]{:S(2)}, u32[]{:S(2)}) collective-permute-start(bf16[256,2048]{1,0:T(8,128)(2,1)} %pad_maximum_fusion.10), channel_id=1, source_target_pairs={{0,16},{16,0},{8,24},{24,8},{1,17},{17,1},{9,25},{25,9},{2,18},{18... | collective-permute-start | bytes 3145736 | tf_op jit(solution)/shard_map/ppermute | solution.py:353
  902.0 34.1 %collective-permute-start.74 = (bf16[256,2048]{1,0:T(8,128)(2,1)}, bf16[256,2048]{1,0:T(8,128)(2,1)}, u32[]{:S(2)}, u32[]{:S(2)}) collective-permute-start(bf16[256,2048]{1,0:T(8,128)(2,1)} %add_convert_fusion.3), channel_id=1, source_target_pairs={{0,3},{1,0},{2,1},{3,2},{4,7},{5,4},{6,5},{7,6},{8,11},{9,8},{10,9... | collective-permute-start | bytes 3145736 | tf_op jit(solution)/shard_map/ppermute | solution.py:363
  944.5 24.7 %collective-permute-start.82 = (bf16[256,2048]{1,0:T(8,128)(2,1)S(1)}, bf16[256,2048]{1,0:T(8,128)(2,1)S(1)}, u32[]{:S(2)}, u32[]{:S(2)}) collective-permute-start(bf16[256,2048]{1,0:T(8,128)(2,1)S(1)} %pad_maximum_fusion.11.refs_0_), channel_id=1, source_target_pairs={{0,16},{16,0},{8,24},{24,8},{1,17},{17,1},{9,25},{25,9},{2,18},{18... | collective-permute-start | bytes 3145736 | tf_op jit(solution)/shard_map/ppermute | solution.py:353
  945.9 24.4 %collective-permute-start.81 = (bf16[256,2048]{1,0:T(8,128)(2,1)S(1)}, bf16[256,2048]{1,0:T(8,128)(2,1)S(1)}, u32[]{:S(2)}, u32[]{:S(2)}) collective-permute-start(bf16[256,2048]{1,0:T(8,128)(2,1)S(1)} %pad_maximum_fusion.11.refs_0_), channel_id=1, source_target_pairs={{0,8},{8,0},{16,24},{24,16},{1,9},{9,1},{17,25},{25,17},{2,10},{10... | collective-permute-start | bytes 3145736 | tf_op jit(solution)/shard_map/ppermute | solution.py:349
  (147 other events, 2464.0 us)
Sparse Core Ops, SparseCore 0:
  39.3 208.9 all-gather.8
  580.4 101.1 reduce-scatter.4
  684.0 80.8 reduce-scatter.2
  766.6 88.1 all-gather.6
  856.5 59.2 all-gather.4

commit v7 on v6

--- a/solution.py
+++ b/solution.py
@@ -1489,6 +1489,7 @@
         total = lax.psum_scatter(total, "col", scatter_dimension=0, tiled=False)
         ff_grads.append(lax.all_gather(total, "dp"))
 
+    down_via_x, down_via_y = plane.both(top(down_parts[3]), bottom(down_parts[3]), True)
     head_grad = order.run(head_grads, grad_rows, own_parts, other_rows)
     head_rows, bias_rows, group_parts = [None] * ring, [None] * ring, [None] * ring
 
@@ -1523,7 +1524,6 @@
             here = here + total.astype(f32)
         return here.astype(bf16)
 
-    down_via_x, down_via_y = plane.both(top(down_parts[3]), bottom(down_parts[3]))
     def layer_out_rows():
         own_out, sib_out = order.run(
             layer_rows,
@@ -1550,9 +1550,9 @@
     head_weights(1)
     vias[1] = first_messages(1)
     came[2] = second_messages(2, vias[2])
-    total = column.send(step_down, group_total(3, came[3], None))
     backward(0)
     head_weights(0)
+    total = column.send(step_down, group_total(3, came[3], None))
     vias[0] = first_messages(0)
     came[1] = second_messages(1, vias[1])
     total = column.send(step_down, add_rounded(total, group_total(2, came[2], None)))

time: 1020 us -> 1020 us (level)
  waiting for transfers between devices: 273 us -> 297 us
  starting transfers between devices: 136 us -> 122 us
    ppermute x3, starting transfers between devices: 31 us -> 12.4 us  [step_down(): lax.ppermute(values, 'col', [(i, (i - 1) % count) for i in range(count)])]
    reduce_scatter x2, waiting for transfers between devices: 0.01 us -> 13.5 us  [body_local(): total = lax.psum_scatter(total, 'col', scatter_dimension=0, tiled=False)]
    unnamed x256 -> x258, local copies, waits for them, and re-layouts: 43.6 us -> 42.4 us
  transfers between devices with their start and end apart: 90 -> 90, of which waited for: 33 -> 33; matrix products, arithmetic and copies ran while one was open for 12% -> 12% of each run, Pallas kernels for 37% -> 36%
where the time goes in v7:
time: 1020 us; the launch traced here: 1010 us
  Pallas kernels  418 us (41%)
  waiting for transfers between devices  297 us (29%)
  starting transfers between devices  122 us (12%)
  local copies, waits for them, and re-layouts  98.1 us (10%)
  other arithmetic  61.9 us (6%)
  between operations  15.6 us (2%)
    ppermute x29, waiting for transfers between devices, step_y(): return lax.ppermute(values, 'dp', [(0, 2), (2, 0), (1, 3), (3, 1)])  153 us
    pallas_call x4, Pallas kernels, ffn_rows_of(): pl.pallas_call(ffn_kernel, grid_spec=pltpu.PrefetchScalarGridSpec(num_sca...  102 us
    ppermute x3, waiting for transfers between devices, step_up(): lax.ppermute(values, 'col', [(i, (i + 1) % count) for i in range(count)])  82.7 us
    pallas_call x2, Pallas kernels, weight_products(): pl.pallas_call(functools.partial(weight_products_kernel, count), grid=(ri...  58 us
    pallas_call x4, Pallas kernels, local_backward(): pl.pallas_call(functools.partial(local_backward_kernel, min(512, length))...  50.3 us
    unnamed x258, local copies, waits for them, and re-layouts  42.4 us
    ppermute x29, waiting for transfers between devices, step_x(): return lax.ppermute(values, 'dp', [(0, 1), (1, 0), (2, 3), (3, 2)])  37.3 us
    pallas_call x3, Pallas kernels, sum_rows(): pl.pallas_call(functools.partial(sum_rows_kernel, count), grid=(tokens //...  35 us
  transfers between devices with their start and end apart: 90, of which 33 were waited for; matrix products, arithmetic and copies ran while one was open for 12% of the time, Pallas kernels for 36%

profile of v7, /device:TPU:0, one launch (start us, length us, event | category | flops | bytes accessed | tf_op | source)
XLA Modules:
  0.0 1012.7 jit_solution(12142723172134705596)
XLA Ops:
  43.0 36.7 %collective-permute-done.6.refs_0_ = bf16[512,1024]{1,0:T(8,128)(2,1)} collective-permute-done((bf16[512,1024]{1,0:T(8,128)(2,1)}, bf16[512,1024]{1,0:T(8,128)(2,1)}, u32[]{:S(2)}, u32[]{:S(2)}) %collective-permute-start.6) | collective-permute-done | bytes 1048608 | tf_op jit(solution)/shard_map/ppermute | solution.py:358
  84.4 3.6 shard_map.316
  91.5 6.1 collective-permute-start.15
  97.8 6.7 shard_map.317
  104.5 9.2 collective-permute-done.12.refs_2_
  116.2 6.1 shard_map.318.query_ref.key_ref.value_ref
  122.4 6.5 shard_map.319.refs_0_.refs_5_
  130.9 21.1 %collective-permute-done.15.refs_0_ = bf16[512,1024]{1,0:T(8,128)(2,1)S(1)} collective-permute-done((bf16[512,1024]{1,0:T(8,128)(2,1)}, bf16[512,1024]{1,0:T(8,128)(2,1)S(1)}, u32[]{:S(2)}, u32[]{:S(2)}) %collective-permute-start.15) | collective-permute-done | bytes 1048608 | tf_op jit(solution)/shard_map/ppermute | solution.py:358
  152.9 23.8 %collective-permute-start.20 = (bf16[512,1024]{1,0:T(8,128)(2,1)S(1)}, bf16[512,1024]{1,0:T(8,128)(2,1)S(1)}, u32[]{:S(2)}, u32[]{:S(2)}) collective-permute-start(bf16[512,1024]{1,0:T(8,128)(2,1)S(1)} %collective-permute-done.15.refs_0_), channel_id=1, source_target_pairs={{0,1},{1,2},{2,3},{3,0},{4,5},{5,6},{6,7},{7,4},{8,9},{9,10},{10,1... | collective-permute-start | bytes 3145736 | tf_op jit(solution)/shard_map/ppermute | solution.py:358
  176.7 3.8 shard_map.320
  183.8 5.6 shard_map.321.query_ref.key_ref.value_ref
  189.5 6.5 shard_map.322.refs_1_.refs_5_
  197.2 24.9 %collective-permute-done.20.refs_0_ = bf16[512,1024]{1,0:T(8,128)(2,1)S(1)} collective-permute-done((bf16[512,1024]{1,0:T(8,128)(2,1)S(1)}, bf16[512,1024]{1,0:T(8,128)(2,1)S(1)}, u32[]{:S(2)}, u32[]{:S(2)}) %collective-permute-start.20) | collective-permute-done | bytes 1048608 | tf_op jit(solution)/shard_map/ppermute | solution.py:358
  231.2 5.4 shard_map.324.query_ref.key_ref.value_ref
  236.7 6.5 shard_map.325.refs_2_.refs_5_
  250.4 8.8 collective-permute-done.24.refs_4_
  263.7 7.6 shard_map.327.refs_3_
  273.4 5.5 shard_map.328.query_ref.key_ref.value_ref
  278.9 6.7 shard_map.329.refs_0_.refs_5_
  285.6 6.5 collective-permute-done.28
  294.3 6.3 shard_map.330.rows_ref
  309.3 6.5 shard_map.331
  315.8 3.7 collective-permute-done.32
  331.2 25.4 %shard_map.332 = (bf16[512,4096]{1,0:T(8,128)(2,1)}, f32[4,1,512]{2,1,0:T(1,128)S(1)}, bf16[512,2048]{1,0:T(8,128)(2,1)S(1)}, bf16[512,2048]{1,0:T(8,128)(2,1)S(1)}) custom-call(s32[3]{0:T(128)S(1)} %pad_add_fusion.index_ref.refs_0_, bf16[512,2048]{1,0:T(8,128)(2,1)} %get-tuple-element.425.refs_0_.refs_1_, ...), custom_call_target="tpu_custom_call" | custom-call | flops 1717986944 | bytes 5033164 | tf_op jit(solution)/shard_map/pallas_call | solution.py:621
  356.6 10.5 %collective-permute-done.33.refs_0_.refs_1_.refs_2_ = bf16[512,2048]{1,0:T(8,128)(2,1)} collective-permute-done((bf16[512,2048]{1,0:T(8,128)(2,1)}, bf16[512,2048]{1,0:T(8,128)(2,1)}, u32[]{:S(2)}, u32[]{:S(2)}) %collective-permute-start.33) | collective-permute-done | bytes 2097184 | tf_op jit(solution)/shard_map/ppermute | solution.py:353
  378.0 25.6 %shard_map.333 = (bf16[512,4096]{1,0:T(8,128)(2,1)}, f32[4,1,512]{2,1,0:T(1,128)S(1)}, bf16[512,2048]{1,0:T(8,128)(2,1)S(1)}, bf16[512,2048]{1,0:T(8,128)(2,1)S(1)}) custom-call(s32[3]{0:T(128)S(1)} %pad_add_fusion.index_ref.refs_0_, bf16[512,2048]{1,0:T(8,128)(2,1)} %collective-permute-done.31.refs_0_.refs_1_, ...), custom_call_target="tpu_custom_call" | custom-call | flops 1717986944 | bytes 5033164 | tf_op jit(solution)/shard_map/pallas_call | solution.py:621
  405.5 25.3 %shard_map.334 = (bf16[512,4096]{1,0:T(8,128)(2,1)}, f32[4,1,512]{2,1,0:T(1,128)S(1)}, bf16[512,2048]{1,0:T(8,128)(2,1)S(1)}, bf16[512,2048]{1,0:T(8,128)(2,1)S(1)}) custom-call(s32[3]{0:T(128)S(1)} %pad_add_fusion.index_ref.refs_0_, bf16[512,2048]{1,0:T(8,128)(2,1)} %collective-permute-done.33.refs_0_.refs_1_.refs_2_, ...), custom_call_target="tpu_custom_call" | custom-call | flops 1717986944 | bytes 5033164 | tf_op jit(solution)/shard_map/pallas_call | solution.py:621
  434.9 25.4 %shard_map.335 = (bf16[512,4096]{1,0:T(8,128)(2,1)}, f32[4,1,512]{2,1,0:T(1,128)S(1)}, bf16[512,2048]{1,0:T(8,128)(2,1)S(1)}, bf16[512,2048]{1,0:T(8,128)(2,1)S(1)}) custom-call(s32[3]{0:T(128)S(1)} %pad_add_fusion.index_ref.refs_0_, bf16[512,2048]{1,0:T(8,128)(2,1)} %constant_dynamic-update-slice_fusion.refs_0_.refs_1_.refs_3_, ...), custom_call_target="tpu_custom_call" | custom-call | flops 1717986944 | bytes 5033164 | tf_op jit(solution)/shard_map/pallas_call | solution.py:621
  464.8 29.0 %shard_map.336 = bf16[4,1024,1024]{2,1,0:T(8,128)(2,1)} custom-call(bf16[512,2048]{1,0:T(8,128)(2,1)} %get-tuple-element.425.refs_0_.refs_1_, bf16[512,2048]{1,0:T(8,128)(2,1)} %collective-permute-done.31.refs_0_.refs_1_, bf16[512,2048]{1,0:T(8,128)(2,1)} %collective-permute-done.33.refs_0_.refs_1_.refs_2_, ...), custom_call_target="tpu_custom_call" | custom-call | flops 1717986944 | bytes 6710886 | tf_op jit(solution)/shard_map/pallas_call | solution.py:667
  493.8 3.7 add_convert_fusion.10
  497.5 29.1 %shard_map.337 = bf16[4,1024,1024]{2,1,0:T(8,128)(2,1)} custom-call(bf16[512,2048]{1,0:T(8,128)(2,1)} %get-tuple-element.425.refs_0_.refs_1_, bf16[512,2048]{1,0:T(8,128)(2,1)} %collective-permute-done.31.refs_0_.refs_1_, bf16[512,2048]{1,0:T(8,128)(2,1)} %collective-permute-done.33.refs_0_.refs_1_.refs_2_, ...), custom_call_target="tpu_custom_call" | custom-call | flops 1717986944 | bytes 6710886 | tf_op jit(solution)/shard_map/pallas_call | solution.py:667
  530.5 21.7 %collective-permute-done.40.refs_2_ = bf16[256,2048]{1,0:T(8,128)(2,1)S(1)} collective-permute-done((bf16[256,2048]{1,0:T(8,128)(2,1)S(1)}, bf16[256,2048]{1,0:T(8,128)(2,1)S(1)}, u32[]{:S(2)}, u32[]{:S(2)}) %collective-permute-start.40) | collective-permute-done | bytes 1048608 | tf_op jit(solution)/shard_map/ppermute | solution.py:353
  552.5 12.2 %shard_map.338 = (f32[512,2048]{1,0:T(8,128)}, bf16[512,2048]{1,0:T(8,128)(2,1)}, bf16[512,2048]{1,0:T(8,128)(2,1)}, f32[8,2048]{1,0:T(8,128)S(1)}) custom-call(s32[3]{0:T(128)S(1)} %pad_add_fusion.index_ref.refs_0_, bf16[512,2048]{1,0:T(8,128)(2,1)} %copy-done.38, bf16[256,2048]{1,0:T(8,128)(2,1)S(1)} %collective-permute-done.36.refs_1_, ...), custom_call_target="tpu_custom_call" | custom-call | bytes 2516582 | tf_op jit(solution)/shard_map/pallas_call | solution.py:1048
  567.0 10.2 %add_convert_fusion = (bf16[4,512,1024]{2,1,0:T(8,128)(2,1)}, bf16[4,512,1024]{2,1,0:T(8,128)(2,1)}) fusion(bf16[4,1024,1024]{2,1,0:T(8,128)(2,1)} %collective-permute-done.42, bf16[4,1024,1024]{2,1,0:T(8,128)(2,1)} %shard_map.336), kind=kLoop, calls=%fused_computation.2 | loop fusion | flops 16777216 | bytes 25165824 | tf_op jit(solution)/shard_map/convert_element_type | solution.py:418
  582.1 3.2 fusion.17
  587.6 8.0 shard_map.340.grad_ref
  595.6 12.4 %shard_map.341.refs_4_.refs_3_ = bf16[1024,768]{1,0:T(8,128)(2,1)S(1)} custom-call(s32[1,1024]{1,0:T(1,128)S(1)} %bitcast.54, bf16[1024,768]{1,0:T(8,128)(2,1)S(1)} %shard_map.328.query_ref.key_ref.value_ref, bf16[1024,1024]{1,0:T(8,128)(2,1)S(1)} %shard_map.340.grad_ref, bf16[1024,768]{1,0:T(8,128)(2,1)S(1)} %shard_map.328.query_ref.key_ref.value_ref, ...), custom_call_target="tpu_custom_call" | custom-call | flops 858993472 | bytes 629145 | tf_op jit(solution)/shard_map/pallas_call | solution.py:544
  608.0 8.9 shard_map.342
  626.1 12.5 %shard_map.343.refs_4_.refs_2_ = bf16[1024,768]{1,0:T(8,128)(2,1)S(1)} custom-call(s32[1,1024]{1,0:T(1,128)S(1)} %bitcast.55, bf16[1024,768]{1,0:T(8,128)(2,1)S(1)} %copy-done.5, bf16[1024,1024]{1,0:T(8,128)(2,1)S(1)} %shard_map.340.grad_ref, bf16[1024,768]{1,0:T(8,128)(2,1)S(1)} %copy-done.5, bf16[1024,768]{1,0:T(8,128)(2,1)S(1)} %copy-done.5), custom_call_target="tpu_custom_call" | custom-call | flops 858993472 | bytes 629145 | tf_op jit(solution)/shard_map/pallas_call | solution.py:544
  638.7 8.3 shard_map.344
  655.6 8.0 collective-permute-done.50
  668.2 13.5 %reduce-scatter.5.cloned.1.call-done = bf16[1,512,1024]{2,1,0:T(8,128)(2,1)} async-done(((bf16[4,512,1024]{2,1,0:T(8,128)(2,1)}), bf16[1,512,1024]{2,1,0:T(8,128)(2,1)}) %reduce-scatter.5.cloned.1.call-update) | async-done | bytes 1048592 | tf_op jit(solution)/shard_map/reduce_scatter | solution.py:1489
  683.3 12.6 %shard_map.345.refs_4_.refs_1_ = bf16[1024,768]{1,0:T(8,128)(2,1)S(1)} custom-call(s32[1,1024]{1,0:T(1,128)S(1)} %bitcast.56, bf16[1024,768]{1,0:T(8,128)(2,1)S(1)} %copy-done.3, bf16[1024,1024]{1,0:T(8,128)(2,1)S(1)} %copy-done.7, bf16[1024,768]{1,0:T(8,128)(2,1)S(1)} %copy-done.3, bf16[1024,768]{1,0:T(8,128)(2,1)S(1)} %copy-done.3), custom_call_target="tpu_custom_call" | custom-call | flops 858993472 | bytes 629145 | tf_op jit(solution)/shard_map/pallas_call | solution.py:544
  696.0 8.8 shard_map.346
  714.9 7.5 collective-permute-done.52
  725.3 12.8 %shard_map.347.refs_4_.refs_0_ = bf16[1024,768]{1,0:T(8,128)(2,1)S(1)} custom-call(s32[1,1024]{1,0:T(1,128)S(1)} %bitcast.57, bf16[1024,768]{1,0:T(8,128)(2,1)S(1)} %copy-done.1, bf16[1024,1024]{1,0:T(8,128)(2,1)S(1)} %copy-done.8, bf16[1024,768]{1,0:T(8,128)(2,1)S(1)} %copy-done.1, bf16[1024,768]{1,0:T(8,128)(2,1)S(1)} %copy-done.1), custom_call_target="tpu_custom_call" | custom-call | flops 858993472 | bytes 629145 | tf_op jit(solution)/shard_map/pallas_call | solution.py:544
  738.2 8.3 shard_map.348
  756.0 11.6 %collective-permute-start.57 = (bf16[256,2048]{1,0:T(8,128)(2,1)}, bf16[256,2048]{1,0:T(8,128)(2,1)}, u32[]{:S(2)}, u32[]{:S(2)}) collective-permute-start(bf16[256,2048]{1,0:T(8,128)(2,1)} %add_convert_fusion.7), channel_id=1, source_target_pairs={{0,3},{1,0},{2,1},{3,2},{4,7},{5,4},{6,5},{7,6},{8,11},{9,8},{10,9... | collective-permute-start | bytes 3145736 | tf_op jit(solution)/shard_map/ppermute | solution.py:363
  776.3 15.8 %collective-permute-done.56 = bf16[256,1024]{1,0:T(8,128)(2,1)S(1)} collective-permute-done((bf16[256,1024]{1,0:T(8,128)(2,1)}, bf16[256,1024]{1,0:T(8,128)(2,1)S(1)}, u32[]{:S(2)}, u32[]{:S(2)}) %collective-permute-start.56) | collective-permute-done | bytes 524320 | tf_op jit(solution)/shard_map/ppermute | solution.py:353
  796.6 3.7 add_convert_fusion.5
  800.3 21.2 %shard_map.349.refs_0_ = f32[1024,2048]{1,0:T(8,128)} custom-call(bf16[1024,768]{1,0:T(8,128)(2,1)S(1)} %shard_map.347.refs_4_.refs_0_, bf16[1024,768]{1,0:T(8,128)(2,1)S(1)} %copy-done.29, bf16[1024,768]{1,0:T(8,128)(2,1)S(1)} %shard_map.343.refs_4_.refs_2_, bf16[1024,768]{1,0:T(8,128)(2,1)} %copy-done.27, ...), custom_call_target="tpu_custom_call" | custom-call | flops 1288490240 | bytes 838860 | tf_op jit(solution)/shard_map/pallas_call | solution.py:862
  828.2 32.6 %collective-permute-done.61 = bf16[256,2048]{1,0:T(8,128)(2,1)} collective-permute-done((bf16[256,2048]{1,0:T(8,128)(2,1)}, bf16[256,2048]{1,0:T(8,128)(2,1)}, u32[]{:S(2)}, u32[]{:S(2)}) %collective-permute-start.61) | collective-permute-done | bytes 1048608 | tf_op jit(solution)/shard_map/ppermute | solution.py:353
  868.2 3.6 add_convert_fusion.3
  871.8 19.2 %collective-permute-done.64.refs_3_ = bf16[256,2048]{1,0:T(8,128)(2,1)S(1)} collective-permute-done((bf16[256,2048]{1,0:T(8,128)(2,1)}, bf16[256,2048]{1,0:T(8,128)(2,1)S(1)}, u32[]{:S(2)}, u32[]{:S(2)}) %collective-permute-start.64) | collective-permute-done | bytes 1048608 | tf_op jit(solution)/shard_map/ppermute | solution.py:353
  890.9 8.4 shard_map.350
  908.5 7.9 shard_map.351
  920.9 4.2 shard_map.352
  925.2 11.8 %collective-permute-done.71 = bf16[256,2048]{1,0:T(8,128)(2,1)} collective-permute-done((bf16[256,2048]{1,0:T(8,128)(2,1)}, bf16[256,2048]{1,0:T(8,128)(2,1)}, u32[]{:S(2)}, u32[]{:S(2)}) %collective-permute-start.71) | collective-permute-done | bytes 1048608 | tf_op jit(solution)/shard_map/ppermute | solution.py:349
  937.3 4.1 collective-permute-done.72
  946.6 3.2 collective-permute-done.76
  959.4 15.1 %collective-permute-done.82.refs_2_ = bf16[256,2048]{1,0:T(8,128)(2,1)S(1)} collective-permute-done((bf16[256,2048]{1,0:T(8,128)(2,1)S(1)}, bf16[256,2048]{1,0:T(8,128)(2,1)S(1)}, u32[]{:S(2)}, u32[]{:S(2)}) %collective-permute-start.82) | collective-permute-done | bytes 1048608 | tf_op jit(solution)/shard_map/ppermute | solution.py:353
  978.7 8.0 shard_map.354
  995.8 3.6 collective-permute-done.83.refs_3_
  1000.5 5.5 shard_map.355
  (561 shorter events, 250.7 us)
Async XLA Ops:
  7.2 299.4 %all-gather.9.cloned.1.call-start = ((), (), s32[]{:S(2)}) async-start(), calls=%async_computation.6 | async-start | bytes 18874368 | tf_op jit(solution)/shard_map/all_gather | solution.py:1358
  10.5 18.7 %collective-permute-start.4 = (bf16[512,1024]{1,0:T(8,128)(2,1)}, bf16[512,1024]{1,0:T(8,128)(2,1)}, u32[]{:S(2)}, u32[]{:S(2)}) collective-permute-start(bf16[512,1024]{1,0:T(8,128)(2,1)} %get-tuple-element.620), channel_id=1, source_target_pairs={{0,4},{4,0},{1,5},{5,1},{2,6},{6,2},{3,7},{7,3},{8,12},{12,8},{9,1... | collective-permute-start | bytes 3145736 | tf_op jit(solution)/shard_map/ppermute | solution.py:345
  11.9 17.3 %collective-permute-start.1 = (f32[1280]{0:T(1024)S(1)}, f32[1280]{0:T(1024)S(1)}, u32[]{:S(2)}, u32[]{:S(2)}) collective-permute-start(f32[1280]{0:T(1024)S(1)} %pad_maximum_fusion.18), channel_id=1, source_target_pairs={{0,1},{1,2},{2,3},{3,0},{4,5},{5,6},{6,7},{7,4},{8,9},{9,10},{10,1... | collective-permute-start | bytes 15368 | tf_op jit(solution)/shard_map/ppermute | solution.py:1342
  17.1 17.5 %collective-permute-start.5 = (bf16[1024,1024]{1,0:T(8,128)(2,1)S(1)}, bf16[1024,1024]{1,0:T(8,128)(2,1)}, u32[]{:S(2)}, u32[]{:S(2)}) collective-permute-start(bf16[1024,1024]{1,0:T(8,128)(2,1)S(1)} %copy-done.9), channel_id=1, source_target_pairs={{0,4},{4,0},{1,5},{5,1},{2,6},{6,2},{3,7},{7,3},{8,12},{12,8},{9,1... | collective-permute-start | bytes 6291464 | tf_op jit(solution)/shard_map/ppermute | solution.py:345
  39.2 642.4 %reduce-scatter.5.cloned.1.call-start = ((), (), s32[]{:S(2)}) async-start(), calls=%async_computation.4 | async-start | bytes 5242880 | tf_op jit(solution)/shard_map/reduce_scatter | solution.py:1489
  39.3 40.4 %collective-permute-start.6 = (bf16[512,1024]{1,0:T(8,128)(2,1)}, bf16[512,1024]{1,0:T(8,128)(2,1)}, u32[]{:S(2)}, u32[]{:S(2)}) collective-permute-start(bf16[512,1024]{1,0:T(8,128)(2,1)} %pad_maximum_fusion.2), channel_id=1, source_target_pairs={{0,1},{1,2},{2,3},{3,0},{4,5},{5,6},{6,7},{7,4},{8,9},{9,10},{10,1... | collective-permute-start | bytes 3145736 | tf_op jit(solution)/shard_map/ppermute | solution.py:358
  40.0 39.7 %collective-permute-start.7 = (bf16[256,2048]{1,0:T(8,128)(2,1)}, bf16[256,2048]{1,0:T(8,128)(2,1)S(1)}, u32[]{:S(2)}, u32[]{:S(2)}) collective-permute-start(bf16[256,2048]{1,0:T(8,128)(2,1)} %get-tuple-element.303), channel_id=1, source_target_pairs={{0,8},{8,0},{16,24},{24,16},{1,9},{9,1},{17,25},{25,17},{2,10},{10... | collective-permute-start | bytes 3145736 | tf_op jit(solution)/shard_map/ppermute | solution.py:349
  41.5 39.2 %collective-permute-start.8 = (bf16[256,2048]{1,0:T(8,128)(2,1)}, bf16[256,2048]{1,0:T(8,128)(2,1)}, u32[]{:S(2)}, u32[]{:S(2)}) collective-permute-start(bf16[256,2048]{1,0:T(8,128)(2,1)} %get-tuple-element.303), channel_id=1, source_target_pairs={{0,16},{16,0},{8,24},{24,8},{1,17},{17,1},{9,25},{25,9},{2,18},{18... | collective-permute-start | bytes 3145736 | tf_op jit(solution)/shard_map/ppermute | solution.py:353
  88.0 28.3 %collective-permute-start.10 = (bf16[1024,1024]{1,0:T(8,128)(2,1)}, bf16[1024,1024]{1,0:T(8,128)(2,1)}, u32[]{:S(2)}, u32[]{:S(2)}) collective-permute-start(bf16[1024,1024]{1,0:T(8,128)(2,1)} %get-tuple-element.314), channel_id=1, source_target_pairs={{0,4},{4,0},{1,5},{5,1},{2,6},{6,2},{3,7},{7,3},{8,12},{12,8},{9,1... | collective-permute-start | bytes 6291464 | tf_op jit(solution)/shard_map/ppermute | solution.py:345
  88.0 25.8 %collective-permute-start.12 = (bf16[512,1024]{1,0:T(8,128)(2,1)}, bf16[512,1024]{1,0:T(8,128)(2,1)S(1)}, u32[]{:S(2)}, u32[]{:S(2)}) collective-permute-start(bf16[512,1024]{1,0:T(8,128)(2,1)} %collective-permute-done.6.refs_0_), channel_id=1, source_target_pairs={{0,16},{16,0},{8,24},{24,8},{1,17},{17,1},{9,25},{25,9},{2,18},{18... | collective-permute-start | bytes 3145736 | tf_op jit(solution)/shard_map/ppermute | solution.py:353
  89.5 25.6 %collective-permute-start.11 = (bf16[512,1024]{1,0:T(8,128)(2,1)}, bf16[512,1024]{1,0:T(8,128)(2,1)}, u32[]{:S(2)}, u32[]{:S(2)}) collective-permute-start(bf16[512,1024]{1,0:T(8,128)(2,1)} %collective-permute-done.6.refs_0_), channel_id=1, source_target_pairs={{0,8},{8,0},{16,24},{24,16},{1,9},{9,1},{17,25},{25,17},{2,10},{10... | collective-permute-start | bytes 3145736 | tf_op jit(solution)/shard_map/ppermute | solution.py:349
  91.5 60.4 %collective-permute-start.15 = (bf16[512,1024]{1,0:T(8,128)(2,1)}, bf16[512,1024]{1,0:T(8,128)(2,1)S(1)}, u32[]{:S(2)}, u32[]{:S(2)}) collective-permute-start(bf16[512,1024]{1,0:T(8,128)(2,1)} %collective-permute-done.6.refs_0_), channel_id=1, source_target_pairs={{0,1},{1,2},{2,3},{3,0},{4,5},{5,6},{6,7},{7,4},{8,9},{9,10},{10,1... | collective-permute-start | bytes 3145736 | tf_op jit(solution)/shard_map/ppermute | solution.py:358
  128.9 23.0 %collective-permute-start.13 = (bf16[256,1024]{1,0:T(8,128)(2,1)S(1)}, bf16[256,1024]{1,0:T(8,128)(2,1)S(1)}, u32[]{:S(2)}, u32[]{:S(2)}) collective-permute-start(bf16[256,1024]{1,0:T(8,128)(2,1)S(1)} %slice.429), channel_id=1, source_target_pairs={{0,16},{16,0},{8,24},{24,8},{1,17},{17,1},{9,25},{25,9},{2,18},{18... | collective-permute-start | bytes 1572872 | tf_op jit(solution)/shard_map/ppermute | solution.py:353
  129.4 22.6 %collective-permute-start.14 = (bf16[256,1024]{1,0:T(8,128)(2,1)S(1)}, bf16[256,1024]{1,0:T(8,128)(2,1)S(1)}, u32[]{:S(2)}, u32[]{:S(2)}) collective-permute-start(bf16[256,1024]{1,0:T(8,128)(2,1)S(1)} %slice.430), channel_id=1, source_target_pairs={{0,8},{8,0},{16,24},{24,16},{1,9},{9,1},{17,25},{25,17},{2,10},{10... | collective-permute-start | bytes 1572872 | tf_op jit(solution)/shard_map/ppermute | solution.py:349
  152.0 44.0 %collective-permute-start.17 = (bf16[512,1024]{1,0:T(8,128)(2,1)S(1)}, bf16[512,1024]{1,0:T(8,128)(2,1)S(1)}, u32[]{:S(2)}, u32[]{:S(2)}) collective-permute-start(bf16[512,1024]{1,0:T(8,128)(2,1)S(1)} %collective-permute-done.15.refs_0_), channel_id=1, source_target_pairs={{0,16},{16,0},{8,24},{24,8},{1,17},{17,1},{9,25},{25,9},{2,18},{18... | collective-permute-start | bytes 3145736 | tf_op jit(solution)/shard_map/ppermute | solution.py:353
  152.4 43.7 %collective-permute-start.16 = (bf16[512,1024]{1,0:T(8,128)(2,1)S(1)}, bf16[512,1024]{1,0:T(8,128)(2,1)S(1)}, u32[]{:S(2)}, u32[]{:S(2)}) collective-permute-start(bf16[512,1024]{1,0:T(8,128)(2,1)S(1)} %collective-permute-done.15.refs_0_), channel_id=1, source_target_pairs={{0,8},{8,0},{16,24},{24,16},{1,9},{9,1},{17,25},{25,17},{2,10},{10... | collective-permute-start | bytes 3145736 | tf_op jit(solution)/shard_map/ppermute | solution.py:349
  152.9 69.2 %collective-permute-start.20 = (bf16[512,1024]{1,0:T(8,128)(2,1)S(1)}, bf16[512,1024]{1,0:T(8,128)(2,1)S(1)}, u32[]{:S(2)}, u32[]{:S(2)}) collective-permute-start(bf16[512,1024]{1,0:T(8,128)(2,1)S(1)} %collective-permute-done.15.refs_0_), channel_id=1, source_target_pairs={{0,1},{1,2},{2,3},{3,0},{4,5},{5,6},{6,7},{7,4},{8,9},{9,10},{10,1... | collective-permute-start | bytes 3145736 | tf_op jit(solution)/shard_map/ppermute | solution.py:358
  196.1 26.0 %collective-permute-start.18 = (bf16[256,1024]{1,0:T(8,128)(2,1)S(1)}, bf16[256,1024]{1,0:T(8,128)(2,1)S(1)}, u32[]{:S(2)}, u32[]{:S(2)}) collective-permute-start(bf16[256,1024]{1,0:T(8,128)(2,1)S(1)} %slice.432), channel_id=1, source_target_pairs={{0,16},{16,0},{8,24},{24,8},{1,17},{17,1},{9,25},{25,9},{2,18},{18... | collective-permute-start | bytes 1572872 | tf_op jit(solution)/shard_map/ppermute | solution.py:353
  196.6 25.5 %collective-permute-start.19 = (bf16[256,1024]{1,0:T(8,128)(2,1)S(1)}, bf16[256,1024]{1,0:T(8,128)(2,1)S(1)}, u32[]{:S(2)}, u32[]{:S(2)}) collective-permute-start(bf16[256,1024]{1,0:T(8,128)(2,1)S(1)} %slice.433), channel_id=1, source_target_pairs={{0,8},{8,0},{16,24},{24,16},{1,9},{9,1},{17,25},{25,17},{2,10},{10... | collective-permute-start | bytes 1572872 | tf_op jit(solution)/shard_map/ppermute | solution.py:349
  222.1 23.7 %collective-permute-start.22 = (bf16[512,1024]{1,0:T(8,128)(2,1)S(1)}, bf16[512,1024]{1,0:T(8,128)(2,1)S(1)}, u32[]{:S(2)}, u32[]{:S(2)}) collective-permute-start(bf16[512,1024]{1,0:T(8,128)(2,1)S(1)} %collective-permute-done.20.refs_0_), channel_id=1, source_target_pairs={{0,16},{16,0},{8,24},{24,8},{1,17},{17,1},{9,25},{25,9},{2,18},{18... | collective-permute-start | bytes 3145736 | tf_op jit(solution)/shard_map/ppermute | solution.py:353
  223.7 23.4 %collective-permute-start.21 = (bf16[512,1024]{1,0:T(8,128)(2,1)S(1)}, bf16[512,1024]{1,0:T(8,128)(2,1)S(1)}, u32[]{:S(2)}, u32[]{:S(2)}) collective-permute-start(bf16[512,1024]{1,0:T(8,128)(2,1)S(1)} %collective-permute-done.20.refs_0_), channel_id=1, source_target_pairs={{0,8},{8,0},{16,24},{24,16},{1,9},{9,1},{17,25},{25,17},{2,10},{10... | collective-permute-start | bytes 3145736 | tf_op jit(solution)/shard_map/ppermute | solution.py:349
  271.3 20.8 %collective-permute-start.28 = (bf16[256,2048]{1,0:T(8,128)(2,1)S(1)}, bf16[256,2048]{1,0:T(8,128)(2,1)S(1)}, u32[]{:S(2)}, u32[]{:S(2)}) collective-permute-start(bf16[256,2048]{1,0:T(8,128)(2,1)S(1)} %copy-done.85), channel_id=1, source_target_pairs={{0,8},{8,0},{16,24},{24,16},{1,9},{9,1},{17,25},{25,17},{2,10},{10... | collective-permute-start | bytes 3145736 | tf_op jit(solution)/shard_map/ppermute | solution.py:349
  272.3 21.1 %collective-permute-start.27 = (bf16[256,2048]{1,0:T(8,128)(2,1)S(1)}, bf16[256,2048]{1,0:T(8,128)(2,1)S(1)}, u32[]{:S(2)}, u32[]{:S(2)}) collective-permute-start(bf16[256,2048]{1,0:T(8,128)(2,1)S(1)} %copy-done.85), channel_id=1, source_target_pairs={{0,16},{16,0},{8,24},{24,8},{1,17},{17,1},{9,25},{25,9},{2,18},{18... | collective-permute-start | bytes 3145736 | tf_op jit(solution)/shard_map/ppermute | solution.py:353
  319.9 47.3 %collective-permute-start.33 = (bf16[512,2048]{1,0:T(8,128)(2,1)}, bf16[512,2048]{1,0:T(8,128)(2,1)}, u32[]{:S(2)}, u32[]{:S(2)}) collective-permute-start(bf16[512,2048]{1,0:T(8,128)(2,1)} %get-tuple-element.425.refs_0_.refs_1_), channel_id=1, source_target_pairs={{0,16},{16,0},{8,24},{24,8},{1,17},{17,1},{9,25},{25,9},{2,18},{18... | collective-permute-start | bytes 6291464 | tf_op jit(solution)/shard_map/ppermute | solution.py:353
  321.2 47.3 %collective-permute-start.31 = (bf16[512,2048]{1,0:T(8,128)(2,1)}, bf16[512,2048]{1,0:T(8,128)(2,1)}, u32[]{:S(2)}, u32[]{:S(2)}) collective-permute-start(bf16[512,2048]{1,0:T(8,128)(2,1)} %get-tuple-element.425.refs_0_.refs_1_), channel_id=1, source_target_pairs={{0,8},{8,0},{16,24},{24,16},{1,9},{9,1},{17,25},{25,17},{2,10},{10... | collective-permute-start | bytes 6291464 | tf_op jit(solution)/shard_map/ppermute | solution.py:349
  369.9 34.8 %collective-permute-start.35 = (bf16[256,2048]{1,0:T(8,128)(2,1)S(1)}, bf16[256,2048]{1,0:T(8,128)(2,1)S(1)}, u32[]{:S(2)}, u32[]{:S(2)}) collective-permute-start(bf16[256,2048]{1,0:T(8,128)(2,1)S(1)} %slice.449), channel_id=1, source_target_pairs={{0,8},{8,0},{16,24},{24,16},{1,9},{9,1},{17,25},{25,17},{2,10},{10... | collective-permute-start | bytes 3145736 | tf_op jit(solution)/shard_map/ppermute | solution.py:349
  371.1 60.9 %collective-permute-start.34 = (bf16[256,2048]{1,0:T(8,128)(2,1)S(1)}, bf16[256,2048]{1,0:T(8,128)(2,1)S(1)}, u32[]{:S(2)}, u32[]{:S(2)}) collective-permute-start(bf16[256,2048]{1,0:T(8,128)(2,1)S(1)} %slice.445), channel_id=1, source_target_pairs={{0,16},{16,0},{8,24},{24,8},{1,17},{17,1},{9,25},{25,9},{2,18},{18... | collective-permute-start | bytes 3145736 | tf_op jit(solution)/shard_map/ppermute | solution.py:353
  404.7 57.5 %collective-permute-start.36 = (bf16[256,2048]{1,0:T(8,128)(2,1)}, bf16[256,2048]{1,0:T(8,128)(2,1)S(1)}, u32[]{:S(2)}, u32[]{:S(2)}) collective-permute-start(bf16[256,2048]{1,0:T(8,128)(2,1)} %slice.346), channel_id=1, source_target_pairs={{0,8},{8,0},{16,24},{24,16},{1,9},{9,1},{17,25},{25,17},{2,10},{10... | collective-permute-start | bytes 3145736 | tf_op jit(solution)/shard_map/ppermute | solution.py:349
  431.9 30.3 %collective-permute-start.37 = (bf16[256,2048]{1,0:T(8,128)(2,1)}, bf16[256,2048]{1,0:T(8,128)(2,1)}, u32[]{:S(2)}, u32[]{:S(2)}) collective-permute-start(bf16[256,2048]{1,0:T(8,128)(2,1)} %slice.347), channel_id=1, source_target_pairs={{0,16},{16,0},{8,24},{24,8},{1,17},{17,1},{9,25},{25,9},{2,18},{18... | collective-permute-start | bytes 3145736 | tf_op jit(solution)/shard_map/ppermute | solution.py:353
  462.2 31.6 %collective-permute-start.39 = (bf16[256,2048]{1,0:T(8,128)(2,1)}, bf16[256,2048]{1,0:T(8,128)(2,1)}, u32[]{:S(2)}, u32[]{:S(2)}) collective-permute-start(bf16[256,2048]{1,0:T(8,128)(2,1)} %get-tuple-element.414), channel_id=1, source_target_pairs={{0,16},{16,0},{8,24},{24,8},{1,17},{17,1},{9,25},{25,9},{2,18},{18... | collective-permute-start | bytes 3145736 | tf_op jit(solution)/shard_map/ppermute | solution.py:353
  463.6 30.2 %collective-permute-start.38 = (bf16[256,2048]{1,0:T(8,128)(2,1)}, bf16[256,2048]{1,0:T(8,128)(2,1)}, u32[]{:S(2)}, u32[]{:S(2)}) collective-permute-start(bf16[256,2048]{1,0:T(8,128)(2,1)} %get-tuple-element.412), channel_id=1, source_target_pairs={{0,8},{8,0},{16,24},{24,16},{1,9},{9,1},{17,25},{25,17},{2,10},{10... | collective-permute-start | bytes 3145736 | tf_op jit(solution)/shard_map/ppermute | solution.py:349
  526.6 40.5 %collective-permute-start.42 = (bf16[4,1024,1024]{2,1,0:T(8,128)(2,1)}, bf16[4,1024,1024]{2,1,0:T(8,128)(2,1)}, u32[]{:S(2)}, u32[]{:S(2)}) collective-permute-start(bf16[4,1024,1024]{2,1,0:T(8,128)(2,1)} %shard_map.337), channel_id=1, source_target_pairs={{0,4},{4,0},{1,5},{5,1},{2,6},{6,2},{3,7},{7,3},{8,12},{12,8},{9,1... | collective-permute-start | bytes 25165832 | tf_op jit(solution)/shard_map/ppermute | solution.py:345
  526.6 25.6 %collective-permute-start.40 = (bf16[256,2048]{1,0:T(8,128)(2,1)S(1)}, bf16[256,2048]{1,0:T(8,128)(2,1)S(1)}, u32[]{:S(2)}, u32[]{:S(2)}) collective-permute-start(bf16[256,2048]{1,0:T(8,128)(2,1)S(1)} %copy-done.89), channel_id=1, source_target_pairs={{0,16},{16,0},{8,24},{24,8},{1,17},{17,1},{9,25},{25,9},{2,18},{18... | collective-permute-start | bytes 3145736 | tf_op jit(solution)/shard_map/ppermute | solution.py:353
  527.3 25.2 %collective-permute-start.41 = (bf16[256,2048]{1,0:T(8,128)(2,1)S(1)}, bf16[256,2048]{1,0:T(8,128)(2,1)S(1)}, u32[]{:S(2)}, u32[]{:S(2)}) collective-permute-start(bf16[256,2048]{1,0:T(8,128)(2,1)S(1)} %copy-done.88), channel_id=1, source_target_pairs={{0,8},{8,0},{16,24},{24,16},{1,9},{9,1},{17,25},{25,17},{2,10},{10... | collective-permute-start | bytes 3145736 | tf_op jit(solution)/shard_map/ppermute | solution.py:349
  580.3 247.8 %reduce-scatter.3.cloned.1.call-start = ((), (), s32[]{:S(2)}) async-start(), calls=%async_computation.2 | async-start | bytes 5242880 | tf_op jit(solution)/shard_map/reduce_scatter | solution.py:1489
  581.1 395.5 %all-gather.7.cloned.1.call-start = ((), (), s32[]{:S(2)}) async-start(), calls=%async_computation.5 | async-start | bytes 5242880 | tf_op jit(solution)/shard_map/all_gather | solution.py:1490
  585.3 34.3 %collective-permute-start.45 = (bf16[256,2048]{1,0:T(8,128)(2,1)}, bf16[256,2048]{1,0:T(8,128)(2,1)S(1)}, u32[]{:S(2)}, u32[]{:S(2)}) collective-permute-start(bf16[256,2048]{1,0:T(8,128)(2,1)} %get-tuple-element.448), channel_id=1, source_target_pairs={{0,8},{8,0},{16,24},{24,16},{1,9},{9,1},{17,25},{25,17},{2,10},{10... | collective-permute-start | bytes 3145736 | tf_op jit(solution)/shard_map/ppermute | solution.py:349
  586.2 33.4 %collective-permute-start.46 = (bf16[256,2048]{1,0:T(8,128)(2,1)}, bf16[256,2048]{1,0:T(8,128)(2,1)}, u32[]{:S(2)}, u32[]{:S(2)}) collective-permute-start(bf16[256,2048]{1,0:T(8,128)(2,1)} %get-tuple-element.449), channel_id=1, source_target_pairs={{0,16},{16,0},{8,24},{24,8},{1,17},{17,1},{9,25},{25,9},{2,18},{18... | collective-permute-start | bytes 3145736 | tf_op jit(solution)/shard_map/ppermute | solution.py:353
  624.3 30.0 %collective-permute-start.48 = (bf16[256,1024]{1,0:T(8,128)(2,1)S(1)}, bf16[256,1024]{1,0:T(8,128)(2,1)S(1)}, u32[]{:S(2)}, u32[]{:S(2)}) collective-permute-start(bf16[256,1024]{1,0:T(8,128)(2,1)S(1)} %get-tuple-element.462), channel_id=1, source_target_pairs={{0,16},{16,0},{8,24},{24,8},{1,17},{17,1},{9,25},{25,9},{2,18},{18... | collective-permute-start | bytes 1572872 | tf_op jit(solution)/shard_map/ppermute | solution.py:353
  625.0 29.3 %collective-permute-start.47 = (bf16[256,1024]{1,0:T(8,128)(2,1)S(1)}, bf16[256,1024]{1,0:T(8,128)(2,1)S(1)}, u32[]{:S(2)}, u32[]{:S(2)}) collective-permute-start(bf16[256,1024]{1,0:T(8,128)(2,1)S(1)} %get-tuple-element.460), channel_id=1, source_target_pairs={{0,8},{8,0},{16,24},{24,16},{1,9},{9,1},{17,25},{25,17},{2,10},{10... | collective-permute-start | bytes 1572872 | tf_op jit(solution)/shard_map/ppermute | solution.py:349
  666.8 85.7 %collective-permute-start.54 = (bf16[256,2048]{1,0:T(8,128)(2,1)}, bf16[256,2048]{1,0:T(8,128)(2,1)}, u32[]{:S(2)}, u32[]{:S(2)}) collective-permute-start(bf16[256,2048]{1,0:T(8,128)(2,1)} %pad_maximum_fusion.4), channel_id=1, source_target_pairs={{0,16},{16,0},{8,24},{24,8},{1,17},{17,1},{9,25},{25,9},{2,18},{18... | collective-permute-start | bytes 3145736 | tf_op jit(solution)/shard_map/ppermute | solution.py:353
  667.3 85.1 %collective-permute-start.53 = (bf16[256,2048]{1,0:T(8,128)(2,1)}, bf16[256,2048]{1,0:T(8,128)(2,1)}, u32[]{:S(2)}, u32[]{:S(2)}) collective-permute-start(bf16[256,2048]{1,0:T(8,128)(2,1)} %pad_maximum_fusion.3), channel_id=1, source_target_pairs={{0,8},{8,0},{16,24},{24,16},{1,9},{9,1},{17,25},{25,17},{2,10},{10... | collective-permute-start | bytes 3145736 | tf_op jit(solution)/shard_map/ppermute | solution.py:349
  681.7 294.8 %all-gather.5.cloned.1.call-start = ((), (), s32[]{:S(2)}) async-start(), calls=%async_computation.3 | async-start | bytes 5242880 | tf_op jit(solution)/shard_map/all_gather | solution.py:1490
  705.9 16.4 %collective-permute-start.51 = (bf16[256,1024]{1,0:T(8,128)(2,1)S(1)}, bf16[256,1024]{1,0:T(8,128)(2,1)S(1)}, u32[]{:S(2)}, u32[]{:S(2)}) collective-permute-start(bf16[256,1024]{1,0:T(8,128)(2,1)S(1)} %get-tuple-element.478), channel_id=1, source_target_pairs={{0,8},{8,0},{16,24},{24,16},{1,9},{9,1},{17,25},{25,17},{2,10},{10... | collective-permute-start | bytes 1572872 | tf_op jit(solution)/shard_map/ppermute | solution.py:349
  722.3 73.2 %collective-permute-start.59 = (bf16[256,2048]{1,0:T(8,128)(2,1)}, bf16[256,2048]{1,0:T(8,128)(2,1)}, u32[]{:S(2)}, u32[]{:S(2)}) collective-permute-start(bf16[256,2048]{1,0:T(8,128)(2,1)} %pad_maximum_fusion.6), channel_id=1, source_target_pairs={{0,16},{16,0},{8,24},{24,8},{1,17},{17,1},{9,25},{25,9},{2,18},{18... | collective-permute-start | bytes 3145736 | tf_op jit(solution)/shard_map/ppermute | solution.py:353
  723.9 72.7 %collective-permute-start.58 = (bf16[256,2048]{1,0:T(8,128)(2,1)}, bf16[256,2048]{1,0:T(8,128)(2,1)}, u32[]{:S(2)}, u32[]{:S(2)}) collective-permute-start(bf16[256,2048]{1,0:T(8,128)(2,1)} %pad_maximum_fusion.5), channel_id=1, source_target_pairs={{0,8},{8,0},{16,24},{24,16},{1,9},{9,1},{17,25},{25,17},{2,10},{10... | collective-permute-start | bytes 3145736 | tf_op jit(solution)/shard_map/ppermute | solution.py:349
  756.0 40.5 %collective-permute-start.57 = (bf16[256,2048]{1,0:T(8,128)(2,1)}, bf16[256,2048]{1,0:T(8,128)(2,1)}, u32[]{:S(2)}, u32[]{:S(2)}) collective-permute-start(bf16[256,2048]{1,0:T(8,128)(2,1)} %add_convert_fusion.7), channel_id=1, source_target_pairs={{0,3},{1,0},{2,1},{3,2},{4,7},{5,4},{6,5},{7,6},{8,11},{9,8},{10,9... | collective-permute-start | bytes 3145736 | tf_op jit(solution)/shard_map/ppermute | solution.py:363
  767.7 26.8 %collective-permute-start.55 = (bf16[256,1024]{1,0:T(8,128)(2,1)}, bf16[256,1024]{1,0:T(8,128)(2,1)S(1)}, u32[]{:S(2)}, u32[]{:S(2)}) collective-permute-start(bf16[256,1024]{1,0:T(8,128)(2,1)} %get-tuple-element.494), channel_id=1, source_target_pairs={{0,8},{8,0},{16,24},{24,16},{1,9},{9,1},{17,25},{25,17},{2,10},{10... | collective-permute-start | bytes 1572872 | tf_op jit(solution)/shard_map/ppermute | solution.py:349
  768.6 23.5 %collective-permute-start.56 = (bf16[256,1024]{1,0:T(8,128)(2,1)}, bf16[256,1024]{1,0:T(8,128)(2,1)S(1)}, u32[]{:S(2)}, u32[]{:S(2)}) collective-permute-start(bf16[256,1024]{1,0:T(8,128)(2,1)} %get-tuple-element.496), channel_id=1, source_target_pairs={{0,16},{16,0},{8,24},{24,8},{1,17},{17,1},{9,25},{25,9},{2,18},{18... | collective-permute-start | bytes 1572872 | tf_op jit(solution)/shard_map/ppermute | solution.py:353
  792.1 79.7 %collective-permute-start.66 = (bf16[256,2048]{1,0:T(8,128)(2,1)}, bf16[256,2048]{1,0:T(8,128)(2,1)}, u32[]{:S(2)}, u32[]{:S(2)}) collective-permute-start(bf16[256,2048]{1,0:T(8,128)(2,1)} %slice.353), channel_id=1, source_target_pairs={{0,16},{16,0},{8,24},{24,8},{1,17},{17,1},{9,25},{25,9},{2,18},{18... | collective-permute-start | bytes 3145736 | tf_op jit(solution)/shard_map/ppermute | solution.py:353
  794.5 77.3 %collective-permute-start.63 = (bf16[256,2048]{1,0:T(8,128)(2,1)}, bf16[256,2048]{1,0:T(8,128)(2,1)}, u32[]{:S(2)}, u32[]{:S(2)}) collective-permute-start(bf16[256,2048]{1,0:T(8,128)(2,1)} %slice.352), channel_id=1, source_target_pairs={{0,8},{8,0},{16,24},{24,16},{1,9},{9,1},{17,25},{25,17},{2,10},{10... | collective-permute-start | bytes 3145736 | tf_op jit(solution)/shard_map/ppermute | solution.py:349
  795.6 67.7 %collective-permute-start.60 = (bf16[256,2048]{1,0:T(8,128)(2,1)}, bf16[256,2048]{1,0:T(8,128)(2,1)}, u32[]{:S(2)}, u32[]{:S(2)}) collective-permute-start(bf16[256,2048]{1,0:T(8,128)(2,1)} %pad_maximum_fusion.7), channel_id=1, source_target_pairs={{0,8},{8,0},{16,24},{24,16},{1,9},{9,1},{17,25},{25,17},{2,10},{10... | collective-permute-start | bytes 3145736 | tf_op jit(solution)/shard_map/ppermute | solution.py:349
  796.5 64.3 %collective-permute-start.61 = (bf16[256,2048]{1,0:T(8,128)(2,1)}, bf16[256,2048]{1,0:T(8,128)(2,1)}, u32[]{:S(2)}, u32[]{:S(2)}) collective-permute-start(bf16[256,2048]{1,0:T(8,128)(2,1)} %pad_maximum_fusion.8), channel_id=1, source_target_pairs={{0,16},{16,0},{8,24},{24,8},{1,17},{17,1},{9,25},{25,9},{2,18},{18... | collective-permute-start | bytes 3145736 | tf_op jit(solution)/shard_map/ppermute | solution.py:353
  800.3 63.5 %collective-permute-start.62 = (bf16[256,2048]{1,0:T(8,128)(2,1)}, bf16[256,2048]{1,0:T(8,128)(2,1)}, u32[]{:S(2)}, u32[]{:S(2)}) collective-permute-start(bf16[256,2048]{1,0:T(8,128)(2,1)} %add_convert_fusion.5), channel_id=1, source_target_pairs={{0,3},{1,0},{2,1},{3,2},{4,7},{5,4},{6,5},{7,6},{8,11},{9,8},{10,9... | collective-permute-start | bytes 3145736 | tf_op jit(solution)/shard_map/ppermute | solution.py:363
  860.8 30.1 %collective-permute-start.64 = (bf16[256,2048]{1,0:T(8,128)(2,1)}, bf16[256,2048]{1,0:T(8,128)(2,1)S(1)}, u32[]{:S(2)}, u32[]{:S(2)}) collective-permute-start(bf16[256,2048]{1,0:T(8,128)(2,1)} %add_convert_fusion.8), channel_id=1, source_target_pairs={{0,16},{16,0},{8,24},{24,8},{1,17},{17,1},{9,25},{25,9},{2,18},{18... | collective-permute-start | bytes 3145736 | tf_op jit(solution)/shard_map/ppermute | solution.py:353
  863.3 27.7 %collective-permute-start.65 = (bf16[256,2048]{1,0:T(8,128)(2,1)}, bf16[256,2048]{1,0:T(8,128)(2,1)S(1)}, u32[]{:S(2)}, u32[]{:S(2)}) collective-permute-start(bf16[256,2048]{1,0:T(8,128)(2,1)} %add_convert_fusion.9), channel_id=1, source_target_pairs={{0,8},{8,0},{16,24},{24,16},{1,9},{9,1},{17,25},{25,17},{2,10},{10... | collective-permute-start | bytes 3145736 | tf_op jit(solution)/shard_map/ppermute | solution.py:349
  863.8 42.7 %collective-permute-start.67 = (bf16[512,2048]{1,0:T(8,128)(2,1)}, bf16[512,2048]{1,0:T(8,128)(2,1)}, u32[]{:S(2)}, u32[]{:S(2)}) collective-permute-start(bf16[512,2048]{1,0:T(8,128)(2,1)} %pad_maximum_fusion.1), channel_id=1, source_target_pairs={{0,4},{4,0},{1,5},{5,1},{2,6},{6,2},{3,7},{7,3},{8,12},{12,8},{9,1... | collective-permute-start | bytes 6291464 | tf_op jit(solution)/shard_map/ppermute | solution.py:345
  902.5 15.3 %collective-permute-start.69 = (f32[256,1024]{1,0:T(8,128)}, f32[256,1024]{1,0:T(8,128)S(1)}, u32[]{:S(2)}, u32[]{:S(2)}) collective-permute-start(f32[256,1024]{1,0:T(8,128)} %get-tuple-element.527), channel_id=1, source_target_pairs={{0,4},{4,0},{1,5},{5,1},{2,6},{6,2},{3,7},{7,3},{8,12},{12,8},{9,1... | collective-permute-start | bytes 3145736 | tf_op jit(solution)/shard_map/ppermute | solution.py:345
  902.5 16.8 %collective-permute-start.68 = (f32[256,1024]{1,0:T(8,128)}, f32[256,1024]{1,0:T(8,128)}, u32[]{:S(2)}, u32[]{:S(2)}) collective-permute-start(f32[256,1024]{1,0:T(8,128)} %get-tuple-element.526), channel_id=1, source_target_pairs={{0,4},{4,0},{1,5},{5,1},{2,6},{6,2},{3,7},{7,3},{8,12},{12,8},{9,1... | collective-permute-start | bytes 3145736 | tf_op jit(solution)/shard_map/ppermute | solution.py:345
  903.2 33.8 %collective-permute-start.71 = (bf16[256,2048]{1,0:T(8,128)(2,1)}, bf16[256,2048]{1,0:T(8,128)(2,1)}, u32[]{:S(2)}, u32[]{:S(2)}) collective-permute-start(bf16[256,2048]{1,0:T(8,128)(2,1)} %pad_maximum_fusion.9), channel_id=1, source_target_pairs={{0,8},{8,0},{16,24},{24,16},{1,9},{9,1},{17,25},{25,17},{2,10},{10... | collective-permute-start | bytes 3145736 | tf_op jit(solution)/shard_map/ppermute | solution.py:349
  904.8 36.7 %collective-permute-start.73 = (bf16[256,2048]{1,0:T(8,128)(2,1)}, bf16[256,2048]{1,0:T(8,128)(2,1)}, u32[]{:S(2)}, u32[]{:S(2)}) collective-permute-start(bf16[256,2048]{1,0:T(8,128)(2,1)} %pad_maximum_fusion.10), channel_id=1, source_target_pairs={{0,16},{16,0},{8,24},{24,8},{1,17},{17,1},{9,25},{25,9},{2,18},{18... | collective-permute-start | bytes 3145736 | tf_op jit(solution)/shard_map/ppermute | solution.py:353
  906.6 34.9 %collective-permute-start.74 = (bf16[256,2048]{1,0:T(8,128)(2,1)}, bf16[256,2048]{1,0:T(8,128)(2,1)}, u32[]{:S(2)}, u32[]{:S(2)}) collective-permute-start(bf16[256,2048]{1,0:T(8,128)(2,1)} %add_convert_fusion.3), channel_id=1, source_target_pairs={{0,3},{1,0},{2,1},{3,2},{4,7},{5,4},{6,5},{7,6},{8,11},{9,8},{10,9... | collective-permute-start | bytes 3145736 | tf_op jit(solution)/shard_map/ppermute | solution.py:363
  949.8 24.7 %collective-permute-start.82 = (bf16[256,2048]{1,0:T(8,128)(2,1)S(1)}, bf16[256,2048]{1,0:T(8,128)(2,1)S(1)}, u32[]{:S(2)}, u32[]{:S(2)}) collective-permute-start(bf16[256,2048]{1,0:T(8,128)(2,1)S(1)} %pad_maximum_fusion.11.refs_0_), channel_id=1, source_target_pairs={{0,16},{16,0},{8,24},{24,8},{1,17},{17,1},{9,25},{25,9},{2,18},{18... | collective-permute-start | bytes 3145736 | tf_op jit(solution)/shard_map/ppermute | solution.py:353
  951.3 24.4 %collective-permute-start.81 = (bf16[256,2048]{1,0:T(8,128)(2,1)S(1)}, bf16[256,2048]{1,0:T(8,128)(2,1)S(1)}, u32[]{:S(2)}, u32[]{:S(2)}) collective-permute-start(bf16[256,2048]{1,0:T(8,128)(2,1)S(1)} %pad_maximum_fusion.11.refs_0_), channel_id=1, source_target_pairs={{0,8},{8,0},{16,24},{24,16},{1,9},{9,1},{17,25},{25,17},{2,10},{10... | collective-permute-start | bytes 3145736 | tf_op jit(solution)/shard_map/ppermute | solution.py:349
  (148 other events, 2393.0 us)
Sparse Core Ops, SparseCore 0:
  39.4 208.9 all-gather.8
  580.4 101.1 reduce-scatter.4
  684.1 77.4 reduce-scatter.2
  763.3 85.6 all-gather.6
  850.6 72.3 all-gather.4

commit v8 on v7

--- a/solution.py
+++ b/solution.py
@@ -1514,6 +1514,7 @@
         return plane.both(
             jnp.concatenate([part_of(k, 1, 0), add_rounded(part_of(k, 1, 1), via_y)], axis=1),
             jnp.concatenate([add_rounded(part_of(k, 2, 0), via_x), part_of(k, 2, 1)], axis=1),
+            k == 0,
         )
 
     def group_total(k, came, total):
@@ -1546,20 +1547,22 @@
     head_weights(2)
     vias[2] = first_messages(2)
     came[3] = second_messages(3, vias[3])
+    order.tokens += [down_x_bottom, down_y_top]
     backward(1)
     head_weights(1)
     vias[1] = first_messages(1)
     came[2] = second_messages(2, vias[2])
     backward(0)
+    order.tokens += came[3]
     head_weights(0)
-    total = column.send(step_down, group_total(3, came[3], None))
     vias[0] = first_messages(0)
     came[1] = second_messages(1, vias[1])
+    total = column.send(step_down, group_total(3, came[3], None))
+    order.tokens += came[2]
+    back_rows = order.run(sum_rows, head_rows, own_parts, other_rows, 0)
+    came[0] = second_messages(0, vias[0])
+    arrived = order.swap(mirrored(other_tokens(back_rows)).astype(bf16))
     total = column.send(step_down, add_rounded(total, group_total(2, came[2], None)))
-    back_rows = order.run(sum_rows, head_rows, own_parts, other_rows, 0)
-    arrived = order.swap(mirrored(other_tokens(back_rows)).astype(bf16))
-    came[0] = second_messages(0, vias[0])
-    total = column.send(step_down, add_rounded(total, group_total(1, came[1], None)))
     layer_parts = layer_out_rows()
 
     input_mine, input_other, sums_one = order.run(
@@ -1577,6 +1580,7 @@
         vectors_all,
     )
     input_others = [order.swap(top(input_other)), order.swap(bottom(input_other))]
+    total = column.send(step_down, add_rounded(total, group_total(1, came[1], None)))
     layer_out = order.run(join_tokens, index, *layer_parts)
 
     row_hot = (jnp.arange(2) == row_i).astype(f32)

time: 1020 us -> 982 us (0.963)
  waiting for transfers between devices: 297 us -> 255 us
  starting transfers between devices: 122 us -> 138 us
    ppermute x29, waiting for transfers between devices: 153 us -> 90.5 us  [step_y(): return lax.ppermute(values, 'dp', [(0, 2), (2, 0), (1, 3), (3, 1)])]
    ppermute x3, starting transfers between devices: 12.4 us -> 31.6 us  [step_down(): lax.ppermute(values, 'col', [(i, (i - 1) % count) for i in range(count)])]
    unnamed x258 -> x238, local copies, waits for them, and re-layouts: 42.4 us -> 35 us
  transfers between devices with their start and end apart: 90 -> 90, of which waited for: 33 -> 28; matrix products, arithmetic and copies ran while one was open for 12% -> 12% of each run, Pallas kernels for 36% -> 38%
where the time goes in v8:
time: 982 us; the launch traced here: 973 us
  Pallas kernels  418 us (43%)
  waiting for transfers between devices  255 us (26%)
  starting transfers between devices  138 us (14%)
  local copies, waits for them, and re-layouts  89.3 us (9%)
  other arithmetic  57.7 us (6%)
  between operations  15.7 us (2%)
    pallas_call x4, Pallas kernels, ffn_rows_of(): pl.pallas_call(ffn_kernel, grid_spec=pltpu.PrefetchScalarGridSpec(num_sca...  102 us
    ppermute x29, waiting for transfers between devices, step_y(): return lax.ppermute(values, 'dp', [(0, 2), (2, 0), (1, 3), (3, 1)])  90.5 us
    ppermute x3, waiting for transfers between devices, step_up(): lax.ppermute(values, 'col', [(i, (i + 1) % count) for i in range(count)])  82.7 us
    pallas_call x2, Pallas kernels, weight_products(): pl.pallas_call(functools.partial(weight_products_kernel, count), grid=(ri...  58 us
    pallas_call x4, Pallas kernels, local_backward(): pl.pallas_call(functools.partial(local_backward_kernel, min(512, length))...  50.4 us
    ppermute x29, waiting for transfers between devices, step_x(): return lax.ppermute(values, 'dp', [(0, 1), (1, 0), (2, 3), (3, 2)])  47 us
    unnamed x238, local copies, waits for them, and re-layouts  35 us
    pallas_call x3, Pallas kernels, sum_rows(): pl.pallas_call(functools.partial(sum_rows_kernel, count), grid=(tokens //...  34.3 us
  transfers between devices with their start and end apart: 90, of which 28 were waited for; matrix products, arithmetic and copies ran while one was open for 12% of the time, Pallas kernels for 38%

profile of v8, /device:TPU:0, one launch (start us, length us, event | category | flops | bytes accessed | tf_op | source)
XLA Modules:
  0.0 972.7 jit_solution(16688023842227210170)
XLA Ops:
  7.3 3.2 constant_dynamic-slice_fusion.1
  34.6 3.2 shard_map.315
  43.0 36.7 %collective-permute-done.6.refs_0_ = bf16[512,1024]{1,0:T(8,128)(2,1)} collective-permute-done((bf16[512,1024]{1,0:T(8,128)(2,1)}, bf16[512,1024]{1,0:T(8,128)(2,1)}, u32[]{:S(2)}, u32[]{:S(2)}) %collective-permute-start.6) | collective-permute-done | bytes 1048608 | tf_op jit(solution)/shard_map/ppermute | solution.py:358
  84.4 3.6 shard_map.316
  91.6 6.2 collective-permute-start.15
  97.9 6.7 shard_map.317
  104.6 9.2 collective-permute-done.12.refs_2_
  116.3 6.1 shard_map.318.query_ref.key_ref.value_ref
  122.4 6.5 shard_map.319.refs_0_.refs_5_
  130.9 21.1 %collective-permute-done.15.refs_0_ = bf16[512,1024]{1,0:T(8,128)(2,1)S(1)} collective-permute-done((bf16[512,1024]{1,0:T(8,128)(2,1)}, bf16[512,1024]{1,0:T(8,128)(2,1)S(1)}, u32[]{:S(2)}, u32[]{:S(2)}) %collective-permute-start.15) | collective-permute-done | bytes 1048608 | tf_op jit(solution)/shard_map/ppermute | solution.py:358
  152.9 23.7 %collective-permute-start.20 = (bf16[512,1024]{1,0:T(8,128)(2,1)S(1)}, bf16[512,1024]{1,0:T(8,128)(2,1)S(1)}, u32[]{:S(2)}, u32[]{:S(2)}) collective-permute-start(bf16[512,1024]{1,0:T(8,128)(2,1)S(1)} %collective-permute-done.15.refs_0_), channel_id=1, source_target_pairs={{0,1},{1,2},{2,3},{3,0},{4,5},{5,6},{6,7},{7,4},{8,9},{9,10},{10,1... | collective-permute-start | bytes 3145736 | tf_op jit(solution)/shard_map/ppermute | solution.py:358
  176.7 3.8 shard_map.320
  183.8 5.6 shard_map.321.query_ref.key_ref.value_ref
  189.4 6.5 shard_map.322.refs_1_.refs_5_
  197.2 24.9 %collective-permute-done.20.refs_0_ = bf16[512,1024]{1,0:T(8,128)(2,1)S(1)} collective-permute-done((bf16[512,1024]{1,0:T(8,128)(2,1)S(1)}, bf16[512,1024]{1,0:T(8,128)(2,1)S(1)}, u32[]{:S(2)}, u32[]{:S(2)}) %collective-permute-start.20) | collective-permute-done | bytes 1048608 | tf_op jit(solution)/shard_map/ppermute | solution.py:358
  231.3 5.4 shard_map.324.query_ref.key_ref.value_ref
  236.8 6.5 shard_map.325.refs_2_.refs_5_
  250.5 8.8 collective-permute-done.24.refs_4_
  263.8 7.6 shard_map.327.refs_3_
  273.5 5.5 shard_map.328.query_ref.key_ref.value_ref
  279.0 6.7 shard_map.329.refs_0_.refs_5_
  285.7 6.5 collective-permute-done.28
  294.3 6.3 shard_map.330.rows_ref
  309.4 6.5 shard_map.331
  315.9 3.7 collective-permute-done.32
  331.4 25.4 %shard_map.332 = (bf16[512,4096]{1,0:T(8,128)(2,1)}, f32[4,1,512]{2,1,0:T(1,128)S(1)}, bf16[512,2048]{1,0:T(8,128)(2,1)S(1)}, bf16[512,2048]{1,0:T(8,128)(2,1)S(1)}) custom-call(s32[3]{0:T(128)S(1)} %pad_add_fusion.index_ref.refs_0_, bf16[512,2048]{1,0:T(8,128)(2,1)} %get-tuple-element.423.refs_0_.refs_1_, ...), custom_call_target="tpu_custom_call" | custom-call | flops 1717986944 | bytes 5033164 | tf_op jit(solution)/shard_map/pallas_call | solution.py:621
  356.8 10.4 %collective-permute-done.33.refs_0_.refs_1_.refs_2_ = bf16[512,2048]{1,0:T(8,128)(2,1)} collective-permute-done((bf16[512,2048]{1,0:T(8,128)(2,1)}, bf16[512,2048]{1,0:T(8,128)(2,1)}, u32[]{:S(2)}, u32[]{:S(2)}) %collective-permute-start.33) | collective-permute-done | bytes 2097184 | tf_op jit(solution)/shard_map/ppermute | solution.py:353
  378.1 25.7 %shard_map.333 = (bf16[512,4096]{1,0:T(8,128)(2,1)}, f32[4,1,512]{2,1,0:T(1,128)S(1)}, bf16[512,2048]{1,0:T(8,128)(2,1)S(1)}, bf16[512,2048]{1,0:T(8,128)(2,1)S(1)}) custom-call(s32[3]{0:T(128)S(1)} %pad_add_fusion.index_ref.refs_0_, bf16[512,2048]{1,0:T(8,128)(2,1)} %collective-permute-done.31.refs_0_.refs_1_, ...), custom_call_target="tpu_custom_call" | custom-call | flops 1717986944 | bytes 5033164 | tf_op jit(solution)/shard_map/pallas_call | solution.py:621
  405.7 25.3 %shard_map.334 = (bf16[512,4096]{1,0:T(8,128)(2,1)}, f32[4,1,512]{2,1,0:T(1,128)S(1)}, bf16[512,2048]{1,0:T(8,128)(2,1)S(1)}, bf16[512,2048]{1,0:T(8,128)(2,1)S(1)}) custom-call(s32[3]{0:T(128)S(1)} %pad_add_fusion.index_ref.refs_0_, bf16[512,2048]{1,0:T(8,128)(2,1)} %collective-permute-done.33.refs_0_.refs_1_.refs_2_, ...), custom_call_target="tpu_custom_call" | custom-call | flops 1717986944 | bytes 5033164 | tf_op jit(solution)/shard_map/pallas_call | solution.py:621
  435.2 25.4 %shard_map.335 = (bf16[512,4096]{1,0:T(8,128)(2,1)}, f32[4,1,512]{2,1,0:T(1,128)S(1)}, bf16[512,2048]{1,0:T(8,128)(2,1)S(1)}, bf16[512,2048]{1,0:T(8,128)(2,1)S(1)}) custom-call(s32[3]{0:T(128)S(1)} %pad_add_fusion.index_ref.refs_0_, bf16[512,2048]{1,0:T(8,128)(2,1)} %constant_dynamic-update-slice_fusion.refs_0_.refs_1_.refs_3_, ...), custom_call_target="tpu_custom_call" | custom-call | flops 1717986944 | bytes 5033164 | tf_op jit(solution)/shard_map/pallas_call | solution.py:621
  465.2 29.0 %shard_map.336 = bf16[4,1024,1024]{2,1,0:T(8,128)(2,1)} custom-call(bf16[512,2048]{1,0:T(8,128)(2,1)} %get-tuple-element.423.refs_0_.refs_1_, bf16[512,2048]{1,0:T(8,128)(2,1)} %collective-permute-done.31.refs_0_.refs_1_, bf16[512,2048]{1,0:T(8,128)(2,1)} %collective-permute-done.33.refs_0_.refs_1_.refs_2_, ...), custom_call_target="tpu_custom_call" | custom-call | flops 1717986944 | bytes 6710886 | tf_op jit(solution)/shard_map/pallas_call | solution.py:667
  494.2 3.7 add_convert_fusion.10
  497.8 29.1 %shard_map.337 = bf16[4,1024,1024]{2,1,0:T(8,128)(2,1)} custom-call(bf16[512,2048]{1,0:T(8,128)(2,1)} %get-tuple-element.423.refs_0_.refs_1_, bf16[512,2048]{1,0:T(8,128)(2,1)} %collective-permute-done.31.refs_0_.refs_1_, bf16[512,2048]{1,0:T(8,128)(2,1)} %collective-permute-done.33.refs_0_.refs_1_.refs_2_, ...), custom_call_target="tpu_custom_call" | custom-call | flops 1717986944 | bytes 6710886 | tf_op jit(solution)/shard_map/pallas_call | solution.py:667
  530.8 21.8 %collective-permute-done.40.refs_2_ = bf16[256,2048]{1,0:T(8,128)(2,1)S(1)} collective-permute-done((bf16[256,2048]{1,0:T(8,128)(2,1)S(1)}, bf16[256,2048]{1,0:T(8,128)(2,1)S(1)}, u32[]{:S(2)}, u32[]{:S(2)}) %collective-permute-start.40) | collective-permute-done | bytes 1048608 | tf_op jit(solution)/shard_map/ppermute | solution.py:353
  552.9 12.1 %shard_map.338 = (f32[512,2048]{1,0:T(8,128)}, bf16[512,2048]{1,0:T(8,128)(2,1)}, bf16[512,2048]{1,0:T(8,128)(2,1)}, f32[8,2048]{1,0:T(8,128)S(1)}) custom-call(s32[3]{0:T(128)S(1)} %pad_add_fusion.index_ref.refs_0_, bf16[512,2048]{1,0:T(8,128)(2,1)} %copy-done.35, bf16[256,2048]{1,0:T(8,128)(2,1)S(1)} %collective-permute-done.36.refs_1_, ...), custom_call_target="tpu_custom_call" | custom-call | bytes 2516582 | tf_op jit(solution)/shard_map/pallas_call | solution.py:1048
  567.4 10.1 %add_convert_fusion = (bf16[4,512,1024]{2,1,0:T(8,128)(2,1)}, bf16[4,512,1024]{2,1,0:T(8,128)(2,1)}) fusion(bf16[4,1024,1024]{2,1,0:T(8,128)(2,1)} %collective-permute-done.42, bf16[4,1024,1024]{2,1,0:T(8,128)(2,1)} %shard_map.336), kind=kLoop, calls=%fused_computation.2 | loop fusion | flops 16777216 | bytes 25165824 | tf_op jit(solution)/shard_map/convert_element_type | solution.py:418
  582.4 3.3 fusion.17
  589.9 8.0 shard_map.340.grad_ref
  597.9 12.4 %shard_map.341.refs_4_.refs_3_ = bf16[1024,768]{1,0:T(8,128)(2,1)S(1)} custom-call(s32[1,1024]{1,0:T(1,128)S(1)} %bitcast.54, bf16[1024,768]{1,0:T(8,128)(2,1)S(1)} %shard_map.328.query_ref.key_ref.value_ref, bf16[1024,1024]{1,0:T(8,128)(2,1)S(1)} %shard_map.340.grad_ref, bf16[1024,768]{1,0:T(8,128)(2,1)S(1)} %shard_map.328.query_ref.key_ref.value_ref, ...), custom_call_target="tpu_custom_call" | custom-call | flops 858993472 | bytes 629145 | tf_op jit(solution)/shard_map/pallas_call | solution.py:544
  610.3 9.1 shard_map.342
  629.8 12.5 %shard_map.343.refs_4_.refs_2_ = bf16[1024,768]{1,0:T(8,128)(2,1)S(1)} custom-call(s32[1,1024]{1,0:T(1,128)S(1)} %bitcast.55, bf16[1024,768]{1,0:T(8,128)(2,1)S(1)} %copy-done.5, bf16[1024,1024]{1,0:T(8,128)(2,1)S(1)} %shard_map.340.grad_ref, bf16[1024,768]{1,0:T(8,128)(2,1)S(1)} %copy-done.5, bf16[1024,768]{1,0:T(8,128)(2,1)S(1)} %copy-done.5), custom_call_target="tpu_custom_call" | custom-call | flops 858993472 | bytes 629145 | tf_op jit(solution)/shard_map/pallas_call | solution.py:544
  642.4 8.3 shard_map.344
  660.0 21.7 %reduce-scatter.5.cloned.1.call-done = bf16[1,512,1024]{2,1,0:T(8,128)(2,1)} async-done(((bf16[4,512,1024]{2,1,0:T(8,128)(2,1)}), bf16[1,512,1024]{2,1,0:T(8,128)(2,1)}) %reduce-scatter.5.cloned.1.call-update) | async-done | bytes 1048592 | tf_op jit(solution)/shard_map/reduce_scatter | solution.py:1489
  687.2 12.6 %shard_map.345.refs_4_.refs_1_ = bf16[1024,768]{1,0:T(8,128)(2,1)S(1)} custom-call(s32[1,1024]{1,0:T(1,128)S(1)} %bitcast.56, bf16[1024,768]{1,0:T(8,128)(2,1)S(1)} %copy-done.3, bf16[1024,1024]{1,0:T(8,128)(2,1)S(1)} %copy-done.7, bf16[1024,768]{1,0:T(8,128)(2,1)S(1)} %copy-done.3, bf16[1024,768]{1,0:T(8,128)(2,1)S(1)} %copy-done.3), custom_call_target="tpu_custom_call" | custom-call | flops 858993472 | bytes 629145 | tf_op jit(solution)/shard_map/pallas_call | solution.py:544
  699.9 8.3 shard_map.346
  716.5 7.5 collective-permute-done.54
  725.8 12.8 %shard_map.347.refs_4_.refs_0_ = bf16[1024,768]{1,0:T(8,128)(2,1)S(1)} custom-call(s32[1,1024]{1,0:T(1,128)S(1)} %bitcast.57, bf16[1024,768]{1,0:T(8,128)(2,1)S(1)} %copy-done.1, bf16[1024,1024]{1,0:T(8,128)(2,1)S(1)} %copy-done.7, bf16[1024,768]{1,0:T(8,128)(2,1)S(1)} %copy-done.1, bf16[1024,768]{1,0:T(8,128)(2,1)S(1)} %copy-done.1), custom_call_target="tpu_custom_call" | custom-call | flops 858993472 | bytes 629145 | tf_op jit(solution)/shard_map/pallas_call | solution.py:544
  738.7 8.3 shard_map.348
  753.8 8.2 collective-permute-done.58
  766.2 26.3 %collective-permute-start.61 = (bf16[256,2048]{1,0:T(8,128)(2,1)}, bf16[256,2048]{1,0:T(8,128)(2,1)}, u32[]{:S(2)}, u32[]{:S(2)}) collective-permute-start(bf16[256,2048]{1,0:T(8,128)(2,1)} %add_convert_fusion.7), channel_id=1, source_target_pairs={{0,3},{1,0},{2,1},{3,2},{4,7},{5,4},{6,5},{7,6},{8,11},{9,8},{10,9... | collective-permute-start | bytes 3145736 | tf_op jit(solution)/shard_map/ppermute | solution.py:363
  792.5 20.5 %shard_map.349.refs_0_ = f32[1024,2048]{1,0:T(8,128)} custom-call(bf16[1024,768]{1,0:T(8,128)(2,1)S(1)} %shard_map.347.refs_4_.refs_0_, bf16[1024,768]{1,0:T(8,128)(2,1)S(1)} %shard_map.345.refs_4_.refs_1_, bf16[1024,768]{1,0:T(8,128)(2,1)S(1)} %shard_map.343.refs_4_.refs_2_, bf16[1024,768]{1,0:T(8,128)(2,1)} %copy-done.26, ...), custom_call_target="tpu_custom_call" | custom-call | flops 1288490240 | bytes 838860 | tf_op jit(solution)/shard_map/pallas_call | solution.py:862
  826.2 3.7 add_convert_fusion.5
  830.0 8.8 shard_map.350
  842.5 7.7 shard_map.351
  855.3 4.0 add_convert_fusion.3
  859.3 5.3 collective-permute-start.74
  864.7 4.4 shard_map.352
  869.2 22.1 %collective-permute-done.71 = bf16[256,2048]{1,0:T(8,128)(2,1)} collective-permute-done((bf16[256,2048]{1,0:T(8,128)(2,1)}, bf16[256,2048]{1,0:T(8,128)(2,1)}, u32[]{:S(2)}, u32[]{:S(2)}) %collective-permute-start.71) | collective-permute-done | bytes 1048608 | tf_op jit(solution)/shard_map/ppermute | solution.py:349
  891.5 6.2 collective-permute-done.72
  902.8 5.3 collective-permute-done.76
  917.7 17.0 %collective-permute-done.82.refs_2_ = bf16[256,2048]{1,0:T(8,128)(2,1)S(1)} collective-permute-done((bf16[256,2048]{1,0:T(8,128)(2,1)S(1)}, bf16[256,2048]{1,0:T(8,128)(2,1)S(1)}, u32[]{:S(2)}, u32[]{:S(2)}) %collective-permute-start.82) | collective-permute-done | bytes 1048608 | tf_op jit(solution)/shard_map/ppermute | solution.py:353
  938.6 8.0 shard_map.354
  956.0 4.5 collective-permute-done.83.refs_3_
  960.5 5.5 shard_map.355
  (541 shorter events, 226.5 us)
Async XLA Ops:
  7.2 299.6 %all-gather.9.cloned.1.call-start = ((), (), s32[]{:S(2)}) async-start(), calls=%async_computation.6 | async-start | bytes 18874368 | tf_op jit(solution)/shard_map/all_gather | solution.py:1358
  10.5 18.7 %collective-permute-start.4 = (bf16[512,1024]{1,0:T(8,128)(2,1)}, bf16[512,1024]{1,0:T(8,128)(2,1)}, u32[]{:S(2)}, u32[]{:S(2)}) collective-permute-start(bf16[512,1024]{1,0:T(8,128)(2,1)} %get-tuple-element.616), channel_id=1, source_target_pairs={{0,4},{4,0},{1,5},{5,1},{2,6},{6,2},{3,7},{7,3},{8,12},{12,8},{9,1... | collective-permute-start | bytes 3145736 | tf_op jit(solution)/shard_map/ppermute | solution.py:345
  11.9 17.3 %collective-permute-start.1 = (f32[1280]{0:T(1024)S(1)}, f32[1280]{0:T(1024)S(1)}, u32[]{:S(2)}, u32[]{:S(2)}) collective-permute-start(f32[1280]{0:T(1024)S(1)} %pad_maximum_fusion.18), channel_id=1, source_target_pairs={{0,1},{1,2},{2,3},{3,0},{4,5},{5,6},{6,7},{7,4},{8,9},{9,10},{10,1... | collective-permute-start | bytes 15368 | tf_op jit(solution)/shard_map/ppermute | solution.py:1342
  17.1 17.5 %collective-permute-start.5 = (bf16[1024,1024]{1,0:T(8,128)(2,1)S(1)}, bf16[1024,1024]{1,0:T(8,128)(2,1)}, u32[]{:S(2)}, u32[]{:S(2)}) collective-permute-start(bf16[1024,1024]{1,0:T(8,128)(2,1)S(1)} %copy-done.8), channel_id=1, source_target_pairs={{0,4},{4,0},{1,5},{5,1},{2,6},{6,2},{3,7},{7,3},{8,12},{12,8},{9,1... | collective-permute-start | bytes 6291464 | tf_op jit(solution)/shard_map/ppermute | solution.py:345
  39.2 642.5 %reduce-scatter.5.cloned.1.call-start = ((), (), s32[]{:S(2)}) async-start(), calls=%async_computation.4 | async-start | bytes 5242880 | tf_op jit(solution)/shard_map/reduce_scatter | solution.py:1489
  39.3 40.4 %collective-permute-start.6 = (bf16[512,1024]{1,0:T(8,128)(2,1)}, bf16[512,1024]{1,0:T(8,128)(2,1)}, u32[]{:S(2)}, u32[]{:S(2)}) collective-permute-start(bf16[512,1024]{1,0:T(8,128)(2,1)} %pad_maximum_fusion.2), channel_id=1, source_target_pairs={{0,1},{1,2},{2,3},{3,0},{4,5},{5,6},{6,7},{7,4},{8,9},{9,10},{10,1... | collective-permute-start | bytes 3145736 | tf_op jit(solution)/shard_map/ppermute | solution.py:358
  40.0 39.7 %collective-permute-start.7 = (bf16[256,2048]{1,0:T(8,128)(2,1)}, bf16[256,2048]{1,0:T(8,128)(2,1)S(1)}, u32[]{:S(2)}, u32[]{:S(2)}) collective-permute-start(bf16[256,2048]{1,0:T(8,128)(2,1)} %get-tuple-element.301), channel_id=1, source_target_pairs={{0,8},{8,0},{16,24},{24,16},{1,9},{9,1},{17,25},{25,17},{2,10},{10... | collective-permute-start | bytes 3145736 | tf_op jit(solution)/shard_map/ppermute | solution.py:349
  41.5 39.3 %collective-permute-start.8 = (bf16[256,2048]{1,0:T(8,128)(2,1)}, bf16[256,2048]{1,0:T(8,128)(2,1)}, u32[]{:S(2)}, u32[]{:S(2)}) collective-permute-start(bf16[256,2048]{1,0:T(8,128)(2,1)} %get-tuple-element.301), channel_id=1, source_target_pairs={{0,16},{16,0},{8,24},{24,8},{1,17},{17,1},{9,25},{25,9},{2,18},{18... | collective-permute-start | bytes 3145736 | tf_op jit(solution)/shard_map/ppermute | solution.py:353
  88.0 28.3 %collective-permute-start.10 = (bf16[1024,1024]{1,0:T(8,128)(2,1)}, bf16[1024,1024]{1,0:T(8,128)(2,1)}, u32[]{:S(2)}, u32[]{:S(2)}) collective-permute-start(bf16[1024,1024]{1,0:T(8,128)(2,1)} %get-tuple-element.312), channel_id=1, source_target_pairs={{0,4},{4,0},{1,5},{5,1},{2,6},{6,2},{3,7},{7,3},{8,12},{12,8},{9,1... | collective-permute-start | bytes 6291464 | tf_op jit(solution)/shard_map/ppermute | solution.py:345
  88.0 25.8 %collective-permute-start.12 = (bf16[512,1024]{1,0:T(8,128)(2,1)}, bf16[512,1024]{1,0:T(8,128)(2,1)S(1)}, u32[]{:S(2)}, u32[]{:S(2)}) collective-permute-start(bf16[512,1024]{1,0:T(8,128)(2,1)} %collective-permute-done.6.refs_0_), channel_id=1, source_target_pairs={{0,16},{16,0},{8,24},{24,8},{1,17},{17,1},{9,25},{25,9},{2,18},{18... | collective-permute-start | bytes 3145736 | tf_op jit(solution)/shard_map/ppermute | solution.py:353
  89.6 25.6 %collective-permute-start.11 = (bf16[512,1024]{1,0:T(8,128)(2,1)}, bf16[512,1024]{1,0:T(8,128)(2,1)}, u32[]{:S(2)}, u32[]{:S(2)}) collective-permute-start(bf16[512,1024]{1,0:T(8,128)(2,1)} %collective-permute-done.6.refs_0_), channel_id=1, source_target_pairs={{0,8},{8,0},{16,24},{24,16},{1,9},{9,1},{17,25},{25,17},{2,10},{10... | collective-permute-start | bytes 3145736 | tf_op jit(solution)/shard_map/ppermute | solution.py:349
  91.6 60.4 %collective-permute-start.15 = (bf16[512,1024]{1,0:T(8,128)(2,1)}, bf16[512,1024]{1,0:T(8,128)(2,1)S(1)}, u32[]{:S(2)}, u32[]{:S(2)}) collective-permute-start(bf16[512,1024]{1,0:T(8,128)(2,1)} %collective-permute-done.6.refs_0_), channel_id=1, source_target_pairs={{0,1},{1,2},{2,3},{3,0},{4,5},{5,6},{6,7},{7,4},{8,9},{9,10},{10,1... | collective-permute-start | bytes 3145736 | tf_op jit(solution)/shard_map/ppermute | solution.py:358
  129.0 23.0 %collective-permute-start.13 = (bf16[256,1024]{1,0:T(8,128)(2,1)S(1)}, bf16[256,1024]{1,0:T(8,128)(2,1)S(1)}, u32[]{:S(2)}, u32[]{:S(2)}) collective-permute-start(bf16[256,1024]{1,0:T(8,128)(2,1)S(1)} %slice.429), channel_id=1, source_target_pairs={{0,16},{16,0},{8,24},{24,8},{1,17},{17,1},{9,25},{25,9},{2,18},{18... | collective-permute-start | bytes 1572872 | tf_op jit(solution)/shard_map/ppermute | solution.py:353
  129.4 22.6 %collective-permute-start.14 = (bf16[256,1024]{1,0:T(8,128)(2,1)S(1)}, bf16[256,1024]{1,0:T(8,128)(2,1)S(1)}, u32[]{:S(2)}, u32[]{:S(2)}) collective-permute-start(bf16[256,1024]{1,0:T(8,128)(2,1)S(1)} %slice.430), channel_id=1, source_target_pairs={{0,8},{8,0},{16,24},{24,16},{1,9},{9,1},{17,25},{25,17},{2,10},{10... | collective-permute-start | bytes 1572872 | tf_op jit(solution)/shard_map/ppermute | solution.py:349
  152.0 43.9 %collective-permute-start.17 = (bf16[512,1024]{1,0:T(8,128)(2,1)S(1)}, bf16[512,1024]{1,0:T(8,128)(2,1)S(1)}, u32[]{:S(2)}, u32[]{:S(2)}) collective-permute-start(bf16[512,1024]{1,0:T(8,128)(2,1)S(1)} %collective-permute-done.15.refs_0_), channel_id=1, source_target_pairs={{0,16},{16,0},{8,24},{24,8},{1,17},{17,1},{9,25},{25,9},{2,18},{18... | collective-permute-start | bytes 3145736 | tf_op jit(solution)/shard_map/ppermute | solution.py:353
  152.4 43.6 %collective-permute-start.16 = (bf16[512,1024]{1,0:T(8,128)(2,1)S(1)}, bf16[512,1024]{1,0:T(8,128)(2,1)S(1)}, u32[]{:S(2)}, u32[]{:S(2)}) collective-permute-start(bf16[512,1024]{1,0:T(8,128)(2,1)S(1)} %collective-permute-done.15.refs_0_), channel_id=1, source_target_pairs={{0,8},{8,0},{16,24},{24,16},{1,9},{9,1},{17,25},{25,17},{2,10},{10... | collective-permute-start | bytes 3145736 | tf_op jit(solution)/shard_map/ppermute | solution.py:349
  152.9 69.2 %collective-permute-start.20 = (bf16[512,1024]{1,0:T(8,128)(2,1)S(1)}, bf16[512,1024]{1,0:T(8,128)(2,1)S(1)}, u32[]{:S(2)}, u32[]{:S(2)}) collective-permute-start(bf16[512,1024]{1,0:T(8,128)(2,1)S(1)} %collective-permute-done.15.refs_0_), channel_id=1, source_target_pairs={{0,1},{1,2},{2,3},{3,0},{4,5},{5,6},{6,7},{7,4},{8,9},{9,10},{10,1... | collective-permute-start | bytes 3145736 | tf_op jit(solution)/shard_map/ppermute | solution.py:358
  196.1 26.0 %collective-permute-start.18 = (bf16[256,1024]{1,0:T(8,128)(2,1)S(1)}, bf16[256,1024]{1,0:T(8,128)(2,1)S(1)}, u32[]{:S(2)}, u32[]{:S(2)}) collective-permute-start(bf16[256,1024]{1,0:T(8,128)(2,1)S(1)} %slice.432), channel_id=1, source_target_pairs={{0,16},{16,0},{8,24},{24,8},{1,17},{17,1},{9,25},{25,9},{2,18},{18... | collective-permute-start | bytes 1572872 | tf_op jit(solution)/shard_map/ppermute | solution.py:353
  196.7 25.4 %collective-permute-start.19 = (bf16[256,1024]{1,0:T(8,128)(2,1)S(1)}, bf16[256,1024]{1,0:T(8,128)(2,1)S(1)}, u32[]{:S(2)}, u32[]{:S(2)}) collective-permute-start(bf16[256,1024]{1,0:T(8,128)(2,1)S(1)} %slice.433), channel_id=1, source_target_pairs={{0,8},{8,0},{16,24},{24,16},{1,9},{9,1},{17,25},{25,17},{2,10},{10... | collective-permute-start | bytes 1572872 | tf_op jit(solution)/shard_map/ppermute | solution.py:349
  222.1 23.8 %collective-permute-start.22 = (bf16[512,1024]{1,0:T(8,128)(2,1)S(1)}, bf16[512,1024]{1,0:T(8,128)(2,1)S(1)}, u32[]{:S(2)}, u32[]{:S(2)}) collective-permute-start(bf16[512,1024]{1,0:T(8,128)(2,1)S(1)} %collective-permute-done.20.refs_0_), channel_id=1, source_target_pairs={{0,16},{16,0},{8,24},{24,8},{1,17},{17,1},{9,25},{25,9},{2,18},{18... | collective-permute-start | bytes 3145736 | tf_op jit(solution)/shard_map/ppermute | solution.py:353
  223.8 23.4 %collective-permute-start.21 = (bf16[512,1024]{1,0:T(8,128)(2,1)S(1)}, bf16[512,1024]{1,0:T(8,128)(2,1)S(1)}, u32[]{:S(2)}, u32[]{:S(2)}) collective-permute-start(bf16[512,1024]{1,0:T(8,128)(2,1)S(1)} %collective-permute-done.20.refs_0_), channel_id=1, source_target_pairs={{0,8},{8,0},{16,24},{24,16},{1,9},{9,1},{17,25},{25,17},{2,10},{10... | collective-permute-start | bytes 3145736 | tf_op jit(solution)/shard_map/ppermute | solution.py:349
  271.4 20.8 %collective-permute-start.28 = (bf16[256,2048]{1,0:T(8,128)(2,1)S(1)}, bf16[256,2048]{1,0:T(8,128)(2,1)S(1)}, u32[]{:S(2)}, u32[]{:S(2)}) collective-permute-start(bf16[256,2048]{1,0:T(8,128)(2,1)S(1)} %copy-done.78), channel_id=1, source_target_pairs={{0,8},{8,0},{16,24},{24,16},{1,9},{9,1},{17,25},{25,17},{2,10},{10... | collective-permute-start | bytes 3145736 | tf_op jit(solution)/shard_map/ppermute | solution.py:349
  272.4 21.1 %collective-permute-start.27 = (bf16[256,2048]{1,0:T(8,128)(2,1)S(1)}, bf16[256,2048]{1,0:T(8,128)(2,1)S(1)}, u32[]{:S(2)}, u32[]{:S(2)}) collective-permute-start(bf16[256,2048]{1,0:T(8,128)(2,1)S(1)} %copy-done.78), channel_id=1, source_target_pairs={{0,16},{16,0},{8,24},{24,8},{1,17},{17,1},{9,25},{25,9},{2,18},{18... | collective-permute-start | bytes 3145736 | tf_op jit(solution)/shard_map/ppermute | solution.py:353
  320.0 47.3 %collective-permute-start.33 = (bf16[512,2048]{1,0:T(8,128)(2,1)}, bf16[512,2048]{1,0:T(8,128)(2,1)}, u32[]{:S(2)}, u32[]{:S(2)}) collective-permute-start(bf16[512,2048]{1,0:T(8,128)(2,1)} %get-tuple-element.423.refs_0_.refs_1_), channel_id=1, source_target_pairs={{0,16},{16,0},{8,24},{24,8},{1,17},{17,1},{9,25},{25,9},{2,18},{18... | collective-permute-start | bytes 6291464 | tf_op jit(solution)/shard_map/ppermute | solution.py:353
  321.3 47.3 %collective-permute-start.31 = (bf16[512,2048]{1,0:T(8,128)(2,1)}, bf16[512,2048]{1,0:T(8,128)(2,1)}, u32[]{:S(2)}, u32[]{:S(2)}) collective-permute-start(bf16[512,2048]{1,0:T(8,128)(2,1)} %get-tuple-element.423.refs_0_.refs_1_), channel_id=1, source_target_pairs={{0,8},{8,0},{16,24},{24,16},{1,9},{9,1},{17,25},{25,17},{2,10},{10... | collective-permute-start | bytes 6291464 | tf_op jit(solution)/shard_map/ppermute | solution.py:349
  370.0 35.0 %collective-permute-start.35 = (bf16[256,2048]{1,0:T(8,128)(2,1)S(1)}, bf16[256,2048]{1,0:T(8,128)(2,1)S(1)}, u32[]{:S(2)}, u32[]{:S(2)}) collective-permute-start(bf16[256,2048]{1,0:T(8,128)(2,1)S(1)} %slice.449), channel_id=1, source_target_pairs={{0,8},{8,0},{16,24},{24,16},{1,9},{9,1},{17,25},{25,17},{2,10},{10... | collective-permute-start | bytes 3145736 | tf_op jit(solution)/shard_map/ppermute | solution.py:349
  371.2 61.0 %collective-permute-start.34 = (bf16[256,2048]{1,0:T(8,128)(2,1)S(1)}, bf16[256,2048]{1,0:T(8,128)(2,1)S(1)}, u32[]{:S(2)}, u32[]{:S(2)}) collective-permute-start(bf16[256,2048]{1,0:T(8,128)(2,1)S(1)} %slice.445), channel_id=1, source_target_pairs={{0,16},{16,0},{8,24},{24,8},{1,17},{17,1},{9,25},{25,9},{2,18},{18... | collective-permute-start | bytes 3145736 | tf_op jit(solution)/shard_map/ppermute | solution.py:353
  404.9 57.6 %collective-permute-start.36 = (bf16[256,2048]{1,0:T(8,128)(2,1)}, bf16[256,2048]{1,0:T(8,128)(2,1)S(1)}, u32[]{:S(2)}, u32[]{:S(2)}) collective-permute-start(bf16[256,2048]{1,0:T(8,128)(2,1)} %slice.346), channel_id=1, source_target_pairs={{0,8},{8,0},{16,24},{24,16},{1,9},{9,1},{17,25},{25,17},{2,10},{10... | collective-permute-start | bytes 3145736 | tf_op jit(solution)/shard_map/ppermute | solution.py:349
  432.2 30.4 %collective-permute-start.37 = (bf16[256,2048]{1,0:T(8,128)(2,1)}, bf16[256,2048]{1,0:T(8,128)(2,1)}, u32[]{:S(2)}, u32[]{:S(2)}) collective-permute-start(bf16[256,2048]{1,0:T(8,128)(2,1)} %slice.347), channel_id=1, source_target_pairs={{0,16},{16,0},{8,24},{24,8},{1,17},{17,1},{9,25},{25,9},{2,18},{18... | collective-permute-start | bytes 3145736 | tf_op jit(solution)/shard_map/ppermute | solution.py:353
  462.6 31.6 %collective-permute-start.39 = (bf16[256,2048]{1,0:T(8,128)(2,1)}, bf16[256,2048]{1,0:T(8,128)(2,1)}, u32[]{:S(2)}, u32[]{:S(2)}) collective-permute-start(bf16[256,2048]{1,0:T(8,128)(2,1)} %get-tuple-element.412), channel_id=1, source_target_pairs={{0,16},{16,0},{8,24},{24,8},{1,17},{17,1},{9,25},{25,9},{2,18},{18... | collective-permute-start | bytes 3145736 | tf_op jit(solution)/shard_map/ppermute | solution.py:353
  463.9 30.2 %collective-permute-start.38 = (bf16[256,2048]{1,0:T(8,128)(2,1)}, bf16[256,2048]{1,0:T(8,128)(2,1)}, u32[]{:S(2)}, u32[]{:S(2)}) collective-permute-start(bf16[256,2048]{1,0:T(8,128)(2,1)} %get-tuple-element.410), channel_id=1, source_target_pairs={{0,8},{8,0},{16,24},{24,16},{1,9},{9,1},{17,25},{25,17},{2,10},{10... | collective-permute-start | bytes 3145736 | tf_op jit(solution)/shard_map/ppermute | solution.py:349
  526.9 40.5 %collective-permute-start.42 = (bf16[4,1024,1024]{2,1,0:T(8,128)(2,1)}, bf16[4,1024,1024]{2,1,0:T(8,128)(2,1)}, u32[]{:S(2)}, u32[]{:S(2)}) collective-permute-start(bf16[4,1024,1024]{2,1,0:T(8,128)(2,1)} %shard_map.337), channel_id=1, source_target_pairs={{0,4},{4,0},{1,5},{5,1},{2,6},{6,2},{3,7},{7,3},{8,12},{12,8},{9,1... | collective-permute-start | bytes 25165832 | tf_op jit(solution)/shard_map/ppermute | solution.py:345
  527.0 25.6 %collective-permute-start.40 = (bf16[256,2048]{1,0:T(8,128)(2,1)S(1)}, bf16[256,2048]{1,0:T(8,128)(2,1)S(1)}, u32[]{:S(2)}, u32[]{:S(2)}) collective-permute-start(bf16[256,2048]{1,0:T(8,128)(2,1)S(1)} %copy-done.82), channel_id=1, source_target_pairs={{0,16},{16,0},{8,24},{24,8},{1,17},{17,1},{9,25},{25,9},{2,18},{18... | collective-permute-start | bytes 3145736 | tf_op jit(solution)/shard_map/ppermute | solution.py:353
  527.7 25.2 %collective-permute-start.41 = (bf16[256,2048]{1,0:T(8,128)(2,1)S(1)}, bf16[256,2048]{1,0:T(8,128)(2,1)S(1)}, u32[]{:S(2)}, u32[]{:S(2)}) collective-permute-start(bf16[256,2048]{1,0:T(8,128)(2,1)S(1)} %copy-done.81), channel_id=1, source_target_pairs={{0,8},{8,0},{16,24},{24,16},{1,9},{9,1},{17,25},{25,17},{2,10},{10... | collective-permute-start | bytes 3145736 | tf_op jit(solution)/shard_map/ppermute | solution.py:349
  580.6 242.1 %reduce-scatter.3.cloned.1.call-start = ((), (), s32[]{:S(2)}) async-start(), calls=%async_computation.2 | async-start | bytes 5242880 | tf_op jit(solution)/shard_map/reduce_scatter | solution.py:1489
  581.4 355.1 %all-gather.7.cloned.1.call-start = ((), (), s32[]{:S(2)}) async-start(), calls=%async_computation.5 | async-start | bytes 5242880 | tf_op jit(solution)/shard_map/all_gather | solution.py:1490
  585.7 36.6 %collective-permute-start.45 = (bf16[256,2048]{1,0:T(8,128)(2,1)}, bf16[256,2048]{1,0:T(8,128)(2,1)S(1)}, u32[]{:S(2)}, u32[]{:S(2)}) collective-permute-start(bf16[256,2048]{1,0:T(8,128)(2,1)} %get-tuple-element.446), channel_id=1, source_target_pairs={{0,8},{8,0},{16,24},{24,16},{1,9},{9,1},{17,25},{25,17},{2,10},{10... | collective-permute-start | bytes 3145736 | tf_op jit(solution)/shard_map/ppermute | solution.py:349
  586.6 35.7 %collective-permute-start.46 = (bf16[256,2048]{1,0:T(8,128)(2,1)}, bf16[256,2048]{1,0:T(8,128)(2,1)S(1)}, u32[]{:S(2)}, u32[]{:S(2)}) collective-permute-start(bf16[256,2048]{1,0:T(8,128)(2,1)} %get-tuple-element.447), channel_id=1, source_target_pairs={{0,16},{16,0},{8,24},{24,8},{1,17},{17,1},{9,25},{25,9},{2,18},{18... | collective-permute-start | bytes 3145736 | tf_op jit(solution)/shard_map/ppermute | solution.py:353
  588.5 241.4 %collective-permute-start.63 = (bf16[256,2048]{1,0:T(8,128)(2,1)}, bf16[256,2048]{1,0:T(8,128)(2,1)}, u32[]{:S(2)}, u32[]{:S(2)}) collective-permute-start(bf16[256,2048]{1,0:T(8,128)(2,1)} %slice.353), channel_id=1, source_target_pairs={{0,16},{16,0},{8,24},{24,8},{1,17},{17,1},{9,25},{25,9},{2,18},{18... | collective-permute-start | bytes 3145736 | tf_op jit(solution)/shard_map/ppermute | solution.py:353
  625.8 29.0 %collective-permute-start.48 = (bf16[256,1024]{1,0:T(8,128)(2,1)S(1)}, bf16[256,1024]{1,0:T(8,128)(2,1)S(1)}, u32[]{:S(2)}, u32[]{:S(2)}) collective-permute-start(bf16[256,1024]{1,0:T(8,128)(2,1)S(1)} %get-tuple-element.460), channel_id=1, source_target_pairs={{0,16},{16,0},{8,24},{24,8},{1,17},{17,1},{9,25},{25,9},{2,18},{18... | collective-permute-start | bytes 1572872 | tf_op jit(solution)/shard_map/ppermute | solution.py:353
  627.3 29.0 %collective-permute-start.47 = (bf16[256,1024]{1,0:T(8,128)(2,1)S(1)}, bf16[256,1024]{1,0:T(8,128)(2,1)S(1)}, u32[]{:S(2)}, u32[]{:S(2)}) collective-permute-start(bf16[256,1024]{1,0:T(8,128)(2,1)S(1)} %get-tuple-element.458), channel_id=1, source_target_pairs={{0,8},{8,0},{16,24},{24,16},{1,9},{9,1},{17,25},{25,17},{2,10},{10... | collective-permute-start | bytes 1572872 | tf_op jit(solution)/shard_map/ppermute | solution.py:349
  628.7 58.5 %collective-permute-start.52 = (bf16[256,2048]{1,0:T(8,128)(2,1)}, bf16[256,2048]{1,0:T(8,128)(2,1)}, u32[]{:S(2)}, u32[]{:S(2)}) collective-permute-start(bf16[256,2048]{1,0:T(8,128)(2,1)} %add_convert_fusion.8), channel_id=1, source_target_pairs={{0,16},{16,0},{8,24},{24,8},{1,17},{17,1},{9,25},{25,9},{2,18},{18... | collective-permute-start | bytes 3145736 | tf_op jit(solution)/shard_map/ppermute | solution.py:353
  629.3 58.0 %collective-permute-start.51 = (bf16[256,2048]{1,0:T(8,128)(2,1)}, bf16[256,2048]{1,0:T(8,128)(2,1)}, u32[]{:S(2)}, u32[]{:S(2)}) collective-permute-start(bf16[256,2048]{1,0:T(8,128)(2,1)} %add_convert_fusion.9), channel_id=1, source_target_pairs={{0,8},{8,0},{16,24},{24,16},{1,9},{9,1},{17,25},{25,17},{2,10},{10... | collective-permute-start | bytes 3145736 | tf_op jit(solution)/shard_map/ppermute | solution.py:349
  654.8 29.4 %collective-permute-start.49 = (bf16[256,1024]{1,0:T(8,128)(2,1)}, bf16[256,1024]{1,0:T(8,128)(2,1)}, u32[]{:S(2)}, u32[]{:S(2)}) collective-permute-start(bf16[256,1024]{1,0:T(8,128)(2,1)} %get-tuple-element.464), channel_id=1, source_target_pairs={{0,8},{8,0},{16,24},{24,16},{1,9},{9,1},{17,25},{25,17},{2,10},{10... | collective-permute-start | bytes 1572872 | tf_op jit(solution)/shard_map/ppermute | solution.py:349
  656.3 27.9 %collective-permute-start.50 = (bf16[256,1024]{1,0:T(8,128)(2,1)}, bf16[256,1024]{1,0:T(8,128)(2,1)}, u32[]{:S(2)}, u32[]{:S(2)}) collective-permute-start(bf16[256,1024]{1,0:T(8,128)(2,1)} %get-tuple-element.466), channel_id=1, source_target_pairs={{0,16},{16,0},{8,24},{24,8},{1,17},{17,1},{9,25},{25,9},{2,18},{18... | collective-permute-start | bytes 1572872 | tf_op jit(solution)/shard_map/ppermute | solution.py:353
  681.7 254.7 %all-gather.5.cloned.1.call-start = ((), (), s32[]{:S(2)}) async-start(), calls=%async_computation.3 | async-start | bytes 5242880 | tf_op jit(solution)/shard_map/all_gather | solution.py:1490
  684.2 54.4 %collective-permute-start.55 = (bf16[256,2048]{1,0:T(8,128)(2,1)}, bf16[256,2048]{1,0:T(8,128)(2,1)}, u32[]{:S(2)}, u32[]{:S(2)}) collective-permute-start(bf16[256,2048]{1,0:T(8,128)(2,1)} %pad_maximum_fusion.3), channel_id=1, source_target_pairs={{0,8},{8,0},{16,24},{24,16},{1,9},{9,1},{17,25},{25,17},{2,10},{10... | collective-permute-start | bytes 3145736 | tf_op jit(solution)/shard_map/ppermute | solution.py:349
  685.7 52.9 %collective-permute-start.56 = (bf16[256,2048]{1,0:T(8,128)(2,1)}, bf16[256,2048]{1,0:T(8,128)(2,1)}, u32[]{:S(2)}, u32[]{:S(2)}) collective-permute-start(bf16[256,2048]{1,0:T(8,128)(2,1)} %pad_maximum_fusion.4), channel_id=1, source_target_pairs={{0,16},{16,0},{8,24},{24,8},{1,17},{17,1},{9,25},{25,9},{2,18},{18... | collective-permute-start | bytes 3145736 | tf_op jit(solution)/shard_map/ppermute | solution.py:353
  724.0 68.5 %collective-permute-start.60 = (bf16[256,2048]{1,0:T(8,128)(2,1)}, bf16[256,2048]{1,0:T(8,128)(2,1)}, u32[]{:S(2)}, u32[]{:S(2)}) collective-permute-start(bf16[256,2048]{1,0:T(8,128)(2,1)} %pad_maximum_fusion.6), channel_id=1, source_target_pairs={{0,16},{16,0},{8,24},{24,8},{1,17},{17,1},{9,25},{25,9},{2,18},{18... | collective-permute-start | bytes 3145736 | tf_op jit(solution)/shard_map/ppermute | solution.py:353
  725.0 67.6 %collective-permute-start.59 = (bf16[256,2048]{1,0:T(8,128)(2,1)}, bf16[256,2048]{1,0:T(8,128)(2,1)}, u32[]{:S(2)}, u32[]{:S(2)}) collective-permute-start(bf16[256,2048]{1,0:T(8,128)(2,1)} %pad_maximum_fusion.5), channel_id=1, source_target_pairs={{0,8},{8,0},{16,24},{24,16},{1,9},{9,1},{17,25},{25,17},{2,10},{10... | collective-permute-start | bytes 3145736 | tf_op jit(solution)/shard_map/ppermute | solution.py:349
  747.8 15.3 %collective-permute-start.57 = (bf16[256,1024]{1,0:T(8,128)(2,1)S(1)}, bf16[256,1024]{1,0:T(8,128)(2,1)}, u32[]{:S(2)}, u32[]{:S(2)}) collective-permute-start(bf16[256,1024]{1,0:T(8,128)(2,1)S(1)} %get-tuple-element.488), channel_id=1, source_target_pairs={{0,8},{8,0},{16,24},{24,16},{1,9},{9,1},{17,25},{25,17},{2,10},{10... | collective-permute-start | bytes 1572872 | tf_op jit(solution)/shard_map/ppermute | solution.py:349
  762.0 68.0 %collective-permute-start.62 = (bf16[256,2048]{1,0:T(8,128)(2,1)}, bf16[256,2048]{1,0:T(8,128)(2,1)S(1)}, u32[]{:S(2)}, u32[]{:S(2)}) collective-permute-start(bf16[256,2048]{1,0:T(8,128)(2,1)} %slice.352), channel_id=1, source_target_pairs={{0,8},{8,0},{16,24},{24,16},{1,9},{9,1},{17,25},{25,17},{2,10},{10... | collective-permute-start | bytes 3145736 | tf_op jit(solution)/shard_map/ppermute | solution.py:349
  766.2 58.0 %collective-permute-start.61 = (bf16[256,2048]{1,0:T(8,128)(2,1)}, bf16[256,2048]{1,0:T(8,128)(2,1)}, u32[]{:S(2)}, u32[]{:S(2)}) collective-permute-start(bf16[256,2048]{1,0:T(8,128)(2,1)} %add_convert_fusion.7), channel_id=1, source_target_pairs={{0,3},{1,0},{2,1},{3,2},{4,7},{5,4},{6,5},{7,6},{8,11},{9,8},{10,9... | collective-permute-start | bytes 3145736 | tf_op jit(solution)/shard_map/ppermute | solution.py:363
  821.9 20.1 %collective-permute-start.64 = (bf16[512,2048]{1,0:T(8,128)(2,1)}, bf16[512,2048]{1,0:T(8,128)(2,1)}, u32[]{:S(2)}, u32[]{:S(2)}) collective-permute-start(bf16[512,2048]{1,0:T(8,128)(2,1)} %pad_maximum_fusion.1), channel_id=1, source_target_pairs={{0,4},{4,0},{1,5},{5,1},{2,6},{6,2},{3,7},{7,3},{8,12},{12,8},{9,1... | collective-permute-start | bytes 6291464 | tf_op jit(solution)/shard_map/ppermute | solution.py:345
  822.8 29.5 %collective-permute-start.67 = (bf16[256,2048]{1,0:T(8,128)(2,1)}, bf16[256,2048]{1,0:T(8,128)(2,1)S(1)}, u32[]{:S(2)}, u32[]{:S(2)}) collective-permute-start(bf16[256,2048]{1,0:T(8,128)(2,1)} %pad_maximum_fusion.8), channel_id=1, source_target_pairs={{0,16},{16,0},{8,24},{24,8},{1,17},{17,1},{9,25},{25,9},{2,18},{18... | collective-permute-start | bytes 3145736 | tf_op jit(solution)/shard_map/ppermute | solution.py:353
  824.2 28.1 %collective-permute-start.66 = (bf16[256,2048]{1,0:T(8,128)(2,1)}, bf16[256,2048]{1,0:T(8,128)(2,1)}, u32[]{:S(2)}, u32[]{:S(2)}) collective-permute-start(bf16[256,2048]{1,0:T(8,128)(2,1)} %pad_maximum_fusion.7), channel_id=1, source_target_pairs={{0,8},{8,0},{16,24},{24,16},{1,9},{9,1},{17,25},{25,17},{2,10},{10... | collective-permute-start | bytes 3145736 | tf_op jit(solution)/shard_map/ppermute | solution.py:349
  830.0 25.3 %collective-permute-start.65 = (bf16[256,2048]{1,0:T(8,128)(2,1)}, bf16[256,2048]{1,0:T(8,128)(2,1)}, u32[]{:S(2)}, u32[]{:S(2)}) collective-permute-start(bf16[256,2048]{1,0:T(8,128)(2,1)} %add_convert_fusion.5), channel_id=1, source_target_pairs={{0,3},{1,0},{2,1},{3,2},{4,7},{5,4},{6,5},{7,6},{8,11},{9,8},{10,9... | collective-permute-start | bytes 3145736 | tf_op jit(solution)/shard_map/ppermute | solution.py:363
  842.0 22.7 %collective-permute-start.68 = (f32[256,1024]{1,0:T(8,128)}, f32[256,1024]{1,0:T(8,128)S(1)}, u32[]{:S(2)}, u32[]{:S(2)}) collective-permute-start(f32[256,1024]{1,0:T(8,128)} %get-tuple-element.518), channel_id=1, source_target_pairs={{0,4},{4,0},{1,5},{5,1},{2,6},{6,2},{3,7},{7,3},{8,12},{12,8},{9,1... | collective-permute-start | bytes 3145736 | tf_op jit(solution)/shard_map/ppermute | solution.py:345
  842.0 22.6 %collective-permute-start.69 = (f32[256,1024]{1,0:T(8,128)}, f32[256,1024]{1,0:T(8,128)}, u32[]{:S(2)}, u32[]{:S(2)}) collective-permute-start(f32[256,1024]{1,0:T(8,128)} %get-tuple-element.519), channel_id=1, source_target_pairs={{0,4},{4,0},{1,5},{5,1},{2,6},{6,2},{3,7},{7,3},{8,12},{12,8},{9,1... | collective-permute-start | bytes 3145736 | tf_op jit(solution)/shard_map/ppermute | solution.py:345
  852.3 39.0 %collective-permute-start.71 = (bf16[256,2048]{1,0:T(8,128)(2,1)}, bf16[256,2048]{1,0:T(8,128)(2,1)}, u32[]{:S(2)}, u32[]{:S(2)}) collective-permute-start(bf16[256,2048]{1,0:T(8,128)(2,1)} %pad_maximum_fusion.9), channel_id=1, source_target_pairs={{0,8},{8,0},{16,24},{24,16},{1,9},{9,1},{17,25},{25,17},{2,10},{10... | collective-permute-start | bytes 3145736 | tf_op jit(solution)/shard_map/ppermute | solution.py:349
  852.4 45.3 %collective-permute-start.73 = (bf16[256,2048]{1,0:T(8,128)(2,1)}, bf16[256,2048]{1,0:T(8,128)(2,1)}, u32[]{:S(2)}, u32[]{:S(2)}) collective-permute-start(bf16[256,2048]{1,0:T(8,128)(2,1)} %pad_maximum_fusion.10), channel_id=1, source_target_pairs={{0,16},{16,0},{8,24},{24,8},{1,17},{17,1},{9,25},{25,9},{2,18},{18... | collective-permute-start | bytes 3145736 | tf_op jit(solution)/shard_map/ppermute | solution.py:353
  859.3 38.4 %collective-permute-start.74 = (bf16[256,2048]{1,0:T(8,128)(2,1)}, bf16[256,2048]{1,0:T(8,128)(2,1)}, u32[]{:S(2)}, u32[]{:S(2)}) collective-permute-start(bf16[256,2048]{1,0:T(8,128)(2,1)} %add_convert_fusion.3), channel_id=1, source_target_pairs={{0,3},{1,0},{2,1},{3,2},{4,7},{5,4},{6,5},{7,6},{8,11},{9,8},{10,9... | collective-permute-start | bytes 3145736 | tf_op jit(solution)/shard_map/ppermute | solution.py:363
  908.1 26.7 %collective-permute-start.82 = (bf16[256,2048]{1,0:T(8,128)(2,1)S(1)}, bf16[256,2048]{1,0:T(8,128)(2,1)S(1)}, u32[]{:S(2)}, u32[]{:S(2)}) collective-permute-start(bf16[256,2048]{1,0:T(8,128)(2,1)S(1)} %pad_maximum_fusion.11.refs_0_), channel_id=1, source_target_pairs={{0,16},{16,0},{8,24},{24,8},{1,17},{17,1},{9,25},{25,9},{2,18},{18... | collective-permute-start | bytes 3145736 | tf_op jit(solution)/shard_map/ppermute | solution.py:353
  909.6 26.0 %collective-permute-start.81 = (bf16[256,2048]{1,0:T(8,128)(2,1)S(1)}, bf16[256,2048]{1,0:T(8,128)(2,1)S(1)}, u32[]{:S(2)}, u32[]{:S(2)}) collective-permute-start(bf16[256,2048]{1,0:T(8,128)(2,1)S(1)} %pad_maximum_fusion.11.refs_0_), channel_id=1, source_target_pairs={{0,8},{8,0},{16,24},{24,16},{1,9},{9,1},{17,25},{25,17},{2,10},{10... | collective-permute-start | bytes 3145736 | tf_op jit(solution)/shard_map/ppermute | solution.py:349
  (138 other events, 2322.6 us)
Sparse Core Ops, SparseCore 0:
  39.3 208.9 all-gather.8
  580.7 100.9 reduce-scatter.4
  684.1 77.2 reduce-scatter.2
  763.1 60.6 all-gather.6
  825.4 88.6 all-gather.4

commit v9 on v8

--- a/solution.py
+++ b/solution.py
@@ -1486,8 +1486,7 @@
     for part in range(2):
         span = slice(part * width // 2, (part + 1) * width // 2)
         total = order.tie(add_rounded(ff_mine[:, span], ff_other[:, span]))
-        total = lax.psum_scatter(total, "col", scatter_dimension=0, tiled=False)
-        ff_grads.append(lax.all_gather(total, "dp"))
+        ff_grads.append(lax.psum_scatter(total, "col", scatter_dimension=0, tiled=False))
 
     down_via_x, down_via_y = plane.both(top(down_parts[3]), bottom(down_parts[3]), True)
     head_grad = order.run(head_grads, grad_rows, own_parts, other_rows)
@@ -1557,6 +1556,7 @@
     head_weights(0)
     vias[0] = first_messages(0)
     came[1] = second_messages(1, vias[1])
+    ff_grads = [lax.all_gather(after(g, *order.tokens), "dp") for g in ff_grads]
     total = column.send(step_down, group_total(3, came[3], None))
     order.tokens += came[2]
     back_rows = order.run(sum_rows, head_rows, own_parts, other_rows, 0)
@@ -1606,10 +1606,10 @@
         summed = summed + column.send(lambda v: lax.ppermute(v, "col", pairs), summed)
         step *= 2
     input_grad = order.run(join_tokens, index, input_mine, *input_others)
+    far = plane.far(*near)
     up_weight_grad, down_weight_grad = order.run(place_ff, ff_grads)
-    far = plane.far(*near)
-    query_weight_grad, key_weight_grad, value_weight_grad, out_weight_grad = place_heads(
-        index, [total, *near, *far]
+    query_weight_grad, key_weight_grad, value_weight_grad, out_weight_grad = order.run(
+        place_heads, index, [total, *near, *far]
     )
 
     bias_here = picked(summed[: bias_vector.size].reshape(ring, -1), col_i)

time: 982 us -> 1010 us (1.029)
  starting transfers between devices: 138 us -> 189 us
  waiting for transfers between devices: 255 us -> 221 us
    ppermute x3, starting transfers between devices: 31.6 us -> 67.6 us  [step_down(): lax.ppermute(values, 'col', [(i, (i - 1) % count) for i in range(count)])]
    reduce_scatter x2, waiting for transfers between devices: 21.7 us -> 0.01 us  [body_local(): lax.psum_scatter(total, 'col', scatter_dimension=0, tiled=False)]
    unnamed x238 -> x256, local copies, waits for them, and re-layouts: 35 us -> 36.4 us
where the time goes in v9:
time: 1010 us; the launch traced here: 994 us
  Pallas kernels  418 us (41%)
  waiting for transfers between devices  221 us (22%)
  starting transfers between devices  189 us (19%)
  local copies, waits for them, and re-layouts  90.3 us (9%)
  other arithmetic  59 us (6%)
  between operations  15.8 us (2%)
    pallas_call x4, Pallas kernels, ffn_rows_of(): pl.pallas_call(ffn_kernel, grid_spec=pltpu.PrefetchScalarGridSpec(num_sca...  102 us
    ppermute x29, waiting for transfers between devices, step_y(): return lax.ppermute(values, 'dp', [(0, 2), (2, 0), (1, 3), (3, 1)])  85.1 us
    ppermute x3, waiting for transfers between devices, step_up(): lax.ppermute(values, 'col', [(i, (i + 1) % count) for i in range(count)])  82.7 us
    ppermute x3, starting transfers between devices, step_down(): lax.ppermute(values, 'col', [(i, (i - 1) % count) for i in range(count)])  67.6 us
    pallas_call x2, Pallas kernels, weight_products(): pl.pallas_call(functools.partial(weight_products_kernel, count), grid=(ri...  58 us
    pallas_call x4, Pallas kernels, local_backward(): pl.pallas_call(functools.partial(local_backward_kernel, min(512, length))...  50.3 us
    ppermute x29, waiting for transfers between devices, step_x(): return lax.ppermute(values, 'dp', [(0, 1), (1, 0), (2, 3), (3, 2)])  43.9 us
    ppermute x29, starting transfers between devices, step_x(): return lax.ppermute(values, 'dp', [(0, 1), (1, 0), (2, 3), (3, 2)])  37.2 us
  transfers between devices with their start and end apart: 90, of which 28 were waited for; matrix products, arithmetic and copies ran while one was open for 12% of the time, Pallas kernels for 38%

profile of v9, /device:TPU:0, one launch (start us, length us, event | category | flops | bytes accessed | tf_op | source)
XLA Modules:
  0.0 993.7 jit_solution(12839891436048459597)
XLA Ops:
  43.0 36.7 %collective-permute-done.6.refs_0_ = bf16[512,1024]{1,0:T(8,128)(2,1)} collective-permute-done((bf16[512,1024]{1,0:T(8,128)(2,1)}, bf16[512,1024]{1,0:T(8,128)(2,1)}, u32[]{:S(2)}, u32[]{:S(2)}) %collective-permute-start.6) | collective-permute-done | bytes 1048608 | tf_op jit(solution)/shard_map/ppermute | solution.py:358
  84.4 3.6 shard_map.316
  91.5 6.1 collective-permute-start.15
  97.8 6.7 shard_map.317
  104.5 9.2 collective-permute-done.12.refs_2_
  116.2 6.1 shard_map.318.query_ref.key_ref.value_ref
  122.4 6.5 shard_map.319.refs_0_.refs_5_
  130.9 21.1 %collective-permute-done.15.refs_0_ = bf16[512,1024]{1,0:T(8,128)(2,1)S(1)} collective-permute-done((bf16[512,1024]{1,0:T(8,128)(2,1)}, bf16[512,1024]{1,0:T(8,128)(2,1)S(1)}, u32[]{:S(2)}, u32[]{:S(2)}) %collective-permute-start.15) | collective-permute-done | bytes 1048608 | tf_op jit(solution)/shard_map/ppermute | solution.py:358
  152.9 23.8 %collective-permute-start.20 = (bf16[512,1024]{1,0:T(8,128)(2,1)S(1)}, bf16[512,1024]{1,0:T(8,128)(2,1)S(1)}, u32[]{:S(2)}, u32[]{:S(2)}) collective-permute-start(bf16[512,1024]{1,0:T(8,128)(2,1)S(1)} %collective-permute-done.15.refs_0_), channel_id=1, source_target_pairs={{0,1},{1,2},{2,3},{3,0},{4,5},{5,6},{6,7},{7,4},{8,9},{9,10},{10,1... | collective-permute-start | bytes 3145736 | tf_op jit(solution)/shard_map/ppermute | solution.py:358
  176.7 3.8 shard_map.320
  183.8 5.6 shard_map.321.query_ref.key_ref.value_ref
  189.4 6.5 shard_map.322.refs_1_.refs_5_
  197.2 24.9 %collective-permute-done.20.refs_0_ = bf16[512,1024]{1,0:T(8,128)(2,1)S(1)} collective-permute-done((bf16[512,1024]{1,0:T(8,128)(2,1)S(1)}, bf16[512,1024]{1,0:T(8,128)(2,1)S(1)}, u32[]{:S(2)}, u32[]{:S(2)}) %collective-permute-start.20) | collective-permute-done | bytes 1048608 | tf_op jit(solution)/shard_map/ppermute | solution.py:358
  231.2 5.4 shard_map.324.query_ref.key_ref.value_ref
  236.7 6.5 shard_map.325.refs_2_.refs_5_
  250.4 8.8 collective-permute-done.24.refs_4_
  263.8 7.6 shard_map.327.refs_3_
  273.4 5.5 shard_map.328.query_ref.key_ref.value_ref
  278.9 6.7 shard_map.329.refs_0_.refs_5_
  285.6 6.5 collective-permute-done.28
  294.3 6.3 shard_map.330.rows_ref
  309.3 6.5 shard_map.331
  315.8 3.7 collective-permute-done.32
  329.2 25.4 %shard_map.332 = (bf16[512,4096]{1,0:T(8,128)(2,1)}, f32[4,1,512]{2,1,0:T(1,128)S(1)}, bf16[512,2048]{1,0:T(8,128)(2,1)S(1)}, bf16[512,2048]{1,0:T(8,128)(2,1)S(1)}) custom-call(s32[3]{0:T(128)S(1)} %pad_add_fusion.index_ref.refs_0_, bf16[512,2048]{1,0:T(8,128)(2,1)} %get-tuple-element.426.refs_0_.refs_1_, ...), custom_call_target="tpu_custom_call" | custom-call | flops 1717986944 | bytes 5033164 | tf_op jit(solution)/shard_map/pallas_call | solution.py:621
  354.6 12.5 %collective-permute-done.33.refs_0_.refs_1_.refs_2_ = bf16[512,2048]{1,0:T(8,128)(2,1)} collective-permute-done((bf16[512,2048]{1,0:T(8,128)(2,1)}, bf16[512,2048]{1,0:T(8,128)(2,1)}, u32[]{:S(2)}, u32[]{:S(2)}) %collective-permute-start.33) | collective-permute-done | bytes 2097184 | tf_op jit(solution)/shard_map/ppermute | solution.py:353
  378.0 25.6 %shard_map.333 = (bf16[512,4096]{1,0:T(8,128)(2,1)}, f32[4,1,512]{2,1,0:T(1,128)S(1)}, bf16[512,2048]{1,0:T(8,128)(2,1)S(1)}, bf16[512,2048]{1,0:T(8,128)(2,1)S(1)}) custom-call(s32[3]{0:T(128)S(1)} %pad_add_fusion.index_ref.refs_0_, bf16[512,2048]{1,0:T(8,128)(2,1)} %collective-permute-done.31.refs_0_.refs_1_, ...), custom_call_target="tpu_custom_call" | custom-call | flops 1717986944 | bytes 5033164 | tf_op jit(solution)/shard_map/pallas_call | solution.py:621
  405.5 25.4 %shard_map.334 = (bf16[512,4096]{1,0:T(8,128)(2,1)}, f32[4,1,512]{2,1,0:T(1,128)S(1)}, bf16[512,2048]{1,0:T(8,128)(2,1)S(1)}, bf16[512,2048]{1,0:T(8,128)(2,1)S(1)}) custom-call(s32[3]{0:T(128)S(1)} %pad_add_fusion.index_ref.refs_0_, bf16[512,2048]{1,0:T(8,128)(2,1)} %collective-permute-done.33.refs_0_.refs_1_.refs_2_, ...), custom_call_target="tpu_custom_call" | custom-call | flops 1717986944 | bytes 5033164 | tf_op jit(solution)/shard_map/pallas_call | solution.py:621
  435.0 25.4 %shard_map.335 = (bf16[512,4096]{1,0:T(8,128)(2,1)}, f32[4,1,512]{2,1,0:T(1,128)S(1)}, bf16[512,2048]{1,0:T(8,128)(2,1)S(1)}, bf16[512,2048]{1,0:T(8,128)(2,1)S(1)}) custom-call(s32[3]{0:T(128)S(1)} %pad_add_fusion.index_ref.refs_0_, bf16[512,2048]{1,0:T(8,128)(2,1)} %constant_dynamic-update-slice_fusion.refs_0_.refs_1_.refs_3_, ...), custom_call_target="tpu_custom_call" | custom-call | flops 1717986944 | bytes 5033164 | tf_op jit(solution)/shard_map/pallas_call | solution.py:621
  465.0 29.0 %shard_map.336 = bf16[4,1024,1024]{2,1,0:T(8,128)(2,1)} custom-call(bf16[512,2048]{1,0:T(8,128)(2,1)} %get-tuple-element.426.refs_0_.refs_1_, bf16[512,2048]{1,0:T(8,128)(2,1)} %collective-permute-done.31.refs_0_.refs_1_, bf16[512,2048]{1,0:T(8,128)(2,1)} %collective-permute-done.33.refs_0_.refs_1_.refs_2_, ...), custom_call_target="tpu_custom_call" | custom-call | flops 1717986944 | bytes 6710886 | tf_op jit(solution)/shard_map/pallas_call | solution.py:667
  494.0 3.7 add_convert_fusion.10
  497.6 29.1 %shard_map.337 = bf16[4,1024,1024]{2,1,0:T(8,128)(2,1)} custom-call(bf16[512,2048]{1,0:T(8,128)(2,1)} %get-tuple-element.426.refs_0_.refs_1_, bf16[512,2048]{1,0:T(8,128)(2,1)} %collective-permute-done.31.refs_0_.refs_1_, bf16[512,2048]{1,0:T(8,128)(2,1)} %collective-permute-done.33.refs_0_.refs_1_.refs_2_, ...), custom_call_target="tpu_custom_call" | custom-call | flops 1717986944 | bytes 6710886 | tf_op jit(solution)/shard_map/pallas_call | solution.py:667
  530.6 21.7 %collective-permute-done.40.refs_2_ = bf16[256,2048]{1,0:T(8,128)(2,1)S(1)} collective-permute-done((bf16[256,2048]{1,0:T(8,128)(2,1)S(1)}, bf16[256,2048]{1,0:T(8,128)(2,1)S(1)}, u32[]{:S(2)}, u32[]{:S(2)}) %collective-permute-start.40) | collective-permute-done | bytes 1048608 | tf_op jit(solution)/shard_map/ppermute | solution.py:353
  552.7 12.1 %shard_map.338 = (f32[512,2048]{1,0:T(8,128)}, bf16[512,2048]{1,0:T(8,128)(2,1)}, bf16[512,2048]{1,0:T(8,128)(2,1)}, f32[8,2048]{1,0:T(8,128)S(1)}) custom-call(s32[3]{0:T(128)S(1)} %pad_add_fusion.index_ref.refs_0_, bf16[512,2048]{1,0:T(8,128)(2,1)} %copy-done.35, bf16[256,2048]{1,0:T(8,128)(2,1)S(1)} %collective-permute-done.36.refs_1_, ...), custom_call_target="tpu_custom_call" | custom-call | bytes 2516582 | tf_op jit(solution)/shard_map/pallas_call | solution.py:1048
  567.3 10.1 %add_convert_fusion = (bf16[4,512,1024]{2,1,0:T(8,128)(2,1)}, bf16[4,512,1024]{2,1,0:T(8,128)(2,1)}) fusion(bf16[4,1024,1024]{2,1,0:T(8,128)(2,1)} %collective-permute-done.42, bf16[4,1024,1024]{2,1,0:T(8,128)(2,1)} %shard_map.336), kind=kLoop, calls=%fused_computation.2 | loop fusion | flops 16777216 | bytes 25165824 | tf_op jit(solution)/shard_map/convert_element_type | solution.py:418
  586.3 8.0 shard_map.340.grad_ref
  594.3 12.4 %shard_map.341.refs_4_.refs_3_ = bf16[1024,768]{1,0:T(8,128)(2,1)S(1)} custom-call(s32[1,1024]{1,0:T(1,128)S(1)} %bitcast.59, bf16[1024,768]{1,0:T(8,128)(2,1)S(1)} %shard_map.328.query_ref.key_ref.value_ref, bf16[1024,1024]{1,0:T(8,128)(2,1)S(1)} %shard_map.340.grad_ref, bf16[1024,768]{1,0:T(8,128)(2,1)S(1)} %shard_map.328.query_ref.key_ref.value_ref, ...), custom_call_target="tpu_custom_call" | custom-call | flops 858993472 | bytes 629145 | tf_op jit(solution)/shard_map/pallas_call | solution.py:544
  606.7 8.8 shard_map.342
  626.6 12.5 %shard_map.343.refs_4_.refs_2_ = bf16[1024,768]{1,0:T(8,128)(2,1)S(1)} custom-call(s32[1,1024]{1,0:T(1,128)S(1)} %bitcast.60, bf16[1024,768]{1,0:T(8,128)(2,1)S(1)} %copy-done.5, bf16[1024,1024]{1,0:T(8,128)(2,1)S(1)} %shard_map.340.grad_ref, bf16[1024,768]{1,0:T(8,128)(2,1)S(1)} %copy-done.5, bf16[1024,768]{1,0:T(8,128)(2,1)S(1)} %copy-done.5), custom_call_target="tpu_custom_call" | custom-call | flops 858993472 | bytes 629145 | tf_op jit(solution)/shard_map/pallas_call | solution.py:544
  639.2 8.3 shard_map.344
  654.7 15.2 %collective-permute-done.50 = bf16[256,1024]{1,0:T(8,128)(2,1)S(1)} collective-permute-done((bf16[256,1024]{1,0:T(8,128)(2,1)S(1)}, bf16[256,1024]{1,0:T(8,128)(2,1)S(1)}, u32[]{:S(2)}, u32[]{:S(2)}) %collective-permute-start.50) | collective-permute-done | bytes 524320 | tf_op jit(solution)/shard_map/ppermute | solution.py:353
  675.2 12.6 %shard_map.345.refs_4_.refs_1_ = bf16[1024,768]{1,0:T(8,128)(2,1)S(1)} custom-call(s32[1,1024]{1,0:T(1,128)S(1)} %bitcast.61, bf16[1024,768]{1,0:T(8,128)(2,1)S(1)} %copy-done.3, bf16[1024,1024]{1,0:T(8,128)(2,1)S(1)} %shard_map.340.grad_ref, bf16[1024,768]{1,0:T(8,128)(2,1)S(1)} %copy-done.3, bf16[1024,768]{1,0:T(8,128)(2,1)S(1)} %copy-done.3), custom_call_target="tpu_custom_call" | custom-call | flops 858993472 | bytes 629145 | tf_op jit(solution)/shard_map/pallas_call | solution.py:544
  687.8 8.3 shard_map.346
  703.2 8.0 collective-permute-done.54
  711.9 12.8 %shard_map.347.refs_4_.refs_0_ = bf16[1024,768]{1,0:T(8,128)(2,1)S(1)} custom-call(s32[1,1024]{1,0:T(1,128)S(1)} %bitcast.62, bf16[1024,768]{1,0:T(8,128)(2,1)S(1)} %copy-done.1, bf16[1024,1024]{1,0:T(8,128)(2,1)S(1)} %shard_map.340.grad_ref, bf16[1024,768]{1,0:T(8,128)(2,1)S(1)} %copy-done.1, bf16[1024,768]{1,0:T(8,128)(2,1)S(1)} %copy-done.1), custom_call_target="tpu_custom_call" | custom-call | flops 858993472 | bytes 629145 | tf_op jit(solution)/shard_map/pallas_call | solution.py:544
  724.7 8.8 shard_map.348
  742.5 6.2 collective-permute-done.58
  757.1 3.5 add_convert_fusion.7
  760.6 28.5 %collective-permute-start.61 = (bf16[256,2048]{1,0:T(8,128)(2,1)}, bf16[256,2048]{1,0:T(8,128)(2,1)}, u32[]{:S(2)}, u32[]{:S(2)}) collective-permute-start(bf16[256,2048]{1,0:T(8,128)(2,1)} %add_convert_fusion.7), channel_id=1, source_target_pairs={{0,3},{1,0},{2,1},{3,2},{4,7},{5,4},{6,5},{7,6},{8,11},{9,8},{10,9... | collective-permute-start | bytes 3145736 | tf_op jit(solution)/shard_map/ppermute | solution.py:363
  789.2 21.0 %shard_map.349.refs_0_ = f32[1024,2048]{1,0:T(8,128)} custom-call(bf16[1024,768]{1,0:T(8,128)(2,1)S(1)} %copy-done.26, bf16[1024,768]{1,0:T(8,128)(2,1)S(1)} %shard_map.345.refs_4_.refs_1_, bf16[1024,768]{1,0:T(8,128)(2,1)S(1)} %shard_map.343.refs_4_.refs_2_, bf16[1024,768]{1,0:T(8,128)(2,1)} %copy-done.24, ...), custom_call_target="tpu_custom_call" | custom-call | flops 1288490240 | bytes 838860 | tf_op jit(solution)/shard_map/pallas_call | solution.py:862
  823.7 3.9 add_convert_fusion.5
  827.6 30.2 %collective-permute-start.65 = (bf16[256,2048]{1,0:T(8,128)(2,1)}, bf16[256,2048]{1,0:T(8,128)(2,1)}, u32[]{:S(2)}, u32[]{:S(2)}) collective-permute-start(bf16[256,2048]{1,0:T(8,128)(2,1)} %add_convert_fusion.5), channel_id=1, source_target_pairs={{0,3},{1,0},{2,1},{3,2},{4,7},{5,4},{6,5},{7,6},{8,11},{9,8},{10,9... | collective-permute-start | bytes 3145736 | tf_op jit(solution)/shard_map/ppermute | solution.py:363
  857.8 8.4 shard_map.350
  866.3 3.4 fusion.11
  870.2 7.7 shard_map.351
  884.6 4.0 add_convert_fusion.3
  888.6 8.9 collective-permute-start.74
  897.6 4.6 shard_map.352
  903.1 9.7 collective-permute-done.71
  915.3 4.1 collective-permute-done.72
  923.0 3.3 collective-permute-start.76
  941.1 11.3 %collective-permute-done.82.refs_1_ = bf16[256,2048]{1,0:T(8,128)(2,1)S(1)} collective-permute-done((bf16[256,2048]{1,0:T(8,128)(2,1)S(1)}, bf16[256,2048]{1,0:T(8,128)(2,1)S(1)}, u32[]{:S(2)}, u32[]{:S(2)}) %collective-permute-start.82) | collective-permute-done | bytes 1048608 | tf_op jit(solution)/shard_map/ppermute | solution.py:349
  960.2 6.6 collective-permute-start.80
  973.4 8.0 shard_map.354
  981.5 5.5 shard_map.355
  (559 shorter events, 239.4 us)
Async XLA Ops:
  7.2 299.5 %all-gather.7.cloned.1.call-start = ((), (), s32[]{:S(2)}) async-start(), calls=%async_computation.4 | async-start | bytes 18874368 | tf_op jit(solution)/shard_map/all_gather | solution.py:1358
  10.5 18.7 %collective-permute-start.4 = (bf16[512,1024]{1,0:T(8,128)(2,1)}, bf16[512,1024]{1,0:T(8,128)(2,1)}, u32[]{:S(2)}, u32[]{:S(2)}) collective-permute-start(bf16[512,1024]{1,0:T(8,128)(2,1)} %get-tuple-element.622), channel_id=1, source_target_pairs={{0,4},{4,0},{1,5},{5,1},{2,6},{6,2},{3,7},{7,3},{8,12},{12,8},{9,1... | collective-permute-start | bytes 3145736 | tf_op jit(solution)/shard_map/ppermute | solution.py:345
  17.1 17.5 %collective-permute-start.5 = (bf16[1024,1024]{1,0:T(8,128)(2,1)S(1)}, bf16[1024,1024]{1,0:T(8,128)(2,1)}, u32[]{:S(2)}, u32[]{:S(2)}) collective-permute-start(bf16[1024,1024]{1,0:T(8,128)(2,1)S(1)} %copy-done.6), channel_id=1, source_target_pairs={{0,4},{4,0},{1,5},{5,1},{2,6},{6,2},{3,7},{7,3},{8,12},{12,8},{9,1... | collective-permute-start | bytes 6291464 | tf_op jit(solution)/shard_map/ppermute | solution.py:345
  39.2 709.4 %reduce-scatter.5.cloned.1.call-start = ((), (), s32[]{:S(2)}) async-start(), calls=%async_computation.3 | async-start | bytes 5242880 | tf_op jit(solution)/shard_map/reduce_scatter | solution.py:1489
  39.3 40.4 %collective-permute-start.6 = (bf16[512,1024]{1,0:T(8,128)(2,1)}, bf16[512,1024]{1,0:T(8,128)(2,1)}, u32[]{:S(2)}, u32[]{:S(2)}) collective-permute-start(bf16[512,1024]{1,0:T(8,128)(2,1)} %pad_maximum_fusion.2), channel_id=1, source_target_pairs={{0,1},{1,2},{2,3},{3,0},{4,5},{5,6},{6,7},{7,4},{8,9},{9,10},{10,1... | collective-permute-start | bytes 3145736 | tf_op jit(solution)/shard_map/ppermute | solution.py:358
  40.0 39.7 %collective-permute-start.7 = (bf16[256,2048]{1,0:T(8,128)(2,1)}, bf16[256,2048]{1,0:T(8,128)(2,1)S(1)}, u32[]{:S(2)}, u32[]{:S(2)}) collective-permute-start(bf16[256,2048]{1,0:T(8,128)(2,1)} %get-tuple-element.304), channel_id=1, source_target_pairs={{0,8},{8,0},{16,24},{24,16},{1,9},{9,1},{17,25},{25,17},{2,10},{10... | collective-permute-start | bytes 3145736 | tf_op jit(solution)/shard_map/ppermute | solution.py:349
  41.5 39.2 %collective-permute-start.8 = (bf16[256,2048]{1,0:T(8,128)(2,1)}, bf16[256,2048]{1,0:T(8,128)(2,1)}, u32[]{:S(2)}, u32[]{:S(2)}) collective-permute-start(bf16[256,2048]{1,0:T(8,128)(2,1)} %get-tuple-element.304), channel_id=1, source_target_pairs={{0,16},{16,0},{8,24},{24,8},{1,17},{17,1},{9,25},{25,9},{2,18},{18... | collective-permute-start | bytes 3145736 | tf_op jit(solution)/shard_map/ppermute | solution.py:353
  88.0 28.3 %collective-permute-start.10 = (bf16[1024,1024]{1,0:T(8,128)(2,1)}, bf16[1024,1024]{1,0:T(8,128)(2,1)}, u32[]{:S(2)}, u32[]{:S(2)}) collective-permute-start(bf16[1024,1024]{1,0:T(8,128)(2,1)} %get-tuple-element.315), channel_id=1, source_target_pairs={{0,4},{4,0},{1,5},{5,1},{2,6},{6,2},{3,7},{7,3},{8,12},{12,8},{9,1... | collective-permute-start | bytes 6291464 | tf_op jit(solution)/shard_map/ppermute | solution.py:345
  88.0 25.8 %collective-permute-start.12 = (bf16[512,1024]{1,0:T(8,128)(2,1)}, bf16[512,1024]{1,0:T(8,128)(2,1)S(1)}, u32[]{:S(2)}, u32[]{:S(2)}) collective-permute-start(bf16[512,1024]{1,0:T(8,128)(2,1)} %collective-permute-done.6.refs_0_), channel_id=1, source_target_pairs={{0,16},{16,0},{8,24},{24,8},{1,17},{17,1},{9,25},{25,9},{2,18},{18... | collective-permute-start | bytes 3145736 | tf_op jit(solution)/shard_map/ppermute | solution.py:353
  89.5 25.6 %collective-permute-start.11 = (bf16[512,1024]{1,0:T(8,128)(2,1)}, bf16[512,1024]{1,0:T(8,128)(2,1)}, u32[]{:S(2)}, u32[]{:S(2)}) collective-permute-start(bf16[512,1024]{1,0:T(8,128)(2,1)} %collective-permute-done.6.refs_0_), channel_id=1, source_target_pairs={{0,8},{8,0},{16,24},{24,16},{1,9},{9,1},{17,25},{25,17},{2,10},{10... | collective-permute-start | bytes 3145736 | tf_op jit(solution)/shard_map/ppermute | solution.py:349
  91.5 60.5 %collective-permute-start.15 = (bf16[512,1024]{1,0:T(8,128)(2,1)}, bf16[512,1024]{1,0:T(8,128)(2,1)S(1)}, u32[]{:S(2)}, u32[]{:S(2)}) collective-permute-start(bf16[512,1024]{1,0:T(8,128)(2,1)} %collective-permute-done.6.refs_0_), channel_id=1, source_target_pairs={{0,1},{1,2},{2,3},{3,0},{4,5},{5,6},{6,7},{7,4},{8,9},{9,10},{10,1... | collective-permute-start | bytes 3145736 | tf_op jit(solution)/shard_map/ppermute | solution.py:358
  128.9 23.1 %collective-permute-start.13 = (bf16[256,1024]{1,0:T(8,128)(2,1)S(1)}, bf16[256,1024]{1,0:T(8,128)(2,1)S(1)}, u32[]{:S(2)}, u32[]{:S(2)}) collective-permute-start(bf16[256,1024]{1,0:T(8,128)(2,1)S(1)} %slice.429), channel_id=1, source_target_pairs={{0,16},{16,0},{8,24},{24,8},{1,17},{17,1},{9,25},{25,9},{2,18},{18... | collective-permute-start | bytes 1572872 | tf_op jit(solution)/shard_map/ppermute | solution.py:353
  129.4 22.6 %collective-permute-start.14 = (bf16[256,1024]{1,0:T(8,128)(2,1)S(1)}, bf16[256,1024]{1,0:T(8,128)(2,1)S(1)}, u32[]{:S(2)}, u32[]{:S(2)}) collective-permute-start(bf16[256,1024]{1,0:T(8,128)(2,1)S(1)} %slice.430), channel_id=1, source_target_pairs={{0,8},{8,0},{16,24},{24,16},{1,9},{9,1},{17,25},{25,17},{2,10},{10... | collective-permute-start | bytes 1572872 | tf_op jit(solution)/shard_map/ppermute | solution.py:349
  152.0 44.0 %collective-permute-start.17 = (bf16[512,1024]{1,0:T(8,128)(2,1)S(1)}, bf16[512,1024]{1,0:T(8,128)(2,1)S(1)}, u32[]{:S(2)}, u32[]{:S(2)}) collective-permute-start(bf16[512,1024]{1,0:T(8,128)(2,1)S(1)} %collective-permute-done.15.refs_0_), channel_id=1, source_target_pairs={{0,16},{16,0},{8,24},{24,8},{1,17},{17,1},{9,25},{25,9},{2,18},{18... | collective-permute-start | bytes 3145736 | tf_op jit(solution)/shard_map/ppermute | solution.py:353
  152.4 43.6 %collective-permute-start.16 = (bf16[512,1024]{1,0:T(8,128)(2,1)S(1)}, bf16[512,1024]{1,0:T(8,128)(2,1)S(1)}, u32[]{:S(2)}, u32[]{:S(2)}) collective-permute-start(bf16[512,1024]{1,0:T(8,128)(2,1)S(1)} %collective-permute-done.15.refs_0_), channel_id=1, source_target_pairs={{0,8},{8,0},{16,24},{24,16},{1,9},{9,1},{17,25},{25,17},{2,10},{10... | collective-permute-start | bytes 3145736 | tf_op jit(solution)/shard_map/ppermute | solution.py:349
  152.9 69.2 %collective-permute-start.20 = (bf16[512,1024]{1,0:T(8,128)(2,1)S(1)}, bf16[512,1024]{1,0:T(8,128)(2,1)S(1)}, u32[]{:S(2)}, u32[]{:S(2)}) collective-permute-start(bf16[512,1024]{1,0:T(8,128)(2,1)S(1)} %collective-permute-done.15.refs_0_), channel_id=1, source_target_pairs={{0,1},{1,2},{2,3},{3,0},{4,5},{5,6},{6,7},{7,4},{8,9},{9,10},{10,1... | collective-permute-start | bytes 3145736 | tf_op jit(solution)/shard_map/ppermute | solution.py:358
  196.1 26.0 %collective-permute-start.18 = (bf16[256,1024]{1,0:T(8,128)(2,1)S(1)}, bf16[256,1024]{1,0:T(8,128)(2,1)S(1)}, u32[]{:S(2)}, u32[]{:S(2)}) collective-permute-start(bf16[256,1024]{1,0:T(8,128)(2,1)S(1)} %slice.432), channel_id=1, source_target_pairs={{0,16},{16,0},{8,24},{24,8},{1,17},{17,1},{9,25},{25,9},{2,18},{18... | collective-permute-start | bytes 1572872 | tf_op jit(solution)/shard_map/ppermute | solution.py:353
  196.6 25.5 %collective-permute-start.19 = (bf16[256,1024]{1,0:T(8,128)(2,1)S(1)}, bf16[256,1024]{1,0:T(8,128)(2,1)S(1)}, u32[]{:S(2)}, u32[]{:S(2)}) collective-permute-start(bf16[256,1024]{1,0:T(8,128)(2,1)S(1)} %slice.433), channel_id=1, source_target_pairs={{0,8},{8,0},{16,24},{24,16},{1,9},{9,1},{17,25},{25,17},{2,10},{10... | collective-permute-start | bytes 1572872 | tf_op jit(solution)/shard_map/ppermute | solution.py:349
  222.1 23.7 %collective-permute-start.22 = (bf16[512,1024]{1,0:T(8,128)(2,1)S(1)}, bf16[512,1024]{1,0:T(8,128)(2,1)S(1)}, u32[]{:S(2)}, u32[]{:S(2)}) collective-permute-start(bf16[512,1024]{1,0:T(8,128)(2,1)S(1)} %collective-permute-done.20.refs_0_), channel_id=1, source_target_pairs={{0,16},{16,0},{8,24},{24,8},{1,17},{17,1},{9,25},{25,9},{2,18},{18... | collective-permute-start | bytes 3145736 | tf_op jit(solution)/shard_map/ppermute | solution.py:353
  223.7 23.4 %collective-permute-start.21 = (bf16[512,1024]{1,0:T(8,128)(2,1)S(1)}, bf16[512,1024]{1,0:T(8,128)(2,1)S(1)}, u32[]{:S(2)}, u32[]{:S(2)}) collective-permute-start(bf16[512,1024]{1,0:T(8,128)(2,1)S(1)} %collective-permute-done.20.refs_0_), channel_id=1, source_target_pairs={{0,8},{8,0},{16,24},{24,16},{1,9},{9,1},{17,25},{25,17},{2,10},{10... | collective-permute-start | bytes 3145736 | tf_op jit(solution)/shard_map/ppermute | solution.py:349
  271.3 20.8 %collective-permute-start.28 = (bf16[256,2048]{1,0:T(8,128)(2,1)S(1)}, bf16[256,2048]{1,0:T(8,128)(2,1)S(1)}, u32[]{:S(2)}, u32[]{:S(2)}) collective-permute-start(bf16[256,2048]{1,0:T(8,128)(2,1)S(1)} %copy-done.88), channel_id=1, source_target_pairs={{0,8},{8,0},{16,24},{24,16},{1,9},{9,1},{17,25},{25,17},{2,10},{10... | collective-permute-start | bytes 3145736 | tf_op jit(solution)/shard_map/ppermute | solution.py:349
  272.4 21.0 %collective-permute-start.27 = (bf16[256,2048]{1,0:T(8,128)(2,1)S(1)}, bf16[256,2048]{1,0:T(8,128)(2,1)S(1)}, u32[]{:S(2)}, u32[]{:S(2)}) collective-permute-start(bf16[256,2048]{1,0:T(8,128)(2,1)S(1)} %copy-done.88), channel_id=1, source_target_pairs={{0,16},{16,0},{8,24},{24,8},{1,17},{17,1},{9,25},{25,9},{2,18},{18... | collective-permute-start | bytes 3145736 | tf_op jit(solution)/shard_map/ppermute | solution.py:353
  319.9 47.3 %collective-permute-start.33 = (bf16[512,2048]{1,0:T(8,128)(2,1)}, bf16[512,2048]{1,0:T(8,128)(2,1)}, u32[]{:S(2)}, u32[]{:S(2)}) collective-permute-start(bf16[512,2048]{1,0:T(8,128)(2,1)} %get-tuple-element.426.refs_0_.refs_1_), channel_id=1, source_target_pairs={{0,16},{16,0},{8,24},{24,8},{1,17},{17,1},{9,25},{25,9},{2,18},{18... | collective-permute-start | bytes 6291464 | tf_op jit(solution)/shard_map/ppermute | solution.py:353
  321.2 47.2 %collective-permute-start.31 = (bf16[512,2048]{1,0:T(8,128)(2,1)}, bf16[512,2048]{1,0:T(8,128)(2,1)}, u32[]{:S(2)}, u32[]{:S(2)}) collective-permute-start(bf16[512,2048]{1,0:T(8,128)(2,1)} %get-tuple-element.426.refs_0_.refs_1_), channel_id=1, source_target_pairs={{0,8},{8,0},{16,24},{24,16},{1,9},{9,1},{17,25},{25,17},{2,10},{10... | collective-permute-start | bytes 6291464 | tf_op jit(solution)/shard_map/ppermute | solution.py:349
  369.9 34.9 %collective-permute-start.35 = (bf16[256,2048]{1,0:T(8,128)(2,1)S(1)}, bf16[256,2048]{1,0:T(8,128)(2,1)S(1)}, u32[]{:S(2)}, u32[]{:S(2)}) collective-permute-start(bf16[256,2048]{1,0:T(8,128)(2,1)S(1)} %slice.449), channel_id=1, source_target_pairs={{0,8},{8,0},{16,24},{24,16},{1,9},{9,1},{17,25},{25,17},{2,10},{10... | collective-permute-start | bytes 3145736 | tf_op jit(solution)/shard_map/ppermute | solution.py:349
  371.1 60.9 %collective-permute-start.34 = (bf16[256,2048]{1,0:T(8,128)(2,1)S(1)}, bf16[256,2048]{1,0:T(8,128)(2,1)S(1)}, u32[]{:S(2)}, u32[]{:S(2)}) collective-permute-start(bf16[256,2048]{1,0:T(8,128)(2,1)S(1)} %slice.445), channel_id=1, source_target_pairs={{0,16},{16,0},{8,24},{24,8},{1,17},{17,1},{9,25},{25,9},{2,18},{18... | collective-permute-start | bytes 3145736 | tf_op jit(solution)/shard_map/ppermute | solution.py:353
  404.7 57.6 %collective-permute-start.36 = (bf16[256,2048]{1,0:T(8,128)(2,1)}, bf16[256,2048]{1,0:T(8,128)(2,1)S(1)}, u32[]{:S(2)}, u32[]{:S(2)}) collective-permute-start(bf16[256,2048]{1,0:T(8,128)(2,1)} %slice.346), channel_id=1, source_target_pairs={{0,8},{8,0},{16,24},{24,16},{1,9},{9,1},{17,25},{25,17},{2,10},{10... | collective-permute-start | bytes 3145736 | tf_op jit(solution)/shard_map/ppermute | solution.py:349
  432.0 30.3 %collective-permute-start.37 = (bf16[256,2048]{1,0:T(8,128)(2,1)}, bf16[256,2048]{1,0:T(8,128)(2,1)}, u32[]{:S(2)}, u32[]{:S(2)}) collective-permute-start(bf16[256,2048]{1,0:T(8,128)(2,1)} %slice.347), channel_id=1, source_target_pairs={{0,16},{16,0},{8,24},{24,8},{1,17},{17,1},{9,25},{25,9},{2,18},{18... | collective-permute-start | bytes 3145736 | tf_op jit(solution)/shard_map/ppermute | solution.py:353
  462.3 31.6 %collective-permute-start.39 = (bf16[256,2048]{1,0:T(8,128)(2,1)}, bf16[256,2048]{1,0:T(8,128)(2,1)}, u32[]{:S(2)}, u32[]{:S(2)}) collective-permute-start(bf16[256,2048]{1,0:T(8,128)(2,1)} %get-tuple-element.415), channel_id=1, source_target_pairs={{0,16},{16,0},{8,24},{24,8},{1,17},{17,1},{9,25},{25,9},{2,18},{18... | collective-permute-start | bytes 3145736 | tf_op jit(solution)/shard_map/ppermute | solution.py:353
  463.7 30.2 %collective-permute-start.38 = (bf16[256,2048]{1,0:T(8,128)(2,1)}, bf16[256,2048]{1,0:T(8,128)(2,1)}, u32[]{:S(2)}, u32[]{:S(2)}) collective-permute-start(bf16[256,2048]{1,0:T(8,128)(2,1)} %get-tuple-element.413), channel_id=1, source_target_pairs={{0,8},{8,0},{16,24},{24,16},{1,9},{9,1},{17,25},{25,17},{2,10},{10... | collective-permute-start | bytes 3145736 | tf_op jit(solution)/shard_map/ppermute | solution.py:349
  526.7 40.5 %collective-permute-start.42 = (bf16[4,1024,1024]{2,1,0:T(8,128)(2,1)}, bf16[4,1024,1024]{2,1,0:T(8,128)(2,1)}, u32[]{:S(2)}, u32[]{:S(2)}) collective-permute-start(bf16[4,1024,1024]{2,1,0:T(8,128)(2,1)} %shard_map.337), channel_id=1, source_target_pairs={{0,4},{4,0},{1,5},{5,1},{2,6},{6,2},{3,7},{7,3},{8,12},{12,8},{9,1... | collective-permute-start | bytes 25165832 | tf_op jit(solution)/shard_map/ppermute | solution.py:345
  526.8 25.6 %collective-permute-start.40 = (bf16[256,2048]{1,0:T(8,128)(2,1)S(1)}, bf16[256,2048]{1,0:T(8,128)(2,1)S(1)}, u32[]{:S(2)}, u32[]{:S(2)}) collective-permute-start(bf16[256,2048]{1,0:T(8,128)(2,1)S(1)} %copy-done.92), channel_id=1, source_target_pairs={{0,16},{16,0},{8,24},{24,8},{1,17},{17,1},{9,25},{25,9},{2,18},{18... | collective-permute-start | bytes 3145736 | tf_op jit(solution)/shard_map/ppermute | solution.py:353
  527.5 25.2 %collective-permute-start.41 = (bf16[256,2048]{1,0:T(8,128)(2,1)S(1)}, bf16[256,2048]{1,0:T(8,128)(2,1)S(1)}, u32[]{:S(2)}, u32[]{:S(2)}) collective-permute-start(bf16[256,2048]{1,0:T(8,128)(2,1)S(1)} %copy-done.91), channel_id=1, source_target_pairs={{0,8},{8,0},{16,24},{24,16},{1,9},{9,1},{17,25},{25,17},{2,10},{10... | collective-permute-start | bytes 3145736 | tf_op jit(solution)/shard_map/ppermute | solution.py:349
  580.5 241.6 %reduce-scatter.3.cloned.1.call-start = ((), (), s32[]{:S(2)}) async-start(), calls=%async_computation.2 | async-start | bytes 5242880 | tf_op jit(solution)/shard_map/reduce_scatter | solution.py:1489
  581.2 390.0 %all-gather.11.cloned.1.call-start = ((), (), s32[]{:S(2)}) async-start(), calls=%async_computation.6 | async-start | bytes 5242880 | tf_op jit(solution)/shard_map/all_gather | solution.py:1559
  584.2 35.1 %collective-permute-start.46 = (bf16[256,2048]{1,0:T(8,128)(2,1)}, bf16[256,2048]{1,0:T(8,128)(2,1)S(1)}, u32[]{:S(2)}, u32[]{:S(2)}) collective-permute-start(bf16[256,2048]{1,0:T(8,128)(2,1)} %get-tuple-element.450), channel_id=1, source_target_pairs={{0,16},{16,0},{8,24},{24,8},{1,17},{17,1},{9,25},{25,9},{2,18},{18... | collective-permute-start | bytes 3145736 | tf_op jit(solution)/shard_map/ppermute | solution.py:353
  585.5 33.7 %collective-permute-start.45 = (bf16[256,2048]{1,0:T(8,128)(2,1)S(1)}, bf16[256,2048]{1,0:T(8,128)(2,1)S(1)}, u32[]{:S(2)}, u32[]{:S(2)}) collective-permute-start(bf16[256,2048]{1,0:T(8,128)(2,1)S(1)} %get-tuple-element.449), channel_id=1, source_target_pairs={{0,8},{8,0},{16,24},{24,16},{1,9},{9,1},{17,25},{25,17},{2,10},{10... | collective-permute-start | bytes 3145736 | tf_op jit(solution)/shard_map/ppermute | solution.py:349
  622.6 28.5 %collective-permute-start.48 = (bf16[256,1024]{1,0:T(8,128)(2,1)}, bf16[256,1024]{1,0:T(8,128)(2,1)}, u32[]{:S(2)}, u32[]{:S(2)}) collective-permute-start(bf16[256,1024]{1,0:T(8,128)(2,1)} %get-tuple-element.463), channel_id=1, source_target_pairs={{0,16},{16,0},{8,24},{24,8},{1,17},{17,1},{9,25},{25,9},{2,18},{18... | collective-permute-start | bytes 1572872 | tf_op jit(solution)/shard_map/ppermute | solution.py:353
  623.3 29.0 %collective-permute-start.47 = (bf16[256,1024]{1,0:T(8,128)(2,1)}, bf16[256,1024]{1,0:T(8,128)(2,1)}, u32[]{:S(2)}, u32[]{:S(2)}) collective-permute-start(bf16[256,1024]{1,0:T(8,128)(2,1)} %get-tuple-element.461), channel_id=1, source_target_pairs={{0,8},{8,0},{16,24},{24,16},{1,9},{9,1},{17,25},{25,17},{2,10},{10... | collective-permute-start | bytes 1572872 | tf_op jit(solution)/shard_map/ppermute | solution.py:349
  624.5 49.7 %collective-permute-start.52 = (bf16[256,2048]{1,0:T(8,128)(2,1)}, bf16[256,2048]{1,0:T(8,128)(2,1)S(1)}, u32[]{:S(2)}, u32[]{:S(2)}) collective-permute-start(bf16[256,2048]{1,0:T(8,128)(2,1)} %add_convert_fusion.8), channel_id=1, source_target_pairs={{0,16},{16,0},{8,24},{24,8},{1,17},{17,1},{9,25},{25,9},{2,18},{18... | collective-permute-start | bytes 3145736 | tf_op jit(solution)/shard_map/ppermute | solution.py:353
  625.9 49.3 %collective-permute-start.51 = (bf16[256,2048]{1,0:T(8,128)(2,1)}, bf16[256,2048]{1,0:T(8,128)(2,1)S(1)}, u32[]{:S(2)}, u32[]{:S(2)}) collective-permute-start(bf16[256,2048]{1,0:T(8,128)(2,1)} %add_convert_fusion.9), channel_id=1, source_target_pairs={{0,8},{8,0},{16,24},{24,16},{1,9},{9,1},{17,25},{25,17},{2,10},{10... | collective-permute-start | bytes 3145736 | tf_op jit(solution)/shard_map/ppermute | solution.py:349
  650.5 19.3 %collective-permute-start.50 = (bf16[256,1024]{1,0:T(8,128)(2,1)S(1)}, bf16[256,1024]{1,0:T(8,128)(2,1)S(1)}, u32[]{:S(2)}, u32[]{:S(2)}) collective-permute-start(bf16[256,1024]{1,0:T(8,128)(2,1)S(1)} %get-tuple-element.469), channel_id=1, source_target_pairs={{0,16},{16,0},{8,24},{24,8},{1,17},{17,1},{9,25},{25,9},{2,18},{18... | collective-permute-start | bytes 1572872 | tf_op jit(solution)/shard_map/ppermute | solution.py:353
  651.1 21.2 %collective-permute-start.49 = (bf16[256,1024]{1,0:T(8,128)(2,1)S(1)}, bf16[256,1024]{1,0:T(8,128)(2,1)S(1)}, u32[]{:S(2)}, u32[]{:S(2)}) collective-permute-start(bf16[256,1024]{1,0:T(8,128)(2,1)S(1)} %get-tuple-element.467), channel_id=1, source_target_pairs={{0,8},{8,0},{16,24},{24,16},{1,9},{9,1},{17,25},{25,17},{2,10},{10... | collective-permute-start | bytes 1572872 | tf_op jit(solution)/shard_map/ppermute | solution.py:349
  672.3 52.4 %collective-permute-start.55 = (bf16[256,2048]{1,0:T(8,128)(2,1)}, bf16[256,2048]{1,0:T(8,128)(2,1)}, u32[]{:S(2)}, u32[]{:S(2)}) collective-permute-start(bf16[256,2048]{1,0:T(8,128)(2,1)} %pad_maximum_fusion.3), channel_id=1, source_target_pairs={{0,8},{8,0},{16,24},{24,16},{1,9},{9,1},{17,25},{25,17},{2,10},{10... | collective-permute-start | bytes 3145736 | tf_op jit(solution)/shard_map/ppermute | solution.py:349
  673.6 51.1 %collective-permute-start.56 = (bf16[256,2048]{1,0:T(8,128)(2,1)}, bf16[256,2048]{1,0:T(8,128)(2,1)}, u32[]{:S(2)}, u32[]{:S(2)}) collective-permute-start(bf16[256,2048]{1,0:T(8,128)(2,1)} %pad_maximum_fusion.4), channel_id=1, source_target_pairs={{0,16},{16,0},{8,24},{24,8},{1,17},{17,1},{9,25},{25,9},{2,18},{18... | collective-permute-start | bytes 3145736 | tf_op jit(solution)/shard_map/ppermute | solution.py:353
  748.7 222.6 %all-gather.9.cloned.1.call-start = ((), (), s32[]{:S(2)}) async-start(), calls=%async_computation.5 | async-start | bytes 5242880 | tf_op jit(solution)/shard_map/all_gather | solution.py:1559
  751.7 37.4 %collective-permute-start.60 = (bf16[256,2048]{1,0:T(8,128)(2,1)}, bf16[256,2048]{1,0:T(8,128)(2,1)S(1)}, u32[]{:S(2)}, u32[]{:S(2)}) collective-permute-start(bf16[256,2048]{1,0:T(8,128)(2,1)} %pad_maximum_fusion.6), channel_id=1, source_target_pairs={{0,16},{16,0},{8,24},{24,8},{1,17},{17,1},{9,25},{25,9},{2,18},{18... | collective-permute-start | bytes 3145736 | tf_op jit(solution)/shard_map/ppermute | solution.py:353
  753.2 36.0 %collective-permute-start.59 = (bf16[256,2048]{1,0:T(8,128)(2,1)}, bf16[256,2048]{1,0:T(8,128)(2,1)S(1)}, u32[]{:S(2)}, u32[]{:S(2)}) collective-permute-start(bf16[256,2048]{1,0:T(8,128)(2,1)} %pad_maximum_fusion.5), channel_id=1, source_target_pairs={{0,8},{8,0},{16,24},{24,16},{1,9},{9,1},{17,25},{25,17},{2,10},{10... | collective-permute-start | bytes 3145736 | tf_op jit(solution)/shard_map/ppermute | solution.py:349
  754.4 73.2 %collective-permute-start.63 = (bf16[256,2048]{1,0:T(8,128)(2,1)}, bf16[256,2048]{1,0:T(8,128)(2,1)}, u32[]{:S(2)}, u32[]{:S(2)}) collective-permute-start(bf16[256,2048]{1,0:T(8,128)(2,1)} %slice.353), channel_id=1, source_target_pairs={{0,16},{16,0},{8,24},{24,8},{1,17},{17,1},{9,25},{25,9},{2,18},{18... | collective-permute-start | bytes 3145736 | tf_op jit(solution)/shard_map/ppermute | solution.py:353
  755.1 102.7 %collective-permute-start.62 = (bf16[256,2048]{1,0:T(8,128)(2,1)}, bf16[256,2048]{1,0:T(8,128)(2,1)}, u32[]{:S(2)}, u32[]{:S(2)}) collective-permute-start(bf16[256,2048]{1,0:T(8,128)(2,1)} %slice.352), channel_id=1, source_target_pairs={{0,8},{8,0},{16,24},{24,16},{1,9},{9,1},{17,25},{25,17},{2,10},{10... | collective-permute-start | bytes 3145736 | tf_op jit(solution)/shard_map/ppermute | solution.py:349
  760.6 61.5 %collective-permute-start.61 = (bf16[256,2048]{1,0:T(8,128)(2,1)}, bf16[256,2048]{1,0:T(8,128)(2,1)}, u32[]{:S(2)}, u32[]{:S(2)}) collective-permute-start(bf16[256,2048]{1,0:T(8,128)(2,1)} %add_convert_fusion.7), channel_id=1, source_target_pairs={{0,3},{1,0},{2,1},{3,2},{4,7},{5,4},{6,5},{7,6},{8,11},{9,8},{10,9... | collective-permute-start | bytes 3145736 | tf_op jit(solution)/shard_map/ppermute | solution.py:363
  819.5 50.2 %collective-permute-start.64 = (bf16[512,2048]{1,0:T(8,128)(2,1)}, bf16[512,2048]{1,0:T(8,128)(2,1)}, u32[]{:S(2)}, u32[]{:S(2)}) collective-permute-start(bf16[512,2048]{1,0:T(8,128)(2,1)} %pad_maximum_fusion.1), channel_id=1, source_target_pairs={{0,4},{4,0},{1,5},{5,1},{2,6},{6,2},{3,7},{7,3},{8,12},{12,8},{9,1... | collective-permute-start | bytes 6291464 | tf_op jit(solution)/shard_map/ppermute | solution.py:345
  820.4 59.6 %collective-permute-start.67 = (bf16[256,2048]{1,0:T(8,128)(2,1)}, bf16[256,2048]{1,0:T(8,128)(2,1)}, u32[]{:S(2)}, u32[]{:S(2)}) collective-permute-start(bf16[256,2048]{1,0:T(8,128)(2,1)} %pad_maximum_fusion.8), channel_id=1, source_target_pairs={{0,16},{16,0},{8,24},{24,8},{1,17},{17,1},{9,25},{25,9},{2,18},{18... | collective-permute-start | bytes 3145736 | tf_op jit(solution)/shard_map/ppermute | solution.py:353
  822.1 60.0 %collective-permute-start.66 = (bf16[256,2048]{1,0:T(8,128)(2,1)}, bf16[256,2048]{1,0:T(8,128)(2,1)}, u32[]{:S(2)}, u32[]{:S(2)}) collective-permute-start(bf16[256,2048]{1,0:T(8,128)(2,1)} %pad_maximum_fusion.7), channel_id=1, source_target_pairs={{0,8},{8,0},{16,24},{24,16},{1,9},{9,1},{17,25},{25,17},{2,10},{10... | collective-permute-start | bytes 3145736 | tf_op jit(solution)/shard_map/ppermute | solution.py:349
  827.6 57.0 %collective-permute-start.65 = (bf16[256,2048]{1,0:T(8,128)(2,1)}, bf16[256,2048]{1,0:T(8,128)(2,1)}, u32[]{:S(2)}, u32[]{:S(2)}) collective-permute-start(bf16[256,2048]{1,0:T(8,128)(2,1)} %add_convert_fusion.5), channel_id=1, source_target_pairs={{0,3},{1,0},{2,1},{3,2},{4,7},{5,4},{6,5},{7,6},{8,11},{9,8},{10,9... | collective-permute-start | bytes 3145736 | tf_op jit(solution)/shard_map/ppermute | solution.py:363
  869.7 28.0 %collective-permute-start.68 = (f32[256,1024]{1,0:T(8,128)}, f32[256,1024]{1,0:T(8,128)S(1)}, u32[]{:S(2)}, u32[]{:S(2)}) collective-permute-start(f32[256,1024]{1,0:T(8,128)} %get-tuple-element.521), channel_id=1, source_target_pairs={{0,4},{4,0},{1,5},{5,1},{2,6},{6,2},{3,7},{7,3},{8,12},{12,8},{9,1... | collective-permute-start | bytes 3145736 | tf_op jit(solution)/shard_map/ppermute | solution.py:345
  869.7 27.8 %collective-permute-start.69 = (f32[256,1024]{1,0:T(8,128)}, f32[256,1024]{1,0:T(8,128)}, u32[]{:S(2)}, u32[]{:S(2)}) collective-permute-start(f32[256,1024]{1,0:T(8,128)} %get-tuple-element.522), channel_id=1, source_target_pairs={{0,4},{4,0},{1,5},{5,1},{2,6},{6,2},{3,7},{7,3},{8,12},{12,8},{9,1... | collective-permute-start | bytes 3145736 | tf_op jit(solution)/shard_map/ppermute | solution.py:345
  880.0 32.8 %collective-permute-start.71 = (bf16[256,2048]{1,0:T(8,128)(2,1)}, bf16[256,2048]{1,0:T(8,128)(2,1)}, u32[]{:S(2)}, u32[]{:S(2)}) collective-permute-start(bf16[256,2048]{1,0:T(8,128)(2,1)} %pad_maximum_fusion.9), channel_id=1, source_target_pairs={{0,8},{8,0},{16,24},{24,16},{1,9},{9,1},{17,25},{25,17},{2,10},{10... | collective-permute-start | bytes 3145736 | tf_op jit(solution)/shard_map/ppermute | solution.py:349
  882.1 37.4 %collective-permute-start.73 = (bf16[256,2048]{1,0:T(8,128)(2,1)}, bf16[256,2048]{1,0:T(8,128)(2,1)}, u32[]{:S(2)}, u32[]{:S(2)}) collective-permute-start(bf16[256,2048]{1,0:T(8,128)(2,1)} %pad_maximum_fusion.10), channel_id=1, source_target_pairs={{0,16},{16,0},{8,24},{24,8},{1,17},{17,1},{9,25},{25,9},{2,18},{18... | collective-permute-start | bytes 3145736 | tf_op jit(solution)/shard_map/ppermute | solution.py:353
  888.6 30.9 %collective-permute-start.74 = (bf16[256,2048]{1,0:T(8,128)(2,1)}, bf16[256,2048]{1,0:T(8,128)(2,1)}, u32[]{:S(2)}, u32[]{:S(2)}) collective-permute-start(bf16[256,2048]{1,0:T(8,128)(2,1)} %add_convert_fusion.3), channel_id=1, source_target_pairs={{0,3},{1,0},{2,1},{3,2},{4,7},{5,4},{6,5},{7,6},{8,11},{9,8},{10,9... | collective-permute-start | bytes 3145736 | tf_op jit(solution)/shard_map/ppermute | solution.py:363
  926.4 26.0 %collective-permute-start.82 = (bf16[256,2048]{1,0:T(8,128)(2,1)S(1)}, bf16[256,2048]{1,0:T(8,128)(2,1)S(1)}, u32[]{:S(2)}, u32[]{:S(2)}) collective-permute-start(bf16[256,2048]{1,0:T(8,128)(2,1)S(1)} %pad_maximum_fusion.11.refs_0_), channel_id=1, source_target_pairs={{0,8},{8,0},{16,24},{24,16},{1,9},{9,1},{17,25},{25,17},{2,10},{10... | collective-permute-start | bytes 3145736 | tf_op jit(solution)/shard_map/ppermute | solution.py:349
  931.2 25.0 %collective-permute-start.81 = (bf16[256,2048]{1,0:T(8,128)(2,1)S(1)}, bf16[256,2048]{1,0:T(8,128)(2,1)S(1)}, u32[]{:S(2)}, u32[]{:S(2)}) collective-permute-start(bf16[256,2048]{1,0:T(8,128)(2,1)S(1)} %pad_maximum_fusion.11.refs_0_), channel_id=1, source_target_pairs={{0,16},{16,0},{8,24},{24,8},{1,17},{17,1},{9,25},{25,9},{2,18},{18... | collective-permute-start | bytes 3145736 | tf_op jit(solution)/shard_map/ppermute | solution.py:353
  957.1 24.4 %collective-permute-start.83 = (bf16[128,2048]{1,0:T(8,128)(2,1)}, bf16[128,2048]{1,0:T(8,128)(2,1)}, u32[]{:S(2)}, u32[]{:S(2)}) collective-permute-start(bf16[128,2048]{1,0:T(8,128)(2,1)} %slice.463), channel_id=1, source_target_pairs={{0,16},{16,0},{8,24},{24,8},{1,17},{17,1},{9,25},{25,9},{2,18},{18... | collective-permute-start | bytes 1572872 | tf_op jit(solution)/shard_map/ppermute | solution.py:353
  958.7 22.7 %collective-permute-start.84 = (bf16[128,2048]{1,0:T(8,128)(2,1)}, bf16[128,2048]{1,0:T(8,128)(2,1)}, u32[]{:S(2)}, u32[]{:S(2)}) collective-permute-start(bf16[128,2048]{1,0:T(8,128)(2,1)} %slice.462), channel_id=1, source_target_pairs={{0,8},{8,0},{16,24},{24,16},{1,9},{9,1},{17,25},{25,17},{2,10},{10... | collective-permute-start | bytes 1572872 | tf_op jit(solution)/shard_map/ppermute | solution.py:349
  (147 other events, 1930.2 us)
Sparse Core Ops, SparseCore 0:
  39.4 208.9 all-gather.6
  580.6 101.1 reduce-scatter.4
  684.2 77.2 reduce-scatter.2
  763.2 90.6 all-gather.10
  855.6 76.8 all-gather.8

commit v10 on v9

--- a/solution.py
+++ b/solution.py
@@ -1486,7 +1486,8 @@
     for part in range(2):
         span = slice(part * width // 2, (part + 1) * width // 2)
         total = order.tie(add_rounded(ff_mine[:, span], ff_other[:, span]))
-        ff_grads.append(lax.psum_scatter(total, "col", scatter_dimension=0, tiled=False))
+        total = lax.psum_scatter(total, "col", scatter_dimension=0, tiled=False)
+        ff_grads.append(lax.all_gather(total, "dp"))
 
     down_via_x, down_via_y = plane.both(top(down_parts[3]), bottom(down_parts[3]), True)
     head_grad = order.run(head_grads, grad_rows, own_parts, other_rows)
@@ -1556,7 +1557,6 @@
     head_weights(0)
     vias[0] = first_messages(0)
     came[1] = second_messages(1, vias[1])
-    ff_grads = [lax.all_gather(after(g, *order.tokens), "dp") for g in ff_grads]
     total = column.send(step_down, group_total(3, came[3], None))
     order.tokens += came[2]
     back_rows = order.run(sum_rows, head_rows, own_parts, other_rows, 0)

time: 1010 us -> 996 us (0.986)
  starting transfers between devices: 189 us -> 169 us
  waiting for transfers between devices: 221 us -> 233 us
    ppermute x3, starting transfers between devices: 67.6 us -> 51.5 us  [step_down(): lax.ppermute(values, 'col', [(i, (i - 1) % count) for i in range(count)])]
  transfers between devices with their start and end apart: 90 -> 90, of which waited for: 28 -> 29; matrix products, arithmetic and copies ran while one was open for 12% -> 12% of each run, Pallas kernels for 38% -> 38%
where the time goes in v10:
time: 996 us; the launch traced here: 987 us
  Pallas kernels  419 us (42%)
  waiting for transfers between devices  233 us (23%)
  starting transfers between devices  169 us (17%)
  local copies, waits for them, and re-layouts  92.5 us (9%)
  other arithmetic  58.1 us (6%)
  between operations  15.8 us (2%)
    pallas_call x4, Pallas kernels, ffn_rows_of(): pl.pallas_call(ffn_kernel, grid_spec=pltpu.PrefetchScalarGridSpec(num_sca...  102 us
    ppermute x29, waiting for transfers between devices, step_y(): return lax.ppermute(values, 'dp', [(0, 2), (2, 0), (1, 3), (3, 1)])  90 us
    ppermute x3, waiting for transfers between devices, step_up(): lax.ppermute(values, 'col', [(i, (i + 1) % count) for i in range(count)])  82.7 us
    pallas_call x2, Pallas kernels, weight_products(): pl.pallas_call(functools.partial(weight_products_kernel, count), grid=(ri...  58 us
    ppermute x3, starting transfers between devices, step_down(): lax.ppermute(values, 'col', [(i, (i - 1) % count) for i in range(count)])  51.5 us
    pallas_call x4, Pallas kernels, local_backward(): pl.pallas_call(functools.partial(local_backward_kernel, min(512, length))...  50.3 us
    ppermute x29, waiting for transfers between devices, step_x(): return lax.ppermute(values, 'dp', [(0, 1), (1, 0), (2, 3), (3, 2)])  49.1 us
    unnamed x256, local copies, waits for them, and re-layouts  36.4 us
  transfers between devices with their start and end apart: 90, of which 29 were waited for; matrix products, arithmetic and copies ran while one was open for 12% of the time, Pallas kernels for 38%

profile of v10, /device:TPU:0, one launch (start us, length us, event | category | flops | bytes accessed | tf_op | source)
XLA Modules:
  0.0 986.9 jit_solution(17232068664764755947)
XLA Ops:
  7.3 3.2 constant_dynamic-slice_fusion.1
  43.0 36.7 %collective-permute-done.6.refs_0_ = bf16[512,1024]{1,0:T(8,128)(2,1)} collective-permute-done((bf16[512,1024]{1,0:T(8,128)(2,1)}, bf16[512,1024]{1,0:T(8,128)(2,1)}, u32[]{:S(2)}, u32[]{:S(2)}) %collective-permute-start.6) | collective-permute-done | bytes 1048608 | tf_op jit(solution)/shard_map/ppermute | solution.py:358
  84.4 3.6 shard_map.316
  91.5 6.1 collective-permute-start.15
  97.8 6.7 shard_map.317
  104.5 9.2 collective-permute-done.12.refs_2_
  116.2 6.1 shard_map.318.query_ref.key_ref.value_ref
  122.4 6.5 shard_map.319.refs_0_.refs_5_
  130.9 21.1 %collective-permute-done.15.refs_0_ = bf16[512,1024]{1,0:T(8,128)(2,1)S(1)} collective-permute-done((bf16[512,1024]{1,0:T(8,128)(2,1)}, bf16[512,1024]{1,0:T(8,128)(2,1)S(1)}, u32[]{:S(2)}, u32[]{:S(2)}) %collective-permute-start.15) | collective-permute-done | bytes 1048608 | tf_op jit(solution)/shard_map/ppermute | solution.py:358
  152.9 23.8 %collective-permute-start.20 = (bf16[512,1024]{1,0:T(8,128)(2,1)S(1)}, bf16[512,1024]{1,0:T(8,128)(2,1)S(1)}, u32[]{:S(2)}, u32[]{:S(2)}) collective-permute-start(bf16[512,1024]{1,0:T(8,128)(2,1)S(1)} %collective-permute-done.15.refs_0_), channel_id=1, source_target_pairs={{0,1},{1,2},{2,3},{3,0},{4,5},{5,6},{6,7},{7,4},{8,9},{9,10},{10,1... | collective-permute-start | bytes 3145736 | tf_op jit(solution)/shard_map/ppermute | solution.py:358
  176.7 3.8 shard_map.320
  183.8 5.6 shard_map.321.query_ref.key_ref.value_ref
  189.4 6.5 shard_map.322.refs_1_.refs_5_
  197.2 24.9 %collective-permute-done.20.refs_0_ = bf16[512,1024]{1,0:T(8,128)(2,1)S(1)} collective-permute-done((bf16[512,1024]{1,0:T(8,128)(2,1)S(1)}, bf16[512,1024]{1,0:T(8,128)(2,1)S(1)}, u32[]{:S(2)}, u32[]{:S(2)}) %collective-permute-start.20) | collective-permute-done | bytes 1048608 | tf_op jit(solution)/shard_map/ppermute | solution.py:358
  231.2 5.4 shard_map.324.query_ref.key_ref.value_ref
  236.7 6.5 shard_map.325.refs_2_.refs_5_
  250.4 8.8 collective-permute-done.24.refs_4_
  263.8 7.6 shard_map.327.refs_3_
  273.4 5.5 shard_map.328.query_ref.key_ref.value_ref
  278.9 6.7 shard_map.329.refs_0_.refs_5_
  285.6 6.5 collective-permute-done.28
  294.3 6.3 shard_map.330.rows_ref
  309.3 6.5 shard_map.331
  315.8 3.7 collective-permute-done.32
  331.2 25.4 %shard_map.332 = (bf16[512,4096]{1,0:T(8,128)(2,1)}, f32[4,1,512]{2,1,0:T(1,128)S(1)}, bf16[512,2048]{1,0:T(8,128)(2,1)S(1)}, bf16[512,2048]{1,0:T(8,128)(2,1)S(1)}) custom-call(s32[3]{0:T(128)S(1)} %pad_add_fusion.index_ref.refs_0_, bf16[512,2048]{1,0:T(8,128)(2,1)} %get-tuple-element.424.refs_0_.refs_1_, ...), custom_call_target="tpu_custom_call" | custom-call | flops 1717986944 | bytes 5033164 | tf_op jit(solution)/shard_map/pallas_call | solution.py:621
  356.7 10.5 %collective-permute-done.33.refs_0_.refs_1_.refs_2_ = bf16[512,2048]{1,0:T(8,128)(2,1)} collective-permute-done((bf16[512,2048]{1,0:T(8,128)(2,1)}, bf16[512,2048]{1,0:T(8,128)(2,1)}, u32[]{:S(2)}, u32[]{:S(2)}) %collective-permute-start.33) | collective-permute-done | bytes 2097184 | tf_op jit(solution)/shard_map/ppermute | solution.py:353
  378.0 25.6 %shard_map.333 = (bf16[512,4096]{1,0:T(8,128)(2,1)}, f32[4,1,512]{2,1,0:T(1,128)S(1)}, bf16[512,2048]{1,0:T(8,128)(2,1)S(1)}, bf16[512,2048]{1,0:T(8,128)(2,1)S(1)}) custom-call(s32[3]{0:T(128)S(1)} %pad_add_fusion.index_ref.refs_0_, bf16[512,2048]{1,0:T(8,128)(2,1)} %collective-permute-done.31.refs_0_.refs_1_, ...), custom_call_target="tpu_custom_call" | custom-call | flops 1717986944 | bytes 5033164 | tf_op jit(solution)/shard_map/pallas_call | solution.py:621
  405.5 25.3 %shard_map.334 = (bf16[512,4096]{1,0:T(8,128)(2,1)}, f32[4,1,512]{2,1,0:T(1,128)S(1)}, bf16[512,2048]{1,0:T(8,128)(2,1)S(1)}, bf16[512,2048]{1,0:T(8,128)(2,1)S(1)}) custom-call(s32[3]{0:T(128)S(1)} %pad_add_fusion.index_ref.refs_0_, bf16[512,2048]{1,0:T(8,128)(2,1)} %collective-permute-done.33.refs_0_.refs_1_.refs_2_, ...), custom_call_target="tpu_custom_call" | custom-call | flops 1717986944 | bytes 5033164 | tf_op jit(solution)/shard_map/pallas_call | solution.py:621
  434.9 25.4 %shard_map.335 = (bf16[512,4096]{1,0:T(8,128)(2,1)}, f32[4,1,512]{2,1,0:T(1,128)S(1)}, bf16[512,2048]{1,0:T(8,128)(2,1)S(1)}, bf16[512,2048]{1,0:T(8,128)(2,1)S(1)}) custom-call(s32[3]{0:T(128)S(1)} %pad_add_fusion.index_ref.refs_0_, bf16[512,2048]{1,0:T(8,128)(2,1)} %constant_dynamic-update-slice_fusion.refs_0_.refs_1_.refs_3_, ...), custom_call_target="tpu_custom_call" | custom-call | flops 1717986944 | bytes 5033164 | tf_op jit(solution)/shard_map/pallas_call | solution.py:621
  465.0 29.0 %shard_map.336 = bf16[4,1024,1024]{2,1,0:T(8,128)(2,1)} custom-call(bf16[512,2048]{1,0:T(8,128)(2,1)} %get-tuple-element.424.refs_0_.refs_1_, bf16[512,2048]{1,0:T(8,128)(2,1)} %collective-permute-done.31.refs_0_.refs_1_, bf16[512,2048]{1,0:T(8,128)(2,1)} %collective-permute-done.33.refs_0_.refs_1_.refs_2_, ...), custom_call_target="tpu_custom_call" | custom-call | flops 1717986944 | bytes 6710886 | tf_op jit(solution)/shard_map/pallas_call | solution.py:667
  494.0 3.6 add_convert_fusion.10
  497.6 29.1 %shard_map.337 = bf16[4,1024,1024]{2,1,0:T(8,128)(2,1)} custom-call(bf16[512,2048]{1,0:T(8,128)(2,1)} %get-tuple-element.424.refs_0_.refs_1_, bf16[512,2048]{1,0:T(8,128)(2,1)} %collective-permute-done.31.refs_0_.refs_1_, bf16[512,2048]{1,0:T(8,128)(2,1)} %collective-permute-done.33.refs_0_.refs_1_.refs_2_, ...), custom_call_target="tpu_custom_call" | custom-call | flops 1717986944 | bytes 6710886 | tf_op jit(solution)/shard_map/pallas_call | solution.py:667
  530.6 21.7 %collective-permute-done.40.refs_2_ = bf16[256,2048]{1,0:T(8,128)(2,1)S(1)} collective-permute-done((bf16[256,2048]{1,0:T(8,128)(2,1)S(1)}, bf16[256,2048]{1,0:T(8,128)(2,1)S(1)}, u32[]{:S(2)}, u32[]{:S(2)}) %collective-permute-start.40) | collective-permute-done | bytes 1048608 | tf_op jit(solution)/shard_map/ppermute | solution.py:353
  552.7 12.1 %shard_map.338 = (f32[512,2048]{1,0:T(8,128)}, bf16[512,2048]{1,0:T(8,128)(2,1)}, bf16[512,2048]{1,0:T(8,128)(2,1)}, f32[8,2048]{1,0:T(8,128)S(1)}) custom-call(s32[3]{0:T(128)S(1)} %pad_add_fusion.index_ref.refs_0_, bf16[512,2048]{1,0:T(8,128)(2,1)} %copy-done.35, bf16[256,2048]{1,0:T(8,128)(2,1)S(1)} %collective-permute-done.36.refs_1_, ...), custom_call_target="tpu_custom_call" | custom-call | bytes 2516582 | tf_op jit(solution)/shard_map/pallas_call | solution.py:1048
  567.1 10.1 %add_convert_fusion = (bf16[4,512,1024]{2,1,0:T(8,128)(2,1)}, bf16[4,512,1024]{2,1,0:T(8,128)(2,1)}) fusion(bf16[4,1024,1024]{2,1,0:T(8,128)(2,1)} %collective-permute-done.42, bf16[4,1024,1024]{2,1,0:T(8,128)(2,1)} %shard_map.336), kind=kLoop, calls=%fused_computation.2 | loop fusion | flops 16777216 | bytes 25165824 | tf_op jit(solution)/shard_map/convert_element_type | solution.py:418
  582.0 3.3 fusion.17
  587.7 8.0 shard_map.340.grad_ref
  595.7 12.4 %shard_map.341.refs_4_.refs_3_ = bf16[1024,768]{1,0:T(8,128)(2,1)S(1)} custom-call(s32[1,1024]{1,0:T(1,128)S(1)} %bitcast.54, bf16[1024,768]{1,0:T(8,128)(2,1)S(1)} %shard_map.328.query_ref.key_ref.value_ref, bf16[1024,1024]{1,0:T(8,128)(2,1)S(1)} %shard_map.340.grad_ref, bf16[1024,768]{1,0:T(8,128)(2,1)S(1)} %shard_map.328.query_ref.key_ref.value_ref, ...), custom_call_target="tpu_custom_call" | custom-call | flops 858993472 | bytes 629145 | tf_op jit(solution)/shard_map/pallas_call | solution.py:544
  608.1 9.0 shard_map.342
  628.9 12.5 %shard_map.343.refs_4_.refs_2_ = bf16[1024,768]{1,0:T(8,128)(2,1)S(1)} custom-call(s32[1,1024]{1,0:T(1,128)S(1)} %bitcast.55, bf16[1024,768]{1,0:T(8,128)(2,1)S(1)} %copy-done.5, bf16[1024,1024]{1,0:T(8,128)(2,1)S(1)} %shard_map.340.grad_ref, bf16[1024,768]{1,0:T(8,128)(2,1)S(1)} %copy-done.5, bf16[1024,768]{1,0:T(8,128)(2,1)S(1)} %copy-done.5), custom_call_target="tpu_custom_call" | custom-call | flops 858993472 | bytes 629145 | tf_op jit(solution)/shard_map/pallas_call | solution.py:544
  641.5 8.3 shard_map.344
  660.4 13.3 %collective-permute-done.50 = bf16[256,1024]{1,0:T(8,128)(2,1)S(1)} collective-permute-done((bf16[256,1024]{1,0:T(8,128)(2,1)S(1)}, bf16[256,1024]{1,0:T(8,128)(2,1)S(1)}, u32[]{:S(2)}, u32[]{:S(2)}) %collective-permute-start.50) | collective-permute-done | bytes 524320 | tf_op jit(solution)/shard_map/ppermute | solution.py:353
  677.6 12.6 %shard_map.345.refs_4_.refs_1_ = bf16[1024,768]{1,0:T(8,128)(2,1)S(1)} custom-call(s32[1,1024]{1,0:T(1,128)S(1)} %bitcast.56, bf16[1024,768]{1,0:T(8,128)(2,1)S(1)} %copy-done.3, bf16[1024,1024]{1,0:T(8,128)(2,1)S(1)} %shard_map.340.grad_ref, bf16[1024,768]{1,0:T(8,128)(2,1)S(1)} %copy-done.3, bf16[1024,768]{1,0:T(8,128)(2,1)S(1)} %copy-done.3), custom_call_target="tpu_custom_call" | custom-call | flops 858993472 | bytes 629145 | tf_op jit(solution)/shard_map/pallas_call | solution.py:544
  690.3 8.6 shard_map.346
  709.5 18.6 %collective-permute-done.54 = bf16[256,1024]{1,0:T(8,128)(2,1)S(1)} collective-permute-done((bf16[256,1024]{1,0:T(8,128)(2,1)S(1)}, bf16[256,1024]{1,0:T(8,128)(2,1)S(1)}, u32[]{:S(2)}, u32[]{:S(2)}) %collective-permute-start.54) | collective-permute-done | bytes 524320 | tf_op jit(solution)/shard_map/ppermute | solution.py:353
  730.0 12.8 %shard_map.347.refs_4_.refs_0_ = bf16[1024,768]{1,0:T(8,128)(2,1)S(1)} custom-call(s32[1,1024]{1,0:T(1,128)S(1)} %bitcast.57, bf16[1024,768]{1,0:T(8,128)(2,1)S(1)} %copy-done.1, bf16[1024,1024]{1,0:T(8,128)(2,1)S(1)} %copy-done.7, bf16[1024,768]{1,0:T(8,128)(2,1)S(1)} %copy-done.1, bf16[1024,768]{1,0:T(8,128)(2,1)S(1)} %copy-done.1), custom_call_target="tpu_custom_call" | custom-call | flops 858993472 | bytes 629145 | tf_op jit(solution)/shard_map/pallas_call | solution.py:544
  742.8 8.3 shard_map.348
  760.2 5.6 collective-permute-done.58
  769.9 36.7 %collective-permute-start.61 = (bf16[256,2048]{1,0:T(8,128)(2,1)}, bf16[256,2048]{1,0:T(8,128)(2,1)}, u32[]{:S(2)}, u32[]{:S(2)}) collective-permute-start(bf16[256,2048]{1,0:T(8,128)(2,1)} %add_convert_fusion.7), channel_id=1, source_target_pairs={{0,3},{1,0},{2,1},{3,2},{4,7},{5,4},{6,5},{7,6},{8,11},{9,8},{10,9... | collective-permute-start | bytes 3145736 | tf_op jit(solution)/shard_map/ppermute | solution.py:363
  806.6 21.0 %shard_map.349.refs_0_ = f32[1024,2048]{1,0:T(8,128)} custom-call(bf16[1024,768]{1,0:T(8,128)(2,1)S(1)} %shard_map.347.refs_4_.refs_0_, bf16[1024,768]{1,0:T(8,128)(2,1)S(1)} %shard_map.345.refs_4_.refs_1_, bf16[1024,768]{1,0:T(8,128)(2,1)S(1)} %shard_map.343.refs_4_.refs_2_, bf16[1024,768]{1,0:T(8,128)(2,1)} %copy-done.26, ...), custom_call_target="tpu_custom_call" | custom-call | flops 1288490240 | bytes 838860 | tf_op jit(solution)/shard_map/pallas_call | solution.py:862
  839.8 3.6 add_convert_fusion.5
  843.9 8.4 shard_map.350
  856.0 8.7 shard_map.351
  868.9 4.0 add_convert_fusion.3
  872.9 14.4 %collective-permute-start.74 = (bf16[256,2048]{1,0:T(8,128)(2,1)}, bf16[256,2048]{1,0:T(8,128)(2,1)}, u32[]{:S(2)}, u32[]{:S(2)}) collective-permute-start(bf16[256,2048]{1,0:T(8,128)(2,1)} %add_convert_fusion.3), channel_id=1, source_target_pairs={{0,3},{1,0},{2,1},{3,2},{4,7},{5,4},{6,5},{7,6},{8,11},{9,8},{10,9... | collective-permute-start | bytes 3145736 | tf_op jit(solution)/shard_map/ppermute | solution.py:363
  887.4 4.4 shard_map.352
  891.9 12.9 %collective-permute-done.71 = bf16[256,2048]{1,0:T(8,128)(2,1)} collective-permute-done((bf16[256,2048]{1,0:T(8,128)(2,1)}, bf16[256,2048]{1,0:T(8,128)(2,1)}, u32[]{:S(2)}, u32[]{:S(2)}) %collective-permute-start.71) | collective-permute-done | bytes 1048608 | tf_op jit(solution)/shard_map/ppermute | solution.py:349
  905.9 5.3 collective-permute-done.72
  917.4 3.8 collective-permute-done.76
  921.8 5.6 collective-permute-start.77
  932.9 11.9 %collective-permute-done.82.refs_1_ = bf16[256,2048]{1,0:T(8,128)(2,1)S(1)} collective-permute-done((bf16[256,2048]{1,0:T(8,128)(2,1)S(1)}, bf16[256,2048]{1,0:T(8,128)(2,1)S(1)}, u32[]{:S(2)}, u32[]{:S(2)}) %collective-permute-start.82) | collective-permute-done | bytes 1048608 | tf_op jit(solution)/shard_map/ppermute | solution.py:349
  948.8 11.2 %collective-permute-start.80 = (f32[20480]{0:T(1024)S(1)}, f32[20480]{0:T(1024)S(1)}, u32[]{:S(2)}, u32[]{:S(2)}) collective-permute-start(f32[20480]{0:T(1024)S(1)} %add.206), channel_id=1, source_target_pairs={{0,2},{1,3},{2,0},{3,1},{4,6},{5,7},{6,4},{7,5},{8,10},{9,11},{10,... | collective-permute-start | bytes 245768 | tf_op jit(solution)/shard_map/ppermute | solution.py:1606
  966.6 8.0 shard_map.354
  974.7 5.5 shard_map.355
  (559 shorter events, 227.0 us)
Async XLA Ops:
  7.2 299.4 %all-gather.9.cloned.1.call-start = ((), (), s32[]{:S(2)}) async-start(), calls=%async_computation.6 | async-start | bytes 18874368 | tf_op jit(solution)/shard_map/all_gather | solution.py:1358
  10.5 18.7 %collective-permute-start.4 = (bf16[512,1024]{1,0:T(8,128)(2,1)}, bf16[512,1024]{1,0:T(8,128)(2,1)}, u32[]{:S(2)}, u32[]{:S(2)}) collective-permute-start(bf16[512,1024]{1,0:T(8,128)(2,1)} %get-tuple-element.618), channel_id=1, source_target_pairs={{0,4},{4,0},{1,5},{5,1},{2,6},{6,2},{3,7},{7,3},{8,12},{12,8},{9,1... | collective-permute-start | bytes 3145736 | tf_op jit(solution)/shard_map/ppermute | solution.py:345
  39.2 663.5 %reduce-scatter.5.cloned.1.call-start = ((), (), s32[]{:S(2)}) async-start(), calls=%async_computation.4 | async-start | bytes 5242880 | tf_op jit(solution)/shard_map/reduce_scatter | solution.py:1489
  39.3 40.4 %collective-permute-start.6 = (bf16[512,1024]{1,0:T(8,128)(2,1)}, bf16[512,1024]{1,0:T(8,128)(2,1)}, u32[]{:S(2)}, u32[]{:S(2)}) collective-permute-start(bf16[512,1024]{1,0:T(8,128)(2,1)} %pad_maximum_fusion.2), channel_id=1, source_target_pairs={{0,1},{1,2},{2,3},{3,0},{4,5},{5,6},{6,7},{7,4},{8,9},{9,10},{10,1... | collective-permute-start | bytes 3145736 | tf_op jit(solution)/shard_map/ppermute | solution.py:358
  40.0 39.7 %collective-permute-start.7 = (bf16[256,2048]{1,0:T(8,128)(2,1)}, bf16[256,2048]{1,0:T(8,128)(2,1)S(1)}, u32[]{:S(2)}, u32[]{:S(2)}) collective-permute-start(bf16[256,2048]{1,0:T(8,128)(2,1)} %get-tuple-element.302), channel_id=1, source_target_pairs={{0,8},{8,0},{16,24},{24,16},{1,9},{9,1},{17,25},{25,17},{2,10},{10... | collective-permute-start | bytes 3145736 | tf_op jit(solution)/shard_map/ppermute | solution.py:349
  41.5 39.2 %collective-permute-start.8 = (bf16[256,2048]{1,0:T(8,128)(2,1)}, bf16[256,2048]{1,0:T(8,128)(2,1)}, u32[]{:S(2)}, u32[]{:S(2)}) collective-permute-start(bf16[256,2048]{1,0:T(8,128)(2,1)} %get-tuple-element.302), channel_id=1, source_target_pairs={{0,16},{16,0},{8,24},{24,8},{1,17},{17,1},{9,25},{25,9},{2,18},{18... | collective-permute-start | bytes 3145736 | tf_op jit(solution)/shard_map/ppermute | solution.py:353
  88.0 28.3 %collective-permute-start.10 = (bf16[1024,1024]{1,0:T(8,128)(2,1)}, bf16[1024,1024]{1,0:T(8,128)(2,1)}, u32[]{:S(2)}, u32[]{:S(2)}) collective-permute-start(bf16[1024,1024]{1,0:T(8,128)(2,1)} %get-tuple-element.313), channel_id=1, source_target_pairs={{0,4},{4,0},{1,5},{5,1},{2,6},{6,2},{3,7},{7,3},{8,12},{12,8},{9,1... | collective-permute-start | bytes 6291464 | tf_op jit(solution)/shard_map/ppermute | solution.py:345
  88.0 25.8 %collective-permute-start.12 = (bf16[512,1024]{1,0:T(8,128)(2,1)}, bf16[512,1024]{1,0:T(8,128)(2,1)S(1)}, u32[]{:S(2)}, u32[]{:S(2)}) collective-permute-start(bf16[512,1024]{1,0:T(8,128)(2,1)} %collective-permute-done.6.refs_0_), channel_id=1, source_target_pairs={{0,16},{16,0},{8,24},{24,8},{1,17},{17,1},{9,25},{25,9},{2,18},{18... | collective-permute-start | bytes 3145736 | tf_op jit(solution)/shard_map/ppermute | solution.py:353
  89.5 25.6 %collective-permute-start.11 = (bf16[512,1024]{1,0:T(8,128)(2,1)}, bf16[512,1024]{1,0:T(8,128)(2,1)}, u32[]{:S(2)}, u32[]{:S(2)}) collective-permute-start(bf16[512,1024]{1,0:T(8,128)(2,1)} %collective-permute-done.6.refs_0_), channel_id=1, source_target_pairs={{0,8},{8,0},{16,24},{24,16},{1,9},{9,1},{17,25},{25,17},{2,10},{10... | collective-permute-start | bytes 3145736 | tf_op jit(solution)/shard_map/ppermute | solution.py:349
  91.5 60.4 %collective-permute-start.15 = (bf16[512,1024]{1,0:T(8,128)(2,1)}, bf16[512,1024]{1,0:T(8,128)(2,1)S(1)}, u32[]{:S(2)}, u32[]{:S(2)}) collective-permute-start(bf16[512,1024]{1,0:T(8,128)(2,1)} %collective-permute-done.6.refs_0_), channel_id=1, source_target_pairs={{0,1},{1,2},{2,3},{3,0},{4,5},{5,6},{6,7},{7,4},{8,9},{9,10},{10,1... | collective-permute-start | bytes 3145736 | tf_op jit(solution)/shard_map/ppermute | solution.py:358
  128.9 23.0 %collective-permute-start.13 = (bf16[256,1024]{1,0:T(8,128)(2,1)S(1)}, bf16[256,1024]{1,0:T(8,128)(2,1)S(1)}, u32[]{:S(2)}, u32[]{:S(2)}) collective-permute-start(bf16[256,1024]{1,0:T(8,128)(2,1)S(1)} %slice.429), channel_id=1, source_target_pairs={{0,16},{16,0},{8,24},{24,8},{1,17},{17,1},{9,25},{25,9},{2,18},{18... | collective-permute-start | bytes 1572872 | tf_op jit(solution)/shard_map/ppermute | solution.py:353
  129.4 22.6 %collective-permute-start.14 = (bf16[256,1024]{1,0:T(8,128)(2,1)S(1)}, bf16[256,1024]{1,0:T(8,128)(2,1)S(1)}, u32[]{:S(2)}, u32[]{:S(2)}) collective-permute-start(bf16[256,1024]{1,0:T(8,128)(2,1)S(1)} %slice.430), channel_id=1, source_target_pairs={{0,8},{8,0},{16,24},{24,16},{1,9},{9,1},{17,25},{25,17},{2,10},{10... | collective-permute-start | bytes 1572872 | tf_op jit(solution)/shard_map/ppermute | solution.py:349
  152.0 44.0 %collective-permute-start.17 = (bf16[512,1024]{1,0:T(8,128)(2,1)S(1)}, bf16[512,1024]{1,0:T(8,128)(2,1)S(1)}, u32[]{:S(2)}, u32[]{:S(2)}) collective-permute-start(bf16[512,1024]{1,0:T(8,128)(2,1)S(1)} %collective-permute-done.15.refs_0_), channel_id=1, source_target_pairs={{0,16},{16,0},{8,24},{24,8},{1,17},{17,1},{9,25},{25,9},{2,18},{18... | collective-permute-start | bytes 3145736 | tf_op jit(solution)/shard_map/ppermute | solution.py:353
  152.4 43.7 %collective-permute-start.16 = (bf16[512,1024]{1,0:T(8,128)(2,1)S(1)}, bf16[512,1024]{1,0:T(8,128)(2,1)S(1)}, u32[]{:S(2)}, u32[]{:S(2)}) collective-permute-start(bf16[512,1024]{1,0:T(8,128)(2,1)S(1)} %collective-permute-done.15.refs_0_), channel_id=1, source_target_pairs={{0,8},{8,0},{16,24},{24,16},{1,9},{9,1},{17,25},{25,17},{2,10},{10... | collective-permute-start | bytes 3145736 | tf_op jit(solution)/shard_map/ppermute | solution.py:349
  152.9 69.2 %collective-permute-start.20 = (bf16[512,1024]{1,0:T(8,128)(2,1)S(1)}, bf16[512,1024]{1,0:T(8,128)(2,1)S(1)}, u32[]{:S(2)}, u32[]{:S(2)}) collective-permute-start(bf16[512,1024]{1,0:T(8,128)(2,1)S(1)} %collective-permute-done.15.refs_0_), channel_id=1, source_target_pairs={{0,1},{1,2},{2,3},{3,0},{4,5},{5,6},{6,7},{7,4},{8,9},{9,10},{10,1... | collective-permute-start | bytes 3145736 | tf_op jit(solution)/shard_map/ppermute | solution.py:358
  196.1 26.0 %collective-permute-start.18 = (bf16[256,1024]{1,0:T(8,128)(2,1)S(1)}, bf16[256,1024]{1,0:T(8,128)(2,1)S(1)}, u32[]{:S(2)}, u32[]{:S(2)}) collective-permute-start(bf16[256,1024]{1,0:T(8,128)(2,1)S(1)} %slice.432), channel_id=1, source_target_pairs={{0,16},{16,0},{8,24},{24,8},{1,17},{17,1},{9,25},{25,9},{2,18},{18... | collective-permute-start | bytes 1572872 | tf_op jit(solution)/shard_map/ppermute | solution.py:353
  196.6 25.5 %collective-permute-start.19 = (bf16[256,1024]{1,0:T(8,128)(2,1)S(1)}, bf16[256,1024]{1,0:T(8,128)(2,1)S(1)}, u32[]{:S(2)}, u32[]{:S(2)}) collective-permute-start(bf16[256,1024]{1,0:T(8,128)(2,1)S(1)} %slice.433), channel_id=1, source_target_pairs={{0,8},{8,0},{16,24},{24,16},{1,9},{9,1},{17,25},{25,17},{2,10},{10... | collective-permute-start | bytes 1572872 | tf_op jit(solution)/shard_map/ppermute | solution.py:349
  222.1 23.7 %collective-permute-start.22 = (bf16[512,1024]{1,0:T(8,128)(2,1)S(1)}, bf16[512,1024]{1,0:T(8,128)(2,1)S(1)}, u32[]{:S(2)}, u32[]{:S(2)}) collective-permute-start(bf16[512,1024]{1,0:T(8,128)(2,1)S(1)} %collective-permute-done.20.refs_0_), channel_id=1, source_target_pairs={{0,16},{16,0},{8,24},{24,8},{1,17},{17,1},{9,25},{25,9},{2,18},{18... | collective-permute-start | bytes 3145736 | tf_op jit(solution)/shard_map/ppermute | solution.py:353
  223.7 23.4 %collective-permute-start.21 = (bf16[512,1024]{1,0:T(8,128)(2,1)S(1)}, bf16[512,1024]{1,0:T(8,128)(2,1)S(1)}, u32[]{:S(2)}, u32[]{:S(2)}) collective-permute-start(bf16[512,1024]{1,0:T(8,128)(2,1)S(1)} %collective-permute-done.20.refs_0_), channel_id=1, source_target_pairs={{0,8},{8,0},{16,24},{24,16},{1,9},{9,1},{17,25},{25,17},{2,10},{10... | collective-permute-start | bytes 3145736 | tf_op jit(solution)/shard_map/ppermute | solution.py:349
  271.3 20.8 %collective-permute-start.28 = (bf16[256,2048]{1,0:T(8,128)(2,1)S(1)}, bf16[256,2048]{1,0:T(8,128)(2,1)S(1)}, u32[]{:S(2)}, u32[]{:S(2)}) collective-permute-start(bf16[256,2048]{1,0:T(8,128)(2,1)S(1)} %copy-done.83), channel_id=1, source_target_pairs={{0,8},{8,0},{16,24},{24,16},{1,9},{9,1},{17,25},{25,17},{2,10},{10... | collective-permute-start | bytes 3145736 | tf_op jit(solution)/shard_map/ppermute | solution.py:349
  272.3 21.1 %collective-permute-start.27 = (bf16[256,2048]{1,0:T(8,128)(2,1)S(1)}, bf16[256,2048]{1,0:T(8,128)(2,1)S(1)}, u32[]{:S(2)}, u32[]{:S(2)}) collective-permute-start(bf16[256,2048]{1,0:T(8,128)(2,1)S(1)} %copy-done.83), channel_id=1, source_target_pairs={{0,16},{16,0},{8,24},{24,8},{1,17},{17,1},{9,25},{25,9},{2,18},{18... | collective-permute-start | bytes 3145736 | tf_op jit(solution)/shard_map/ppermute | solution.py:353
  319.9 47.3 %collective-permute-start.33 = (bf16[512,2048]{1,0:T(8,128)(2,1)}, bf16[512,2048]{1,0:T(8,128)(2,1)}, u32[]{:S(2)}, u32[]{:S(2)}) collective-permute-start(bf16[512,2048]{1,0:T(8,128)(2,1)} %get-tuple-element.424.refs_0_.refs_1_), channel_id=1, source_target_pairs={{0,16},{16,0},{8,24},{24,8},{1,17},{17,1},{9,25},{25,9},{2,18},{18... | collective-permute-start | bytes 6291464 | tf_op jit(solution)/shard_map/ppermute | solution.py:353
  321.2 47.3 %collective-permute-start.31 = (bf16[512,2048]{1,0:T(8,128)(2,1)}, bf16[512,2048]{1,0:T(8,128)(2,1)}, u32[]{:S(2)}, u32[]{:S(2)}) collective-permute-start(bf16[512,2048]{1,0:T(8,128)(2,1)} %get-tuple-element.424.refs_0_.refs_1_), channel_id=1, source_target_pairs={{0,8},{8,0},{16,24},{24,16},{1,9},{9,1},{17,25},{25,17},{2,10},{10... | collective-permute-start | bytes 6291464 | tf_op jit(solution)/shard_map/ppermute | solution.py:349
  369.9 34.8 %collective-permute-start.35 = (bf16[256,2048]{1,0:T(8,128)(2,1)S(1)}, bf16[256,2048]{1,0:T(8,128)(2,1)S(1)}, u32[]{:S(2)}, u32[]{:S(2)}) collective-permute-start(bf16[256,2048]{1,0:T(8,128)(2,1)S(1)} %slice.449), channel_id=1, source_target_pairs={{0,8},{8,0},{16,24},{24,16},{1,9},{9,1},{17,25},{25,17},{2,10},{10... | collective-permute-start | bytes 3145736 | tf_op jit(solution)/shard_map/ppermute | solution.py:349
  371.1 60.9 %collective-permute-start.34 = (bf16[256,2048]{1,0:T(8,128)(2,1)S(1)}, bf16[256,2048]{1,0:T(8,128)(2,1)S(1)}, u32[]{:S(2)}, u32[]{:S(2)}) collective-permute-start(bf16[256,2048]{1,0:T(8,128)(2,1)S(1)} %slice.445), channel_id=1, source_target_pairs={{0,16},{16,0},{8,24},{24,8},{1,17},{17,1},{9,25},{25,9},{2,18},{18... | collective-permute-start | bytes 3145736 | tf_op jit(solution)/shard_map/ppermute | solution.py:353
  404.7 57.7 %collective-permute-start.36 = (bf16[256,2048]{1,0:T(8,128)(2,1)}, bf16[256,2048]{1,0:T(8,128)(2,1)S(1)}, u32[]{:S(2)}, u32[]{:S(2)}) collective-permute-start(bf16[256,2048]{1,0:T(8,128)(2,1)} %slice.346), channel_id=1, source_target_pairs={{0,8},{8,0},{16,24},{24,16},{1,9},{9,1},{17,25},{25,17},{2,10},{10... | collective-permute-start | bytes 3145736 | tf_op jit(solution)/shard_map/ppermute | solution.py:349
  432.0 30.4 %collective-permute-start.37 = (bf16[256,2048]{1,0:T(8,128)(2,1)}, bf16[256,2048]{1,0:T(8,128)(2,1)}, u32[]{:S(2)}, u32[]{:S(2)}) collective-permute-start(bf16[256,2048]{1,0:T(8,128)(2,1)} %slice.347), channel_id=1, source_target_pairs={{0,16},{16,0},{8,24},{24,8},{1,17},{17,1},{9,25},{25,9},{2,18},{18... | collective-permute-start | bytes 3145736 | tf_op jit(solution)/shard_map/ppermute | solution.py:353
  462.4 31.6 %collective-permute-start.39 = (bf16[256,2048]{1,0:T(8,128)(2,1)}, bf16[256,2048]{1,0:T(8,128)(2,1)}, u32[]{:S(2)}, u32[]{:S(2)}) collective-permute-start(bf16[256,2048]{1,0:T(8,128)(2,1)} %get-tuple-element.413), channel_id=1, source_target_pairs={{0,16},{16,0},{8,24},{24,8},{1,17},{17,1},{9,25},{25,9},{2,18},{18... | collective-permute-start | bytes 3145736 | tf_op jit(solution)/shard_map/ppermute | solution.py:353
  463.8 30.2 %collective-permute-start.38 = (bf16[256,2048]{1,0:T(8,128)(2,1)}, bf16[256,2048]{1,0:T(8,128)(2,1)}, u32[]{:S(2)}, u32[]{:S(2)}) collective-permute-start(bf16[256,2048]{1,0:T(8,128)(2,1)} %get-tuple-element.411), channel_id=1, source_target_pairs={{0,8},{8,0},{16,24},{24,16},{1,9},{9,1},{17,25},{25,17},{2,10},{10... | collective-permute-start | bytes 3145736 | tf_op jit(solution)/shard_map/ppermute | solution.py:349
  526.7 40.4 %collective-permute-start.42 = (bf16[4,1024,1024]{2,1,0:T(8,128)(2,1)}, bf16[4,1024,1024]{2,1,0:T(8,128)(2,1)}, u32[]{:S(2)}, u32[]{:S(2)}) collective-permute-start(bf16[4,1024,1024]{2,1,0:T(8,128)(2,1)} %shard_map.337), channel_id=1, source_target_pairs={{0,4},{4,0},{1,5},{5,1},{2,6},{6,2},{3,7},{7,3},{8,12},{12,8},{9,1... | collective-permute-start | bytes 25165832 | tf_op jit(solution)/shard_map/ppermute | solution.py:345
  526.8 25.6 %collective-permute-start.40 = (bf16[256,2048]{1,0:T(8,128)(2,1)S(1)}, bf16[256,2048]{1,0:T(8,128)(2,1)S(1)}, u32[]{:S(2)}, u32[]{:S(2)}) collective-permute-start(bf16[256,2048]{1,0:T(8,128)(2,1)S(1)} %copy-done.87), channel_id=1, source_target_pairs={{0,16},{16,0},{8,24},{24,8},{1,17},{17,1},{9,25},{25,9},{2,18},{18... | collective-permute-start | bytes 3145736 | tf_op jit(solution)/shard_map/ppermute | solution.py:353
  527.5 25.2 %collective-permute-start.41 = (bf16[256,2048]{1,0:T(8,128)(2,1)S(1)}, bf16[256,2048]{1,0:T(8,128)(2,1)S(1)}, u32[]{:S(2)}, u32[]{:S(2)}) collective-permute-start(bf16[256,2048]{1,0:T(8,128)(2,1)S(1)} %copy-done.86), channel_id=1, source_target_pairs={{0,8},{8,0},{16,24},{24,16},{1,9},{9,1},{17,25},{25,17},{2,10},{10... | collective-permute-start | bytes 3145736 | tf_op jit(solution)/shard_map/ppermute | solution.py:349
  580.3 258.7 %reduce-scatter.3.cloned.1.call-start = ((), (), s32[]{:S(2)}) async-start(), calls=%async_computation.2 | async-start | bytes 5242880 | tf_op jit(solution)/shard_map/reduce_scatter | solution.py:1489
  581.0 383.4 %all-gather.7.cloned.1.call-start = ((), (), s32[]{:S(2)}) async-start(), calls=%async_computation.5 | async-start | bytes 5242880 | tf_op jit(solution)/shard_map/all_gather | solution.py:1490
  585.3 34.9 %collective-permute-start.45 = (bf16[256,2048]{1,0:T(8,128)(2,1)}, bf16[256,2048]{1,0:T(8,128)(2,1)S(1)}, u32[]{:S(2)}, u32[]{:S(2)}) collective-permute-start(bf16[256,2048]{1,0:T(8,128)(2,1)} %get-tuple-element.447), channel_id=1, source_target_pairs={{0,8},{8,0},{16,24},{24,16},{1,9},{9,1},{17,25},{25,17},{2,10},{10... | collective-permute-start | bytes 3145736 | tf_op jit(solution)/shard_map/ppermute | solution.py:349
  586.2 34.0 %collective-permute-start.46 = (bf16[256,2048]{1,0:T(8,128)(2,1)}, bf16[256,2048]{1,0:T(8,128)(2,1)}, u32[]{:S(2)}, u32[]{:S(2)}) collective-permute-start(bf16[256,2048]{1,0:T(8,128)(2,1)} %get-tuple-element.448), channel_id=1, source_target_pairs={{0,16},{16,0},{8,24},{24,8},{1,17},{17,1},{9,25},{25,9},{2,18},{18... | collective-permute-start | bytes 3145736 | tf_op jit(solution)/shard_map/ppermute | solution.py:353
  624.9 30.5 %collective-permute-start.48 = (bf16[256,1024]{1,0:T(8,128)(2,1)}, bf16[256,1024]{1,0:T(8,128)(2,1)S(1)}, u32[]{:S(2)}, u32[]{:S(2)}) collective-permute-start(bf16[256,1024]{1,0:T(8,128)(2,1)} %get-tuple-element.461), channel_id=1, source_target_pairs={{0,16},{16,0},{8,24},{24,8},{1,17},{17,1},{9,25},{25,9},{2,18},{18... | collective-permute-start | bytes 1572872 | tf_op jit(solution)/shard_map/ppermute | solution.py:353
  625.4 31.5 %collective-permute-start.47 = (bf16[256,1024]{1,0:T(8,128)(2,1)}, bf16[256,1024]{1,0:T(8,128)(2,1)}, u32[]{:S(2)}, u32[]{:S(2)}) collective-permute-start(bf16[256,1024]{1,0:T(8,128)(2,1)} %get-tuple-element.459), channel_id=1, source_target_pairs={{0,8},{8,0},{16,24},{24,16},{1,9},{9,1},{17,25},{25,17},{2,10},{10... | collective-permute-start | bytes 1572872 | tf_op jit(solution)/shard_map/ppermute | solution.py:349
  626.5 50.1 %collective-permute-start.52 = (bf16[256,2048]{1,0:T(8,128)(2,1)}, bf16[256,2048]{1,0:T(8,128)(2,1)S(1)}, u32[]{:S(2)}, u32[]{:S(2)}) collective-permute-start(bf16[256,2048]{1,0:T(8,128)(2,1)} %add_convert_fusion.8), channel_id=1, source_target_pairs={{0,16},{16,0},{8,24},{24,8},{1,17},{17,1},{9,25},{25,9},{2,18},{18... | collective-permute-start | bytes 3145736 | tf_op jit(solution)/shard_map/ppermute | solution.py:353
  628.0 49.6 %collective-permute-start.51 = (bf16[256,2048]{1,0:T(8,128)(2,1)}, bf16[256,2048]{1,0:T(8,128)(2,1)S(1)}, u32[]{:S(2)}, u32[]{:S(2)}) collective-permute-start(bf16[256,2048]{1,0:T(8,128)(2,1)} %add_convert_fusion.9), channel_id=1, source_target_pairs={{0,8},{8,0},{16,24},{24,16},{1,9},{9,1},{17,25},{25,17},{2,10},{10... | collective-permute-start | bytes 3145736 | tf_op jit(solution)/shard_map/ppermute | solution.py:349
  653.7 20.0 %collective-permute-start.50 = (bf16[256,1024]{1,0:T(8,128)(2,1)S(1)}, bf16[256,1024]{1,0:T(8,128)(2,1)S(1)}, u32[]{:S(2)}, u32[]{:S(2)}) collective-permute-start(bf16[256,1024]{1,0:T(8,128)(2,1)S(1)} %get-tuple-element.467), channel_id=1, source_target_pairs={{0,16},{16,0},{8,24},{24,8},{1,17},{17,1},{9,25},{25,9},{2,18},{18... | collective-permute-start | bytes 1572872 | tf_op jit(solution)/shard_map/ppermute | solution.py:353
  655.4 188.0 %collective-permute-start.63 = (bf16[256,2048]{1,0:T(8,128)(2,1)}, bf16[256,2048]{1,0:T(8,128)(2,1)}, u32[]{:S(2)}, u32[]{:S(2)}) collective-permute-start(bf16[256,2048]{1,0:T(8,128)(2,1)} %slice.353), channel_id=1, source_target_pairs={{0,16},{16,0},{8,24},{24,8},{1,17},{17,1},{9,25},{25,9},{2,18},{18... | collective-permute-start | bytes 3145736 | tf_op jit(solution)/shard_map/ppermute | solution.py:353
  675.0 67.8 %collective-permute-start.55 = (bf16[256,2048]{1,0:T(8,128)(2,1)}, bf16[256,2048]{1,0:T(8,128)(2,1)}, u32[]{:S(2)}, u32[]{:S(2)}) collective-permute-start(bf16[256,2048]{1,0:T(8,128)(2,1)} %pad_maximum_fusion.3), channel_id=1, source_target_pairs={{0,8},{8,0},{16,24},{24,16},{1,9},{9,1},{17,25},{25,17},{2,10},{10... | collective-permute-start | bytes 3145736 | tf_op jit(solution)/shard_map/ppermute | solution.py:349
  676.0 66.7 %collective-permute-start.56 = (bf16[256,2048]{1,0:T(8,128)(2,1)}, bf16[256,2048]{1,0:T(8,128)(2,1)}, u32[]{:S(2)}, u32[]{:S(2)}) collective-permute-start(bf16[256,2048]{1,0:T(8,128)(2,1)} %pad_maximum_fusion.4), channel_id=1, source_target_pairs={{0,16},{16,0},{8,24},{24,8},{1,17},{17,1},{9,25},{25,9},{2,18},{18... | collective-permute-start | bytes 3145736 | tf_op jit(solution)/shard_map/ppermute | solution.py:353
  701.4 26.8 %collective-permute-start.53 = (bf16[256,1024]{1,0:T(8,128)(2,1)}, bf16[256,1024]{1,0:T(8,128)(2,1)}, u32[]{:S(2)}, u32[]{:S(2)}) collective-permute-start(bf16[256,1024]{1,0:T(8,128)(2,1)} %get-tuple-element.477), channel_id=1, source_target_pairs={{0,8},{8,0},{16,24},{24,16},{1,9},{9,1},{17,25},{25,17},{2,10},{10... | collective-permute-start | bytes 1572872 | tf_op jit(solution)/shard_map/ppermute | solution.py:349
  702.7 261.7 %all-gather.5.cloned.1.call-start = ((), (), s32[]{:S(2)}) async-start(), calls=%async_computation.3 | async-start | bytes 5242880 | tf_op jit(solution)/shard_map/all_gather | solution.py:1490
  705.2 23.0 %collective-permute-start.54 = (bf16[256,1024]{1,0:T(8,128)(2,1)S(1)}, bf16[256,1024]{1,0:T(8,128)(2,1)S(1)}, u32[]{:S(2)}, u32[]{:S(2)}) collective-permute-start(bf16[256,1024]{1,0:T(8,128)(2,1)S(1)} %get-tuple-element.479), channel_id=1, source_target_pairs={{0,16},{16,0},{8,24},{24,8},{1,17},{17,1},{9,25},{25,9},{2,18},{18... | collective-permute-start | bytes 1572872 | tf_op jit(solution)/shard_map/ppermute | solution.py:353
  728.1 78.4 %collective-permute-start.60 = (bf16[256,2048]{1,0:T(8,128)(2,1)S(1)}, bf16[256,2048]{1,0:T(8,128)(2,1)S(1)}, u32[]{:S(2)}, u32[]{:S(2)}) collective-permute-start(bf16[256,2048]{1,0:T(8,128)(2,1)S(1)} %pad_maximum_fusion.6), channel_id=1, source_target_pairs={{0,16},{16,0},{8,24},{24,8},{1,17},{17,1},{9,25},{25,9},{2,18},{18... | collective-permute-start | bytes 3145736 | tf_op jit(solution)/shard_map/ppermute | solution.py:353
  728.9 77.7 %collective-permute-start.59 = (bf16[256,2048]{1,0:T(8,128)(2,1)S(1)}, bf16[256,2048]{1,0:T(8,128)(2,1)S(1)}, u32[]{:S(2)}, u32[]{:S(2)}) collective-permute-start(bf16[256,2048]{1,0:T(8,128)(2,1)S(1)} %pad_maximum_fusion.5), channel_id=1, source_target_pairs={{0,8},{8,0},{16,24},{24,16},{1,9},{9,1},{17,25},{25,17},{2,10},{10... | collective-permute-start | bytes 3145736 | tf_op jit(solution)/shard_map/ppermute | solution.py:349
  765.8 78.0 %collective-permute-start.62 = (bf16[256,2048]{1,0:T(8,128)(2,1)}, bf16[256,2048]{1,0:T(8,128)(2,1)}, u32[]{:S(2)}, u32[]{:S(2)}) collective-permute-start(bf16[256,2048]{1,0:T(8,128)(2,1)} %slice.352), channel_id=1, source_target_pairs={{0,8},{8,0},{16,24},{24,16},{1,9},{9,1},{17,25},{25,17},{2,10},{10... | collective-permute-start | bytes 3145736 | tf_op jit(solution)/shard_map/ppermute | solution.py:349
  769.9 69.1 %collective-permute-start.61 = (bf16[256,2048]{1,0:T(8,128)(2,1)}, bf16[256,2048]{1,0:T(8,128)(2,1)}, u32[]{:S(2)}, u32[]{:S(2)}) collective-permute-start(bf16[256,2048]{1,0:T(8,128)(2,1)} %add_convert_fusion.7), channel_id=1, source_target_pairs={{0,3},{1,0},{2,1},{3,2},{4,7},{5,4},{6,5},{7,6},{8,11},{9,8},{10,9... | collective-permute-start | bytes 3145736 | tf_op jit(solution)/shard_map/ppermute | solution.py:363
  836.5 19.0 %collective-permute-start.64 = (bf16[512,2048]{1,0:T(8,128)(2,1)}, bf16[512,2048]{1,0:T(8,128)(2,1)}, u32[]{:S(2)}, u32[]{:S(2)}) collective-permute-start(bf16[512,2048]{1,0:T(8,128)(2,1)} %pad_maximum_fusion.1), channel_id=1, source_target_pairs={{0,4},{4,0},{1,5},{5,1},{2,6},{6,2},{3,7},{7,3},{8,12},{12,8},{9,1... | collective-permute-start | bytes 6291464 | tf_op jit(solution)/shard_map/ppermute | solution.py:345
  837.6 29.2 %collective-permute-start.67 = (bf16[256,2048]{1,0:T(8,128)(2,1)}, bf16[256,2048]{1,0:T(8,128)(2,1)}, u32[]{:S(2)}, u32[]{:S(2)}) collective-permute-start(bf16[256,2048]{1,0:T(8,128)(2,1)} %pad_maximum_fusion.8), channel_id=1, source_target_pairs={{0,16},{16,0},{8,24},{24,8},{1,17},{17,1},{9,25},{25,9},{2,18},{18... | collective-permute-start | bytes 3145736 | tf_op jit(solution)/shard_map/ppermute | solution.py:353
  839.0 29.3 %collective-permute-start.66 = (bf16[256,2048]{1,0:T(8,128)(2,1)}, bf16[256,2048]{1,0:T(8,128)(2,1)}, u32[]{:S(2)}, u32[]{:S(2)}) collective-permute-start(bf16[256,2048]{1,0:T(8,128)(2,1)} %pad_maximum_fusion.7), channel_id=1, source_target_pairs={{0,8},{8,0},{16,24},{24,16},{1,9},{9,1},{17,25},{25,17},{2,10},{10... | collective-permute-start | bytes 3145736 | tf_op jit(solution)/shard_map/ppermute | solution.py:349
  843.4 25.5 %collective-permute-start.65 = (bf16[256,2048]{1,0:T(8,128)(2,1)}, bf16[256,2048]{1,0:T(8,128)(2,1)}, u32[]{:S(2)}, u32[]{:S(2)}) collective-permute-start(bf16[256,2048]{1,0:T(8,128)(2,1)} %add_convert_fusion.5), channel_id=1, source_target_pairs={{0,3},{1,0},{2,1},{3,2},{4,7},{5,4},{6,5},{7,6},{8,11},{9,8},{10,9... | collective-permute-start | bytes 3145736 | tf_op jit(solution)/shard_map/ppermute | solution.py:363
  855.5 31.9 %collective-permute-start.68 = (f32[256,1024]{1,0:T(8,128)}, f32[256,1024]{1,0:T(8,128)S(1)}, u32[]{:S(2)}, u32[]{:S(2)}) collective-permute-start(f32[256,1024]{1,0:T(8,128)} %get-tuple-element.519), channel_id=1, source_target_pairs={{0,4},{4,0},{1,5},{5,1},{2,6},{6,2},{3,7},{7,3},{8,12},{12,8},{9,1... | collective-permute-start | bytes 3145736 | tf_op jit(solution)/shard_map/ppermute | solution.py:345
  855.5 31.8 %collective-permute-start.69 = (f32[256,1024]{1,0:T(8,128)}, f32[256,1024]{1,0:T(8,128)}, u32[]{:S(2)}, u32[]{:S(2)}) collective-permute-start(f32[256,1024]{1,0:T(8,128)} %get-tuple-element.520), channel_id=1, source_target_pairs={{0,4},{4,0},{1,5},{5,1},{2,6},{6,2},{3,7},{7,3},{8,12},{12,8},{9,1... | collective-permute-start | bytes 3145736 | tf_op jit(solution)/shard_map/ppermute | solution.py:345
  866.8 38.0 %collective-permute-start.71 = (bf16[256,2048]{1,0:T(8,128)(2,1)}, bf16[256,2048]{1,0:T(8,128)(2,1)}, u32[]{:S(2)}, u32[]{:S(2)}) collective-permute-start(bf16[256,2048]{1,0:T(8,128)(2,1)} %pad_maximum_fusion.9), channel_id=1, source_target_pairs={{0,8},{8,0},{16,24},{24,16},{1,9},{9,1},{17,25},{25,17},{2,10},{10... | collective-permute-start | bytes 3145736 | tf_op jit(solution)/shard_map/ppermute | solution.py:349
  868.3 43.0 %collective-permute-start.73 = (bf16[256,2048]{1,0:T(8,128)(2,1)}, bf16[256,2048]{1,0:T(8,128)(2,1)}, u32[]{:S(2)}, u32[]{:S(2)}) collective-permute-start(bf16[256,2048]{1,0:T(8,128)(2,1)} %pad_maximum_fusion.10), channel_id=1, source_target_pairs={{0,16},{16,0},{8,24},{24,8},{1,17},{17,1},{9,25},{25,9},{2,18},{18... | collective-permute-start | bytes 3145736 | tf_op jit(solution)/shard_map/ppermute | solution.py:353
  872.9 38.4 %collective-permute-start.74 = (bf16[256,2048]{1,0:T(8,128)(2,1)}, bf16[256,2048]{1,0:T(8,128)(2,1)}, u32[]{:S(2)}, u32[]{:S(2)}) collective-permute-start(bf16[256,2048]{1,0:T(8,128)(2,1)} %add_convert_fusion.3), channel_id=1, source_target_pairs={{0,3},{1,0},{2,1},{3,2},{4,7},{5,4},{6,5},{7,6},{8,11},{9,8},{10,9... | collective-permute-start | bytes 3145736 | tf_op jit(solution)/shard_map/ppermute | solution.py:363
  916.3 28.6 %collective-permute-start.82 = (bf16[256,2048]{1,0:T(8,128)(2,1)S(1)}, bf16[256,2048]{1,0:T(8,128)(2,1)S(1)}, u32[]{:S(2)}, u32[]{:S(2)}) collective-permute-start(bf16[256,2048]{1,0:T(8,128)(2,1)S(1)} %pad_maximum_fusion.11.refs_0_), channel_id=1, source_target_pairs={{0,8},{8,0},{16,24},{24,16},{1,9},{9,1},{17,25},{25,17},{2,10},{10... | collective-permute-start | bytes 3145736 | tf_op jit(solution)/shard_map/ppermute | solution.py:349
  921.2 25.1 %collective-permute-start.81 = (bf16[256,2048]{1,0:T(8,128)(2,1)S(1)}, bf16[256,2048]{1,0:T(8,128)(2,1)S(1)}, u32[]{:S(2)}, u32[]{:S(2)}) collective-permute-start(bf16[256,2048]{1,0:T(8,128)(2,1)S(1)} %pad_maximum_fusion.11.refs_0_), channel_id=1, source_target_pairs={{0,16},{16,0},{8,24},{24,8},{1,17},{17,1},{9,25},{25,9},{2,18},{18... | collective-permute-start | bytes 3145736 | tf_op jit(solution)/shard_map/ppermute | solution.py:353
  947.1 27.5 %collective-permute-start.83 = (bf16[128,2048]{1,0:T(8,128)(2,1)}, bf16[128,2048]{1,0:T(8,128)(2,1)}, u32[]{:S(2)}, u32[]{:S(2)}) collective-permute-start(bf16[128,2048]{1,0:T(8,128)(2,1)} %slice.463), channel_id=1, source_target_pairs={{0,16},{16,0},{8,24},{24,8},{1,17},{17,1},{9,25},{25,9},{2,18},{18... | collective-permute-start | bytes 1572872 | tf_op jit(solution)/shard_map/ppermute | solution.py:353
  947.7 27.0 %collective-permute-start.84 = (bf16[128,2048]{1,0:T(8,128)(2,1)}, bf16[128,2048]{1,0:T(8,128)(2,1)}, u32[]{:S(2)}, u32[]{:S(2)}) collective-permute-start(bf16[128,2048]{1,0:T(8,128)(2,1)} %slice.462), channel_id=1, source_target_pairs={{0,8},{8,0},{16,24},{24,16},{1,9},{9,1},{17,25},{25,17},{2,10},{10... | collective-permute-start | bytes 1572872 | tf_op jit(solution)/shard_map/ppermute | solution.py:349
  (147 other events, 2558.8 us)
Sparse Core Ops, SparseCore 0:
  39.3 208.9 all-gather.8
  580.4 101.1 reduce-scatter.4
  684.0 77.2 reduce-scatter.2
  763.0 63.5 all-gather.6
  839.1 86.5 all-gather.4
